TPU v7x, 32 devices: a whole 2x2x4 slice. The times are simulated.
32 devices in a mesh: parts: 2 (over y), dp: 4 (over x, core), tensor: 4 (over z).
Axes of the slice: x: 2, y: 2, z: 4, core: 2. Of those that a mesh axis runs over, the one named last changes fastest.
Arguments:
- residual: bfloat16 [2048, 8192], P(('parts', 'dp'), 'tensor'), parts along dimension 0, may hold values from -6 to 6
- query: bfloat16 [2048, 32, 128], P(('parts', 'dp'), 'tensor'), parts along dimension 0, may hold values from -6 to 6
- cached_key_rows: bfloat16 [2048, 16, 8, 128], P(('parts', 'dp'), None, 'tensor'), parts along dimension 0, may hold values from -6 to 6
- cached_value_rows: bfloat16 [2048, 16, 8, 128], P(('parts', 'dp'), None, 'tensor'), parts along dimension 0, may hold values from -6 to 6
- new_token_key: bfloat16 [2048, 8, 128], P(('parts', 'dp'), 'tensor'), parts along dimension 0, may hold values from -6 to 6
- new_token_value: bfloat16 [2048, 8, 128], P(('parts', 'dp'), 'tensor'), parts along dimension 0, may hold values from -6 to 6
- lengths: int32 [2048], P(('parts', 'dp')), parts along dimension 0, may hold values from 2 to 16, as said below
- output_weight: bfloat16 [4096, 8192], P('tensor'), may hold values from -0.09375 to 0.09375
- slot_down_weight: bfloat16 [32, 64, 4096], P('dp', None, 'tensor'), may hold values from -0.09375 to 0.09375
- slot_up_weight: bfloat16 [32, 64, 8192], P('dp', None, 'tensor'), may hold values from -0.75 to 0.75
- placement: int32 [64], P('parts'), parts along dimension 0, may hold values from 0 to 31, as said below
- request_adapter: int32 [2048], P(('parts', 'dp')), parts along dimension 0, may hold values from 0 to 31, as said below
Outputs:
- hidden: bfloat16 [2048, 8192], P(('parts', 'dp'), 'tensor'), parts along dimension 0
There are 2 independent parts, one for each index of `parts`. A program takes and returns all parts, laid end to end along the dimension named above; an argument that names none is the same for every part. Nothing has to cross between parts.
Inputs may be any that keep to these rules, and one draw needn't show every extreme that they name: `lengths`: at least 2 cached positions; some request holds 16. `placement`: each slot once; slot s is entry s % 8 of the adapter store on replica s // 8. `request_adapter`: of one replica's 256 requests at most 64 name adapters held by any one replica; in every part one replica, drawn afresh, is named by exactly 64 requests of every replica.
All inputs are finite; a program needn't handle non-finite values.
Results may differ from a plain program's by a relative error of at most 0.0095.
Values may be sent and summed in bfloat16 or wider, within the bound.
No kernel may reach another device: no remote copies, remote signals or barrier semaphores. Data moves between devices by JAX's collectives and lax.ppermute only.
A program may use at most 128 MiB of HBM per device.

v0:
```python
import math

import jax
import jax.numpy as jnp
from jax import lax
from jax.sharding import PartitionSpec as P


def attend_local(
    query, cached_key_rows, cached_value_rows, new_token_key, new_token_value, lengths
):
    request_rows, head_count, head_width = query.shape
    cache_len = cached_key_rows.shape[1]
    kv_count = cached_key_rows.shape[2]
    query_group_size = head_count // kv_count
    attention_scale = 1.0 / math.sqrt(head_width)
    grouped_queries = query.reshape(request_rows, kv_count, query_group_size, head_width)
    cached = (
        jnp.einsum(
            "bkgd,blkd->bkgl", grouped_queries, cached_key_rows, preferred_element_type=jnp.float32
        )
        * attention_scale
    )
    fresh_scores = (
        jnp.einsum(
            "cfwt,cft->cfw", grouped_queries, new_token_key, preferred_element_type=jnp.float32
        )
        * attention_scale
    )
    valid = jnp.arange(cache_len, dtype=jnp.int32)[None, :] < lengths[:, None]
    cached = jnp.where(valid[:, None, None, :], cached, -jnp.inf)
    top = jnp.maximum(jnp.max(cached, axis=-1), fresh_scores)
    cached_exp = jnp.exp(cached - top[..., None])
    fresh_exp = jnp.exp(fresh_scores - top)
    total_output = jnp.sum(cached_exp, axis=-1) + fresh_exp
    cached_weight = (cached_exp / total_output[..., None]).astype(jnp.bfloat16)
    fresh_weight = (fresh_exp / total_output).astype(jnp.bfloat16)
    mixed = jnp.einsum(
        "bkgl,blkd->bkgd", cached_weight, cached_value_rows, preferred_element_type=jnp.float32
    )
    mixed = (
        mixed
        + fresh_weight.astype(jnp.float32)[..., None]
        * new_token_value.astype(jnp.float32)[:, :, None, :]
    )
    return mixed.astype(jnp.bfloat16).reshape(request_rows, head_count * head_width)


def per_device(
    residual,
    query,
    cached_key_rows,
    cached_value_rows,
    new_token_key,
    new_token_value,
    lengths,
    output_weight,
    slot_down_weight,
    slot_up_weight,
    placement,
    request_adapter,
):
    attended_output = attend_local(
        query, cached_key_rows, cached_value_rows, new_token_key, new_token_value, lengths
    )
    partial_out = jnp.dot(attended_output, output_weight, preferred_element_type=jnp.float32)
    base_output = lax.psum_scatter(
        partial_out.astype(jnp.bfloat16), "tensor", scatter_dimension=1, tiled=True
    ).astype(jnp.float32)
    table_size = placement.shape[0]
    matches = request_adapter[:, None] == jnp.arange(table_size, dtype=jnp.int32)[None, :]
    request_slot = jnp.sum(jnp.where(matches, placement[None, :], 0), axis=1)
    partial_piece = lax.all_gather(slot_down_weight, "dp", axis=0, tiled=True)
    count = partial_piece.shape[0]
    chosen = (request_slot[:, None] == jnp.arange(count, dtype=jnp.int32)[None, :]).astype(
        jnp.float32
    )
    projected = jnp.einsum(
        "nf,arf->nar", attended_output, partial_piece, preferred_element_type=jnp.float32
    )
    mid_part = jnp.sum(chosen[:, :, None] * projected, axis=1)
    rank_mid = lax.psum(mid_part.astype(jnp.bfloat16), "tensor")
    partial_piece = lax.all_gather(slot_up_weight, "dp", axis=0, tiled=True)
    count = partial_piece.shape[0]
    chosen = (request_slot[:, None] == jnp.arange(count, dtype=jnp.int32)[None, :]).astype(
        jnp.bfloat16
    )
    masked_mid = chosen[:, :, None] * rank_mid[:, None, :]
    adapter_delta = jnp.einsum(
        "nar,arc->nc", masked_mid, partial_piece, preferred_element_type=jnp.float32
    ).astype(jnp.bfloat16)
    total_output = residual.astype(jnp.float32) + base_output + adapter_delta.astype(jnp.float32)
    return total_output.astype(jnp.bfloat16)


def solution(mesh):
    placed = (
        P(("parts", "dp"), "tensor"),
        P(("parts", "dp"), "tensor", None),
        P(("parts", "dp"), None, "tensor", None),
        P(("parts", "dp"), None, "tensor", None),
        P(("parts", "dp"), "tensor", None),
        P(("parts", "dp"), "tensor", None),
        P(("parts", "dp")),
        P("tensor", None),
        P("dp", None, "tensor"),
        P("dp", None, "tensor"),
        P("parts"),
        P(("parts", "dp")),
    )
    return jax.shard_map(
        per_device,
        mesh=mesh,
        in_specs=placed,
        out_specs=P(("parts", "dp"), "tensor"),
        check_vma=False,
    )
```

profile of v0, /device:TPU:0, one launch (start us, length us, event | category | flops | bytes accessed | tf_op | source)
XLA Modules:
  0.0 132.2 jit_solution(7565765972088205778)
XLA Ops:
  7.4 0.0 copy-start
  7.4 0.7 all-gather.3.cloned.1.call-update
  8.1 0.0 reduce-scatter.2.cloned.1.call-start
  8.1 0.8 iota_compare_fusion
  8.9 3.2 %fusion.33 = (f32[256,2,4]{2,1,0:T(2,128)S(1)}, f32[256,2,4,16]{3,2,1,0:T(4,128)S(1)}) fusion(bf16[256,2,4,128]{3,2,1,0:T(4,128)(2,1)} %bitcast.35, bf16[256,16,2,128]{3,2,1,0:T(2,128)(2,1)} %param.14, pred[256,16]{1,0:T(8,128)(4,1)S(1)} %iota_compare_fusion), kind=kOutput, calls=%fused_computation.37 | convolution fusion | flops 8484864 | bytes 2764800 | tf_op jit(solution)/shard_map/bkgd,blkd->bkgl/dot_general | solution.py:19
  12.1 0.0 copy-start.1
  12.2 0.1 copy.27
  12.3 2.0 %fusion.26 = f32[256,2,1,4]{3,2,1,0:T(1,128)S(1)} fusion(bf16[256,2,4,128]{3,2,1,0:T(4,128)(2,1)} %bitcast.36, bf16[256,2,128,1]{2,1,0,3:T(2,128)(2,1)} %bitcast.37), kind=kOutput, calls=%fused_computation.23 | convolution fusion | flops 524288 | bytes 663552 | tf_op jit(solution)/shard_map/cfwt,cft->cfw/dot_general | solution.py:25
  14.3 0.1 copy.34
  14.4 0.6 fusion.30
  15.0 0.9 copy.28
  15.9 2.1 %fusion.21 = f32[256,2,4]{2,1,0:T(2,128)} fusion(f32[256,2,4,16]{3,2,1,0:T(4,128)S(1)} %get-tuple-element.10, f32[256,2,4]{2,1,0:T(2,128)S(1)} %copy.28), kind=kLoop, calls=%fused_computation.18 | loop fusion | flops 63488 | bytes 147456 | tf_op jit(solution)/shard_map/reduce_sum | solution.py:35
  18.0 1.7 %copy.29 = f32[256,2,4]{0,2,1:T(4,128)} copy(f32[256,2,4]{2,1,0:T(2,128)} %fusion.21) | data formatting | bytes 16384 | tf_op jit(solution)/shard_map/reduce_sum | solution.py:35
  19.7 0.7 fusion.32
  20.4 0.2 copy.30
  20.6 0.9 copy.32
  21.5 0.1 convert_element_type.54
  21.6 3.4 %fusion.17 = bf16[256,2,4,128]{3,2,1,0:T(4,128)(2,1)S(1)} fusion(bf16[256,16,2,128]{3,2,1,0:T(2,128)(2,1)S(1)} %copy-done, f32[256,2,4,16]{3,2,1,0:T(4,128)} %copy-done.1, f32[256,2,128]{2,1,0:T(2,128)S(1)} %convert_element_type.54, f32[256,2,4]{2,1,0:T(2,128)} %copy.32, f32[256,2,4]{2,1,0:T(2,128)S(1)} %copy.30, f32[256,2,4]{2,1,0:T(2,128)S(1)} %copy.28), kind=kOutput, calls=%fused_computation.14 | convolution fusion | flops 9273344 | bytes 3039232 | tf_op jit(solution)/shard_map/bkgl,blkd->bkgd/dot_general | solution.py:38
  25.0 0.4 reshape.71
  25.3 11.9 %convolution_convert_fusion = bf16[256,8192]{1,0:T(8,128)(2,1)} fusion(bf16[256,1024]{1,0:T(8,128)(2,1)S(1)} %reshape.71, bf16[1024,8192]{1,0:T(8,128)(2,1)} %param.19), kind=kOutput, calls=%fused_computation | convolution fusion | flops 4297064448 | bytes 21495808 | tf_op jit(solution)/shard_map/dot_general | solution.py:66
  37.3 0.0 reduce-scatter.2.cloned.1.call-update
  37.3 0.0 copy-start.4
  37.3 0.0 copy-start.5
  37.3 0.0 all-gather.5.cloned.1.call-start
  37.4 0.7 all-gather.5.cloned.1.call-update
  38.1 1.2 reshape.74
  39.2 0.1 select_reduce_fusion
  39.3 7.6 %all-gather.3.cloned.1.call-done = bf16[32,64,1024]{2,1,0:T(8,128)(2,1)} async-done(((bf16[8,64,1024]{2,1,0:T(8,128)(2,1)}), bf16[32,64,1024]{2,1,0:T(8,128)(2,1)}) %all-gather.3.cloned.1.call-update) | async-done | bytes 4194320 | tf_op jit(solution)/shard_map/all_gather | solution.py:73
  47.0 3.7 %multiply_reduce_fusion = bf16[256,64]{0,1:T(8,128)(2,1)S(1)} fusion(bf16[256,1024,1]{1,0,2:T(8,128)(2,1)} %reshape.74, bf16[32,64,1024]{2,1,0:T(8,128)(2,1)} %all-gather.3.cloned.1.call-done, f32[256,32]{0,1:T(8,128)S(1)} %get-tuple-element.8), kind=kOutput, calls=%fused_computation.10 | convolution fusion | flops 1074774016 | bytes 4784128 | tf_op jit(solution)/shard_map/nf,arf->nar/dot_general | solution.py:78
  50.7 20.7 %psum.7 = bf16[256,64]{0,1:T(8,128)(2,1)S(1)} all-reduce(bf16[256,64]{0,1:T(8,128)(2,1)S(1)} %multiply_reduce_fusion), channel_id=1, replica_groups=mesh['parts'=2,'dp'=4,'tensor'=4] {'tensor'}, use_global_device_ids=true, to_apply=%region_5.6 | all-reduce | flops 16384 | bytes 65536 | tf_op jit(solution)/shard_map/psum | solution.py:82
  71.4 46.4 %reduce-scatter.2.cloned.1.call-done = bf16[256,2048]{1,0:T(8,128)(2,1)} async-done(((bf16[256,8192]{1,0:T(8,128)(2,1)}), bf16[256,2048]{1,0:T(8,128)(2,1)}) %reduce-scatter.2.cloned.1.call-update) | async-done | bytes 1048592 | tf_op jit(solution)/shard_map/reduce_scatter | solution.py:67
  117.8 7.0 %fusion.3 = bf16[256,2048]{1,0:T(8,128)(2,1)} fusion(bf16[32,64,2048]{2,1,0:T(8,128)(2,1)} %all-gather.5.cloned.1.call-done, bf16[256,2048]{1,0:T(8,128)(2,1)} %reduce-scatter.2.cloned.1.call-done, bf16[256,2048]{1,0:T(8,128)(2,1)S(1)} %copy-done.2, bf16[256,64]{0,1:T(8,128)(2,1)S(1)} %psum.7, bf16[256,32]{0,1:T(8,128)(2,1)S(1)} %get-tuple-element.7), kind=kOutput, calls=%fused_computation.5 | convolution fusion | flops 2151677952 | bytes 11583488 | tf_op jit(solution)/shard_map/nar,arc->nc/dot_general | solution.py:89
  (11 shorter events, 0.0 us)
Async XLA Ops:
  7.4 14.2 %copy-start = (bf16[256,16,2,128]{3,2,1,0:T(2,128)(2,1)S(1)}, bf16[256,16,2,128]{3,2,1,0:T(2,128)(2,1)}, u32[]{:S(2)}) copy-start(bf16[256,16,2,128]{3,2,1,0:T(2,128)(2,1)} %param.15) | copy-start | bytes 6291460
  7.4 39.6 %all-gather.3.cloned.1.call-start = ((), (), s32[]{:S(2)}) async-start(), calls=%async_computation.2 | async-start | bytes 5242880 | tf_op jit(solution)/shard_map/all_gather | solution.py:73
  8.1 109.7 %reduce-scatter.2.cloned.1.call-start = ((), (), s32[]{:S(2)}) async-start(), calls=%async_computation.1 | async-start | bytes 5242880 | tf_op jit(solution)/shard_map/reduce_scatter | solution.py:67
  12.1 5.9 %copy-start.1 = (f32[256,2,4,16]{3,2,1,0:T(4,128)}, f32[256,2,4,16]{3,2,1,0:T(4,128)S(1)}, u32[]{:S(2)}) copy-start(f32[256,2,4,16]{3,2,1,0:T(4,128)S(1)} %get-tuple-element.10) | copy-start | bytes 393220
  12.3 9.2 %copy-start.3 = (bf16[256,2,128]{2,1,0:T(2,128)(2,1)S(1)}, bf16[256,2,128]{2,1,0:T(2,128)(2,1)}, u32[]{:S(2)}) copy-start(bf16[256,2,128]{2,1,0:T(2,128)(2,1)} %param.17) | copy-start | bytes 393220
  37.3 1.9 %copy-start.4 = (s32[256]{0:T(256)S(1)}, s32[256]{0:T(256)}, u32[]{:S(2)}) copy-start(s32[256]{0:T(256)} %param.23) | copy-start | bytes 3076
  37.3 1.9 %copy-start.5 = (s32[32]{0:T(128)S(1)}, s32[32]{0:T(128)}, u32[]{:S(2)}) copy-start(s32[32]{0:T(128)} %param.22) | copy-start | bytes 388
  37.3 80.5 %all-gather.5.cloned.1.call-start = ((), (), s32[]{:S(2)}) async-start(), calls=%async_computation.3 | async-start | bytes 10485760 | tf_op jit(solution)/shard_map/all_gather | solution.py:83
  47.0 70.8 %copy-start.2 = (bf16[256,2048]{1,0:T(8,128)(2,1)S(1)}, bf16[256,2048]{1,0:T(8,128)(2,1)}, u32[]{:S(2)}) copy-start(bf16[256,2048]{1,0:T(8,128)(2,1)} %param.12) | copy-start | bytes 3145732
Sparse Core Ops, SparseCore 0:
  9.8 37.1 all-gather.2
  48.5 58.3 all-gather.4
Sparse Core Ops, SparseCore 1:
  37.4 80.4 reduce-scatter.1
where the time goes:
time: 133 us; the launch traced here: 132 us
  waiting for transfers between devices  55.5 us (42%)
  matrix products  31.2 us (23%)
  blocking collectives  20.7 us (16%)
  between operations  15 us (11%)
  local copies, waits for them, and re-layouts  5.37 us (4%)
  other arithmetic  4.42 us (3%)
    reduce_scatter x1, waiting for transfers between devices, per_device(): lax.psum_scatter(partial_out.astype(jnp.bfloat16), 'tensor', scatter_dime...  46.4 us
    psum x1, blocking collectives, per_device(): rank_mid = lax.psum(mid_part.astype(jnp.bfloat16), 'tensor')  20.7 us
    dot_general x1, matrix products, per_device(): jnp.dot(attended_output, output_weight, preferred_element_type=jnp.float32)  11.9 us
    all_gather x1, waiting for transfers between devices, per_device(): partial_piece = lax.all_gather(slot_down_weight, 'dp', axis=0, tiled=True)  7.64 us
    dot_general x1, matrix products, per_device(): jnp.einsum('nar,arc->nc', masked_mid, partial_piece, preferred_element_ty...  6.96 us
    dot_general x1, matrix products, per_device(): jnp.einsum('nf,arf->nar', attended_output, partial_piece, preferred_eleme...  3.73 us
    dot_general x1, matrix products, attend_local(): jnp.einsum('bkgl,blkd->bkgd', cached_weight, cached_value_rows, preferred...  3.38 us
    dot_general x1, matrix products, attend_local(): jnp.einsum('bkgd,blkd->bkgl', grouped_queries, cached_key_rows, preferred...  3.2 us
  transfers between devices with their start and end apart: 3, of which 2 were waited for; matrix products, arithmetic and copies ran while one was open for 26% of the time, Pallas kernels for 0%

commit v1 on v0

v1 whole, which is shorter than its diff:
```python
import functools
import math

import jax
import jax.numpy as jnp
from jax import lax
from jax.experimental import pallas as pl
from jax.experimental.pallas import tpu as pltpu
from jax.sharding import PartitionSpec as P

GROUP = 8
PAIR = 2
MASKED = -1e30
VMEM_LIMIT = 48 * 1024 * 1024
CHAINS = 2


def _dot(a, b, dims):
    return lax.dot_general(a, b, (dims, ((), ())), preferred_element_type=jnp.float32)


def _iota(shape, axis):
    return lax.broadcasted_iota(jnp.int32, shape, axis)


def attend_kernel(heads, kv, cache, q_ref, k_ref, v_ref, nk_ref, nv_ref, len_ref, out_ref, held):
    group_rows = GROUP * heads
    group_cols = GROUP * cache * kv
    fresh_cols = GROUP * kv
    per_kv = heads // kv
    requests = len_ref.shape[1]
    groups = requests // GROUP
    step_groups = out_ref.shape[0] // GROUP
    scale = 1.0 / math.sqrt(q_ref.shape[1])

    row = _iota((group_rows, group_cols), 0)
    col = _iota((group_rows, group_cols), 1)
    same = (row // heads == col // (cache * kv)) & ((row % heads) // per_kv == col % kv)
    own_bias = jnp.where(same, 0.0, MASKED)
    row = _iota((group_rows, fresh_cols), 0)
    col = _iota((group_rows, fresh_cols), 1)
    same = (row // heads == col // kv) & ((row % heads) // per_kv == col % kv)
    fresh_bias = jnp.where(same, 0.0, MASKED)

    first = pl.program_id(0) * step_groups
    counts = len_ref[...].astype(jnp.float32)
    group_of = _iota((step_groups, requests), 1) // GROUP == _iota((step_groups, requests), 0) + first
    counts = jnp.where(group_of, counts, 0.0).astype(jnp.bfloat16)
    spread = _iota((requests, group_cols), 0) % GROUP == _iota((requests, group_cols), 1) // (cache * kv)
    counts = _dot(counts, spread.astype(jnp.bfloat16), ((1,), (0,)))
    position = (_iota((step_groups, group_cols), 1) // kv) % cache
    length_bias = jnp.where(position.astype(jnp.float32) < counts, 0.0, MASKED)

    for pair in range(step_groups // PAIR):
        for side in range(PAIR):
            g = pair * PAIR + side
            q = q_ref[pl.ds(g * group_rows, group_rows), :]
            k = k_ref[pl.ds(g * group_cols, group_cols), :]
            v = v_ref[pl.ds(g * group_cols, group_cols), :]
            nk = nk_ref[pl.ds(g * fresh_cols, fresh_cols), :]
            nv = nv_ref[pl.ds(g * fresh_cols, fresh_cols), :]
            scores = _dot(q, k, ((1,), (1,))) * scale + (own_bias + length_bias[g : g + 1, :])
            fresh = _dot(q, nk, ((1,), (1,))) * scale + fresh_bias
            top = jnp.maximum(
                jnp.max(scores, axis=1, keepdims=True), jnp.max(fresh, axis=1, keepdims=True)
            )
            scores = jnp.exp(scores - top)
            fresh = jnp.exp(fresh - top)
            total = jnp.sum(scores, axis=1, keepdims=True) + jnp.sum(fresh, axis=1, keepdims=True)
            inverse = 1.0 / total
            mixed = _dot((scores * inverse).astype(jnp.bfloat16), v, ((1,), (0,)))
            mixed = mixed + _dot((fresh * inverse).astype(jnp.bfloat16), nv, ((1,), (0,)))
            held[pair % 2, pl.ds(side * group_rows, group_rows), :] = mixed
        width = q_ref.shape[1]
        for h in range(heads):
            part = held[pair % 2, pl.ds(h, PAIR * GROUP, stride=heads), :]
            out_ref[pl.ds(pair * PAIR * GROUP, PAIR * GROUP), pl.ds(h * width, width)] = part.astype(
                jnp.bfloat16
            )


def attend(query, keys, values, new_key, new_value, lengths):
    requests, heads, width = query.shape
    cache, kv = keys.shape[1], keys.shape[2]
    steps = 4
    per = requests // steps

    def rows(count):
        return pl.BlockSpec((per * count, width), lambda i: (i, 0))

    return pl.pallas_call(
        functools.partial(attend_kernel, heads, kv, cache),
        grid=(steps,),
        in_specs=[
            rows(heads),
            rows(cache * kv),
            rows(cache * kv),
            rows(kv),
            rows(kv),
            pl.BlockSpec((1, requests), lambda i: (0, 0)),
        ],
        out_specs=pl.BlockSpec((per, heads * width), lambda i: (i, 0)),
        out_shape=jax.ShapeDtypeStruct((requests, heads * width), jnp.bfloat16),
        scratch_shapes=[pltpu.VMEM((2, PAIR * GROUP * heads, width), jnp.float32)],
        compiler_params=pltpu.CompilerParams(vmem_limit_bytes=VMEM_LIMIT),
        name="attend",
    )(
        query.reshape(requests * heads, width),
        keys.reshape(requests * cache * kv, width),
        values.reshape(requests * cache * kv, width),
        new_key.reshape(requests * kv, width),
        new_value.reshape(requests * kv, width),
        lengths.reshape(1, requests),
    )


def project_kernel(blocks_ref, a_ref, w_ref, out_ref):
    out_ref[...] = _dot(a_ref[...], w_ref[...], ((1,), (0,))).astype(jnp.bfloat16)


def project(attended, weight, blocks, block_width):
    rows, depth = attended.shape
    count = blocks.shape[0]
    return pl.pallas_call(
        project_kernel,
        grid_spec=pltpu.PrefetchScalarGridSpec(
            num_scalar_prefetch=1,
            grid=(count,),
            in_specs=[
                pl.BlockSpec((rows, depth), lambda i, b: (0, 0)),
                pl.BlockSpec((depth, block_width), lambda i, b: (0, b[i])),
            ],
            out_specs=pl.BlockSpec((rows, block_width), lambda i, b: (0, i)),
        ),
        out_shape=jax.ShapeDtypeStruct((rows, count * block_width), jnp.bfloat16),
        compiler_params=pltpu.CompilerParams(vmem_limit_bytes=VMEM_LIMIT),
        name="project",
    )(blocks, attended, weight)


def ring_order(count):
    return list(range(0, count, 2)) + list(range(1, count, 2))[::-1]


def gather_by_exchange(blocks, count):
    held = [blocks]
    reach = count // 2
    place = [0]
    while reach:
        perm = [(i, i ^ reach) for i in range(count)]
        held = held + [lax.ppermute(h, "dp", perm) for h in held]
        place = place + [p ^ reach for p in place]
        reach //= 2
    return held, place


def per_device(
    residual,
    query,
    cached_key_rows,
    cached_value_rows,
    new_token_key,
    new_token_value,
    lengths,
    output_weight,
    slot_down_weight,
    slot_up_weight,
    placement,
    request_adapter,
):
    tensor_count = lax.axis_size("tensor")
    dp_count = lax.axis_size("dp")
    order = ring_order(tensor_count)
    spot = {device: p for p, device in enumerate(order)}
    ring = [(order[p], order[(p + 1) % tensor_count]) for p in range(tensor_count)]
    table = [
        [order[(spot[t] - 1 - s) % tensor_count] for s in range(tensor_count)]
        for t in range(tensor_count)
    ]
    here = lax.axis_index("tensor")
    owners = jnp.asarray(table, jnp.int32)[here]

    downs, places = gather_by_exchange(slot_down_weight, dp_count)
    ups, _ = gather_by_exchange(slot_up_weight, dp_count)

    attended = attend(
        query, cached_key_rows, cached_value_rows, new_token_key, new_token_value, lengths
    )
    rows = attended.shape[0]
    out_width = residual.shape[1]
    chain_width = out_width // CHAINS
    block_width = min(512, chain_width)
    per_chain = chain_width // block_width
    blocks = owners[:, None, None] * (CHAINS * per_chain) + jnp.arange(
        CHAINS * per_chain, dtype=jnp.int32
    ).reshape(1, CHAINS, per_chain)

    first = [project(attended, output_weight, blocks[0, c], block_width) for c in range(CHAINS)]
    rest = project(attended, output_weight, blocks[1:].reshape(-1), block_width)

    table_size = placement.shape[0]
    matches = request_adapter[:, None] == jnp.arange(table_size, dtype=jnp.int32)[None, :]
    request_slot = jnp.sum(jnp.where(matches, placement[None, :], 0), axis=1)
    slots, rank = slot_down_weight.shape[0], slot_down_weight.shape[1]
    holder = (request_slot // slots) ^ lax.axis_index("dp")
    inside = request_slot % slots

    mid = jnp.zeros((rows, rank), jnp.float32)
    chosen = []
    for down, place in zip(downs, places):
        pick = (holder == place)[:, None] & (
            inside[:, None] == jnp.arange(slots, dtype=jnp.int32)[None, :]
        )
        chosen.append(pick)
        projected = jnp.einsum("nf,arf->nar", attended, down, preferred_element_type=jnp.float32)
        mid = mid + jnp.sum(jnp.where(pick[:, :, None], projected, 0.0), axis=1)
    mid = mid.astype(jnp.bfloat16)
    mids = [mid]
    for step in range(1, tensor_count):
        perm = [(i, (i + step) % tensor_count) for i in range(tensor_count)]
        mids.append(lax.ppermute(mid, "tensor", perm))
    rank_mid = sum(m.astype(jnp.float32) for m in mids).astype(jnp.bfloat16)

    delta = jnp.zeros((rows, out_width), jnp.float32)
    for up, pick in zip(ups, chosen):
        masked = pick.astype(jnp.bfloat16)[:, :, None] * rank_mid[:, None, :]
        delta = delta + jnp.einsum("nar,arc->nc", masked, up, preferred_element_type=jnp.float32)
    delta = delta.astype(jnp.bfloat16)

    outs = []
    travelling = list(first)
    for step in range(1, tensor_count):
        for c in range(CHAINS):
            arrived = lax.ppermute(travelling[c], "tensor", ring)
            at = ((step - 1) * CHAINS + c) * chain_width
            own = lax.slice_in_dim(rest, at, at + chain_width, axis=1)
            total = arrived.astype(jnp.float32) + own.astype(jnp.float32)
            if step < tensor_count - 1:
                travelling[c] = total.astype(jnp.bfloat16)
            else:
                cols = slice(c * chain_width, (c + 1) * chain_width)
                total = (
                    residual[:, cols].astype(jnp.float32)
                    + total
                    + delta[:, cols].astype(jnp.float32)
                )
                outs.append(total.astype(jnp.bfloat16))
    return jnp.concatenate(outs, axis=1)


def solution(mesh):
    placed = (
        P(("parts", "dp"), "tensor"),
        P(("parts", "dp"), "tensor", None),
        P(("parts", "dp"), None, "tensor", None),
        P(("parts", "dp"), None, "tensor", None),
        P(("parts", "dp"), "tensor", None),
        P(("parts", "dp"), "tensor", None),
        P(("parts", "dp")),
        P("tensor", None),
        P("dp", None, "tensor"),
        P("dp", None, "tensor"),
        P("parts"),
        P(("parts", "dp")),
    )
    return jax.shard_map(
        per_device,
        mesh=mesh,
        in_specs=placed,
        out_specs=P(("parts", "dp"), "tensor"),
        check_vma=False,
    )
```

time: 133 us -> 112 us (0.84)
  Pallas kernels: 0 us -> 28.3 us
  starting transfers between devices: 0.09 us -> 22 us
  blocking collectives: 20.7 us -> 0 us
  matrix products: 31.2 us -> 11.4 us
  waiting for transfers between devices: 55.5 us -> 37.4 us
  between operations: 15 us -> 0.24 us
  local copies, waits for them, and re-layouts: 5.37 us -> 6.82 us
    reduce_scatter x1 -> x0, waiting for transfers between devices: 46.4 us -> none  [per_device(): lax.psum_scatter(partial_out.astype(jnp.bfloat16), 'tensor', scatter_dime...]
    ppermute x0 -> x15, waiting for transfers between devices: none -> 37.4 us  [the longest x6 28.7 us: per_device(): arrived = lax.ppermute(travelling[c], 'tensor', ring)]
    pallas_call x0 -> x4, Pallas kernels: none -> 28.3 us  [the longest x3 16.9 us: project(): pl.pallas_call(project_kernel, grid_spec=pltpu.PrefetchScalarGridSpec(num...]
    ppermute x0 -> x15, starting transfers between devices: none -> 22 us  [the longest x6 11.9 us: per_device(): arrived = lax.ppermute(travelling[c], 'tensor', ring)]
    psum x1 -> x0, blocking collectives: 20.7 us -> none  [per_device(): rank_mid = lax.psum(mid_part.astype(jnp.bfloat16), 'tensor')]
    dot_general x6 -> x8, matrix products: 31.2 us -> 11.4 us  [the longest x4 6.83 us: per_device(): jnp.einsum('nf,arf->nar', attended, down, preferred_element_type=jnp.floa...]
    all_gather x2 -> x0, waiting for transfers between devices: 7.64 us -> none  [the longest x1 7.64 us: per_device(): partial_piece = lax.all_gather(slot_down_weight, 'dp', axis=0, tiled=True)]
    unnamed x12 -> x20, local copies, waits for them, and re-layouts: 0.03 us -> 6.73 us
  transfers between devices with their start and end apart: 3 -> 15, of which waited for: 2 -> 5; matrix products, arithmetic and copies ran while one was open for 26% -> 13% of each run, Pallas kernels for 0% -> 26%
where the time goes in v1:
time: 112 us; the launch traced here: 111 us
  waiting for transfers between devices  37.4 us (33%)
  Pallas kernels  28.3 us (25%)
  starting transfers between devices  22 us (20%)
  matrix products  11.4 us (10%)
  local copies, waits for them, and re-layouts  6.82 us (6%)
  other arithmetic  4.86 us (4%)
    ppermute x6, waiting for transfers between devices, per_device(): arrived = lax.ppermute(travelling[c], 'tensor', ring)  28.7 us
    pallas_call x3, Pallas kernels, project(): pl.pallas_call(project_kernel, grid_spec=pltpu.PrefetchScalarGridSpec(num...  16.9 us
    ppermute x6, starting transfers between devices, per_device(): arrived = lax.ppermute(travelling[c], 'tensor', ring)  11.9 us
    pallas_call x1, Pallas kernels, attend(): pl.pallas_call(functools.partial(attend_kernel, heads, kv, cache), grid=(...  11.4 us
    ppermute x6, waiting for transfers between devices, gather_by_exchange(): held = held + [lax.ppermute(h, 'dp', perm) for h in held]  8.67 us
    ppermute x3, starting transfers between devices, per_device(): mids.append(lax.ppermute(mid, 'tensor', perm))  6.99 us
    dot_general x4, matrix products, per_device(): jnp.einsum('nf,arf->nar', attended, down, preferred_element_type=jnp.floa...  6.83 us
    unnamed x20, local copies, waits for them, and re-layouts  6.73 us
  transfers between devices with their start and end apart: 15, of which 5 were waited for; matrix products, arithmetic and copies ran while one was open for 13% of the time, Pallas kernels for 26%

profile of v1, /device:TPU:0, one launch (start us, length us, event | category | flops | bytes accessed | tf_op | source)
XLA Modules:
  0.0 111.1 jit_solution(7510221263711179881)
XLA Ops:
  0.0 2.9 %collective-permute-start.3 = (bf16[8,64,1024]{2,1,0:T(8,128)(2,1)}, bf16[8,64,1024]{2,1,0:T(8,128)(2,1)}, u32[]{:S(2)}, u32[]{:S(2)}) collective-permute-start(bf16[8,64,1024]{2,1,0:T(8,128)(2,1)} %param.21), channel_id=1, source_target_pairs={{0,8},{4,12},{8,0},{12,4},{1,9},{5,13},{9,1},{13,5},{2,10},{6,14},... | collective-permute-start | bytes 3145736 | tf_op jit(solution)/shard_map/ppermute | solution.py:151
  3.8 1.6 %copy-done = bf16[256,16,2,128]{3,2,1,0:T(2,128)(2,1)S(1)} copy-done((bf16[256,16,2,128]{3,2,1,0:T(2,128)(2,1)S(1)}, bf16[256,16,2,128]{3,2,1,0:T(2,128)(2,1)}, u32[]{:S(2)}) %copy-start) | copy-done | bytes 2097176
  5.4 1.6 %copy-done.1 = bf16[256,16,2,128]{3,2,1,0:T(2,128)(2,1)S(1)} copy-done((bf16[256,16,2,128]{3,2,1,0:T(2,128)(2,1)S(1)}, bf16[256,16,2,128]{3,2,1,0:T(2,128)(2,1)}, u32[]{:S(2)}) %copy-start.1) | copy-done | bytes 2097176
  7.0 1.0 copy-done.2
  8.0 0.9 copy-done.3
  8.9 0.9 copy-done.4
  10.5 11.4 %attend.1.a_ref = bf16[256,1024]{1,0:T(8,128)(2,1)S(1)} custom-call(bf16[2048,128]{1,0:T(8,128)(2,1)S(1)} %bitcast.47, bf16[8192,128]{1,0:T(8,128)(2,1)S(1)} %bitcast.45, bf16[8192,128]{1,0:T(8,128)(2,1)S(1)} %bitcast.46, bf16[512,128]{1,0:T(8,128)(2,1)S(1)} %bitcast.48, bf16[512,128]{1,0:T(8,128)(2,1)S(1)} %bitcast.49, s32[1,256]{1,0:T(1,128)S(1)} %bitcast.50), custom_call_target="tpu_custom_call" | custom-call | tf_op jit(solution)/shard_map/attend/pallas_call | solution.py:91
  21.9 2.7 %project.3 = bf16[256,1024]{1,0:T(8,128)(2,1)S(1)} custom-call(s32[2]{0:T(128)S(1)} %get-tuple-element.13.blocks_ref, bf16[256,1024]{1,0:T(8,128)(2,1)S(1)} %attend.1.a_ref, bf16[1024,8192]{1,0:T(8,128)(2,1)} %w_ref.5), custom_call_target="tpu_custom_call" | custom-call | tf_op jit(solution)/shard_map/project/pallas_call | solution.py:124
  24.7 3.1 %collective-permute-start = (bf16[256,1024]{1,0:T(8,128)(2,1)S(1)}, bf16[256,1024]{1,0:T(8,128)(2,1)}, u32[]{:S(2)}, u32[]{:S(2)}) collective-permute-start(bf16[256,1024]{1,0:T(8,128)(2,1)S(1)} %project.3), channel_id=1, source_target_pairs={{0,2},{2,3},{3,1},{1,0},{4,6},{6,7},{7,5},{5,4},{8,10},{10,11},{11... | collective-permute-start | bytes 1572872 | tf_op jit(solution)/shard_map/ppermute | solution.py:234
  27.8 2.7 %project.5 = bf16[256,1024]{1,0:T(8,128)(2,1)S(1)} custom-call(s32[2]{0:T(128)S(1)} %get-tuple-element.14.blocks_ref, bf16[256,1024]{1,0:T(8,128)(2,1)S(1)} %attend.1.a_ref, bf16[1024,8192]{1,0:T(8,128)(2,1)} %w_ref.5), custom_call_target="tpu_custom_call" | custom-call | tf_op jit(solution)/shard_map/project/pallas_call | solution.py:124
  30.5 1.6 %collective-permute-start.12 = (bf16[256,1024]{1,0:T(8,128)(2,1)S(1)}, bf16[256,1024]{1,0:T(8,128)(2,1)}, u32[]{:S(2)}, u32[]{:S(2)}) collective-permute-start(bf16[256,1024]{1,0:T(8,128)(2,1)S(1)} %project.5), channel_id=1, source_target_pairs={{0,2},{2,3},{3,1},{1,0},{4,6},{6,7},{7,5},{5,4},{8,10},{10,11},{11... | collective-permute-start | bytes 1572872 | tf_op jit(solution)/shard_map/ppermute | solution.py:234
  32.4 7.7 %collective-permute-done = bf16[256,1024]{1,0:T(8,128)(2,1)} collective-permute-done((bf16[256,1024]{1,0:T(8,128)(2,1)S(1)}, bf16[256,1024]{1,0:T(8,128)(2,1)}, u32[]{:S(2)}, u32[]{:S(2)}) %collective-permute-start) | collective-permute-done | bytes 524320 | tf_op jit(solution)/shard_map/ppermute | solution.py:234
  40.0 1.7 %fusion.4 = f32[256,64]{0,1:T(8,128)S(1)} fusion(bf16[8,64,1024]{2,1,0:T(8,128)(2,1)} %param.21, bf16[256,1024]{1,0:T(8,128)(2,1)S(1)} %attend.1.a_ref, pred[256,8]{0,1:T(8,128)(4,1)S(1)} %get-tuple-element.25), kind=kOutput, calls=%fused_computation.12 | convolution fusion | flops 268681216 | bytes 1640448 | tf_op jit(solution)/shard_map/nf,arf->nar/dot_general | solution.py:215
  41.9 11.5 %project.4 = bf16[256,6144]{1,0:T(8,128)(2,1)S(1)} custom-call(s32[12]{0:T(128)S(1)} %reshape.366.blocks_ref, bf16[256,1024]{1,0:T(8,128)(2,1)S(1)} %attend.1.a_ref, bf16[1024,8192]{1,0:T(8,128)(2,1)} %w_ref.5), custom_call_target="tpu_custom_call" | custom-call | tf_op jit(solution)/shard_map/project/pallas_call | solution.py:124
  53.4 1.6 %add_convert_fusion.5 = (bf16[256,1024]{1,0:T(8,128)(2,1)S(1)}, bf16[256,1024]{1,0:T(8,128)(2,1)S(1)}) fusion(bf16[256,1024]{1,0:T(8,128)(2,1)} %collective-permute-done, bf16[256,6144]{1,0:T(8,128)(2,1)S(1)} %project.4, bf16[256,1024]{1,0:T(8,128)(2,1)} %collective-permute-done.12), kind=kLoop, calls=%fused_computation.22 | loop fusion | flops 2097152 | bytes 3145728 | tf_op jit(solution)/shard_map/convert_element_type | solution.py:239
  55.0 3.5 %collective-permute-start.1 = (bf16[256,1024]{1,0:T(8,128)(2,1)S(1)}, bf16[256,1024]{1,0:T(8,128)(2,1)S(1)}, u32[]{:S(2)}, u32[]{:S(2)}) collective-permute-start(bf16[256,1024]{1,0:T(8,128)(2,1)S(1)} %get-tuple-element.11), channel_id=1, source_target_pairs={{0,2},{2,3},{3,1},{1,0},{4,6},{6,7},{7,5},{5,4},{8,10},{10,11},{11... | collective-permute-start | bytes 1572872 | tf_op jit(solution)/shard_map/ppermute | solution.py:234
  58.5 1.7 %fusion.5 = f32[256,64]{0,1:T(8,128)S(1)} fusion(bf16[8,64,1024]{2,1,0:T(8,128)(2,1)} %collective-permute-done.3, bf16[256,1024]{1,0:T(8,128)(2,1)S(1)} %attend.1.a_ref, pred[256,8]{0,1:T(8,128)(4,1)S(1)} %get-tuple-element.23), kind=kOutput, calls=%fused_computation.13 | convolution fusion | flops 268681216 | bytes 1640448 | tf_op jit(solution)/shard_map/nf,arf->nar/dot_general | solution.py:215
  61.0 1.7 %fusion.6 = f32[256,64]{0,1:T(8,128)S(1)} fusion(bf16[8,64,1024]{2,1,0:T(8,128)(2,1)} %collective-permute-done.4, bf16[256,1024]{1,0:T(8,128)(2,1)S(1)} %attend.1.a_ref, pred[256,8]{0,1:T(8,128)(4,1)S(1)} %get-tuple-element.28), kind=kOutput, calls=%fused_computation.14 | convolution fusion | flops 268681216 | bytes 1640448 | tf_op jit(solution)/shard_map/nf,arf->nar/dot_general | solution.py:215
  62.7 8.7 %collective-permute-done.9 = bf16[8,64,2048]{2,1,0:T(8,128)(2,1)} collective-permute-done((bf16[8,64,2048]{2,1,0:T(8,128)(2,1)}, bf16[8,64,2048]{2,1,0:T(8,128)(2,1)}, u32[]{:S(2)}, u32[]{:S(2)}) %collective-permute-start.9) | collective-permute-done | bytes 2097184 | tf_op jit(solution)/shard_map/ppermute | solution.py:151
  71.4 1.7 %fusion.7 = f32[256,64]{0,1:T(8,128)S(1)} fusion(bf16[8,64,1024]{2,1,0:T(8,128)(2,1)} %collective-permute-done.5, bf16[256,1024]{1,0:T(8,128)(2,1)S(1)} %attend.1.a_ref, pred[256,8]{0,1:T(8,128)(4,1)S(1)} %get-tuple-element.16), kind=kOutput, calls=%fused_computation.15 | convolution fusion | flops 268681216 | bytes 1640448 | tf_op jit(solution)/shard_map/nf,arf->nar/dot_general | solution.py:215
  73.1 1.9 %collective-permute-start.6 = (bf16[256,64]{0,1:T(8,128)(2,1)S(1)}, bf16[256,64]{0,1:T(8,128)(2,1)S(1)}, u32[]{:S(2)}, u32[]{:S(2)}) collective-permute-start(bf16[256,64]{0,1:T(8,128)(2,1)S(1)} %add_convert_fusion.7), channel_id=1, source_target_pairs={{0,1},{1,2},{2,3},{3,0},{4,5},{5,6},{6,7},{7,4},{8,9},{9,10},{10,1... | collective-permute-start | bytes 98312 | tf_op jit(solution)/shard_map/ppermute | solution.py:221
  75.0 2.6 %collective-permute-start.7 = (bf16[256,64]{0,1:T(8,128)(2,1)S(1)}, bf16[256,64]{0,1:T(8,128)(2,1)S(1)}, u32[]{:S(2)}, u32[]{:S(2)}) collective-permute-start(bf16[256,64]{0,1:T(8,128)(2,1)S(1)} %add_convert_fusion.7), channel_id=1, source_target_pairs={{0,2},{1,3},{2,0},{3,1},{4,6},{5,7},{6,4},{7,5},{8,10},{9,11},{10,... | collective-permute-start | bytes 98312 | tf_op jit(solution)/shard_map/ppermute | solution.py:221
  77.6 4.4 %collective-permute-done.13 = bf16[256,1024]{1,0:T(8,128)(2,1)S(1)} collective-permute-done((bf16[256,1024]{1,0:T(8,128)(2,1)S(1)}, bf16[256,1024]{1,0:T(8,128)(2,1)S(1)}, u32[]{:S(2)}, u32[]{:S(2)}) %collective-permute-start.13) | collective-permute-done | bytes 524320 | tf_op jit(solution)/shard_map/ppermute | solution.py:234
  82.0 2.5 %collective-permute-start.8 = (bf16[256,64]{0,1:T(8,128)(2,1)S(1)}, bf16[256,64]{0,1:T(8,128)(2,1)S(1)}, u32[]{:S(2)}, u32[]{:S(2)}) collective-permute-start(bf16[256,64]{0,1:T(8,128)(2,1)S(1)} %add_convert_fusion.7), channel_id=1, source_target_pairs={{0,3},{1,0},{2,1},{3,2},{4,7},{5,4},{6,5},{7,6},{8,11},{9,8},{10,9... | collective-permute-start | bytes 98312 | tf_op jit(solution)/shard_map/ppermute | solution.py:221
  84.9 1.4 %collective-permute-start.14 = (bf16[256,1024]{1,0:T(8,128)(2,1)S(1)}, bf16[256,1024]{1,0:T(8,128)(2,1)S(1)}, u32[]{:S(2)}, u32[]{:S(2)}) collective-permute-start(bf16[256,1024]{1,0:T(8,128)(2,1)S(1)} %get-tuple-element.10), channel_id=1, source_target_pairs={{0,2},{2,3},{3,1},{1,0},{4,6},{6,7},{7,5},{5,4},{8,10},{10,11},{11... | collective-permute-start | bytes 1572872 | tf_op jit(solution)/shard_map/ppermute | solution.py:234
  86.4 1.5 %collective-permute-start.2 = (bf16[256,1024]{1,0:T(8,128)(2,1)S(1)}, bf16[256,1024]{1,0:T(8,128)(2,1)S(1)}, u32[]{:S(2)}, u32[]{:S(2)}) collective-permute-start(bf16[256,1024]{1,0:T(8,128)(2,1)S(1)} %get-tuple-element.9), channel_id=1, source_target_pairs={{0,2},{2,3},{3,1},{1,0},{4,6},{6,7},{7,5},{5,4},{8,10},{10,11},{11... | collective-permute-start | bytes 1572872 | tf_op jit(solution)/shard_map/ppermute | solution.py:234
  89.4 2.3 %fusion.1 = f32[256,2048]{1,0:T(8,128)S(1)} fusion(f32[256,2048]{1,0:T(8,128)S(1)} %convolution_bitcast_fusion.1, f32[256,2048]{1,0:T(8,128)S(1)} %convolution_bitcast_fusion.3, bf16[8,64,2048]{2,1,0:T(8,128)(2,1)} %collective-permute-done.9, bf16[256,8]{0,1:T(8,128)(2,1)S(1)} %get-tuple-element.24, bf16[256,64]{0,1:T(8,128)(2,1)S(1)} %add_convert_fusion.6), kind=kOutput, calls=%fused_computation.5 | convolution fusion | flops 538050560 | bytes 8425472 | tf_op jit(solution)/shard_map/nar,arc->nc/dot_general | solution.py:227
  91.8 0.7 fusion.3
  92.5 7.3 %collective-permute-done.14 = bf16[256,1024]{1,0:T(8,128)(2,1)S(1)} collective-permute-done((bf16[256,1024]{1,0:T(8,128)(2,1)S(1)}, bf16[256,1024]{1,0:T(8,128)(2,1)S(1)}, u32[]{:S(2)}, u32[]{:S(2)}) %collective-permute-start.14) | collective-permute-done | bytes 524320 | tf_op jit(solution)/shard_map/ppermute | solution.py:234
  99.9 9.3 %collective-permute-done.2 = bf16[256,1024]{1,0:T(8,128)(2,1)S(1)} collective-permute-done((bf16[256,1024]{1,0:T(8,128)(2,1)S(1)}, bf16[256,1024]{1,0:T(8,128)(2,1)S(1)}, u32[]{:S(2)}, u32[]{:S(2)}) %collective-permute-start.2) | collective-permute-done | bytes 524320 | tf_op jit(solution)/shard_map/ppermute | solution.py:234
  109.1 0.9 add_convert_fusion.3
  110.0 1.1 pad_maximum_fusion
  (47 shorter events, 4.5 us)
Async XLA Ops:
  0.0 32.2 %collective-permute-start.3 = (bf16[8,64,1024]{2,1,0:T(8,128)(2,1)}, bf16[8,64,1024]{2,1,0:T(8,128)(2,1)}, u32[]{:S(2)}, u32[]{:S(2)}) collective-permute-start(bf16[8,64,1024]{2,1,0:T(8,128)(2,1)} %param.21), channel_id=1, source_target_pairs={{0,8},{4,12},{8,0},{12,4},{1,9},{5,13},{9,1},{13,5},{2,10},{6,14},... | collective-permute-start | bytes 3145736 | tf_op jit(solution)/shard_map/ppermute | solution.py:151
  2.9 57.3 %collective-permute-start.4 = (bf16[8,64,1024]{2,1,0:T(8,128)(2,1)}, bf16[8,64,1024]{2,1,0:T(8,128)(2,1)}, u32[]{:S(2)}, u32[]{:S(2)}) collective-permute-start(bf16[8,64,1024]{2,1,0:T(8,128)(2,1)} %param.21), channel_id=1, source_target_pairs={{0,4},{4,0},{8,12},{12,8},{1,5},{5,1},{9,13},{13,9},{2,6},{6,2},{1... | collective-permute-start | bytes 3145736 | tf_op jit(solution)/shard_map/ppermute | solution.py:151
  2.9 68.4 %collective-permute-start.9 = (bf16[8,64,2048]{2,1,0:T(8,128)(2,1)}, bf16[8,64,2048]{2,1,0:T(8,128)(2,1)}, u32[]{:S(2)}, u32[]{:S(2)}) collective-permute-start(bf16[8,64,2048]{2,1,0:T(8,128)(2,1)} %param.22), channel_id=1, source_target_pairs={{0,8},{4,12},{8,0},{12,4},{1,9},{5,13},{9,1},{13,5},{2,10},{6,14},... | collective-permute-start | bytes 6291464 | tf_op jit(solution)/shard_map/ppermute | solution.py:151
  3.8 1.6 %copy-start = (bf16[256,16,2,128]{3,2,1,0:T(2,128)(2,1)S(1)}, bf16[256,16,2,128]{3,2,1,0:T(2,128)(2,1)}, u32[]{:S(2)}) copy-start(bf16[256,16,2,128]{3,2,1,0:T(2,128)(2,1)} %param.15) | copy-start | bytes 6291460
  5.4 1.6 %copy-start.1 = (bf16[256,16,2,128]{3,2,1,0:T(2,128)(2,1)S(1)}, bf16[256,16,2,128]{3,2,1,0:T(2,128)(2,1)}, u32[]{:S(2)}) copy-start(bf16[256,16,2,128]{3,2,1,0:T(2,128)(2,1)} %param.16) | copy-start | bytes 6291460
  7.0 1.0 copy-start.2
  8.0 0.9 copy-start.3
  8.9 0.9 copy-start.4
  9.8 0.7 copy-start.5
  24.7 15.4 %collective-permute-start = (bf16[256,1024]{1,0:T(8,128)(2,1)S(1)}, bf16[256,1024]{1,0:T(8,128)(2,1)}, u32[]{:S(2)}, u32[]{:S(2)}) collective-permute-start(bf16[256,1024]{1,0:T(8,128)(2,1)S(1)} %project.3), channel_id=1, source_target_pairs={{0,2},{2,3},{3,1},{1,0},{4,6},{6,7},{7,5},{5,4},{8,10},{10,11},{11... | collective-permute-start | bytes 1572872 | tf_op jit(solution)/shard_map/ppermute | solution.py:234
  27.8 4.3 %copy-start.8 = (s32[256]{0:T(256)S(1)}, s32[256]{0:T(256)}, u32[]{:S(2)}) copy-start(s32[256]{0:T(256)} %param.24) | copy-start | bytes 3076
  27.8 4.3 %copy-start.9 = (s32[32]{0:T(128)S(1)}, s32[32]{0:T(128)}, u32[]{:S(2)}) copy-start(s32[32]{0:T(128)} %param.23) | copy-start | bytes 388
  30.5 22.9 %collective-permute-start.12 = (bf16[256,1024]{1,0:T(8,128)(2,1)S(1)}, bf16[256,1024]{1,0:T(8,128)(2,1)}, u32[]{:S(2)}, u32[]{:S(2)}) collective-permute-start(bf16[256,1024]{1,0:T(8,128)(2,1)S(1)} %project.5), channel_id=1, source_target_pairs={{0,2},{2,3},{3,1},{1,0},{4,6},{6,7},{7,5},{5,4},{8,10},{10,11},{11... | collective-permute-start | bytes 1572872 | tf_op jit(solution)/shard_map/ppermute | solution.py:234
  32.3 39.1 %collective-permute-start.5 = (bf16[8,64,1024]{2,1,0:T(8,128)(2,1)}, bf16[8,64,1024]{2,1,0:T(8,128)(2,1)}, u32[]{:S(2)}, u32[]{:S(2)}) collective-permute-start(bf16[8,64,1024]{2,1,0:T(8,128)(2,1)} %collective-permute-done.3), channel_id=1, source_target_pairs={{0,4},{4,0},{8,12},{12,8},{1,5},{5,1},{9,13},{13,9},{2,6},{6,2},{1... | collective-permute-start | bytes 3145736 | tf_op jit(solution)/shard_map/ppermute | solution.py:151
  40.0 48.6 %collective-permute-start.10 = (bf16[8,64,2048]{2,1,0:T(8,128)(2,1)}, bf16[8,64,2048]{2,1,0:T(8,128)(2,1)S(1)}, u32[]{:S(2)}, u32[]{:S(2)}) collective-permute-start(bf16[8,64,2048]{2,1,0:T(8,128)(2,1)} %param.22), channel_id=1, source_target_pairs={{0,4},{4,0},{8,12},{12,8},{1,5},{5,1},{9,13},{13,9},{2,6},{6,2},{1... | collective-permute-start | bytes 6291464 | tf_op jit(solution)/shard_map/ppermute | solution.py:151
  55.0 20.0 %collective-permute-start.1 = (bf16[256,1024]{1,0:T(8,128)(2,1)S(1)}, bf16[256,1024]{1,0:T(8,128)(2,1)S(1)}, u32[]{:S(2)}, u32[]{:S(2)}) collective-permute-start(bf16[256,1024]{1,0:T(8,128)(2,1)S(1)} %get-tuple-element.11), channel_id=1, source_target_pairs={{0,2},{2,3},{3,1},{1,0},{4,6},{6,7},{7,5},{5,4},{8,10},{10,11},{11... | collective-permute-start | bytes 1572872 | tf_op jit(solution)/shard_map/ppermute | solution.py:234
  60.2 21.8 %collective-permute-start.13 = (bf16[256,1024]{1,0:T(8,128)(2,1)S(1)}, bf16[256,1024]{1,0:T(8,128)(2,1)S(1)}, u32[]{:S(2)}, u32[]{:S(2)}) collective-permute-start(bf16[256,1024]{1,0:T(8,128)(2,1)S(1)} %get-tuple-element.12), channel_id=1, source_target_pairs={{0,2},{2,3},{3,1},{1,0},{4,6},{6,7},{7,5},{5,4},{8,10},{10,11},{11... | collective-permute-start | bytes 1572872 | tf_op jit(solution)/shard_map/ppermute | solution.py:234
  71.4 20.4 %collective-permute-start.11 = (bf16[8,64,2048]{2,1,0:T(8,128)(2,1)}, bf16[8,64,2048]{2,1,0:T(8,128)(2,1)S(1)}, u32[]{:S(2)}, u32[]{:S(2)}) collective-permute-start(bf16[8,64,2048]{2,1,0:T(8,128)(2,1)} %collective-permute-done.9), channel_id=1, source_target_pairs={{0,4},{4,0},{8,12},{12,8},{1,5},{5,1},{9,13},{13,9},{2,6},{6,2},{1... | collective-permute-start | bytes 6291464 | tf_op jit(solution)/shard_map/ppermute | solution.py:151
  73.1 14.8 %copy-start.6 = (bf16[8,64,2048]{2,1,0:T(8,128)(2,1)S(1)}, bf16[8,64,2048]{2,1,0:T(8,128)(2,1)}, u32[]{:S(2)}) copy-start(bf16[8,64,2048]{2,1,0:T(8,128)(2,1)} %param.22) | copy-start | bytes 6291460
  73.1 11.8 %collective-permute-start.6 = (bf16[256,64]{0,1:T(8,128)(2,1)S(1)}, bf16[256,64]{0,1:T(8,128)(2,1)S(1)}, u32[]{:S(2)}, u32[]{:S(2)}) collective-permute-start(bf16[256,64]{0,1:T(8,128)(2,1)S(1)} %add_convert_fusion.7), channel_id=1, source_target_pairs={{0,1},{1,2},{2,3},{3,0},{4,5},{5,6},{6,7},{7,4},{8,9},{9,10},{10,1... | collective-permute-start | bytes 98312 | tf_op jit(solution)/shard_map/ppermute | solution.py:221
  75.0 11.4 %collective-permute-start.7 = (bf16[256,64]{0,1:T(8,128)(2,1)S(1)}, bf16[256,64]{0,1:T(8,128)(2,1)S(1)}, u32[]{:S(2)}, u32[]{:S(2)}) collective-permute-start(bf16[256,64]{0,1:T(8,128)(2,1)S(1)} %add_convert_fusion.7), channel_id=1, source_target_pairs={{0,2},{1,3},{2,0},{3,1},{4,6},{5,7},{6,4},{7,5},{8,10},{9,11},{10,... | collective-permute-start | bytes 98312 | tf_op jit(solution)/shard_map/ppermute | solution.py:221
  82.0 5.9 %collective-permute-start.8 = (bf16[256,64]{0,1:T(8,128)(2,1)S(1)}, bf16[256,64]{0,1:T(8,128)(2,1)S(1)}, u32[]{:S(2)}, u32[]{:S(2)}) collective-permute-start(bf16[256,64]{0,1:T(8,128)(2,1)S(1)} %add_convert_fusion.7), channel_id=1, source_target_pairs={{0,3},{1,0},{2,1},{3,2},{4,7},{5,4},{6,5},{7,6},{8,11},{9,8},{10,9... | collective-permute-start | bytes 98312 | tf_op jit(solution)/shard_map/ppermute | solution.py:221
  84.9 14.9 %collective-permute-start.14 = (bf16[256,1024]{1,0:T(8,128)(2,1)S(1)}, bf16[256,1024]{1,0:T(8,128)(2,1)S(1)}, u32[]{:S(2)}, u32[]{:S(2)}) collective-permute-start(bf16[256,1024]{1,0:T(8,128)(2,1)S(1)} %get-tuple-element.10), channel_id=1, source_target_pairs={{0,2},{2,3},{3,1},{1,0},{4,6},{6,7},{7,5},{5,4},{8,10},{10,11},{11... | collective-permute-start | bytes 1572872 | tf_op jit(solution)/shard_map/ppermute | solution.py:234
  86.4 22.8 %collective-permute-start.2 = (bf16[256,1024]{1,0:T(8,128)(2,1)S(1)}, bf16[256,1024]{1,0:T(8,128)(2,1)S(1)}, u32[]{:S(2)}, u32[]{:S(2)}) collective-permute-start(bf16[256,1024]{1,0:T(8,128)(2,1)S(1)} %get-tuple-element.9), channel_id=1, source_target_pairs={{0,2},{2,3},{3,1},{1,0},{4,6},{6,7},{7,5},{5,4},{8,10},{10,11},{11... | collective-permute-start | bytes 1572872 | tf_op jit(solution)/shard_map/ppermute | solution.py:234
  91.8 17.4 %copy-start.7 = (bf16[256,2048]{1,0:T(8,128)(2,1)S(1)}, bf16[256,2048]{1,0:T(8,128)(2,1)}, u32[]{:S(2)}) copy-start(bf16[256,2048]{1,0:T(8,128)(2,1)} %param.13) | copy-start | bytes 3145732

commit v2 on v0

v2 whole, which is shorter than its diff:
```python
import functools
import math

import jax
import jax.numpy as jnp
from jax import lax
from jax.experimental import pallas as pl
from jax.experimental.pallas import tpu as pltpu
from jax.sharding import PartitionSpec as P

GROUP = 8
CAP = 64
LANES = 128
MASKED = -1e30
VMEM_LIMIT = 60 * 1024 * 1024
CHAINS = 2
PIECE = 512
SPLIT = 2

VMEM = pl.BlockSpec(memory_space=pltpu.VMEM)
ANY = pl.BlockSpec(memory_space=pl.ANY)
PARAMS = pltpu.CompilerParams(vmem_limit_bytes=VMEM_LIMIT)


def _dot(a, b, left=1, right=0):
    return lax.dot_general(
        a, b, (((left,), (right,)), ((), ())), preferred_element_type=jnp.float32
    )


def _iota(shape, axis):
    return lax.broadcasted_iota(jnp.int32, shape, axis)


def ring_order(count):
    return list(range(0, count, 2)) + list(range(1, count, 2))[::-1]


def column_owner(step):
    count = lax.axis_size("tensor")
    here = lax.axis_index("tensor")
    half = here // 2
    spot = jnp.where(here % 2 == 0, half, count - 1 - half)
    spot = lax.rem(spot - 1 - step + 2 * count, count)
    return jnp.where(2 * spot < count, 2 * spot, 2 * (count - spot) - 1)


class Weights:
    def __init__(self, w_ref, held, sems, first, width):
        depth = w_ref.shape[0] // SPLIT
        self.piece = min(PIECE, width)
        self.held = held
        self.copies = []
        for p in range(width // self.piece):
            at = pl.multiple_of(first + p * self.piece, self.piece)
            self.copies.append(
                [
                    pltpu.make_async_copy(
                        w_ref.at[pl.ds(s * depth, depth), pl.ds(at, self.piece)],
                        held.at[p, pl.ds(s * depth, depth), :],
                        sems.at[p, s],
                    )
                    for s in range(SPLIT)
                ]
            )

    def start(self):
        for piece in self.copies:
            for copy in piece:
                copy.start()

    def products(self, a):
        for p, piece in enumerate(self.copies):
            for copy in piece:
                copy.wait()
            yield pl.ds(p * self.piece, self.piece), _dot(a, self.held[p])

    @staticmethod
    def scratch(depth, width):
        piece = min(PIECE, width)
        count = width // piece
        return [
            pltpu.VMEM((count, depth, piece), jnp.bfloat16),
            pltpu.SemaphoreType.DMA((count, SPLIT)),
        ]


def attend_kernel(
    heads, kv, cache, steps,
    len_ref, q_hbm, k_hbm, v_hbm, nk_hbm, nv_hbm, w_hbm,
    a_ref, out_ref,
    q_ref, k_ref, v_ref, nk_ref, nv_ref, scores_ref, mixed_ref, sems, fresh_sems, w_held, w_sems,
):
    requests = len_ref.shape[1]
    width = q_hbm.shape[1]
    per = requests // steps
    groups = per // GROUP
    group_rows = GROUP * heads
    group_cols = GROUP * cache * kv
    per_kv = heads // kv
    scale = 1.0 / math.sqrt(width)

    def part(kind, step):
        source, target, count = (
            (q_hbm, q_ref, heads),
            (k_hbm, k_ref, cache * kv),
            (v_hbm, v_ref, cache * kv),
        )[kind]
        rows = pl.ds(step * per * count, per * count)
        return pltpu.make_async_copy(source.at[rows, :], target.at[rows, :], sems.at[kind, step])

    fresh = [
        pltpu.make_async_copy(source, target, fresh_sems.at[i])
        for i, (source, target) in enumerate(((nk_hbm, nk_ref), (nv_hbm, nv_ref)))
    ]
    chunk = out_ref.shape[1]
    first = column_owner(0) * (CHAINS * chunk)
    weights = Weights(w_hbm, w_held, w_sems, first, chunk)
    part(0, 0).start()
    part(1, 0).start()
    fresh[0].start()
    part(2, 0).start()
    fresh[1].start()
    for step in range(1, steps):
        for kind in range(3):
            part(kind, step).start()
    weights.start()

    row = _iota((group_rows, group_cols), 0)
    col = _iota((group_rows, group_cols), 1)
    same = (row // heads == col // (cache * kv)) & ((row % heads) // per_kv == col % kv)
    own_bias = jnp.where(same, 0.0, MASKED)
    row = _iota((group_rows, per * kv), 0)
    col = _iota((group_rows, per * kv), 1)
    fresh_kv = (row % heads) // per_kv == col % kv
    fresh_distance = col // kv - row // heads

    counts = len_ref[...].astype(jnp.float32)
    all_groups = requests // GROUP
    of_group = _iota((all_groups, requests), 1) // GROUP == _iota((all_groups, requests), 0)
    counts = jnp.where(of_group, counts, 0.0).astype(jnp.bfloat16)
    spread = _iota((requests, group_cols), 0) % GROUP == _iota((requests, group_cols), 1) // (cache * kv)
    counts = _dot(counts, spread.astype(jnp.bfloat16))
    position = (_iota((all_groups, group_cols), 1) // kv) % cache
    length_bias = jnp.where(position.astype(jnp.float32) < counts, 0.0, MASKED)

    for step in range(steps):
        side = step % 2
        part(0, step).wait()
        part(1, step).wait()
        if step == 0:
            fresh[0].wait()
        q_at = step * per * heads
        k_at = step * per * cache * kv
        f_at = step * per * kv
        for g in range(groups):
            rows = pl.ds(g * group_rows, group_rows)
            scores_ref[side, rows, pl.ds(0, group_cols)] = _dot(
                q_ref[pl.ds(q_at + g * group_rows, group_rows), :],
                k_ref[pl.ds(k_at + g * group_cols, group_cols), :],
                1,
                1,
            )
        scores_ref[side, :, pl.ds(group_cols, per * kv)] = _dot(
            q_ref[pl.ds(q_at, per * heads), :], nk_ref[pl.ds(f_at, per * kv), :], 1, 1
        )
        part(2, step).wait()
        if step == 0:
            fresh[1].wait()
        inverses = []
        weights_cached = []
        weights_fresh = []
        for g in range(groups):
            rows = pl.ds(g * group_rows, group_rows)
            bias = own_bias + length_bias[step * groups + g : step * groups + g + 1, :]
            cached = scores_ref[side, rows, pl.ds(0, group_cols)] * scale + bias
            new = scores_ref[side, rows, pl.ds(group_cols, per * kv)] * scale
            new = jnp.where(fresh_kv & (fresh_distance == g * GROUP), new, MASKED)
            top = jnp.maximum(
                jnp.max(cached, axis=1, keepdims=True), jnp.max(new, axis=1, keepdims=True)
            )
            cached = jnp.exp(cached - top)
            new = jnp.exp(new - top)
            total = jnp.sum(cached, axis=1, keepdims=True) + jnp.sum(new, axis=1, keepdims=True)
            inverse = 1.0 / total
            weights_cached.append((cached * inverse).astype(jnp.bfloat16))
            weights_fresh.append((new * inverse).astype(jnp.bfloat16))
        new = _dot(jnp.concatenate(weights_fresh, axis=0), nv_ref[pl.ds(f_at, per * kv), :])
        for g in range(groups):
            rows = slice(g * group_rows, (g + 1) * group_rows)
            mixed_ref[side, rows, :] = new[rows, :] + _dot(
                weights_cached[g], v_ref[pl.ds(k_at + g * group_cols, group_cols), :]
            )
        for h in range(heads):
            a_ref[pl.ds(step * per, per), pl.ds(h * width, width)] = mixed_ref[
                side, pl.ds(h, per, stride=heads), :
            ].astype(jnp.bfloat16)

    for columns, product in weights.products(a_ref[...]):
        out_ref[:, columns] = product.astype(jnp.bfloat16)


def attend(query, keys, values, new_key, new_value, lengths, weight, chunk):
    requests, heads, width = query.shape
    cache, kv = keys.shape[1], keys.shape[2]
    steps = 4
    per = requests // steps
    columns = GROUP * cache * kv + per * kv
    return pl.pallas_call(
        functools.partial(attend_kernel, heads, kv, cache, steps),
        in_specs=[VMEM] + [ANY] * 6,
        out_specs=[VMEM, VMEM],
        out_shape=[
            jax.ShapeDtypeStruct((requests, heads * width), jnp.bfloat16),
            jax.ShapeDtypeStruct((requests, chunk), jnp.bfloat16),
        ],
        scratch_shapes=[
            pltpu.VMEM((requests * heads, width), jnp.bfloat16),
            pltpu.VMEM((requests * cache * kv, width), jnp.bfloat16),
            pltpu.VMEM((requests * cache * kv, width), jnp.bfloat16),
            pltpu.VMEM((requests * kv, width), jnp.bfloat16),
            pltpu.VMEM((requests * kv, width), jnp.bfloat16),
            pltpu.VMEM((2, per * heads, columns), jnp.float32),
            pltpu.VMEM((2, per * heads, width), jnp.float32),
            pltpu.SemaphoreType.DMA((3, steps)),
            pltpu.SemaphoreType.DMA((2,)),
        ]
        + Weights.scratch(weight.shape[0], chunk),
        compiler_params=PARAMS,
        name="attend",
    )(
        lengths.reshape(1, requests),
        query.reshape(requests * heads, width),
        keys.reshape(requests * cache * kv, width),
        values.reshape(requests * cache * kv, width),
        new_key.reshape(requests * kv, width),
        new_value.reshape(requests * kv, width),
        weight,
    )


def hop_kernel(step, chain, arriving, after, *refs):
    if arriving:
        arrived_ref, *refs = refs
    a_ref, w_hbm, *refs = refs
    out_ref, held, sems = refs[after:]
    chunk = out_ref.shape[1]
    first = column_owner(step) * (CHAINS * chunk) + chain * chunk
    weights = Weights(w_hbm, held, sems, first, chunk)
    weights.start()
    for columns, product in weights.products(a_ref[...]):
        if arriving:
            product = product + arrived_ref[:, columns].astype(jnp.float32)
        out_ref[:, columns] = product.astype(jnp.bfloat16)


def hop(step, chain, arrived, attended, weight, chunk, after=()):
    arriving = arrived is not None
    operands = ([arrived] if arriving else []) + [attended, weight, *after]
    return pl.pallas_call(
        functools.partial(hop_kernel, step, chain, arriving, len(after)),
        in_specs=[VMEM] * (1 + arriving) + [ANY] * (1 + len(after)),
        out_specs=VMEM,
        out_shape=jax.ShapeDtypeStruct((attended.shape[0], chunk), jnp.bfloat16),
        scratch_shapes=Weights.scratch(weight.shape[0], chunk),
        compiler_params=PARAMS,
        name="hop",
    )(*operands)


def route_kernel(replicas, slots, after, *refs):
    a_ref, adapter_ref, placement_ref, *refs = refs
    chosen_ref, *sent_refs = refs[after:]
    requests = adapter_ref.shape[1]
    table = placement_ref.shape[1]
    matches = _iota((table, requests), 0) == adapter_ref[...]
    placed = jnp.broadcast_to(placement_ref[...].astype(jnp.float32), (8, table))
    slot = _dot(placed.astype(jnp.bfloat16), matches.astype(jnp.bfloat16)).astype(jnp.int32)
    slot = slot[0:1, :]
    holder = (slot // slots) ^ lax.axis_index("dp")
    inside = slot % slots
    of_holder = _iota((max(replicas, 8), requests), 0) == holder
    earlier = _iota((requests, requests), 0) < _iota((requests, requests), 1)
    before = _dot(of_holder.astype(jnp.bfloat16), earlier.astype(jnp.bfloat16))
    before = jnp.sum(jnp.where(of_holder, before, 0.0), axis=0, keepdims=True).astype(jnp.int32)
    target = holder * CAP + before
    here = _iota((replicas * CAP, requests), 0) == target
    chosen = here.astype(jnp.bfloat16)
    chosen_ref[...] = chosen
    rows = _dot(chosen, a_ref[...]).astype(jnp.bfloat16)
    inner = jnp.sum(jnp.where(here, inside.astype(jnp.float32), 0.0), axis=1, keepdims=True)
    inner = jnp.broadcast_to(inner, (replicas * CAP, LANES)).astype(jnp.bfloat16)
    width = a_ref.shape[1]
    for r, sent_ref in enumerate(sent_refs):
        sent_ref[:, pl.ds(0, width)] = rows[r * CAP : (r + 1) * CAP, :]
        sent_ref[:, pl.ds(width, LANES)] = inner[r * CAP : (r + 1) * CAP, :]


def route(attended, request_adapter, placement, replicas, slots, after=()):
    requests, width = attended.shape
    return pl.pallas_call(
        functools.partial(route_kernel, replicas, slots, len(after)),
        in_specs=[VMEM] * 3 + [ANY] * len(after),
        out_specs=[VMEM] * (1 + replicas),
        out_shape=[jax.ShapeDtypeStruct((replicas * CAP, requests), jnp.bfloat16)]
        + [jax.ShapeDtypeStruct((CAP, width + LANES), jnp.bfloat16)] * replicas,
        compiler_params=PARAMS,
        name="route",
    )(attended, request_adapter.reshape(1, -1), placement.reshape(1, -1), *after)


def down_kernel(replicas, after, *refs):
    received = refs[:replicas]
    down_ref = refs[replicas]
    mid_ref, inside_ref = refs[replicas + 1 + after :]
    slots, rank, width = down_ref.shape
    rows = jnp.concatenate([r[:, pl.ds(0, width)] for r in received], axis=0)
    inside = jnp.concatenate([r[:, pl.ds(width, LANES)] for r in received], axis=0)
    inside_ref[...] = inside
    projected = _dot(rows, down_ref[...].reshape(slots * rank, width), 1, 1)
    lane_slot = _iota(projected.shape, 1) // rank
    mine = lane_slot == inside[:, 0:1].astype(jnp.int32)
    projected = jnp.where(mine, projected, 0.0).astype(jnp.bfloat16)
    fold = _iota((slots * rank, LANES), 0) % rank == _iota((slots * rank, LANES), 1)
    mid_ref[...] = _dot(projected, fold.astype(jnp.bfloat16)).astype(jnp.bfloat16)


def down(received, slot_down_weight, after=()):
    replicas = len(received)
    rows = replicas * CAP
    return pl.pallas_call(
        functools.partial(down_kernel, replicas, len(after)),
        in_specs=[VMEM] * (replicas + 1) + [ANY] * len(after),
        out_specs=[VMEM, VMEM],
        out_shape=[jax.ShapeDtypeStruct((rows, LANES), jnp.bfloat16)] * 2,
        compiler_params=PARAMS,
        name="down",
    )(*received, slot_down_weight, *after)


def up_kernel(parts, after, *refs):
    mids = refs[:parts]
    inside_ref, up_ref = refs[parts : parts + 2]
    out_refs = refs[parts + 2 + after :]
    slots, rank, width = up_ref.shape
    mid = mids[0][...].astype(jnp.float32)
    for m in mids[1:]:
        mid = mid + m[...].astype(jnp.float32)
    spread = _iota((LANES, slots * rank), 1) % rank == _iota((LANES, slots * rank), 0)
    wide = _dot(mid.astype(jnp.bfloat16), spread.astype(jnp.bfloat16))
    mine = _iota(wide.shape, 1) // rank == inside_ref[:, 0:1].astype(jnp.int32)
    wide = jnp.where(mine, wide, 0.0).astype(jnp.bfloat16)
    delta = _dot(wide, up_ref[...].reshape(slots * rank, width)).astype(jnp.bfloat16)
    for r, out_ref in enumerate(out_refs):
        out_ref[...] = delta[r * CAP : (r + 1) * CAP, :]


def up(mids, inside, slot_up_weight, after=()):
    rows = inside.shape[0]
    replicas = rows // CAP
    width = slot_up_weight.shape[2]
    return pl.pallas_call(
        functools.partial(up_kernel, len(mids), len(after)),
        in_specs=[VMEM] * (len(mids) + 2) + [ANY] * len(after),
        out_specs=[VMEM] * replicas,
        out_shape=[jax.ShapeDtypeStruct((CAP, width), jnp.bfloat16)] * replicas,
        compiler_params=PARAMS,
        name="up",
    )(*mids, inside, slot_up_weight, *after)


def settle_kernel(step, replicas, after, *refs):
    returned = refs[:replicas]
    chosen_ref, a_ref, residual_ref, w_hbm = refs[replicas : replicas + 4]
    out_ref, held, sems = refs[replicas + 4 + after :]
    width = out_ref.shape[1]
    weights = Weights(w_hbm, held, sems, column_owner(step) * width, width)
    weights.start()
    rows = jnp.concatenate([r[...] for r in returned], axis=0)
    delta = _dot(chosen_ref[...], rows, 0, 0)
    for columns, product in weights.products(a_ref[...]):
        own = residual_ref[:, columns].astype(jnp.float32) + product
        out_ref[:, columns] = own + delta[:, columns.start : columns.start + columns.size]


def settle(step, returned, chosen, attended, residual, weight, after=()):
    replicas = len(returned)
    return pl.pallas_call(
        functools.partial(settle_kernel, step, replicas, len(after)),
        in_specs=[VMEM] * (replicas + 3) + [ANY] * (1 + len(after)),
        out_specs=VMEM,
        out_shape=jax.ShapeDtypeStruct(residual.shape, jnp.float32),
        scratch_shapes=Weights.scratch(weight.shape[0], residual.shape[1]),
        compiler_params=PARAMS,
        name="settle",
    )(*returned, chosen, attended, residual, weight, *after)


def finish_kernel(arrived_ref, settled_ref, *refs):
    refs[-1][...] = (settled_ref[...] + arrived_ref[...].astype(jnp.float32)).astype(jnp.bfloat16)


def finish(chain, arrived, settled, earlier):
    rows, chunk = arrived.shape
    piece = min(PIECE, chunk)
    count = chunk // piece
    operands = [arrived, settled] + ([earlier] if earlier is not None else [])
    return pl.pallas_call(
        finish_kernel,
        grid=(count,),
        in_specs=[
            pl.BlockSpec((rows, piece), lambda i: (0, i)),
            pl.BlockSpec((rows, piece), lambda i: (0, chain * count + i)),
        ]
        + ([ANY] if earlier is not None else []),
        out_specs=pl.BlockSpec((rows, piece), lambda i: (0, chain * count + i)),
        out_shape=jax.ShapeDtypeStruct(settled.shape, jnp.bfloat16),
        input_output_aliases={2: 0} if earlier is not None else {},
        compiler_params=PARAMS,
        name="finish",
    )(*operands)


def per_device(
    residual,
    query,
    cached_key_rows,
    cached_value_rows,
    new_token_key,
    new_token_value,
    lengths,
    output_weight,
    slot_down_weight,
    slot_up_weight,
    placement,
    request_adapter,
):
    count = lax.axis_size("tensor")
    replicas = lax.axis_size("dp")
    chunk = residual.shape[1] // CHAINS
    order = ring_order(count)
    ring = [(order[p], order[(p + 1) % count]) for p in range(count)]

    def forward(x):
        return lax.ppermute(x, "tensor", ring)

    def exchange(blocks):
        moved = [
            lax.ppermute(blocks[r], "dp", [(i, i ^ r) for i in range(replicas)])
            for r in range(1, replicas)
        ]
        return [blocks[0]] + moved

    attended, first = attend(
        query, cached_key_rows, cached_value_rows, new_token_key, new_token_value, lengths,
        output_weight, chunk,
    )
    travelling = [first] + [
        hop(0, c, None, attended, output_weight, chunk) for c in range(1, CHAINS)
    ]
    chosen, *leaving = route(
        attended, request_adapter, placement, replicas, slot_down_weight.shape[0],
        after=travelling[1:],
    )
    rows_here = exchange(leaving)

    latest = chosen
    stage = 0
    for step in range(1, count - 1):
        for c in range(CHAINS):
            arrived = forward(travelling[c])
            travelling[c] = hop(step, c, arrived, attended, output_weight, chunk, after=[latest])
            latest = travelling[c]
            if stage == 1:
                mid, inside = down(rows_here, slot_down_weight, after=[latest])
                latest = mid
            if stage == 2:
                mids = [mid] + [
                    lax.ppermute(mid, "tensor", [(i, (i + k) % count) for i in range(count)])
                    for k in range(1, count)
                ]
                deltas = up(mids, inside, slot_up_weight, after=[latest])
                latest = deltas[0]
            stage += 1
    returned = exchange(deltas)
    settled = settle(
        count - 1, returned, chosen, attended, residual, output_weight, after=[latest]
    )
    out = None
    for c in range(CHAINS):
        out = finish(c, forward(travelling[c]), settled, out)
    return out


def solution(mesh):
    placed = (
        P(("parts", "dp"), "tensor"),
        P(("parts", "dp"), "tensor", None),
        P(("parts", "dp"), None, "tensor", None),
        P(("parts", "dp"), None, "tensor", None),
        P(("parts", "dp"), "tensor", None),
        P(("parts", "dp"), "tensor", None),
        P(("parts", "dp")),
        P("tensor", None),
        P("dp", None, "tensor"),
        P("dp", None, "tensor"),
        P("parts"),
        P(("parts", "dp")),
    )
    return jax.shard_map(
        per_device,
        mesh=mesh,
        in_specs=placed,
        out_specs=P(("parts", "dp"), "tensor"),
        check_vma=False,
    )
```

time: 133 us -> 105 us (0.79)
  Pallas kernels: 0 us -> 48.5 us
  matrix products: 31.2 us -> 0 us
  waiting for transfers between devices: 55.5 us -> 26.7 us
  starting transfers between devices: 0.09 us -> 22 us
  blocking collectives: 20.7 us -> 0 us
  between operations: 15 us -> 0.17 us
  other arithmetic: 4.42 us -> 0 us
  local copies, waits for them, and re-layouts: 5.37 us -> 6.83 us
    pallas_call x0 -> x12, Pallas kernels: none -> 48.5 us  [the longest x5 20.6 us: hop(): pl.pallas_call(functools.partial(hop_kernel, step, chain, arriving, len(a...]
    reduce_scatter x1 -> x0, waiting for transfers between devices: 46.4 us -> none  [per_device(): lax.psum_scatter(partial_out.astype(jnp.bfloat16), 'tensor', scatter_dime...]
    dot_general x6 -> x0, matrix products: 31.2 us -> none  [the longest x1 11.9 us: per_device(): jnp.dot(attended_output, output_weight, preferred_element_type=jnp.float32)]
    ppermute x0 -> x15, waiting for transfers between devices: none -> 26.7 us  [the longest x6 19.1 us: exchange(): lax.ppermute(blocks[r], 'dp', [(i, i ^ r) for i in range(replicas)])]
    ppermute x0 -> x15, starting transfers between devices: none -> 22 us  [the longest x6 15.6 us: forward(): return lax.ppermute(x, 'tensor', ring)]
    psum x1 -> x0, blocking collectives: 20.7 us -> none  [per_device(): rank_mid = lax.psum(mid_part.astype(jnp.bfloat16), 'tensor')]
    all_gather x2 -> x0, waiting for transfers between devices: 7.64 us -> none  [the longest x1 7.64 us: per_device(): partial_piece = lax.all_gather(slot_down_weight, 'dp', axis=0, tiled=True)]
    unnamed x12 -> x42, local copies, waits for them, and re-layouts: 0.03 us -> 6.83 us
  transfers between devices with their start and end apart: 3 -> 15, of which waited for: 2 -> 6; matrix products, arithmetic and copies ran while one was open for 26% -> 0% of each run, Pallas kernels for 0% -> 36%
where the time goes in v2:
time: 105 us; the launch traced here: 104 us
  Pallas kernels  48.5 us (46%)
  waiting for transfers between devices  26.7 us (25%)
  starting transfers between devices  22 us (21%)
  local copies, waits for them, and re-layouts  6.83 us (7%)
    pallas_call x5, Pallas kernels, hop(): pl.pallas_call(functools.partial(hop_kernel, step, chain, arriving, len(a...  20.6 us
    ppermute x6, waiting for transfers between devices, exchange(): lax.ppermute(blocks[r], 'dp', [(i, i ^ r) for i in range(replicas)])  19.1 us
    ppermute x6, starting transfers between devices, forward(): return lax.ppermute(x, 'tensor', ring)  15.6 us
    pallas_call x1, Pallas kernels, attend(): pl.pallas_call(functools.partial(attend_kernel, heads, kv, cache, steps),...  8.79 us
    ppermute x6, waiting for transfers between devices, forward(): return lax.ppermute(x, 'tensor', ring)  7.56 us
    unnamed x42, local copies, waits for them, and re-layouts  6.83 us
    pallas_call x1, Pallas kernels, settle(): pl.pallas_call(functools.partial(settle_kernel, step, replicas, len(after...  6.16 us
    pallas_call x2, Pallas kernels, finish(): pl.pallas_call(finish_kernel, grid=(count,), in_specs=[pl.BlockSpec((rows...  4.22 us
  transfers between devices with their start and end apart: 15, of which 6 were waited for; matrix products, arithmetic and copies ran while one was open for 0% of the time, Pallas kernels for 36%

profile of v2, /device:TPU:0, one launch (start us, length us, event | category | flops | bytes accessed | tf_op | source)
XLA Modules:
  0.0 104.2 jit_solution(17551817824130829730)
XLA Ops:
  0.0 8.8 %attend.1 = (bf16[256,1024]{1,0:T(8,128)(2,1)}, bf16[256,1024]{1,0:T(8,128)(2,1)}) custom-call(s32[1,256]{1,0:T(1,128)} %bitcast.13, bf16[2048,128]{1,0:T(8,128)(2,1)} %bitcast.10, bf16[8192,128]{1,0:T(8,128)(2,1)} %bitcast.8, bf16[8192,128]{1,0:T(8,128)(2,1)} %bitcast.9, bf16[512,128]{1,0:T(8,128)(2,1)} %bitcast.11, bf16[512,128]{1,0:T(8,128)(2,1)} %bitcast.12, ...), custom_call_target="tpu_custom_call" | custom-call | tf_op jit(solution)/shard_map/attend/pallas_call | solution.py:209
  8.8 4.1 %collective-permute-start.1 = (bf16[256,1024]{1,0:T(8,128)(2,1)}, bf16[256,1024]{1,0:T(8,128)(2,1)S(1)}, u32[]{:S(2)}, u32[]{:S(2)}) collective-permute-start(bf16[256,1024]{1,0:T(8,128)(2,1)} %get-tuple-element.19), channel_id=1, source_target_pairs={{0,2},{2,3},{3,1},{1,0},{4,6},{6,7},{7,5},{5,4},{8,10},{10,11},{11... | collective-permute-start | bytes 1572872 | tf_op jit(solution)/shard_map/ppermute | solution.py:445
  12.9 4.0 %hop.5.refs_3_ = bf16[256,1024]{1,0:T(8,128)(2,1)} custom-call(bf16[256,1024]{1,0:T(8,128)(2,1)} %get-tuple-element.18.refs_0_.refs_1_.refs_5_, bf16[1024,8192]{1,0:T(8,128)(2,1)} %refs_7_.1), custom_call_target="tpu_custom_call" | custom-call | tf_op jit(solution)/shard_map/hop/pallas_call | solution.py:260
  16.9 1.6 %collective-permute-start = (bf16[256,1024]{1,0:T(8,128)(2,1)}, bf16[256,1024]{1,0:T(8,128)(2,1)S(1)}, u32[]{:S(2)}, u32[]{:S(2)}) collective-permute-start(bf16[256,1024]{1,0:T(8,128)(2,1)} %hop.5.refs_3_), channel_id=1, source_target_pairs={{0,2},{2,3},{3,1},{1,0},{4,6},{6,7},{7,5},{5,4},{8,10},{10,11},{11... | collective-permute-start | bytes 1572872 | tf_op jit(solution)/shard_map/ppermute | solution.py:445
  18.5 2.4 %route.1 = (bf16[256,256]{1,0:T(8,128)(2,1)}, bf16[64,1152]{1,0:T(8,128)(2,1)}, bf16[64,1152]{1,0:T(8,128)(2,1)}, bf16[64,1152]{1,0:T(8,128)(2,1)}, bf16[64,1152]{1,0:T(8,128)(2,1)}) custom-call(bf16[256,1024]{1,0:T(8,128)(2,1)} %get-tuple-element.18.refs_0_.refs_1_.refs_5_, s32[1,256]{1,0:T(1,128)} %bitcast.14, s32[1,32]{1,0:T(1,128)} %bitcast.15, ...), custom_call_target="tpu_custom_call" | custom-call | tf_op jit(solution)/shard_map/route/pallas_call | solution.py:301
  20.9 4.6 %collective-permute-done.1.refs_0_ = bf16[256,1024]{1,0:T(8,128)(2,1)S(1)} collective-permute-done((bf16[256,1024]{1,0:T(8,128)(2,1)}, bf16[256,1024]{1,0:T(8,128)(2,1)S(1)}, u32[]{:S(2)}, u32[]{:S(2)}) %collective-permute-start.1) | collective-permute-done | bytes 524320 | tf_op jit(solution)/shard_map/ppermute | solution.py:445
  25.5 0.8 copy-done.5
  26.3 4.2 %hop.6.refs_3_ = bf16[256,1024]{1,0:T(8,128)(2,1)} custom-call(bf16[256,1024]{1,0:T(8,128)(2,1)} %copy-done.5, bf16[256,1024]{1,0:T(8,128)(2,1)} %get-tuple-element.18.refs_0_.refs_1_.refs_5_, bf16[1024,8192]{1,0:T(8,128)(2,1)} %refs_7_.1, bf16[256,256]{1,0:T(8,128)(2,1)} %get-tuple-element.20.refs_3_.refs_4_), custom_call_target="tpu_custom_call" | custom-call | tf_op jit(solution)/shard_map/hop/pallas_call | solution.py:260
  30.5 3.3 %collective-permute-start.9 = (bf16[256,1024]{1,0:T(8,128)(2,1)}, bf16[256,1024]{1,0:T(8,128)(2,1)S(1)}, u32[]{:S(2)}, u32[]{:S(2)}) collective-permute-start(bf16[256,1024]{1,0:T(8,128)(2,1)} %hop.6.refs_3_), channel_id=1, source_target_pairs={{0,2},{2,3},{3,1},{1,0},{4,6},{6,7},{7,5},{5,4},{8,10},{10,11},{11... | collective-permute-start | bytes 1572872 | tf_op jit(solution)/shard_map/ppermute | solution.py:445
  33.9 2.9 %collective-permute-done.refs_0_ = bf16[256,1024]{1,0:T(8,128)(2,1)S(1)} collective-permute-done((bf16[256,1024]{1,0:T(8,128)(2,1)}, bf16[256,1024]{1,0:T(8,128)(2,1)S(1)}, u32[]{:S(2)}, u32[]{:S(2)}) %collective-permute-start) | collective-permute-done | bytes 524320 | tf_op jit(solution)/shard_map/ppermute | solution.py:445
  37.6 4.1 %hop.7.refs_5_ = bf16[256,1024]{1,0:T(8,128)(2,1)} custom-call(bf16[256,1024]{1,0:T(8,128)(2,1)} %copy-done.4, bf16[256,1024]{1,0:T(8,128)(2,1)} %get-tuple-element.18.refs_0_.refs_1_.refs_5_, bf16[1024,8192]{1,0:T(8,128)(2,1)} %refs_7_.1, bf16[256,1024]{1,0:T(8,128)(2,1)} %hop.6.refs_3_), custom_call_target="tpu_custom_call" | custom-call | tf_op jit(solution)/shard_map/hop/pallas_call | solution.py:260
  41.7 3.3 %collective-permute-start.2 = (bf16[256,1024]{1,0:T(8,128)(2,1)}, bf16[256,1024]{1,0:T(8,128)(2,1)S(1)}, u32[]{:S(2)}, u32[]{:S(2)}) collective-permute-start(bf16[256,1024]{1,0:T(8,128)(2,1)} %hop.7.refs_5_), channel_id=1, source_target_pairs={{0,2},{2,3},{3,1},{1,0},{4,6},{6,7},{7,5},{5,4},{8,10},{10,11},{11... | collective-permute-start | bytes 1572872 | tf_op jit(solution)/shard_map/ppermute | solution.py:445
  45.0 1.6 %collective-permute-start.4 = (bf16[64,1152]{1,0:T(8,128)(2,1)S(1)}, bf16[64,1152]{1,0:T(8,128)(2,1)S(1)}, u32[]{:S(2)}, u32[]{:S(2)}) collective-permute-start(bf16[64,1152]{1,0:T(8,128)(2,1)S(1)} %copy-done.19), channel_id=1, source_target_pairs={{0,8},{4,12},{8,0},{12,4},{1,9},{5,13},{9,1},{13,5},{2,10},{6,14},... | collective-permute-start | bytes 442376 | tf_op jit(solution)/shard_map/ppermute | solution.py:449
  46.9 4.9 %collective-permute-done.4.refs_2_ = bf16[64,1152]{1,0:T(8,128)(2,1)S(1)} collective-permute-done((bf16[64,1152]{1,0:T(8,128)(2,1)S(1)}, bf16[64,1152]{1,0:T(8,128)(2,1)S(1)}, u32[]{:S(2)}, u32[]{:S(2)}) %collective-permute-start.4) | collective-permute-done | bytes 147488 | tf_op jit(solution)/shard_map/ppermute | solution.py:449
  51.8 2.2 %collective-permute-done.5.refs_3_ = bf16[64,1152]{1,0:T(8,128)(2,1)S(1)} collective-permute-done((bf16[64,1152]{1,0:T(8,128)(2,1)S(1)}, bf16[64,1152]{1,0:T(8,128)(2,1)S(1)}, u32[]{:S(2)}, u32[]{:S(2)}) %collective-permute-start.5) | collective-permute-done | bytes 147488 | tf_op jit(solution)/shard_map/ppermute | solution.py:449
  54.6 2.8 %down.1 = (bf16[256,128]{1,0:T(8,128)(2,1)}, bf16[256,128]{1,0:T(8,128)(2,1)}) custom-call(bf16[64,1152]{1,0:T(8,128)(2,1)} %get-tuple-element.21.refs_0_, bf16[64,1152]{1,0:T(8,128)(2,1)} %copy-done.9, bf16[64,1152]{1,0:T(8,128)(2,1)} %copy-done.10, bf16[64,1152]{1,0:T(8,128)(2,1)} %copy-done.11, bf16[8,64,1024]{2,1,0:T(8,128)(2,1)} %refs_4_.1, ...), custom_call_target="tpu_custom_call" | custom-call | tf_op jit(solution)/shard_map/down/pallas_call | solution.py:331
  57.4 1.3 %collective-permute-start.8 = (bf16[256,128]{1,0:T(8,128)(2,1)}, bf16[256,128]{1,0:T(8,128)(2,1)S(1)}, u32[]{:S(2)}, u32[]{:S(2)}) collective-permute-start(bf16[256,128]{1,0:T(8,128)(2,1)} %get-tuple-element.25.refs_3_.refs_0_), channel_id=1, source_target_pairs={{0,3},{1,0},{2,1},{3,2},{4,7},{5,4},{6,5},{7,6},{8,11},{9,8},{10,9... | collective-permute-start | bytes 196616 | tf_op jit(solution)/shard_map/ppermute | solution.py:479
  58.8 1.3 %collective-permute-start.6 = (bf16[256,128]{1,0:T(8,128)(2,1)}, bf16[256,128]{1,0:T(8,128)(2,1)S(1)}, u32[]{:S(2)}, u32[]{:S(2)}) collective-permute-start(bf16[256,128]{1,0:T(8,128)(2,1)} %get-tuple-element.25.refs_3_.refs_0_), channel_id=1, source_target_pairs={{0,1},{1,2},{2,3},{3,0},{4,5},{5,6},{6,7},{7,4},{8,9},{9,10},{10,1... | collective-permute-start | bytes 196616 | tf_op jit(solution)/shard_map/ppermute | solution.py:479
  60.1 0.8 copy-done.2
  60.9 4.1 %hop.8.refs_6_ = bf16[256,1024]{1,0:T(8,128)(2,1)} custom-call(bf16[256,1024]{1,0:T(8,128)(2,1)} %copy-done.2, bf16[256,1024]{1,0:T(8,128)(2,1)} %get-tuple-element.18.refs_0_.refs_1_.refs_5_, bf16[1024,8192]{1,0:T(8,128)(2,1)} %refs_7_.1, bf16[256,128]{1,0:T(8,128)(2,1)} %get-tuple-element.25.refs_3_.refs_0_), custom_call_target="tpu_custom_call" | custom-call | tf_op jit(solution)/shard_map/hop/pallas_call | solution.py:260
  65.1 2.3 %collective-permute-start.14 = (bf16[256,1024]{1,0:T(8,128)(2,1)}, bf16[256,1024]{1,0:T(8,128)(2,1)S(1)}, u32[]{:S(2)}, u32[]{:S(2)}) collective-permute-start(bf16[256,1024]{1,0:T(8,128)(2,1)} %hop.8.refs_6_), channel_id=1, source_target_pairs={{0,2},{2,3},{3,1},{1,0},{4,6},{6,7},{7,5},{5,4},{8,10},{10,11},{11... | collective-permute-start | bytes 1572872 | tf_op jit(solution)/shard_map/ppermute | solution.py:445
  68.1 3.6 %up.1 = (bf16[64,2048]{1,0:T(8,128)(2,1)}, bf16[64,2048]{1,0:T(8,128)(2,1)}, bf16[64,2048]{1,0:T(8,128)(2,1)}, bf16[64,2048]{1,0:T(8,128)(2,1)}) custom-call(bf16[256,128]{1,0:T(8,128)(2,1)} %get-tuple-element.25.refs_3_.refs_0_, bf16[256,128]{1,0:T(8,128)(2,1)} %copy-done.14, bf16[256,128]{1,0:T(8,128)(2,1)} %copy-done.13, bf16[256,128]{1,0:T(8,128)(2,1)} %copy-done.12, ...), custom_call_target="tpu_custom_call" | custom-call | tf_op jit(solution)/shard_map/up/pallas_call | solution.py:362
  72.4 4.2 %hop.9.refs_8_ = bf16[256,1024]{1,0:T(8,128)(2,1)} custom-call(bf16[256,1024]{1,0:T(8,128)(2,1)} %copy-done, bf16[256,1024]{1,0:T(8,128)(2,1)} %get-tuple-element.18.refs_0_.refs_1_.refs_5_, bf16[1024,8192]{1,0:T(8,128)(2,1)} %refs_7_.1, bf16[64,2048]{1,0:T(8,128)(2,1)} %get-tuple-element.27.refs_3_.refs_0_), custom_call_target="tpu_custom_call" | custom-call | tf_op jit(solution)/shard_map/hop/pallas_call | solution.py:260
  76.7 0.9 collective-permute-start.10
  77.5 1.6 %collective-permute-start.12 = (bf16[64,2048]{1,0:T(8,128)(2,1)S(1)}, bf16[64,2048]{1,0:T(8,128)(2,1)S(1)}, u32[]{:S(2)}, u32[]{:S(2)}) collective-permute-start(bf16[64,2048]{1,0:T(8,128)(2,1)S(1)} %copy-done.16), channel_id=1, source_target_pairs={{0,8},{4,12},{8,0},{12,4},{1,9},{5,13},{9,1},{13,5},{2,10},{6,14},... | collective-permute-start | bytes 786440 | tf_op jit(solution)/shard_map/ppermute | solution.py:449
  79.4 7.3 %collective-permute-done.12.refs_2_ = bf16[64,2048]{1,0:T(8,128)(2,1)S(1)} collective-permute-done((bf16[64,2048]{1,0:T(8,128)(2,1)S(1)}, bf16[64,2048]{1,0:T(8,128)(2,1)S(1)}, u32[]{:S(2)}, u32[]{:S(2)}) %collective-permute-start.12) | collective-permute-done | bytes 262176 | tf_op jit(solution)/shard_map/ppermute | solution.py:449
  86.7 4.7 %collective-permute-done.13.refs_3_ = bf16[64,2048]{1,0:T(8,128)(2,1)S(1)} collective-permute-done((bf16[64,2048]{1,0:T(8,128)(2,1)S(1)}, bf16[64,2048]{1,0:T(8,128)(2,1)S(1)}, u32[]{:S(2)}, u32[]{:S(2)}) %collective-permute-start.13) | collective-permute-done | bytes 262176 | tf_op jit(solution)/shard_map/ppermute | solution.py:449
  92.1 6.2 %settle.1.settled_ref = f32[256,2048]{1,0:T(8,128)} custom-call(bf16[64,2048]{1,0:T(8,128)(2,1)} %get-tuple-element.27.refs_3_.refs_0_, bf16[64,2048]{1,0:T(8,128)(2,1)} %copy-done.6, bf16[64,2048]{1,0:T(8,128)(2,1)} %copy-done.7, bf16[64,2048]{1,0:T(8,128)(2,1)} %copy-done.8, bf16[256,256]{1,0:T(8,128)(2,1)} %get-tuple-element.20.refs_3_.refs_4_, ...), custom_call_target="tpu_custom_call" | custom-call | tf_op jit(solution)/shard_map/settle/pallas_call | solution.py:388
  98.3 0.8 copy-done.1
  99.1 2.1 %finish.2.refs_0_ = bf16[256,2048]{1,0:T(8,128)(2,1)} custom-call(bf16[256,1024]{1,0:T(8,128)(2,1)} %copy-done.1, f32[256,2048]{1,0:T(8,128)} %settle.1.settled_ref), custom_call_target="tpu_custom_call" | custom-call | tf_op jit(solution)/shard_map/finish/pallas_call | solution.py:408
  101.2 0.8 copy-done.3
  102.0 2.1 %finish.3 = bf16[256,2048]{1,0:T(8,128)(2,1)} custom-call(bf16[256,1024]{1,0:T(8,128)(2,1)} %copy-done.3, f32[256,2048]{1,0:T(8,128)} %settle.1.settled_ref, bf16[256,2048]{1,0:T(8,128)(2,1)} %finish.2.refs_0_), custom_call_target="tpu_custom_call", output_to_operand_aliasing={{}: (2, {})} | custom-call | tf_op jit(solution)/shard_map/finish/pallas_call | solution.py:408
  (52 shorter events, 4.2 us)
Async XLA Ops:
  8.8 16.7 %collective-permute-start.1 = (bf16[256,1024]{1,0:T(8,128)(2,1)}, bf16[256,1024]{1,0:T(8,128)(2,1)S(1)}, u32[]{:S(2)}, u32[]{:S(2)}) collective-permute-start(bf16[256,1024]{1,0:T(8,128)(2,1)} %get-tuple-element.19), channel_id=1, source_target_pairs={{0,2},{2,3},{3,1},{1,0},{4,6},{6,7},{7,5},{5,4},{8,10},{10,11},{11... | collective-permute-start | bytes 1572872 | tf_op jit(solution)/shard_map/ppermute | solution.py:445
  16.9 19.9 %collective-permute-start = (bf16[256,1024]{1,0:T(8,128)(2,1)}, bf16[256,1024]{1,0:T(8,128)(2,1)S(1)}, u32[]{:S(2)}, u32[]{:S(2)}) collective-permute-start(bf16[256,1024]{1,0:T(8,128)(2,1)} %hop.5.refs_3_), channel_id=1, source_target_pairs={{0,2},{2,3},{3,1},{1,0},{4,6},{6,7},{7,5},{5,4},{8,10},{10,11},{11... | collective-permute-start | bytes 1572872 | tf_op jit(solution)/shard_map/ppermute | solution.py:445
  25.5 0.8 copy-start.5
  30.5 14.5 %copy-start.20 = (bf16[64,1152]{1,0:T(8,128)(2,1)S(1)}, bf16[64,1152]{1,0:T(8,128)(2,1)}, u32[]{:S(2)}) copy-start(bf16[64,1152]{1,0:T(8,128)(2,1)} %get-tuple-element.22) | copy-start | bytes 442372
  30.5 14.5 %copy-start.19 = (bf16[64,1152]{1,0:T(8,128)(2,1)S(1)}, bf16[64,1152]{1,0:T(8,128)(2,1)}, u32[]{:S(2)}) copy-start(bf16[64,1152]{1,0:T(8,128)(2,1)} %get-tuple-element.23) | copy-start | bytes 442372
  30.5 16.1 %copy-start.18 = (bf16[64,1152]{1,0:T(8,128)(2,1)S(1)}, bf16[64,1152]{1,0:T(8,128)(2,1)}, u32[]{:S(2)}) copy-start(bf16[64,1152]{1,0:T(8,128)(2,1)} %get-tuple-element.24) | copy-start | bytes 442372
  30.5 29.6 %collective-permute-start.9 = (bf16[256,1024]{1,0:T(8,128)(2,1)}, bf16[256,1024]{1,0:T(8,128)(2,1)S(1)}, u32[]{:S(2)}, u32[]{:S(2)}) collective-permute-start(bf16[256,1024]{1,0:T(8,128)(2,1)} %hop.6.refs_3_), channel_id=1, source_target_pairs={{0,2},{2,3},{3,1},{1,0},{4,6},{6,7},{7,5},{5,4},{8,10},{10,11},{11... | collective-permute-start | bytes 1572872 | tf_op jit(solution)/shard_map/ppermute | solution.py:445
  36.8 0.8 copy-start.4
  41.7 29.9 %collective-permute-start.2 = (bf16[256,1024]{1,0:T(8,128)(2,1)}, bf16[256,1024]{1,0:T(8,128)(2,1)S(1)}, u32[]{:S(2)}, u32[]{:S(2)}) collective-permute-start(bf16[256,1024]{1,0:T(8,128)(2,1)} %hop.7.refs_5_), channel_id=1, source_target_pairs={{0,2},{2,3},{3,1},{1,0},{4,6},{6,7},{7,5},{5,4},{8,10},{10,11},{11... | collective-permute-start | bytes 1572872 | tf_op jit(solution)/shard_map/ppermute | solution.py:445
  45.0 1.9 %collective-permute-start.3 = (bf16[64,1152]{1,0:T(8,128)(2,1)S(1)}, bf16[64,1152]{1,0:T(8,128)(2,1)S(1)}, u32[]{:S(2)}, u32[]{:S(2)}) collective-permute-start(bf16[64,1152]{1,0:T(8,128)(2,1)S(1)} %copy-done.20), channel_id=1, source_target_pairs={{0,4},{4,0},{8,12},{12,8},{1,5},{5,1},{9,13},{13,9},{2,6},{6,2},{1... | collective-permute-start | bytes 442376 | tf_op jit(solution)/shard_map/ppermute | solution.py:449
  45.0 6.7 %collective-permute-start.4 = (bf16[64,1152]{1,0:T(8,128)(2,1)S(1)}, bf16[64,1152]{1,0:T(8,128)(2,1)S(1)}, u32[]{:S(2)}, u32[]{:S(2)}) collective-permute-start(bf16[64,1152]{1,0:T(8,128)(2,1)S(1)} %copy-done.19), channel_id=1, source_target_pairs={{0,8},{4,12},{8,0},{12,4},{1,9},{5,13},{9,1},{13,5},{2,10},{6,14},... | collective-permute-start | bytes 442376 | tf_op jit(solution)/shard_map/ppermute | solution.py:449
  46.6 7.4 %collective-permute-start.5 = (bf16[64,1152]{1,0:T(8,128)(2,1)S(1)}, bf16[64,1152]{1,0:T(8,128)(2,1)S(1)}, u32[]{:S(2)}, u32[]{:S(2)}) collective-permute-start(bf16[64,1152]{1,0:T(8,128)(2,1)S(1)} %copy-done.18), channel_id=1, source_target_pairs={{0,12},{4,8},{8,4},{12,0},{1,13},{5,9},{9,5},{13,1},{2,14},{6,10},... | collective-permute-start | bytes 442376 | tf_op jit(solution)/shard_map/ppermute | solution.py:449
  46.9 7.1 %copy-start.9 = (bf16[64,1152]{1,0:T(8,128)(2,1)}, bf16[64,1152]{1,0:T(8,128)(2,1)S(1)}, u32[]{:S(2)}) copy-start(bf16[64,1152]{1,0:T(8,128)(2,1)S(1)} %collective-permute-done.3.refs_1_) | copy-start | bytes 442372
  51.8 2.2 %copy-start.10 = (bf16[64,1152]{1,0:T(8,128)(2,1)}, bf16[64,1152]{1,0:T(8,128)(2,1)S(1)}, u32[]{:S(2)}) copy-start(bf16[64,1152]{1,0:T(8,128)(2,1)S(1)} %collective-permute-done.4.refs_2_) | copy-start | bytes 442372
  57.4 10.0 %collective-permute-start.8 = (bf16[256,128]{1,0:T(8,128)(2,1)}, bf16[256,128]{1,0:T(8,128)(2,1)S(1)}, u32[]{:S(2)}, u32[]{:S(2)}) collective-permute-start(bf16[256,128]{1,0:T(8,128)(2,1)} %get-tuple-element.25.refs_3_.refs_0_), channel_id=1, source_target_pairs={{0,3},{1,0},{2,1},{3,2},{4,7},{5,4},{6,5},{7,6},{8,11},{9,8},{10,9... | collective-permute-start | bytes 196616 | tf_op jit(solution)/shard_map/ppermute | solution.py:479
  58.8 8.6 %collective-permute-start.7 = (bf16[256,128]{1,0:T(8,128)(2,1)}, bf16[256,128]{1,0:T(8,128)(2,1)S(1)}, u32[]{:S(2)}, u32[]{:S(2)}) collective-permute-start(bf16[256,128]{1,0:T(8,128)(2,1)} %get-tuple-element.25.refs_3_.refs_0_), channel_id=1, source_target_pairs={{0,2},{1,3},{2,0},{3,1},{4,6},{5,7},{6,4},{7,5},{8,10},{9,11},{10,... | collective-permute-start | bytes 196616 | tf_op jit(solution)/shard_map/ppermute | solution.py:479
  58.8 8.6 %collective-permute-start.6 = (bf16[256,128]{1,0:T(8,128)(2,1)}, bf16[256,128]{1,0:T(8,128)(2,1)S(1)}, u32[]{:S(2)}, u32[]{:S(2)}) collective-permute-start(bf16[256,128]{1,0:T(8,128)(2,1)} %get-tuple-element.25.refs_3_.refs_0_), channel_id=1, source_target_pairs={{0,1},{1,2},{2,3},{3,0},{4,5},{5,6},{6,7},{7,4},{8,9},{9,10},{10,1... | collective-permute-start | bytes 196616 | tf_op jit(solution)/shard_map/ppermute | solution.py:479
  60.1 0.8 copy-start.2
  65.1 33.2 %collective-permute-start.14 = (bf16[256,1024]{1,0:T(8,128)(2,1)}, bf16[256,1024]{1,0:T(8,128)(2,1)S(1)}, u32[]{:S(2)}, u32[]{:S(2)}) collective-permute-start(bf16[256,1024]{1,0:T(8,128)(2,1)} %hop.8.refs_6_), channel_id=1, source_target_pairs={{0,2},{2,3},{3,1},{1,0},{4,6},{6,7},{7,5},{5,4},{8,10},{10,11},{11... | collective-permute-start | bytes 1572872 | tf_op jit(solution)/shard_map/ppermute | solution.py:445
  71.7 0.8 copy-start
  72.4 5.1 %copy-start.17 = (bf16[64,2048]{1,0:T(8,128)(2,1)S(1)}, bf16[64,2048]{1,0:T(8,128)(2,1)}, u32[]{:S(2)}) copy-start(bf16[64,2048]{1,0:T(8,128)(2,1)} %get-tuple-element.28) | copy-start | bytes 786436
  72.4 5.1 %copy-start.16 = (bf16[64,2048]{1,0:T(8,128)(2,1)S(1)}, bf16[64,2048]{1,0:T(8,128)(2,1)}, u32[]{:S(2)}) copy-start(bf16[64,2048]{1,0:T(8,128)(2,1)} %get-tuple-element.29) | copy-start | bytes 786436
  72.4 6.7 %copy-start.15 = (bf16[64,2048]{1,0:T(8,128)(2,1)S(1)}, bf16[64,2048]{1,0:T(8,128)(2,1)}, u32[]{:S(2)}) copy-start(bf16[64,2048]{1,0:T(8,128)(2,1)} %get-tuple-element.30) | copy-start | bytes 786436
  76.7 24.6 %collective-permute-start.10 = (bf16[256,1024]{1,0:T(8,128)(2,1)}, bf16[256,1024]{1,0:T(8,128)(2,1)S(1)}, u32[]{:S(2)}, u32[]{:S(2)}) collective-permute-start(bf16[256,1024]{1,0:T(8,128)(2,1)} %hop.9.refs_8_), channel_id=1, source_target_pairs={{0,2},{2,3},{3,1},{1,0},{4,6},{6,7},{7,5},{5,4},{8,10},{10,11},{11... | collective-permute-start | bytes 1572872 | tf_op jit(solution)/shard_map/ppermute | solution.py:445
  77.5 1.9 %collective-permute-start.11 = (bf16[64,2048]{1,0:T(8,128)(2,1)S(1)}, bf16[64,2048]{1,0:T(8,128)(2,1)S(1)}, u32[]{:S(2)}, u32[]{:S(2)}) collective-permute-start(bf16[64,2048]{1,0:T(8,128)(2,1)S(1)} %copy-done.17), channel_id=1, source_target_pairs={{0,4},{4,0},{8,12},{12,8},{1,5},{5,1},{9,13},{13,9},{2,6},{6,2},{1... | collective-permute-start | bytes 786440 | tf_op jit(solution)/shard_map/ppermute | solution.py:449
  77.5 9.2 %collective-permute-start.12 = (bf16[64,2048]{1,0:T(8,128)(2,1)S(1)}, bf16[64,2048]{1,0:T(8,128)(2,1)S(1)}, u32[]{:S(2)}, u32[]{:S(2)}) collective-permute-start(bf16[64,2048]{1,0:T(8,128)(2,1)S(1)} %copy-done.16), channel_id=1, source_target_pairs={{0,8},{4,12},{8,0},{12,4},{1,9},{5,13},{9,1},{13,5},{2,10},{6,14},... | collective-permute-start | bytes 786440 | tf_op jit(solution)/shard_map/ppermute | solution.py:449
  79.1 12.3 %collective-permute-start.13 = (bf16[64,2048]{1,0:T(8,128)(2,1)S(1)}, bf16[64,2048]{1,0:T(8,128)(2,1)S(1)}, u32[]{:S(2)}, u32[]{:S(2)}) collective-permute-start(bf16[64,2048]{1,0:T(8,128)(2,1)S(1)} %copy-done.15), channel_id=1, source_target_pairs={{0,12},{4,8},{8,4},{12,0},{1,13},{5,9},{9,5},{13,1},{2,14},{6,10},... | collective-permute-start | bytes 786440 | tf_op jit(solution)/shard_map/ppermute | solution.py:449
  79.4 12.0 %copy-start.6 = (bf16[64,2048]{1,0:T(8,128)(2,1)}, bf16[64,2048]{1,0:T(8,128)(2,1)S(1)}, u32[]{:S(2)}) copy-start(bf16[64,2048]{1,0:T(8,128)(2,1)S(1)} %collective-permute-done.11.refs_1_) | copy-start | bytes 786436
  86.7 4.7 %copy-start.7 = (bf16[64,2048]{1,0:T(8,128)(2,1)}, bf16[64,2048]{1,0:T(8,128)(2,1)S(1)}, u32[]{:S(2)}) copy-start(bf16[64,2048]{1,0:T(8,128)(2,1)S(1)} %collective-permute-done.12.refs_2_) | copy-start | bytes 786436
  91.4 0.7 copy-start.8
  98.3 0.8 copy-start.1
  101.2 0.8 copy-start.3
  (4 other events, 2.6 us)

commit v3 on v2

--- a/solution.py
+++ b/solution.py
@@ -12,13 +12,15 @@
 CAP = 64
 LANES = 128
 MASKED = -1e30
-VMEM_LIMIT = 60 * 1024 * 1024
+VMEM_LIMIT = 50 * 1024 * 1024
+FULL_VMEM = 61 * 1024 * 1024
 CHAINS = 2
 PIECE = 512
 SPLIT = 2
 
 VMEM = pl.BlockSpec(memory_space=pltpu.VMEM)
 ANY = pl.BlockSpec(memory_space=pl.ANY)
+BRIEF = pl.CostEstimate(flops=1, transcendentals=0, bytes_accessed=1)
 PARAMS = pltpu.CompilerParams(vmem_limit_bytes=VMEM_LIMIT)
 
 
@@ -226,7 +228,7 @@
             pltpu.SemaphoreType.DMA((2,)),
         ]
         + Weights.scratch(weight.shape[0], chunk),
-        compiler_params=PARAMS,
+        compiler_params=pltpu.CompilerParams(vmem_limit_bytes=FULL_VMEM),
         name="attend",
     )(
         lengths.reshape(1, requests),
@@ -259,11 +261,12 @@
     operands = ([arrived] if arriving else []) + [attended, weight, *after]
     return pl.pallas_call(
         functools.partial(hop_kernel, step, chain, arriving, len(after)),
-        in_specs=[VMEM] * (1 + arriving) + [ANY] * (1 + len(after)),
+        in_specs=[VMEM] * (1 + arriving) + [ANY] + [ANY] * len(after),
         out_specs=VMEM,
         out_shape=jax.ShapeDtypeStruct((attended.shape[0], chunk), jnp.bfloat16),
         scratch_shapes=Weights.scratch(weight.shape[0], chunk),
         compiler_params=PARAMS,
+        cost_estimate=BRIEF,
         name="hop",
     )(*operands)
 
@@ -305,6 +308,7 @@
         out_shape=[jax.ShapeDtypeStruct((replicas * CAP, requests), jnp.bfloat16)]
         + [jax.ShapeDtypeStruct((CAP, width + LANES), jnp.bfloat16)] * replicas,
         compiler_params=PARAMS,
+        cost_estimate=BRIEF,
         name="route",
     )(attended, request_adapter.reshape(1, -1), placement.reshape(1, -1), *after)
 
@@ -334,6 +338,7 @@
         out_specs=[VMEM, VMEM],
         out_shape=[jax.ShapeDtypeStruct((rows, LANES), jnp.bfloat16)] * 2,
         compiler_params=PARAMS,
+        cost_estimate=BRIEF,
         name="down",
     )(*received, slot_down_weight, *after)
 
@@ -365,6 +370,7 @@
         out_specs=[VMEM] * replicas,
         out_shape=[jax.ShapeDtypeStruct((CAP, width), jnp.bfloat16)] * replicas,
         compiler_params=PARAMS,
+        cost_estimate=BRIEF,
         name="up",
     )(*mids, inside, slot_up_weight, *after)
 
@@ -387,11 +393,12 @@
     replicas = len(returned)
     return pl.pallas_call(
         functools.partial(settle_kernel, step, replicas, len(after)),
-        in_specs=[VMEM] * (replicas + 3) + [ANY] * (1 + len(after)),
+        in_specs=[VMEM] * (replicas + 3) + [ANY] + [ANY] * len(after),
         out_specs=VMEM,
         out_shape=jax.ShapeDtypeStruct(residual.shape, jnp.float32),
         scratch_shapes=Weights.scratch(weight.shape[0], residual.shape[1]),
         compiler_params=PARAMS,
+        cost_estimate=BRIEF,
         name="settle",
     )(*returned, chosen, attended, residual, weight, *after)
 
@@ -417,6 +424,7 @@
         out_shape=jax.ShapeDtypeStruct(settled.shape, jnp.bfloat16),
         input_output_aliases={2: 0} if earlier is not None else {},
         compiler_params=PARAMS,
+        cost_estimate=BRIEF,
         name="finish",
     )(*operands)
 
@@ -464,27 +472,30 @@
     )
     rows_here = exchange(leaving)
 
-    latest = chosen
-    stage = 0
+    def take_hop(step, c, after):
+        arrived = forward(travelling[c])
+        travelling[c] = hop(step, c, arrived, attended, output_weight, chunk, after=after)
+
+    rank_sums = deltas = returned = None
     for step in range(1, count - 1):
         for c in range(CHAINS):
-            arrived = forward(travelling[c])
-            travelling[c] = hop(step, c, arrived, attended, output_weight, chunk, after=[latest])
-            latest = travelling[c]
-            if stage == 1:
-                mid, inside = down(rows_here, slot_down_weight, after=[latest])
-                latest = mid
-            if stage == 2:
-                mids = [mid] + [
+            if step == 1 and c == 0:
+                take_hop(step, c, rows_here)
+                mid, inside = down(rows_here, slot_down_weight, after=[travelling[c]])
+                rank_sums = [mid] + [
                     lax.ppermute(mid, "tensor", [(i, (i + k) % count) for i in range(count)])
                     for k in range(1, count)
                 ]
-                deltas = up(mids, inside, slot_up_weight, after=[latest])
-                latest = deltas[0]
-            stage += 1
-    returned = exchange(deltas)
+            elif step == 1 and c == 1:
+                take_hop(step, c, rank_sums)
+                deltas = up(rank_sums, inside, slot_up_weight, after=[travelling[c]])
+                returned = exchange(deltas)
+            elif step == count - 2 and c == CHAINS - 1:
+                take_hop(step, c, returned)
+            else:
+                take_hop(step, c, [deltas[0]])
     settled = settle(
-        count - 1, returned, chosen, attended, residual, output_weight, after=[latest]
+        count - 1, returned, chosen, attended, residual, output_weight, after=[travelling[-1]]
     )
     out = None
     for c in range(CHAINS):

time: 105 us -> 94 us (0.90)
  Pallas kernels: 48.5 us -> 28.1 us
  waiting for transfers between devices: 26.7 us -> 45.4 us
  starting transfers between devices: 22 us -> 17.4 us
  local copies, waits for them, and re-layouts: 6.83 us -> 2.66 us
    ppermute x3, waiting for transfers between devices: 0.01 us -> 17.5 us  [per_device(): lax.ppermute(mid, 'tensor', [(i, (i + k) % count) for i in range(count)])]
    pallas_call x5, Pallas kernels: 20.6 us -> 10.8 us  [hop(): pl.pallas_call(functools.partial(hop_kernel, step, chain, arriving, len(a...]
    ppermute x6, starting transfers between devices: 15.6 us -> 9.95 us  [forward(): return lax.ppermute(x, 'tensor', ring)]
    unnamed x42 -> x16, local copies, waits for them, and re-layouts: 6.83 us -> 2.66 us
    ppermute x6, waiting for transfers between devices: 7.56 us -> 11.2 us  [forward(): return lax.ppermute(x, 'tensor', ring)]
    pallas_call x1, Pallas kernels: 3.57 us -> 0.81 us  [up(): pl.pallas_call(functools.partial(up_kernel, len(mids), len(after)), in_sp...]
    ppermute x6, waiting for transfers between devices: 19.1 us -> 16.7 us  [exchange(): lax.ppermute(blocks[r], 'dp', [(i, i ^ r) for i in range(replicas)])]
    pallas_call x2, Pallas kernels: 4.22 us -> 1.92 us  [finish(): pl.pallas_call(finish_kernel, grid=(count,), in_specs=[pl.BlockSpec((rows...]
  transfers between devices with their start and end apart: 15 -> 15, of which waited for: 6 -> 9; matrix products, arithmetic and copies ran while one was open for 0% -> 0% of each run, Pallas kernels for 36% -> 20%
where the time goes in v3:
time: 94 us; the launch traced here: 93.7 us
  waiting for transfers between devices  45.4 us (48%)
  Pallas kernels  28.1 us (30%)
  starting transfers between devices  17.4 us (19%)
  local copies, waits for them, and re-layouts  2.66 us (3%)
    ppermute x3, waiting for transfers between devices, per_device(): lax.ppermute(mid, 'tensor', [(i, (i + k) % count) for i in range(count)])  17.5 us
    ppermute x6, waiting for transfers between devices, exchange(): lax.ppermute(blocks[r], 'dp', [(i, i ^ r) for i in range(replicas)])  16.7 us
    ppermute x6, waiting for transfers between devices, forward(): return lax.ppermute(x, 'tensor', ring)  11.2 us
    pallas_call x5, Pallas kernels, hop(): pl.pallas_call(functools.partial(hop_kernel, step, chain, arriving, len(a...  10.8 us
    ppermute x6, starting transfers between devices, forward(): return lax.ppermute(x, 'tensor', ring)  9.95 us
    pallas_call x1, Pallas kernels, attend(): pl.pallas_call(functools.partial(attend_kernel, heads, kv, cache, steps),...  8.78 us
    pallas_call x1, Pallas kernels, settle(): pl.pallas_call(functools.partial(settle_kernel, step, replicas, len(after...  4.61 us
    ppermute x6, starting transfers between devices, exchange(): lax.ppermute(blocks[r], 'dp', [(i, i ^ r) for i in range(replicas)])  3.87 us
  transfers between devices with their start and end apart: 15, of which 9 were waited for; matrix products, arithmetic and copies ran while one was open for 0% of the time, Pallas kernels for 20%

profile of v3, /device:TPU:0, one launch (start us, length us, event | category | flops | bytes accessed | tf_op | source)
XLA Modules:
  0.0 93.7 jit_solution(5286018723418024281)
XLA Ops:
  0.0 8.8 %attend.1 = (bf16[256,1024]{1,0:T(8,128)(2,1)}, bf16[256,1024]{1,0:T(8,128)(2,1)}) custom-call(s32[1,256]{1,0:T(1,128)} %bitcast.15, bf16[2048,128]{1,0:T(8,128)(2,1)} %bitcast.12, bf16[8192,128]{1,0:T(8,128)(2,1)} %bitcast.10, bf16[8192,128]{1,0:T(8,128)(2,1)} %bitcast.11, bf16[512,128]{1,0:T(8,128)(2,1)} %bitcast.13, bf16[512,128]{1,0:T(8,128)(2,1)} %bitcast.14, ...), custom_call_target="tpu_custom_call" | custom-call | tf_op jit(solution)/shard_map/attend/pallas_call | solution.py:211
  8.8 4.1 %collective-permute-start.4 = (bf16[256,1024]{1,0:T(8,128)(2,1)}, bf16[256,1024]{1,0:T(8,128)(2,1)S(1)}, u32[]{:S(2)}, u32[]{:S(2)}) collective-permute-start(bf16[256,1024]{1,0:T(8,128)(2,1)} %get-tuple-element.23), channel_id=1, source_target_pairs={{0,2},{2,3},{3,1},{1,0},{4,6},{6,7},{7,5},{5,4},{8,10},{10,11},{11... | collective-permute-start | bytes 1572872 | tf_op jit(solution)/shard_map/ppermute | solution.py:453
  12.9 1.0 %copy-done = bf16[256,1024]{1,0:T(8,128)(2,1)S(1)} copy-done((bf16[256,1024]{1,0:T(8,128)(2,1)S(1)}, bf16[256,1024]{1,0:T(8,128)(2,1)}, u32[]{:S(2)}) %copy-start) | copy-done | bytes 524312
  13.9 2.1 %hop.5.refs_3_ = bf16[256,1024]{1,0:T(8,128)(2,1)S(1)} custom-call(bf16[256,1024]{1,0:T(8,128)(2,1)S(1)} %copy-done, bf16[1024,8192]{1,0:T(8,128)(2,1)} %refs_2_.7), custom_call_target="tpu_custom_call" | custom-call | flops 1 | bytes 1 | tf_op jit(solution)/shard_map/hop/pallas_call | solution.py:262
  16.1 1.6 %collective-permute-start = (bf16[256,1024]{1,0:T(8,128)(2,1)S(1)}, bf16[256,1024]{1,0:T(8,128)(2,1)S(1)}, u32[]{:S(2)}, u32[]{:S(2)}) collective-permute-start(bf16[256,1024]{1,0:T(8,128)(2,1)S(1)} %hop.5.refs_3_), channel_id=1, source_target_pairs={{0,2},{2,3},{3,1},{1,0},{4,6},{6,7},{7,5},{5,4},{8,10},{10,11},{11... | collective-permute-start | bytes 1572872 | tf_op jit(solution)/shard_map/ppermute | solution.py:453
  17.7 0.6 route.1
  18.3 1.6 %collective-permute-start.2 = (bf16[64,1152]{1,0:T(8,128)(2,1)S(1)}, bf16[64,1152]{1,0:T(8,128)(2,1)S(1)}, u32[]{:S(2)}, u32[]{:S(2)}) collective-permute-start(bf16[64,1152]{1,0:T(8,128)(2,1)S(1)} %get-tuple-element.21), channel_id=1, source_target_pairs={{0,8},{4,12},{8,0},{12,4},{1,9},{5,13},{9,1},{13,5},{2,10},{6,14},... | collective-permute-start | bytes 442376 | tf_op jit(solution)/shard_map/ppermute | solution.py:457
  20.2 4.8 %collective-permute-done.2.refs_5_.refs_2_ = bf16[64,1152]{1,0:T(8,128)(2,1)S(1)} collective-permute-done((bf16[64,1152]{1,0:T(8,128)(2,1)S(1)}, bf16[64,1152]{1,0:T(8,128)(2,1)S(1)}, u32[]{:S(2)}, u32[]{:S(2)}) %collective-permute-start.2) | collective-permute-done | bytes 147488 | tf_op jit(solution)/shard_map/ppermute | solution.py:457
  25.1 2.3 %collective-permute-done.3.refs_6_.refs_3_ = bf16[64,1152]{1,0:T(8,128)(2,1)S(1)} collective-permute-done((bf16[64,1152]{1,0:T(8,128)(2,1)S(1)}, bf16[64,1152]{1,0:T(8,128)(2,1)S(1)}, u32[]{:S(2)}, u32[]{:S(2)}) %collective-permute-start.3) | collective-permute-done | bytes 147488 | tf_op jit(solution)/shard_map/ppermute | solution.py:457
  27.3 2.2 %hop.6.refs_5_ = bf16[256,1024]{1,0:T(8,128)(2,1)S(1)} custom-call(bf16[256,1024]{1,0:T(8,128)(2,1)S(1)} %collective-permute-done.4.refs_0_, bf16[256,1024]{1,0:T(8,128)(2,1)S(1)} %copy-done, bf16[1024,8192]{1,0:T(8,128)(2,1)} %refs_2_.7, bf16[64,1152]{1,0:T(8,128)(2,1)S(1)} %get-tuple-element.19.refs_3_.refs_0_, ...), custom_call_target="tpu_custom_call" | custom-call | flops 1 | bytes 1 | tf_op jit(solution)/shard_map/hop/pallas_call | solution.py:262
  29.6 0.6 down.1
  30.2 1.6 %collective-permute-start.7 = (bf16[256,128]{1,0:T(8,128)(2,1)S(1)}, bf16[256,128]{1,0:T(8,128)(2,1)S(1)}, u32[]{:S(2)}, u32[]{:S(2)}) collective-permute-start(bf16[256,128]{1,0:T(8,128)(2,1)S(1)} %get-tuple-element.24.refs_3_.refs_0_), channel_id=1, source_target_pairs={{0,3},{1,0},{2,1},{3,2},{4,7},{5,4},{6,5},{7,6},{8,11},{9,8},{10,9... | collective-permute-start | bytes 196616 | tf_op jit(solution)/shard_map/ppermute | solution.py:486
  32.2 1.6 %collective-permute-start.5 = (bf16[256,128]{1,0:T(8,128)(2,1)S(1)}, bf16[256,128]{1,0:T(8,128)(2,1)S(1)}, u32[]{:S(2)}, u32[]{:S(2)}) collective-permute-start(bf16[256,128]{1,0:T(8,128)(2,1)S(1)} %get-tuple-element.24.refs_3_.refs_0_), channel_id=1, source_target_pairs={{0,1},{1,2},{2,3},{3,0},{4,5},{5,6},{6,7},{7,4},{8,9},{9,10},{10,1... | collective-permute-start | bytes 196616 | tf_op jit(solution)/shard_map/ppermute | solution.py:486
  33.8 1.5 %collective-permute-start.13 = (bf16[256,1024]{1,0:T(8,128)(2,1)S(1)}, bf16[256,1024]{1,0:T(8,128)(2,1)S(1)}, u32[]{:S(2)}, u32[]{:S(2)}) collective-permute-start(bf16[256,1024]{1,0:T(8,128)(2,1)S(1)} %hop.6.refs_5_), channel_id=1, source_target_pairs={{0,2},{2,3},{3,1},{1,0},{4,6},{6,7},{7,5},{5,4},{8,10},{10,11},{11... | collective-permute-start | bytes 1572872 | tf_op jit(solution)/shard_map/ppermute | solution.py:453
  35.2 1.5 %collective-permute-done.refs_0_ = bf16[256,1024]{1,0:T(8,128)(2,1)S(1)} collective-permute-done((bf16[256,1024]{1,0:T(8,128)(2,1)S(1)}, bf16[256,1024]{1,0:T(8,128)(2,1)S(1)}, u32[]{:S(2)}, u32[]{:S(2)}) %collective-permute-start) | collective-permute-done | bytes 524320 | tf_op jit(solution)/shard_map/ppermute | solution.py:453
  36.7 1.4 %collective-permute-done.7.refs_6_.refs_3_ = bf16[256,128]{1,0:T(8,128)(2,1)S(1)} collective-permute-done((bf16[256,128]{1,0:T(8,128)(2,1)S(1)}, bf16[256,128]{1,0:T(8,128)(2,1)S(1)}, u32[]{:S(2)}, u32[]{:S(2)}) %collective-permute-start.7) | collective-permute-done | bytes 65568 | tf_op jit(solution)/shard_map/ppermute | solution.py:486
  38.1 16.1 %collective-permute-done.6.refs_5_.refs_2_ = bf16[256,128]{1,0:T(8,128)(2,1)S(1)} collective-permute-done((bf16[256,128]{1,0:T(8,128)(2,1)S(1)}, bf16[256,128]{1,0:T(8,128)(2,1)S(1)}, u32[]{:S(2)}, u32[]{:S(2)}) %collective-permute-start.6) | collective-permute-done | bytes 65568 | tf_op jit(solution)/shard_map/ppermute | solution.py:486
  54.2 2.1 %hop.7.refs_6_ = bf16[256,1024]{1,0:T(8,128)(2,1)S(1)} custom-call(bf16[256,1024]{1,0:T(8,128)(2,1)S(1)} %collective-permute-done.refs_0_, bf16[256,1024]{1,0:T(8,128)(2,1)S(1)} %copy-done.1, bf16[1024,8192]{1,0:T(8,128)(2,1)} %refs_2_.7, bf16[256,128]{1,0:T(8,128)(2,1)S(1)} %get-tuple-element.24.refs_3_.refs_0_, ...), custom_call_target="tpu_custom_call" | custom-call | flops 1 | bytes 1 | tf_op jit(solution)/shard_map/hop/pallas_call | solution.py:262
  56.3 1.6 %collective-permute-start.8 = (bf16[256,1024]{1,0:T(8,128)(2,1)S(1)}, bf16[256,1024]{1,0:T(8,128)(2,1)S(1)}, u32[]{:S(2)}, u32[]{:S(2)}) collective-permute-start(bf16[256,1024]{1,0:T(8,128)(2,1)S(1)} %hop.7.refs_6_), channel_id=1, source_target_pairs={{0,2},{2,3},{3,1},{1,0},{4,6},{6,7},{7,5},{5,4},{8,10},{10,11},{11... | collective-permute-start | bytes 1572872 | tf_op jit(solution)/shard_map/ppermute | solution.py:453
  57.9 0.8 up.1
  58.8 1.6 %collective-permute-start.10 = (bf16[64,2048]{1,0:T(8,128)(2,1)S(1)}, bf16[64,2048]{1,0:T(8,128)(2,1)S(1)}, u32[]{:S(2)}, u32[]{:S(2)}) collective-permute-start(bf16[64,2048]{1,0:T(8,128)(2,1)S(1)} %get-tuple-element.28), channel_id=1, source_target_pairs={{0,8},{4,12},{8,0},{12,4},{1,9},{5,13},{9,1},{13,5},{2,10},{6,14},... | collective-permute-start | bytes 786440 | tf_op jit(solution)/shard_map/ppermute | solution.py:457
  60.7 2.1 %hop.9 = bf16[256,1024]{1,0:T(8,128)(2,1)S(1)} custom-call(bf16[256,1024]{1,0:T(8,128)(2,1)S(1)} %collective-permute-done.13.refs_0_, bf16[256,1024]{1,0:T(8,128)(2,1)S(1)} %copy-done.1, bf16[1024,8192]{1,0:T(8,128)(2,1)} %refs_2_.7, bf16[64,2048]{1,0:T(8,128)(2,1)S(1)} %get-tuple-element.26.refs_3_.refs_0_), custom_call_target="tpu_custom_call" | custom-call | flops 1 | bytes 1 | tf_op jit(solution)/shard_map/hop/pallas_call | solution.py:262
  63.1 4.9 %collective-permute-done.10.refs_5_.refs_2_ = bf16[64,2048]{1,0:T(8,128)(2,1)S(1)} collective-permute-done((bf16[64,2048]{1,0:T(8,128)(2,1)S(1)}, bf16[64,2048]{1,0:T(8,128)(2,1)S(1)}, u32[]{:S(2)}, u32[]{:S(2)}) %collective-permute-start.10) | collective-permute-done | bytes 262176 | tf_op jit(solution)/shard_map/ppermute | solution.py:457
  68.0 4.7 %collective-permute-done.11.refs_6_.refs_3_ = bf16[64,2048]{1,0:T(8,128)(2,1)S(1)} collective-permute-done((bf16[64,2048]{1,0:T(8,128)(2,1)S(1)}, bf16[64,2048]{1,0:T(8,128)(2,1)S(1)}, u32[]{:S(2)}, u32[]{:S(2)}) %collective-permute-start.11) | collective-permute-done | bytes 262176 | tf_op jit(solution)/shard_map/ppermute | solution.py:457
  72.7 2.1 %hop.8.refs_8_ = bf16[256,1024]{1,0:T(8,128)(2,1)S(1)} custom-call(bf16[256,1024]{1,0:T(8,128)(2,1)S(1)} %collective-permute-done.8.refs_0_, bf16[256,1024]{1,0:T(8,128)(2,1)S(1)} %copy-done.1, bf16[1024,8192]{1,0:T(8,128)(2,1)} %refs_2_.7, bf16[64,2048]{1,0:T(8,128)(2,1)S(1)} %get-tuple-element.26.refs_3_.refs_0_, ...), custom_call_target="tpu_custom_call" | custom-call | flops 1 | bytes 1 | tf_op jit(solution)/shard_map/hop/pallas_call | solution.py:262
  74.9 0.9 %collective-permute-start.12 = (bf16[256,1024]{1,0:T(8,128)(2,1)S(1)}, bf16[256,1024]{1,0:T(8,128)(2,1)S(1)}, u32[]{:S(2)}, u32[]{:S(2)}) collective-permute-start(bf16[256,1024]{1,0:T(8,128)(2,1)S(1)} %hop.8.refs_8_), channel_id=1, source_target_pairs={{0,2},{2,3},{3,1},{1,0},{4,6},{6,7},{7,5},{5,4},{8,10},{10,11},{11... | collective-permute-start | bytes 1572872 | tf_op jit(solution)/shard_map/ppermute | solution.py:453
  75.8 4.6 %settle.1.settled_ref = f32[256,2048]{1,0:T(8,128)} custom-call(bf16[64,2048]{1,0:T(8,128)(2,1)S(1)} %get-tuple-element.26.refs_3_.refs_0_, bf16[64,2048]{1,0:T(8,128)(2,1)S(1)} %collective-permute-done.9.refs_4_.refs_1_, bf16[64,2048]{1,0:T(8,128)(2,1)S(1)} %collective-permute-done.10.refs_5_.refs_2_, ...), custom_call_target="tpu_custom_call" | custom-call | flops 1 | bytes 1 | tf_op jit(solution)/shard_map/settle/pallas_call | solution.py:394
  80.4 1.9 %collective-permute-done.14.arrived_ref = bf16[256,1024]{1,0:T(8,128)(2,1)S(1)} collective-permute-done((bf16[256,1024]{1,0:T(8,128)(2,1)S(1)}, bf16[256,1024]{1,0:T(8,128)(2,1)S(1)}, u32[]{:S(2)}, u32[]{:S(2)}) %collective-permute-start.14) | collective-permute-done | bytes 524320 | tf_op jit(solution)/shard_map/ppermute | solution.py:453
  82.4 1.6 %copy-done.2 = f32[256,2048]{1,0:T(8,128)S(1)} copy-done((f32[256,2048]{1,0:T(8,128)S(1)}, f32[256,2048]{1,0:T(8,128)}, u32[]{:S(2)}) %copy-start.2) | copy-done | bytes 2097176
  84.0 1.0 %finish.2.refs_0_ = bf16[256,2048]{1,0:T(8,128)(2,1)} custom-call(bf16[256,1024]{1,0:T(8,128)(2,1)S(1)} %collective-permute-done.14.arrived_ref, f32[256,2048]{1,0:T(8,128)S(1)} %copy-done.2), custom_call_target="tpu_custom_call" | custom-call | flops 1 | bytes 1 | tf_op jit(solution)/shard_map/finish/pallas_call | solution.py:415
  84.9 7.8 %collective-permute-done.12.arrived_ref = bf16[256,1024]{1,0:T(8,128)(2,1)S(1)} collective-permute-done((bf16[256,1024]{1,0:T(8,128)(2,1)S(1)}, bf16[256,1024]{1,0:T(8,128)(2,1)S(1)}, u32[]{:S(2)}, u32[]{:S(2)}) %collective-permute-start.12) | collective-permute-done | bytes 524320 | tf_op jit(solution)/shard_map/ppermute | solution.py:453
  92.7 1.0 %finish.3 = bf16[256,2048]{1,0:T(8,128)(2,1)} custom-call(bf16[256,1024]{1,0:T(8,128)(2,1)S(1)} %collective-permute-done.12.arrived_ref, f32[256,2048]{1,0:T(8,128)S(1)} %copy-done.2, bf16[256,2048]{1,0:T(8,128)(2,1)} %finish.2.refs_0_), custom_call_target="tpu_custom_call", output_to_operand_aliasing={{}: (2, {})} | custom-call | flops 1 | bytes 1 | tf_op jit(solution)/shard_map/finish/pallas_call | solution.py:415
  (26 shorter events, 1.3 us)
Async XLA Ops:
  8.8 18.5 %collective-permute-start.4 = (bf16[256,1024]{1,0:T(8,128)(2,1)}, bf16[256,1024]{1,0:T(8,128)(2,1)S(1)}, u32[]{:S(2)}, u32[]{:S(2)}) collective-permute-start(bf16[256,1024]{1,0:T(8,128)(2,1)} %get-tuple-element.23), channel_id=1, source_target_pairs={{0,2},{2,3},{3,1},{1,0},{4,6},{6,7},{7,5},{5,4},{8,10},{10,11},{11... | collective-permute-start | bytes 1572872 | tf_op jit(solution)/shard_map/ppermute | solution.py:453
  12.9 1.0 %copy-start = (bf16[256,1024]{1,0:T(8,128)(2,1)S(1)}, bf16[256,1024]{1,0:T(8,128)(2,1)}, u32[]{:S(2)}) copy-start(bf16[256,1024]{1,0:T(8,128)(2,1)} %get-tuple-element.18.refs_0_.refs_1_.refs_5_) | copy-start | bytes 1572868
  13.9 3.8 %copy-start.6 = (s32[256]{0:T(256)S(1)}, s32[256]{0:T(256)}, u32[]{:S(2)}) copy-start(s32[256]{0:T(256)} %param.23) | copy-start | bytes 3076
  13.9 3.8 %copy-start.7 = (s32[32]{0:T(128)S(1)}, s32[32]{0:T(128)}, u32[]{:S(2)}) copy-start(s32[32]{0:T(128)} %param.22) | copy-start | bytes 388
  16.1 20.6 %collective-permute-start = (bf16[256,1024]{1,0:T(8,128)(2,1)S(1)}, bf16[256,1024]{1,0:T(8,128)(2,1)S(1)}, u32[]{:S(2)}, u32[]{:S(2)}) collective-permute-start(bf16[256,1024]{1,0:T(8,128)(2,1)S(1)} %hop.5.refs_3_), channel_id=1, source_target_pairs={{0,2},{2,3},{3,1},{1,0},{4,6},{6,7},{7,5},{5,4},{8,10},{10,11},{11... | collective-permute-start | bytes 1572872 | tf_op jit(solution)/shard_map/ppermute | solution.py:453
  18.3 1.9 %collective-permute-start.1 = (bf16[64,1152]{1,0:T(8,128)(2,1)S(1)}, bf16[64,1152]{1,0:T(8,128)(2,1)S(1)}, u32[]{:S(2)}, u32[]{:S(2)}) collective-permute-start(bf16[64,1152]{1,0:T(8,128)(2,1)S(1)} %get-tuple-element.20), channel_id=1, source_target_pairs={{0,4},{4,0},{8,12},{12,8},{1,5},{5,1},{9,13},{13,9},{2,6},{6,2},{1... | collective-permute-start | bytes 442376 | tf_op jit(solution)/shard_map/ppermute | solution.py:457
  18.3 6.7 %collective-permute-start.2 = (bf16[64,1152]{1,0:T(8,128)(2,1)S(1)}, bf16[64,1152]{1,0:T(8,128)(2,1)S(1)}, u32[]{:S(2)}, u32[]{:S(2)}) collective-permute-start(bf16[64,1152]{1,0:T(8,128)(2,1)S(1)} %get-tuple-element.21), channel_id=1, source_target_pairs={{0,8},{4,12},{8,0},{12,4},{1,9},{5,13},{9,1},{13,5},{2,10},{6,14},... | collective-permute-start | bytes 442376 | tf_op jit(solution)/shard_map/ppermute | solution.py:457
  19.9 7.4 %collective-permute-start.3 = (bf16[64,1152]{1,0:T(8,128)(2,1)S(1)}, bf16[64,1152]{1,0:T(8,128)(2,1)S(1)}, u32[]{:S(2)}, u32[]{:S(2)}) collective-permute-start(bf16[64,1152]{1,0:T(8,128)(2,1)S(1)} %get-tuple-element.22), channel_id=1, source_target_pairs={{0,12},{4,8},{8,4},{12,0},{1,13},{5,9},{9,5},{13,1},{2,14},{6,10},... | collective-permute-start | bytes 442376 | tf_op jit(solution)/shard_map/ppermute | solution.py:457
  27.3 2.2 %copy-start.4 = (bf16[8,64,1024]{2,1,0:T(8,128)(2,1)S(1)}, bf16[8,64,1024]{2,1,0:T(8,128)(2,1)}, u32[]{:S(2)}) copy-start(bf16[8,64,1024]{2,1,0:T(8,128)(2,1)} %refs_4_.1) | copy-start | bytes 3145732
  29.6 24.6 %copy-start.1 = (bf16[256,1024]{1,0:T(8,128)(2,1)S(1)}, bf16[256,1024]{1,0:T(8,128)(2,1)}, u32[]{:S(2)}) copy-start(bf16[256,1024]{1,0:T(8,128)(2,1)} %get-tuple-element.18.refs_0_.refs_1_.refs_5_) | copy-start | bytes 1572868
  30.2 27.7 %copy-start.3 = (bf16[8,64,2048]{2,1,0:T(8,128)(2,1)S(1)}, bf16[8,64,2048]{2,1,0:T(8,128)(2,1)}, u32[]{:S(2)}) copy-start(bf16[8,64,2048]{2,1,0:T(8,128)(2,1)} %refs_5_.1) | copy-start | bytes 6291460
  30.2 7.9 %collective-permute-start.7 = (bf16[256,128]{1,0:T(8,128)(2,1)S(1)}, bf16[256,128]{1,0:T(8,128)(2,1)S(1)}, u32[]{:S(2)}, u32[]{:S(2)}) collective-permute-start(bf16[256,128]{1,0:T(8,128)(2,1)S(1)} %get-tuple-element.24.refs_3_.refs_0_), channel_id=1, source_target_pairs={{0,3},{1,0},{2,1},{3,2},{4,7},{5,4},{6,5},{7,6},{8,11},{9,8},{10,9... | collective-permute-start | bytes 196616 | tf_op jit(solution)/shard_map/ppermute | solution.py:486
  31.9 22.3 %collective-permute-start.6 = (bf16[256,128]{1,0:T(8,128)(2,1)S(1)}, bf16[256,128]{1,0:T(8,128)(2,1)S(1)}, u32[]{:S(2)}, u32[]{:S(2)}) collective-permute-start(bf16[256,128]{1,0:T(8,128)(2,1)S(1)} %get-tuple-element.24.refs_3_.refs_0_), channel_id=1, source_target_pairs={{0,2},{1,3},{2,0},{3,1},{4,6},{5,7},{6,4},{7,5},{8,10},{9,11},{10,... | collective-permute-start | bytes 196616 | tf_op jit(solution)/shard_map/ppermute | solution.py:486
  32.2 22.0 %collective-permute-start.5 = (bf16[256,128]{1,0:T(8,128)(2,1)S(1)}, bf16[256,128]{1,0:T(8,128)(2,1)S(1)}, u32[]{:S(2)}, u32[]{:S(2)}) collective-permute-start(bf16[256,128]{1,0:T(8,128)(2,1)S(1)} %get-tuple-element.24.refs_3_.refs_0_), channel_id=1, source_target_pairs={{0,1},{1,2},{2,3},{3,0},{4,5},{5,6},{6,7},{7,4},{8,9},{9,10},{10,1... | collective-permute-start | bytes 196616 | tf_op jit(solution)/shard_map/ppermute | solution.py:486
  33.8 26.9 %collective-permute-start.13 = (bf16[256,1024]{1,0:T(8,128)(2,1)S(1)}, bf16[256,1024]{1,0:T(8,128)(2,1)S(1)}, u32[]{:S(2)}, u32[]{:S(2)}) collective-permute-start(bf16[256,1024]{1,0:T(8,128)(2,1)S(1)} %hop.6.refs_5_), channel_id=1, source_target_pairs={{0,2},{2,3},{3,1},{1,0},{4,6},{6,7},{7,5},{5,4},{8,10},{10,11},{11... | collective-permute-start | bytes 1572872 | tf_op jit(solution)/shard_map/ppermute | solution.py:453
  56.3 16.4 %collective-permute-start.8 = (bf16[256,1024]{1,0:T(8,128)(2,1)S(1)}, bf16[256,1024]{1,0:T(8,128)(2,1)S(1)}, u32[]{:S(2)}, u32[]{:S(2)}) collective-permute-start(bf16[256,1024]{1,0:T(8,128)(2,1)S(1)} %hop.7.refs_6_), channel_id=1, source_target_pairs={{0,2},{2,3},{3,1},{1,0},{4,6},{6,7},{7,5},{5,4},{8,10},{10,11},{11... | collective-permute-start | bytes 1572872 | tf_op jit(solution)/shard_map/ppermute | solution.py:453
  58.8 4.3 %collective-permute-start.9 = (bf16[64,2048]{1,0:T(8,128)(2,1)S(1)}, bf16[64,2048]{1,0:T(8,128)(2,1)S(1)}, u32[]{:S(2)}, u32[]{:S(2)}) collective-permute-start(bf16[64,2048]{1,0:T(8,128)(2,1)S(1)} %get-tuple-element.27), channel_id=1, source_target_pairs={{0,4},{4,0},{8,12},{12,8},{1,5},{5,1},{9,13},{13,9},{2,6},{6,2},{1... | collective-permute-start | bytes 786440 | tf_op jit(solution)/shard_map/ppermute | solution.py:457
  58.8 9.2 %collective-permute-start.10 = (bf16[64,2048]{1,0:T(8,128)(2,1)S(1)}, bf16[64,2048]{1,0:T(8,128)(2,1)S(1)}, u32[]{:S(2)}, u32[]{:S(2)}) collective-permute-start(bf16[64,2048]{1,0:T(8,128)(2,1)S(1)} %get-tuple-element.28), channel_id=1, source_target_pairs={{0,8},{4,12},{8,0},{12,4},{1,9},{5,13},{9,1},{13,5},{2,10},{6,14},... | collective-permute-start | bytes 786440 | tf_op jit(solution)/shard_map/ppermute | solution.py:457
  60.4 12.3 %collective-permute-start.11 = (bf16[64,2048]{1,0:T(8,128)(2,1)S(1)}, bf16[64,2048]{1,0:T(8,128)(2,1)S(1)}, u32[]{:S(2)}, u32[]{:S(2)}) collective-permute-start(bf16[64,2048]{1,0:T(8,128)(2,1)S(1)} %get-tuple-element.29), channel_id=1, source_target_pairs={{0,12},{4,8},{8,4},{12,0},{1,13},{5,9},{9,5},{13,1},{2,14},{6,10},... | collective-permute-start | bytes 786440 | tf_op jit(solution)/shard_map/ppermute | solution.py:457
  62.9 13.0 %copy-start.5 = (bf16[256,2048]{1,0:T(8,128)(2,1)S(1)}, bf16[256,2048]{1,0:T(8,128)(2,1)}, u32[]{:S(2)}) copy-start(bf16[256,2048]{1,0:T(8,128)(2,1)} %refs_6_.1) | copy-start | bytes 3145732
  62.9 19.5 %collective-permute-start.14 = (bf16[256,1024]{1,0:T(8,128)(2,1)S(1)}, bf16[256,1024]{1,0:T(8,128)(2,1)S(1)}, u32[]{:S(2)}, u32[]{:S(2)}) collective-permute-start(bf16[256,1024]{1,0:T(8,128)(2,1)S(1)} %hop.9), channel_id=1, source_target_pairs={{0,2},{2,3},{3,1},{1,0},{4,6},{6,7},{7,5},{5,4},{8,10},{10,11},{11... | collective-permute-start | bytes 1572872 | tf_op jit(solution)/shard_map/ppermute | solution.py:453
  74.9 17.9 %collective-permute-start.12 = (bf16[256,1024]{1,0:T(8,128)(2,1)S(1)}, bf16[256,1024]{1,0:T(8,128)(2,1)S(1)}, u32[]{:S(2)}, u32[]{:S(2)}) collective-permute-start(bf16[256,1024]{1,0:T(8,128)(2,1)S(1)} %hop.8.refs_8_), channel_id=1, source_target_pairs={{0,2},{2,3},{3,1},{1,0},{4,6},{6,7},{7,5},{5,4},{8,10},{10,11},{11... | collective-permute-start | bytes 1572872 | tf_op jit(solution)/shard_map/ppermute | solution.py:453
  82.4 1.6 %copy-start.2 = (f32[256,2048]{1,0:T(8,128)S(1)}, f32[256,2048]{1,0:T(8,128)}, u32[]{:S(2)}) copy-start(f32[256,2048]{1,0:T(8,128)} %settle.1.settled_ref) | copy-start | bytes 6291460

commit v4 on v3

--- a/solution.py
+++ b/solution.py
@@ -325,8 +325,14 @@
     lane_slot = _iota(projected.shape, 1) // rank
     mine = lane_slot == inside[:, 0:1].astype(jnp.int32)
     projected = jnp.where(mine, projected, 0.0).astype(jnp.bfloat16)
-    fold = _iota((slots * rank, LANES), 0) % rank == _iota((slots * rank, LANES), 1)
-    mid_ref[...] = _dot(projected, fold.astype(jnp.bfloat16)).astype(jnp.bfloat16)
+    beside = LANES // rank
+    some = projected.shape[0] // beside
+    packed = 0.0
+    for b in range(beside):
+        lane = _iota((slots * rank, LANES), 1) - b * rank
+        fold = _iota((slots * rank, LANES), 0) % rank == lane
+        packed = packed + _dot(projected[b * some : (b + 1) * some, :], fold.astype(jnp.bfloat16))
+    mid_ref[...] = packed.astype(jnp.bfloat16)
 
 
 def down(received, slot_down_weight, after=()):
@@ -336,7 +342,10 @@
         functools.partial(down_kernel, replicas, len(after)),
         in_specs=[VMEM] * (replicas + 1) + [ANY] * len(after),
         out_specs=[VMEM, VMEM],
-        out_shape=[jax.ShapeDtypeStruct((rows, LANES), jnp.bfloat16)] * 2,
+        out_shape=[
+            jax.ShapeDtypeStruct((rows * slot_down_weight.shape[1] // LANES, LANES), jnp.bfloat16),
+            jax.ShapeDtypeStruct((rows, LANES), jnp.bfloat16),
+        ],
         compiler_params=PARAMS,
         cost_estimate=BRIEF,
         name="down",
@@ -351,8 +360,13 @@
     mid = mids[0][...].astype(jnp.float32)
     for m in mids[1:]:
         mid = mid + m[...].astype(jnp.float32)
-    spread = _iota((LANES, slots * rank), 1) % rank == _iota((LANES, slots * rank), 0)
-    wide = _dot(mid.astype(jnp.bfloat16), spread.astype(jnp.bfloat16))
+    mid = mid.astype(jnp.bfloat16)
+    wide = []
+    for b in range(LANES // rank):
+        lane = _iota((LANES, slots * rank), 0) - b * rank
+        spread = _iota((LANES, slots * rank), 1) % rank == lane
+        wide.append(_dot(mid, spread.astype(jnp.bfloat16)))
+    wide = jnp.concatenate(wide, axis=0)
     mine = _iota(wide.shape, 1) // rank == inside_ref[:, 0:1].astype(jnp.int32)
     wide = jnp.where(mine, wide, 0.0).astype(jnp.bfloat16)
     delta = _dot(wide, up_ref[...].reshape(slots * rank, width)).astype(jnp.bfloat16)
@@ -486,12 +500,12 @@
                     lax.ppermute(mid, "tensor", [(i, (i + k) % count) for i in range(count)])
                     for k in range(1, count)
                 ]
-            elif step == 1 and c == 1:
-                take_hop(step, c, rank_sums)
+            elif step == 1:
+                take_hop(step, c, [mid])
+            elif step == 2 and c == 0:
+                take_hop(step, c, [])
                 deltas = up(rank_sums, inside, slot_up_weight, after=[travelling[c]])
                 returned = exchange(deltas)
-            elif step == count - 2 and c == CHAINS - 1:
-                take_hop(step, c, returned)
             else:
                 take_hop(step, c, [deltas[0]])
     settled = settle(

time: 94 us -> 101 us (1.074)
  starting transfers between devices: 17.4 us -> 22.3 us
  waiting for transfers between devices: 45.4 us -> 47.3 us
    ppermute x6, starting transfers between devices: 9.95 us -> 15.8 us  [forward(): return lax.ppermute(x, 'tensor', ring)]
    ppermute x6, waiting for transfers between devices: 11.2 us -> 7.88 us  [forward(): return lax.ppermute(x, 'tensor', ring)]
    ppermute x3, waiting for transfers between devices: 17.5 us -> 20.2 us  [per_device(): lax.ppermute(mid, 'tensor', [(i, (i + k) % count) for i in range(count)])]
    ppermute x6, waiting for transfers between devices: 16.7 us -> 19.2 us  [exchange(): lax.ppermute(blocks[r], 'dp', [(i, i ^ r) for i in range(replicas)])]
  transfers between devices with their start and end apart: 15 -> 15, of which waited for: 9 -> 8; matrix products, arithmetic and copies ran while one was open for 0% -> 0% of each run, Pallas kernels for 20% -> 18%
where the time goes in v4:
time: 101 us
  waiting for transfers between devices  47.3 us (47%)
  Pallas kernels  28.2 us (28%)
  starting transfers between devices  22.3 us (22%)
  local copies, waits for them, and re-layouts  2.66 us (3%)
    ppermute x3, waiting for transfers between devices, per_device(): lax.ppermute(mid, 'tensor', [(i, (i + k) % count) for i in range(count)])  20.2 us
    ppermute x6, waiting for transfers between devices, exchange(): lax.ppermute(blocks[r], 'dp', [(i, i ^ r) for i in range(replicas)])  19.2 us
    ppermute x6, starting transfers between devices, forward(): return lax.ppermute(x, 'tensor', ring)  15.8 us
    pallas_call x5, Pallas kernels, hop(): pl.pallas_call(functools.partial(hop_kernel, step, chain, arriving, len(a...  10.9 us
    pallas_call x1, Pallas kernels, attend(): pl.pallas_call(functools.partial(attend_kernel, heads, kv, cache, steps),...  8.78 us
    ppermute x6, waiting for transfers between devices, forward(): return lax.ppermute(x, 'tensor', ring)  7.88 us
    pallas_call x1, Pallas kernels, settle(): pl.pallas_call(functools.partial(settle_kernel, step, replicas, len(after...  4.61 us
    ppermute x6, starting transfers between devices, exchange(): lax.ppermute(blocks[r], 'dp', [(i, i ^ r) for i in range(replicas)])  3.79 us
  transfers between devices with their start and end apart: 15, of which 8 were waited for; matrix products, arithmetic and copies ran while one was open for 0% of the time, Pallas kernels for 18%

profile of v4, /device:TPU:0, one launch (start us, length us, event | category | flops | bytes accessed | tf_op | source)
XLA Modules:
  0.0 100.6 jit_solution(2588852310538591692)
XLA Ops:
  0.0 8.8 %attend.1 = (bf16[256,1024]{1,0:T(8,128)(2,1)}, bf16[256,1024]{1,0:T(8,128)(2,1)}) custom-call(s32[1,256]{1,0:T(1,128)} %bitcast.15, bf16[2048,128]{1,0:T(8,128)(2,1)} %bitcast.12, bf16[8192,128]{1,0:T(8,128)(2,1)} %bitcast.10, bf16[8192,128]{1,0:T(8,128)(2,1)} %bitcast.11, bf16[512,128]{1,0:T(8,128)(2,1)} %bitcast.13, bf16[512,128]{1,0:T(8,128)(2,1)} %bitcast.14, ...), custom_call_target="tpu_custom_call" | custom-call | tf_op jit(solution)/shard_map/attend/pallas_call | solution.py:211
  8.8 4.1 %collective-permute-start.4 = (bf16[256,1024]{1,0:T(8,128)(2,1)}, bf16[256,1024]{1,0:T(8,128)(2,1)S(1)}, u32[]{:S(2)}, u32[]{:S(2)}) collective-permute-start(bf16[256,1024]{1,0:T(8,128)(2,1)} %get-tuple-element.23), channel_id=1, source_target_pairs={{0,2},{2,3},{3,1},{1,0},{4,6},{6,7},{7,5},{5,4},{8,10},{10,11},{11... | collective-permute-start | bytes 1572872 | tf_op jit(solution)/shard_map/ppermute | solution.py:467
  12.9 1.0 %copy-done = bf16[256,1024]{1,0:T(8,128)(2,1)S(1)} copy-done((bf16[256,1024]{1,0:T(8,128)(2,1)S(1)}, bf16[256,1024]{1,0:T(8,128)(2,1)}, u32[]{:S(2)}) %copy-start) | copy-done | bytes 524312
  13.9 2.1 %hop.5.refs_3_ = bf16[256,1024]{1,0:T(8,128)(2,1)S(1)} custom-call(bf16[256,1024]{1,0:T(8,128)(2,1)S(1)} %copy-done, bf16[1024,8192]{1,0:T(8,128)(2,1)} %refs_7_.1), custom_call_target="tpu_custom_call" | custom-call | flops 1 | bytes 1 | tf_op jit(solution)/shard_map/hop/pallas_call | solution.py:262
  16.1 1.6 %collective-permute-start = (bf16[256,1024]{1,0:T(8,128)(2,1)S(1)}, bf16[256,1024]{1,0:T(8,128)(2,1)S(1)}, u32[]{:S(2)}, u32[]{:S(2)}) collective-permute-start(bf16[256,1024]{1,0:T(8,128)(2,1)S(1)} %hop.5.refs_3_), channel_id=1, source_target_pairs={{0,2},{2,3},{3,1},{1,0},{4,6},{6,7},{7,5},{5,4},{8,10},{10,11},{11... | collective-permute-start | bytes 1572872 | tf_op jit(solution)/shard_map/ppermute | solution.py:467
  17.7 0.6 route.1
  18.3 1.6 %collective-permute-start.2 = (bf16[64,1152]{1,0:T(8,128)(2,1)S(1)}, bf16[64,1152]{1,0:T(8,128)(2,1)S(1)}, u32[]{:S(2)}, u32[]{:S(2)}) collective-permute-start(bf16[64,1152]{1,0:T(8,128)(2,1)S(1)} %get-tuple-element.21), channel_id=1, source_target_pairs={{0,8},{4,12},{8,0},{12,4},{1,9},{5,13},{9,1},{13,5},{2,10},{6,14},... | collective-permute-start | bytes 442376 | tf_op jit(solution)/shard_map/ppermute | solution.py:471
  20.2 4.8 %collective-permute-done.2.refs_5_.refs_2_ = bf16[64,1152]{1,0:T(8,128)(2,1)S(1)} collective-permute-done((bf16[64,1152]{1,0:T(8,128)(2,1)S(1)}, bf16[64,1152]{1,0:T(8,128)(2,1)S(1)}, u32[]{:S(2)}, u32[]{:S(2)}) %collective-permute-start.2) | collective-permute-done | bytes 147488 | tf_op jit(solution)/shard_map/ppermute | solution.py:471
  25.1 2.3 %collective-permute-done.3.refs_6_.refs_3_ = bf16[64,1152]{1,0:T(8,128)(2,1)S(1)} collective-permute-done((bf16[64,1152]{1,0:T(8,128)(2,1)S(1)}, bf16[64,1152]{1,0:T(8,128)(2,1)S(1)}, u32[]{:S(2)}, u32[]{:S(2)}) %collective-permute-start.3) | collective-permute-done | bytes 147488 | tf_op jit(solution)/shard_map/ppermute | solution.py:471
  27.3 2.2 %hop.6.refs_5_ = bf16[256,1024]{1,0:T(8,128)(2,1)S(1)} custom-call(bf16[256,1024]{1,0:T(8,128)(2,1)S(1)} %collective-permute-done.4.refs_0_, bf16[256,1024]{1,0:T(8,128)(2,1)S(1)} %copy-done, bf16[1024,8192]{1,0:T(8,128)(2,1)} %refs_7_.1, bf16[64,1152]{1,0:T(8,128)(2,1)S(1)} %get-tuple-element.19.refs_3_.refs_0_, ...), custom_call_target="tpu_custom_call" | custom-call | flops 1 | bytes 1 | tf_op jit(solution)/shard_map/hop/pallas_call | solution.py:262
  29.6 1.5 %collective-permute-start.9 = (bf16[256,1024]{1,0:T(8,128)(2,1)S(1)}, bf16[256,1024]{1,0:T(8,128)(2,1)S(1)}, u32[]{:S(2)}, u32[]{:S(2)}) collective-permute-start(bf16[256,1024]{1,0:T(8,128)(2,1)S(1)} %hop.6.refs_5_), channel_id=1, source_target_pairs={{0,2},{2,3},{3,1},{1,0},{4,6},{6,7},{7,5},{5,4},{8,10},{10,11},{11... | collective-permute-start | bytes 1572872 | tf_op jit(solution)/shard_map/ppermute | solution.py:467
  31.1 0.6 down.1
  31.8 4.9 %collective-permute-done.refs_0_ = bf16[256,1024]{1,0:T(8,128)(2,1)S(1)} collective-permute-done((bf16[256,1024]{1,0:T(8,128)(2,1)S(1)}, bf16[256,1024]{1,0:T(8,128)(2,1)S(1)}, u32[]{:S(2)}, u32[]{:S(2)}) %collective-permute-start) | collective-permute-done | bytes 524320 | tf_op jit(solution)/shard_map/ppermute | solution.py:467
  36.7 2.1 %hop.7 = bf16[256,1024]{1,0:T(8,128)(2,1)S(1)} custom-call(bf16[256,1024]{1,0:T(8,128)(2,1)S(1)} %collective-permute-done.refs_0_, bf16[256,1024]{1,0:T(8,128)(2,1)S(1)} %copy-done.1, bf16[1024,8192]{1,0:T(8,128)(2,1)} %refs_7_.1, bf16[128,128]{1,0:T(8,128)(2,1)S(1)} %get-tuple-element.24.refs_3_.refs_0_), custom_call_target="tpu_custom_call" | custom-call | flops 1 | bytes 1 | tf_op jit(solution)/shard_map/hop/pallas_call | solution.py:262
  38.8 3.4 %collective-permute-start.5 = (bf16[256,1024]{1,0:T(8,128)(2,1)S(1)}, bf16[256,1024]{1,0:T(8,128)(2,1)S(1)}, u32[]{:S(2)}, u32[]{:S(2)}) collective-permute-start(bf16[256,1024]{1,0:T(8,128)(2,1)S(1)} %hop.7), channel_id=1, source_target_pairs={{0,2},{2,3},{3,1},{1,0},{4,6},{6,7},{7,5},{5,4},{8,10},{10,11},{11... | collective-permute-start | bytes 1572872 | tf_op jit(solution)/shard_map/ppermute | solution.py:467
  42.3 1.3 %collective-permute-start.8 = (bf16[128,128]{1,0:T(8,128)(2,1)S(1)}, bf16[128,128]{1,0:T(8,128)(2,1)S(1)}, u32[]{:S(2)}, u32[]{:S(2)}) collective-permute-start(bf16[128,128]{1,0:T(8,128)(2,1)S(1)} %get-tuple-element.24.refs_3_.refs_0_), channel_id=1, source_target_pairs={{0,3},{1,0},{2,1},{3,2},{4,7},{5,4},{6,5},{7,6},{8,11},{9,8},{10,9... | collective-permute-start | bytes 98312 | tf_op jit(solution)/shard_map/ppermute | solution.py:500
  43.6 1.3 %collective-permute-start.6 = (bf16[128,128]{1,0:T(8,128)(2,1)S(1)}, bf16[128,128]{1,0:T(8,128)(2,1)S(1)}, u32[]{:S(2)}, u32[]{:S(2)}) collective-permute-start(bf16[128,128]{1,0:T(8,128)(2,1)S(1)} %get-tuple-element.24.refs_3_.refs_0_), channel_id=1, source_target_pairs={{0,1},{1,2},{2,3},{3,0},{4,5},{5,6},{6,7},{7,4},{8,9},{9,10},{10,1... | collective-permute-start | bytes 98312 | tf_op jit(solution)/shard_map/ppermute | solution.py:500
  45.0 3.0 %collective-permute-done.9.refs_0_ = bf16[256,1024]{1,0:T(8,128)(2,1)S(1)} collective-permute-done((bf16[256,1024]{1,0:T(8,128)(2,1)S(1)}, bf16[256,1024]{1,0:T(8,128)(2,1)S(1)}, u32[]{:S(2)}, u32[]{:S(2)}) %collective-permute-start.9) | collective-permute-done | bytes 524320 | tf_op jit(solution)/shard_map/ppermute | solution.py:467
  47.9 2.1 %hop.8.refs_6_ = bf16[256,1024]{1,0:T(8,128)(2,1)S(1)} custom-call(bf16[256,1024]{1,0:T(8,128)(2,1)S(1)} %collective-permute-done.9.refs_0_, bf16[256,1024]{1,0:T(8,128)(2,1)S(1)} %copy-done.1, bf16[1024,8192]{1,0:T(8,128)(2,1)} %refs_7_.1), custom_call_target="tpu_custom_call" | custom-call | flops 1 | bytes 1 | tf_op jit(solution)/shard_map/hop/pallas_call | solution.py:262
  50.1 3.5 %collective-permute-start.14 = (bf16[256,1024]{1,0:T(8,128)(2,1)S(1)}, bf16[256,1024]{1,0:T(8,128)(2,1)S(1)}, u32[]{:S(2)}, u32[]{:S(2)}) collective-permute-start(bf16[256,1024]{1,0:T(8,128)(2,1)S(1)} %hop.8.refs_6_), channel_id=1, source_target_pairs={{0,2},{2,3},{3,1},{1,0},{4,6},{6,7},{7,5},{5,4},{8,10},{10,11},{11... | collective-permute-start | bytes 1572872 | tf_op jit(solution)/shard_map/ppermute | solution.py:467
  53.6 6.3 %collective-permute-done.8.refs_3_ = bf16[128,128]{1,0:T(8,128)(2,1)S(1)} collective-permute-done((bf16[128,128]{1,0:T(8,128)(2,1)S(1)}, bf16[128,128]{1,0:T(8,128)(2,1)S(1)}, u32[]{:S(2)}, u32[]{:S(2)}) %collective-permute-start.8) | collective-permute-done | bytes 32800 | tf_op jit(solution)/shard_map/ppermute | solution.py:500
  59.9 13.9 %collective-permute-done.7.refs_2_ = bf16[128,128]{1,0:T(8,128)(2,1)S(1)} collective-permute-done((bf16[128,128]{1,0:T(8,128)(2,1)S(1)}, bf16[128,128]{1,0:T(8,128)(2,1)S(1)}, u32[]{:S(2)}, u32[]{:S(2)}) %collective-permute-start.7) | collective-permute-done | bytes 32800 | tf_op jit(solution)/shard_map/ppermute | solution.py:500
  73.8 0.8 up.1
  74.7 2.2 %hop.9.refs_8_ = bf16[256,1024]{1,0:T(8,128)(2,1)S(1)} custom-call(bf16[256,1024]{1,0:T(8,128)(2,1)S(1)} %collective-permute-done.5.refs_0_, bf16[256,1024]{1,0:T(8,128)(2,1)S(1)} %copy-done.1, bf16[1024,8192]{1,0:T(8,128)(2,1)} %refs_7_.1, bf16[64,2048]{1,0:T(8,128)(2,1)S(1)} %get-tuple-element.26.refs_3_.refs_0_), custom_call_target="tpu_custom_call" | custom-call | flops 1 | bytes 1 | tf_op jit(solution)/shard_map/hop/pallas_call | solution.py:262
  76.9 1.6 %collective-permute-start.10 = (bf16[256,1024]{1,0:T(8,128)(2,1)S(1)}, bf16[256,1024]{1,0:T(8,128)(2,1)S(1)}, u32[]{:S(2)}, u32[]{:S(2)}) collective-permute-start(bf16[256,1024]{1,0:T(8,128)(2,1)S(1)} %hop.9.refs_8_), channel_id=1, source_target_pairs={{0,2},{2,3},{3,1},{1,0},{4,6},{6,7},{7,5},{5,4},{8,10},{10,11},{11... | collective-permute-start | bytes 1572872 | tf_op jit(solution)/shard_map/ppermute | solution.py:467
  78.5 1.5 %collective-permute-start.12 = (bf16[64,2048]{1,0:T(8,128)(2,1)S(1)}, bf16[64,2048]{1,0:T(8,128)(2,1)S(1)}, u32[]{:S(2)}, u32[]{:S(2)}) collective-permute-start(bf16[64,2048]{1,0:T(8,128)(2,1)S(1)} %get-tuple-element.28), channel_id=1, source_target_pairs={{0,8},{4,12},{8,0},{12,4},{1,9},{5,13},{9,1},{13,5},{2,10},{6,14},... | collective-permute-start | bytes 786440 | tf_op jit(solution)/shard_map/ppermute | solution.py:471
  80.4 7.2 %collective-permute-done.12.refs_2_ = bf16[64,2048]{1,0:T(8,128)(2,1)S(1)} collective-permute-done((bf16[64,2048]{1,0:T(8,128)(2,1)S(1)}, bf16[64,2048]{1,0:T(8,128)(2,1)S(1)}, u32[]{:S(2)}, u32[]{:S(2)}) %collective-permute-start.12) | collective-permute-done | bytes 262176 | tf_op jit(solution)/shard_map/ppermute | solution.py:471
  87.6 4.8 %collective-permute-done.13.refs_3_ = bf16[64,2048]{1,0:T(8,128)(2,1)S(1)} collective-permute-done((bf16[64,2048]{1,0:T(8,128)(2,1)S(1)}, bf16[64,2048]{1,0:T(8,128)(2,1)S(1)}, u32[]{:S(2)}, u32[]{:S(2)}) %collective-permute-start.13) | collective-permute-done | bytes 262176 | tf_op jit(solution)/shard_map/ppermute | solution.py:471
  92.5 4.6 %settle.1.settled_ref = f32[256,2048]{1,0:T(8,128)} custom-call(bf16[64,2048]{1,0:T(8,128)(2,1)S(1)} %get-tuple-element.26.refs_3_.refs_0_, bf16[64,2048]{1,0:T(8,128)(2,1)S(1)} %collective-permute-done.11.refs_1_, bf16[64,2048]{1,0:T(8,128)(2,1)S(1)} %collective-permute-done.12.refs_2_, bf16[64,2048]{1,0:T(8,128)(2,1)S(1)} %collective-permute-done.13.refs_3_, ...), custom_call_target="tpu_custom_call" | custom-call | flops 1 | bytes 1 | tf_op jit(solution)/shard_map/settle/pallas_call | solution.py:408
  97.1 1.6 %copy-done.2 = f32[256,2048]{1,0:T(8,128)S(1)} copy-done((f32[256,2048]{1,0:T(8,128)S(1)}, f32[256,2048]{1,0:T(8,128)}, u32[]{:S(2)}) %copy-start.2) | copy-done | bytes 2097176
  98.7 1.0 finish.2.refs_0_
  99.7 1.0 finish.3
  (26 shorter events, 0.8 us)
Async XLA Ops:
  8.8 18.5 %collective-permute-start.4 = (bf16[256,1024]{1,0:T(8,128)(2,1)}, bf16[256,1024]{1,0:T(8,128)(2,1)S(1)}, u32[]{:S(2)}, u32[]{:S(2)}) collective-permute-start(bf16[256,1024]{1,0:T(8,128)(2,1)} %get-tuple-element.23), channel_id=1, source_target_pairs={{0,2},{2,3},{3,1},{1,0},{4,6},{6,7},{7,5},{5,4},{8,10},{10,11},{11... | collective-permute-start | bytes 1572872 | tf_op jit(solution)/shard_map/ppermute | solution.py:467
  12.9 1.0 %copy-start = (bf16[256,1024]{1,0:T(8,128)(2,1)S(1)}, bf16[256,1024]{1,0:T(8,128)(2,1)}, u32[]{:S(2)}) copy-start(bf16[256,1024]{1,0:T(8,128)(2,1)} %get-tuple-element.18.refs_0_.refs_1_.refs_5_) | copy-start | bytes 1572868
  13.9 3.8 %copy-start.6 = (s32[256]{0:T(256)S(1)}, s32[256]{0:T(256)}, u32[]{:S(2)}) copy-start(s32[256]{0:T(256)} %param.23) | copy-start | bytes 3076
  13.9 3.8 %copy-start.7 = (s32[32]{0:T(128)S(1)}, s32[32]{0:T(128)}, u32[]{:S(2)}) copy-start(s32[32]{0:T(128)} %param.22) | copy-start | bytes 388
  16.1 20.6 %collective-permute-start = (bf16[256,1024]{1,0:T(8,128)(2,1)S(1)}, bf16[256,1024]{1,0:T(8,128)(2,1)S(1)}, u32[]{:S(2)}, u32[]{:S(2)}) collective-permute-start(bf16[256,1024]{1,0:T(8,128)(2,1)S(1)} %hop.5.refs_3_), channel_id=1, source_target_pairs={{0,2},{2,3},{3,1},{1,0},{4,6},{6,7},{7,5},{5,4},{8,10},{10,11},{11... | collective-permute-start | bytes 1572872 | tf_op jit(solution)/shard_map/ppermute | solution.py:467
  18.3 1.9 %collective-permute-start.1 = (bf16[64,1152]{1,0:T(8,128)(2,1)S(1)}, bf16[64,1152]{1,0:T(8,128)(2,1)S(1)}, u32[]{:S(2)}, u32[]{:S(2)}) collective-permute-start(bf16[64,1152]{1,0:T(8,128)(2,1)S(1)} %get-tuple-element.20), channel_id=1, source_target_pairs={{0,4},{4,0},{8,12},{12,8},{1,5},{5,1},{9,13},{13,9},{2,6},{6,2},{1... | collective-permute-start | bytes 442376 | tf_op jit(solution)/shard_map/ppermute | solution.py:471
  18.3 6.7 %collective-permute-start.2 = (bf16[64,1152]{1,0:T(8,128)(2,1)S(1)}, bf16[64,1152]{1,0:T(8,128)(2,1)S(1)}, u32[]{:S(2)}, u32[]{:S(2)}) collective-permute-start(bf16[64,1152]{1,0:T(8,128)(2,1)S(1)} %get-tuple-element.21), channel_id=1, source_target_pairs={{0,8},{4,12},{8,0},{12,4},{1,9},{5,13},{9,1},{13,5},{2,10},{6,14},... | collective-permute-start | bytes 442376 | tf_op jit(solution)/shard_map/ppermute | solution.py:471
  19.9 7.4 %collective-permute-start.3 = (bf16[64,1152]{1,0:T(8,128)(2,1)S(1)}, bf16[64,1152]{1,0:T(8,128)(2,1)S(1)}, u32[]{:S(2)}, u32[]{:S(2)}) collective-permute-start(bf16[64,1152]{1,0:T(8,128)(2,1)S(1)} %get-tuple-element.22), channel_id=1, source_target_pairs={{0,12},{4,8},{8,4},{12,0},{1,13},{5,9},{9,5},{13,1},{2,14},{6,10},... | collective-permute-start | bytes 442376 | tf_op jit(solution)/shard_map/ppermute | solution.py:471
  27.3 3.8 %copy-start.4 = (bf16[8,64,1024]{2,1,0:T(8,128)(2,1)S(1)}, bf16[8,64,1024]{2,1,0:T(8,128)(2,1)}, u32[]{:S(2)}) copy-start(bf16[8,64,1024]{2,1,0:T(8,128)(2,1)} %refs_4_.1) | copy-start | bytes 3145732
  29.6 7.1 %copy-start.1 = (bf16[256,1024]{1,0:T(8,128)(2,1)S(1)}, bf16[256,1024]{1,0:T(8,128)(2,1)}, u32[]{:S(2)}) copy-start(bf16[256,1024]{1,0:T(8,128)(2,1)} %get-tuple-element.18.refs_0_.refs_1_.refs_5_) | copy-start | bytes 1572868
  29.6 18.4 %collective-permute-start.9 = (bf16[256,1024]{1,0:T(8,128)(2,1)S(1)}, bf16[256,1024]{1,0:T(8,128)(2,1)S(1)}, u32[]{:S(2)}, u32[]{:S(2)}) collective-permute-start(bf16[256,1024]{1,0:T(8,128)(2,1)S(1)} %hop.6.refs_5_), channel_id=1, source_target_pairs={{0,2},{2,3},{3,1},{1,0},{4,6},{6,7},{7,5},{5,4},{8,10},{10,11},{11... | collective-permute-start | bytes 1572872 | tf_op jit(solution)/shard_map/ppermute | solution.py:467
  38.8 35.0 %copy-start.3 = (bf16[8,64,2048]{2,1,0:T(8,128)(2,1)S(1)}, bf16[8,64,2048]{2,1,0:T(8,128)(2,1)}, u32[]{:S(2)}) copy-start(bf16[8,64,2048]{2,1,0:T(8,128)(2,1)} %refs_5_.1) | copy-start | bytes 6291460
  38.8 35.8 %collective-permute-start.5 = (bf16[256,1024]{1,0:T(8,128)(2,1)S(1)}, bf16[256,1024]{1,0:T(8,128)(2,1)S(1)}, u32[]{:S(2)}, u32[]{:S(2)}) collective-permute-start(bf16[256,1024]{1,0:T(8,128)(2,1)S(1)} %hop.7), channel_id=1, source_target_pairs={{0,2},{2,3},{3,1},{1,0},{4,6},{6,7},{7,5},{5,4},{8,10},{10,11},{11... | collective-permute-start | bytes 1572872 | tf_op jit(solution)/shard_map/ppermute | solution.py:467
  42.3 17.6 %collective-permute-start.8 = (bf16[128,128]{1,0:T(8,128)(2,1)S(1)}, bf16[128,128]{1,0:T(8,128)(2,1)S(1)}, u32[]{:S(2)}, u32[]{:S(2)}) collective-permute-start(bf16[128,128]{1,0:T(8,128)(2,1)S(1)} %get-tuple-element.24.refs_3_.refs_0_), channel_id=1, source_target_pairs={{0,3},{1,0},{2,1},{3,2},{4,7},{5,4},{6,5},{7,6},{8,11},{9,8},{10,9... | collective-permute-start | bytes 98312 | tf_op jit(solution)/shard_map/ppermute | solution.py:500
  43.6 30.2 %collective-permute-start.7 = (bf16[128,128]{1,0:T(8,128)(2,1)S(1)}, bf16[128,128]{1,0:T(8,128)(2,1)S(1)}, u32[]{:S(2)}, u32[]{:S(2)}) collective-permute-start(bf16[128,128]{1,0:T(8,128)(2,1)S(1)} %get-tuple-element.24.refs_3_.refs_0_), channel_id=1, source_target_pairs={{0,2},{1,3},{2,0},{3,1},{4,6},{5,7},{6,4},{7,5},{8,10},{9,11},{10,... | collective-permute-start | bytes 98312 | tf_op jit(solution)/shard_map/ppermute | solution.py:500
  43.6 30.2 %collective-permute-start.6 = (bf16[128,128]{1,0:T(8,128)(2,1)S(1)}, bf16[128,128]{1,0:T(8,128)(2,1)S(1)}, u32[]{:S(2)}, u32[]{:S(2)}) collective-permute-start(bf16[128,128]{1,0:T(8,128)(2,1)S(1)} %get-tuple-element.24.refs_3_.refs_0_), channel_id=1, source_target_pairs={{0,1},{1,2},{2,3},{3,0},{4,5},{5,6},{6,7},{7,4},{8,9},{9,10},{10,1... | collective-permute-start | bytes 98312 | tf_op jit(solution)/shard_map/ppermute | solution.py:500
  50.1 47.0 %collective-permute-start.14 = (bf16[256,1024]{1,0:T(8,128)(2,1)S(1)}, bf16[256,1024]{1,0:T(8,128)(2,1)S(1)}, u32[]{:S(2)}, u32[]{:S(2)}) collective-permute-start(bf16[256,1024]{1,0:T(8,128)(2,1)S(1)} %hop.8.refs_6_), channel_id=1, source_target_pairs={{0,2},{2,3},{3,1},{1,0},{4,6},{6,7},{7,5},{5,4},{8,10},{10,11},{11... | collective-permute-start | bytes 1572872 | tf_op jit(solution)/shard_map/ppermute | solution.py:467
  74.7 17.8 %copy-start.5 = (bf16[256,2048]{1,0:T(8,128)(2,1)S(1)}, bf16[256,2048]{1,0:T(8,128)(2,1)}, u32[]{:S(2)}) copy-start(bf16[256,2048]{1,0:T(8,128)(2,1)} %refs_6_.1) | copy-start | bytes 3145732
  76.9 22.8 %collective-permute-start.10 = (bf16[256,1024]{1,0:T(8,128)(2,1)S(1)}, bf16[256,1024]{1,0:T(8,128)(2,1)S(1)}, u32[]{:S(2)}, u32[]{:S(2)}) collective-permute-start(bf16[256,1024]{1,0:T(8,128)(2,1)S(1)} %hop.9.refs_8_), channel_id=1, source_target_pairs={{0,2},{2,3},{3,1},{1,0},{4,6},{6,7},{7,5},{5,4},{8,10},{10,11},{11... | collective-permute-start | bytes 1572872 | tf_op jit(solution)/shard_map/ppermute | solution.py:467
  78.5 1.9 %collective-permute-start.11 = (bf16[64,2048]{1,0:T(8,128)(2,1)S(1)}, bf16[64,2048]{1,0:T(8,128)(2,1)S(1)}, u32[]{:S(2)}, u32[]{:S(2)}) collective-permute-start(bf16[64,2048]{1,0:T(8,128)(2,1)S(1)} %get-tuple-element.27), channel_id=1, source_target_pairs={{0,4},{4,0},{8,12},{12,8},{1,5},{5,1},{9,13},{13,9},{2,6},{6,2},{1... | collective-permute-start | bytes 786440 | tf_op jit(solution)/shard_map/ppermute | solution.py:471
  78.5 9.1 %collective-permute-start.12 = (bf16[64,2048]{1,0:T(8,128)(2,1)S(1)}, bf16[64,2048]{1,0:T(8,128)(2,1)S(1)}, u32[]{:S(2)}, u32[]{:S(2)}) collective-permute-start(bf16[64,2048]{1,0:T(8,128)(2,1)S(1)} %get-tuple-element.28), channel_id=1, source_target_pairs={{0,8},{4,12},{8,0},{12,4},{1,9},{5,13},{9,1},{13,5},{2,10},{6,14},... | collective-permute-start | bytes 786440 | tf_op jit(solution)/shard_map/ppermute | solution.py:471
  80.0 12.5 %collective-permute-start.13 = (bf16[64,2048]{1,0:T(8,128)(2,1)S(1)}, bf16[64,2048]{1,0:T(8,128)(2,1)S(1)}, u32[]{:S(2)}, u32[]{:S(2)}) collective-permute-start(bf16[64,2048]{1,0:T(8,128)(2,1)S(1)} %get-tuple-element.29), channel_id=1, source_target_pairs={{0,12},{4,8},{8,4},{12,0},{1,13},{5,9},{9,5},{13,1},{2,14},{6,10},... | collective-permute-start | bytes 786440 | tf_op jit(solution)/shard_map/ppermute | solution.py:471
  97.1 1.6 %copy-start.2 = (f32[256,2048]{1,0:T(8,128)S(1)}, f32[256,2048]{1,0:T(8,128)}, u32[]{:S(2)}) copy-start(f32[256,2048]{1,0:T(8,128)} %settle.1.settled_ref) | copy-start | bytes 6291460

commit v5 on v4

--- a/solution.py
+++ b/solution.py
@@ -14,8 +14,8 @@
 MASKED = -1e30
 VMEM_LIMIT = 50 * 1024 * 1024
 FULL_VMEM = 61 * 1024 * 1024
-CHAINS = 2
-PIECE = 512
+SHARES = (5, 3)
+PIECE = 256
 SPLIT = 2
 
 VMEM = pl.BlockSpec(memory_space=pltpu.VMEM)
@@ -47,10 +47,19 @@
     return jnp.where(2 * spot < count, 2 * spot, 2 * (count - spot) - 1)
 
 
+def chain_columns(width):
+    unit = width // sum(SHARES)
+    return [(sum(SHARES[:c]) * unit, SHARES[c] * unit) for c in range(len(SHARES))]
+
+
+def piece_of(width):
+    return math.gcd(width, PIECE)
+
+
 class Weights:
     def __init__(self, w_ref, held, sems, first, width):
         depth = w_ref.shape[0] // SPLIT
-        self.piece = min(PIECE, width)
+        self.piece = piece_of(width)
         self.held = held
         self.copies = []
         for p in range(width // self.piece):
@@ -79,7 +88,7 @@
 
     @staticmethod
     def scratch(depth, width):
-        piece = min(PIECE, width)
+        piece = piece_of(width)
         count = width // piece
         return [
             pltpu.VMEM((count, depth, piece), jnp.bfloat16),
@@ -88,7 +97,7 @@
 
 
 def attend_kernel(
-    heads, kv, cache, steps,
+    heads, kv, cache, steps, block,
     len_ref, q_hbm, k_hbm, v_hbm, nk_hbm, nv_hbm, w_hbm,
     a_ref, out_ref,
     q_ref, k_ref, v_ref, nk_ref, nv_ref, scores_ref, mixed_ref, sems, fresh_sems, w_held, w_sems,
@@ -116,7 +125,7 @@
         for i, (source, target) in enumerate(((nk_hbm, nk_ref), (nv_hbm, nv_ref)))
     ]
     chunk = out_ref.shape[1]
-    first = column_owner(0) * (CHAINS * chunk)
+    first = column_owner(0) * block
     weights = Weights(w_hbm, w_held, w_sems, first, chunk)
     part(0, 0).start()
     part(1, 0).start()
@@ -202,14 +211,15 @@
         out_ref[:, columns] = product.astype(jnp.bfloat16)
 
 
-def attend(query, keys, values, new_key, new_value, lengths, weight, chunk):
+def attend(query, keys, values, new_key, new_value, lengths, weight, block):
     requests, heads, width = query.shape
     cache, kv = keys.shape[1], keys.shape[2]
     steps = 4
     per = requests // steps
     columns = GROUP * cache * kv + per * kv
-    return pl.pallas_call(
-        functools.partial(attend_kernel, heads, kv, cache, steps),
+    chunk = chain_columns(block)[0][1]
+    return pl.pallas_call(
+        functools.partial(attend_kernel, heads, kv, cache, steps, block),
         in_specs=[VMEM] + [ANY] * 6,
         out_specs=[VMEM, VMEM],
         out_shape=[
@@ -241,13 +251,13 @@
     )
 
 
-def hop_kernel(step, chain, arriving, after, *refs):
+def hop_kernel(step, block, start, arriving, after, *refs):
     if arriving:
         arrived_ref, *refs = refs
     a_ref, w_hbm, *refs = refs
     out_ref, held, sems = refs[after:]
     chunk = out_ref.shape[1]
-    first = column_owner(step) * (CHAINS * chunk) + chain * chunk
+    first = column_owner(step) * block + start
     weights = Weights(w_hbm, held, sems, first, chunk)
     weights.start()
     for columns, product in weights.products(a_ref[...]):
@@ -256,11 +266,12 @@
         out_ref[:, columns] = product.astype(jnp.bfloat16)
 
 
-def hop(step, chain, arrived, attended, weight, chunk, after=()):
+def hop(step, chain, arrived, attended, weight, block, after=()):
     arriving = arrived is not None
+    start, chunk = chain_columns(block)[chain]
     operands = ([arrived] if arriving else []) + [attended, weight, *after]
     return pl.pallas_call(
-        functools.partial(hop_kernel, step, chain, arriving, len(after)),
+        functools.partial(hop_kernel, step, block, start, arriving, len(after)),
         in_specs=[VMEM] * (1 + arriving) + [ANY] + [ANY] * len(after),
         out_specs=VMEM,
         out_shape=jax.ShapeDtypeStruct((attended.shape[0], chunk), jnp.bfloat16),
@@ -422,19 +433,20 @@
 
 
 def finish(chain, arrived, settled, earlier):
-    rows, chunk = arrived.shape
-    piece = min(PIECE, chunk)
-    count = chunk // piece
+    rows = arrived.shape[0]
+    start, chunk = chain_columns(settled.shape[1])[chain]
+    piece = math.gcd(start, chunk)
+    first, count = start // piece, chunk // piece
     operands = [arrived, settled] + ([earlier] if earlier is not None else [])
     return pl.pallas_call(
         finish_kernel,
         grid=(count,),
         in_specs=[
             pl.BlockSpec((rows, piece), lambda i: (0, i)),
-            pl.BlockSpec((rows, piece), lambda i: (0, chain * count + i)),
+            pl.BlockSpec((rows, piece), lambda i: (0, first + i)),
         ]
         + ([ANY] if earlier is not None else []),
-        out_specs=pl.BlockSpec((rows, piece), lambda i: (0, chain * count + i)),
+        out_specs=pl.BlockSpec((rows, piece), lambda i: (0, first + i)),
         out_shape=jax.ShapeDtypeStruct(settled.shape, jnp.bfloat16),
         input_output_aliases={2: 0} if earlier is not None else {},
         compiler_params=PARAMS,
@@ -459,12 +471,9 @@
 ):
     count = lax.axis_size("tensor")
     replicas = lax.axis_size("dp")
-    chunk = residual.shape[1] // CHAINS
+    block = residual.shape[1]
     order = ring_order(count)
     ring = [(order[p], order[(p + 1) % count]) for p in range(count)]
-
-    def forward(x):
-        return lax.ppermute(x, "tensor", ring)
 
     def exchange(blocks):
         moved = [
@@ -473,47 +482,39 @@
         ]
         return [blocks[0]] + moved
 
+    def next_hop(step, chain, after):
+        arrived = lax.ppermute(travelling[chain], "tensor", ring)
+        travelling[chain] = hop(step, chain, arrived, attended, output_weight, block, after)
+
     attended, first = attend(
         query, cached_key_rows, cached_value_rows, new_token_key, new_token_value, lengths,
-        output_weight, chunk,
-    )
-    travelling = [first] + [
-        hop(0, c, None, attended, output_weight, chunk) for c in range(1, CHAINS)
+        output_weight, block,
+    )
+    chosen, *leaving = route(
+        attended, request_adapter, placement, replicas, slot_down_weight.shape[0]
+    )
+    rows_here = exchange(leaving)
+    mid, inside = down(rows_here, slot_down_weight)
+    rank_sums = [mid] + [
+        lax.ppermute(mid, "tensor", [(i, (i + k) % count) for i in range(count)])
+        for k in range(1, count)
     ]
-    chosen, *leaving = route(
-        attended, request_adapter, placement, replicas, slot_down_weight.shape[0],
-        after=travelling[1:],
-    )
-    rows_here = exchange(leaving)
-
-    def take_hop(step, c, after):
-        arrived = forward(travelling[c])
-        travelling[c] = hop(step, c, arrived, attended, output_weight, chunk, after=after)
-
-    rank_sums = deltas = returned = None
-    for step in range(1, count - 1):
-        for c in range(CHAINS):
-            if step == 1 and c == 0:
-                take_hop(step, c, rows_here)
-                mid, inside = down(rows_here, slot_down_weight, after=[travelling[c]])
-                rank_sums = [mid] + [
-                    lax.ppermute(mid, "tensor", [(i, (i + k) % count) for i in range(count)])
-                    for k in range(1, count)
-                ]
-            elif step == 1:
-                take_hop(step, c, [mid])
-            elif step == 2 and c == 0:
-                take_hop(step, c, [])
-                deltas = up(rank_sums, inside, slot_up_weight, after=[travelling[c]])
-                returned = exchange(deltas)
-            else:
-                take_hop(step, c, [deltas[0]])
+
+    travelling = [first, hop(0, 1, None, attended, output_weight, block, after=[mid])]
+    next_hop(1, 0, after=rank_sums + travelling[1:])
+    next_hop(1, 1, after=())
+    deltas = up(rank_sums, inside, slot_up_weight, after=[travelling[1]])
+    returned = exchange(deltas)
+    for step in range(2, count - 1):
+        for chain in range(2):
+            next_hop(step, chain, after=returned if (step, chain) == (2, 0) else ())
     settled = settle(
-        count - 1, returned, chosen, attended, residual, output_weight, after=[travelling[-1]]
+        count - 1, returned, chosen, attended, residual, output_weight, after=[travelling[1]]
     )
     out = None
-    for c in range(CHAINS):
-        out = finish(c, forward(travelling[c]), settled, out)
+    for chain in range(2):
+        arrived = lax.ppermute(travelling[chain], "tensor", ring)
+        out = finish(chain, arrived, settled, out)
     return out
 
 

time: 101 us -> 90.3 us (0.89)
  waiting for transfers between devices: 47.3 us -> 31.9 us
  Pallas kernels: 28.2 us -> 34.1 us
  starting transfers between devices: 22.3 us -> 21.1 us
    ppermute x3, waiting for transfers between devices: 20.2 us -> 0.01 us  [per_device(): lax.ppermute(mid, 'tensor', [(i, (i + k) % count) for i in range(count)])]
    ppermute x6, waiting for transfers between devices: 7.88 us -> 18.2 us  [the longest x2 9.23 us: per_device(): arrived = lax.ppermute(travelling[chain], 'tensor', ring)]
    ppermute x6, waiting for transfers between devices: 19.2 us -> 13.7 us  [exchange(): lax.ppermute(blocks[r], 'dp', [(i, i ^ r) for i in range(replicas)])]
    pallas_call x6, Pallas kernels: 19.7 us -> 23.6 us  [the longest x5 13.1 us: hop(): pl.pallas_call(functools.partial(hop_kernel, step, block, start, arriving...]
    ppermute x6, starting transfers between devices: 15.8 us -> 12.4 us  [the longest x4 7.85 us: next_hop(): arrived = lax.ppermute(travelling[chain], 'tensor', ring)]
    ppermute x3, starting transfers between devices: 2.7 us -> 4.54 us  [per_device(): lax.ppermute(mid, 'tensor', [(i, (i + k) % count) for i in range(count)])]
    pallas_call x1, Pallas kernels: 4.61 us -> 6.12 us  [settle(): pl.pallas_call(functools.partial(settle_kernel, step, replicas, len(after...]
  transfers between devices with their start and end apart: 15 -> 15, of which waited for: 8 -> 8; matrix products, arithmetic and copies ran while one was open for 0% -> 0% of each run, Pallas kernels for 18% -> 25%
where the time goes in v5:
time: 90.3 us; the launch traced here: 90 us
  Pallas kernels  34.1 us (38%)
  waiting for transfers between devices  31.9 us (35%)
  starting transfers between devices  21.1 us (23%)
  local copies, waits for them, and re-layouts  2.66 us (3%)
    ppermute x6, waiting for transfers between devices, exchange(): lax.ppermute(blocks[r], 'dp', [(i, i ^ r) for i in range(replicas)])  13.7 us
    pallas_call x5, Pallas kernels, hop(): pl.pallas_call(functools.partial(hop_kernel, step, block, start, arriving...  13.1 us
    pallas_call x1, Pallas kernels, attend(): pl.pallas_call(functools.partial(attend_kernel, heads, kv, cache, steps,...  10.5 us
    ppermute x2, waiting for transfers between devices, per_device(): arrived = lax.ppermute(travelling[chain], 'tensor', ring)  9.23 us
    ppermute x4, waiting for transfers between devices, next_hop(): arrived = lax.ppermute(travelling[chain], 'tensor', ring)  9.01 us
    ppermute x4, starting transfers between devices, next_hop(): arrived = lax.ppermute(travelling[chain], 'tensor', ring)  7.85 us
    pallas_call x1, Pallas kernels, settle(): pl.pallas_call(functools.partial(settle_kernel, step, replicas, len(after...  6.12 us
    ppermute x2, starting transfers between devices, per_device(): arrived = lax.ppermute(travelling[chain], 'tensor', ring)  4.58 us
  transfers between devices with their start and end apart: 15, of which 8 were waited for; matrix products, arithmetic and copies ran while one was open for 0% of the time, Pallas kernels for 25%

profile of v5, /device:TPU:0, one launch (start us, length us, event | category | flops | bytes accessed | tf_op | source)
XLA Modules:
  0.0 90.0 jit_solution(15807299717204876456)
XLA Ops:
  0.0 10.5 %attend.1 = (bf16[256,1024]{1,0:T(8,128)(2,1)}, bf16[256,1280]{1,0:T(8,128)(2,1)}) custom-call(s32[1,256]{1,0:T(1,128)} %bitcast.15, bf16[2048,128]{1,0:T(8,128)(2,1)} %bitcast.12, bf16[8192,128]{1,0:T(8,128)(2,1)} %bitcast.10, bf16[8192,128]{1,0:T(8,128)(2,1)} %bitcast.11, bf16[512,128]{1,0:T(8,128)(2,1)} %bitcast.13, bf16[512,128]{1,0:T(8,128)(2,1)} %bitcast.14, ...), custom_call_target="tpu_custom_call" | custom-call | tf_op jit(solution)/shard_map/attend/pallas_call | solution.py:221
  10.5 4.1 %collective-permute-start.12 = (bf16[256,1280]{1,0:T(8,128)(2,1)}, bf16[256,1280]{1,0:T(8,128)(2,1)S(1)}, u32[]{:S(2)}, u32[]{:S(2)}) collective-permute-start(bf16[256,1280]{1,0:T(8,128)(2,1)} %get-tuple-element.30), channel_id=1, source_target_pairs={{0,2},{2,3},{3,1},{1,0},{4,6},{6,7},{7,5},{5,4},{8,10},{10,11},{11... | collective-permute-start | bytes 1966088 | tf_op jit(solution)/shard_map/ppermute | solution.py:486
  14.6 1.0 %copy-done = bf16[256,1024]{1,0:T(8,128)(2,1)S(1)} copy-done((bf16[256,1024]{1,0:T(8,128)(2,1)S(1)}, bf16[256,1024]{1,0:T(8,128)(2,1)}, u32[]{:S(2)}) %copy-start) | copy-done | bytes 524312
  15.7 0.6 route.1
  16.3 1.6 %collective-permute-start.1 = (bf16[64,1152]{1,0:T(8,128)(2,1)S(1)}, bf16[64,1152]{1,0:T(8,128)(2,1)S(1)}, u32[]{:S(2)}, u32[]{:S(2)}) collective-permute-start(bf16[64,1152]{1,0:T(8,128)(2,1)S(1)} %get-tuple-element.21), channel_id=1, source_target_pairs={{0,8},{4,12},{8,0},{12,4},{1,9},{5,13},{9,1},{13,5},{2,10},{6,14},... | collective-permute-start | bytes 442376 | tf_op jit(solution)/shard_map/ppermute | solution.py:480
  18.2 4.8 %collective-permute-done.1.refs_2_ = bf16[64,1152]{1,0:T(8,128)(2,1)S(1)} collective-permute-done((bf16[64,1152]{1,0:T(8,128)(2,1)S(1)}, bf16[64,1152]{1,0:T(8,128)(2,1)S(1)}, u32[]{:S(2)}, u32[]{:S(2)}) %collective-permute-start.1) | collective-permute-done | bytes 147488 | tf_op jit(solution)/shard_map/ppermute | solution.py:480
  23.0 2.3 %collective-permute-done.2.refs_3_ = bf16[64,1152]{1,0:T(8,128)(2,1)S(1)} collective-permute-done((bf16[64,1152]{1,0:T(8,128)(2,1)S(1)}, bf16[64,1152]{1,0:T(8,128)(2,1)S(1)}, u32[]{:S(2)}, u32[]{:S(2)}) %collective-permute-start.2) | collective-permute-done | bytes 147488 | tf_op jit(solution)/shard_map/ppermute | solution.py:480
  25.3 0.6 down.1
  26.0 1.9 %collective-permute-start.7 = (bf16[128,128]{1,0:T(8,128)(2,1)S(1)}, bf16[128,128]{1,0:T(8,128)(2,1)S(1)}, u32[]{:S(2)}, u32[]{:S(2)}) collective-permute-start(bf16[128,128]{1,0:T(8,128)(2,1)S(1)} %get-tuple-element.23.refs_2_.refs_0_.refs_3_), channel_id=1, source_target_pairs={{0,2},{1,3},{2,0},{3,1},{4,6},{5,7},{6,4},{7,5},{8,10},{9,11},{10,... | collective-permute-start | bytes 98312 | tf_op jit(solution)/shard_map/ppermute | solution.py:499
  27.9 2.6 %collective-permute-start.8 = (bf16[128,128]{1,0:T(8,128)(2,1)S(1)}, bf16[128,128]{1,0:T(8,128)(2,1)S(1)}, u32[]{:S(2)}, u32[]{:S(2)}) collective-permute-start(bf16[128,128]{1,0:T(8,128)(2,1)S(1)} %get-tuple-element.23.refs_2_.refs_0_.refs_3_), channel_id=1, source_target_pairs={{0,3},{1,0},{2,1},{3,2},{4,7},{5,4},{6,5},{7,6},{8,11},{9,8},{10,9... | collective-permute-start | bytes 98312 | tf_op jit(solution)/shard_map/ppermute | solution.py:499
  30.5 2.3 %hop.5.refs_7_ = bf16[256,768]{1,0:T(8,128)(2,1)S(1)} custom-call(bf16[256,1024]{1,0:T(8,128)(2,1)S(1)} %copy-done.1, bf16[1024,8192]{1,0:T(8,128)(2,1)} %refs_2_.7, bf16[128,128]{1,0:T(8,128)(2,1)S(1)} %get-tuple-element.23.refs_2_.refs_0_.refs_3_), custom_call_target="tpu_custom_call" | custom-call | flops 1 | bytes 1 | tf_op jit(solution)/shard_map/hop/pallas_call | solution.py:273
  32.8 1.4 %collective-permute-start.3 = (bf16[256,768]{1,0:T(8,128)(2,1)S(1)}, bf16[256,768]{1,0:T(8,128)(2,1)S(1)}, u32[]{:S(2)}, u32[]{:S(2)}) collective-permute-start(bf16[256,768]{1,0:T(8,128)(2,1)S(1)} %hop.5.refs_7_), channel_id=1, source_target_pairs={{0,2},{2,3},{3,1},{1,0},{4,6},{6,7},{7,5},{5,4},{8,10},{10,11},{11... | collective-permute-start | bytes 1179656 | tf_op jit(solution)/shard_map/ppermute | solution.py:486
  34.2 3.1 %hop.8 = bf16[256,1280]{1,0:T(8,128)(2,1)S(1)} custom-call(bf16[256,1280]{1,0:T(8,128)(2,1)S(1)} %collective-permute-done.12.refs_0_, bf16[256,1024]{1,0:T(8,128)(2,1)S(1)} %copy-done.1, bf16[1024,8192]{1,0:T(8,128)(2,1)} %refs_2_.7, bf16[128,128]{1,0:T(8,128)(2,1)S(1)} %get-tuple-element.23.refs_2_.refs_0_.refs_3_, ...), custom_call_target="tpu_custom_call" | custom-call | flops 1 | bytes 1 | tf_op jit(solution)/shard_map/hop/pallas_call | solution.py:273
  37.5 7.4 %collective-permute-done.3.refs_0_ = bf16[256,768]{1,0:T(8,128)(2,1)S(1)} collective-permute-done((bf16[256,768]{1,0:T(8,128)(2,1)S(1)}, bf16[256,768]{1,0:T(8,128)(2,1)S(1)}, u32[]{:S(2)}, u32[]{:S(2)}) %collective-permute-start.3) | collective-permute-done | bytes 393248 | tf_op jit(solution)/shard_map/ppermute | solution.py:486
  44.8 2.3 %hop.6.refs_6_ = bf16[256,768]{1,0:T(8,128)(2,1)S(1)} custom-call(bf16[256,768]{1,0:T(8,128)(2,1)S(1)} %collective-permute-done.3.refs_0_, bf16[256,1024]{1,0:T(8,128)(2,1)S(1)} %copy-done.1, bf16[1024,8192]{1,0:T(8,128)(2,1)} %refs_2_.7), custom_call_target="tpu_custom_call" | custom-call | flops 1 | bytes 1 | tf_op jit(solution)/shard_map/hop/pallas_call | solution.py:273
  47.1 0.8 up.1
  47.9 1.6 %collective-permute-start.10 = (bf16[64,2048]{1,0:T(8,128)(2,1)S(1)}, bf16[64,2048]{1,0:T(8,128)(2,1)S(1)}, u32[]{:S(2)}, u32[]{:S(2)}) collective-permute-start(bf16[64,2048]{1,0:T(8,128)(2,1)S(1)} %get-tuple-element.27), channel_id=1, source_target_pairs={{0,8},{4,12},{8,0},{12,4},{1,9},{5,13},{9,1},{13,5},{2,10},{6,14},... | collective-permute-start | bytes 786440 | tf_op jit(solution)/shard_map/ppermute | solution.py:480
  49.5 0.6 collective-permute-start.9
  50.2 2.3 %collective-permute-start.4 = (bf16[256,768]{1,0:T(8,128)(2,1)S(1)}, bf16[256,768]{1,0:T(8,128)(2,1)S(1)}, u32[]{:S(2)}, u32[]{:S(2)}) collective-permute-start(bf16[256,768]{1,0:T(8,128)(2,1)S(1)} %hop.6.refs_6_), channel_id=1, source_target_pairs={{0,2},{2,3},{3,1},{1,0},{4,6},{6,7},{7,5},{5,4},{8,10},{10,11},{11... | collective-permute-start | bytes 1179656 | tf_op jit(solution)/shard_map/ppermute | solution.py:486
  52.4 3.9 %collective-permute-done.10.refs_2_.refs_5_ = bf16[64,2048]{1,0:T(8,128)(2,1)S(1)} collective-permute-done((bf16[64,2048]{1,0:T(8,128)(2,1)S(1)}, bf16[64,2048]{1,0:T(8,128)(2,1)S(1)}, u32[]{:S(2)}, u32[]{:S(2)}) %collective-permute-start.10) | collective-permute-done | bytes 262176 | tf_op jit(solution)/shard_map/ppermute | solution.py:480
  56.3 2.7 %collective-permute-done.11.refs_3_.refs_6_ = bf16[64,2048]{1,0:T(8,128)(2,1)S(1)} collective-permute-done((bf16[64,2048]{1,0:T(8,128)(2,1)S(1)}, bf16[64,2048]{1,0:T(8,128)(2,1)S(1)}, u32[]{:S(2)}, u32[]{:S(2)}) %collective-permute-start.11) | collective-permute-done | bytes 262176 | tf_op jit(solution)/shard_map/ppermute | solution.py:480
  59.0 3.1 %hop.9 = bf16[256,1280]{1,0:T(8,128)(2,1)S(1)} custom-call(bf16[256,1280]{1,0:T(8,128)(2,1)S(1)} %collective-permute-done.13.refs_0_, bf16[256,1024]{1,0:T(8,128)(2,1)S(1)} %copy-done.1, bf16[1024,8192]{1,0:T(8,128)(2,1)} %refs_2_.7, bf16[64,2048]{1,0:T(8,128)(2,1)S(1)} %get-tuple-element.25.refs_0_.refs_3_, ...), custom_call_target="tpu_custom_call" | custom-call | flops 1 | bytes 1 | tf_op jit(solution)/shard_map/hop/pallas_call | solution.py:273
  62.1 2.3 %collective-permute-start.14 = (bf16[256,1280]{1,0:T(8,128)(2,1)S(1)}, bf16[256,1280]{1,0:T(8,128)(2,1)S(1)}, u32[]{:S(2)}, u32[]{:S(2)}) collective-permute-start(bf16[256,1280]{1,0:T(8,128)(2,1)S(1)} %hop.9), channel_id=1, source_target_pairs={{0,2},{2,3},{3,1},{1,0},{4,6},{6,7},{7,5},{5,4},{8,10},{10,11},{11... | collective-permute-start | bytes 1966088 | tf_op jit(solution)/shard_map/ppermute | solution.py:516
  64.5 1.6 %collective-permute-done.4.refs_0_ = bf16[256,768]{1,0:T(8,128)(2,1)S(1)} collective-permute-done((bf16[256,768]{1,0:T(8,128)(2,1)S(1)}, bf16[256,768]{1,0:T(8,128)(2,1)S(1)}, u32[]{:S(2)}, u32[]{:S(2)}) %collective-permute-start.4) | collective-permute-done | bytes 393248 | tf_op jit(solution)/shard_map/ppermute | solution.py:486
  66.1 2.3 %hop.7.refs_8_ = bf16[256,768]{1,0:T(8,128)(2,1)S(1)} custom-call(bf16[256,768]{1,0:T(8,128)(2,1)S(1)} %collective-permute-done.4.refs_0_, bf16[256,1024]{1,0:T(8,128)(2,1)S(1)} %copy-done.1, bf16[1024,8192]{1,0:T(8,128)(2,1)} %refs_2_.7), custom_call_target="tpu_custom_call" | custom-call | flops 1 | bytes 1 | tf_op jit(solution)/shard_map/hop/pallas_call | solution.py:273
  68.4 2.3 %collective-permute-start.5 = (bf16[256,768]{1,0:T(8,128)(2,1)S(1)}, bf16[256,768]{1,0:T(8,128)(2,1)S(1)}, u32[]{:S(2)}, u32[]{:S(2)}) collective-permute-start(bf16[256,768]{1,0:T(8,128)(2,1)S(1)} %hop.7.refs_8_), channel_id=1, source_target_pairs={{0,2},{2,3},{3,1},{1,0},{4,6},{6,7},{7,5},{5,4},{8,10},{10,11},{11... | collective-permute-start | bytes 1179656 | tf_op jit(solution)/shard_map/ppermute | solution.py:516
  70.6 6.1 %settle.1.settled_ref = f32[256,2048]{1,0:T(8,128)} custom-call(bf16[64,2048]{1,0:T(8,128)(2,1)S(1)} %get-tuple-element.25.refs_0_.refs_3_, bf16[64,2048]{1,0:T(8,128)(2,1)S(1)} %collective-permute-done.9.refs_1_.refs_4_, bf16[64,2048]{1,0:T(8,128)(2,1)S(1)} %collective-permute-done.10.refs_2_.refs_5_, ...), custom_call_target="tpu_custom_call" | custom-call | flops 1 | bytes 1 | tf_op jit(solution)/shard_map/settle/pallas_call | solution.py:419
  76.8 3.4 %collective-permute-done.14.arrived_ref = bf16[256,1280]{1,0:T(8,128)(2,1)S(1)} collective-permute-done((bf16[256,1280]{1,0:T(8,128)(2,1)S(1)}, bf16[256,1280]{1,0:T(8,128)(2,1)S(1)}, u32[]{:S(2)}, u32[]{:S(2)}) %collective-permute-start.14) | collective-permute-done | bytes 655392 | tf_op jit(solution)/shard_map/ppermute | solution.py:516
  80.1 1.6 %copy-done.2 = f32[256,2048]{1,0:T(8,128)S(1)} copy-done((f32[256,2048]{1,0:T(8,128)S(1)}, f32[256,2048]{1,0:T(8,128)}, u32[]{:S(2)}) %copy-start.2) | copy-done | bytes 2097176
  81.7 0.9 %finish.2.refs_0_ = bf16[256,2048]{1,0:T(8,128)(2,1)} custom-call(bf16[256,1280]{1,0:T(8,128)(2,1)S(1)} %collective-permute-done.14.arrived_ref, f32[256,2048]{1,0:T(8,128)S(1)} %copy-done.2), custom_call_target="tpu_custom_call" | custom-call | flops 1 | bytes 1 | tf_op jit(solution)/shard_map/finish/pallas_call | solution.py:441
  82.7 5.9 %collective-permute-done.5.arrived_ref = bf16[256,768]{1,0:T(8,128)(2,1)S(1)} collective-permute-done((bf16[256,768]{1,0:T(8,128)(2,1)S(1)}, bf16[256,768]{1,0:T(8,128)(2,1)S(1)}, u32[]{:S(2)}, u32[]{:S(2)}) %collective-permute-start.5) | collective-permute-done | bytes 393248 | tf_op jit(solution)/shard_map/ppermute | solution.py:516
  88.5 1.4 %finish.3 = bf16[256,2048]{1,0:T(8,128)(2,1)} custom-call(bf16[256,768]{1,0:T(8,128)(2,1)S(1)} %collective-permute-done.5.arrived_ref, f32[256,2048]{1,0:T(8,128)S(1)} %copy-done.2, bf16[256,2048]{1,0:T(8,128)(2,1)} %finish.2.refs_0_), custom_call_target="tpu_custom_call", output_to_operand_aliasing={{}: (2, {})} | custom-call | flops 1 | bytes 1 | tf_op jit(solution)/shard_map/finish/pallas_call | solution.py:441
  (26 shorter events, 0.6 us)
Async XLA Ops:
  0.0 14.6 %copy-start.6 = (s32[256]{0:T(256)S(1)}, s32[256]{0:T(256)}, u32[]{:S(2)}) copy-start(s32[256]{0:T(256)} %param.23) | copy-start | bytes 3076
  0.0 14.6 %copy-start.7 = (s32[32]{0:T(128)S(1)}, s32[32]{0:T(128)}, u32[]{:S(2)}) copy-start(s32[32]{0:T(128)} %param.22) | copy-start | bytes 388
  0.0 25.3 %copy-start.4 = (bf16[8,64,1024]{2,1,0:T(8,128)(2,1)S(1)}, bf16[8,64,1024]{2,1,0:T(8,128)(2,1)}, u32[]{:S(2)}) copy-start(bf16[8,64,1024]{2,1,0:T(8,128)(2,1)} %refs_4_.1) | copy-start | bytes 3145732
  10.5 23.7 %collective-permute-start.12 = (bf16[256,1280]{1,0:T(8,128)(2,1)}, bf16[256,1280]{1,0:T(8,128)(2,1)S(1)}, u32[]{:S(2)}, u32[]{:S(2)}) collective-permute-start(bf16[256,1280]{1,0:T(8,128)(2,1)} %get-tuple-element.30), channel_id=1, source_target_pairs={{0,2},{2,3},{3,1},{1,0},{4,6},{6,7},{7,5},{5,4},{8,10},{10,11},{11... | collective-permute-start | bytes 1966088 | tf_op jit(solution)/shard_map/ppermute | solution.py:486
  14.6 1.0 %copy-start = (bf16[256,1024]{1,0:T(8,128)(2,1)S(1)}, bf16[256,1024]{1,0:T(8,128)(2,1)}, u32[]{:S(2)}) copy-start(bf16[256,1024]{1,0:T(8,128)(2,1)} %get-tuple-element.18.refs_0_.refs_1_.refs_5_) | copy-start | bytes 1572868
  15.7 14.8 %copy-start.1 = (bf16[256,1024]{1,0:T(8,128)(2,1)S(1)}, bf16[256,1024]{1,0:T(8,128)(2,1)}, u32[]{:S(2)}) copy-start(bf16[256,1024]{1,0:T(8,128)(2,1)} %get-tuple-element.18.refs_0_.refs_1_.refs_5_) | copy-start | bytes 1572868
  16.2 1.9 %collective-permute-start = (bf16[64,1152]{1,0:T(8,128)(2,1)S(1)}, bf16[64,1152]{1,0:T(8,128)(2,1)S(1)}, u32[]{:S(2)}, u32[]{:S(2)}) collective-permute-start(bf16[64,1152]{1,0:T(8,128)(2,1)S(1)} %get-tuple-element.20), channel_id=1, source_target_pairs={{0,4},{4,0},{8,12},{12,8},{1,5},{5,1},{9,13},{13,9},{2,6},{6,2},{1... | collective-permute-start | bytes 442376 | tf_op jit(solution)/shard_map/ppermute | solution.py:480
  16.3 6.7 %collective-permute-start.1 = (bf16[64,1152]{1,0:T(8,128)(2,1)S(1)}, bf16[64,1152]{1,0:T(8,128)(2,1)S(1)}, u32[]{:S(2)}, u32[]{:S(2)}) collective-permute-start(bf16[64,1152]{1,0:T(8,128)(2,1)S(1)} %get-tuple-element.21), channel_id=1, source_target_pairs={{0,8},{4,12},{8,0},{12,4},{1,9},{5,13},{9,1},{13,5},{2,10},{6,14},... | collective-permute-start | bytes 442376 | tf_op jit(solution)/shard_map/ppermute | solution.py:480
  17.9 7.4 %collective-permute-start.2 = (bf16[64,1152]{1,0:T(8,128)(2,1)S(1)}, bf16[64,1152]{1,0:T(8,128)(2,1)S(1)}, u32[]{:S(2)}, u32[]{:S(2)}) collective-permute-start(bf16[64,1152]{1,0:T(8,128)(2,1)S(1)} %get-tuple-element.22), channel_id=1, source_target_pairs={{0,12},{4,8},{8,4},{12,0},{1,13},{5,9},{9,5},{13,1},{2,14},{6,10},... | collective-permute-start | bytes 442376 | tf_op jit(solution)/shard_map/ppermute | solution.py:480
  25.9 8.2 %collective-permute-start.6 = (bf16[128,128]{1,0:T(8,128)(2,1)S(1)}, bf16[128,128]{1,0:T(8,128)(2,1)S(1)}, u32[]{:S(2)}, u32[]{:S(2)}) collective-permute-start(bf16[128,128]{1,0:T(8,128)(2,1)S(1)} %get-tuple-element.23.refs_2_.refs_0_.refs_3_), channel_id=1, source_target_pairs={{0,1},{1,2},{2,3},{3,0},{4,5},{5,6},{6,7},{7,4},{8,9},{9,10},{10,1... | collective-permute-start | bytes 98312 | tf_op jit(solution)/shard_map/ppermute | solution.py:499
  26.0 8.2 %collective-permute-start.7 = (bf16[128,128]{1,0:T(8,128)(2,1)S(1)}, bf16[128,128]{1,0:T(8,128)(2,1)S(1)}, u32[]{:S(2)}, u32[]{:S(2)}) collective-permute-start(bf16[128,128]{1,0:T(8,128)(2,1)S(1)} %get-tuple-element.23.refs_2_.refs_0_.refs_3_), channel_id=1, source_target_pairs={{0,2},{1,3},{2,0},{3,1},{4,6},{5,7},{6,4},{7,5},{8,10},{9,11},{10,... | collective-permute-start | bytes 98312 | tf_op jit(solution)/shard_map/ppermute | solution.py:499
  27.9 6.3 %collective-permute-start.8 = (bf16[128,128]{1,0:T(8,128)(2,1)S(1)}, bf16[128,128]{1,0:T(8,128)(2,1)S(1)}, u32[]{:S(2)}, u32[]{:S(2)}) collective-permute-start(bf16[128,128]{1,0:T(8,128)(2,1)S(1)} %get-tuple-element.23.refs_2_.refs_0_.refs_3_), channel_id=1, source_target_pairs={{0,3},{1,0},{2,1},{3,2},{4,7},{5,4},{6,5},{7,6},{8,11},{9,8},{10,9... | collective-permute-start | bytes 98312 | tf_op jit(solution)/shard_map/ppermute | solution.py:499
  32.8 12.1 %collective-permute-start.3 = (bf16[256,768]{1,0:T(8,128)(2,1)S(1)}, bf16[256,768]{1,0:T(8,128)(2,1)S(1)}, u32[]{:S(2)}, u32[]{:S(2)}) collective-permute-start(bf16[256,768]{1,0:T(8,128)(2,1)S(1)} %hop.5.refs_7_), channel_id=1, source_target_pairs={{0,2},{2,3},{3,1},{1,0},{4,6},{6,7},{7,5},{5,4},{8,10},{10,11},{11... | collective-permute-start | bytes 1179656 | tf_op jit(solution)/shard_map/ppermute | solution.py:486
  37.4 9.8 %copy-start.3 = (bf16[8,64,2048]{2,1,0:T(8,128)(2,1)S(1)}, bf16[8,64,2048]{2,1,0:T(8,128)(2,1)}, u32[]{:S(2)}) copy-start(bf16[8,64,2048]{2,1,0:T(8,128)(2,1)} %refs_5_.1) | copy-start | bytes 6291460
  37.4 21.6 %collective-permute-start.13 = (bf16[256,1280]{1,0:T(8,128)(2,1)S(1)}, bf16[256,1280]{1,0:T(8,128)(2,1)S(1)}, u32[]{:S(2)}, u32[]{:S(2)}) collective-permute-start(bf16[256,1280]{1,0:T(8,128)(2,1)S(1)} %hop.8), channel_id=1, source_target_pairs={{0,2},{2,3},{3,1},{1,0},{4,6},{6,7},{7,5},{5,4},{8,10},{10,11},{11... | collective-permute-start | bytes 1966088 | tf_op jit(solution)/shard_map/ppermute | solution.py:486
  47.9 8.3 %collective-permute-start.10 = (bf16[64,2048]{1,0:T(8,128)(2,1)S(1)}, bf16[64,2048]{1,0:T(8,128)(2,1)S(1)}, u32[]{:S(2)}, u32[]{:S(2)}) collective-permute-start(bf16[64,2048]{1,0:T(8,128)(2,1)S(1)} %get-tuple-element.27), channel_id=1, source_target_pairs={{0,8},{4,12},{8,0},{12,4},{1,9},{5,13},{9,1},{13,5},{2,10},{6,14},... | collective-permute-start | bytes 786440 | tf_op jit(solution)/shard_map/ppermute | solution.py:480
  49.5 9.5 %collective-permute-start.11 = (bf16[64,2048]{1,0:T(8,128)(2,1)S(1)}, bf16[64,2048]{1,0:T(8,128)(2,1)S(1)}, u32[]{:S(2)}, u32[]{:S(2)}) collective-permute-start(bf16[64,2048]{1,0:T(8,128)(2,1)S(1)} %get-tuple-element.28), channel_id=1, source_target_pairs={{0,12},{4,8},{8,4},{12,0},{1,13},{5,9},{9,5},{13,1},{2,14},{6,10},... | collective-permute-start | bytes 786440 | tf_op jit(solution)/shard_map/ppermute | solution.py:480
  49.5 9.5 %collective-permute-start.9 = (bf16[64,2048]{1,0:T(8,128)(2,1)S(1)}, bf16[64,2048]{1,0:T(8,128)(2,1)S(1)}, u32[]{:S(2)}, u32[]{:S(2)}) collective-permute-start(bf16[64,2048]{1,0:T(8,128)(2,1)S(1)} %get-tuple-element.26), channel_id=1, source_target_pairs={{0,4},{4,0},{8,12},{12,8},{1,5},{5,1},{9,13},{13,9},{2,6},{6,2},{1... | collective-permute-start | bytes 786440 | tf_op jit(solution)/shard_map/ppermute | solution.py:480
  50.2 15.9 %collective-permute-start.4 = (bf16[256,768]{1,0:T(8,128)(2,1)S(1)}, bf16[256,768]{1,0:T(8,128)(2,1)S(1)}, u32[]{:S(2)}, u32[]{:S(2)}) collective-permute-start(bf16[256,768]{1,0:T(8,128)(2,1)S(1)} %hop.6.refs_6_), channel_id=1, source_target_pairs={{0,2},{2,3},{3,1},{1,0},{4,6},{6,7},{7,5},{5,4},{8,10},{10,11},{11... | collective-permute-start | bytes 1179656 | tf_op jit(solution)/shard_map/ppermute | solution.py:486
  62.1 8.5 %copy-start.5 = (bf16[256,2048]{1,0:T(8,128)(2,1)S(1)}, bf16[256,2048]{1,0:T(8,128)(2,1)}, u32[]{:S(2)}) copy-start(bf16[256,2048]{1,0:T(8,128)(2,1)} %refs_6_.1) | copy-start | bytes 3145732
  62.1 18.0 %collective-permute-start.14 = (bf16[256,1280]{1,0:T(8,128)(2,1)S(1)}, bf16[256,1280]{1,0:T(8,128)(2,1)S(1)}, u32[]{:S(2)}, u32[]{:S(2)}) collective-permute-start(bf16[256,1280]{1,0:T(8,128)(2,1)S(1)} %hop.9), channel_id=1, source_target_pairs={{0,2},{2,3},{3,1},{1,0},{4,6},{6,7},{7,5},{5,4},{8,10},{10,11},{11... | collective-permute-start | bytes 1966088 | tf_op jit(solution)/shard_map/ppermute | solution.py:516
  68.4 20.2 %collective-permute-start.5 = (bf16[256,768]{1,0:T(8,128)(2,1)S(1)}, bf16[256,768]{1,0:T(8,128)(2,1)S(1)}, u32[]{:S(2)}, u32[]{:S(2)}) collective-permute-start(bf16[256,768]{1,0:T(8,128)(2,1)S(1)} %hop.7.refs_8_), channel_id=1, source_target_pairs={{0,2},{2,3},{3,1},{1,0},{4,6},{6,7},{7,5},{5,4},{8,10},{10,11},{11... | collective-permute-start | bytes 1179656 | tf_op jit(solution)/shard_map/ppermute | solution.py:516
  80.1 1.6 %copy-start.2 = (f32[256,2048]{1,0:T(8,128)S(1)}, f32[256,2048]{1,0:T(8,128)}, u32[]{:S(2)}) copy-start(f32[256,2048]{1,0:T(8,128)} %settle.1.settled_ref) | copy-start | bytes 6291460

commit v6 on v5

v6 whole, which is shorter than its diff:
```python
import functools
import math

import jax
import jax.numpy as jnp
from jax import lax
from jax.experimental import pallas as pl
from jax.experimental.pallas import tpu as pltpu
from jax.sharding import PartitionSpec as P

GROUP = 8
CAP = 64
LANES = 128
MASKED = -1e30
VMEM_LIMIT = 50 * 1024 * 1024
FULL_VMEM = 61 * 1024 * 1024
SHARES = ((5, 3),)
PIECE = 512
SPLIT = 4

VMEM = pl.BlockSpec(memory_space=pltpu.VMEM)
ANY = pl.BlockSpec(memory_space=pl.ANY)
PARAMS = pltpu.CompilerParams(vmem_limit_bytes=VMEM_LIMIT)


def _dot(a, b, left=1, right=0):
    return lax.dot_general(
        a, b, (((left,), (right,)), ((), ())), preferred_element_type=jnp.float32
    )


def _iota(shape, axis):
    return lax.broadcasted_iota(jnp.int32, shape, axis)


def ring_order(count):
    return list(range(0, count, 2)) + list(range(1, count, 2))[::-1]


def column_owner(step):
    count = lax.axis_size("tensor")
    here = lax.axis_index("tensor")
    half = here // 2
    spot = jnp.where(here % 2 == 0, half, count - 1 - half)
    spot = lax.rem(spot - 1 - step + 2 * count, count)
    return jnp.where(2 * spot < count, 2 * spot, 2 * (count - spot) - 1)


def chain_columns(width):
    shares = next(s for s in SHARES if width % (sum(s) * LANES) == 0)
    unit = width // sum(shares)
    return [(sum(shares[:c]) * unit, shares[c] * unit) for c in range(len(shares))]


class Weights:
    def __init__(self, w_ref, held, sems, first, width):
        depth = w_ref.shape[0] // SPLIT
        first = pl.multiple_of(first, LANES)
        self.held = held
        self.copies = [
            pltpu.make_async_copy(
                w_ref.at[pl.ds(s * depth, depth), pl.ds(first, width)],
                held.at[pl.ds(s * depth, depth), :],
                sems.at[s],
            )
            for s in range(SPLIT)
        ]

    def start(self):
        for copy in self.copies:
            copy.start()

    def products(self, a):
        for copy in self.copies:
            copy.wait()
        width = self.held.shape[1]
        for at in range(0, width, PIECE):
            columns = pl.ds(at, min(PIECE, width - at))
            yield columns, _dot(a, self.held[:, columns])

    @staticmethod
    def scratch(depth, width):
        return [
            pltpu.VMEM((depth, width), jnp.bfloat16),
            pltpu.SemaphoreType.DMA((SPLIT,)),
        ]


def row_max(arrays):
    full = None
    tops = []
    for x in arrays:
        width = x.shape[1]
        if width % LANES:
            tops.append(jnp.max(x, axis=1, keepdims=True))
            continue
        for at in range(0, width, LANES):
            tile = x[:, at : at + LANES]
            full = tile if full is None else jnp.maximum(full, tile)
    if full is not None:
        tops.append(jnp.max(full, axis=1, keepdims=True))
    return functools.reduce(jnp.maximum, tops)


def attend_kernel(
    heads, kv, cache, steps, block, replicas, slots,
    len_hbm, adapter_hbm, placement_hbm, q_hbm, k_hbm, v_hbm, nk_hbm, nv_hbm, w_hbm,
    *refs,
):
    a_ref, out_ref, chosen_ref, *sent_refs = refs[: 3 + replicas]
    (
        len_ref, adapter_ref, placement_ref, q_ref, k_ref, v_ref, nk_ref, nv_ref,
        scores_ref, mixed_ref, sems, small_sems, w_held, w_sems,
    ) = refs[3 + replicas :]
    requests = len_ref.shape[1]
    width = q_hbm.shape[1]
    per = requests // steps
    groups = per // GROUP
    group_rows = GROUP * heads
    group_cols = GROUP * cache * kv
    per_kv = heads // kv
    scale = math.log2(math.e) / math.sqrt(width)

    def part(kind, step):
        source, target, count = (
            (q_hbm, q_ref, heads),
            (k_hbm, k_ref, cache * kv),
            (v_hbm, v_ref, cache * kv),
        )[kind]
        rows = pl.ds(step * per * count, per * count)
        return pltpu.make_async_copy(source.at[rows, :], target.at[rows, :], sems.at[kind, step])

    small = [
        pltpu.make_async_copy(source, target, small_sems.at[i])
        for i, (source, target) in enumerate(
            (
                (nk_hbm, nk_ref),
                (len_hbm, len_ref),
                (nv_hbm, nv_ref),
                (adapter_hbm, adapter_ref),
                (placement_hbm, placement_ref),
            )
        )
    ]
    chunk = out_ref.shape[1]
    weights = Weights(w_hbm, w_held, w_sems, column_owner(0) * block, chunk)
    part(0, 0).start()
    part(1, 0).start()
    for copy in small[:2]:
        copy.start()
    part(0, 1).start()
    part(1, 1).start()
    part(2, 0).start()
    for copy in small[2:]:
        copy.start()
    part(2, 1).start()
    for step in range(2, steps):
        for kind in range(3):
            part(kind, step).start()
    weights.start()

    row = _iota((group_rows, group_cols), 0)
    col = _iota((group_rows, group_cols), 1)
    same = (row // heads == col // (cache * kv)) & ((row % heads) // per_kv == col % kv)
    own_bias = jnp.where(same, 0.0, MASKED)
    row = _iota((group_rows, per * kv), 0)
    col = _iota((group_rows, per * kv), 1)
    fresh_kv = (row % heads) // per_kv == col % kv
    fresh_distance = col // kv - row // heads
    ones = jnp.ones((max(group_cols, per * kv), LANES), jnp.bfloat16)

    def scores(step):
        side = step % 2
        part(0, step).wait()
        part(1, step).wait()
        q_at = step * per * heads
        k_at = step * per * cache * kv
        for g in range(groups):
            scores_ref[side, pl.ds(g * group_rows, group_rows), pl.ds(0, group_cols)] = _dot(
                q_ref[pl.ds(q_at + g * group_rows, group_rows), :],
                k_ref[pl.ds(k_at + g * group_cols, group_cols), :],
                1,
                1,
            )
        if step == 0:
            small[0].wait()
        scores_ref[side, :, pl.ds(group_cols, per * kv)] = _dot(
            q_ref[pl.ds(q_at, per * heads), :], nk_ref[pl.ds(step * per * kv, per * kv), :], 1, 1
        )

    scores(0)
    small[1].wait()
    counts = len_ref[...].astype(jnp.float32)
    all_groups = requests // GROUP
    of_group = _iota((all_groups, requests), 1) // GROUP == _iota((all_groups, requests), 0)
    counts = jnp.where(of_group, counts, 0.0).astype(jnp.bfloat16)
    spread = _iota((requests, group_cols), 0) % GROUP == _iota((requests, group_cols), 1) // (cache * kv)
    counts = _dot(counts, spread.astype(jnp.bfloat16))
    position = (_iota((all_groups, group_cols), 1) // kv) % cache
    length_bias = jnp.where(position.astype(jnp.float32) < counts, 0.0, MASKED)

    for step in range(steps):
        side = step % 2
        if step + 1 < steps:
            scores(step + 1)
        k_at = step * per * cache * kv
        f_at = step * per * kv
        part(2, step).wait()
        if step == 0:
            small[2].wait()
        held = []
        fresh = []
        for g in range(groups):
            rows = pl.ds(g * group_rows, group_rows)
            bias = own_bias + length_bias[step * groups + g : step * groups + g + 1, :]
            cached = scores_ref[side, rows, pl.ds(0, group_cols)] + bias
            new = scores_ref[side, rows, pl.ds(group_cols, per * kv)]
            new = jnp.where(fresh_kv & (fresh_distance == g * GROUP), new, MASKED)
            top = row_max([cached, new])
            held.append(jnp.exp2((cached - top) * scale).astype(jnp.bfloat16))
            fresh.append(jnp.exp2((new - top) * scale).astype(jnp.bfloat16))
        values = jnp.concatenate([nv_ref[pl.ds(f_at, per * kv), :], ones[: per * kv]], axis=1)
        fresh = _dot(jnp.concatenate(fresh, axis=0), values)
        for g in range(groups):
            rows = slice(g * group_rows, (g + 1) * group_rows)
            values = v_ref[pl.ds(k_at + g * group_cols, group_cols), :]
            values = jnp.concatenate([values, ones[:group_cols]], axis=1)
            mixed = fresh[rows, :] + _dot(held[g], values)
            mixed_ref[side, rows, :] = mixed[:, :width] / mixed[:, width : width + 1]
        for h in range(heads):
            a_ref[pl.ds(step * per, per), pl.ds(h * width, width)] = mixed_ref[
                side, pl.ds(h, per, stride=heads), :
            ].astype(jnp.bfloat16)

    for copy in small[3:]:
        copy.wait()
    route(slots, a_ref, adapter_ref, placement_ref, chosen_ref, sent_refs)
    for columns, product in weights.products(a_ref[...]):
        out_ref[:, columns] = product.astype(jnp.bfloat16)


def route(slots, a_ref, adapter_ref, placement_ref, chosen_ref, sent_refs):
    replicas = len(sent_refs)
    requests = adapter_ref.shape[1]
    table = placement_ref.shape[1]
    matches = _iota((table, requests), 0) == adapter_ref[...]
    placed = jnp.broadcast_to(placement_ref[...].astype(jnp.float32), (8, table))
    slot = _dot(placed.astype(jnp.bfloat16), matches.astype(jnp.bfloat16)).astype(jnp.int32)
    slot = slot[0:1, :]
    holder = (slot // slots) ^ lax.axis_index("dp")
    inside = slot % slots
    of_holder = _iota((max(replicas, 8), requests), 0) == holder
    earlier = _iota((requests, requests), 0) < _iota((requests, requests), 1)
    before = _dot(of_holder.astype(jnp.bfloat16), earlier.astype(jnp.bfloat16))
    before = jnp.sum(jnp.where(of_holder, before, 0.0), axis=0, keepdims=True).astype(jnp.int32)
    target = holder * CAP + before
    here = _iota((replicas * CAP, requests), 0) == target
    chosen = here.astype(jnp.bfloat16)
    chosen_ref[...] = chosen
    rows = _dot(chosen, a_ref[...]).astype(jnp.bfloat16)
    inner = jnp.sum(jnp.where(here, inside.astype(jnp.float32), 0.0), axis=1, keepdims=True)
    inner = jnp.broadcast_to(inner, (replicas * CAP, LANES)).astype(jnp.bfloat16)
    width = a_ref.shape[1]
    for r, sent_ref in enumerate(sent_refs):
        sent_ref[:, pl.ds(0, width)] = rows[r * CAP : (r + 1) * CAP, :]
        sent_ref[:, pl.ds(width, LANES)] = inner[r * CAP : (r + 1) * CAP, :]


def attend(
    query, keys, values, new_key, new_value, lengths, weight, request_adapter, placement,
    block, replicas, slots,
):
    requests, heads, width = query.shape
    cache, kv = keys.shape[1], keys.shape[2]
    steps = 4
    per = requests // steps
    columns = GROUP * cache * kv + per * kv
    features = heads * width
    chunk = chain_columns(block)[0][1]
    small = [lengths.reshape(1, -1), request_adapter.reshape(1, -1), placement.reshape(1, -1)]
    operands = [
        query.reshape(requests * heads, width),
        keys.reshape(requests * cache * kv, width),
        values.reshape(requests * cache * kv, width),
        new_key.reshape(requests * kv, width),
        new_value.reshape(requests * kv, width),
    ]
    return pl.pallas_call(
        functools.partial(attend_kernel, heads, kv, cache, steps, block, replicas, slots),
        in_specs=[ANY] * 9,
        out_specs=[VMEM] * (3 + replicas),
        out_shape=[
            jax.ShapeDtypeStruct((requests, features), jnp.bfloat16),
            jax.ShapeDtypeStruct((requests, chunk), jnp.bfloat16),
            jax.ShapeDtypeStruct((replicas * CAP, requests), jnp.bfloat16),
        ]
        + [jax.ShapeDtypeStruct((CAP, features + LANES), jnp.bfloat16)] * replicas,
        scratch_shapes=[pltpu.VMEM(x.shape, x.dtype) for x in small + operands]
        + [
            pltpu.VMEM((2, per * heads, columns), jnp.float32),
            pltpu.VMEM((2, per * heads, width), jnp.float32),
            pltpu.SemaphoreType.DMA((3, steps)),
            pltpu.SemaphoreType.DMA((5,)),
        ]
        + Weights.scratch(weight.shape[0], chunk),
        compiler_params=pltpu.CompilerParams(vmem_limit_bytes=FULL_VMEM),
        name="attend",
    )(*small, *operands, weight)


def hop_kernel(step, block, start, arriving, after, *refs):
    if arriving:
        arrived_ref, *refs = refs
    a_ref, w_hbm, *refs = refs
    out_ref, held, sems = refs[after:]
    chunk = out_ref.shape[1]
    first = column_owner(step) * block + start
    weights = Weights(w_hbm, held, sems, first, chunk)
    weights.start()
    for columns, product in weights.products(a_ref[...]):
        if arriving:
            product = product + arrived_ref[:, columns].astype(jnp.float32)
        out_ref[:, columns] = product.astype(jnp.bfloat16)


def hop(step, chain, arrived, attended, weight, block, after=()):
    arriving = arrived is not None
    start, chunk = chain_columns(block)[chain]
    operands = ([arrived] if arriving else []) + [attended, weight, *after]
    return pl.pallas_call(
        functools.partial(hop_kernel, step, block, start, arriving, len(after)),
        in_specs=[VMEM] * (1 + arriving) + [ANY] + [ANY] * len(after),
        out_specs=VMEM,
        out_shape=jax.ShapeDtypeStruct((attended.shape[0], chunk), jnp.bfloat16),
        scratch_shapes=Weights.scratch(weight.shape[0], chunk),
        compiler_params=PARAMS,
        name="hop",
    )(*operands)


def down_kernel(replicas, after, *refs):
    received = refs[:replicas]
    down_ref = refs[replicas]
    mid_ref, inside_ref = refs[replicas + 1 + after :]
    slots, rank, width = down_ref.shape
    rows = jnp.concatenate([r[:, pl.ds(0, width)] for r in received], axis=0)
    inside = jnp.concatenate([r[:, pl.ds(width, LANES)] for r in received], axis=0)
    inside_ref[...] = inside
    projected = _dot(rows, down_ref[...].reshape(slots * rank, width), 1, 1)
    lane_slot = _iota(projected.shape, 1) // rank
    mine = lane_slot == inside[:, 0:1].astype(jnp.int32)
    projected = jnp.where(mine, projected, 0.0).astype(jnp.bfloat16)
    beside = LANES // rank
    some = projected.shape[0] // beside
    packed = 0.0
    for b in range(beside):
        lane = _iota((slots * rank, LANES), 1) - b * rank
        fold = _iota((slots * rank, LANES), 0) % rank == lane
        packed = packed + _dot(projected[b * some : (b + 1) * some, :], fold.astype(jnp.bfloat16))
    mid_ref[...] = packed.astype(jnp.bfloat16)


def down(received, slot_down_weight, after=()):
    replicas = len(received)
    rows = replicas * CAP
    return pl.pallas_call(
        functools.partial(down_kernel, replicas, len(after)),
        in_specs=[VMEM] * (replicas + 1) + [ANY] * len(after),
        out_specs=[VMEM, VMEM],
        out_shape=[
            jax.ShapeDtypeStruct((rows * slot_down_weight.shape[1] // LANES, LANES), jnp.bfloat16),
            jax.ShapeDtypeStruct((rows, LANES), jnp.bfloat16),
        ],
        compiler_params=PARAMS,
        name="down",
    )(*received, slot_down_weight, *after)


def up_kernel(parts, after, *refs):
    mids = refs[:parts]
    inside_ref, up_ref = refs[parts : parts + 2]
    out_refs = refs[parts + 2 + after :]
    slots, rank, width = up_ref.shape
    mid = mids[0][...].astype(jnp.float32)
    for m in mids[1:]:
        mid = mid + m[...].astype(jnp.float32)
    mid = mid.astype(jnp.bfloat16)
    wide = []
    for b in range(LANES // rank):
        lane = _iota((LANES, slots * rank), 0) - b * rank
        spread = _iota((LANES, slots * rank), 1) % rank == lane
        wide.append(_dot(mid, spread.astype(jnp.bfloat16)))
    wide = jnp.concatenate(wide, axis=0)
    mine = _iota(wide.shape, 1) // rank == inside_ref[:, 0:1].astype(jnp.int32)
    wide = jnp.where(mine, wide, 0.0).astype(jnp.bfloat16)
    delta = _dot(wide, up_ref[...].reshape(slots * rank, width)).astype(jnp.bfloat16)
    for r, out_ref in enumerate(out_refs):
        out_ref[...] = delta[r * CAP : (r + 1) * CAP, :]


def up(mids, inside, slot_up_weight, after=()):
    rows = inside.shape[0]
    replicas = rows // CAP
    width = slot_up_weight.shape[2]
    return pl.pallas_call(
        functools.partial(up_kernel, len(mids), len(after)),
        in_specs=[VMEM] * (len(mids) + 2) + [ANY] * len(after),
        out_specs=[VMEM] * replicas,
        out_shape=[jax.ShapeDtypeStruct((CAP, width), jnp.bfloat16)] * replicas,
        compiler_params=PARAMS,
        name="up",
    )(*mids, inside, slot_up_weight, *after)


def settle_kernel(step, replicas, after, *refs):
    returned = refs[:replicas]
    chosen_ref, a_ref, residual_ref, w_hbm = refs[replicas : replicas + 4]
    *out_refs, held, sems = refs[replicas + 4 + after :]
    width = residual_ref.shape[1]
    weights = Weights(w_hbm, held, sems, column_owner(step) * width, width)
    weights.start()
    rows = jnp.concatenate([r[...] for r in returned], axis=0)
    delta = _dot(chosen_ref[...], rows, 0, 0)
    total = residual_ref[...].astype(jnp.float32) + delta
    total = total + jnp.concatenate([p for _, p in weights.products(a_ref[...])], axis=1)
    for (start, chunk), out_ref in zip(chain_columns(width), out_refs):
        out_ref[...] = total[:, start : start + chunk]


def settle(step, returned, chosen, attended, residual, weight, after=()):
    replicas = len(returned)
    rows, width = residual.shape
    chains = chain_columns(width)
    return pl.pallas_call(
        functools.partial(settle_kernel, step, replicas, len(after)),
        in_specs=[VMEM] * (replicas + 3) + [ANY] * (1 + len(after)),
        out_specs=[VMEM] * len(chains),
        out_shape=[jax.ShapeDtypeStruct((rows, chunk), jnp.float32) for _, chunk in chains],
        scratch_shapes=Weights.scratch(weight.shape[0], width),
        compiler_params=PARAMS,
        name="settle",
    )(*returned, chosen, attended, residual, weight, *after)


def finish_kernel(start, arrived_ref, settled_ref, *refs):
    out_hbm, held, sems = refs[-3:]
    rows, chunk = arrived_ref.shape
    half = rows // 2
    copies = []
    for i in range(2):
        part = pl.ds(i * half, half)
        total = settled_ref[part, :] + arrived_ref[part, :].astype(jnp.float32)
        held[part, :] = total.astype(jnp.bfloat16)
        target = out_hbm.at[part, pl.ds(start, chunk)]
        copies.append(pltpu.make_async_copy(held.at[part, :], target, sems.at[i]))
        copies[-1].start()
    for copy in copies:
        copy.wait()


def finish(chain, arrived, settled, earlier, width):
    rows = arrived.shape[0]
    start, chunk = chain_columns(width)[chain]
    operands = [arrived, settled] + ([earlier] if earlier is not None else [])
    return pl.pallas_call(
        functools.partial(finish_kernel, start),
        in_specs=[VMEM, VMEM] + ([ANY] if earlier is not None else []),
        out_specs=ANY,
        out_shape=jax.ShapeDtypeStruct((rows, width), jnp.bfloat16),
        input_output_aliases={2: 0} if earlier is not None else {},
        scratch_shapes=[
            pltpu.VMEM((rows, chunk), jnp.bfloat16),
            pltpu.SemaphoreType.DMA((2,)),
        ],
        compiler_params=PARAMS,
        name="finish",
    )(*operands)


def hold_kernel(*refs):
    pass


def hold(x, after):
    return pl.pallas_call(
        hold_kernel,
        in_specs=[ANY] * (1 + len(after)),
        out_specs=ANY,
        out_shape=jax.ShapeDtypeStruct(x.shape, x.dtype),
        input_output_aliases={0: 0},
        compiler_params=PARAMS,
        name="hold",
    )(x, *after)


def per_device(
    residual,
    query,
    cached_key_rows,
    cached_value_rows,
    new_token_key,
    new_token_value,
    lengths,
    output_weight,
    slot_down_weight,
    slot_up_weight,
    placement,
    request_adapter,
):
    count = lax.axis_size("tensor")
    replicas = lax.axis_size("dp")
    block = residual.shape[1]
    order = ring_order(count)
    ring = [(order[p], order[(p + 1) % count]) for p in range(count)]

    def exchange(blocks):
        moved = [
            lax.ppermute(blocks[r], "dp", [(i, i ^ r) for i in range(replicas)])
            for r in range(1, replicas)
        ]
        return [blocks[0]] + moved

    def next_hop(step, chain, after):
        arrived = lax.ppermute(travelling[chain], "tensor", ring)
        travelling[chain] = hop(step, chain, arrived, attended, output_weight, block, after)

    attended, first, chosen, *leaving = attend(
        query, cached_key_rows, cached_value_rows, new_token_key, new_token_value, lengths,
        output_weight, request_adapter, placement, block, replicas, slot_down_weight.shape[0],
    )
    second = hop(0, 1, None, attended, output_weight, block)
    rows_here = exchange(leaving)
    mid, inside = down(rows_here, slot_down_weight, after=[second])
    rank_sums = [mid] + [
        lax.ppermute(mid, "tensor", [(i, (i + k) % count) for i in range(count)])
        for k in range(1, count)
    ]

    travelling = [first, hold(second, after=[mid])]
    next_hop(1, 0, after=rank_sums + travelling[1:])
    next_hop(1, 1, after=())
    deltas = up(rank_sums, inside, slot_up_weight, after=[travelling[1]])
    returned = exchange(deltas)
    for step in range(2, count - 1):
        for chain in range(2):
            next_hop(step, chain, after=returned if (step, chain) == (2, 0) else ())
    settled = settle(
        count - 1, returned, chosen, attended, residual, output_weight, after=[travelling[1]]
    )
    out = None
    for chain in range(2):
        arrived = lax.ppermute(travelling[chain], "tensor", ring)
        out = finish(chain, arrived, settled[chain], out, block)
    return out


def solution(mesh):
    placed = (
        P(("parts", "dp"), "tensor"),
        P(("parts", "dp"), "tensor", None),
        P(("parts", "dp"), None, "tensor", None),
        P(("parts", "dp"), None, "tensor", None),
        P(("parts", "dp"), "tensor", None),
        P(("parts", "dp"), "tensor", None),
        P(("parts", "dp")),
        P("tensor", None),
        P("dp", None, "tensor"),
        P("dp", None, "tensor"),
        P("parts"),
        P(("parts", "dp")),
    )
    return jax.shard_map(
        per_device,
        mesh=mesh,
        in_specs=placed,
        out_specs=P(("parts", "dp"), "tensor"),
        check_vma=False,
    )
```

time: 90.3 us -> 90.4 us (level)
  starting transfers between devices: 21.1 us -> 30 us
  Pallas kernels: 34.1 us -> 27.8 us
  waiting for transfers between devices: 31.9 us -> 29.7 us
    ppermute x4, starting transfers between devices: 7.85 us -> 16.8 us  [next_hop(): arrived = lax.ppermute(travelling[chain], 'tensor', ring)]
    ppermute x4, waiting for transfers between devices: 9.01 us -> 4.4 us  [next_hop(): arrived = lax.ppermute(travelling[chain], 'tensor', ring)]
    ppermute x3, waiting for transfers between devices: 0.01 us -> 3.2 us  [per_device(): lax.ppermute(mid, 'tensor', [(i, (i + k) % count) for i in range(count)])]
    ppermute x6, waiting for transfers between devices: 13.7 us -> 11.1 us  [exchange(): lax.ppermute(blocks[r], 'dp', [(i, i ^ r) for i in range(replicas)])]
    pallas_call x5, Pallas kernels: 13.1 us -> 11.3 us  [hop(): pl.pallas_call(functools.partial(hop_kernel, step, block, start, arriving...]
    ppermute x2, waiting for transfers between devices: 9.23 us -> 11 us  [per_device(): arrived = lax.ppermute(travelling[chain], 'tensor', ring)]
    pallas_call x1, Pallas kernels: 10.5 us -> 8.81 us  [attend(): pl.pallas_call(functools.partial(attend_kernel, heads, kv, cache, steps,...]
    pallas_call x1, Pallas kernels: 6.12 us -> 4.51 us  [settle(): pl.pallas_call(functools.partial(settle_kernel, step, replicas, len(after...]
  transfers between devices with their start and end apart: 15 -> 15, of which waited for: 8 -> 10; matrix products, arithmetic and copies ran while one was open for 0% -> 0% of each run, Pallas kernels for 25% -> 20%
where the time goes in v6:
time: 90.4 us; the launch traced here: 90 us
  starting transfers between devices  30 us (33%)
  waiting for transfers between devices  29.7 us (33%)
  Pallas kernels  27.8 us (31%)
  local copies, waits for them, and re-layouts  2.39 us (3%)
    ppermute x4, starting transfers between devices, next_hop(): arrived = lax.ppermute(travelling[chain], 'tensor', ring)  16.8 us
    pallas_call x5, Pallas kernels, hop(): pl.pallas_call(functools.partial(hop_kernel, step, block, start, arriving...  11.3 us
    ppermute x6, waiting for transfers between devices, exchange(): lax.ppermute(blocks[r], 'dp', [(i, i ^ r) for i in range(replicas)])  11.1 us
    ppermute x2, waiting for transfers between devices, per_device(): arrived = lax.ppermute(travelling[chain], 'tensor', ring)  11 us
    pallas_call x1, Pallas kernels, attend(): pl.pallas_call(functools.partial(attend_kernel, heads, kv, cache, steps,...  8.81 us
    ppermute x2, starting transfers between devices, per_device(): arrived = lax.ppermute(travelling[chain], 'tensor', ring)  4.67 us
    ppermute x3, starting transfers between devices, per_device(): lax.ppermute(mid, 'tensor', [(i, (i + k) % count) for i in range(count)])  4.55 us
    pallas_call x1, Pallas kernels, settle(): pl.pallas_call(functools.partial(settle_kernel, step, replicas, len(after...  4.51 us
  transfers between devices with their start and end apart: 15, of which 10 were waited for; matrix products, arithmetic and copies ran while one was open for 0% of the time, Pallas kernels for 20%

profile of v6, /device:TPU:0, one launch (start us, length us, event | category | flops | bytes accessed | tf_op | source)
XLA Modules:
  0.0 90.0 jit_solution(15652228018960110292)
XLA Ops:
  0.0 8.8 %attend.1 = (bf16[256,1024]{1,0:T(8,128)(2,1)}, bf16[256,1280]{1,0:T(8,128)(2,1)}, bf16[256,256]{1,0:T(8,128)(2,1)}, bf16[64,1152]{1,0:T(8,128)(2,1)}, bf16[64,1...) custom-call(s32[1,256]{1,0:T(1,128)} %bitcast.13, s32[1,256]{1,0:T(1,128)} %bitcast.14, ...), custom_call_target="tpu_custom_call" | custom-call | tf_op jit(solution)/shard_map/attend/pallas_call | solution.py:288
  8.8 4.1 %collective-permute-start.12 = (bf16[256,1280]{1,0:T(8,128)(2,1)}, bf16[256,1280]{1,0:T(8,128)(2,1)S(1)}, u32[]{:S(2)}, u32[]{:S(2)}) collective-permute-start(bf16[256,1280]{1,0:T(8,128)(2,1)} %get-tuple-element.33), channel_id=1, source_target_pairs={{0,2},{2,3},{3,1},{1,0},{4,6},{6,7},{7,5},{5,4},{8,10},{10,11},{11... | collective-permute-start | bytes 1966088 | tf_op jit(solution)/shard_map/ppermute | solution.py:524
  12.9 1.5 %collective-permute-start.1 = (bf16[64,1152]{1,0:T(8,128)(2,1)}, bf16[64,1152]{1,0:T(8,128)(2,1)S(1)}, u32[]{:S(2)}, u32[]{:S(2)}) collective-permute-start(bf16[64,1152]{1,0:T(8,128)(2,1)} %get-tuple-element.23), channel_id=1, source_target_pairs={{0,8},{4,12},{8,0},{12,4},{1,9},{5,13},{9,1},{13,5},{2,10},{6,14},... | collective-permute-start | bytes 442376 | tf_op jit(solution)/shard_map/ppermute | solution.py:518
  14.8 1.0 %copy-done = bf16[256,1024]{1,0:T(8,128)(2,1)S(1)} copy-done((bf16[256,1024]{1,0:T(8,128)(2,1)S(1)}, bf16[256,1024]{1,0:T(8,128)(2,1)}, u32[]{:S(2)}) %copy-start) | copy-done | bytes 524312
  15.8 2.1 %hop.5.refs_5_.refs_0_ = bf16[256,768]{1,0:T(8,128)(2,1)S(1)} custom-call(bf16[256,1024]{1,0:T(8,128)(2,1)S(1)} %copy-done, bf16[1024,8192]{1,0:T(8,128)(2,1)} %refs_2_.7), custom_call_target="tpu_custom_call" | custom-call | tf_op jit(solution)/shard_map/hop/pallas_call | solution.py:330
  17.9 1.8 %collective-permute-done.1.refs_2_ = bf16[64,1152]{1,0:T(8,128)(2,1)S(1)} collective-permute-done((bf16[64,1152]{1,0:T(8,128)(2,1)}, bf16[64,1152]{1,0:T(8,128)(2,1)S(1)}, u32[]{:S(2)}, u32[]{:S(2)}) %collective-permute-start.1) | collective-permute-done | bytes 147488 | tf_op jit(solution)/shard_map/ppermute | solution.py:518
  19.8 2.4 %collective-permute-done.2.refs_3_ = bf16[64,1152]{1,0:T(8,128)(2,1)S(1)} collective-permute-done((bf16[64,1152]{1,0:T(8,128)(2,1)}, bf16[64,1152]{1,0:T(8,128)(2,1)S(1)}, u32[]{:S(2)}, u32[]{:S(2)}) %collective-permute-start.2) | collective-permute-done | bytes 147488 | tf_op jit(solution)/shard_map/ppermute | solution.py:518
  22.9 1.9 %collective-permute-start.7 = (bf16[128,128]{1,0:T(8,128)(2,1)S(1)}, bf16[128,128]{1,0:T(8,128)(2,1)S(1)}, u32[]{:S(2)}, u32[]{:S(2)}) collective-permute-start(bf16[128,128]{1,0:T(8,128)(2,1)S(1)} %get-tuple-element.25.refs_1_.refs_0_.refs_3_), channel_id=1, source_target_pairs={{0,2},{1,3},{2,0},{3,1},{4,6},{5,7},{6,4},{7,5},{8,10},{9,11},{10,... | collective-permute-start | bytes 98312 | tf_op jit(solution)/shard_map/ppermute | solution.py:535
  24.8 2.6 %collective-permute-start.8 = (bf16[128,128]{1,0:T(8,128)(2,1)S(1)}, bf16[128,128]{1,0:T(8,128)(2,1)S(1)}, u32[]{:S(2)}, u32[]{:S(2)}) collective-permute-start(bf16[128,128]{1,0:T(8,128)(2,1)S(1)} %get-tuple-element.25.refs_1_.refs_0_.refs_3_), channel_id=1, source_target_pairs={{0,3},{1,0},{2,1},{3,2},{4,7},{5,4},{6,5},{7,6},{8,11},{9,8},{10,9... | collective-permute-start | bytes 98312 | tf_op jit(solution)/shard_map/ppermute | solution.py:535
  27.4 1.3 %collective-permute-start.3 = (bf16[256,768]{1,0:T(8,128)(2,1)S(1)}, bf16[256,768]{1,0:T(8,128)(2,1)S(1)}, u32[]{:S(2)}, u32[]{:S(2)}) collective-permute-start(bf16[256,768]{1,0:T(8,128)(2,1)S(1)} %hold.1.refs_7_), channel_id=1, source_target_pairs={{0,2},{2,3},{3,1},{1,0},{4,6},{6,7},{7,5},{5,4},{8,10},{10,11},{11... | collective-permute-start | bytes 1179656 | tf_op jit(solution)/shard_map/ppermute | solution.py:524
  28.7 1.8 %collective-permute-done.6.refs_1_.refs_4_ = bf16[128,128]{1,0:T(8,128)(2,1)S(1)} collective-permute-done((bf16[128,128]{1,0:T(8,128)(2,1)S(1)}, bf16[128,128]{1,0:T(8,128)(2,1)S(1)}, u32[]{:S(2)}, u32[]{:S(2)}) %collective-permute-start.6) | collective-permute-done | bytes 32800 | tf_op jit(solution)/shard_map/ppermute | solution.py:535
  30.5 1.4 %collective-permute-done.7.refs_2_.refs_5_ = bf16[128,128]{1,0:T(8,128)(2,1)S(1)} collective-permute-done((bf16[128,128]{1,0:T(8,128)(2,1)S(1)}, bf16[128,128]{1,0:T(8,128)(2,1)S(1)}, u32[]{:S(2)}, u32[]{:S(2)}) %collective-permute-start.7) | collective-permute-done | bytes 32800 | tf_op jit(solution)/shard_map/ppermute | solution.py:535
  31.9 2.6 %hop.8 = bf16[256,1280]{1,0:T(8,128)(2,1)S(1)} custom-call(bf16[256,1280]{1,0:T(8,128)(2,1)S(1)} %collective-permute-done.12.refs_0_, bf16[256,1024]{1,0:T(8,128)(2,1)S(1)} %copy-done.1, bf16[1024,8192]{1,0:T(8,128)(2,1)} %refs_2_.7, bf16[128,128]{1,0:T(8,128)(2,1)S(1)} %get-tuple-element.25.refs_1_.refs_0_.refs_3_, ...), custom_call_target="tpu_custom_call" | custom-call | tf_op jit(solution)/shard_map/hop/pallas_call | solution.py:330
  34.5 7.9 %collective-permute-start.13 = (bf16[256,1280]{1,0:T(8,128)(2,1)S(1)}, bf16[256,1280]{1,0:T(8,128)(2,1)S(1)}, u32[]{:S(2)}, u32[]{:S(2)}) collective-permute-start(bf16[256,1280]{1,0:T(8,128)(2,1)S(1)} %hop.8), channel_id=1, source_target_pairs={{0,2},{2,3},{3,1},{1,0},{4,6},{6,7},{7,5},{5,4},{8,10},{10,11},{11... | collective-permute-start | bytes 1966088 | tf_op jit(solution)/shard_map/ppermute | solution.py:524
  42.4 2.0 %hop.6.refs_6_ = bf16[256,768]{1,0:T(8,128)(2,1)S(1)} custom-call(bf16[256,768]{1,0:T(8,128)(2,1)S(1)} %collective-permute-done.3.refs_0_, bf16[256,1024]{1,0:T(8,128)(2,1)S(1)} %copy-done.1, bf16[1024,8192]{1,0:T(8,128)(2,1)} %refs_2_.7), custom_call_target="tpu_custom_call" | custom-call | tf_op jit(solution)/shard_map/hop/pallas_call | solution.py:330
  44.4 0.8 up.1
  45.2 1.6 %collective-permute-start.10 = (bf16[64,2048]{1,0:T(8,128)(2,1)S(1)}, bf16[64,2048]{1,0:T(8,128)(2,1)S(1)}, u32[]{:S(2)}, u32[]{:S(2)}) collective-permute-start(bf16[64,2048]{1,0:T(8,128)(2,1)S(1)} %get-tuple-element.29), channel_id=1, source_target_pairs={{0,8},{4,12},{8,0},{12,4},{1,9},{5,13},{9,1},{13,5},{2,10},{6,14},... | collective-permute-start | bytes 786440 | tf_op jit(solution)/shard_map/ppermute | solution.py:518
  47.5 3.5 %collective-permute-start.4 = (bf16[256,768]{1,0:T(8,128)(2,1)S(1)}, bf16[256,768]{1,0:T(8,128)(2,1)S(1)}, u32[]{:S(2)}, u32[]{:S(2)}) collective-permute-start(bf16[256,768]{1,0:T(8,128)(2,1)S(1)} %hop.6.refs_6_), channel_id=1, source_target_pairs={{0,2},{2,3},{3,1},{1,0},{4,6},{6,7},{7,5},{5,4},{8,10},{10,11},{11... | collective-permute-start | bytes 1179656 | tf_op jit(solution)/shard_map/ppermute | solution.py:524
  50.9 3.6 %collective-permute-done.10.refs_2_.refs_5_ = bf16[64,2048]{1,0:T(8,128)(2,1)S(1)} collective-permute-done((bf16[64,2048]{1,0:T(8,128)(2,1)S(1)}, bf16[64,2048]{1,0:T(8,128)(2,1)S(1)}, u32[]{:S(2)}, u32[]{:S(2)}) %collective-permute-start.10) | collective-permute-done | bytes 262176 | tf_op jit(solution)/shard_map/ppermute | solution.py:518
  54.5 3.2 %collective-permute-done.11.refs_3_.refs_6_ = bf16[64,2048]{1,0:T(8,128)(2,1)S(1)} collective-permute-done((bf16[64,2048]{1,0:T(8,128)(2,1)S(1)}, bf16[64,2048]{1,0:T(8,128)(2,1)S(1)}, u32[]{:S(2)}, u32[]{:S(2)}) %collective-permute-start.11) | collective-permute-done | bytes 262176 | tf_op jit(solution)/shard_map/ppermute | solution.py:518
  57.8 1.1 %collective-permute-done.13.refs_0_ = bf16[256,1280]{1,0:T(8,128)(2,1)S(1)} collective-permute-done((bf16[256,1280]{1,0:T(8,128)(2,1)S(1)}, bf16[256,1280]{1,0:T(8,128)(2,1)S(1)}, u32[]{:S(2)}, u32[]{:S(2)}) %collective-permute-start.13) | collective-permute-done | bytes 655392 | tf_op jit(solution)/shard_map/ppermute | solution.py:524
  58.9 2.6 %hop.9 = bf16[256,1280]{1,0:T(8,128)(2,1)S(1)} custom-call(bf16[256,1280]{1,0:T(8,128)(2,1)S(1)} %collective-permute-done.13.refs_0_, bf16[256,1024]{1,0:T(8,128)(2,1)S(1)} %copy-done.1, bf16[1024,8192]{1,0:T(8,128)(2,1)} %refs_2_.7, bf16[64,2048]{1,0:T(8,128)(2,1)S(1)} %get-tuple-element.27.refs_0_.refs_3_, ...), custom_call_target="tpu_custom_call" | custom-call | tf_op jit(solution)/shard_map/hop/pallas_call | solution.py:330
  61.5 2.6 %collective-permute-start.14 = (bf16[256,1280]{1,0:T(8,128)(2,1)S(1)}, bf16[256,1280]{1,0:T(8,128)(2,1)S(1)}, u32[]{:S(2)}, u32[]{:S(2)}) collective-permute-start(bf16[256,1280]{1,0:T(8,128)(2,1)S(1)} %hop.9), channel_id=1, source_target_pairs={{0,2},{2,3},{3,1},{1,0},{4,6},{6,7},{7,5},{5,4},{8,10},{10,11},{11... | collective-permute-start | bytes 1966088 | tf_op jit(solution)/shard_map/ppermute | solution.py:552
  64.1 3.2 %collective-permute-done.4.refs_0_ = bf16[256,768]{1,0:T(8,128)(2,1)S(1)} collective-permute-done((bf16[256,768]{1,0:T(8,128)(2,1)S(1)}, bf16[256,768]{1,0:T(8,128)(2,1)S(1)}, u32[]{:S(2)}, u32[]{:S(2)}) %collective-permute-start.4) | collective-permute-done | bytes 393248 | tf_op jit(solution)/shard_map/ppermute | solution.py:524
  67.3 2.0 %hop.7.refs_8_ = bf16[256,768]{1,0:T(8,128)(2,1)S(1)} custom-call(bf16[256,768]{1,0:T(8,128)(2,1)S(1)} %collective-permute-done.4.refs_0_, bf16[256,1024]{1,0:T(8,128)(2,1)S(1)} %copy-done.1, bf16[1024,8192]{1,0:T(8,128)(2,1)} %refs_2_.7), custom_call_target="tpu_custom_call" | custom-call | tf_op jit(solution)/shard_map/hop/pallas_call | solution.py:330
  69.3 2.1 %collective-permute-start.5 = (bf16[256,768]{1,0:T(8,128)(2,1)S(1)}, bf16[256,768]{1,0:T(8,128)(2,1)S(1)}, u32[]{:S(2)}, u32[]{:S(2)}) collective-permute-start(bf16[256,768]{1,0:T(8,128)(2,1)S(1)} %hop.7.refs_8_), channel_id=1, source_target_pairs={{0,2},{2,3},{3,1},{1,0},{4,6},{6,7},{7,5},{5,4},{8,10},{10,11},{11... | collective-permute-start | bytes 1179656 | tf_op jit(solution)/shard_map/ppermute | solution.py:552
  71.5 4.5 %settle.1 = (f32[256,1280]{1,0:T(8,128)}, f32[256,768]{1,0:T(8,128)S(1)}) custom-call(bf16[64,2048]{1,0:T(8,128)(2,1)S(1)} %get-tuple-element.27.refs_0_.refs_3_, bf16[64,2048]{1,0:T(8,128)(2,1)S(1)} %collective-permute-done.9.refs_1_.refs_4_, bf16[64,2048]{1,0:T(8,128)(2,1)S(1)} %collective-permute-done.10.refs_2_.refs_5_, ...), custom_call_target="tpu_custom_call" | custom-call | tf_op jit(solution)/shard_map/settle/pallas_call | solution.py:434
  76.0 5.4 %collective-permute-done.14.arrived_ref = bf16[256,1280]{1,0:T(8,128)(2,1)S(1)} collective-permute-done((bf16[256,1280]{1,0:T(8,128)(2,1)S(1)}, bf16[256,1280]{1,0:T(8,128)(2,1)S(1)}, u32[]{:S(2)}, u32[]{:S(2)}) %collective-permute-start.14) | collective-permute-done | bytes 655392 | tf_op jit(solution)/shard_map/ppermute | solution.py:552
  81.4 1.3 %copy-done.3 = f32[256,1280]{1,0:T(8,128)S(1)} copy-done((f32[256,1280]{1,0:T(8,128)S(1)}, f32[256,1280]{1,0:T(8,128)}, u32[]{:S(2)}) %copy-start.3) | copy-done | bytes 1310744
  82.7 0.9 %finish.2.refs_0_ = bf16[256,2048]{1,0:T(8,128)(2,1)} custom-call(bf16[256,1280]{1,0:T(8,128)(2,1)S(1)} %collective-permute-done.14.arrived_ref, f32[256,1280]{1,0:T(8,128)S(1)} %copy-done.3), custom_call_target="tpu_custom_call" | custom-call | tf_op jit(solution)/shard_map/finish/pallas_call | solution.py:465
  83.6 5.6 %collective-permute-done.5.arrived_ref = bf16[256,768]{1,0:T(8,128)(2,1)S(1)} collective-permute-done((bf16[256,768]{1,0:T(8,128)(2,1)S(1)}, bf16[256,768]{1,0:T(8,128)(2,1)S(1)}, u32[]{:S(2)}, u32[]{:S(2)}) %collective-permute-start.5) | collective-permute-done | bytes 393248 | tf_op jit(solution)/shard_map/ppermute | solution.py:552
  89.3 0.8 finish.3
  (26 shorter events, 1.8 us)
Async XLA Ops:
  8.8 23.1 %collective-permute-start.12 = (bf16[256,1280]{1,0:T(8,128)(2,1)}, bf16[256,1280]{1,0:T(8,128)(2,1)S(1)}, u32[]{:S(2)}, u32[]{:S(2)}) collective-permute-start(bf16[256,1280]{1,0:T(8,128)(2,1)} %get-tuple-element.33), channel_id=1, source_target_pairs={{0,2},{2,3},{3,1},{1,0},{4,6},{6,7},{7,5},{5,4},{8,10},{10,11},{11... | collective-permute-start | bytes 1966088 | tf_op jit(solution)/shard_map/ppermute | solution.py:524
  12.9 5.0 %collective-permute-start = (bf16[64,1152]{1,0:T(8,128)(2,1)}, bf16[64,1152]{1,0:T(8,128)(2,1)S(1)}, u32[]{:S(2)}, u32[]{:S(2)}) collective-permute-start(bf16[64,1152]{1,0:T(8,128)(2,1)} %get-tuple-element.22), channel_id=1, source_target_pairs={{0,4},{4,0},{8,12},{12,8},{1,5},{5,1},{9,13},{13,9},{2,6},{6,2},{1... | collective-permute-start | bytes 442376 | tf_op jit(solution)/shard_map/ppermute | solution.py:518
  12.9 6.9 %collective-permute-start.1 = (bf16[64,1152]{1,0:T(8,128)(2,1)}, bf16[64,1152]{1,0:T(8,128)(2,1)S(1)}, u32[]{:S(2)}, u32[]{:S(2)}) collective-permute-start(bf16[64,1152]{1,0:T(8,128)(2,1)} %get-tuple-element.23), channel_id=1, source_target_pairs={{0,8},{4,12},{8,0},{12,4},{1,9},{5,13},{9,1},{13,5},{2,10},{6,14},... | collective-permute-start | bytes 442376 | tf_op jit(solution)/shard_map/ppermute | solution.py:518
  14.4 7.8 %collective-permute-start.2 = (bf16[64,1152]{1,0:T(8,128)(2,1)}, bf16[64,1152]{1,0:T(8,128)(2,1)S(1)}, u32[]{:S(2)}, u32[]{:S(2)}) collective-permute-start(bf16[64,1152]{1,0:T(8,128)(2,1)} %get-tuple-element.24), channel_id=1, source_target_pairs={{0,12},{4,8},{8,4},{12,0},{1,13},{5,9},{9,5},{13,1},{2,14},{6,10},... | collective-permute-start | bytes 442376 | tf_op jit(solution)/shard_map/ppermute | solution.py:518
  14.8 1.0 %copy-start = (bf16[256,1024]{1,0:T(8,128)(2,1)S(1)}, bf16[256,1024]{1,0:T(8,128)(2,1)}, u32[]{:S(2)}) copy-start(bf16[256,1024]{1,0:T(8,128)(2,1)} %get-tuple-element.20.refs_0_.refs_1_.refs_5_) | copy-start | bytes 1572868
  15.8 6.3 %copy-start.5 = (bf16[8,64,1024]{2,1,0:T(8,128)(2,1)S(1)}, bf16[8,64,1024]{2,1,0:T(8,128)(2,1)}, u32[]{:S(2)}) copy-start(bf16[8,64,1024]{2,1,0:T(8,128)(2,1)} %refs_4_.1) | copy-start | bytes 3145732
  15.8 6.3 %copy-start.6 = (bf16[64,1152]{1,0:T(8,128)(2,1)S(1)}, bf16[64,1152]{1,0:T(8,128)(2,1)}, u32[]{:S(2)}) copy-start(bf16[64,1152]{1,0:T(8,128)(2,1)} %get-tuple-element.21.refs_0_) | copy-start | bytes 442372
  17.9 14.0 %copy-start.1 = (bf16[256,1024]{1,0:T(8,128)(2,1)S(1)}, bf16[256,1024]{1,0:T(8,128)(2,1)}, u32[]{:S(2)}) copy-start(bf16[256,1024]{1,0:T(8,128)(2,1)} %get-tuple-element.20.refs_0_.refs_1_.refs_5_) | copy-start | bytes 1572868
  22.8 7.7 %collective-permute-start.6 = (bf16[128,128]{1,0:T(8,128)(2,1)S(1)}, bf16[128,128]{1,0:T(8,128)(2,1)S(1)}, u32[]{:S(2)}, u32[]{:S(2)}) collective-permute-start(bf16[128,128]{1,0:T(8,128)(2,1)S(1)} %get-tuple-element.25.refs_1_.refs_0_.refs_3_), channel_id=1, source_target_pairs={{0,1},{1,2},{2,3},{3,0},{4,5},{5,6},{6,7},{7,4},{8,9},{9,10},{10,1... | collective-permute-start | bytes 98312 | tf_op jit(solution)/shard_map/ppermute | solution.py:535
  22.9 9.0 %collective-permute-start.7 = (bf16[128,128]{1,0:T(8,128)(2,1)S(1)}, bf16[128,128]{1,0:T(8,128)(2,1)S(1)}, u32[]{:S(2)}, u32[]{:S(2)}) collective-permute-start(bf16[128,128]{1,0:T(8,128)(2,1)S(1)} %get-tuple-element.25.refs_1_.refs_0_.refs_3_), channel_id=1, source_target_pairs={{0,2},{1,3},{2,0},{3,1},{4,6},{5,7},{6,4},{7,5},{8,10},{9,11},{10,... | collective-permute-start | bytes 98312 | tf_op jit(solution)/shard_map/ppermute | solution.py:535
  24.8 7.1 %collective-permute-start.8 = (bf16[128,128]{1,0:T(8,128)(2,1)S(1)}, bf16[128,128]{1,0:T(8,128)(2,1)S(1)}, u32[]{:S(2)}, u32[]{:S(2)}) collective-permute-start(bf16[128,128]{1,0:T(8,128)(2,1)S(1)} %get-tuple-element.25.refs_1_.refs_0_.refs_3_), channel_id=1, source_target_pairs={{0,3},{1,0},{2,1},{3,2},{4,7},{5,4},{6,5},{7,6},{8,11},{9,8},{10,9... | collective-permute-start | bytes 98312 | tf_op jit(solution)/shard_map/ppermute | solution.py:535
  27.4 15.0 %collective-permute-start.3 = (bf16[256,768]{1,0:T(8,128)(2,1)S(1)}, bf16[256,768]{1,0:T(8,128)(2,1)S(1)}, u32[]{:S(2)}, u32[]{:S(2)}) collective-permute-start(bf16[256,768]{1,0:T(8,128)(2,1)S(1)} %hold.1.refs_7_), channel_id=1, source_target_pairs={{0,2},{2,3},{3,1},{1,0},{4,6},{6,7},{7,5},{5,4},{8,10},{10,11},{11... | collective-permute-start | bytes 1179656 | tf_op jit(solution)/shard_map/ppermute | solution.py:524
  34.5 9.9 %copy-start.2 = (bf16[8,64,2048]{2,1,0:T(8,128)(2,1)S(1)}, bf16[8,64,2048]{2,1,0:T(8,128)(2,1)}, u32[]{:S(2)}) copy-start(bf16[8,64,2048]{2,1,0:T(8,128)(2,1)} %refs_5_.1) | copy-start | bytes 6291460
  34.5 24.4 %collective-permute-start.13 = (bf16[256,1280]{1,0:T(8,128)(2,1)S(1)}, bf16[256,1280]{1,0:T(8,128)(2,1)S(1)}, u32[]{:S(2)}, u32[]{:S(2)}) collective-permute-start(bf16[256,1280]{1,0:T(8,128)(2,1)S(1)} %hop.8), channel_id=1, source_target_pairs={{0,2},{2,3},{3,1},{1,0},{4,6},{6,7},{7,5},{5,4},{8,10},{10,11},{11... | collective-permute-start | bytes 1966088 | tf_op jit(solution)/shard_map/ppermute | solution.py:524
  45.2 9.3 %collective-permute-start.10 = (bf16[64,2048]{1,0:T(8,128)(2,1)S(1)}, bf16[64,2048]{1,0:T(8,128)(2,1)S(1)}, u32[]{:S(2)}, u32[]{:S(2)}) collective-permute-start(bf16[64,2048]{1,0:T(8,128)(2,1)S(1)} %get-tuple-element.29), channel_id=1, source_target_pairs={{0,8},{4,12},{8,0},{12,4},{1,9},{5,13},{9,1},{13,5},{2,10},{6,14},... | collective-permute-start | bytes 786440 | tf_op jit(solution)/shard_map/ppermute | solution.py:518
  46.8 11.0 %collective-permute-start.11 = (bf16[64,2048]{1,0:T(8,128)(2,1)S(1)}, bf16[64,2048]{1,0:T(8,128)(2,1)S(1)}, u32[]{:S(2)}, u32[]{:S(2)}) collective-permute-start(bf16[64,2048]{1,0:T(8,128)(2,1)S(1)} %get-tuple-element.30), channel_id=1, source_target_pairs={{0,12},{4,8},{8,4},{12,0},{1,13},{5,9},{9,5},{13,1},{2,14},{6,10},... | collective-permute-start | bytes 786440 | tf_op jit(solution)/shard_map/ppermute | solution.py:518
  46.8 11.0 %collective-permute-start.9 = (bf16[64,2048]{1,0:T(8,128)(2,1)S(1)}, bf16[64,2048]{1,0:T(8,128)(2,1)S(1)}, u32[]{:S(2)}, u32[]{:S(2)}) collective-permute-start(bf16[64,2048]{1,0:T(8,128)(2,1)S(1)} %get-tuple-element.28), channel_id=1, source_target_pairs={{0,4},{4,0},{8,12},{12,8},{1,5},{5,1},{9,13},{13,9},{2,6},{6,2},{1... | collective-permute-start | bytes 786440 | tf_op jit(solution)/shard_map/ppermute | solution.py:518
  47.5 19.9 %collective-permute-start.4 = (bf16[256,768]{1,0:T(8,128)(2,1)S(1)}, bf16[256,768]{1,0:T(8,128)(2,1)S(1)}, u32[]{:S(2)}, u32[]{:S(2)}) collective-permute-start(bf16[256,768]{1,0:T(8,128)(2,1)S(1)} %hop.6.refs_6_), channel_id=1, source_target_pairs={{0,2},{2,3},{3,1},{1,0},{4,6},{6,7},{7,5},{5,4},{8,10},{10,11},{11... | collective-permute-start | bytes 1179656 | tf_op jit(solution)/shard_map/ppermute | solution.py:524
  61.5 9.9 %copy-start.4 = (bf16[256,2048]{1,0:T(8,128)(2,1)S(1)}, bf16[256,2048]{1,0:T(8,128)(2,1)}, u32[]{:S(2)}) copy-start(bf16[256,2048]{1,0:T(8,128)(2,1)} %refs_6_.1) | copy-start | bytes 3145732
  61.5 9.9 %copy-start.7 = (bf16[256,256]{1,0:T(8,128)(2,1)S(1)}, bf16[256,256]{1,0:T(8,128)(2,1)}, u32[]{:S(2)}) copy-start(bf16[256,256]{1,0:T(8,128)(2,1)} %get-tuple-element.31.refs_4_) | copy-start | bytes 393220
  61.5 19.8 %collective-permute-start.14 = (bf16[256,1280]{1,0:T(8,128)(2,1)S(1)}, bf16[256,1280]{1,0:T(8,128)(2,1)S(1)}, u32[]{:S(2)}, u32[]{:S(2)}) collective-permute-start(bf16[256,1280]{1,0:T(8,128)(2,1)S(1)} %hop.9), channel_id=1, source_target_pairs={{0,2},{2,3},{3,1},{1,0},{4,6},{6,7},{7,5},{5,4},{8,10},{10,11},{11... | collective-permute-start | bytes 1966088 | tf_op jit(solution)/shard_map/ppermute | solution.py:552
  69.3 19.9 %collective-permute-start.5 = (bf16[256,768]{1,0:T(8,128)(2,1)S(1)}, bf16[256,768]{1,0:T(8,128)(2,1)S(1)}, u32[]{:S(2)}, u32[]{:S(2)}) collective-permute-start(bf16[256,768]{1,0:T(8,128)(2,1)S(1)} %hop.7.refs_8_), channel_id=1, source_target_pairs={{0,2},{2,3},{3,1},{1,0},{4,6},{6,7},{7,5},{5,4},{8,10},{10,11},{11... | collective-permute-start | bytes 1179656 | tf_op jit(solution)/shard_map/ppermute | solution.py:552
  81.4 1.3 %copy-start.3 = (f32[256,1280]{1,0:T(8,128)S(1)}, f32[256,1280]{1,0:T(8,128)}, u32[]{:S(2)}) copy-start(f32[256,1280]{1,0:T(8,128)} %get-tuple-element.34.settled_ref) | copy-start | bytes 3932164

commit v7 on v6

--- a/solution.py
+++ b/solution.py
@@ -103,15 +103,15 @@
 
 
 def attend_kernel(
-    heads, kv, cache, steps, block, replicas, slots,
+    heads, kv, cache, steps, block, slots,
     len_hbm, adapter_hbm, placement_hbm, q_hbm, k_hbm, v_hbm, nk_hbm, nv_hbm, w_hbm,
     *refs,
 ):
-    a_ref, out_ref, chosen_ref, *sent_refs = refs[: 3 + replicas]
+    a_ref, out_ref, chosen_ref, sent_ref = refs[:4]
     (
         len_ref, adapter_ref, placement_ref, q_ref, k_ref, v_ref, nk_ref, nv_ref,
         scores_ref, mixed_ref, sems, small_sems, w_held, w_sems,
-    ) = refs[3 + replicas :]
+    ) = refs[4:]
     requests = len_ref.shape[1]
     width = q_hbm.shape[1]
     per = requests // steps
@@ -234,20 +234,20 @@
 
     for copy in small[3:]:
         copy.wait()
-    route(slots, a_ref, adapter_ref, placement_ref, chosen_ref, sent_refs)
+    route(slots, a_ref, adapter_ref, placement_ref, chosen_ref, sent_ref)
     for columns, product in weights.products(a_ref[...]):
         out_ref[:, columns] = product.astype(jnp.bfloat16)
 
 
-def route(slots, a_ref, adapter_ref, placement_ref, chosen_ref, sent_refs):
-    replicas = len(sent_refs)
+def route(slots, a_ref, adapter_ref, placement_ref, chosen_ref, sent_ref):
+    replicas = sent_ref.shape[0] // CAP
     requests = adapter_ref.shape[1]
     table = placement_ref.shape[1]
     matches = _iota((table, requests), 0) == adapter_ref[...]
     placed = jnp.broadcast_to(placement_ref[...].astype(jnp.float32), (8, table))
     slot = _dot(placed.astype(jnp.bfloat16), matches.astype(jnp.bfloat16)).astype(jnp.int32)
     slot = slot[0:1, :]
-    holder = (slot // slots) ^ lax.axis_index("dp")
+    holder = slot // slots
     inside = slot % slots
     of_holder = _iota((max(replicas, 8), requests), 0) == holder
     earlier = _iota((requests, requests), 0) < _iota((requests, requests), 1)
@@ -261,9 +261,8 @@
     inner = jnp.sum(jnp.where(here, inside.astype(jnp.float32), 0.0), axis=1, keepdims=True)
     inner = jnp.broadcast_to(inner, (replicas * CAP, LANES)).astype(jnp.bfloat16)
     width = a_ref.shape[1]
-    for r, sent_ref in enumerate(sent_refs):
-        sent_ref[:, pl.ds(0, width)] = rows[r * CAP : (r + 1) * CAP, :]
-        sent_ref[:, pl.ds(width, LANES)] = inner[r * CAP : (r + 1) * CAP, :]
+    sent_ref[:, pl.ds(0, width)] = rows
+    sent_ref[:, pl.ds(width, LANES)] = inner
 
 
 def attend(
@@ -286,15 +285,15 @@
         new_value.reshape(requests * kv, width),
     ]
     return pl.pallas_call(
-        functools.partial(attend_kernel, heads, kv, cache, steps, block, replicas, slots),
+        functools.partial(attend_kernel, heads, kv, cache, steps, block, slots),
         in_specs=[ANY] * 9,
-        out_specs=[VMEM] * (3 + replicas),
+        out_specs=[VMEM] * 4,
         out_shape=[
             jax.ShapeDtypeStruct((requests, features), jnp.bfloat16),
             jax.ShapeDtypeStruct((requests, chunk), jnp.bfloat16),
             jax.ShapeDtypeStruct((replicas * CAP, requests), jnp.bfloat16),
-        ]
-        + [jax.ShapeDtypeStruct((CAP, features + LANES), jnp.bfloat16)] * replicas,
+            jax.ShapeDtypeStruct((replicas * CAP, features + LANES), jnp.bfloat16),
+        ],
         scratch_shapes=[pltpu.VMEM(x.shape, x.dtype) for x in small + operands]
         + [
             pltpu.VMEM((2, per * heads, columns), jnp.float32),
@@ -338,17 +337,15 @@
     )(*operands)
 
 
-def down_kernel(replicas, after, *refs):
-    received = refs[:replicas]
-    down_ref = refs[replicas]
-    mid_ref, inside_ref = refs[replicas + 1 + after :]
+def down_kernel(count, after, *refs):
+    received_ref, down_ref = refs[:2]
+    mid_ref = refs[2 + after]
     slots, rank, width = down_ref.shape
-    rows = jnp.concatenate([r[:, pl.ds(0, width)] for r in received], axis=0)
-    inside = jnp.concatenate([r[:, pl.ds(width, LANES)] for r in received], axis=0)
-    inside_ref[...] = inside
-    projected = _dot(rows, down_ref[...].reshape(slots * rank, width), 1, 1)
+    projected = _dot(
+        received_ref[:, pl.ds(0, width)], down_ref[...].reshape(slots * rank, width), 1, 1
+    )
     lane_slot = _iota(projected.shape, 1) // rank
-    mine = lane_slot == inside[:, 0:1].astype(jnp.int32)
+    mine = lane_slot == received_ref[:, pl.ds(width, LANES)][:, 0:1].astype(jnp.int32)
     projected = jnp.where(mine, projected, 0.0).astype(jnp.bfloat16)
     beside = LANES // rank
     some = projected.shape[0] // beside
@@ -357,33 +354,31 @@
         lane = _iota((slots * rank, LANES), 1) - b * rank
         fold = _iota((slots * rank, LANES), 0) % rank == lane
         packed = packed + _dot(projected[b * some : (b + 1) * some, :], fold.astype(jnp.bfloat16))
-    mid_ref[...] = packed.astype(jnp.bfloat16)
-
-
-def down(received, slot_down_weight, after=()):
-    replicas = len(received)
-    rows = replicas * CAP
-    return pl.pallas_call(
-        functools.partial(down_kernel, replicas, len(after)),
-        in_specs=[VMEM] * (replicas + 1) + [ANY] * len(after),
-        out_specs=[VMEM, VMEM],
-        out_shape=[
-            jax.ShapeDtypeStruct((rows * slot_down_weight.shape[1] // LANES, LANES), jnp.bfloat16),
-            jax.ShapeDtypeStruct((rows, LANES), jnp.bfloat16),
-        ],
+    packed = packed.astype(jnp.bfloat16)
+    for t in range(count):
+        mid_ref[pl.ds(t * some, some), :] = packed
+
+
+def down(received, slot_down_weight, count, after=()):
+    rows = received.shape[0] * slot_down_weight.shape[1] // LANES
+    return pl.pallas_call(
+        functools.partial(down_kernel, count, len(after)),
+        in_specs=[VMEM] * 2 + [ANY] * len(after),
+        out_specs=VMEM,
+        out_shape=jax.ShapeDtypeStruct((count * rows, LANES), jnp.bfloat16),
         compiler_params=PARAMS,
         name="down",
-    )(*received, slot_down_weight, *after)
-
-
-def up_kernel(parts, after, *refs):
-    mids = refs[:parts]
-    inside_ref, up_ref = refs[parts : parts + 2]
-    out_refs = refs[parts + 2 + after :]
+    )(received, slot_down_weight, *after)
+
+
+def up_kernel(count, after, *refs):
+    mid_ref, received_ref, up_ref = refs[:3]
+    out_ref = refs[3 + after]
     slots, rank, width = up_ref.shape
-    mid = mids[0][...].astype(jnp.float32)
-    for m in mids[1:]:
-        mid = mid + m[...].astype(jnp.float32)
+    some = mid_ref.shape[0] // count
+    mid = 0.0
+    for t in range(count):
+        mid = mid + mid_ref[pl.ds(t * some, some), :].astype(jnp.float32)
     mid = mid.astype(jnp.bfloat16)
     wide = []
     for b in range(LANES // rank):
@@ -391,36 +386,32 @@
         spread = _iota((LANES, slots * rank), 1) % rank == lane
         wide.append(_dot(mid, spread.astype(jnp.bfloat16)))
     wide = jnp.concatenate(wide, axis=0)
-    mine = _iota(wide.shape, 1) // rank == inside_ref[:, 0:1].astype(jnp.int32)
+    inside = received_ref[:, pl.ds(received_ref.shape[1] - LANES, LANES)][:, 0:1]
+    mine = _iota(wide.shape, 1) // rank == inside.astype(jnp.int32)
     wide = jnp.where(mine, wide, 0.0).astype(jnp.bfloat16)
-    delta = _dot(wide, up_ref[...].reshape(slots * rank, width)).astype(jnp.bfloat16)
-    for r, out_ref in enumerate(out_refs):
-        out_ref[...] = delta[r * CAP : (r + 1) * CAP, :]
-
-
-def up(mids, inside, slot_up_weight, after=()):
-    rows = inside.shape[0]
-    replicas = rows // CAP
-    width = slot_up_weight.shape[2]
-    return pl.pallas_call(
-        functools.partial(up_kernel, len(mids), len(after)),
-        in_specs=[VMEM] * (len(mids) + 2) + [ANY] * len(after),
-        out_specs=[VMEM] * replicas,
-        out_shape=[jax.ShapeDtypeStruct((CAP, width), jnp.bfloat16)] * replicas,
+    out_ref[...] = _dot(wide, up_ref[...].reshape(slots * rank, width)).astype(jnp.bfloat16)
+
+
+def up(mids, count, received, slot_up_weight, after=()):
+    return pl.pallas_call(
+        functools.partial(up_kernel, count, len(after)),
+        in_specs=[VMEM] * 3 + [ANY] * len(after),
+        out_specs=VMEM,
+        out_shape=jax.ShapeDtypeStruct(
+            (received.shape[0], slot_up_weight.shape[2]), jnp.bfloat16
+        ),
         compiler_params=PARAMS,
         name="up",
-    )(*mids, inside, slot_up_weight, *after)
-
-
-def settle_kernel(step, replicas, after, *refs):
-    returned = refs[:replicas]
-    chosen_ref, a_ref, residual_ref, w_hbm = refs[replicas : replicas + 4]
-    *out_refs, held, sems = refs[replicas + 4 + after :]
+    )(mids, received, slot_up_weight, *after)
+
+
+def settle_kernel(step, after, *refs):
+    returned_ref, chosen_ref, a_ref, residual_ref, w_hbm = refs[:5]
+    *out_refs, held, sems = refs[5 + after :]
     width = residual_ref.shape[1]
     weights = Weights(w_hbm, held, sems, column_owner(step) * width, width)
     weights.start()
-    rows = jnp.concatenate([r[...] for r in returned], axis=0)
-    delta = _dot(chosen_ref[...], rows, 0, 0)
+    delta = _dot(chosen_ref[...], returned_ref[...], 0, 0)
     total = residual_ref[...].astype(jnp.float32) + delta
     total = total + jnp.concatenate([p for _, p in weights.products(a_ref[...])], axis=1)
     for (start, chunk), out_ref in zip(chain_columns(width), out_refs):
@@ -428,18 +419,17 @@
 
 
 def settle(step, returned, chosen, attended, residual, weight, after=()):
-    replicas = len(returned)
     rows, width = residual.shape
     chains = chain_columns(width)
     return pl.pallas_call(
-        functools.partial(settle_kernel, step, replicas, len(after)),
-        in_specs=[VMEM] * (replicas + 3) + [ANY] * (1 + len(after)),
+        functools.partial(settle_kernel, step, len(after)),
+        in_specs=[VMEM] * 4 + [ANY] * (1 + len(after)),
         out_specs=[VMEM] * len(chains),
         out_shape=[jax.ShapeDtypeStruct((rows, chunk), jnp.float32) for _, chunk in chains],
         scratch_shapes=Weights.scratch(weight.shape[0], width),
         compiler_params=PARAMS,
         name="settle",
-    )(*returned, chosen, attended, residual, weight, *after)
+    )(returned, chosen, attended, residual, weight, *after)
 
 
 def finish_kernel(start, arrived_ref, settled_ref, *refs):
@@ -513,37 +503,30 @@
     order = ring_order(count)
     ring = [(order[p], order[(p + 1) % count]) for p in range(count)]
 
-    def exchange(blocks):
-        moved = [
-            lax.ppermute(blocks[r], "dp", [(i, i ^ r) for i in range(replicas)])
-            for r in range(1, replicas)
-        ]
-        return [blocks[0]] + moved
+    def exchange(x, axis):
+        return lax.all_to_all(x, axis, split_axis=0, concat_axis=0, tiled=True)
 
     def next_hop(step, chain, after):
         arrived = lax.ppermute(travelling[chain], "tensor", ring)
         travelling[chain] = hop(step, chain, arrived, attended, output_weight, block, after)
 
-    attended, first, chosen, *leaving = attend(
+    attended, first, chosen, leaving = attend(
         query, cached_key_rows, cached_value_rows, new_token_key, new_token_value, lengths,
         output_weight, request_adapter, placement, block, replicas, slot_down_weight.shape[0],
     )
     second = hop(0, 1, None, attended, output_weight, block)
-    rows_here = exchange(leaving)
-    mid, inside = down(rows_here, slot_down_weight, after=[second])
-    rank_sums = [mid] + [
-        lax.ppermute(mid, "tensor", [(i, (i + k) % count) for i in range(count)])
-        for k in range(1, count)
-    ]
-
-    travelling = [first, hold(second, after=[mid])]
-    next_hop(1, 0, after=rank_sums + travelling[1:])
-    next_hop(1, 1, after=())
-    deltas = up(rank_sums, inside, slot_up_weight, after=[travelling[1]])
-    returned = exchange(deltas)
+    rows_here = exchange(leaving, "dp")
+    rank_terms = down(rows_here, slot_down_weight, count, after=[second])
+    rank_sums = exchange(rank_terms, "tensor")
+
+    travelling = [first, hold(second, after=[rank_sums])]
+    next_hop(1, 0, after=travelling[1:])
+    deltas = up(rank_sums, count, rows_here, slot_up_weight, after=travelling[:1])
+    returned = exchange(deltas, "dp")
+    next_hop(1, 1, after=[returned])
     for step in range(2, count - 1):
         for chain in range(2):
-            next_hop(step, chain, after=returned if (step, chain) == (2, 0) else ())
+            next_hop(step, chain, after=[travelling[1 - chain]])
     settled = settle(
         count - 1, returned, chosen, attended, residual, output_weight, after=[travelling[1]]
     )

time: 90.4 us -> 110 us (1.22)
  waiting for transfers between devices: 29.7 us -> 47.3 us
  starting transfers between devices: 30 us -> 17.8 us
  blocking collectives: 0 us -> 8.72 us
  Pallas kernels: 27.8 us -> 31.4 us
  local copies, waits for them, and re-layouts: 2.39 us -> 4.11 us
    ppermute x4, waiting for transfers between devices: 4.4 us -> 30.9 us  [next_hop(): arrived = lax.ppermute(travelling[chain], 'tensor', ring)]
    ppermute x9 -> x0, waiting for transfers between devices: 14.3 us -> none  [the longest x6 11.1 us: exchange(): lax.ppermute(blocks[r], 'dp', [(i, i ^ r) for i in range(replicas)])]
    ppermute x4, starting transfers between devices: 16.8 us -> 7.78 us  [next_hop(): arrived = lax.ppermute(travelling[chain], 'tensor', ring)]
    all_to_all x0 -> x1, blocking collectives: none -> 8.72 us  [exchange(): return lax.all_to_all(x, axis, split_axis=0, concat_axis=0, tiled=True)]
    ppermute x9 -> x0, starting transfers between devices: 8.62 us -> none  [the longest x3 4.55 us: per_device(): lax.ppermute(mid, 'tensor', [(i, (i + k) % count) for i in range(count)])]
    all_to_all x0 -> x2, starting transfers between devices: none -> 6.99 us  [exchange(): return lax.all_to_all(x, axis, split_axis=0, concat_axis=0, tiled=True)]
    all_to_all x0 -> x2, waiting for transfers between devices: none -> 6.38 us  [exchange(): return lax.all_to_all(x, axis, split_axis=0, concat_axis=0, tiled=True)]
    pallas_call x3, Pallas kernels: 5.98 us -> 8.57 us  [the longest x1 4.53 us: settle(): pl.pallas_call(functools.partial(settle_kernel, step, len(after)), in_spe...]
  transfers between devices with their start and end apart: 15 -> 8, of which waited for: 10 -> 5; matrix products, arithmetic and copies ran while one was open for 0% -> 0% of each run, Pallas kernels for 20% -> 13%
where the time goes in v7:
time: 110 us; the launch traced here: 109 us
  waiting for transfers between devices  47.3 us (43%)
  Pallas kernels  31.4 us (29%)
  starting transfers between devices  17.8 us (16%)
  blocking collectives  8.72 us (8%)
  local copies, waits for them, and re-layouts  4.11 us (4%)
    ppermute x4, waiting for transfers between devices, next_hop(): arrived = lax.ppermute(travelling[chain], 'tensor', ring)  30.9 us
    pallas_call x5, Pallas kernels, hop(): pl.pallas_call(functools.partial(hop_kernel, step, block, start, arriving...  12.3 us
    ppermute x2, waiting for transfers between devices, per_device(): arrived = lax.ppermute(travelling[chain], 'tensor', ring)  9.98 us
    pallas_call x1, Pallas kernels, attend(): pl.pallas_call(functools.partial(attend_kernel, heads, kv, cache, steps,...  8.81 us
    all_to_all x1, blocking collectives, exchange(): return lax.all_to_all(x, axis, split_axis=0, concat_axis=0, tiled=True)  8.72 us
    ppermute x4, starting transfers between devices, next_hop(): arrived = lax.ppermute(travelling[chain], 'tensor', ring)  7.78 us
    all_to_all x2, starting transfers between devices, exchange(): return lax.all_to_all(x, axis, split_axis=0, concat_axis=0, tiled=True)  6.99 us
    all_to_all x2, waiting for transfers between devices, exchange(): return lax.all_to_all(x, axis, split_axis=0, concat_axis=0, tiled=True)  6.38 us
  transfers between devices with their start and end apart: 8, of which 5 were waited for; matrix products, arithmetic and copies ran while one was open for 0% of the time, Pallas kernels for 13%

profile of v7, /device:TPU:0, one launch (start us, length us, event | category | flops | bytes accessed | tf_op | source)
XLA Modules:
  0.0 109.4 jit_solution(11602935218564956120)
XLA Ops:
  0.0 8.8 %attend.1 = (bf16[256,1024]{1,0:T(8,128)(2,1)}, bf16[256,1280]{1,0:T(8,128)(2,1)}, bf16[256,256]{1,0:T(8,128)(2,1)}, bf16[256,1152]{1,0:T(8,128)(2,1)}) custom-call(s32[1,256]{1,0:T(1,128)} %bitcast.27, s32[1,256]{1,0:T(1,128)} %bitcast.28, s32[1,32]{1,0:T(1,128)} %bitcast.29, bf16[2048,128]{1,0:T(8,128)(2,1)} %bitcast.24, bf16[8192,128]{1,0:T(8,128)(2,1)} %bitcast.21, ...), custom_call_target="tpu_custom_call" | custom-call | tf_op jit(solution)/shard_map/attend/pallas_call | solution.py:287
  8.8 4.1 %collective-permute-start.1 = (bf16[256,1280]{1,0:T(8,128)(2,1)}, bf16[256,1280]{1,0:T(8,128)(2,1)}, u32[]{:S(2)}, u32[]{:S(2)}) collective-permute-start(bf16[256,1280]{1,0:T(8,128)(2,1)} %get-tuple-element.13), channel_id=1, source_target_pairs={{0,2},{2,3},{3,1},{1,0},{4,6},{6,7},{7,5},{5,4},{8,10},{10,11},{11... | collective-permute-start | bytes 1966088 | tf_op jit(solution)/shard_map/ppermute | solution.py:510
  12.9 3.5 %all-to-all-start = ((bf16[4,64,1152]{2,1,0:T(8,128)(2,1)}), bf16[4,64,1152]{2,1,0:T(8,128)(2,1)S(1)}, u32[]{:S(2)}, u32[]{:S(2)}) async-start(bf16[4,64,1152]{2,1,0:T(8,128)(2,1)} %bitcast.23), calls=%async_computation | async-start | bytes 1179648 | tf_op jit(solution)/shard_map/all_to_all | solution.py:507
  16.4 1.0 copy-done
  17.4 2.1 %hop.5.refs_2_.refs_0_ = bf16[256,768]{1,0:T(8,128)(2,1)S(1)} custom-call(bf16[256,1024]{1,0:T(8,128)(2,1)S(1)} %copy-done, bf16[1024,8192]{1,0:T(8,128)(2,1)} %refs_4_.1), custom_call_target="tpu_custom_call" | custom-call | tf_op jit(solution)/shard_map/hop/pallas_call | solution.py:329
  19.5 6.4 %all-to-all-done = bf16[4,64,1152]{2,1,0:T(8,128)(2,1)S(1)} async-done(((bf16[4,64,1152]{2,1,0:T(8,128)(2,1)}), bf16[4,64,1152]{2,1,0:T(8,128)(2,1)S(1)}, u32[]{:S(2)}, u32[]{:S(2)}) %all-to-all-start) | async-done | bytes 589856 | tf_op jit(solution)/shard_map/all_to_all | solution.py:507
  25.9 0.6 down.1
  26.6 8.7 %all_to_all.33 = bf16[4,128,128]{2,1,0:T(8,128)(2,1)S(1)} all-to-all(bf16[4,128,128]{2,1,0:T(8,128)(2,1)S(1)} %bitcast.20), channel_id=1, replica_groups=mesh['parts'=2,'dp'=4,'tensor'=4] {'tensor'}, dimensions={0} | all-to-all | bytes 262144 | tf_op jit(solution)/shard_map/all_to_all | solution.py:507
  35.3 0.0 collective-permute-done.1.refs_0_
  35.3 3.7 %hop.6.refs_3_ = bf16[256,1280]{1,0:T(8,128)(2,1)S(1)} custom-call(bf16[256,1280]{1,0:T(8,128)(2,1)} %collective-permute-done.1.refs_0_, bf16[256,1024]{1,0:T(8,128)(2,1)S(1)} %copy-done.1, bf16[1024,8192]{1,0:T(8,128)(2,1)} %refs_4_.1, bf16[256,768]{1,0:T(8,128)(2,1)S(1)} %hold.1.refs_3_), custom_call_target="tpu_custom_call" | custom-call | tf_op jit(solution)/shard_map/hop/pallas_call | solution.py:329
  39.0 3.4 %up.1 = bf16[256,2048]{1,0:T(8,128)(2,1)} custom-call(bf16[512,128]{1,0:T(8,128)(2,1)S(1)} %bitcast.19, bf16[256,1152]{1,0:T(8,128)(2,1)S(1)} %bitcast.17, bf16[8,64,2048]{2,1,0:T(8,128)(2,1)} %refs_2_.6, bf16[256,1280]{1,0:T(8,128)(2,1)S(1)} %hop.6.refs_3_), custom_call_target="tpu_custom_call" | custom-call | tf_op jit(solution)/shard_map/up/pallas_call | solution.py:396
  42.4 3.5 %all-to-all-start.2 = ((bf16[4,64,2048]{2,1,0:T(8,128)(2,1)}), bf16[4,64,2048]{2,1,0:T(8,128)(2,1)S(1)}, u32[]{:S(2)}, u32[]{:S(2)}) async-start(bf16[4,64,2048]{2,1,0:T(8,128)(2,1)} %bitcast.12), calls=%async_computation.2 | async-start | bytes 2097152 | tf_op jit(solution)/shard_map/all_to_all | solution.py:507
  45.9 0.8 collective-permute-start.3
  46.7 1.2 %collective-permute-start = (bf16[256,768]{1,0:T(8,128)(2,1)S(1)}, bf16[256,768]{1,0:T(8,128)(2,1)S(1)}, u32[]{:S(2)}, u32[]{:S(2)}) collective-permute-start(bf16[256,768]{1,0:T(8,128)(2,1)S(1)} %hold.1.refs_3_), channel_id=1, source_target_pairs={{0,2},{2,3},{3,1},{1,0},{4,6},{6,7},{7,5},{5,4},{8,10},{10,11},{11... | collective-permute-start | bytes 1179656 | tf_op jit(solution)/shard_map/ppermute | solution.py:510
  47.9 23.6 %collective-permute-done.refs_0_ = bf16[256,768]{1,0:T(8,128)(2,1)S(1)} collective-permute-done((bf16[256,768]{1,0:T(8,128)(2,1)S(1)}, bf16[256,768]{1,0:T(8,128)(2,1)S(1)}, u32[]{:S(2)}, u32[]{:S(2)}) %collective-permute-start) | collective-permute-done | bytes 393248 | tf_op jit(solution)/shard_map/ppermute | solution.py:510
  71.4 0.7 copy-done.5
  72.2 0.0 all-to-all-done.2
  72.2 1.0 copy-done.6
  73.2 2.0 %hop.7.refs_3_ = bf16[256,768]{1,0:T(8,128)(2,1)S(1)} custom-call(bf16[256,768]{1,0:T(8,128)(2,1)S(1)} %copy-done.6, bf16[256,1024]{1,0:T(8,128)(2,1)S(1)} %copy-done.1, bf16[1024,8192]{1,0:T(8,128)(2,1)} %refs_4_.1, bf16[256,2048]{1,0:T(8,128)(2,1)S(1)} %bitcast.14), custom_call_target="tpu_custom_call" | custom-call | tf_op jit(solution)/shard_map/hop/pallas_call | solution.py:329
  75.2 1.7 %collective-permute-start.2 = (bf16[256,768]{1,0:T(8,128)(2,1)S(1)}, bf16[256,768]{1,0:T(8,128)(2,1)S(1)}, u32[]{:S(2)}, u32[]{:S(2)}) collective-permute-start(bf16[256,768]{1,0:T(8,128)(2,1)S(1)} %hop.7.refs_3_), channel_id=1, source_target_pairs={{0,2},{2,3},{3,1},{1,0},{4,6},{6,7},{7,5},{5,4},{8,10},{10,11},{11... | collective-permute-start | bytes 1179656 | tf_op jit(solution)/shard_map/ppermute | solution.py:510
  76.9 2.6 %hop.8.refs_3_ = bf16[256,1280]{1,0:T(8,128)(2,1)S(1)} custom-call(bf16[256,1280]{1,0:T(8,128)(2,1)S(1)} %collective-permute-done.3.refs_0_, bf16[256,1024]{1,0:T(8,128)(2,1)S(1)} %copy-done.1, bf16[1024,8192]{1,0:T(8,128)(2,1)} %refs_4_.1, bf16[256,768]{1,0:T(8,128)(2,1)S(1)} %hop.7.refs_3_), custom_call_target="tpu_custom_call" | custom-call | tf_op jit(solution)/shard_map/hop/pallas_call | solution.py:329
  79.5 0.0 copy-start.3
  79.5 0.3 collective-permute-start.5
  79.9 7.4 %collective-permute-done.2.refs_0_ = bf16[256,768]{1,0:T(8,128)(2,1)S(1)} collective-permute-done((bf16[256,768]{1,0:T(8,128)(2,1)S(1)}, bf16[256,768]{1,0:T(8,128)(2,1)S(1)}, u32[]{:S(2)}, u32[]{:S(2)}) %collective-permute-start.2) | collective-permute-done | bytes 393248 | tf_op jit(solution)/shard_map/ppermute | solution.py:510
  87.2 2.0 %hop.9.refs_5_ = bf16[256,768]{1,0:T(8,128)(2,1)S(1)} custom-call(bf16[256,768]{1,0:T(8,128)(2,1)S(1)} %collective-permute-done.2.refs_0_, bf16[256,1024]{1,0:T(8,128)(2,1)S(1)} %copy-done.1, bf16[1024,8192]{1,0:T(8,128)(2,1)} %refs_4_.1, bf16[256,1280]{1,0:T(8,128)(2,1)S(1)} %hop.8.refs_3_), custom_call_target="tpu_custom_call" | custom-call | tf_op jit(solution)/shard_map/hop/pallas_call | solution.py:329
  89.2 2.6 %collective-permute-start.4 = (bf16[256,768]{1,0:T(8,128)(2,1)S(1)}, bf16[256,768]{1,0:T(8,128)(2,1)S(1)}, u32[]{:S(2)}, u32[]{:S(2)}) collective-permute-start(bf16[256,768]{1,0:T(8,128)(2,1)S(1)} %hop.9.refs_5_), channel_id=1, source_target_pairs={{0,2},{2,3},{3,1},{1,0},{4,6},{6,7},{7,5},{5,4},{8,10},{10,11},{11... | collective-permute-start | bytes 1179656 | tf_op jit(solution)/shard_map/ppermute | solution.py:535
  91.9 4.5 %settle.1 = (f32[256,1280]{1,0:T(8,128)}, f32[256,768]{1,0:T(8,128)S(1)}) custom-call(bf16[256,2048]{1,0:T(8,128)(2,1)S(1)} %bitcast.15, bf16[256,256]{1,0:T(8,128)(2,1)S(1)} %copy-done.7, bf16[256,1024]{1,0:T(8,128)(2,1)S(1)} %copy-done.1, bf16[256,2048]{1,0:T(8,128)(2,1)S(1)} %copy-done.3, bf16[1024,8192]{1,0:T(8,128)(2,1)} %refs_4_.1, ...), custom_call_target="tpu_custom_call" | custom-call | tf_op jit(solution)/shard_map/settle/pallas_call | solution.py:424
  96.4 4.9 %collective-permute-done.5.arrived_ref = bf16[256,1280]{1,0:T(8,128)(2,1)S(1)} collective-permute-done((bf16[256,1280]{1,0:T(8,128)(2,1)S(1)}, bf16[256,1280]{1,0:T(8,128)(2,1)S(1)}, u32[]{:S(2)}, u32[]{:S(2)}) %collective-permute-start.5) | collective-permute-done | bytes 655392 | tf_op jit(solution)/shard_map/ppermute | solution.py:535
  101.3 1.3 %copy-done.2 = f32[256,1280]{1,0:T(8,128)S(1)} copy-done((f32[256,1280]{1,0:T(8,128)S(1)}, f32[256,1280]{1,0:T(8,128)}, u32[]{:S(2)}) %copy-start.2) | copy-done | bytes 1310744
  102.6 0.9 finish.2.refs_0_
  103.5 5.1 %collective-permute-done.4.arrived_ref = bf16[256,768]{1,0:T(8,128)(2,1)S(1)} collective-permute-done((bf16[256,768]{1,0:T(8,128)(2,1)S(1)}, bf16[256,768]{1,0:T(8,128)(2,1)S(1)}, u32[]{:S(2)}, u32[]{:S(2)}) %collective-permute-start.4) | collective-permute-done | bytes 393248 | tf_op jit(solution)/shard_map/ppermute | solution.py:535
  108.6 0.8 finish.3
  (13 shorter events, 0.0 us)
Async XLA Ops:
  8.8 26.5 %collective-permute-start.1 = (bf16[256,1280]{1,0:T(8,128)(2,1)}, bf16[256,1280]{1,0:T(8,128)(2,1)}, u32[]{:S(2)}, u32[]{:S(2)}) collective-permute-start(bf16[256,1280]{1,0:T(8,128)(2,1)} %get-tuple-element.13), channel_id=1, source_target_pairs={{0,2},{2,3},{3,1},{1,0},{4,6},{6,7},{7,5},{5,4},{8,10},{10,11},{11... | collective-permute-start | bytes 1966088 | tf_op jit(solution)/shard_map/ppermute | solution.py:510
  12.9 13.0 %all-to-all-start = ((bf16[4,64,1152]{2,1,0:T(8,128)(2,1)}), bf16[4,64,1152]{2,1,0:T(8,128)(2,1)S(1)}, u32[]{:S(2)}, u32[]{:S(2)}) async-start(bf16[4,64,1152]{2,1,0:T(8,128)(2,1)} %bitcast.23), calls=%async_computation | async-start | bytes 1179648 | tf_op jit(solution)/shard_map/all_to_all | solution.py:507
  16.4 1.0 copy-start
  17.4 8.5 %copy-start.4 = (bf16[8,64,1024]{2,1,0:T(8,128)(2,1)S(1)}, bf16[8,64,1024]{2,1,0:T(8,128)(2,1)}, u32[]{:S(2)}) copy-start(bf16[8,64,1024]{2,1,0:T(8,128)(2,1)} %refs_1_.3) | copy-start | bytes 3145732
  19.5 15.8 %copy-start.1 = (bf16[256,1024]{1,0:T(8,128)(2,1)S(1)}, bf16[256,1024]{1,0:T(8,128)(2,1)}, u32[]{:S(2)}) copy-start(bf16[256,1024]{1,0:T(8,128)(2,1)} %get-tuple-element.11.refs_0_.refs_1_.refs_2_) | copy-start | bytes 1572868
  42.4 29.8 %all-to-all-start.2 = ((bf16[4,64,2048]{2,1,0:T(8,128)(2,1)}), bf16[4,64,2048]{2,1,0:T(8,128)(2,1)S(1)}, u32[]{:S(2)}, u32[]{:S(2)}) async-start(bf16[4,64,2048]{2,1,0:T(8,128)(2,1)} %bitcast.12), calls=%async_computation.2 | async-start | bytes 2097152 | tf_op jit(solution)/shard_map/all_to_all | solution.py:507
  45.9 31.0 %collective-permute-start.3 = (bf16[256,1280]{1,0:T(8,128)(2,1)S(1)}, bf16[256,1280]{1,0:T(8,128)(2,1)S(1)}, u32[]{:S(2)}, u32[]{:S(2)}) collective-permute-start(bf16[256,1280]{1,0:T(8,128)(2,1)S(1)} %hop.6.refs_3_), channel_id=1, source_target_pairs={{0,2},{2,3},{3,1},{1,0},{4,6},{6,7},{7,5},{5,4},{8,10},{10,11},{11... | collective-permute-start | bytes 1966088 | tf_op jit(solution)/shard_map/ppermute | solution.py:510
  46.7 24.7 %collective-permute-start = (bf16[256,768]{1,0:T(8,128)(2,1)S(1)}, bf16[256,768]{1,0:T(8,128)(2,1)S(1)}, u32[]{:S(2)}, u32[]{:S(2)}) collective-permute-start(bf16[256,768]{1,0:T(8,128)(2,1)S(1)} %hold.1.refs_3_), channel_id=1, source_target_pairs={{0,2},{2,3},{3,1},{1,0},{4,6},{6,7},{7,5},{5,4},{8,10},{10,11},{11... | collective-permute-start | bytes 1179656 | tf_op jit(solution)/shard_map/ppermute | solution.py:510
  71.4 0.7 copy-start.5
  72.2 1.0 copy-start.6
  75.2 12.0 %collective-permute-start.2 = (bf16[256,768]{1,0:T(8,128)(2,1)S(1)}, bf16[256,768]{1,0:T(8,128)(2,1)S(1)}, u32[]{:S(2)}, u32[]{:S(2)}) collective-permute-start(bf16[256,768]{1,0:T(8,128)(2,1)S(1)} %hop.7.refs_3_), channel_id=1, source_target_pairs={{0,2},{2,3},{3,1},{1,0},{4,6},{6,7},{7,5},{5,4},{8,10},{10,11},{11... | collective-permute-start | bytes 1179656 | tf_op jit(solution)/shard_map/ppermute | solution.py:510
  79.5 12.4 %copy-start.3 = (bf16[256,2048]{1,0:T(8,128)(2,1)S(1)}, bf16[256,2048]{1,0:T(8,128)(2,1)}, u32[]{:S(2)}) copy-start(bf16[256,2048]{1,0:T(8,128)(2,1)} %refs_3_.1) | copy-start | bytes 3145732
  79.5 12.4 %copy-start.7 = (bf16[256,256]{1,0:T(8,128)(2,1)S(1)}, bf16[256,256]{1,0:T(8,128)(2,1)}, u32[]{:S(2)}) copy-start(bf16[256,256]{1,0:T(8,128)(2,1)} %get-tuple-element.14.refs_1_) | copy-start | bytes 393220
  79.5 21.8 %collective-permute-start.5 = (bf16[256,1280]{1,0:T(8,128)(2,1)S(1)}, bf16[256,1280]{1,0:T(8,128)(2,1)S(1)}, u32[]{:S(2)}, u32[]{:S(2)}) collective-permute-start(bf16[256,1280]{1,0:T(8,128)(2,1)S(1)} %hop.8.refs_3_), channel_id=1, source_target_pairs={{0,2},{2,3},{3,1},{1,0},{4,6},{6,7},{7,5},{5,4},{8,10},{10,11},{11... | collective-permute-start | bytes 1966088 | tf_op jit(solution)/shard_map/ppermute | solution.py:535
  89.2 19.4 %collective-permute-start.4 = (bf16[256,768]{1,0:T(8,128)(2,1)S(1)}, bf16[256,768]{1,0:T(8,128)(2,1)S(1)}, u32[]{:S(2)}, u32[]{:S(2)}) collective-permute-start(bf16[256,768]{1,0:T(8,128)(2,1)S(1)} %hop.9.refs_5_), channel_id=1, source_target_pairs={{0,2},{2,3},{3,1},{1,0},{4,6},{6,7},{7,5},{5,4},{8,10},{10,11},{11... | collective-permute-start | bytes 1179656 | tf_op jit(solution)/shard_map/ppermute | solution.py:535
  101.3 1.3 %copy-start.2 = (f32[256,1280]{1,0:T(8,128)S(1)}, f32[256,1280]{1,0:T(8,128)}, u32[]{:S(2)}) copy-start(f32[256,1280]{1,0:T(8,128)} %get-tuple-element.16.settled_ref) | copy-start | bytes 3932164

commit v8 on v6

--- a/solution.py
+++ b/solution.py
@@ -8,7 +8,7 @@
 from jax.experimental.pallas import tpu as pltpu
 from jax.sharding import PartitionSpec as P
 
-GROUP = 8
+GROUP = 4
 CAP = 64
 LANES = 128
 MASKED = -1e30
@@ -70,9 +70,11 @@
         for copy in self.copies:
             copy.start()
 
-    def products(self, a):
+    def wait(self):
         for copy in self.copies:
             copy.wait()
+
+    def products(self, a):
         width = self.held.shape[1]
         for at in range(0, width, PIECE):
             columns = pl.ds(at, min(PIECE, width - at))
@@ -169,10 +171,12 @@
     fresh_distance = col // kv - row // heads
     ones = jnp.ones((max(group_cols, per * kv), LANES), jnp.bfloat16)
 
+    def arrive(step):
+        part(0, step).wait()
+        part(1, step).wait()
+
     def scores(step):
         side = step % 2
-        part(0, step).wait()
-        part(1, step).wait()
         q_at = step * per * heads
         k_at = step * per * cache * kv
         for g in range(groups):
@@ -182,14 +186,13 @@
                 1,
                 1,
             )
-        if step == 0:
-            small[0].wait()
         scores_ref[side, :, pl.ds(group_cols, per * kv)] = _dot(
             q_ref[pl.ds(q_at, per * heads), :], nk_ref[pl.ds(step * per * kv, per * kv), :], 1, 1
         )
 
-    scores(0)
-    small[1].wait()
+    for copy in small:
+        copy.wait()
+    plan_routes(slots, adapter_ref, placement_ref, chosen_ref, sent_refs)
     counts = len_ref[...].astype(jnp.float32)
     all_groups = requests // GROUP
     of_group = _iota((all_groups, requests), 1) // GROUP == _iota((all_groups, requests), 0)
@@ -199,15 +202,16 @@
     position = (_iota((all_groups, group_cols), 1) // kv) % cache
     length_bias = jnp.where(position.astype(jnp.float32) < counts, 0.0, MASKED)
 
+    arrive(0)
+    scores(0)
     for step in range(steps):
         side = step % 2
-        if step + 1 < steps:
-            scores(step + 1)
         k_at = step * per * cache * kv
         f_at = step * per * kv
         part(2, step).wait()
-        if step == 0:
-            small[2].wait()
+        if step + 1 < steps:
+            arrive(step + 1)
+            scores(step + 1)
         held = []
         fresh = []
         for g in range(groups):
@@ -217,29 +221,30 @@
             new = scores_ref[side, rows, pl.ds(group_cols, per * kv)]
             new = jnp.where(fresh_kv & (fresh_distance == g * GROUP), new, MASKED)
             top = row_max([cached, new])
-            held.append(jnp.exp2((cached - top) * scale).astype(jnp.bfloat16))
+            cached = jnp.exp2((cached - top) * scale).astype(jnp.bfloat16)
             fresh.append(jnp.exp2((new - top) * scale).astype(jnp.bfloat16))
+            values = v_ref[pl.ds(k_at + g * group_cols, group_cols), :]
+            held.append(_dot(cached, jnp.concatenate([values, ones[:group_cols]], axis=1)))
         values = jnp.concatenate([nv_ref[pl.ds(f_at, per * kv), :], ones[: per * kv]], axis=1)
         fresh = _dot(jnp.concatenate(fresh, axis=0), values)
         for g in range(groups):
             rows = slice(g * group_rows, (g + 1) * group_rows)
-            values = v_ref[pl.ds(k_at + g * group_cols, group_cols), :]
-            values = jnp.concatenate([values, ones[:group_cols]], axis=1)
-            mixed = fresh[rows, :] + _dot(held[g], values)
-            mixed_ref[side, rows, :] = mixed[:, :width] / mixed[:, width : width + 1]
+            mixed = fresh[rows, :] + held[g]
+            mixed_ref[side, rows, :] = mixed[:, :width] / mixed[:, width:]
         for h in range(heads):
             a_ref[pl.ds(step * per, per), pl.ds(h * width, width)] = mixed_ref[
                 side, pl.ds(h, per, stride=heads), :
             ].astype(jnp.bfloat16)
 
-    for copy in small[3:]:
-        copy.wait()
-    route(slots, a_ref, adapter_ref, placement_ref, chosen_ref, sent_refs)
+    weights.wait()
     for columns, product in weights.products(a_ref[...]):
         out_ref[:, columns] = product.astype(jnp.bfloat16)
-
-
-def route(slots, a_ref, adapter_ref, placement_ref, chosen_ref, sent_refs):
+    rows = _dot(chosen_ref[...], a_ref[...]).astype(jnp.bfloat16)
+    for r, sent_ref in enumerate(sent_refs):
+        sent_ref[:, pl.ds(0, heads * width)] = rows[r * CAP : (r + 1) * CAP, :]
+
+
+def plan_routes(slots, adapter_ref, placement_ref, chosen_ref, sent_refs):
     replicas = len(sent_refs)
     requests = adapter_ref.shape[1]
     table = placement_ref.shape[1]
@@ -255,14 +260,11 @@
     before = jnp.sum(jnp.where(of_holder, before, 0.0), axis=0, keepdims=True).astype(jnp.int32)
     target = holder * CAP + before
     here = _iota((replicas * CAP, requests), 0) == target
-    chosen = here.astype(jnp.bfloat16)
-    chosen_ref[...] = chosen
-    rows = _dot(chosen, a_ref[...]).astype(jnp.bfloat16)
+    chosen_ref[...] = here.astype(jnp.bfloat16)
     inner = jnp.sum(jnp.where(here, inside.astype(jnp.float32), 0.0), axis=1, keepdims=True)
     inner = jnp.broadcast_to(inner, (replicas * CAP, LANES)).astype(jnp.bfloat16)
-    width = a_ref.shape[1]
+    width = sent_refs[0].shape[1] - LANES
     for r, sent_ref in enumerate(sent_refs):
-        sent_ref[:, pl.ds(0, width)] = rows[r * CAP : (r + 1) * CAP, :]
         sent_ref[:, pl.ds(width, LANES)] = inner[r * CAP : (r + 1) * CAP, :]
 
 
@@ -317,6 +319,7 @@
     first = column_owner(step) * block + start
     weights = Weights(w_hbm, held, sems, first, chunk)
     weights.start()
+    weights.wait()
     for columns, product in weights.products(a_ref[...]):
         if arriving:
             product = product + arrived_ref[:, columns].astype(jnp.float32)
@@ -422,6 +425,7 @@
     rows = jnp.concatenate([r[...] for r in returned], axis=0)
     delta = _dot(chosen_ref[...], rows, 0, 0)
     total = residual_ref[...].astype(jnp.float32) + delta
+    weights.wait()
     total = total + jnp.concatenate([p for _, p in weights.products(a_ref[...])], axis=1)
     for (start, chunk), out_ref in zip(chain_columns(width), out_refs):
         out_ref[...] = total[:, start : start + chunk]
@@ -520,8 +524,11 @@
         ]
         return [blocks[0]] + moved
 
+    def forward(x):
+        return lax.ppermute(x, "tensor", ring)
+
     def next_hop(step, chain, after):
-        arrived = lax.ppermute(travelling[chain], "tensor", ring)
+        arrived = forward(travelling[chain])
         travelling[chain] = hop(step, chain, arrived, attended, output_weight, block, after)
 
     attended, first, chosen, *leaving = attend(
@@ -536,8 +543,12 @@
         for k in range(1, count)
     ]
 
-    travelling = [first, hold(second, after=[mid])]
-    next_hop(1, 0, after=rank_sums + travelling[1:])
+    arrived = forward(first)
+    second = hold(second, after=[mid, arrived])
+    travelling = [
+        hop(1, 0, arrived, attended, output_weight, block, after=rank_sums + [second]),
+        second,
+    ]
     next_hop(1, 1, after=())
     deltas = up(rank_sums, inside, slot_up_weight, after=[travelling[1]])
     returned = exchange(deltas)
@@ -549,7 +560,7 @@
     )
     out = None
     for chain in range(2):
-        arrived = lax.ppermute(travelling[chain], "tensor", ring)
+        arrived = forward(travelling[chain])
         out = finish(chain, arrived, settled[chain], out, block)
     return out
 

time: 90.4 us -> 103 us (1.14)
  starting transfers between devices: 30 us -> 54.7 us
  waiting for transfers between devices: 29.7 us -> 18.1 us
    ppermute x6, starting transfers between devices: 21.4 us -> 46.4 us  [forward(): return lax.ppermute(x, 'tensor', ring)]
    ppermute x6, waiting for transfers between devices: 11.1 us -> 4.26 us  [exchange(): lax.ppermute(blocks[r], 'dp', [(i, i ^ r) for i in range(replicas)])]
    ppermute x3, waiting for transfers between devices: 3.2 us -> 0.01 us  [per_device(): lax.ppermute(mid, 'tensor', [(i, (i + k) % count) for i in range(count)])]
    ppermute x6, waiting for transfers between devices: 15.4 us -> 13.8 us  [forward(): return lax.ppermute(x, 'tensor', ring)]
  transfers between devices with their start and end apart: 15 -> 15, of which waited for: 10 -> 6; matrix products, arithmetic and copies ran while one was open for 0% -> 0% of each run, Pallas kernels for 20% -> 18%
where the time goes in v8:
time: 103 us
  starting transfers between devices  54.7 us (53%)
  Pallas kernels  27.2 us (26%)
  waiting for transfers between devices  18.1 us (18%)
  local copies, waits for them, and re-layouts  2.39 us (2%)
    ppermute x6, starting transfers between devices, forward(): return lax.ppermute(x, 'tensor', ring)  46.4 us
    ppermute x6, waiting for transfers between devices, forward(): return lax.ppermute(x, 'tensor', ring)  13.8 us
    pallas_call x5, Pallas kernels, hop(): pl.pallas_call(functools.partial(hop_kernel, step, block, start, arriving...  11.2 us
    pallas_call x1, Pallas kernels, attend(): pl.pallas_call(functools.partial(attend_kernel, heads, kv, cache, steps,...  8.32 us
    ppermute x3, starting transfers between devices, per_device(): lax.ppermute(mid, 'tensor', [(i, (i + k) % count) for i in range(count)])  4.54 us
    pallas_call x1, Pallas kernels, settle(): pl.pallas_call(functools.partial(settle_kernel, step, replicas, len(after...  4.51 us
    ppermute x6, waiting for transfers between devices, exchange(): lax.ppermute(blocks[r], 'dp', [(i, i ^ r) for i in range(replicas)])  4.26 us
    ppermute x6, starting transfers between devices, exchange(): lax.ppermute(blocks[r], 'dp', [(i, i ^ r) for i in range(replicas)])  3.79 us
  transfers between devices with their start and end apart: 15, of which 6 were waited for; matrix products, arithmetic and copies ran while one was open for 0% of the time, Pallas kernels for 18%

profile of v8, /device:TPU:0, one launch (start us, length us, event | category | flops | bytes accessed | tf_op | source)
XLA Modules:
  0.0 102.6 jit_solution(12818023908616431019)
XLA Ops:
  0.0 8.3 %attend.1 = (bf16[256,1024]{1,0:T(8,128)(2,1)}, bf16[256,1280]{1,0:T(8,128)(2,1)}, bf16[256,256]{1,0:T(8,128)(2,1)}, bf16[64,1152]{1,0:T(8,128)(2,1)}, bf16[64,1...) custom-call(s32[1,256]{1,0:T(1,128)} %bitcast.13, s32[1,256]{1,0:T(1,128)} %bitcast.14, ...), custom_call_target="tpu_custom_call" | custom-call | tf_op jit(solution)/shard_map/attend/pallas_call | solution.py:290
  8.3 4.1 %collective-permute-start.3 = (bf16[256,1280]{1,0:T(8,128)(2,1)}, bf16[256,1280]{1,0:T(8,128)(2,1)S(1)}, u32[]{:S(2)}, u32[]{:S(2)}) collective-permute-start(bf16[256,1280]{1,0:T(8,128)(2,1)} %get-tuple-element.26), channel_id=1, source_target_pairs={{0,2},{2,3},{3,1},{1,0},{4,6},{6,7},{7,5},{5,4},{8,10},{10,11},{11... | collective-permute-start | bytes 1966088 | tf_op jit(solution)/shard_map/ppermute | solution.py:528
  12.4 1.5 %collective-permute-start.1 = (bf16[64,1152]{1,0:T(8,128)(2,1)}, bf16[64,1152]{1,0:T(8,128)(2,1)S(1)}, u32[]{:S(2)}, u32[]{:S(2)}) collective-permute-start(bf16[64,1152]{1,0:T(8,128)(2,1)} %get-tuple-element.23), channel_id=1, source_target_pairs={{0,8},{4,12},{8,0},{12,4},{1,9},{5,13},{9,1},{13,5},{2,10},{6,14},... | collective-permute-start | bytes 442376 | tf_op jit(solution)/shard_map/ppermute | solution.py:522
  13.9 0.4 collective-permute-start.2
  14.3 1.0 %copy-done = bf16[256,1024]{1,0:T(8,128)(2,1)S(1)} copy-done((bf16[256,1024]{1,0:T(8,128)(2,1)S(1)}, bf16[256,1024]{1,0:T(8,128)(2,1)}, u32[]{:S(2)}) %copy-start) | copy-done | bytes 524312
  15.3 2.1 %hop.5.refs_5_.refs_0_ = bf16[256,768]{1,0:T(8,128)(2,1)S(1)} custom-call(bf16[256,1024]{1,0:T(8,128)(2,1)S(1)} %copy-done, bf16[1024,8192]{1,0:T(8,128)(2,1)} %refs_2_.7), custom_call_target="tpu_custom_call" | custom-call | tf_op jit(solution)/shard_map/hop/pallas_call | solution.py:333
  17.4 1.9 %collective-permute-done.1.refs_2_ = bf16[64,1152]{1,0:T(8,128)(2,1)S(1)} collective-permute-done((bf16[64,1152]{1,0:T(8,128)(2,1)}, bf16[64,1152]{1,0:T(8,128)(2,1)S(1)}, u32[]{:S(2)}, u32[]{:S(2)}) %collective-permute-start.1) | collective-permute-done | bytes 147488 | tf_op jit(solution)/shard_map/ppermute | solution.py:522
  19.3 2.4 %collective-permute-done.2.refs_3_ = bf16[64,1152]{1,0:T(8,128)(2,1)S(1)} collective-permute-done((bf16[64,1152]{1,0:T(8,128)(2,1)}, bf16[64,1152]{1,0:T(8,128)(2,1)S(1)}, u32[]{:S(2)}, u32[]{:S(2)}) %collective-permute-start.2) | collective-permute-done | bytes 147488 | tf_op jit(solution)/shard_map/ppermute | solution.py:522
  21.7 0.6 down.1
  22.4 1.9 %collective-permute-start.8 = (bf16[128,128]{1,0:T(8,128)(2,1)S(1)}, bf16[128,128]{1,0:T(8,128)(2,1)S(1)}, u32[]{:S(2)}, u32[]{:S(2)}) collective-permute-start(bf16[128,128]{1,0:T(8,128)(2,1)S(1)} %get-tuple-element.25.refs_1_.refs_0_.refs_3_), channel_id=1, source_target_pairs={{0,2},{1,3},{2,0},{3,1},{4,6},{5,7},{6,4},{7,5},{8,10},{9,11},{10,... | collective-permute-start | bytes 98312 | tf_op jit(solution)/shard_map/ppermute | solution.py:542
  24.3 2.6 %collective-permute-start.9 = (bf16[128,128]{1,0:T(8,128)(2,1)S(1)}, bf16[128,128]{1,0:T(8,128)(2,1)S(1)}, u32[]{:S(2)}, u32[]{:S(2)}) collective-permute-start(bf16[128,128]{1,0:T(8,128)(2,1)S(1)} %get-tuple-element.25.refs_1_.refs_0_.refs_3_), channel_id=1, source_target_pairs={{0,3},{1,0},{2,1},{3,2},{4,7},{5,4},{6,5},{7,6},{8,11},{9,8},{10,9... | collective-permute-start | bytes 98312 | tf_op jit(solution)/shard_map/ppermute | solution.py:542
  26.9 0.9 collective-permute-done.3.refs_2_.refs_0_
  27.8 3.3 %collective-permute-start.4 = (bf16[256,768]{1,0:T(8,128)(2,1)S(1)}, bf16[256,768]{1,0:T(8,128)(2,1)S(1)}, u32[]{:S(2)}, u32[]{:S(2)}) collective-permute-start(bf16[256,768]{1,0:T(8,128)(2,1)S(1)} %hold.1.refs_7_), channel_id=1, source_target_pairs={{0,2},{2,3},{3,1},{1,0},{4,6},{6,7},{7,5},{5,4},{8,10},{10,11},{11... | collective-permute-start | bytes 1179656 | tf_op jit(solution)/shard_map/ppermute | solution.py:528
  31.2 2.6 %hop.8 = bf16[256,1280]{1,0:T(8,128)(2,1)S(1)} custom-call(bf16[256,1280]{1,0:T(8,128)(2,1)S(1)} %collective-permute-done.3.refs_2_.refs_0_, bf16[256,1024]{1,0:T(8,128)(2,1)S(1)} %copy-done.1, bf16[1024,8192]{1,0:T(8,128)(2,1)} %refs_2_.7, bf16[128,128]{1,0:T(8,128)(2,1)S(1)} %get-tuple-element.25.refs_1_.refs_0_.refs_3_, ...), custom_call_target="tpu_custom_call" | custom-call | tf_op jit(solution)/shard_map/hop/pallas_call | solution.py:333
  33.8 8.1 %collective-permute-start.13 = (bf16[256,1280]{1,0:T(8,128)(2,1)S(1)}, bf16[256,1280]{1,0:T(8,128)(2,1)S(1)}, u32[]{:S(2)}, u32[]{:S(2)}) collective-permute-start(bf16[256,1280]{1,0:T(8,128)(2,1)S(1)} %hop.8), channel_id=1, source_target_pairs={{0,2},{2,3},{3,1},{1,0},{4,6},{6,7},{7,5},{5,4},{8,10},{10,11},{11... | collective-permute-start | bytes 1966088 | tf_op jit(solution)/shard_map/ppermute | solution.py:528
  41.9 2.0 %hop.6.refs_6_ = bf16[256,768]{1,0:T(8,128)(2,1)S(1)} custom-call(bf16[256,768]{1,0:T(8,128)(2,1)S(1)} %collective-permute-done.4.refs_0_, bf16[256,1024]{1,0:T(8,128)(2,1)S(1)} %copy-done.1, bf16[1024,8192]{1,0:T(8,128)(2,1)} %refs_2_.7), custom_call_target="tpu_custom_call" | custom-call | tf_op jit(solution)/shard_map/hop/pallas_call | solution.py:333
  43.9 0.8 up.1
  44.7 0.1 collective-permute-start.10
  44.8 1.6 %collective-permute-start.11 = (bf16[64,2048]{1,0:T(8,128)(2,1)S(1)}, bf16[64,2048]{1,0:T(8,128)(2,1)S(1)}, u32[]{:S(2)}, u32[]{:S(2)}) collective-permute-start(bf16[64,2048]{1,0:T(8,128)(2,1)S(1)} %get-tuple-element.30), channel_id=1, source_target_pairs={{0,8},{4,12},{8,0},{12,4},{1,9},{5,13},{9,1},{13,5},{2,10},{6,14},... | collective-permute-start | bytes 786440 | tf_op jit(solution)/shard_map/ppermute | solution.py:522
  46.3 0.3 collective-permute-start.12
  46.6 17.5 %collective-permute-start.5 = (bf16[256,768]{1,0:T(8,128)(2,1)S(1)}, bf16[256,768]{1,0:T(8,128)(2,1)S(1)}, u32[]{:S(2)}, u32[]{:S(2)}) collective-permute-start(bf16[256,768]{1,0:T(8,128)(2,1)S(1)} %hop.6.refs_6_), channel_id=1, source_target_pairs={{0,2},{2,3},{3,1},{1,0},{4,6},{6,7},{7,5},{5,4},{8,10},{10,11},{11... | collective-permute-start | bytes 1179656 | tf_op jit(solution)/shard_map/ppermute | solution.py:528
  64.2 2.8 %collective-permute-done.13.refs_0_ = bf16[256,1280]{1,0:T(8,128)(2,1)S(1)} collective-permute-done((bf16[256,1280]{1,0:T(8,128)(2,1)S(1)}, bf16[256,1280]{1,0:T(8,128)(2,1)S(1)}, u32[]{:S(2)}, u32[]{:S(2)}) %collective-permute-start.13) | collective-permute-done | bytes 655392 | tf_op jit(solution)/shard_map/ppermute | solution.py:528
  67.0 2.6 %hop.9 = bf16[256,1280]{1,0:T(8,128)(2,1)S(1)} custom-call(bf16[256,1280]{1,0:T(8,128)(2,1)S(1)} %collective-permute-done.13.refs_0_, bf16[256,1024]{1,0:T(8,128)(2,1)S(1)} %copy-done.1, bf16[1024,8192]{1,0:T(8,128)(2,1)} %refs_2_.7, bf16[64,2048]{1,0:T(8,128)(2,1)S(1)} %get-tuple-element.28.refs_0_.refs_3_, ...), custom_call_target="tpu_custom_call" | custom-call | tf_op jit(solution)/shard_map/hop/pallas_call | solution.py:333
  69.6 9.2 %collective-permute-start.14 = (bf16[256,1280]{1,0:T(8,128)(2,1)S(1)}, bf16[256,1280]{1,0:T(8,128)(2,1)S(1)}, u32[]{:S(2)}, u32[]{:S(2)}) collective-permute-start(bf16[256,1280]{1,0:T(8,128)(2,1)S(1)} %hop.9), channel_id=1, source_target_pairs={{0,2},{2,3},{3,1},{1,0},{4,6},{6,7},{7,5},{5,4},{8,10},{10,11},{11... | collective-permute-start | bytes 1966088 | tf_op jit(solution)/shard_map/ppermute | solution.py:528
  78.8 2.0 %hop.7.refs_8_ = bf16[256,768]{1,0:T(8,128)(2,1)S(1)} custom-call(bf16[256,768]{1,0:T(8,128)(2,1)S(1)} %collective-permute-done.5.refs_0_, bf16[256,1024]{1,0:T(8,128)(2,1)S(1)} %copy-done.1, bf16[1024,8192]{1,0:T(8,128)(2,1)} %refs_2_.7), custom_call_target="tpu_custom_call" | custom-call | tf_op jit(solution)/shard_map/hop/pallas_call | solution.py:333
  80.8 4.1 %collective-permute-start.6 = (bf16[256,768]{1,0:T(8,128)(2,1)S(1)}, bf16[256,768]{1,0:T(8,128)(2,1)S(1)}, u32[]{:S(2)}, u32[]{:S(2)}) collective-permute-start(bf16[256,768]{1,0:T(8,128)(2,1)S(1)} %hop.7.refs_8_), channel_id=1, source_target_pairs={{0,2},{2,3},{3,1},{1,0},{4,6},{6,7},{7,5},{5,4},{8,10},{10,11},{11... | collective-permute-start | bytes 1179656 | tf_op jit(solution)/shard_map/ppermute | solution.py:528
  85.0 4.5 %settle.1 = (f32[256,1280]{1,0:T(8,128)}, f32[256,768]{1,0:T(8,128)S(1)}) custom-call(bf16[64,2048]{1,0:T(8,128)(2,1)S(1)} %get-tuple-element.28.refs_0_.refs_3_, bf16[64,2048]{1,0:T(8,128)(2,1)S(1)} %collective-permute-done.10.refs_1_.refs_4_, bf16[64,2048]{1,0:T(8,128)(2,1)S(1)} %collective-permute-done.11.refs_2_.refs_5_, ...), custom_call_target="tpu_custom_call" | custom-call | tf_op jit(solution)/shard_map/settle/pallas_call | solution.py:438
  89.5 4.4 %collective-permute-done.14.arrived_ref = bf16[256,1280]{1,0:T(8,128)(2,1)S(1)} collective-permute-done((bf16[256,1280]{1,0:T(8,128)(2,1)S(1)}, bf16[256,1280]{1,0:T(8,128)(2,1)S(1)}, u32[]{:S(2)}, u32[]{:S(2)}) %collective-permute-start.14) | collective-permute-done | bytes 655392 | tf_op jit(solution)/shard_map/ppermute | solution.py:528
  93.9 1.3 %copy-done.3 = f32[256,1280]{1,0:T(8,128)S(1)} copy-done((f32[256,1280]{1,0:T(8,128)S(1)}, f32[256,1280]{1,0:T(8,128)}, u32[]{:S(2)}) %copy-start.3) | copy-done | bytes 1310744
  95.2 0.9 finish.2.refs_0_
  96.1 5.6 %collective-permute-done.6.arrived_ref = bf16[256,768]{1,0:T(8,128)(2,1)S(1)} collective-permute-done((bf16[256,768]{1,0:T(8,128)(2,1)S(1)}, bf16[256,768]{1,0:T(8,128)(2,1)S(1)}, u32[]{:S(2)}, u32[]{:S(2)}) %collective-permute-start.6) | collective-permute-done | bytes 393248 | tf_op jit(solution)/shard_map/ppermute | solution.py:528
  101.8 0.8 finish.3
  (26 shorter events, 0.1 us)
Async XLA Ops:
  8.3 19.5 %collective-permute-start.3 = (bf16[256,1280]{1,0:T(8,128)(2,1)}, bf16[256,1280]{1,0:T(8,128)(2,1)S(1)}, u32[]{:S(2)}, u32[]{:S(2)}) collective-permute-start(bf16[256,1280]{1,0:T(8,128)(2,1)} %get-tuple-element.26), channel_id=1, source_target_pairs={{0,2},{2,3},{3,1},{1,0},{4,6},{6,7},{7,5},{5,4},{8,10},{10,11},{11... | collective-permute-start | bytes 1966088 | tf_op jit(solution)/shard_map/ppermute | solution.py:528
  12.4 5.0 %collective-permute-start = (bf16[64,1152]{1,0:T(8,128)(2,1)}, bf16[64,1152]{1,0:T(8,128)(2,1)S(1)}, u32[]{:S(2)}, u32[]{:S(2)}) collective-permute-start(bf16[64,1152]{1,0:T(8,128)(2,1)} %get-tuple-element.22), channel_id=1, source_target_pairs={{0,4},{4,0},{8,12},{12,8},{1,5},{5,1},{9,13},{13,9},{2,6},{6,2},{1... | collective-permute-start | bytes 442376 | tf_op jit(solution)/shard_map/ppermute | solution.py:522
  12.4 6.9 %collective-permute-start.1 = (bf16[64,1152]{1,0:T(8,128)(2,1)}, bf16[64,1152]{1,0:T(8,128)(2,1)S(1)}, u32[]{:S(2)}, u32[]{:S(2)}) collective-permute-start(bf16[64,1152]{1,0:T(8,128)(2,1)} %get-tuple-element.23), channel_id=1, source_target_pairs={{0,8},{4,12},{8,0},{12,4},{1,9},{5,13},{9,1},{13,5},{2,10},{6,14},... | collective-permute-start | bytes 442376 | tf_op jit(solution)/shard_map/ppermute | solution.py:522
  13.9 7.8 %collective-permute-start.2 = (bf16[64,1152]{1,0:T(8,128)(2,1)}, bf16[64,1152]{1,0:T(8,128)(2,1)S(1)}, u32[]{:S(2)}, u32[]{:S(2)}) collective-permute-start(bf16[64,1152]{1,0:T(8,128)(2,1)} %get-tuple-element.24), channel_id=1, source_target_pairs={{0,12},{4,8},{8,4},{12,0},{1,13},{5,9},{9,5},{13,1},{2,14},{6,10},... | collective-permute-start | bytes 442376 | tf_op jit(solution)/shard_map/ppermute | solution.py:522
  14.3 1.0 %copy-start = (bf16[256,1024]{1,0:T(8,128)(2,1)S(1)}, bf16[256,1024]{1,0:T(8,128)(2,1)}, u32[]{:S(2)}) copy-start(bf16[256,1024]{1,0:T(8,128)(2,1)} %get-tuple-element.20.refs_0_.refs_1_.refs_5_) | copy-start | bytes 1572868
  15.3 6.3 %copy-start.5 = (bf16[8,64,1024]{2,1,0:T(8,128)(2,1)S(1)}, bf16[8,64,1024]{2,1,0:T(8,128)(2,1)}, u32[]{:S(2)}) copy-start(bf16[8,64,1024]{2,1,0:T(8,128)(2,1)} %refs_4_.1) | copy-start | bytes 3145732
  15.3 6.3 %copy-start.6 = (bf16[64,1152]{1,0:T(8,128)(2,1)S(1)}, bf16[64,1152]{1,0:T(8,128)(2,1)}, u32[]{:S(2)}) copy-start(bf16[64,1152]{1,0:T(8,128)(2,1)} %get-tuple-element.21.refs_0_) | copy-start | bytes 442372
  17.4 13.8 %copy-start.1 = (bf16[256,1024]{1,0:T(8,128)(2,1)S(1)}, bf16[256,1024]{1,0:T(8,128)(2,1)}, u32[]{:S(2)}) copy-start(bf16[256,1024]{1,0:T(8,128)(2,1)} %get-tuple-element.20.refs_0_.refs_1_.refs_5_) | copy-start | bytes 1572868
  22.3 8.8 %collective-permute-start.7 = (bf16[128,128]{1,0:T(8,128)(2,1)S(1)}, bf16[128,128]{1,0:T(8,128)(2,1)S(1)}, u32[]{:S(2)}, u32[]{:S(2)}) collective-permute-start(bf16[128,128]{1,0:T(8,128)(2,1)S(1)} %get-tuple-element.25.refs_1_.refs_0_.refs_3_), channel_id=1, source_target_pairs={{0,1},{1,2},{2,3},{3,0},{4,5},{5,6},{6,7},{7,4},{8,9},{9,10},{10,1... | collective-permute-start | bytes 98312 | tf_op jit(solution)/shard_map/ppermute | solution.py:542
  22.4 8.8 %collective-permute-start.8 = (bf16[128,128]{1,0:T(8,128)(2,1)S(1)}, bf16[128,128]{1,0:T(8,128)(2,1)S(1)}, u32[]{:S(2)}, u32[]{:S(2)}) collective-permute-start(bf16[128,128]{1,0:T(8,128)(2,1)S(1)} %get-tuple-element.25.refs_1_.refs_0_.refs_3_), channel_id=1, source_target_pairs={{0,2},{1,3},{2,0},{3,1},{4,6},{5,7},{6,4},{7,5},{8,10},{9,11},{10,... | collective-permute-start | bytes 98312 | tf_op jit(solution)/shard_map/ppermute | solution.py:542
  24.3 6.9 %collective-permute-start.9 = (bf16[128,128]{1,0:T(8,128)(2,1)S(1)}, bf16[128,128]{1,0:T(8,128)(2,1)S(1)}, u32[]{:S(2)}, u32[]{:S(2)}) collective-permute-start(bf16[128,128]{1,0:T(8,128)(2,1)S(1)} %get-tuple-element.25.refs_1_.refs_0_.refs_3_), channel_id=1, source_target_pairs={{0,3},{1,0},{2,1},{3,2},{4,7},{5,4},{6,5},{7,6},{8,11},{9,8},{10,9... | collective-permute-start | bytes 98312 | tf_op jit(solution)/shard_map/ppermute | solution.py:542
  27.8 14.1 %collective-permute-start.4 = (bf16[256,768]{1,0:T(8,128)(2,1)S(1)}, bf16[256,768]{1,0:T(8,128)(2,1)S(1)}, u32[]{:S(2)}, u32[]{:S(2)}) collective-permute-start(bf16[256,768]{1,0:T(8,128)(2,1)S(1)} %hold.1.refs_7_), channel_id=1, source_target_pairs={{0,2},{2,3},{3,1},{1,0},{4,6},{6,7},{7,5},{5,4},{8,10},{10,11},{11... | collective-permute-start | bytes 1179656 | tf_op jit(solution)/shard_map/ppermute | solution.py:528
  33.8 10.1 %copy-start.2 = (bf16[8,64,2048]{2,1,0:T(8,128)(2,1)S(1)}, bf16[8,64,2048]{2,1,0:T(8,128)(2,1)}, u32[]{:S(2)}) copy-start(bf16[8,64,2048]{2,1,0:T(8,128)(2,1)} %refs_5_.1) | copy-start | bytes 6291460
  33.8 33.2 %collective-permute-start.13 = (bf16[256,1280]{1,0:T(8,128)(2,1)S(1)}, bf16[256,1280]{1,0:T(8,128)(2,1)S(1)}, u32[]{:S(2)}, u32[]{:S(2)}) collective-permute-start(bf16[256,1280]{1,0:T(8,128)(2,1)S(1)} %hop.8), channel_id=1, source_target_pairs={{0,2},{2,3},{3,1},{1,0},{4,6},{6,7},{7,5},{5,4},{8,10},{10,11},{11... | collective-permute-start | bytes 1966088 | tf_op jit(solution)/shard_map/ppermute | solution.py:528
  44.7 22.3 %collective-permute-start.10 = (bf16[64,2048]{1,0:T(8,128)(2,1)S(1)}, bf16[64,2048]{1,0:T(8,128)(2,1)S(1)}, u32[]{:S(2)}, u32[]{:S(2)}) collective-permute-start(bf16[64,2048]{1,0:T(8,128)(2,1)S(1)} %get-tuple-element.29), channel_id=1, source_target_pairs={{0,4},{4,0},{8,12},{12,8},{1,5},{5,1},{9,13},{13,9},{2,6},{6,2},{1... | collective-permute-start | bytes 786440 | tf_op jit(solution)/shard_map/ppermute | solution.py:522
  44.8 22.2 %collective-permute-start.11 = (bf16[64,2048]{1,0:T(8,128)(2,1)S(1)}, bf16[64,2048]{1,0:T(8,128)(2,1)S(1)}, u32[]{:S(2)}, u32[]{:S(2)}) collective-permute-start(bf16[64,2048]{1,0:T(8,128)(2,1)S(1)} %get-tuple-element.30), channel_id=1, source_target_pairs={{0,8},{4,12},{8,0},{12,4},{1,9},{5,13},{9,1},{13,5},{2,10},{6,14},... | collective-permute-start | bytes 786440 | tf_op jit(solution)/shard_map/ppermute | solution.py:522
  46.3 20.7 %collective-permute-start.12 = (bf16[64,2048]{1,0:T(8,128)(2,1)S(1)}, bf16[64,2048]{1,0:T(8,128)(2,1)S(1)}, u32[]{:S(2)}, u32[]{:S(2)}) collective-permute-start(bf16[64,2048]{1,0:T(8,128)(2,1)S(1)} %get-tuple-element.31), channel_id=1, source_target_pairs={{0,12},{4,8},{8,4},{12,0},{1,13},{5,9},{9,5},{13,1},{2,14},{6,10},... | collective-permute-start | bytes 786440 | tf_op jit(solution)/shard_map/ppermute | solution.py:522
  46.6 32.2 %collective-permute-start.5 = (bf16[256,768]{1,0:T(8,128)(2,1)S(1)}, bf16[256,768]{1,0:T(8,128)(2,1)S(1)}, u32[]{:S(2)}, u32[]{:S(2)}) collective-permute-start(bf16[256,768]{1,0:T(8,128)(2,1)S(1)} %hop.6.refs_6_), channel_id=1, source_target_pairs={{0,2},{2,3},{3,1},{1,0},{4,6},{6,7},{7,5},{5,4},{8,10},{10,11},{11... | collective-permute-start | bytes 1179656 | tf_op jit(solution)/shard_map/ppermute | solution.py:528
  69.6 15.4 %copy-start.4 = (bf16[256,2048]{1,0:T(8,128)(2,1)S(1)}, bf16[256,2048]{1,0:T(8,128)(2,1)}, u32[]{:S(2)}) copy-start(bf16[256,2048]{1,0:T(8,128)(2,1)} %refs_6_.1) | copy-start | bytes 3145732
  69.6 15.3 %copy-start.7 = (bf16[256,256]{1,0:T(8,128)(2,1)S(1)}, bf16[256,256]{1,0:T(8,128)(2,1)}, u32[]{:S(2)}) copy-start(bf16[256,256]{1,0:T(8,128)(2,1)} %get-tuple-element.32.refs_4_) | copy-start | bytes 393220
  69.6 24.3 %collective-permute-start.14 = (bf16[256,1280]{1,0:T(8,128)(2,1)S(1)}, bf16[256,1280]{1,0:T(8,128)(2,1)S(1)}, u32[]{:S(2)}, u32[]{:S(2)}) collective-permute-start(bf16[256,1280]{1,0:T(8,128)(2,1)S(1)} %hop.9), channel_id=1, source_target_pairs={{0,2},{2,3},{3,1},{1,0},{4,6},{6,7},{7,5},{5,4},{8,10},{10,11},{11... | collective-permute-start | bytes 1966088 | tf_op jit(solution)/shard_map/ppermute | solution.py:528
  80.8 20.9 %collective-permute-start.6 = (bf16[256,768]{1,0:T(8,128)(2,1)S(1)}, bf16[256,768]{1,0:T(8,128)(2,1)S(1)}, u32[]{:S(2)}, u32[]{:S(2)}) collective-permute-start(bf16[256,768]{1,0:T(8,128)(2,1)S(1)} %hop.7.refs_8_), channel_id=1, source_target_pairs={{0,2},{2,3},{3,1},{1,0},{4,6},{6,7},{7,5},{5,4},{8,10},{10,11},{11... | collective-permute-start | bytes 1179656 | tf_op jit(solution)/shard_map/ppermute | solution.py:528
  93.9 1.3 %copy-start.3 = (f32[256,1280]{1,0:T(8,128)S(1)}, f32[256,1280]{1,0:T(8,128)}, u32[]{:S(2)}) copy-start(f32[256,1280]{1,0:T(8,128)} %get-tuple-element.34.settled_ref) | copy-start | bytes 3932164

commit v9 on v8

--- a/solution.py
+++ b/solution.py
@@ -109,8 +109,9 @@
     len_hbm, adapter_hbm, placement_hbm, q_hbm, k_hbm, v_hbm, nk_hbm, nv_hbm, w_hbm,
     *refs,
 ):
-    a_ref, out_ref, chosen_ref, *sent_refs = refs[: 3 + replicas]
+    a_hbm, out_hbm, chosen_hbm, *sent_hbm = refs[: 3 + replicas]
     (
+        a_ref, out_ref, chosen_ref, sent_ref, out_sems,
         len_ref, adapter_ref, placement_ref, q_ref, k_ref, v_ref, nk_ref, nv_ref,
         scores_ref, mixed_ref, sems, small_sems, w_held, w_sems,
     ) = refs[3 + replicas :]
@@ -144,6 +145,13 @@
             )
         )
     ]
+    leaving = []
+
+    def leave(source, target):
+        copy = pltpu.make_async_copy(source, target, out_sems.at[len(leaving)])
+        copy.start()
+        leaving.append(copy)
+
     chunk = out_ref.shape[1]
     weights = Weights(w_hbm, w_held, w_sems, column_owner(0) * block, chunk)
     part(0, 0).start()
@@ -192,7 +200,8 @@
 
     for copy in small:
         copy.wait()
-    plan_routes(slots, adapter_ref, placement_ref, chosen_ref, sent_refs)
+    plan_routes(slots, adapter_ref, placement_ref, chosen_ref, sent_ref)
+    leave(chosen_ref, chosen_hbm)
     counts = len_ref[...].astype(jnp.float32)
     all_groups = requests // GROUP
     of_group = _iota((all_groups, requests), 1) // GROUP == _iota((all_groups, requests), 0)
@@ -235,17 +244,22 @@
             a_ref[pl.ds(step * per, per), pl.ds(h * width, width)] = mixed_ref[
                 side, pl.ds(h, per, stride=heads), :
             ].astype(jnp.bfloat16)
+        rows = pl.ds(step * per, per)
+        leave(a_ref.at[rows, :], a_hbm.at[rows, :])
 
     weights.wait()
     for columns, product in weights.products(a_ref[...]):
         out_ref[:, columns] = product.astype(jnp.bfloat16)
-    rows = _dot(chosen_ref[...], a_ref[...]).astype(jnp.bfloat16)
-    for r, sent_ref in enumerate(sent_refs):
-        sent_ref[:, pl.ds(0, heads * width)] = rows[r * CAP : (r + 1) * CAP, :]
-
-
-def plan_routes(slots, adapter_ref, placement_ref, chosen_ref, sent_refs):
-    replicas = len(sent_refs)
+        leave(out_ref.at[:, columns], out_hbm.at[:, columns])
+    sent_ref[:, pl.ds(0, heads * width)] = _dot(chosen_ref[...], a_ref[...]).astype(jnp.bfloat16)
+    for r in range(replicas):
+        leave(sent_ref.at[pl.ds(r * CAP, CAP), :], sent_hbm[r])
+    for copy in leaving:
+        copy.wait()
+
+
+def plan_routes(slots, adapter_ref, placement_ref, chosen_ref, sent_ref):
+    replicas = sent_ref.shape[0] // CAP
     requests = adapter_ref.shape[1]
     table = placement_ref.shape[1]
     matches = _iota((table, requests), 0) == adapter_ref[...]
@@ -263,9 +277,7 @@
     chosen_ref[...] = here.astype(jnp.bfloat16)
     inner = jnp.sum(jnp.where(here, inside.astype(jnp.float32), 0.0), axis=1, keepdims=True)
     inner = jnp.broadcast_to(inner, (replicas * CAP, LANES)).astype(jnp.bfloat16)
-    width = sent_refs[0].shape[1] - LANES
-    for r, sent_ref in enumerate(sent_refs):
-        sent_ref[:, pl.ds(width, LANES)] = inner[r * CAP : (r + 1) * CAP, :]
+    sent_ref[:, pl.ds(sent_ref.shape[1] - LANES, LANES)] = inner
 
 
 def attend(
@@ -290,14 +302,21 @@
     return pl.pallas_call(
         functools.partial(attend_kernel, heads, kv, cache, steps, block, replicas, slots),
         in_specs=[ANY] * 9,
-        out_specs=[VMEM] * (3 + replicas),
+        out_specs=[ANY] * (3 + replicas),
         out_shape=[
             jax.ShapeDtypeStruct((requests, features), jnp.bfloat16),
             jax.ShapeDtypeStruct((requests, chunk), jnp.bfloat16),
             jax.ShapeDtypeStruct((replicas * CAP, requests), jnp.bfloat16),
         ]
         + [jax.ShapeDtypeStruct((CAP, features + LANES), jnp.bfloat16)] * replicas,
-        scratch_shapes=[pltpu.VMEM(x.shape, x.dtype) for x in small + operands]
+        scratch_shapes=[
+            pltpu.VMEM((requests, features), jnp.bfloat16),
+            pltpu.VMEM((requests, chunk), jnp.bfloat16),
+            pltpu.VMEM((replicas * CAP, requests), jnp.bfloat16),
+            pltpu.VMEM((replicas * CAP, features + LANES), jnp.bfloat16),
+            pltpu.SemaphoreType.DMA((1 + steps + pl.cdiv(chunk, PIECE) + replicas,)),
+        ]
+        + [pltpu.VMEM(x.shape, x.dtype) for x in small + operands]
         + [
             pltpu.VMEM((2, per * heads, columns), jnp.float32),
             pltpu.VMEM((2, per * heads, width), jnp.float32),
@@ -481,22 +500,6 @@
     )(*operands)
 
 
-def hold_kernel(*refs):
-    pass
-
-
-def hold(x, after):
-    return pl.pallas_call(
-        hold_kernel,
-        in_specs=[ANY] * (1 + len(after)),
-        out_specs=ANY,
-        out_shape=jax.ShapeDtypeStruct(x.shape, x.dtype),
-        input_output_aliases={0: 0},
-        compiler_params=PARAMS,
-        name="hold",
-    )(x, *after)
-
-
 def per_device(
     residual,
     query,
@@ -535,16 +538,15 @@
         query, cached_key_rows, cached_value_rows, new_token_key, new_token_value, lengths,
         output_weight, request_adapter, placement, block, replicas, slot_down_weight.shape[0],
     )
-    second = hop(0, 1, None, attended, output_weight, block)
     rows_here = exchange(leaving)
-    mid, inside = down(rows_here, slot_down_weight, after=[second])
+    mid, inside = down(rows_here, slot_down_weight)
     rank_sums = [mid] + [
         lax.ppermute(mid, "tensor", [(i, (i + k) % count) for i in range(count)])
         for k in range(1, count)
     ]
 
     arrived = forward(first)
-    second = hold(second, after=[mid, arrived])
+    second = hop(0, 1, None, attended, output_weight, block, after=[mid])
     travelling = [
         hop(1, 0, arrived, attended, output_weight, block, after=rank_sums + [second]),
         second,

time: 103 us -> 87.6 us (0.85)
  starting transfers between devices: 54.7 us -> 20.2 us
  waiting for transfers between devices: 18.1 us -> 36.5 us
    ppermute x6, starting transfers between devices: 46.4 us -> 11.6 us  [forward(): return lax.ppermute(x, 'tensor', ring)]
    ppermute x6, waiting for transfers between devices: 4.26 us -> 14 us  [exchange(): lax.ppermute(blocks[r], 'dp', [(i, i ^ r) for i in range(replicas)])]
    ppermute x6, waiting for transfers between devices: 13.8 us -> 22.6 us  [forward(): return lax.ppermute(x, 'tensor', ring)]
  transfers between devices with their start and end apart: 15 -> 15, of which waited for: 6 -> 9; matrix products, arithmetic and copies ran while one was open for 0% -> 0% of each run, Pallas kernels for 18% -> 21%
where the time goes in v9:
time: 87.6 us; the launch traced here: 87.3 us
  waiting for transfers between devices  36.5 us (42%)
  Pallas kernels  27.1 us (31%)
  starting transfers between devices  20.2 us (23%)
  local copies, waits for them, and re-layouts  3.29 us (4%)
    ppermute x6, waiting for transfers between devices, forward(): return lax.ppermute(x, 'tensor', ring)  22.6 us
    ppermute x6, waiting for transfers between devices, exchange(): lax.ppermute(blocks[r], 'dp', [(i, i ^ r) for i in range(replicas)])  14 us
    ppermute x6, starting transfers between devices, forward(): return lax.ppermute(x, 'tensor', ring)  11.6 us
    pallas_call x5, Pallas kernels, hop(): pl.pallas_call(functools.partial(hop_kernel, step, block, start, arriving...  11.1 us
    pallas_call x1, Pallas kernels, attend(): pl.pallas_call(functools.partial(attend_kernel, heads, kv, cache, steps,...  8.32 us
    ppermute x3, starting transfers between devices, per_device(): lax.ppermute(mid, 'tensor', [(i, (i + k) % count) for i in range(count)])  4.54 us
    pallas_call x1, Pallas kernels, settle(): pl.pallas_call(functools.partial(settle_kernel, step, replicas, len(after...  4.51 us
    ppermute x6, starting transfers between devices, exchange(): lax.ppermute(blocks[r], 'dp', [(i, i ^ r) for i in range(replicas)])  4.07 us
  transfers between devices with their start and end apart: 15, of which 9 were waited for; matrix products, arithmetic and copies ran while one was open for 0% of the time, Pallas kernels for 21%

profile of v9, /device:TPU:0, one launch (start us, length us, event | category | flops | bytes accessed | tf_op | source)
XLA Modules:
  0.0 87.3 jit_solution(17795841629579253318)
XLA Ops:
  0.0 8.3 %attend.1 = (bf16[256,1024]{1,0:T(8,128)(2,1)}, bf16[256,1280]{1,0:T(8,128)(2,1)}, bf16[256,256]{1,0:T(8,128)(2,1)}, bf16[64,1152]{1,0:T(8,128)(2,1)}, bf16[64,1...) custom-call(s32[1,256]{1,0:T(1,128)} %bitcast.13, s32[1,256]{1,0:T(1,128)} %bitcast.14, ...), custom_call_target="tpu_custom_call" | custom-call | tf_op jit(solution)/shard_map/attend/pallas_call | solution.py:302
  8.3 4.1 %collective-permute-start.12 = (bf16[256,1280]{1,0:T(8,128)(2,1)}, bf16[256,1280]{1,0:T(8,128)(2,1)S(1)}, u32[]{:S(2)}, u32[]{:S(2)}) collective-permute-start(bf16[256,1280]{1,0:T(8,128)(2,1)} %get-tuple-element.33), channel_id=1, source_target_pairs={{0,2},{2,3},{3,1},{1,0},{4,6},{6,7},{7,5},{5,4},{8,10},{10,11},{11... | collective-permute-start | bytes 1966088 | tf_op jit(solution)/shard_map/ppermute | solution.py:531
  12.4 1.5 %collective-permute-start.1 = (bf16[64,1152]{1,0:T(8,128)(2,1)}, bf16[64,1152]{1,0:T(8,128)(2,1)S(1)}, u32[]{:S(2)}, u32[]{:S(2)}) collective-permute-start(bf16[64,1152]{1,0:T(8,128)(2,1)} %get-tuple-element.23), channel_id=1, source_target_pairs={{0,8},{4,12},{8,0},{12,4},{1,9},{5,13},{9,1},{13,5},{2,10},{6,14},... | collective-permute-start | bytes 442376 | tf_op jit(solution)/shard_map/ppermute | solution.py:525
  14.3 5.0 %collective-permute-done.1.refs_2_ = bf16[64,1152]{1,0:T(8,128)(2,1)S(1)} collective-permute-done((bf16[64,1152]{1,0:T(8,128)(2,1)}, bf16[64,1152]{1,0:T(8,128)(2,1)S(1)}, u32[]{:S(2)}, u32[]{:S(2)}) %collective-permute-start.1) | collective-permute-done | bytes 147488 | tf_op jit(solution)/shard_map/ppermute | solution.py:525
  19.3 2.4 %collective-permute-done.2.refs_3_ = bf16[64,1152]{1,0:T(8,128)(2,1)S(1)} collective-permute-done((bf16[64,1152]{1,0:T(8,128)(2,1)}, bf16[64,1152]{1,0:T(8,128)(2,1)S(1)}, u32[]{:S(2)}, u32[]{:S(2)}) %collective-permute-start.2) | collective-permute-done | bytes 147488 | tf_op jit(solution)/shard_map/ppermute | solution.py:525
  21.7 0.9 %copy-done.6 = bf16[64,1152]{1,0:T(8,128)(2,1)S(1)} copy-done((bf16[64,1152]{1,0:T(8,128)(2,1)S(1)}, bf16[64,1152]{1,0:T(8,128)(2,1)}, u32[]{:S(2)}) %copy-start.6) | copy-done | bytes 147480
  22.6 0.6 down.1
  23.3 1.9 %collective-permute-start.7 = (bf16[128,128]{1,0:T(8,128)(2,1)S(1)}, bf16[128,128]{1,0:T(8,128)(2,1)S(1)}, u32[]{:S(2)}, u32[]{:S(2)}) collective-permute-start(bf16[128,128]{1,0:T(8,128)(2,1)S(1)} %get-tuple-element.25.refs_2_.refs_0_.refs_3_), channel_id=1, source_target_pairs={{0,2},{1,3},{2,0},{3,1},{4,6},{5,7},{6,4},{7,5},{8,10},{9,11},{10,... | collective-permute-start | bytes 98312 | tf_op jit(solution)/shard_map/ppermute | solution.py:544
  25.2 2.6 %collective-permute-start.8 = (bf16[128,128]{1,0:T(8,128)(2,1)S(1)}, bf16[128,128]{1,0:T(8,128)(2,1)S(1)}, u32[]{:S(2)}, u32[]{:S(2)}) collective-permute-start(bf16[128,128]{1,0:T(8,128)(2,1)S(1)} %get-tuple-element.25.refs_2_.refs_0_.refs_3_), channel_id=1, source_target_pairs={{0,3},{1,0},{2,1},{3,2},{4,7},{5,4},{6,5},{7,6},{8,11},{9,8},{10,9... | collective-permute-start | bytes 98312 | tf_op jit(solution)/shard_map/ppermute | solution.py:544
  27.8 1.0 %copy-done = bf16[256,1024]{1,0:T(8,128)(2,1)S(1)} copy-done((bf16[256,1024]{1,0:T(8,128)(2,1)S(1)}, bf16[256,1024]{1,0:T(8,128)(2,1)}, u32[]{:S(2)}) %copy-start) | copy-done | bytes 524312
  28.8 2.0 %hop.5.refs_7_ = bf16[256,768]{1,0:T(8,128)(2,1)S(1)} custom-call(bf16[256,1024]{1,0:T(8,128)(2,1)S(1)} %copy-done, bf16[1024,8192]{1,0:T(8,128)(2,1)} %refs_2_.7, bf16[128,128]{1,0:T(8,128)(2,1)S(1)} %get-tuple-element.25.refs_2_.refs_0_.refs_3_), custom_call_target="tpu_custom_call" | custom-call | tf_op jit(solution)/shard_map/hop/pallas_call | solution.py:352
  30.8 1.4 %collective-permute-start.3 = (bf16[256,768]{1,0:T(8,128)(2,1)S(1)}, bf16[256,768]{1,0:T(8,128)(2,1)S(1)}, u32[]{:S(2)}, u32[]{:S(2)}) collective-permute-start(bf16[256,768]{1,0:T(8,128)(2,1)S(1)} %hop.5.refs_7_), channel_id=1, source_target_pairs={{0,2},{2,3},{3,1},{1,0},{4,6},{6,7},{7,5},{5,4},{8,10},{10,11},{11... | collective-permute-start | bytes 1179656 | tf_op jit(solution)/shard_map/ppermute | solution.py:531
  32.2 2.6 %hop.8 = bf16[256,1280]{1,0:T(8,128)(2,1)S(1)} custom-call(bf16[256,1280]{1,0:T(8,128)(2,1)S(1)} %collective-permute-done.12.refs_0_, bf16[256,1024]{1,0:T(8,128)(2,1)S(1)} %copy-done, bf16[1024,8192]{1,0:T(8,128)(2,1)} %refs_2_.7, bf16[128,128]{1,0:T(8,128)(2,1)S(1)} %get-tuple-element.25.refs_2_.refs_0_.refs_3_, ...), custom_call_target="tpu_custom_call" | custom-call | tf_op jit(solution)/shard_map/hop/pallas_call | solution.py:352
  34.9 8.0 %collective-permute-done.3.refs_0_ = bf16[256,768]{1,0:T(8,128)(2,1)S(1)} collective-permute-done((bf16[256,768]{1,0:T(8,128)(2,1)S(1)}, bf16[256,768]{1,0:T(8,128)(2,1)S(1)}, u32[]{:S(2)}, u32[]{:S(2)}) %collective-permute-start.3) | collective-permute-done | bytes 393248 | tf_op jit(solution)/shard_map/ppermute | solution.py:531
  42.9 2.0 %hop.6.refs_6_ = bf16[256,768]{1,0:T(8,128)(2,1)S(1)} custom-call(bf16[256,768]{1,0:T(8,128)(2,1)S(1)} %collective-permute-done.3.refs_0_, bf16[256,1024]{1,0:T(8,128)(2,1)S(1)} %copy-done, bf16[1024,8192]{1,0:T(8,128)(2,1)} %refs_2_.7), custom_call_target="tpu_custom_call" | custom-call | tf_op jit(solution)/shard_map/hop/pallas_call | solution.py:352
  44.9 0.8 up.1
  45.7 1.5 %collective-permute-start.10 = (bf16[64,2048]{1,0:T(8,128)(2,1)S(1)}, bf16[64,2048]{1,0:T(8,128)(2,1)S(1)}, u32[]{:S(2)}, u32[]{:S(2)}) collective-permute-start(bf16[64,2048]{1,0:T(8,128)(2,1)S(1)} %get-tuple-element.29), channel_id=1, source_target_pairs={{0,8},{4,12},{8,0},{12,4},{1,9},{5,13},{9,1},{13,5},{2,10},{6,14},... | collective-permute-start | bytes 786440 | tf_op jit(solution)/shard_map/ppermute | solution.py:525
  47.3 0.7 collective-permute-start.9
  47.9 2.2 %collective-permute-start.4 = (bf16[256,768]{1,0:T(8,128)(2,1)S(1)}, bf16[256,768]{1,0:T(8,128)(2,1)S(1)}, u32[]{:S(2)}, u32[]{:S(2)}) collective-permute-start(bf16[256,768]{1,0:T(8,128)(2,1)S(1)} %hop.6.refs_6_), channel_id=1, source_target_pairs={{0,2},{2,3},{3,1},{1,0},{4,6},{6,7},{7,5},{5,4},{8,10},{10,11},{11... | collective-permute-start | bytes 1179656 | tf_op jit(solution)/shard_map/ppermute | solution.py:531
  50.2 3.9 %collective-permute-done.10.refs_2_.refs_5_ = bf16[64,2048]{1,0:T(8,128)(2,1)S(1)} collective-permute-done((bf16[64,2048]{1,0:T(8,128)(2,1)S(1)}, bf16[64,2048]{1,0:T(8,128)(2,1)S(1)}, u32[]{:S(2)}, u32[]{:S(2)}) %collective-permute-start.10) | collective-permute-done | bytes 262176 | tf_op jit(solution)/shard_map/ppermute | solution.py:525
  54.1 2.7 %collective-permute-done.11.refs_3_.refs_6_ = bf16[64,2048]{1,0:T(8,128)(2,1)S(1)} collective-permute-done((bf16[64,2048]{1,0:T(8,128)(2,1)S(1)}, bf16[64,2048]{1,0:T(8,128)(2,1)S(1)}, u32[]{:S(2)}, u32[]{:S(2)}) %collective-permute-start.11) | collective-permute-done | bytes 262176 | tf_op jit(solution)/shard_map/ppermute | solution.py:525
  56.9 2.6 %hop.9 = bf16[256,1280]{1,0:T(8,128)(2,1)S(1)} custom-call(bf16[256,1280]{1,0:T(8,128)(2,1)S(1)} %collective-permute-done.13.refs_0_, bf16[256,1024]{1,0:T(8,128)(2,1)S(1)} %copy-done.1, bf16[1024,8192]{1,0:T(8,128)(2,1)} %refs_2_.7, bf16[64,2048]{1,0:T(8,128)(2,1)S(1)} %get-tuple-element.27.refs_0_.refs_3_, ...), custom_call_target="tpu_custom_call" | custom-call | tf_op jit(solution)/shard_map/hop/pallas_call | solution.py:352
  59.5 2.3 %collective-permute-start.14 = (bf16[256,1280]{1,0:T(8,128)(2,1)S(1)}, bf16[256,1280]{1,0:T(8,128)(2,1)S(1)}, u32[]{:S(2)}, u32[]{:S(2)}) collective-permute-start(bf16[256,1280]{1,0:T(8,128)(2,1)S(1)} %hop.9), channel_id=1, source_target_pairs={{0,2},{2,3},{3,1},{1,0},{4,6},{6,7},{7,5},{5,4},{8,10},{10,11},{11... | collective-permute-start | bytes 1966088 | tf_op jit(solution)/shard_map/ppermute | solution.py:531
  61.8 3.0 %collective-permute-done.4.refs_0_ = bf16[256,768]{1,0:T(8,128)(2,1)S(1)} collective-permute-done((bf16[256,768]{1,0:T(8,128)(2,1)S(1)}, bf16[256,768]{1,0:T(8,128)(2,1)S(1)}, u32[]{:S(2)}, u32[]{:S(2)}) %collective-permute-start.4) | collective-permute-done | bytes 393248 | tf_op jit(solution)/shard_map/ppermute | solution.py:531
  64.8 2.0 %hop.7.refs_8_ = bf16[256,768]{1,0:T(8,128)(2,1)S(1)} custom-call(bf16[256,768]{1,0:T(8,128)(2,1)S(1)} %collective-permute-done.4.refs_0_, bf16[256,1024]{1,0:T(8,128)(2,1)S(1)} %copy-done.1, bf16[1024,8192]{1,0:T(8,128)(2,1)} %refs_2_.7), custom_call_target="tpu_custom_call" | custom-call | tf_op jit(solution)/shard_map/hop/pallas_call | solution.py:352
  66.8 1.5 %collective-permute-start.5 = (bf16[256,768]{1,0:T(8,128)(2,1)S(1)}, bf16[256,768]{1,0:T(8,128)(2,1)S(1)}, u32[]{:S(2)}, u32[]{:S(2)}) collective-permute-start(bf16[256,768]{1,0:T(8,128)(2,1)S(1)} %hop.7.refs_8_), channel_id=1, source_target_pairs={{0,2},{2,3},{3,1},{1,0},{4,6},{6,7},{7,5},{5,4},{8,10},{10,11},{11... | collective-permute-start | bytes 1179656 | tf_op jit(solution)/shard_map/ppermute | solution.py:531
  68.3 4.5 %settle.1 = (f32[256,1280]{1,0:T(8,128)}, f32[256,768]{1,0:T(8,128)S(1)}) custom-call(bf16[64,2048]{1,0:T(8,128)(2,1)S(1)} %get-tuple-element.27.refs_0_.refs_3_, bf16[64,2048]{1,0:T(8,128)(2,1)S(1)} %collective-permute-done.9.refs_1_.refs_4_, bf16[64,2048]{1,0:T(8,128)(2,1)S(1)} %collective-permute-done.10.refs_2_.refs_5_, ...), custom_call_target="tpu_custom_call" | custom-call | tf_op jit(solution)/shard_map/settle/pallas_call | solution.py:457
  72.8 6.0 %collective-permute-done.14.arrived_ref = bf16[256,1280]{1,0:T(8,128)(2,1)S(1)} collective-permute-done((bf16[256,1280]{1,0:T(8,128)(2,1)S(1)}, bf16[256,1280]{1,0:T(8,128)(2,1)S(1)}, u32[]{:S(2)}, u32[]{:S(2)}) %collective-permute-start.14) | collective-permute-done | bytes 655392 | tf_op jit(solution)/shard_map/ppermute | solution.py:531
  78.9 1.3 %copy-done.3 = f32[256,1280]{1,0:T(8,128)S(1)} copy-done((f32[256,1280]{1,0:T(8,128)S(1)}, f32[256,1280]{1,0:T(8,128)}, u32[]{:S(2)}) %copy-start.3) | copy-done | bytes 1310744
  80.2 0.9 %finish.2.refs_0_ = bf16[256,2048]{1,0:T(8,128)(2,1)} custom-call(bf16[256,1280]{1,0:T(8,128)(2,1)S(1)} %collective-permute-done.14.arrived_ref, f32[256,1280]{1,0:T(8,128)S(1)} %copy-done.3), custom_call_target="tpu_custom_call" | custom-call | tf_op jit(solution)/shard_map/finish/pallas_call | solution.py:488
  81.1 5.4 %collective-permute-done.5.arrived_ref = bf16[256,768]{1,0:T(8,128)(2,1)S(1)} collective-permute-done((bf16[256,768]{1,0:T(8,128)(2,1)S(1)}, bf16[256,768]{1,0:T(8,128)(2,1)S(1)}, u32[]{:S(2)}, u32[]{:S(2)}) %collective-permute-start.5) | collective-permute-done | bytes 393248 | tf_op jit(solution)/shard_map/ppermute | solution.py:531
  86.5 0.8 finish.3
  (25 shorter events, 0.8 us)
Async XLA Ops:
  0.0 21.7 %copy-start.5 = (bf16[8,64,1024]{2,1,0:T(8,128)(2,1)S(1)}, bf16[8,64,1024]{2,1,0:T(8,128)(2,1)}, u32[]{:S(2)}) copy-start(bf16[8,64,1024]{2,1,0:T(8,128)(2,1)} %refs_4_.1) | copy-start | bytes 3145732
  8.3 23.9 %collective-permute-start.12 = (bf16[256,1280]{1,0:T(8,128)(2,1)}, bf16[256,1280]{1,0:T(8,128)(2,1)S(1)}, u32[]{:S(2)}, u32[]{:S(2)}) collective-permute-start(bf16[256,1280]{1,0:T(8,128)(2,1)} %get-tuple-element.33), channel_id=1, source_target_pairs={{0,2},{2,3},{3,1},{1,0},{4,6},{6,7},{7,5},{5,4},{8,10},{10,11},{11... | collective-permute-start | bytes 1966088 | tf_op jit(solution)/shard_map/ppermute | solution.py:531
  12.4 1.9 %collective-permute-start = (bf16[64,1152]{1,0:T(8,128)(2,1)}, bf16[64,1152]{1,0:T(8,128)(2,1)S(1)}, u32[]{:S(2)}, u32[]{:S(2)}) collective-permute-start(bf16[64,1152]{1,0:T(8,128)(2,1)} %get-tuple-element.22), channel_id=1, source_target_pairs={{0,4},{4,0},{8,12},{12,8},{1,5},{5,1},{9,13},{13,9},{2,6},{6,2},{1... | collective-permute-start | bytes 442376 | tf_op jit(solution)/shard_map/ppermute | solution.py:525
  12.4 6.9 %collective-permute-start.1 = (bf16[64,1152]{1,0:T(8,128)(2,1)}, bf16[64,1152]{1,0:T(8,128)(2,1)S(1)}, u32[]{:S(2)}, u32[]{:S(2)}) collective-permute-start(bf16[64,1152]{1,0:T(8,128)(2,1)} %get-tuple-element.23), channel_id=1, source_target_pairs={{0,8},{4,12},{8,0},{12,4},{1,9},{5,13},{9,1},{13,5},{2,10},{6,14},... | collective-permute-start | bytes 442376 | tf_op jit(solution)/shard_map/ppermute | solution.py:525
  13.9 7.8 %collective-permute-start.2 = (bf16[64,1152]{1,0:T(8,128)(2,1)}, bf16[64,1152]{1,0:T(8,128)(2,1)S(1)}, u32[]{:S(2)}, u32[]{:S(2)}) collective-permute-start(bf16[64,1152]{1,0:T(8,128)(2,1)} %get-tuple-element.24), channel_id=1, source_target_pairs={{0,12},{4,8},{8,4},{12,0},{1,13},{5,9},{9,5},{13,1},{2,14},{6,10},... | collective-permute-start | bytes 442376 | tf_op jit(solution)/shard_map/ppermute | solution.py:525
  21.7 0.9 %copy-start.6 = (bf16[64,1152]{1,0:T(8,128)(2,1)S(1)}, bf16[64,1152]{1,0:T(8,128)(2,1)}, u32[]{:S(2)}) copy-start(bf16[64,1152]{1,0:T(8,128)(2,1)} %get-tuple-element.21.refs_0_) | copy-start | bytes 442372
  23.2 9.0 %collective-permute-start.6 = (bf16[128,128]{1,0:T(8,128)(2,1)S(1)}, bf16[128,128]{1,0:T(8,128)(2,1)S(1)}, u32[]{:S(2)}, u32[]{:S(2)}) collective-permute-start(bf16[128,128]{1,0:T(8,128)(2,1)S(1)} %get-tuple-element.25.refs_2_.refs_0_.refs_3_), channel_id=1, source_target_pairs={{0,1},{1,2},{2,3},{3,0},{4,5},{5,6},{6,7},{7,4},{8,9},{9,10},{10,1... | collective-permute-start | bytes 98312 | tf_op jit(solution)/shard_map/ppermute | solution.py:544
  23.3 8.9 %collective-permute-start.7 = (bf16[128,128]{1,0:T(8,128)(2,1)S(1)}, bf16[128,128]{1,0:T(8,128)(2,1)S(1)}, u32[]{:S(2)}, u32[]{:S(2)}) collective-permute-start(bf16[128,128]{1,0:T(8,128)(2,1)S(1)} %get-tuple-element.25.refs_2_.refs_0_.refs_3_), channel_id=1, source_target_pairs={{0,2},{1,3},{2,0},{3,1},{4,6},{5,7},{6,4},{7,5},{8,10},{9,11},{10,... | collective-permute-start | bytes 98312 | tf_op jit(solution)/shard_map/ppermute | solution.py:544
  25.2 7.0 %collective-permute-start.8 = (bf16[128,128]{1,0:T(8,128)(2,1)S(1)}, bf16[128,128]{1,0:T(8,128)(2,1)S(1)}, u32[]{:S(2)}, u32[]{:S(2)}) collective-permute-start(bf16[128,128]{1,0:T(8,128)(2,1)S(1)} %get-tuple-element.25.refs_2_.refs_0_.refs_3_), channel_id=1, source_target_pairs={{0,3},{1,0},{2,1},{3,2},{4,7},{5,4},{6,5},{7,6},{8,11},{9,8},{10,9... | collective-permute-start | bytes 98312 | tf_op jit(solution)/shard_map/ppermute | solution.py:544
  27.8 1.0 %copy-start = (bf16[256,1024]{1,0:T(8,128)(2,1)S(1)}, bf16[256,1024]{1,0:T(8,128)(2,1)}, u32[]{:S(2)}) copy-start(bf16[256,1024]{1,0:T(8,128)(2,1)} %get-tuple-element.20.refs_0_.refs_1_.refs_5_) | copy-start | bytes 1572868
  30.8 12.1 %collective-permute-start.3 = (bf16[256,768]{1,0:T(8,128)(2,1)S(1)}, bf16[256,768]{1,0:T(8,128)(2,1)S(1)}, u32[]{:S(2)}, u32[]{:S(2)}) collective-permute-start(bf16[256,768]{1,0:T(8,128)(2,1)S(1)} %hop.5.refs_7_), channel_id=1, source_target_pairs={{0,2},{2,3},{3,1},{1,0},{4,6},{6,7},{7,5},{5,4},{8,10},{10,11},{11... | collective-permute-start | bytes 1179656 | tf_op jit(solution)/shard_map/ppermute | solution.py:531
  34.8 10.0 %copy-start.2 = (bf16[8,64,2048]{2,1,0:T(8,128)(2,1)S(1)}, bf16[8,64,2048]{2,1,0:T(8,128)(2,1)}, u32[]{:S(2)}) copy-start(bf16[8,64,2048]{2,1,0:T(8,128)(2,1)} %refs_5_.1) | copy-start | bytes 6291460
  34.8 22.1 %collective-permute-start.13 = (bf16[256,1280]{1,0:T(8,128)(2,1)S(1)}, bf16[256,1280]{1,0:T(8,128)(2,1)S(1)}, u32[]{:S(2)}, u32[]{:S(2)}) collective-permute-start(bf16[256,1280]{1,0:T(8,128)(2,1)S(1)} %hop.8), channel_id=1, source_target_pairs={{0,2},{2,3},{3,1},{1,0},{4,6},{6,7},{7,5},{5,4},{8,10},{10,11},{11... | collective-permute-start | bytes 1966088 | tf_op jit(solution)/shard_map/ppermute | solution.py:531
  44.9 12.1 %copy-start.1 = (bf16[256,1024]{1,0:T(8,128)(2,1)S(1)}, bf16[256,1024]{1,0:T(8,128)(2,1)}, u32[]{:S(2)}) copy-start(bf16[256,1024]{1,0:T(8,128)(2,1)} %get-tuple-element.20.refs_0_.refs_1_.refs_5_) | copy-start | bytes 1572868
  45.7 8.4 %collective-permute-start.10 = (bf16[64,2048]{1,0:T(8,128)(2,1)S(1)}, bf16[64,2048]{1,0:T(8,128)(2,1)S(1)}, u32[]{:S(2)}, u32[]{:S(2)}) collective-permute-start(bf16[64,2048]{1,0:T(8,128)(2,1)S(1)} %get-tuple-element.29), channel_id=1, source_target_pairs={{0,8},{4,12},{8,0},{12,4},{1,9},{5,13},{9,1},{13,5},{2,10},{6,14},... | collective-permute-start | bytes 786440 | tf_op jit(solution)/shard_map/ppermute | solution.py:525
  47.3 9.5 %collective-permute-start.11 = (bf16[64,2048]{1,0:T(8,128)(2,1)S(1)}, bf16[64,2048]{1,0:T(8,128)(2,1)S(1)}, u32[]{:S(2)}, u32[]{:S(2)}) collective-permute-start(bf16[64,2048]{1,0:T(8,128)(2,1)S(1)} %get-tuple-element.30), channel_id=1, source_target_pairs={{0,12},{4,8},{8,4},{12,0},{1,13},{5,9},{9,5},{13,1},{2,14},{6,10},... | collective-permute-start | bytes 786440 | tf_op jit(solution)/shard_map/ppermute | solution.py:525
  47.3 9.5 %collective-permute-start.9 = (bf16[64,2048]{1,0:T(8,128)(2,1)S(1)}, bf16[64,2048]{1,0:T(8,128)(2,1)S(1)}, u32[]{:S(2)}, u32[]{:S(2)}) collective-permute-start(bf16[64,2048]{1,0:T(8,128)(2,1)S(1)} %get-tuple-element.28), channel_id=1, source_target_pairs={{0,4},{4,0},{8,12},{12,8},{1,5},{5,1},{9,13},{13,9},{2,6},{6,2},{1... | collective-permute-start | bytes 786440 | tf_op jit(solution)/shard_map/ppermute | solution.py:525
  47.9 16.9 %collective-permute-start.4 = (bf16[256,768]{1,0:T(8,128)(2,1)S(1)}, bf16[256,768]{1,0:T(8,128)(2,1)S(1)}, u32[]{:S(2)}, u32[]{:S(2)}) collective-permute-start(bf16[256,768]{1,0:T(8,128)(2,1)S(1)} %hop.6.refs_6_), channel_id=1, source_target_pairs={{0,2},{2,3},{3,1},{1,0},{4,6},{6,7},{7,5},{5,4},{8,10},{10,11},{11... | collective-permute-start | bytes 1179656 | tf_op jit(solution)/shard_map/ppermute | solution.py:531
  59.5 8.8 %copy-start.4 = (bf16[256,2048]{1,0:T(8,128)(2,1)S(1)}, bf16[256,2048]{1,0:T(8,128)(2,1)}, u32[]{:S(2)}) copy-start(bf16[256,2048]{1,0:T(8,128)(2,1)} %refs_6_.1) | copy-start | bytes 3145732
  59.5 8.8 %copy-start.7 = (bf16[256,256]{1,0:T(8,128)(2,1)S(1)}, bf16[256,256]{1,0:T(8,128)(2,1)}, u32[]{:S(2)}) copy-start(bf16[256,256]{1,0:T(8,128)(2,1)} %get-tuple-element.31.refs_4_) | copy-start | bytes 393220
  59.5 19.3 %collective-permute-start.14 = (bf16[256,1280]{1,0:T(8,128)(2,1)S(1)}, bf16[256,1280]{1,0:T(8,128)(2,1)S(1)}, u32[]{:S(2)}, u32[]{:S(2)}) collective-permute-start(bf16[256,1280]{1,0:T(8,128)(2,1)S(1)} %hop.9), channel_id=1, source_target_pairs={{0,2},{2,3},{3,1},{1,0},{4,6},{6,7},{7,5},{5,4},{8,10},{10,11},{11... | collective-permute-start | bytes 1966088 | tf_op jit(solution)/shard_map/ppermute | solution.py:531
  66.8 19.7 %collective-permute-start.5 = (bf16[256,768]{1,0:T(8,128)(2,1)S(1)}, bf16[256,768]{1,0:T(8,128)(2,1)S(1)}, u32[]{:S(2)}, u32[]{:S(2)}) collective-permute-start(bf16[256,768]{1,0:T(8,128)(2,1)S(1)} %hop.7.refs_8_), channel_id=1, source_target_pairs={{0,2},{2,3},{3,1},{1,0},{4,6},{6,7},{7,5},{5,4},{8,10},{10,11},{11... | collective-permute-start | bytes 1179656 | tf_op jit(solution)/shard_map/ppermute | solution.py:531
  78.8 1.3 %copy-start.3 = (f32[256,1280]{1,0:T(8,128)S(1)}, f32[256,1280]{1,0:T(8,128)}, u32[]{:S(2)}) copy-start(f32[256,1280]{1,0:T(8,128)} %get-tuple-element.34.settled_ref) | copy-start | bytes 3932164

commit v10 on v9

--- a/solution.py
+++ b/solution.py
@@ -14,7 +14,7 @@
 MASKED = -1e30
 VMEM_LIMIT = 50 * 1024 * 1024
 FULL_VMEM = 61 * 1024 * 1024
-SHARES = ((5, 3),)
+SHARES = ((1, 1),)
 PIECE = 512
 SPLIT = 4
 
@@ -500,6 +500,22 @@
     )(*operands)
 
 
+def hold_kernel(*refs):
+    pass
+
+
+def hold(x, after):
+    return pl.pallas_call(
+        hold_kernel,
+        in_specs=[ANY] * (1 + len(after)),
+        out_specs=ANY,
+        out_shape=jax.ShapeDtypeStruct(x.shape, x.dtype),
+        input_output_aliases={0: 0},
+        compiler_params=PARAMS,
+        name="hold",
+    )(x, *after)
+
+
 def per_device(
     residual,
     query,
@@ -538,25 +554,25 @@
         query, cached_key_rows, cached_value_rows, new_token_key, new_token_value, lengths,
         output_weight, request_adapter, placement, block, replicas, slot_down_weight.shape[0],
     )
+    second = hop(0, 1, None, attended, output_weight, block)
     rows_here = exchange(leaving)
-    mid, inside = down(rows_here, slot_down_weight)
+    mid, inside = down(rows_here, slot_down_weight, after=[second])
     rank_sums = [mid] + [
         lax.ppermute(mid, "tensor", [(i, (i + k) % count) for i in range(count)])
         for k in range(1, count)
     ]
 
-    arrived = forward(first)
-    second = hop(0, 1, None, attended, output_weight, block, after=[mid])
-    travelling = [
-        hop(1, 0, arrived, attended, output_weight, block, after=rank_sums + [second]),
-        second,
-    ]
-    next_hop(1, 1, after=())
-    deltas = up(rank_sums, inside, slot_up_weight, after=[travelling[1]])
+    travelling = [first, second]
+    next_hop(1, 0, after=[mid])
+    travelling[0] = hold(travelling[0], after=rank_sums)
+    next_hop(1, 1, after=[travelling[0]])
+    next_hop(2, 0, after=[travelling[1]])
+    deltas = up(rank_sums, inside, slot_up_weight, after=[travelling[0]])
     returned = exchange(deltas)
-    for step in range(2, count - 1):
+    next_hop(2, 1, after=returned)
+    for step in range(3, count - 1):
         for chain in range(2):
-            next_hop(step, chain, after=returned if (step, chain) == (2, 0) else ())
+            next_hop(step, chain, after=())
     settled = settle(
         count - 1, returned, chosen, attended, residual, output_weight, after=[travelling[1]]
     )

time: 87.6 us -> 89.1 us (1.017)
  waiting for transfers between devices: 36.5 us -> 39.5 us
  local copies, waits for them, and re-layouts: 3.29 us -> 1.08 us
  Pallas kernels: 27.1 us -> 28.7 us
    ppermute x3, waiting for transfers between devices: 0.01 us -> 7.81 us  [per_device(): lax.ppermute(mid, 'tensor', [(i, (i + k) % count) for i in range(count)])]
    ppermute x6, waiting for transfers between devices: 22.6 us -> 18.8 us  [forward(): return lax.ppermute(x, 'tensor', ring)]
    unnamed x16 -> x20, local copies, waits for them, and re-layouts: 3.29 us -> 1.08 us
    ppermute x3, starting transfers between devices: 4.54 us -> 2.41 us  [per_device(): lax.ppermute(mid, 'tensor', [(i, (i + k) % count) for i in range(count)])]
    ppermute x6, starting transfers between devices: 11.6 us -> 13.2 us  [forward(): return lax.ppermute(x, 'tensor', ring)]
    pallas_call x1, Pallas kernels: 4.51 us -> 6.01 us  [settle(): pl.pallas_call(functools.partial(settle_kernel, step, replicas, len(after...]
    ppermute x6, waiting for transfers between devices: 14 us -> 12.9 us  [exchange(): lax.ppermute(blocks[r], 'dp', [(i, i ^ r) for i in range(replicas)])]
  transfers between devices with their start and end apart: 15 -> 15, of which waited for: 9 -> 9; matrix products, arithmetic and copies ran while one was open for 0% -> 0% of each run, Pallas kernels for 21% -> 22%
where the time goes in v10:
time: 89.1 us; the launch traced here: 88.8 us
  waiting for transfers between devices  39.5 us (44%)
  Pallas kernels  28.7 us (32%)
  starting transfers between devices  19.4 us (22%)
  local copies, waits for them, and re-layouts  1.08 us (1%)
    ppermute x6, waiting for transfers between devices, forward(): return lax.ppermute(x, 'tensor', ring)  18.8 us
    ppermute x6, starting transfers between devices, forward(): return lax.ppermute(x, 'tensor', ring)  13.2 us
    ppermute x6, waiting for transfers between devices, exchange(): lax.ppermute(blocks[r], 'dp', [(i, i ^ r) for i in range(replicas)])  12.9 us
    pallas_call x5, Pallas kernels, hop(): pl.pallas_call(functools.partial(hop_kernel, step, block, start, arriving...  11.5 us
    pallas_call x1, Pallas kernels, attend(): pl.pallas_call(functools.partial(attend_kernel, heads, kv, cache, steps,...  7.99 us
    ppermute x3, waiting for transfers between devices, per_device(): lax.ppermute(mid, 'tensor', [(i, (i + k) % count) for i in range(count)])  7.81 us
    pallas_call x1, Pallas kernels, settle(): pl.pallas_call(functools.partial(settle_kernel, step, replicas, len(after...  6.01 us
    ppermute x6, starting transfers between devices, exchange(): lax.ppermute(blocks[r], 'dp', [(i, i ^ r) for i in range(replicas)])  3.79 us
  transfers between devices with their start and end apart: 15, of which 9 were waited for; matrix products, arithmetic and copies ran while one was open for 0% of the time, Pallas kernels for 22%

profile of v10, /device:TPU:0, one launch (start us, length us, event | category | flops | bytes accessed | tf_op | source)
XLA Modules:
  0.0 88.8 jit_solution(8743055719777650536)
XLA Ops:
  0.0 8.0 %attend.1 = (bf16[256,1024]{1,0:T(8,128)(2,1)}, bf16[256,1024]{1,0:T(8,128)(2,1)}, bf16[256,256]{1,0:T(8,128)(2,1)}, bf16[64,1152]{1,0:T(8,128)(2,1)}, bf16[64,1...) custom-call(s32[1,256]{1,0:T(1,128)} %bitcast.13, s32[1,256]{1,0:T(1,128)} %bitcast.14, ...), custom_call_target="tpu_custom_call" | custom-call | tf_op jit(solution)/shard_map/attend/pallas_call | solution.py:302
  8.0 4.1 %collective-permute-start.1 = (bf16[256,1024]{1,0:T(8,128)(2,1)}, bf16[256,1024]{1,0:T(8,128)(2,1)S(1)}, u32[]{:S(2)}, u32[]{:S(2)}) collective-permute-start(bf16[256,1024]{1,0:T(8,128)(2,1)} %get-tuple-element.21), channel_id=1, source_target_pairs={{0,2},{2,3},{3,1},{1,0},{4,6},{6,7},{7,5},{5,4},{8,10},{10,11},{11... | collective-permute-start | bytes 1572872 | tf_op jit(solution)/shard_map/ppermute | solution.py:547
  12.1 1.0 %copy-done = bf16[256,1024]{1,0:T(8,128)(2,1)S(1)} copy-done((bf16[256,1024]{1,0:T(8,128)(2,1)S(1)}, bf16[256,1024]{1,0:T(8,128)(2,1)}, u32[]{:S(2)}) %copy-start) | copy-done | bytes 524312
  13.1 2.4 %hop.5.refs_5_ = bf16[256,1024]{1,0:T(8,128)(2,1)S(1)} custom-call(bf16[256,1024]{1,0:T(8,128)(2,1)S(1)} %copy-done, bf16[1024,8192]{1,0:T(8,128)(2,1)} %refs_7_.1), custom_call_target="tpu_custom_call" | custom-call | tf_op jit(solution)/shard_map/hop/pallas_call | solution.py:352
  15.6 1.6 %collective-permute-start = (bf16[256,1024]{1,0:T(8,128)(2,1)S(1)}, bf16[256,1024]{1,0:T(8,128)(2,1)S(1)}, u32[]{:S(2)}, u32[]{:S(2)}) collective-permute-start(bf16[256,1024]{1,0:T(8,128)(2,1)S(1)} %hop.5.refs_5_), channel_id=1, source_target_pairs={{0,2},{2,3},{3,1},{1,0},{4,6},{6,7},{7,5},{5,4},{8,10},{10,11},{11... | collective-permute-start | bytes 1572872 | tf_op jit(solution)/shard_map/ppermute | solution.py:547
  17.2 1.6 %collective-permute-start.3 = (bf16[64,1152]{1,0:T(8,128)(2,1)S(1)}, bf16[64,1152]{1,0:T(8,128)(2,1)S(1)}, u32[]{:S(2)}, u32[]{:S(2)}) collective-permute-start(bf16[64,1152]{1,0:T(8,128)(2,1)S(1)} %copy-done.8), channel_id=1, source_target_pairs={{0,8},{4,12},{8,0},{12,4},{1,9},{5,13},{9,1},{13,5},{2,10},{6,14},... | collective-permute-start | bytes 442376 | tf_op jit(solution)/shard_map/ppermute | solution.py:541
  19.1 4.9 %collective-permute-done.3.refs_2_ = bf16[64,1152]{1,0:T(8,128)(2,1)S(1)} collective-permute-done((bf16[64,1152]{1,0:T(8,128)(2,1)S(1)}, bf16[64,1152]{1,0:T(8,128)(2,1)S(1)}, u32[]{:S(2)}, u32[]{:S(2)}) %collective-permute-start.3) | collective-permute-done | bytes 147488 | tf_op jit(solution)/shard_map/ppermute | solution.py:541
  23.9 2.2 %collective-permute-done.4.refs_3_ = bf16[64,1152]{1,0:T(8,128)(2,1)S(1)} collective-permute-done((bf16[64,1152]{1,0:T(8,128)(2,1)S(1)}, bf16[64,1152]{1,0:T(8,128)(2,1)S(1)}, u32[]{:S(2)}, u32[]{:S(2)}) %collective-permute-start.4) | collective-permute-done | bytes 147488 | tf_op jit(solution)/shard_map/ppermute | solution.py:541
  26.2 0.6 down.1
  27.0 1.8 %collective-permute-start.6 = (bf16[128,128]{1,0:T(8,128)(2,1)S(1)}, bf16[128,128]{1,0:T(8,128)(2,1)S(1)}, u32[]{:S(2)}, u32[]{:S(2)}) collective-permute-start(bf16[128,128]{1,0:T(8,128)(2,1)S(1)} %get-tuple-element.26.refs_3_.refs_1_.refs_0_), channel_id=1, source_target_pairs={{0,2},{1,3},{2,0},{3,1},{4,6},{5,7},{6,4},{7,5},{8,10},{9,11},{10,... | collective-permute-start | bytes 98312 | tf_op jit(solution)/shard_map/ppermute | solution.py:561
  28.8 0.5 collective-permute-start.5
  29.2 2.3 %hop.6.refs_0_ = bf16[256,1024]{1,0:T(8,128)(2,1)S(1)} custom-call(bf16[256,1024]{1,0:T(8,128)(2,1)S(1)} %collective-permute-done.1.refs_0_, bf16[256,1024]{1,0:T(8,128)(2,1)S(1)} %copy-done.1, bf16[1024,8192]{1,0:T(8,128)(2,1)} %refs_7_.1, bf16[128,128]{1,0:T(8,128)(2,1)S(1)} %get-tuple-element.26.refs_3_.refs_1_.refs_0_), custom_call_target="tpu_custom_call" | custom-call | tf_op jit(solution)/shard_map/hop/pallas_call | solution.py:352
  31.5 4.6 %collective-permute-done.7.refs_4_.refs_3_ = bf16[128,128]{1,0:T(8,128)(2,1)S(1)} collective-permute-done((bf16[128,128]{1,0:T(8,128)(2,1)S(1)}, bf16[128,128]{1,0:T(8,128)(2,1)S(1)}, u32[]{:S(2)}, u32[]{:S(2)}) %collective-permute-start.7) | collective-permute-done | bytes 32800 | tf_op jit(solution)/shard_map/ppermute | solution.py:561
  36.2 3.2 %collective-permute-done.6.refs_3_.refs_2_ = bf16[128,128]{1,0:T(8,128)(2,1)S(1)} collective-permute-done((bf16[128,128]{1,0:T(8,128)(2,1)S(1)}, bf16[128,128]{1,0:T(8,128)(2,1)S(1)}, u32[]{:S(2)}, u32[]{:S(2)}) %collective-permute-start.6) | collective-permute-done | bytes 32800 | tf_op jit(solution)/shard_map/ppermute | solution.py:561
  39.3 1.6 %collective-permute-start.9 = (bf16[256,1024]{1,0:T(8,128)(2,1)S(1)}, bf16[256,1024]{1,0:T(8,128)(2,1)S(1)}, u32[]{:S(2)}, u32[]{:S(2)}) collective-permute-start(bf16[256,1024]{1,0:T(8,128)(2,1)S(1)} %hold.1.refs_3_), channel_id=1, source_target_pairs={{0,2},{2,3},{3,1},{1,0},{4,6},{6,7},{7,5},{5,4},{8,10},{10,11},{11... | collective-permute-start | bytes 1572872 | tf_op jit(solution)/shard_map/ppermute | solution.py:547
  40.9 2.3 %hop.7.refs_3_ = bf16[256,1024]{1,0:T(8,128)(2,1)S(1)} custom-call(bf16[256,1024]{1,0:T(8,128)(2,1)S(1)} %collective-permute-done.refs_0_, bf16[256,1024]{1,0:T(8,128)(2,1)S(1)} %copy-done.1, bf16[1024,8192]{1,0:T(8,128)(2,1)} %refs_7_.1, bf16[256,1024]{1,0:T(8,128)(2,1)S(1)} %hold.1.refs_3_), custom_call_target="tpu_custom_call" | custom-call | tf_op jit(solution)/shard_map/hop/pallas_call | solution.py:352
  43.2 0.9 collective-permute-start.8
  44.1 10.0 %collective-permute-done.9.refs_0_ = bf16[256,1024]{1,0:T(8,128)(2,1)S(1)} collective-permute-done((bf16[256,1024]{1,0:T(8,128)(2,1)S(1)}, bf16[256,1024]{1,0:T(8,128)(2,1)S(1)}, u32[]{:S(2)}, u32[]{:S(2)}) %collective-permute-start.9) | collective-permute-done | bytes 524320 | tf_op jit(solution)/shard_map/ppermute | solution.py:547
  54.1 2.3 %hop.8.refs_6_ = bf16[256,1024]{1,0:T(8,128)(2,1)S(1)} custom-call(bf16[256,1024]{1,0:T(8,128)(2,1)S(1)} %collective-permute-done.9.refs_0_, bf16[256,1024]{1,0:T(8,128)(2,1)S(1)} %copy-done.1, bf16[1024,8192]{1,0:T(8,128)(2,1)} %refs_7_.1, bf16[256,1024]{1,0:T(8,128)(2,1)S(1)} %hop.7.refs_3_), custom_call_target="tpu_custom_call" | custom-call | tf_op jit(solution)/shard_map/hop/pallas_call | solution.py:352
  56.4 0.8 up.1
  57.3 1.6 %collective-permute-start.11 = (bf16[64,2048]{1,0:T(8,128)(2,1)S(1)}, bf16[64,2048]{1,0:T(8,128)(2,1)S(1)}, u32[]{:S(2)}, u32[]{:S(2)}) collective-permute-start(bf16[64,2048]{1,0:T(8,128)(2,1)S(1)} %get-tuple-element.30), channel_id=1, source_target_pairs={{0,8},{4,12},{8,0},{12,4},{1,9},{5,13},{9,1},{13,5},{2,10},{6,14},... | collective-permute-start | bytes 786440 | tf_op jit(solution)/shard_map/ppermute | solution.py:541
  58.9 0.3 collective-permute-start.12
  59.2 2.5 %collective-permute-start.14 = (bf16[256,1024]{1,0:T(8,128)(2,1)S(1)}, bf16[256,1024]{1,0:T(8,128)(2,1)S(1)}, u32[]{:S(2)}, u32[]{:S(2)}) collective-permute-start(bf16[256,1024]{1,0:T(8,128)(2,1)S(1)} %hop.8.refs_6_), channel_id=1, source_target_pairs={{0,2},{2,3},{3,1},{1,0},{4,6},{6,7},{7,5},{5,4},{8,10},{10,11},{11... | collective-permute-start | bytes 1572872 | tf_op jit(solution)/shard_map/ppermute | solution.py:547
  61.6 3.7 %collective-permute-done.8.refs_0_ = bf16[256,1024]{1,0:T(8,128)(2,1)S(1)} collective-permute-done((bf16[256,1024]{1,0:T(8,128)(2,1)S(1)}, bf16[256,1024]{1,0:T(8,128)(2,1)S(1)}, u32[]{:S(2)}, u32[]{:S(2)}) %collective-permute-start.8) | collective-permute-done | bytes 524320 | tf_op jit(solution)/shard_map/ppermute | solution.py:547
  65.3 1.1 %collective-permute-done.11.refs_5_.refs_2_ = bf16[64,2048]{1,0:T(8,128)(2,1)S(1)} collective-permute-done((bf16[64,2048]{1,0:T(8,128)(2,1)S(1)}, bf16[64,2048]{1,0:T(8,128)(2,1)S(1)}, u32[]{:S(2)}, u32[]{:S(2)}) %collective-permute-start.11) | collective-permute-done | bytes 262176 | tf_op jit(solution)/shard_map/ppermute | solution.py:541
  66.5 4.7 %collective-permute-done.12.refs_6_.refs_3_ = bf16[64,2048]{1,0:T(8,128)(2,1)S(1)} collective-permute-done((bf16[64,2048]{1,0:T(8,128)(2,1)S(1)}, bf16[64,2048]{1,0:T(8,128)(2,1)S(1)}, u32[]{:S(2)}, u32[]{:S(2)}) %collective-permute-start.12) | collective-permute-done | bytes 262176 | tf_op jit(solution)/shard_map/ppermute | solution.py:541
  71.2 2.3 %hop.9.refs_8_ = bf16[256,1024]{1,0:T(8,128)(2,1)S(1)} custom-call(bf16[256,1024]{1,0:T(8,128)(2,1)S(1)} %collective-permute-done.8.refs_0_, bf16[256,1024]{1,0:T(8,128)(2,1)S(1)} %copy-done.1, bf16[1024,8192]{1,0:T(8,128)(2,1)} %refs_7_.1, bf16[64,2048]{1,0:T(8,128)(2,1)S(1)} %get-tuple-element.28.refs_3_.refs_0_, ...), custom_call_target="tpu_custom_call" | custom-call | tf_op jit(solution)/shard_map/hop/pallas_call | solution.py:352
  73.5 2.5 %collective-permute-start.13 = (bf16[256,1024]{1,0:T(8,128)(2,1)S(1)}, bf16[256,1024]{1,0:T(8,128)(2,1)S(1)}, u32[]{:S(2)}, u32[]{:S(2)}) collective-permute-start(bf16[256,1024]{1,0:T(8,128)(2,1)S(1)} %hop.9.refs_8_), channel_id=1, source_target_pairs={{0,2},{2,3},{3,1},{1,0},{4,6},{6,7},{7,5},{5,4},{8,10},{10,11},{11... | collective-permute-start | bytes 1572872 | tf_op jit(solution)/shard_map/ppermute | solution.py:547
  76.0 6.0 %settle.1 = (f32[256,1024]{1,0:T(8,128)S(1)}, f32[256,1024]{1,0:T(8,128)}) custom-call(bf16[64,2048]{1,0:T(8,128)(2,1)S(1)} %get-tuple-element.28.refs_3_.refs_0_, bf16[64,2048]{1,0:T(8,128)(2,1)S(1)} %collective-permute-done.10.refs_4_.refs_1_, bf16[64,2048]{1,0:T(8,128)(2,1)S(1)} %collective-permute-done.11.refs_5_.refs_2_, ...), custom_call_target="tpu_custom_call" | custom-call | tf_op jit(solution)/shard_map/settle/pallas_call | solution.py:457
  82.1 0.9 finish.2.refs_0_
  82.9 5.0 %collective-permute-done.13.arrived_ref = bf16[256,1024]{1,0:T(8,128)(2,1)S(1)} collective-permute-done((bf16[256,1024]{1,0:T(8,128)(2,1)S(1)}, bf16[256,1024]{1,0:T(8,128)(2,1)S(1)}, u32[]{:S(2)}, u32[]{:S(2)}) %collective-permute-start.13) | collective-permute-done | bytes 524320 | tf_op jit(solution)/shard_map/ppermute | solution.py:547
  88.0 0.9 finish.3
  (30 shorter events, 0.6 us)
Async XLA Ops:
  8.0 21.2 %collective-permute-start.1 = (bf16[256,1024]{1,0:T(8,128)(2,1)}, bf16[256,1024]{1,0:T(8,128)(2,1)S(1)}, u32[]{:S(2)}, u32[]{:S(2)}) collective-permute-start(bf16[256,1024]{1,0:T(8,128)(2,1)} %get-tuple-element.21), channel_id=1, source_target_pairs={{0,2},{2,3},{3,1},{1,0},{4,6},{6,7},{7,5},{5,4},{8,10},{10,11},{11... | collective-permute-start | bytes 1572872 | tf_op jit(solution)/shard_map/ppermute | solution.py:547
  12.1 1.0 %copy-start = (bf16[256,1024]{1,0:T(8,128)(2,1)S(1)}, bf16[256,1024]{1,0:T(8,128)(2,1)}, u32[]{:S(2)}) copy-start(bf16[256,1024]{1,0:T(8,128)(2,1)} %get-tuple-element.20.refs_0_.refs_1_.refs_5_) | copy-start | bytes 1572868
  13.1 4.1 %copy-start.9 = (bf16[64,1152]{1,0:T(8,128)(2,1)S(1)}, bf16[64,1152]{1,0:T(8,128)(2,1)}, u32[]{:S(2)}) copy-start(bf16[64,1152]{1,0:T(8,128)(2,1)} %get-tuple-element.23) | copy-start | bytes 442372
  13.1 4.1 %copy-start.8 = (bf16[64,1152]{1,0:T(8,128)(2,1)S(1)}, bf16[64,1152]{1,0:T(8,128)(2,1)}, u32[]{:S(2)}) copy-start(bf16[64,1152]{1,0:T(8,128)(2,1)} %get-tuple-element.24) | copy-start | bytes 442372
  13.1 5.6 %copy-start.7 = (bf16[64,1152]{1,0:T(8,128)(2,1)S(1)}, bf16[64,1152]{1,0:T(8,128)(2,1)}, u32[]{:S(2)}) copy-start(bf16[64,1152]{1,0:T(8,128)(2,1)} %get-tuple-element.25) | copy-start | bytes 442372
  13.1 13.0 %copy-start.4 = (bf16[8,64,1024]{2,1,0:T(8,128)(2,1)S(1)}, bf16[8,64,1024]{2,1,0:T(8,128)(2,1)}, u32[]{:S(2)}) copy-start(bf16[8,64,1024]{2,1,0:T(8,128)(2,1)} %refs_4_.1) | copy-start | bytes 3145732
  13.1 13.0 %copy-start.5 = (bf16[64,1152]{1,0:T(8,128)(2,1)S(1)}, bf16[64,1152]{1,0:T(8,128)(2,1)}, u32[]{:S(2)}) copy-start(bf16[64,1152]{1,0:T(8,128)(2,1)} %get-tuple-element.22.refs_0_) | copy-start | bytes 442372
  15.6 13.7 %copy-start.1 = (bf16[256,1024]{1,0:T(8,128)(2,1)S(1)}, bf16[256,1024]{1,0:T(8,128)(2,1)}, u32[]{:S(2)}) copy-start(bf16[256,1024]{1,0:T(8,128)(2,1)} %get-tuple-element.20.refs_0_.refs_1_.refs_5_) | copy-start | bytes 1572868
  15.6 25.3 %collective-permute-start = (bf16[256,1024]{1,0:T(8,128)(2,1)S(1)}, bf16[256,1024]{1,0:T(8,128)(2,1)S(1)}, u32[]{:S(2)}, u32[]{:S(2)}) collective-permute-start(bf16[256,1024]{1,0:T(8,128)(2,1)S(1)} %hop.5.refs_5_), channel_id=1, source_target_pairs={{0,2},{2,3},{3,1},{1,0},{4,6},{6,7},{7,5},{5,4},{8,10},{10,11},{11... | collective-permute-start | bytes 1572872 | tf_op jit(solution)/shard_map/ppermute | solution.py:547
  17.2 1.9 %collective-permute-start.2 = (bf16[64,1152]{1,0:T(8,128)(2,1)S(1)}, bf16[64,1152]{1,0:T(8,128)(2,1)S(1)}, u32[]{:S(2)}, u32[]{:S(2)}) collective-permute-start(bf16[64,1152]{1,0:T(8,128)(2,1)S(1)} %copy-done.9), channel_id=1, source_target_pairs={{0,4},{4,0},{8,12},{12,8},{1,5},{5,1},{9,13},{13,9},{2,6},{6,2},{1... | collective-permute-start | bytes 442376 | tf_op jit(solution)/shard_map/ppermute | solution.py:541
  17.2 6.7 %collective-permute-start.3 = (bf16[64,1152]{1,0:T(8,128)(2,1)S(1)}, bf16[64,1152]{1,0:T(8,128)(2,1)S(1)}, u32[]{:S(2)}, u32[]{:S(2)}) collective-permute-start(bf16[64,1152]{1,0:T(8,128)(2,1)S(1)} %copy-done.8), channel_id=1, source_target_pairs={{0,8},{4,12},{8,0},{12,4},{1,9},{5,13},{9,1},{13,5},{2,10},{6,14},... | collective-permute-start | bytes 442376 | tf_op jit(solution)/shard_map/ppermute | solution.py:541
  18.8 7.4 %collective-permute-start.4 = (bf16[64,1152]{1,0:T(8,128)(2,1)S(1)}, bf16[64,1152]{1,0:T(8,128)(2,1)S(1)}, u32[]{:S(2)}, u32[]{:S(2)}) collective-permute-start(bf16[64,1152]{1,0:T(8,128)(2,1)S(1)} %copy-done.7), channel_id=1, source_target_pairs={{0,12},{4,8},{8,4},{12,0},{1,13},{5,9},{9,5},{13,1},{2,14},{6,10},... | collective-permute-start | bytes 442376 | tf_op jit(solution)/shard_map/ppermute | solution.py:541
  26.8 9.3 %collective-permute-start.7 = (bf16[128,128]{1,0:T(8,128)(2,1)S(1)}, bf16[128,128]{1,0:T(8,128)(2,1)S(1)}, u32[]{:S(2)}, u32[]{:S(2)}) collective-permute-start(bf16[128,128]{1,0:T(8,128)(2,1)S(1)} %get-tuple-element.26.refs_3_.refs_1_.refs_0_), channel_id=1, source_target_pairs={{0,3},{1,0},{2,1},{3,2},{4,7},{5,4},{6,5},{7,6},{8,11},{9,8},{10,9... | collective-permute-start | bytes 98312 | tf_op jit(solution)/shard_map/ppermute | solution.py:561
  27.0 12.4 %collective-permute-start.6 = (bf16[128,128]{1,0:T(8,128)(2,1)S(1)}, bf16[128,128]{1,0:T(8,128)(2,1)S(1)}, u32[]{:S(2)}, u32[]{:S(2)}) collective-permute-start(bf16[128,128]{1,0:T(8,128)(2,1)S(1)} %get-tuple-element.26.refs_3_.refs_1_.refs_0_), channel_id=1, source_target_pairs={{0,2},{1,3},{2,0},{3,1},{4,6},{5,7},{6,4},{7,5},{8,10},{9,11},{10,... | collective-permute-start | bytes 98312 | tf_op jit(solution)/shard_map/ppermute | solution.py:561
  28.8 10.5 %collective-permute-start.5 = (bf16[128,128]{1,0:T(8,128)(2,1)S(1)}, bf16[128,128]{1,0:T(8,128)(2,1)S(1)}, u32[]{:S(2)}, u32[]{:S(2)}) collective-permute-start(bf16[128,128]{1,0:T(8,128)(2,1)S(1)} %get-tuple-element.26.refs_3_.refs_1_.refs_0_), channel_id=1, source_target_pairs={{0,1},{1,2},{2,3},{3,0},{4,5},{5,6},{6,7},{7,4},{8,9},{9,10},{10,1... | collective-permute-start | bytes 98312 | tf_op jit(solution)/shard_map/ppermute | solution.py:561
  39.3 14.8 %collective-permute-start.9 = (bf16[256,1024]{1,0:T(8,128)(2,1)S(1)}, bf16[256,1024]{1,0:T(8,128)(2,1)S(1)}, u32[]{:S(2)}, u32[]{:S(2)}) collective-permute-start(bf16[256,1024]{1,0:T(8,128)(2,1)S(1)} %hold.1.refs_3_), channel_id=1, source_target_pairs={{0,2},{2,3},{3,1},{1,0},{4,6},{6,7},{7,5},{5,4},{8,10},{10,11},{11... | collective-permute-start | bytes 1572872 | tf_op jit(solution)/shard_map/ppermute | solution.py:547
  43.2 13.2 %copy-start.2 = (bf16[8,64,2048]{2,1,0:T(8,128)(2,1)S(1)}, bf16[8,64,2048]{2,1,0:T(8,128)(2,1)}, u32[]{:S(2)}) copy-start(bf16[8,64,2048]{2,1,0:T(8,128)(2,1)} %refs_5_.1) | copy-start | bytes 6291460
  43.2 22.1 %collective-permute-start.8 = (bf16[256,1024]{1,0:T(8,128)(2,1)S(1)}, bf16[256,1024]{1,0:T(8,128)(2,1)S(1)}, u32[]{:S(2)}, u32[]{:S(2)}) collective-permute-start(bf16[256,1024]{1,0:T(8,128)(2,1)S(1)} %hop.7.refs_3_), channel_id=1, source_target_pairs={{0,2},{2,3},{3,1},{1,0},{4,6},{6,7},{7,5},{5,4},{8,10},{10,11},{11... | collective-permute-start | bytes 1572872 | tf_op jit(solution)/shard_map/ppermute | solution.py:547
  57.2 8.1 %collective-permute-start.10 = (bf16[64,2048]{1,0:T(8,128)(2,1)S(1)}, bf16[64,2048]{1,0:T(8,128)(2,1)S(1)}, u32[]{:S(2)}, u32[]{:S(2)}) collective-permute-start(bf16[64,2048]{1,0:T(8,128)(2,1)S(1)} %get-tuple-element.29), channel_id=1, source_target_pairs={{0,4},{4,0},{8,12},{12,8},{1,5},{5,1},{9,13},{13,9},{2,6},{6,2},{1... | collective-permute-start | bytes 786440 | tf_op jit(solution)/shard_map/ppermute | solution.py:541
  57.3 9.2 %collective-permute-start.11 = (bf16[64,2048]{1,0:T(8,128)(2,1)S(1)}, bf16[64,2048]{1,0:T(8,128)(2,1)S(1)}, u32[]{:S(2)}, u32[]{:S(2)}) collective-permute-start(bf16[64,2048]{1,0:T(8,128)(2,1)S(1)} %get-tuple-element.30), channel_id=1, source_target_pairs={{0,8},{4,12},{8,0},{12,4},{1,9},{5,13},{9,1},{13,5},{2,10},{6,14},... | collective-permute-start | bytes 786440 | tf_op jit(solution)/shard_map/ppermute | solution.py:541
  58.9 12.3 %collective-permute-start.12 = (bf16[64,2048]{1,0:T(8,128)(2,1)S(1)}, bf16[64,2048]{1,0:T(8,128)(2,1)S(1)}, u32[]{:S(2)}, u32[]{:S(2)}) collective-permute-start(bf16[64,2048]{1,0:T(8,128)(2,1)S(1)} %get-tuple-element.31), channel_id=1, source_target_pairs={{0,12},{4,8},{8,4},{12,0},{1,13},{5,9},{9,5},{13,1},{2,14},{6,10},... | collective-permute-start | bytes 786440 | tf_op jit(solution)/shard_map/ppermute | solution.py:541
  59.2 22.9 %collective-permute-start.14 = (bf16[256,1024]{1,0:T(8,128)(2,1)S(1)}, bf16[256,1024]{1,0:T(8,128)(2,1)S(1)}, u32[]{:S(2)}, u32[]{:S(2)}) collective-permute-start(bf16[256,1024]{1,0:T(8,128)(2,1)S(1)} %hop.8.refs_6_), channel_id=1, source_target_pairs={{0,2},{2,3},{3,1},{1,0},{4,6},{6,7},{7,5},{5,4},{8,10},{10,11},{11... | collective-permute-start | bytes 1572872 | tf_op jit(solution)/shard_map/ppermute | solution.py:547
  71.2 4.8 %copy-start.6 = (bf16[256,256]{1,0:T(8,128)(2,1)S(1)}, bf16[256,256]{1,0:T(8,128)(2,1)}, u32[]{:S(2)}) copy-start(bf16[256,256]{1,0:T(8,128)(2,1)} %get-tuple-element.32.refs_4_) | copy-start | bytes 393220
  73.5 14.5 %collective-permute-start.13 = (bf16[256,1024]{1,0:T(8,128)(2,1)S(1)}, bf16[256,1024]{1,0:T(8,128)(2,1)S(1)}, u32[]{:S(2)}, u32[]{:S(2)}) collective-permute-start(bf16[256,1024]{1,0:T(8,128)(2,1)S(1)} %hop.9.refs_8_), channel_id=1, source_target_pairs={{0,2},{2,3},{3,1},{1,0},{4,6},{6,7},{7,5},{5,4},{8,10},{10,11},{11... | collective-permute-start | bytes 1572872 | tf_op jit(solution)/shard_map/ppermute | solution.py:547
  82.0 5.9 %copy-start.3 = (f32[256,1024]{1,0:T(8,128)S(1)}, f32[256,1024]{1,0:T(8,128)}, u32[]{:S(2)}) copy-start(f32[256,1024]{1,0:T(8,128)} %get-tuple-element.33.settled_ref) | copy-start | bytes 3145732

commit v11 on v9

--- a/solution.py
+++ b/solution.py
@@ -14,7 +14,7 @@
 MASKED = -1e30
 VMEM_LIMIT = 50 * 1024 * 1024
 FULL_VMEM = 61 * 1024 * 1024
-SHARES = ((5, 3),)
+SHARES = ((1, 1),)
 PIECE = 512
 SPLIT = 4
 
@@ -33,17 +33,24 @@
     return lax.broadcasted_iota(jnp.int32, shape, axis)
 
 
-def ring_order(count):
-    return list(range(0, count, 2)) + list(range(1, count, 2))[::-1]
-
-
-def column_owner(step):
+def right_owner(step):
     count = lax.axis_size("tensor")
-    here = lax.axis_index("tensor")
-    half = here // 2
-    spot = jnp.where(here % 2 == 0, half, count - 1 - half)
-    spot = lax.rem(spot - 1 - step + 2 * count, count)
-    return jnp.where(2 * spot < count, 2 * spot, 2 * (count - spot) - 1)
+    return jnp.minimum(lax.axis_index("tensor") + count - step, count - 1)
+
+
+def left_owner(step):
+    count = lax.axis_size("tensor")
+    return jnp.maximum(lax.axis_index("tensor") + step - count, 0)
+
+
+def one_way(step):
+    return 2 * step <= lax.axis_size("tensor")
+
+
+def outward_owner(step):
+    count = lax.axis_size("tensor")
+    rightward = lax.axis_index("tensor") < count // 2
+    return jnp.where(rightward, right_owner(step), left_owner(step))
 
 
 def chain_columns(width):
@@ -109,12 +116,12 @@
     len_hbm, adapter_hbm, placement_hbm, q_hbm, k_hbm, v_hbm, nk_hbm, nv_hbm, w_hbm,
     *refs,
 ):
-    a_hbm, out_hbm, chosen_hbm, *sent_hbm = refs[: 3 + replicas]
+    a_hbm, out_hbm, chosen_hbm, *sent_hbm = refs[:5]
     (
         a_ref, out_ref, chosen_ref, sent_ref, out_sems,
         len_ref, adapter_ref, placement_ref, q_ref, k_ref, v_ref, nk_ref, nv_ref,
         scores_ref, mixed_ref, sems, small_sems, w_held, w_sems,
-    ) = refs[3 + replicas :]
+    ) = refs[5:]
     requests = len_ref.shape[1]
     width = q_hbm.shape[1]
     per = requests // steps
@@ -153,7 +160,7 @@
         leaving.append(copy)
 
     chunk = out_ref.shape[1]
-    weights = Weights(w_hbm, w_held, w_sems, column_owner(0) * block, chunk)
+    weights = Weights(w_hbm, w_held, w_sems, outward_owner(1) * block, chunk)
     part(0, 0).start()
     part(1, 0).start()
     for copy in small[:2]:
@@ -252,8 +259,9 @@
         out_ref[:, columns] = product.astype(jnp.bfloat16)
         leave(out_ref.at[:, columns], out_hbm.at[:, columns])
     sent_ref[:, pl.ds(0, heads * width)] = _dot(chosen_ref[...], a_ref[...]).astype(jnp.bfloat16)
-    for r in range(replicas):
-        leave(sent_ref.at[pl.ds(r * CAP, CAP), :], sent_hbm[r])
+    half = sent_ref.shape[0] // 2
+    for i, target in enumerate(sent_hbm):
+        leave(sent_ref.at[pl.ds(i * half, half), :], target)
     for copy in leaving:
         copy.wait()
 
@@ -302,19 +310,19 @@
     return pl.pallas_call(
         functools.partial(attend_kernel, heads, kv, cache, steps, block, replicas, slots),
         in_specs=[ANY] * 9,
-        out_specs=[ANY] * (3 + replicas),
+        out_specs=[ANY] * 5,
         out_shape=[
             jax.ShapeDtypeStruct((requests, features), jnp.bfloat16),
             jax.ShapeDtypeStruct((requests, chunk), jnp.bfloat16),
             jax.ShapeDtypeStruct((replicas * CAP, requests), jnp.bfloat16),
         ]
-        + [jax.ShapeDtypeStruct((CAP, features + LANES), jnp.bfloat16)] * replicas,
+        + [jax.ShapeDtypeStruct((replicas // 2 * CAP, features + LANES), jnp.bfloat16)] * 2,
         scratch_shapes=[
             pltpu.VMEM((requests, features), jnp.bfloat16),
             pltpu.VMEM((requests, chunk), jnp.bfloat16),
             pltpu.VMEM((replicas * CAP, requests), jnp.bfloat16),
             pltpu.VMEM((replicas * CAP, features + LANES), jnp.bfloat16),
-            pltpu.SemaphoreType.DMA((1 + steps + pl.cdiv(chunk, PIECE) + replicas,)),
+            pltpu.SemaphoreType.DMA((3 + steps + pl.cdiv(chunk, PIECE),)),
         ]
         + [pltpu.VMEM(x.shape, x.dtype) for x in small + operands]
         + [
@@ -329,44 +337,47 @@
     )(*small, *operands, weight)
 
 
-def hop_kernel(step, block, start, arriving, after, *refs):
-    if arriving:
-        arrived_ref, *refs = refs
-    a_ref, w_hbm, *refs = refs
-    out_ref, held, sems = refs[after:]
-    chunk = out_ref.shape[1]
-    first = column_owner(step) * block + start
-    weights = Weights(w_hbm, held, sems, first, chunk)
-    weights.start()
-    weights.wait()
-    for columns, product in weights.products(a_ref[...]):
-        if arriving:
-            product = product + arrived_ref[:, columns].astype(jnp.float32)
-        out_ref[:, columns] = product.astype(jnp.bfloat16)
+def hop_kernel(step, block, start, arrivals, after, *refs):
+    arrived = refs[:arrivals]
+    a_ref, w_hbm = refs[arrivals : arrivals + 2]
+    refs = refs[arrivals + 2 + after :]
+    owners = [outward_owner(step)] if one_way(step) else [right_owner(step), left_owner(step)]
+    outs, held, sems = refs[: len(owners)], refs[len(owners) :: 2], refs[len(owners) + 1 :: 2]
+    chunk = outs[0].shape[1]
+    ways = []
+    for owner, buffer, flags in zip(owners, held, sems):
+        ways.append(Weights(w_hbm, buffer, flags, owner * block + start, chunk))
+        ways[-1].start()
+    for i, (weights, out_ref) in enumerate(zip(ways, outs)):
+        weights.wait()
+        for columns, product in weights.products(a_ref[...]):
+            if arrivals:
+                ref = arrived[min(i, arrivals - 1)]
+                product = product + ref[:, columns].astype(jnp.float32)
+            out_ref[:, columns] = product.astype(jnp.bfloat16)
 
 
 def hop(step, chain, arrived, attended, weight, block, after=()):
-    arriving = arrived is not None
     start, chunk = chain_columns(block)[chain]
-    operands = ([arrived] if arriving else []) + [attended, weight, *after]
+    outs = 1 if one_way(step) else 2
     return pl.pallas_call(
-        functools.partial(hop_kernel, step, block, start, arriving, len(after)),
-        in_specs=[VMEM] * (1 + arriving) + [ANY] + [ANY] * len(after),
-        out_specs=VMEM,
-        out_shape=jax.ShapeDtypeStruct((attended.shape[0], chunk), jnp.bfloat16),
-        scratch_shapes=Weights.scratch(weight.shape[0], chunk),
+        functools.partial(hop_kernel, step, block, start, len(arrived), len(after)),
+        in_specs=[VMEM] * (len(arrived) + 1) + [ANY] * (1 + len(after)),
+        out_specs=[VMEM] * outs,
+        out_shape=[jax.ShapeDtypeStruct((attended.shape[0], chunk), jnp.bfloat16)] * outs,
+        scratch_shapes=Weights.scratch(weight.shape[0], chunk) * outs,
         compiler_params=PARAMS,
         name="hop",
-    )(*operands)
-
-
-def down_kernel(replicas, after, *refs):
-    received = refs[:replicas]
-    down_ref = refs[replicas]
-    mid_ref, inside_ref = refs[replicas + 1 + after :]
+    )(*arrived, attended, weight, *after)
+
+
+def down_kernel(places, arrays, after, *refs):
+    down_ref = refs[arrays]
+    mid_ref, inside_ref = refs[arrays + 1 + after :]
     slots, rank, width = down_ref.shape
-    rows = jnp.concatenate([r[:, pl.ds(0, width)] for r in received], axis=0)
-    inside = jnp.concatenate([r[:, pl.ds(width, LANES)] for r in received], axis=0)
+    blocks = [refs[i].at[pl.ds(at, CAP), :] for i, at in places]
+    rows = jnp.concatenate([b[:, pl.ds(0, width)] for b in blocks], axis=0)
+    inside = jnp.concatenate([b[:, pl.ds(width, LANES)] for b in blocks], axis=0)
     inside_ref[...] = inside
     projected = _dot(rows, down_ref[...].reshape(slots * rank, width), 1, 1)
     lane_slot = _iota(projected.shape, 1) // rank
@@ -383,11 +394,11 @@
 
 
 def down(received, slot_down_weight, after=()):
-    replicas = len(received)
-    rows = replicas * CAP
+    arrays, places = received
+    rows = len(places) * CAP
     return pl.pallas_call(
-        functools.partial(down_kernel, replicas, len(after)),
-        in_specs=[VMEM] * (replicas + 1) + [ANY] * len(after),
+        functools.partial(down_kernel, places, len(arrays), len(after)),
+        in_specs=[VMEM] * (len(arrays) + 1) + [ANY] * len(after),
         out_specs=[VMEM, VMEM],
         out_shape=[
             jax.ShapeDtypeStruct((rows * slot_down_weight.shape[1] // LANES, LANES), jnp.bfloat16),
@@ -395,7 +406,7 @@
         ],
         compiler_params=PARAMS,
         name="down",
-    )(*received, slot_down_weight, *after)
+    )(*arrays, slot_down_weight, *after)
 
 
 def up_kernel(parts, after, *refs):
@@ -416,32 +427,31 @@
     mine = _iota(wide.shape, 1) // rank == inside_ref[:, 0:1].astype(jnp.int32)
     wide = jnp.where(mine, wide, 0.0).astype(jnp.bfloat16)
     delta = _dot(wide, up_ref[...].reshape(slots * rank, width)).astype(jnp.bfloat16)
-    for r, out_ref in enumerate(out_refs):
-        out_ref[...] = delta[r * CAP : (r + 1) * CAP, :]
+    half = delta.shape[0] // 2
+    for i, out_ref in enumerate(out_refs):
+        out_ref[...] = delta[i * half : (i + 1) * half, :]
 
 
 def up(mids, inside, slot_up_weight, after=()):
     rows = inside.shape[0]
-    replicas = rows // CAP
     width = slot_up_weight.shape[2]
     return pl.pallas_call(
         functools.partial(up_kernel, len(mids), len(after)),
         in_specs=[VMEM] * (len(mids) + 2) + [ANY] * len(after),
-        out_specs=[VMEM] * replicas,
-        out_shape=[jax.ShapeDtypeStruct((CAP, width), jnp.bfloat16)] * replicas,
+        out_specs=[VMEM] * 2,
+        out_shape=[jax.ShapeDtypeStruct((rows // 2, width), jnp.bfloat16)] * 2,
         compiler_params=PARAMS,
         name="up",
     )(*mids, inside, slot_up_weight, *after)
 
 
-def settle_kernel(step, replicas, after, *refs):
-    returned = refs[:replicas]
-    chosen_ref, a_ref, residual_ref, w_hbm = refs[replicas : replicas + 4]
-    *out_refs, held, sems = refs[replicas + 4 + after :]
+def settle_kernel(places, arrays, after, *refs):
+    chosen_ref, a_ref, residual_ref, w_hbm = refs[arrays : arrays + 4]
+    *out_refs, held, sems = refs[arrays + 4 + after :]
     width = residual_ref.shape[1]
-    weights = Weights(w_hbm, held, sems, column_owner(step) * width, width)
+    weights = Weights(w_hbm, held, sems, lax.axis_index("tensor") * width, width)
     weights.start()
-    rows = jnp.concatenate([r[...] for r in returned], axis=0)
+    rows = jnp.concatenate([refs[i][pl.ds(at, CAP), :] for i, at in places], axis=0)
     delta = _dot(chosen_ref[...], rows, 0, 0)
     total = residual_ref[...].astype(jnp.float32) + delta
     weights.wait()
@@ -450,29 +460,30 @@
         out_ref[...] = total[:, start : start + chunk]
 
 
-def settle(step, returned, chosen, attended, residual, weight, after=()):
-    replicas = len(returned)
+def settle(returned, chosen, attended, residual, weight, after=()):
+    arrays, places = returned
     rows, width = residual.shape
     chains = chain_columns(width)
     return pl.pallas_call(
-        functools.partial(settle_kernel, step, replicas, len(after)),
-        in_specs=[VMEM] * (replicas + 3) + [ANY] * (1 + len(after)),
+        functools.partial(settle_kernel, places, len(arrays), len(after)),
+        in_specs=[VMEM] * (len(arrays) + 3) + [ANY] * (1 + len(after)),
         out_specs=[VMEM] * len(chains),
         out_shape=[jax.ShapeDtypeStruct((rows, chunk), jnp.float32) for _, chunk in chains],
         scratch_shapes=Weights.scratch(weight.shape[0], width),
         compiler_params=PARAMS,
         name="settle",
-    )(*returned, chosen, attended, residual, weight, *after)
-
-
-def finish_kernel(start, arrived_ref, settled_ref, *refs):
+    )(*arrays, chosen, attended, residual, weight, *after)
+
+
+def finish_kernel(start, right_ref, left_ref, settled_ref, *refs):
     out_hbm, held, sems = refs[-3:]
-    rows, chunk = arrived_ref.shape
+    rows, chunk = right_ref.shape
     half = rows // 2
     copies = []
     for i in range(2):
         part = pl.ds(i * half, half)
-        total = settled_ref[part, :] + arrived_ref[part, :].astype(jnp.float32)
+        total = right_ref[part, :].astype(jnp.float32) + left_ref[part, :].astype(jnp.float32)
+        total = total + settled_ref[part, :]
         held[part, :] = total.astype(jnp.bfloat16)
         target = out_hbm.at[part, pl.ds(start, chunk)]
         copies.append(pltpu.make_async_copy(held.at[part, :], target, sems.at[i]))
@@ -482,15 +493,15 @@
 
 
 def finish(chain, arrived, settled, earlier, width):
-    rows = arrived.shape[0]
+    rows = settled.shape[0]
     start, chunk = chain_columns(width)[chain]
-    operands = [arrived, settled] + ([earlier] if earlier is not None else [])
+    operands = [*arrived, settled] + ([earlier] if earlier is not None else [])
     return pl.pallas_call(
         functools.partial(finish_kernel, start),
-        in_specs=[VMEM, VMEM] + ([ANY] if earlier is not None else []),
+        in_specs=[VMEM] * 3 + ([ANY] if earlier is not None else []),
         out_specs=ANY,
         out_shape=jax.ShapeDtypeStruct((rows, width), jnp.bfloat16),
-        input_output_aliases={2: 0} if earlier is not None else {},
+        input_output_aliases={3: 0} if earlier is not None else {},
         scratch_shapes=[
             pltpu.VMEM((rows, chunk), jnp.bfloat16),
             pltpu.SemaphoreType.DMA((2,)),
@@ -517,52 +528,62 @@
     count = lax.axis_size("tensor")
     replicas = lax.axis_size("dp")
     block = residual.shape[1]
-    order = ring_order(count)
-    ring = [(order[p], order[(p + 1) % count]) for p in range(count)]
-
-    def exchange(blocks):
-        moved = [
-            lax.ppermute(blocks[r], "dp", [(i, i ^ r) for i in range(replicas)])
-            for r in range(1, replicas)
+    def exchange(near, far):
+        arrays = [near, far]
+        places = [(r * 2 // replicas, r % (replicas // 2) * CAP) for r in range(replicas)]
+        reach = replicas // 2
+        while reach:
+            moving = [r for r in range(replicas) if r & reach]
+            if 2 * reach == replicas:
+                moved = far
+            else:
+                moved = jnp.concatenate(
+                    [lax.slice_in_dim(arrays[i], at, at + CAP) for i, at in map(places.__getitem__, moving)]
+                )
+            arrays.append(lax.ppermute(moved, "dp", [(i, i ^ reach) for i in range(replicas)]))
+            for j, r in enumerate(moving):
+                places[r] = (len(arrays) - 1, j * CAP)
+            reach //= 2
+        used = sorted({i for i, _ in places})
+        return [arrays[i] for i in used], [(used.index(i), at) for i, at in places]
+
+    def pass_on(step, sums):
+        rightward = [(i, i + 1) for i in range(step)]
+        leftward = [(i, i - 1) for i in range(count - step, count)]
+        if 2 * step < count - 1:
+            return [lax.ppermute(sums[0], "tensor", rightward + leftward)]
+        return [
+            lax.ppermute(sums[0], "tensor", rightward),
+            lax.ppermute(sums[-1], "tensor", leftward),
         ]
-        return [blocks[0]] + moved
-
-    def forward(x):
-        return lax.ppermute(x, "tensor", ring)
 
     def next_hop(step, chain, after):
-        arrived = forward(travelling[chain])
-        travelling[chain] = hop(step, chain, arrived, attended, output_weight, block, after)
-
-    attended, first, chosen, *leaving = attend(
+        arrived = pass_on(step - 1, sums[chain])
+        sums[chain] = hop(step, chain, arrived, attended, output_weight, block, after)
+
+    attended, first, chosen, near, far = attend(
         query, cached_key_rows, cached_value_rows, new_token_key, new_token_value, lengths,
         output_weight, request_adapter, placement, block, replicas, slot_down_weight.shape[0],
     )
-    rows_here = exchange(leaving)
-    mid, inside = down(rows_here, slot_down_weight)
+    sums = [[first], hop(1, 1, [], attended, output_weight, block)]
+    rows_here = exchange(near, far)
+    next_hop(2, 0, after=[*sums[1], *rows_here[0]])
+    mid, inside = down(rows_here, slot_down_weight, after=sums[0])
     rank_sums = [mid] + [
-        lax.ppermute(mid, "tensor", [(i, (i + k) % count) for i in range(count)])
-        for k in range(1, count)
+        lax.ppermute(mid, "tensor", [(i, i ^ k) for i in range(count)]) for k in range(1, count)
     ]
-
-    arrived = forward(first)
-    second = hop(0, 1, None, attended, output_weight, block, after=[mid])
-    travelling = [
-        hop(1, 0, arrived, attended, output_weight, block, after=rank_sums + [second]),
-        second,
-    ]
-    next_hop(1, 1, after=())
-    deltas = up(rank_sums, inside, slot_up_weight, after=[travelling[1]])
-    returned = exchange(deltas)
-    for step in range(2, count - 1):
+    next_hop(2, 1, after=[rank_sums[0]])
+    deltas = up(rank_sums, inside, slot_up_weight, after=sums[1])
+    returned = exchange(*deltas)
+    next_hop(3, 0, after=[deltas[0]])
+    next_hop(3, 1, after=sums[0])
+    for step in range(4, count):
         for chain in range(2):
-            next_hop(step, chain, after=returned if (step, chain) == (2, 0) else ())
-    settled = settle(
-        count - 1, returned, chosen, attended, residual, output_weight, after=[travelling[1]]
-    )
+            next_hop(step, chain, after=sums[1 - chain])
+    settled = settle(returned, chosen, attended, residual, output_weight, after=sums[1])
     out = None
     for chain in range(2):
-        arrived = forward(travelling[chain])
+        arrived = pass_on(count - 1, sums[chain])
         out = finish(chain, arrived, settled[chain], out, block)
     return out
 

time: 87.6 us -> 91.5 us (1.045)
  starting transfers between devices: 20.2 us -> 37 us
  waiting for transfers between devices: 36.5 us -> 20.1 us
  Pallas kernels: 27.1 us -> 31.1 us
  local copies, waits for them, and re-layouts: 3.29 us -> 2.35 us
    ppermute x15 -> x17, starting transfers between devices: 20.2 us -> 37 us  [the longest x4 19.9 us: pass_on(): lax.ppermute(sums[0], 'tensor', rightward)]
    ppermute x15 -> x17, waiting for transfers between devices: 36.5 us -> 20.1 us  [the longest x2 8.06 us: pass_on(): return [lax.ppermute(sums[0], 'tensor', rightward + leftward)]]
    pallas_call x9, Pallas kernels: 17.9 us -> 22.3 us  [the longest x5 13.9 us: hop(): pl.pallas_call(functools.partial(hop_kernel, step, block, start, len(arri...]
    unnamed x16, local copies, waits for them, and re-layouts: 3.29 us -> 2.29 us
  transfers between devices with their start and end apart: 15 -> 17, of which waited for: 9 -> 5; matrix products, arithmetic and copies ran while one was open for 0% -> 0% of each run, Pallas kernels for 21% -> 24%
where the time goes in v11:
time: 91.5 us; the launch traced here: 91 us
  starting transfers between devices  37 us (40%)
  Pallas kernels  31.1 us (34%)
  waiting for transfers between devices  20.1 us (22%)
  local copies, waits for them, and re-layouts  2.35 us (3%)
    ppermute x4, starting transfers between devices, pass_on(): lax.ppermute(sums[0], 'tensor', rightward)  19.9 us
    pallas_call x5, Pallas kernels, hop(): pl.pallas_call(functools.partial(hop_kernel, step, block, start, len(arri...  13.9 us
    ppermute x2, waiting for transfers between devices, pass_on(): return [lax.ppermute(sums[0], 'tensor', rightward + leftward)]  8.06 us
    pallas_call x1, Pallas kernels, attend(): pl.pallas_call(functools.partial(attend_kernel, heads, kv, cache, steps,...  7.98 us
    ppermute x4, waiting for transfers between devices, pass_on(): lax.ppermute(sums[-1], 'tensor', leftward)  6.25 us
    pallas_call x1, Pallas kernels, settle(): pl.pallas_call(functools.partial(settle_kernel, places, len(arrays), len(...  5.98 us
    ppermute x4, waiting for transfers between devices, pass_on(): lax.ppermute(sums[0], 'tensor', rightward)  5.74 us
    ppermute x2, starting transfers between devices, pass_on(): return [lax.ppermute(sums[0], 'tensor', rightward + leftward)]  4.82 us
  transfers between devices with their start and end apart: 17, of which 5 were waited for; matrix products, arithmetic and copies ran while one was open for 0% of the time, Pallas kernels for 24%

profile of v11, /device:TPU:0, one launch (start us, length us, event | category | flops | bytes accessed | tf_op | source)
XLA Modules:
  0.0 91.0 jit_solution(10372154898142184985)
XLA Ops:
  0.0 8.0 %attend.1 = (bf16[256,1024]{1,0:T(8,128)(2,1)}, bf16[256,1024]{1,0:T(8,128)(2,1)}, bf16[256,256]{1,0:T(8,128)(2,1)}, bf16[128,1152]{1,0:T(8,128)(2,1)}, bf16[128,1152]{1,0:T(8,128)(2,1)}) custom-call(s32[1,256]{1,0:T(1,128)} %bitcast.13, s32[1,256]{1,0:T(1,128)} %bitcast.14, s32[1,32]{1,0:T(1,128)} %bitcast.15, bf16[2048,128]{1,0:T(8,128)(2,1)} %bitcast.10, ...), custom_call_target="tpu_custom_call" | custom-call | tf_op jit(solution)/shard_map/attend/pallas_call | solution.py:310
  8.0 3.0 %collective-permute-start.1 = (bf16[128,1152]{1,0:T(8,128)(2,1)}, bf16[128,1152]{1,0:T(8,128)(2,1)S(1)}, u32[]{:S(2)}, u32[]{:S(2)}) collective-permute-start(bf16[128,1152]{1,0:T(8,128)(2,1)} %get-tuple-element.22), channel_id=1, source_target_pairs={{0,8},{4,12},{8,0},{12,4},{1,9},{5,13},{9,1},{13,5},{2,10},{6,14},... | collective-permute-start | bytes 884744 | tf_op jit(solution)/shard_map/ppermute | solution.py:543
  11.0 3.5 %collective-permute-start.3 = (bf16[256,1024]{1,0:T(8,128)(2,1)}, bf16[256,1024]{1,0:T(8,128)(2,1)S(1)}, u32[]{:S(2)}, u32[]{:S(2)}) collective-permute-start(bf16[256,1024]{1,0:T(8,128)(2,1)} %get-tuple-element.23), channel_id=1, source_target_pairs={{0,1},{3,2},{4,5},{7,6},{8,9},{11,10},{12,13},{15,14},{16,17},{19,... | collective-permute-start | bytes 1572872 | tf_op jit(solution)/shard_map/ppermute | solution.py:554
  14.5 1.0 %copy-done = bf16[256,1024]{1,0:T(8,128)(2,1)S(1)} copy-done((bf16[256,1024]{1,0:T(8,128)(2,1)S(1)}, bf16[256,1024]{1,0:T(8,128)(2,1)}, u32[]{:S(2)}) %copy-start) | copy-done | bytes 524312
  15.5 2.3 %hop.5.refs_3_ = bf16[256,1024]{1,0:T(8,128)(2,1)S(1)} custom-call(bf16[256,1024]{1,0:T(8,128)(2,1)S(1)} %copy-done, bf16[1024,8192]{1,0:T(8,128)(2,1)} %refs_6_.1), custom_call_target="tpu_custom_call" | custom-call | tf_op jit(solution)/shard_map/hop/pallas_call | solution.py:363
  17.9 1.3 %collective-permute-start = (bf16[256,1024]{1,0:T(8,128)(2,1)S(1)}, bf16[256,1024]{1,0:T(8,128)(2,1)S(1)}, u32[]{:S(2)}, u32[]{:S(2)}) collective-permute-start(bf16[256,1024]{1,0:T(8,128)(2,1)S(1)} %hop.5.refs_3_), channel_id=1, source_target_pairs={{0,1},{3,2},{4,5},{7,6},{8,9},{11,10},{12,13},{15,14},{16,17},{19,... | collective-permute-start | bytes 1572872 | tf_op jit(solution)/shard_map/ppermute | solution.py:554
  19.4 7.8 %collective-permute-done.3.refs_0_ = bf16[256,1024]{1,0:T(8,128)(2,1)S(1)} collective-permute-done((bf16[256,1024]{1,0:T(8,128)(2,1)}, bf16[256,1024]{1,0:T(8,128)(2,1)S(1)}, u32[]{:S(2)}, u32[]{:S(2)}) %collective-permute-start.3) | collective-permute-done | bytes 524320 | tf_op jit(solution)/shard_map/ppermute | solution.py:554
  27.1 2.3 %hop.6.refs_4_ = bf16[256,1024]{1,0:T(8,128)(2,1)S(1)} custom-call(bf16[256,1024]{1,0:T(8,128)(2,1)S(1)} %collective-permute-done.3.refs_0_, bf16[256,1024]{1,0:T(8,128)(2,1)S(1)} %copy-done, bf16[1024,8192]{1,0:T(8,128)(2,1)} %refs_6_.1, bf16[256,1024]{1,0:T(8,128)(2,1)S(1)} %hop.5.refs_3_, bf16[128,1152]{1,0:T(8,128)(2,1)S(1)} %copy-done.3, ...), custom_call_target="tpu_custom_call" | custom-call | tf_op jit(solution)/shard_map/hop/pallas_call | solution.py:363
  29.4 0.7 down.1
  30.1 2.5 %collective-permute-start.10 = (bf16[128,128]{1,0:T(8,128)(2,1)S(1)}, bf16[128,128]{1,0:T(8,128)(2,1)S(1)}, u32[]{:S(2)}, u32[]{:S(2)}) collective-permute-start(bf16[128,128]{1,0:T(8,128)(2,1)S(1)} %get-tuple-element.24.refs_3_.refs_0_), channel_id=1, source_target_pairs={{0,3},{1,2},{2,1},{3,0},{4,7},{5,6},{6,5},{7,4},{8,11},{9,10},{10,... | collective-permute-start | bytes 98312 | tf_op jit(solution)/shard_map/ppermute | solution.py:573
  32.6 1.5 %collective-permute-start.8 = (bf16[128,128]{1,0:T(8,128)(2,1)S(1)}, bf16[128,128]{1,0:T(8,128)(2,1)S(1)}, u32[]{:S(2)}, u32[]{:S(2)}) collective-permute-start(bf16[128,128]{1,0:T(8,128)(2,1)S(1)} %get-tuple-element.24.refs_3_.refs_0_), channel_id=1, source_target_pairs={{0,1},{1,0},{2,3},{3,2},{4,5},{5,4},{6,7},{7,6},{8,9},{9,8},{10,11... | collective-permute-start | bytes 98312 | tf_op jit(solution)/shard_map/ppermute | solution.py:573
  34.1 0.4 collective-permute-start.9
  34.6 3.4 %collective-permute-start.6 = (bf16[256,1024]{1,0:T(8,128)(2,1)S(1)}, bf16[256,1024]{1,0:T(8,128)(2,1)S(1)}, u32[]{:S(2)}, u32[]{:S(2)}) collective-permute-start(bf16[256,1024]{1,0:T(8,128)(2,1)S(1)} %hop.6.refs_4_), channel_id=1, source_target_pairs={{0,1},{1,2},{4,5},{5,6},{8,9},{9,10},{12,13},{13,14},{16,17},{17,1... | collective-permute-start | bytes 1572872 | tf_op jit(solution)/shard_map/ppermute | solution.py:556
  38.3 0.7 collective-permute-start.7
  39.0 2.3 %hop.7.refs_6_ = bf16[256,1024]{1,0:T(8,128)(2,1)S(1)} custom-call(bf16[256,1024]{1,0:T(8,128)(2,1)S(1)} %collective-permute-done.refs_0_, bf16[256,1024]{1,0:T(8,128)(2,1)S(1)} %copy-done.1, bf16[1024,8192]{1,0:T(8,128)(2,1)} %refs_6_.1, bf16[128,128]{1,0:T(8,128)(2,1)S(1)} %get-tuple-element.24.refs_3_.refs_0_), custom_call_target="tpu_custom_call" | custom-call | tf_op jit(solution)/shard_map/hop/pallas_call | solution.py:363
  41.3 0.8 up.1
  42.1 0.6 collective-permute-start.13
  42.7 5.0 %collective-permute-start.4 = (bf16[256,1024]{1,0:T(8,128)(2,1)S(1)}, bf16[256,1024]{1,0:T(8,128)(2,1)S(1)}, u32[]{:S(2)}, u32[]{:S(2)}) collective-permute-start(bf16[256,1024]{1,0:T(8,128)(2,1)S(1)} %hop.7.refs_6_), channel_id=1, source_target_pairs={{0,1},{1,2},{4,5},{5,6},{8,9},{9,10},{12,13},{13,14},{16,17},{17,1... | collective-permute-start | bytes 1572872 | tf_op jit(solution)/shard_map/ppermute | solution.py:556
  47.7 0.7 collective-permute-start.5
  48.5 3.1 %collective-permute-done.6.refs_0_ = bf16[256,1024]{1,0:T(8,128)(2,1)S(1)} collective-permute-done((bf16[256,1024]{1,0:T(8,128)(2,1)S(1)}, bf16[256,1024]{1,0:T(8,128)(2,1)S(1)}, u32[]{:S(2)}, u32[]{:S(2)}) %collective-permute-start.6) | collective-permute-done | bytes 524320 | tf_op jit(solution)/shard_map/ppermute | solution.py:556
  51.6 3.5 %hop.8 = (bf16[256,1024]{1,0:T(8,128)(2,1)S(1)}, bf16[256,1024]{1,0:T(8,128)(2,1)S(1)}) custom-call(bf16[256,1024]{1,0:T(8,128)(2,1)S(1)} %collective-permute-done.6.refs_0_, bf16[256,1024]{1,0:T(8,128)(2,1)S(1)} %collective-permute-done.7.refs_1_, bf16[256,1024]{1,0:T(8,128)(2,1)S(1)} %copy-done.1, bf16[1024,8192]{1,0:T(8,128)(2,1)} %refs_6_.1, ...), custom_call_target="tpu_custom_call" | custom-call | tf_op jit(solution)/shard_map/hop/pallas_call | solution.py:363
  55.1 6.3 %collective-permute-start.15 = (bf16[256,1024]{1,0:T(8,128)(2,1)S(1)}, bf16[256,1024]{1,0:T(8,128)(2,1)S(1)}, u32[]{:S(2)}, u32[]{:S(2)}) collective-permute-start(bf16[256,1024]{1,0:T(8,128)(2,1)S(1)} %get-tuple-element.27.refs_4_), channel_id=1, source_target_pairs={{0,1},{1,2},{2,3},{4,5},{5,6},{6,7},{8,9},{9,10},{10,11},{12,13},{... | collective-permute-start | bytes 1572872 | tf_op jit(solution)/shard_map/ppermute | solution.py:556
  61.6 1.4 %collective-permute-start.16 = (bf16[256,1024]{1,0:T(8,128)(2,1)S(1)}, bf16[256,1024]{1,0:T(8,128)(2,1)S(1)}, u32[]{:S(2)}, u32[]{:S(2)}) collective-permute-start(bf16[256,1024]{1,0:T(8,128)(2,1)S(1)} %get-tuple-element.28.refs_5_), channel_id=1, source_target_pairs={{1,0},{2,1},{3,2},{5,4},{6,5},{7,6},{9,8},{10,9},{11,10},{13,12},{... | collective-permute-start | bytes 1572872 | tf_op jit(solution)/shard_map/ppermute | solution.py:557
  63.1 3.5 %hop.9 = (bf16[256,1024]{1,0:T(8,128)(2,1)S(1)}, bf16[256,1024]{1,0:T(8,128)(2,1)S(1)}) custom-call(bf16[256,1024]{1,0:T(8,128)(2,1)S(1)} %collective-permute-done.4.refs_0_, bf16[256,1024]{1,0:T(8,128)(2,1)S(1)} %collective-permute-done.5.refs_1_, bf16[256,1024]{1,0:T(8,128)(2,1)S(1)} %copy-done.1, bf16[1024,8192]{1,0:T(8,128)(2,1)} %refs_6_.1, ...), custom_call_target="tpu_custom_call" | custom-call | tf_op jit(solution)/shard_map/hop/pallas_call | solution.py:363
  66.6 5.2 %collective-permute-start.11 = (bf16[256,1024]{1,0:T(8,128)(2,1)S(1)}, bf16[256,1024]{1,0:T(8,128)(2,1)S(1)}, u32[]{:S(2)}, u32[]{:S(2)}) collective-permute-start(bf16[256,1024]{1,0:T(8,128)(2,1)S(1)} %get-tuple-element.29.refs_7_), channel_id=1, source_target_pairs={{0,1},{1,2},{2,3},{4,5},{5,6},{6,7},{8,9},{9,10},{10,11},{12,13},{... | collective-permute-start | bytes 1572872 | tf_op jit(solution)/shard_map/ppermute | solution.py:556
  71.8 1.3 %collective-permute-start.12 = (bf16[256,1024]{1,0:T(8,128)(2,1)S(1)}, bf16[256,1024]{1,0:T(8,128)(2,1)S(1)}, u32[]{:S(2)}, u32[]{:S(2)}) collective-permute-start(bf16[256,1024]{1,0:T(8,128)(2,1)S(1)} %get-tuple-element.30.refs_8_), channel_id=1, source_target_pairs={{1,0},{2,1},{3,2},{5,4},{6,5},{7,6},{9,8},{10,9},{11,10},{13,12},{... | collective-permute-start | bytes 1572872 | tf_op jit(solution)/shard_map/ppermute | solution.py:557
  73.1 6.0 %settle.1 = (f32[256,1024]{1,0:T(8,128)}, f32[256,1024]{1,0:T(8,128)}) custom-call(bf16[128,2048]{1,0:T(8,128)(2,1)S(1)} %get-tuple-element.26.refs_4_.refs_0_, bf16[128,2048]{1,0:T(8,128)(2,1)S(1)} %collective-permute-done.13.refs_1_, bf16[128,2048]{1,0:T(8,128)(2,1)S(1)} %collective-permute-done.14.refs_2_, bf16[256,256]{1,0:T(8,128)(2,1)S(1)} %copy-done.7, ...), custom_call_target="tpu_custom_call" | custom-call | tf_op jit(solution)/shard_map/settle/pallas_call | solution.py:467
  79.1 1.2 %copy-done.4 = f32[256,1024]{1,0:T(8,128)S(1)} copy-done((f32[256,1024]{1,0:T(8,128)S(1)}, f32[256,1024]{1,0:T(8,128)}, u32[]{:S(2)}) %copy-start.4) | copy-done | bytes 1048600
  80.4 0.9 finish.2.refs_0_
  81.3 2.6 %collective-permute-done.11.right_ref = bf16[256,1024]{1,0:T(8,128)(2,1)S(1)} collective-permute-done((bf16[256,1024]{1,0:T(8,128)(2,1)S(1)}, bf16[256,1024]{1,0:T(8,128)(2,1)S(1)}, u32[]{:S(2)}, u32[]{:S(2)}) %collective-permute-start.11) | collective-permute-done | bytes 524320 | tf_op jit(solution)/shard_map/ppermute | solution.py:556
  83.8 6.2 %collective-permute-done.12.left_ref = bf16[256,1024]{1,0:T(8,128)(2,1)S(1)} collective-permute-done((bf16[256,1024]{1,0:T(8,128)(2,1)S(1)}, bf16[256,1024]{1,0:T(8,128)(2,1)S(1)}, u32[]{:S(2)}, u32[]{:S(2)}) %collective-permute-start.12) | collective-permute-done | bytes 524320 | tf_op jit(solution)/shard_map/ppermute | solution.py:557
  90.1 0.9 finish.3
  (35 shorter events, 0.6 us)
Async XLA Ops:
  8.0 11.2 %collective-permute-start.1 = (bf16[128,1152]{1,0:T(8,128)(2,1)}, bf16[128,1152]{1,0:T(8,128)(2,1)S(1)}, u32[]{:S(2)}, u32[]{:S(2)}) collective-permute-start(bf16[128,1152]{1,0:T(8,128)(2,1)} %get-tuple-element.22), channel_id=1, source_target_pairs={{0,8},{4,12},{8,0},{12,4},{1,9},{5,13},{9,1},{13,5},{2,10},{6,14},... | collective-permute-start | bytes 884744 | tf_op jit(solution)/shard_map/ppermute | solution.py:543
  11.0 16.1 %collective-permute-start.3 = (bf16[256,1024]{1,0:T(8,128)(2,1)}, bf16[256,1024]{1,0:T(8,128)(2,1)S(1)}, u32[]{:S(2)}, u32[]{:S(2)}) collective-permute-start(bf16[256,1024]{1,0:T(8,128)(2,1)} %get-tuple-element.23), channel_id=1, source_target_pairs={{0,1},{3,2},{4,5},{7,6},{8,9},{11,10},{12,13},{15,14},{16,17},{19,... | collective-permute-start | bytes 1572872 | tf_op jit(solution)/shard_map/ppermute | solution.py:554
  14.5 1.0 %copy-start = (bf16[256,1024]{1,0:T(8,128)(2,1)S(1)}, bf16[256,1024]{1,0:T(8,128)(2,1)}, u32[]{:S(2)}) copy-start(bf16[256,1024]{1,0:T(8,128)(2,1)} %get-tuple-element.20.refs_0_.refs_1_.refs_2_.refs_4_) | copy-start | bytes 1572868
  15.5 3.7 %copy-start.3 = (bf16[128,1152]{1,0:T(8,128)(2,1)S(1)}, bf16[128,1152]{1,0:T(8,128)(2,1)}, u32[]{:S(2)}) copy-start(bf16[128,1152]{1,0:T(8,128)(2,1)} %get-tuple-element.21.refs_4_.refs_0_) | copy-start | bytes 884740
  17.9 20.4 %collective-permute-start = (bf16[256,1024]{1,0:T(8,128)(2,1)S(1)}, bf16[256,1024]{1,0:T(8,128)(2,1)S(1)}, u32[]{:S(2)}, u32[]{:S(2)}) collective-permute-start(bf16[256,1024]{1,0:T(8,128)(2,1)S(1)} %hop.5.refs_3_), channel_id=1, source_target_pairs={{0,1},{3,2},{4,5},{7,6},{8,9},{11,10},{12,13},{15,14},{16,17},{19,... | collective-permute-start | bytes 1572872 | tf_op jit(solution)/shard_map/ppermute | solution.py:554
  19.3 10.1 %copy-start.5 = (bf16[8,64,1024]{2,1,0:T(8,128)(2,1)S(1)}, bf16[8,64,1024]{2,1,0:T(8,128)(2,1)}, u32[]{:S(2)}) copy-start(bf16[8,64,1024]{2,1,0:T(8,128)(2,1)} %refs_3_.3) | copy-start | bytes 3145732
  19.3 7.8 %collective-permute-start.2 = (bf16[128,1152]{1,0:T(8,128)(2,1)S(1)}, bf16[128,1152]{1,0:T(8,128)(2,1)S(1)}, u32[]{:S(2)}, u32[]{:S(2)}) collective-permute-start(bf16[128,1152]{1,0:T(8,128)(2,1)S(1)} %pad_maximum_fusion.1), channel_id=1, source_target_pairs={{0,4},{4,0},{8,12},{12,8},{1,5},{5,1},{9,13},{13,9},{2,6},{6,2},{1... | collective-permute-start | bytes 884744 | tf_op jit(solution)/shard_map/ppermute | solution.py:543
  29.4 9.5 %copy-start.1 = (bf16[256,1024]{1,0:T(8,128)(2,1)S(1)}, bf16[256,1024]{1,0:T(8,128)(2,1)}, u32[]{:S(2)}) copy-start(bf16[256,1024]{1,0:T(8,128)(2,1)} %get-tuple-element.20.refs_0_.refs_1_.refs_2_.refs_4_) | copy-start | bytes 1572868
  30.1 11.2 %copy-start.2 = (bf16[8,64,2048]{2,1,0:T(8,128)(2,1)S(1)}, bf16[8,64,2048]{2,1,0:T(8,128)(2,1)}, u32[]{:S(2)}) copy-start(bf16[8,64,2048]{2,1,0:T(8,128)(2,1)} %refs_5_.2) | copy-start | bytes 6291460
  30.1 11.2 %collective-permute-start.10 = (bf16[128,128]{1,0:T(8,128)(2,1)S(1)}, bf16[128,128]{1,0:T(8,128)(2,1)S(1)}, u32[]{:S(2)}, u32[]{:S(2)}) collective-permute-start(bf16[128,128]{1,0:T(8,128)(2,1)S(1)} %get-tuple-element.24.refs_3_.refs_0_), channel_id=1, source_target_pairs={{0,3},{1,2},{2,1},{3,0},{4,7},{5,6},{6,5},{7,4},{8,11},{9,10},{10,... | collective-permute-start | bytes 98312 | tf_op jit(solution)/shard_map/ppermute | solution.py:573
  32.6 8.6 %collective-permute-start.8 = (bf16[128,128]{1,0:T(8,128)(2,1)S(1)}, bf16[128,128]{1,0:T(8,128)(2,1)S(1)}, u32[]{:S(2)}, u32[]{:S(2)}) collective-permute-start(bf16[128,128]{1,0:T(8,128)(2,1)S(1)} %get-tuple-element.24.refs_3_.refs_0_), channel_id=1, source_target_pairs={{0,1},{1,0},{2,3},{3,2},{4,5},{5,4},{6,7},{7,6},{8,9},{9,8},{10,11... | collective-permute-start | bytes 98312 | tf_op jit(solution)/shard_map/ppermute | solution.py:573
  34.1 7.2 %collective-permute-start.9 = (bf16[128,128]{1,0:T(8,128)(2,1)S(1)}, bf16[128,128]{1,0:T(8,128)(2,1)S(1)}, u32[]{:S(2)}, u32[]{:S(2)}) collective-permute-start(bf16[128,128]{1,0:T(8,128)(2,1)S(1)} %get-tuple-element.24.refs_3_.refs_0_), channel_id=1, source_target_pairs={{0,2},{1,3},{2,0},{3,1},{4,6},{5,7},{6,4},{7,5},{8,10},{9,11},{10,... | collective-permute-start | bytes 98312 | tf_op jit(solution)/shard_map/ppermute | solution.py:573
  34.6 17.1 %collective-permute-start.6 = (bf16[256,1024]{1,0:T(8,128)(2,1)S(1)}, bf16[256,1024]{1,0:T(8,128)(2,1)S(1)}, u32[]{:S(2)}, u32[]{:S(2)}) collective-permute-start(bf16[256,1024]{1,0:T(8,128)(2,1)S(1)} %hop.6.refs_4_), channel_id=1, source_target_pairs={{0,1},{1,2},{4,5},{5,6},{8,9},{9,10},{12,13},{13,14},{16,17},{17,1... | collective-permute-start | bytes 1572872 | tf_op jit(solution)/shard_map/ppermute | solution.py:556
  38.3 13.3 %collective-permute-start.7 = (bf16[256,1024]{1,0:T(8,128)(2,1)S(1)}, bf16[256,1024]{1,0:T(8,128)(2,1)S(1)}, u32[]{:S(2)}, u32[]{:S(2)}) collective-permute-start(bf16[256,1024]{1,0:T(8,128)(2,1)S(1)} %hop.6.refs_4_), channel_id=1, source_target_pairs={{2,1},{3,2},{6,5},{7,6},{10,9},{11,10},{14,13},{15,14},{18,17},{19... | collective-permute-start | bytes 1572872 | tf_op jit(solution)/shard_map/ppermute | solution.py:557
  42.1 19.4 %collective-permute-start.13 = (bf16[128,2048]{1,0:T(8,128)(2,1)S(1)}, bf16[128,2048]{1,0:T(8,128)(2,1)S(1)}, u32[]{:S(2)}, u32[]{:S(2)}) collective-permute-start(bf16[128,2048]{1,0:T(8,128)(2,1)S(1)} %get-tuple-element.31), channel_id=1, source_target_pairs={{0,8},{4,12},{8,0},{12,4},{1,9},{5,13},{9,1},{13,5},{2,10},{6,14},... | collective-permute-start | bytes 1572872 | tf_op jit(solution)/shard_map/ppermute | solution.py:543
  42.7 20.4 %collective-permute-start.4 = (bf16[256,1024]{1,0:T(8,128)(2,1)S(1)}, bf16[256,1024]{1,0:T(8,128)(2,1)S(1)}, u32[]{:S(2)}, u32[]{:S(2)}) collective-permute-start(bf16[256,1024]{1,0:T(8,128)(2,1)S(1)} %hop.7.refs_6_), channel_id=1, source_target_pairs={{0,1},{1,2},{4,5},{5,6},{8,9},{9,10},{12,13},{13,14},{16,17},{17,1... | collective-permute-start | bytes 1572872 | tf_op jit(solution)/shard_map/ppermute | solution.py:556
  47.7 15.4 %collective-permute-start.5 = (bf16[256,1024]{1,0:T(8,128)(2,1)S(1)}, bf16[256,1024]{1,0:T(8,128)(2,1)S(1)}, u32[]{:S(2)}, u32[]{:S(2)}) collective-permute-start(bf16[256,1024]{1,0:T(8,128)(2,1)S(1)} %hop.7.refs_6_), channel_id=1, source_target_pairs={{2,1},{3,2},{6,5},{7,6},{10,9},{11,10},{14,13},{15,14},{18,17},{19... | collective-permute-start | bytes 1572872 | tf_op jit(solution)/shard_map/ppermute | solution.py:557
  55.1 24.0 %collective-permute-start.15 = (bf16[256,1024]{1,0:T(8,128)(2,1)S(1)}, bf16[256,1024]{1,0:T(8,128)(2,1)S(1)}, u32[]{:S(2)}, u32[]{:S(2)}) collective-permute-start(bf16[256,1024]{1,0:T(8,128)(2,1)S(1)} %get-tuple-element.27.refs_4_), channel_id=1, source_target_pairs={{0,1},{1,2},{2,3},{4,5},{5,6},{6,7},{8,9},{9,10},{10,11},{12,13},{... | collective-permute-start | bytes 1572872 | tf_op jit(solution)/shard_map/ppermute | solution.py:556
  61.6 11.5 %collective-permute-start.14 = (bf16[128,2048]{1,0:T(8,128)(2,1)S(1)}, bf16[128,2048]{1,0:T(8,128)(2,1)S(1)}, u32[]{:S(2)}, u32[]{:S(2)}) collective-permute-start(bf16[128,2048]{1,0:T(8,128)(2,1)S(1)} %pad_maximum_fusion), channel_id=1, source_target_pairs={{0,4},{4,0},{8,12},{12,8},{1,5},{5,1},{9,13},{13,9},{2,6},{6,2},{1... | collective-permute-start | bytes 1572872 | tf_op jit(solution)/shard_map/ppermute | solution.py:543
  61.6 11.5 %copy-start.7 = (bf16[256,256]{1,0:T(8,128)(2,1)S(1)}, bf16[256,256]{1,0:T(8,128)(2,1)}, u32[]{:S(2)}) copy-start(bf16[256,256]{1,0:T(8,128)(2,1)} %get-tuple-element.32.refs_3_) | copy-start | bytes 393220
  61.6 17.5 %collective-permute-start.16 = (bf16[256,1024]{1,0:T(8,128)(2,1)S(1)}, bf16[256,1024]{1,0:T(8,128)(2,1)S(1)}, u32[]{:S(2)}, u32[]{:S(2)}) collective-permute-start(bf16[256,1024]{1,0:T(8,128)(2,1)S(1)} %get-tuple-element.28.refs_5_), channel_id=1, source_target_pairs={{1,0},{2,1},{3,2},{5,4},{6,5},{7,6},{9,8},{10,9},{11,10},{13,12},{... | collective-permute-start | bytes 1572872 | tf_op jit(solution)/shard_map/ppermute | solution.py:557
  66.6 17.2 %collective-permute-start.11 = (bf16[256,1024]{1,0:T(8,128)(2,1)S(1)}, bf16[256,1024]{1,0:T(8,128)(2,1)S(1)}, u32[]{:S(2)}, u32[]{:S(2)}) collective-permute-start(bf16[256,1024]{1,0:T(8,128)(2,1)S(1)} %get-tuple-element.29.refs_7_), channel_id=1, source_target_pairs={{0,1},{1,2},{2,3},{4,5},{5,6},{6,7},{8,9},{9,10},{10,11},{12,13},{... | collective-permute-start | bytes 1572872 | tf_op jit(solution)/shard_map/ppermute | solution.py:556
  71.8 18.3 %collective-permute-start.12 = (bf16[256,1024]{1,0:T(8,128)(2,1)S(1)}, bf16[256,1024]{1,0:T(8,128)(2,1)S(1)}, u32[]{:S(2)}, u32[]{:S(2)}) collective-permute-start(bf16[256,1024]{1,0:T(8,128)(2,1)S(1)} %get-tuple-element.30.refs_8_), channel_id=1, source_target_pairs={{1,0},{2,1},{3,2},{5,4},{6,5},{7,6},{9,8},{10,9},{11,10},{13,12},{... | collective-permute-start | bytes 1572872 | tf_op jit(solution)/shard_map/ppermute | solution.py:557
  79.1 1.2 %copy-start.4 = (f32[256,1024]{1,0:T(8,128)S(1)}, f32[256,1024]{1,0:T(8,128)}, u32[]{:S(2)}) copy-start(f32[256,1024]{1,0:T(8,128)} %get-tuple-element.34.settled_ref) | copy-start | bytes 3145732
  80.4 9.7 %copy-start.6 = (f32[256,1024]{1,0:T(8,128)S(1)}, f32[256,1024]{1,0:T(8,128)}, u32[]{:S(2)}) copy-start(f32[256,1024]{1,0:T(8,128)} %get-tuple-element.33.settled_ref) | copy-start | bytes 3145732

commit v12 on v10

--- a/solution.py
+++ b/solution.py
@@ -14,12 +14,13 @@
 MASKED = -1e30
 VMEM_LIMIT = 50 * 1024 * 1024
 FULL_VMEM = 61 * 1024 * 1024
-SHARES = ((1, 1),)
+SHARES = ((5, 3),)
 PIECE = 512
 SPLIT = 4
 
 VMEM = pl.BlockSpec(memory_space=pltpu.VMEM)
 ANY = pl.BlockSpec(memory_space=pl.ANY)
+LONG = pl.CostEstimate(flops=20 * 10**9, transcendentals=0, bytes_accessed=40 * 10**6)
 PARAMS = pltpu.CompilerParams(vmem_limit_bytes=VMEM_LIMIT)
 
 
@@ -345,7 +346,7 @@
         out_ref[:, columns] = product.astype(jnp.bfloat16)
 
 
-def hop(step, chain, arrived, attended, weight, block, after=()):
+def hop(step, chain, arrived, attended, weight, block, after=(), cost=None):
     arriving = arrived is not None
     start, chunk = chain_columns(block)[chain]
     operands = ([arrived] if arriving else []) + [attended, weight, *after]
@@ -356,6 +357,7 @@
         out_shape=jax.ShapeDtypeStruct((attended.shape[0], chunk), jnp.bfloat16),
         scratch_shapes=Weights.scratch(weight.shape[0], chunk),
         compiler_params=PARAMS,
+        cost_estimate=cost,
         name="hop",
     )(*operands)
 
@@ -546,9 +548,24 @@
     def forward(x):
         return lax.ppermute(x, "tensor", ring)
 
-    def next_hop(step, chain, after):
+    def pair_sums(x):
+        found = []
+        for away in range(1, count // 2):
+            pairs = [(p, (p + away) % (count // 2)) for p in range(count // 2)]
+            near, far = [], []
+            for p, q in pairs:
+                sender = 2 * p if p < q else 2 * p + 1
+                straight = 2 * q + (sender % 2)
+                near.append((sender, straight))
+                far.append((sender, straight ^ 1))
+            one = lax.ppermute(x, "tensor", near)
+            other = lax.ppermute(x, "tensor", far)
+            found += [one, other]
+        return found
+
+    def next_hop(step, chain, after, cost=None):
         arrived = forward(travelling[chain])
-        travelling[chain] = hop(step, chain, arrived, attended, output_weight, block, after)
+        travelling[chain] = hop(step, chain, arrived, attended, output_weight, block, after, cost)
 
     attended, first, chosen, *leaving = attend(
         query, cached_key_rows, cached_value_rows, new_token_key, new_token_value, lengths,
@@ -557,22 +574,23 @@
     second = hop(0, 1, None, attended, output_weight, block)
     rows_here = exchange(leaving)
     mid, inside = down(rows_here, slot_down_weight, after=[second])
-    rank_sums = [mid] + [
-        lax.ppermute(mid, "tensor", [(i, (i + k) % count) for i in range(count)])
-        for k in range(1, count)
-    ]
-
-    travelling = [first, second]
-    next_hop(1, 0, after=[mid])
-    travelling[0] = hold(travelling[0], after=rank_sums)
-    next_hop(1, 1, after=[travelling[0]])
-    next_hop(2, 0, after=[travelling[1]])
-    deltas = up(rank_sums, inside, slot_up_weight, after=[travelling[0]])
-    returned = exchange(deltas)
-    next_hop(2, 1, after=returned)
-    for step in range(3, count - 1):
+    travelling = [first, hold(second, after=[mid])]
+
+    def added(a, b):
+        return (a.astype(jnp.float32) + b.astype(jnp.float32)).astype(a.dtype)
+
+    rank_sum = added(mid, lax.ppermute(mid, "tensor", [(i, i ^ 1) for i in range(count)]))
+    rank_sums = [rank_sum] + pair_sums(rank_sum)
+    next_hop(1, 0, after=[rank_sum, travelling[1]], cost=LONG)
+    next_hop(1, 1, after=rank_sums[1:], cost=LONG)
+    for step in range(2, count - 1):
         for chain in range(2):
-            next_hop(step, chain, after=())
+            if (step, chain) == (2, 0):
+                next_hop(step, chain, after=())
+                deltas = up(rank_sums, inside, slot_up_weight, after=[travelling[0]])
+                returned = exchange(deltas)
+            else:
+                next_hop(step, chain, after=[deltas[0]])
     settled = settle(
         count - 1, returned, chosen, attended, residual, output_weight, after=[travelling[1]]
     )

time: 89.1 us -> 88.9 us (level)
  waiting for transfers between devices: 39.5 us -> 37.9 us
  Pallas kernels: 28.7 us -> 27.2 us
  starting transfers between devices: 19.4 us -> 20.8 us
  local copies, waits for them, and re-layouts: 1.08 us -> 2.38 us
    ppermute x3, starting transfers between devices: 2.41 us -> 6.76 us  [the longest x1 5.4 us: pair_sums(): other = lax.ppermute(x, 'tensor', far)]
    ppermute x6, waiting for transfers between devices: 12.9 us -> 16.3 us  [exchange(): lax.ppermute(blocks[r], 'dp', [(i, i ^ r) for i in range(replicas)])]
    ppermute x6, waiting for transfers between devices: 18.8 us -> 15.9 us  [forward(): return lax.ppermute(x, 'tensor', ring)]
    ppermute x6, starting transfers between devices: 13.2 us -> 10.3 us  [forward(): return lax.ppermute(x, 'tensor', ring)]
    ppermute x3, waiting for transfers between devices: 7.81 us -> 5.71 us  [the longest x1 4.18 us: per_device(): lax.ppermute(mid, 'tensor', [(i, i ^ 1) for i in range(count)])]
    pallas_call x1, Pallas kernels: 6.01 us -> 4.52 us  [settle(): pl.pallas_call(functools.partial(settle_kernel, step, replicas, len(after...]
    unnamed x20 -> x16, local copies, waits for them, and re-layouts: 1.08 us -> 2.38 us
  transfers between devices with their start and end apart: 15 -> 15, of which waited for: 9 -> 8; matrix products, arithmetic and copies ran while one was open for 0% -> 0% of each run, Pallas kernels for 22% -> 21%
where the time goes in v12:
time: 88.9 us; the launch traced here: 88.4 us
  waiting for transfers between devices  37.9 us (43%)
  Pallas kernels  27.2 us (31%)
  starting transfers between devices  20.8 us (23%)
  local copies, waits for them, and re-layouts  2.38 us (3%)
    ppermute x6, waiting for transfers between devices, exchange(): lax.ppermute(blocks[r], 'dp', [(i, i ^ r) for i in range(replicas)])  16.3 us
    ppermute x6, waiting for transfers between devices, forward(): return lax.ppermute(x, 'tensor', ring)  15.9 us
    pallas_call x5, Pallas kernels, hop(): pl.pallas_call(functools.partial(hop_kernel, step, block, start, arriving...  11.3 us
    ppermute x6, starting transfers between devices, forward(): return lax.ppermute(x, 'tensor', ring)  10.3 us
    pallas_call x1, Pallas kernels, attend(): pl.pallas_call(functools.partial(attend_kernel, heads, kv, cache, steps,...  8.24 us
    ppermute x1, starting transfers between devices, pair_sums(): other = lax.ppermute(x, 'tensor', far)  5.4 us
    pallas_call x1, Pallas kernels, settle(): pl.pallas_call(functools.partial(settle_kernel, step, replicas, len(after...  4.52 us
    ppermute x1, waiting for transfers between devices, per_device(): lax.ppermute(mid, 'tensor', [(i, i ^ 1) for i in range(count)])  4.18 us
  transfers between devices with their start and end apart: 15, of which 8 were waited for; matrix products, arithmetic and copies ran while one was open for 0% of the time, Pallas kernels for 21%

profile of v12, /device:TPU:0, one launch (start us, length us, event | category | flops | bytes accessed | tf_op | source)
XLA Modules:
  0.0 88.4 jit_solution(17084687661021018920)
XLA Ops:
  0.0 8.2 %attend.1 = (bf16[256,1024]{1,0:T(8,128)(2,1)}, bf16[256,1280]{1,0:T(8,128)(2,1)}, bf16[256,256]{1,0:T(8,128)(2,1)}, bf16[64,1152]{1,0:T(8,128)(2,1)}, bf16[64,1...) custom-call(s32[1,256]{1,0:T(1,128)} %bitcast.13, s32[1,256]{1,0:T(1,128)} %bitcast.14, ...), custom_call_target="tpu_custom_call" | custom-call | tf_op jit(solution)/shard_map/attend/pallas_call | solution.py:303
  8.2 4.1 %collective-permute-start.8 = (bf16[256,1280]{1,0:T(8,128)(2,1)}, bf16[256,1280]{1,0:T(8,128)(2,1)S(1)}, u32[]{:S(2)}, u32[]{:S(2)}) collective-permute-start(bf16[256,1280]{1,0:T(8,128)(2,1)} %get-tuple-element.27), channel_id=1, source_target_pairs={{0,2},{2,3},{3,1},{1,0},{4,6},{6,7},{7,5},{5,4},{8,10},{10,11},{11... | collective-permute-start | bytes 1966088 | tf_op jit(solution)/shard_map/ppermute | solution.py:549
  12.3 1.5 %collective-permute-start.1 = (bf16[64,1152]{1,0:T(8,128)(2,1)}, bf16[64,1152]{1,0:T(8,128)(2,1)S(1)}, u32[]{:S(2)}, u32[]{:S(2)}) collective-permute-start(bf16[64,1152]{1,0:T(8,128)(2,1)} %get-tuple-element.23), channel_id=1, source_target_pairs={{0,8},{4,12},{8,0},{12,4},{1,9},{5,13},{9,1},{13,5},{2,10},{6,14},... | collective-permute-start | bytes 442376 | tf_op jit(solution)/shard_map/ppermute | solution.py:543
  13.8 0.4 collective-permute-start.2
  14.2 1.0 %copy-done = bf16[256,1024]{1,0:T(8,128)(2,1)S(1)} copy-done((bf16[256,1024]{1,0:T(8,128)(2,1)S(1)}, bf16[256,1024]{1,0:T(8,128)(2,1)}, u32[]{:S(2)}) %copy-start) | copy-done | bytes 524312
  15.2 2.1 %hop.5.refs_5_.refs_0_ = bf16[256,768]{1,0:T(8,128)(2,1)S(1)} custom-call(bf16[256,1024]{1,0:T(8,128)(2,1)S(1)} %copy-done, bf16[1024,8192]{1,0:T(8,128)(2,1)} %refs_7_.1), custom_call_target="tpu_custom_call" | custom-call | tf_op jit(solution)/shard_map/hop/pallas_call | solution.py:353
  17.3 1.9 %collective-permute-done.1.refs_2_ = bf16[64,1152]{1,0:T(8,128)(2,1)S(1)} collective-permute-done((bf16[64,1152]{1,0:T(8,128)(2,1)}, bf16[64,1152]{1,0:T(8,128)(2,1)S(1)}, u32[]{:S(2)}, u32[]{:S(2)}) %collective-permute-start.1) | collective-permute-done | bytes 147488 | tf_op jit(solution)/shard_map/ppermute | solution.py:543
  19.2 2.4 %collective-permute-done.2.refs_3_ = bf16[64,1152]{1,0:T(8,128)(2,1)S(1)} collective-permute-done((bf16[64,1152]{1,0:T(8,128)(2,1)}, bf16[64,1152]{1,0:T(8,128)(2,1)S(1)}, u32[]{:S(2)}, u32[]{:S(2)}) %collective-permute-start.2) | collective-permute-done | bytes 147488 | tf_op jit(solution)/shard_map/ppermute | solution.py:543
  21.6 0.6 down.1
  22.3 1.9 %collective-permute-start.3 = (bf16[256,768]{1,0:T(8,128)(2,1)S(1)}, bf16[256,768]{1,0:T(8,128)(2,1)S(1)}, u32[]{:S(2)}, u32[]{:S(2)}) collective-permute-start(bf16[256,768]{1,0:T(8,128)(2,1)S(1)} %hold.1.refs_4_), channel_id=1, source_target_pairs={{0,2},{2,3},{3,1},{1,0},{4,6},{6,7},{7,5},{5,4},{8,10},{10,11},{11... | collective-permute-start | bytes 1179656 | tf_op jit(solution)/shard_map/ppermute | solution.py:549
  24.2 4.2 %collective-permute-done.4 = bf16[128,128]{1,0:T(8,128)(2,1)S(1)} collective-permute-done((bf16[128,128]{1,0:T(8,128)(2,1)S(1)}, bf16[128,128]{1,0:T(8,128)(2,1)S(1)}, u32[]{:S(2)}, u32[]{:S(2)}) %collective-permute-start.4) | collective-permute-done | bytes 32800 | tf_op jit(solution)/shard_map/ppermute | solution.py:582
  28.4 5.4 %collective-permute-start.6 = (bf16[128,128]{1,0:T(8,128)(2,1)S(1)}, bf16[128,128]{1,0:T(8,128)(2,1)S(1)}, u32[]{:S(2)}, u32[]{:S(2)}) collective-permute-start(bf16[128,128]{1,0:T(8,128)(2,1)S(1)} %add_convert_fusion.refs_3_.refs_0_), channel_id=1, source_target_pairs={{0,3},{3,0},{4,7},{7,4},{8,11},{11,8},{12,15},{15,12},{16,19},{19,... | collective-permute-start | bytes 98312 | tf_op jit(solution)/shard_map/ppermute | solution.py:562
  33.8 1.3 %collective-permute-start.5 = (bf16[128,128]{1,0:T(8,128)(2,1)S(1)}, bf16[128,128]{1,0:T(8,128)(2,1)S(1)}, u32[]{:S(2)}, u32[]{:S(2)}) collective-permute-start(bf16[128,128]{1,0:T(8,128)(2,1)S(1)} %add_convert_fusion.refs_3_.refs_0_), channel_id=1, source_target_pairs={{0,2},{3,1},{4,6},{7,5},{8,10},{11,9},{12,14},{15,13},{16,18},{19,... | collective-permute-start | bytes 98312 | tf_op jit(solution)/shard_map/ppermute | solution.py:561
  35.1 2.6 %hop.7 = bf16[256,1280]{1,0:T(8,128)(2,1)S(1)} custom-call(bf16[256,1280]{1,0:T(8,128)(2,1)S(1)} %collective-permute-done.8.refs_0_, bf16[256,1024]{1,0:T(8,128)(2,1)S(1)} %copy-done.1, bf16[1024,8192]{1,0:T(8,128)(2,1)} %refs_7_.1, bf16[128,128]{1,0:T(8,128)(2,1)S(1)} %add_convert_fusion.refs_3_.refs_0_, bf16[256,768]{1,0:T(8,128)(2,1)S(1)} %hold.1.refs_4_), custom_call_target="tpu_custom_call" | custom-call | flops 20000000000 | bytes 40000000 | tf_op jit(solution)/shard_map/hop/pallas_call | solution.py:353
  37.8 1.5 %collective-permute-done.6.refs_4_.refs_2_ = bf16[128,128]{1,0:T(8,128)(2,1)S(1)} collective-permute-done((bf16[128,128]{1,0:T(8,128)(2,1)S(1)}, bf16[128,128]{1,0:T(8,128)(2,1)S(1)}, u32[]{:S(2)}, u32[]{:S(2)}) %collective-permute-start.6) | collective-permute-done | bytes 32800 | tf_op jit(solution)/shard_map/ppermute | solution.py:562
  39.3 2.0 %hop.6 = bf16[256,768]{1,0:T(8,128)(2,1)S(1)} custom-call(bf16[256,768]{1,0:T(8,128)(2,1)S(1)} %collective-permute-done.3.refs_0_, bf16[256,1024]{1,0:T(8,128)(2,1)S(1)} %copy-done.1, bf16[1024,8192]{1,0:T(8,128)(2,1)} %refs_7_.1, bf16[128,128]{1,0:T(8,128)(2,1)S(1)} %collective-permute-done.5.refs_3_.refs_1_, ...), custom_call_target="tpu_custom_call" | custom-call | flops 20000000000 | bytes 40000000 | tf_op jit(solution)/shard_map/hop/pallas_call | solution.py:353
  41.3 2.3 %collective-permute-start.7 = (bf16[256,768]{1,0:T(8,128)(2,1)S(1)}, bf16[256,768]{1,0:T(8,128)(2,1)S(1)}, u32[]{:S(2)}, u32[]{:S(2)}) collective-permute-start(bf16[256,768]{1,0:T(8,128)(2,1)S(1)} %hop.6), channel_id=1, source_target_pairs={{0,2},{2,3},{3,1},{1,0},{4,6},{6,7},{7,5},{5,4},{8,10},{10,11},{11... | collective-permute-start | bytes 1179656 | tf_op jit(solution)/shard_map/ppermute | solution.py:549
  43.6 11.8 %collective-permute-done.9.refs_0_ = bf16[256,1280]{1,0:T(8,128)(2,1)S(1)} collective-permute-done((bf16[256,1280]{1,0:T(8,128)(2,1)S(1)}, bf16[256,1280]{1,0:T(8,128)(2,1)S(1)}, u32[]{:S(2)}, u32[]{:S(2)}) %collective-permute-start.9) | collective-permute-done | bytes 655392 | tf_op jit(solution)/shard_map/ppermute | solution.py:549
  55.5 2.6 %hop.8.refs_5_ = bf16[256,1280]{1,0:T(8,128)(2,1)S(1)} custom-call(bf16[256,1280]{1,0:T(8,128)(2,1)S(1)} %collective-permute-done.9.refs_0_, bf16[256,1024]{1,0:T(8,128)(2,1)S(1)} %copy-done.1, bf16[1024,8192]{1,0:T(8,128)(2,1)} %refs_7_.1), custom_call_target="tpu_custom_call" | custom-call | tf_op jit(solution)/shard_map/hop/pallas_call | solution.py:353
  58.0 1.0 %collective-permute-start.14 = (bf16[256,1280]{1,0:T(8,128)(2,1)S(1)}, bf16[256,1280]{1,0:T(8,128)(2,1)S(1)}, u32[]{:S(2)}, u32[]{:S(2)}) collective-permute-start(bf16[256,1280]{1,0:T(8,128)(2,1)S(1)} %hop.8.refs_5_), channel_id=1, source_target_pairs={{0,2},{2,3},{3,1},{1,0},{4,6},{6,7},{7,5},{5,4},{8,10},{10,11},{11... | collective-permute-start | bytes 1966088 | tf_op jit(solution)/shard_map/ppermute | solution.py:549
  59.0 0.8 up.1
  59.8 4.1 %collective-permute-done.7.refs_0_ = bf16[256,768]{1,0:T(8,128)(2,1)S(1)} collective-permute-done((bf16[256,768]{1,0:T(8,128)(2,1)S(1)}, bf16[256,768]{1,0:T(8,128)(2,1)S(1)}, u32[]{:S(2)}, u32[]{:S(2)}) %collective-permute-start.7) | collective-permute-done | bytes 393248 | tf_op jit(solution)/shard_map/ppermute | solution.py:549
  63.9 2.1 %hop.9.refs_8_ = bf16[256,768]{1,0:T(8,128)(2,1)S(1)} custom-call(bf16[256,768]{1,0:T(8,128)(2,1)S(1)} %collective-permute-done.7.refs_0_, bf16[256,1024]{1,0:T(8,128)(2,1)S(1)} %copy-done.1, bf16[1024,8192]{1,0:T(8,128)(2,1)} %refs_7_.1, bf16[64,2048]{1,0:T(8,128)(2,1)S(1)} %get-tuple-element.28.refs_3_.refs_0_), custom_call_target="tpu_custom_call" | custom-call | tf_op jit(solution)/shard_map/hop/pallas_call | solution.py:353
  66.0 1.0 %collective-permute-start.10 = (bf16[256,768]{1,0:T(8,128)(2,1)S(1)}, bf16[256,768]{1,0:T(8,128)(2,1)S(1)}, u32[]{:S(2)}, u32[]{:S(2)}) collective-permute-start(bf16[256,768]{1,0:T(8,128)(2,1)S(1)} %hop.9.refs_8_), channel_id=1, source_target_pairs={{0,2},{2,3},{3,1},{1,0},{4,6},{6,7},{7,5},{5,4},{8,10},{10,11},{11... | collective-permute-start | bytes 1179656 | tf_op jit(solution)/shard_map/ppermute | solution.py:549
  66.9 1.5 %collective-permute-start.12 = (bf16[64,2048]{1,0:T(8,128)(2,1)S(1)}, bf16[64,2048]{1,0:T(8,128)(2,1)S(1)}, u32[]{:S(2)}, u32[]{:S(2)}) collective-permute-start(bf16[64,2048]{1,0:T(8,128)(2,1)S(1)} %get-tuple-element.30), channel_id=1, source_target_pairs={{0,8},{4,12},{8,0},{12,4},{1,9},{5,13},{9,1},{13,5},{2,10},{6,14},... | collective-permute-start | bytes 786440 | tf_op jit(solution)/shard_map/ppermute | solution.py:543
  68.4 0.4 collective-permute-start.13
  68.8 7.2 %collective-permute-done.12.refs_2_ = bf16[64,2048]{1,0:T(8,128)(2,1)S(1)} collective-permute-done((bf16[64,2048]{1,0:T(8,128)(2,1)S(1)}, bf16[64,2048]{1,0:T(8,128)(2,1)S(1)}, u32[]{:S(2)}, u32[]{:S(2)}) %collective-permute-start.12) | collective-permute-done | bytes 262176 | tf_op jit(solution)/shard_map/ppermute | solution.py:543
  76.0 4.8 %collective-permute-done.13.refs_3_ = bf16[64,2048]{1,0:T(8,128)(2,1)S(1)} collective-permute-done((bf16[64,2048]{1,0:T(8,128)(2,1)S(1)}, bf16[64,2048]{1,0:T(8,128)(2,1)S(1)}, u32[]{:S(2)}, u32[]{:S(2)}) %collective-permute-start.13) | collective-permute-done | bytes 262176 | tf_op jit(solution)/shard_map/ppermute | solution.py:543
  80.9 4.5 %settle.1 = (f32[256,1280]{1,0:T(8,128)}, f32[256,768]{1,0:T(8,128)S(1)}) custom-call(bf16[64,2048]{1,0:T(8,128)(2,1)S(1)} %get-tuple-element.28.refs_3_.refs_0_, bf16[64,2048]{1,0:T(8,128)(2,1)S(1)} %collective-permute-done.11.refs_1_, bf16[64,2048]{1,0:T(8,128)(2,1)S(1)} %collective-permute-done.12.refs_2_, ...), custom_call_target="tpu_custom_call" | custom-call | tf_op jit(solution)/shard_map/settle/pallas_call | solution.py:459
  85.4 1.3 %copy-done.3 = f32[256,1280]{1,0:T(8,128)S(1)} copy-done((f32[256,1280]{1,0:T(8,128)S(1)}, f32[256,1280]{1,0:T(8,128)}, u32[]{:S(2)}) %copy-start.3) | copy-done | bytes 1310744
  86.7 0.9 %finish.2.refs_0_ = bf16[256,2048]{1,0:T(8,128)(2,1)} custom-call(bf16[256,1280]{1,0:T(8,128)(2,1)S(1)} %collective-permute-done.14.arrived_ref, f32[256,1280]{1,0:T(8,128)S(1)} %copy-done.3), custom_call_target="tpu_custom_call" | custom-call | tf_op jit(solution)/shard_map/finish/pallas_call | solution.py:490
  87.6 0.8 finish.3
  (27 shorter events, 0.2 us)
Async XLA Ops:
  8.2 26.9 %collective-permute-start.8 = (bf16[256,1280]{1,0:T(8,128)(2,1)}, bf16[256,1280]{1,0:T(8,128)(2,1)S(1)}, u32[]{:S(2)}, u32[]{:S(2)}) collective-permute-start(bf16[256,1280]{1,0:T(8,128)(2,1)} %get-tuple-element.27), channel_id=1, source_target_pairs={{0,2},{2,3},{3,1},{1,0},{4,6},{6,7},{7,5},{5,4},{8,10},{10,11},{11... | collective-permute-start | bytes 1966088 | tf_op jit(solution)/shard_map/ppermute | solution.py:549
  12.3 5.0 %collective-permute-start = (bf16[64,1152]{1,0:T(8,128)(2,1)}, bf16[64,1152]{1,0:T(8,128)(2,1)S(1)}, u32[]{:S(2)}, u32[]{:S(2)}) collective-permute-start(bf16[64,1152]{1,0:T(8,128)(2,1)} %get-tuple-element.22), channel_id=1, source_target_pairs={{0,4},{4,0},{8,12},{12,8},{1,5},{5,1},{9,13},{13,9},{2,6},{6,2},{1... | collective-permute-start | bytes 442376 | tf_op jit(solution)/shard_map/ppermute | solution.py:543
  12.3 6.9 %collective-permute-start.1 = (bf16[64,1152]{1,0:T(8,128)(2,1)}, bf16[64,1152]{1,0:T(8,128)(2,1)S(1)}, u32[]{:S(2)}, u32[]{:S(2)}) collective-permute-start(bf16[64,1152]{1,0:T(8,128)(2,1)} %get-tuple-element.23), channel_id=1, source_target_pairs={{0,8},{4,12},{8,0},{12,4},{1,9},{5,13},{9,1},{13,5},{2,10},{6,14},... | collective-permute-start | bytes 442376 | tf_op jit(solution)/shard_map/ppermute | solution.py:543
  13.8 7.7 %collective-permute-start.2 = (bf16[64,1152]{1,0:T(8,128)(2,1)}, bf16[64,1152]{1,0:T(8,128)(2,1)S(1)}, u32[]{:S(2)}, u32[]{:S(2)}) collective-permute-start(bf16[64,1152]{1,0:T(8,128)(2,1)} %get-tuple-element.24), channel_id=1, source_target_pairs={{0,12},{4,8},{8,4},{12,0},{1,13},{5,9},{9,5},{13,1},{2,14},{6,10},... | collective-permute-start | bytes 442376 | tf_op jit(solution)/shard_map/ppermute | solution.py:543
  14.2 1.0 %copy-start = (bf16[256,1024]{1,0:T(8,128)(2,1)S(1)}, bf16[256,1024]{1,0:T(8,128)(2,1)}, u32[]{:S(2)}) copy-start(bf16[256,1024]{1,0:T(8,128)(2,1)} %get-tuple-element.20.refs_0_.refs_1_.refs_5_) | copy-start | bytes 1572868
  15.2 6.3 %copy-start.5 = (bf16[8,64,1024]{2,1,0:T(8,128)(2,1)S(1)}, bf16[8,64,1024]{2,1,0:T(8,128)(2,1)}, u32[]{:S(2)}) copy-start(bf16[8,64,1024]{2,1,0:T(8,128)(2,1)} %refs_4_.2) | copy-start | bytes 3145732
  15.2 6.3 %copy-start.6 = (bf16[64,1152]{1,0:T(8,128)(2,1)S(1)}, bf16[64,1152]{1,0:T(8,128)(2,1)}, u32[]{:S(2)}) copy-start(bf16[64,1152]{1,0:T(8,128)(2,1)} %get-tuple-element.21.refs_0_) | copy-start | bytes 442372
  17.3 17.8 %copy-start.1 = (bf16[256,1024]{1,0:T(8,128)(2,1)S(1)}, bf16[256,1024]{1,0:T(8,128)(2,1)}, u32[]{:S(2)}) copy-start(bf16[256,1024]{1,0:T(8,128)(2,1)} %get-tuple-element.20.refs_0_.refs_1_.refs_5_) | copy-start | bytes 1572868
  22.2 6.2 %collective-permute-start.4 = (bf16[128,128]{1,0:T(8,128)(2,1)S(1)}, bf16[128,128]{1,0:T(8,128)(2,1)S(1)}, u32[]{:S(2)}, u32[]{:S(2)}) collective-permute-start(bf16[128,128]{1,0:T(8,128)(2,1)S(1)} %get-tuple-element.25.refs_1_), channel_id=1, source_target_pairs={{0,1},{1,0},{2,3},{3,2},{4,5},{5,4},{6,7},{7,6},{8,9},{9,8},{10,11... | collective-permute-start | bytes 98312 | tf_op jit(solution)/shard_map/ppermute | solution.py:582
  22.3 17.0 %collective-permute-start.3 = (bf16[256,768]{1,0:T(8,128)(2,1)S(1)}, bf16[256,768]{1,0:T(8,128)(2,1)S(1)}, u32[]{:S(2)}, u32[]{:S(2)}) collective-permute-start(bf16[256,768]{1,0:T(8,128)(2,1)S(1)} %hold.1.refs_4_), channel_id=1, source_target_pairs={{0,2},{2,3},{3,1},{1,0},{4,6},{6,7},{7,5},{5,4},{8,10},{10,11},{11... | collective-permute-start | bytes 1179656 | tf_op jit(solution)/shard_map/ppermute | solution.py:549
  28.4 10.9 %collective-permute-start.6 = (bf16[128,128]{1,0:T(8,128)(2,1)S(1)}, bf16[128,128]{1,0:T(8,128)(2,1)S(1)}, u32[]{:S(2)}, u32[]{:S(2)}) collective-permute-start(bf16[128,128]{1,0:T(8,128)(2,1)S(1)} %add_convert_fusion.refs_3_.refs_0_), channel_id=1, source_target_pairs={{0,3},{3,0},{4,7},{7,4},{8,11},{11,8},{12,15},{15,12},{16,19},{19,... | collective-permute-start | bytes 98312 | tf_op jit(solution)/shard_map/ppermute | solution.py:562
  33.8 5.5 %collective-permute-start.5 = (bf16[128,128]{1,0:T(8,128)(2,1)S(1)}, bf16[128,128]{1,0:T(8,128)(2,1)S(1)}, u32[]{:S(2)}, u32[]{:S(2)}) collective-permute-start(bf16[128,128]{1,0:T(8,128)(2,1)S(1)} %add_convert_fusion.refs_3_.refs_0_), channel_id=1, source_target_pairs={{0,2},{3,1},{4,6},{7,5},{8,10},{11,9},{12,14},{15,13},{16,18},{19,... | collective-permute-start | bytes 98312 | tf_op jit(solution)/shard_map/ppermute | solution.py:561
  37.7 17.7 %collective-permute-start.9 = (bf16[256,1280]{1,0:T(8,128)(2,1)S(1)}, bf16[256,1280]{1,0:T(8,128)(2,1)S(1)}, u32[]{:S(2)}, u32[]{:S(2)}) collective-permute-start(bf16[256,1280]{1,0:T(8,128)(2,1)S(1)} %hop.7), channel_id=1, source_target_pairs={{0,2},{2,3},{3,1},{1,0},{4,6},{6,7},{7,5},{5,4},{8,10},{10,11},{11... | collective-permute-start | bytes 1966088 | tf_op jit(solution)/shard_map/ppermute | solution.py:549
  41.3 17.7 %copy-start.2 = (bf16[8,64,2048]{2,1,0:T(8,128)(2,1)S(1)}, bf16[8,64,2048]{2,1,0:T(8,128)(2,1)}, u32[]{:S(2)}) copy-start(bf16[8,64,2048]{2,1,0:T(8,128)(2,1)} %refs_4_.3) | copy-start | bytes 6291460
  41.3 22.6 %collective-permute-start.7 = (bf16[256,768]{1,0:T(8,128)(2,1)S(1)}, bf16[256,768]{1,0:T(8,128)(2,1)S(1)}, u32[]{:S(2)}, u32[]{:S(2)}) collective-permute-start(bf16[256,768]{1,0:T(8,128)(2,1)S(1)} %hop.6), channel_id=1, source_target_pairs={{0,2},{2,3},{3,1},{1,0},{4,6},{6,7},{7,5},{5,4},{8,10},{10,11},{11... | collective-permute-start | bytes 1179656 | tf_op jit(solution)/shard_map/ppermute | solution.py:549
  58.0 27.4 %collective-permute-start.14 = (bf16[256,1280]{1,0:T(8,128)(2,1)S(1)}, bf16[256,1280]{1,0:T(8,128)(2,1)S(1)}, u32[]{:S(2)}, u32[]{:S(2)}) collective-permute-start(bf16[256,1280]{1,0:T(8,128)(2,1)S(1)} %hop.8.refs_5_), channel_id=1, source_target_pairs={{0,2},{2,3},{3,1},{1,0},{4,6},{6,7},{7,5},{5,4},{8,10},{10,11},{11... | collective-permute-start | bytes 1966088 | tf_op jit(solution)/shard_map/ppermute | solution.py:549
  63.9 17.0 %copy-start.4 = (bf16[256,2048]{1,0:T(8,128)(2,1)S(1)}, bf16[256,2048]{1,0:T(8,128)(2,1)}, u32[]{:S(2)}) copy-start(bf16[256,2048]{1,0:T(8,128)(2,1)} %refs_6_.1) | copy-start | bytes 3145732
  63.9 17.0 %copy-start.7 = (bf16[256,256]{1,0:T(8,128)(2,1)S(1)}, bf16[256,256]{1,0:T(8,128)(2,1)}, u32[]{:S(2)}) copy-start(bf16[256,256]{1,0:T(8,128)(2,1)} %get-tuple-element.32.refs_4_) | copy-start | bytes 393220
  66.0 21.7 %collective-permute-start.10 = (bf16[256,768]{1,0:T(8,128)(2,1)S(1)}, bf16[256,768]{1,0:T(8,128)(2,1)S(1)}, u32[]{:S(2)}, u32[]{:S(2)}) collective-permute-start(bf16[256,768]{1,0:T(8,128)(2,1)S(1)} %hop.9.refs_8_), channel_id=1, source_target_pairs={{0,2},{2,3},{3,1},{1,0},{4,6},{6,7},{7,5},{5,4},{8,10},{10,11},{11... | collective-permute-start | bytes 1179656 | tf_op jit(solution)/shard_map/ppermute | solution.py:549
  66.9 1.9 %collective-permute-start.11 = (bf16[64,2048]{1,0:T(8,128)(2,1)S(1)}, bf16[64,2048]{1,0:T(8,128)(2,1)S(1)}, u32[]{:S(2)}, u32[]{:S(2)}) collective-permute-start(bf16[64,2048]{1,0:T(8,128)(2,1)S(1)} %get-tuple-element.29), channel_id=1, source_target_pairs={{0,4},{4,0},{8,12},{12,8},{1,5},{5,1},{9,13},{13,9},{2,6},{6,2},{1... | collective-permute-start | bytes 786440 | tf_op jit(solution)/shard_map/ppermute | solution.py:543
  66.9 9.1 %collective-permute-start.12 = (bf16[64,2048]{1,0:T(8,128)(2,1)S(1)}, bf16[64,2048]{1,0:T(8,128)(2,1)S(1)}, u32[]{:S(2)}, u32[]{:S(2)}) collective-permute-start(bf16[64,2048]{1,0:T(8,128)(2,1)S(1)} %get-tuple-element.30), channel_id=1, source_target_pairs={{0,8},{4,12},{8,0},{12,4},{1,9},{5,13},{9,1},{13,5},{2,10},{6,14},... | collective-permute-start | bytes 786440 | tf_op jit(solution)/shard_map/ppermute | solution.py:543
  68.4 12.4 %collective-permute-start.13 = (bf16[64,2048]{1,0:T(8,128)(2,1)S(1)}, bf16[64,2048]{1,0:T(8,128)(2,1)S(1)}, u32[]{:S(2)}, u32[]{:S(2)}) collective-permute-start(bf16[64,2048]{1,0:T(8,128)(2,1)S(1)} %get-tuple-element.31), channel_id=1, source_target_pairs={{0,12},{4,8},{8,4},{12,0},{1,13},{5,9},{9,5},{13,1},{2,14},{6,10},... | collective-permute-start | bytes 786440 | tf_op jit(solution)/shard_map/ppermute | solution.py:543
  85.4 1.3 %copy-start.3 = (f32[256,1280]{1,0:T(8,128)S(1)}, f32[256,1280]{1,0:T(8,128)}, u32[]{:S(2)}) copy-start(f32[256,1280]{1,0:T(8,128)} %get-tuple-element.34.settled_ref) | copy-start | bytes 3932164

commit v13 on v12

--- a/solution.py
+++ b/solution.py
@@ -21,6 +21,7 @@
 VMEM = pl.BlockSpec(memory_space=pltpu.VMEM)
 ANY = pl.BlockSpec(memory_space=pl.ANY)
 LONG = pl.CostEstimate(flops=20 * 10**9, transcendentals=0, bytes_accessed=40 * 10**6)
+MEDIUM = pl.CostEstimate(flops=3 * 10**9, transcendentals=0, bytes_accessed=6 * 10**6)
 PARAMS = pltpu.CompilerParams(vmem_limit_bytes=VMEM_LIMIT)
 
 
@@ -463,6 +464,7 @@
         out_shape=[jax.ShapeDtypeStruct((rows, chunk), jnp.float32) for _, chunk in chains],
         scratch_shapes=Weights.scratch(weight.shape[0], width),
         compiler_params=PARAMS,
+        cost_estimate=LONG,
         name="settle",
     )(*returned, chosen, attended, residual, weight, *after)
 
@@ -582,11 +584,11 @@
     rank_sum = added(mid, lax.ppermute(mid, "tensor", [(i, i ^ 1) for i in range(count)]))
     rank_sums = [rank_sum] + pair_sums(rank_sum)
     next_hop(1, 0, after=[rank_sum, travelling[1]], cost=LONG)
-    next_hop(1, 1, after=rank_sums[1:], cost=LONG)
+    next_hop(1, 1, after=[travelling[0]], cost=MEDIUM)
     for step in range(2, count - 1):
         for chain in range(2):
             if (step, chain) == (2, 0):
-                next_hop(step, chain, after=())
+                next_hop(step, chain, after=rank_sums[1:], cost=LONG)
                 deltas = up(rank_sums, inside, slot_up_weight, after=[travelling[0]])
                 returned = exchange(deltas)
             else:

time: 88.9 us -> 85.3 us (0.960)
  waiting for transfers between devices: 37.9 us -> 31.9 us
  starting transfers between devices: 20.8 us -> 23.3 us
    ppermute x1, waiting for transfers between devices: 1.53 us -> 11.1 us  [pair_sums(): other = lax.ppermute(x, 'tensor', far)]
    ppermute x6, waiting for transfers between devices: 15.9 us -> 6.64 us  [forward(): return lax.ppermute(x, 'tensor', ring)]
    ppermute x6, waiting for transfers between devices: 16.3 us -> 9.95 us  [exchange(): lax.ppermute(blocks[r], 'dp', [(i, i ^ r) for i in range(replicas)])]
    ppermute x6, starting transfers between devices: 10.3 us -> 14 us  [forward(): return lax.ppermute(x, 'tensor', ring)]
    ppermute x1, starting transfers between devices: 5.4 us -> 4.12 us  [pair_sums(): other = lax.ppermute(x, 'tensor', far)]
where the time goes in v13:
time: 85.3 us; the launch traced here: 84.9 us
  waiting for transfers between devices  31.9 us (37%)
  Pallas kernels  27.2 us (32%)
  starting transfers between devices  23.3 us (27%)
  local copies, waits for them, and re-layouts  2.38 us (3%)
    ppermute x6, starting transfers between devices, forward(): return lax.ppermute(x, 'tensor', ring)  14 us
    pallas_call x5, Pallas kernels, hop(): pl.pallas_call(functools.partial(hop_kernel, step, block, start, arriving...  11.3 us
    ppermute x1, waiting for transfers between devices, pair_sums(): other = lax.ppermute(x, 'tensor', far)  11.1 us
    ppermute x6, waiting for transfers between devices, exchange(): lax.ppermute(blocks[r], 'dp', [(i, i ^ r) for i in range(replicas)])  9.95 us
    pallas_call x1, Pallas kernels, attend(): pl.pallas_call(functools.partial(attend_kernel, heads, kv, cache, steps,...  8.24 us
    ppermute x6, waiting for transfers between devices, forward(): return lax.ppermute(x, 'tensor', ring)  6.64 us
    pallas_call x1, Pallas kernels, settle(): pl.pallas_call(functools.partial(settle_kernel, step, replicas, len(after...  4.51 us
    ppermute x1, waiting for transfers between devices, per_device(): lax.ppermute(mid, 'tensor', [(i, i ^ 1) for i in range(count)])  4.18 us
  transfers between devices with their start and end apart: 15, of which 8 were waited for; matrix products, arithmetic and copies ran while one was open for 0% of the time, Pallas kernels for 21%

profile of v13, /device:TPU:0, one launch (start us, length us, event | category | flops | bytes accessed | tf_op | source)
XLA Modules:
  0.0 84.9 jit_solution(2350114218758553310)
XLA Ops:
  0.0 8.2 %attend.1 = (bf16[256,1024]{1,0:T(8,128)(2,1)}, bf16[256,1280]{1,0:T(8,128)(2,1)}, bf16[256,256]{1,0:T(8,128)(2,1)}, bf16[64,1152]{1,0:T(8,128)(2,1)}, bf16[64,1...) custom-call(s32[1,256]{1,0:T(1,128)} %bitcast.13, s32[1,256]{1,0:T(1,128)} %bitcast.14, ...), custom_call_target="tpu_custom_call" | custom-call | tf_op jit(solution)/shard_map/attend/pallas_call | solution.py:304
  8.2 4.1 %collective-permute-start.4 = (bf16[256,1280]{1,0:T(8,128)(2,1)}, bf16[256,1280]{1,0:T(8,128)(2,1)S(1)}, u32[]{:S(2)}, u32[]{:S(2)}) collective-permute-start(bf16[256,1280]{1,0:T(8,128)(2,1)} %get-tuple-element.26), channel_id=1, source_target_pairs={{0,2},{2,3},{3,1},{1,0},{4,6},{6,7},{7,5},{5,4},{8,10},{10,11},{11... | collective-permute-start | bytes 1966088 | tf_op jit(solution)/shard_map/ppermute | solution.py:551
  12.3 1.5 %collective-permute-start.1 = (bf16[64,1152]{1,0:T(8,128)(2,1)}, bf16[64,1152]{1,0:T(8,128)(2,1)S(1)}, u32[]{:S(2)}, u32[]{:S(2)}) collective-permute-start(bf16[64,1152]{1,0:T(8,128)(2,1)} %get-tuple-element.23), channel_id=1, source_target_pairs={{0,8},{4,12},{8,0},{12,4},{1,9},{5,13},{9,1},{13,5},{2,10},{6,14},... | collective-permute-start | bytes 442376 | tf_op jit(solution)/shard_map/ppermute | solution.py:545
  13.8 0.4 collective-permute-start.2
  14.2 1.0 %copy-done = bf16[256,1024]{1,0:T(8,128)(2,1)S(1)} copy-done((bf16[256,1024]{1,0:T(8,128)(2,1)S(1)}, bf16[256,1024]{1,0:T(8,128)(2,1)}, u32[]{:S(2)}) %copy-start) | copy-done | bytes 524312
  15.2 2.1 %hop.5.refs_5_.refs_0_ = bf16[256,768]{1,0:T(8,128)(2,1)S(1)} custom-call(bf16[256,1024]{1,0:T(8,128)(2,1)S(1)} %copy-done, bf16[1024,8192]{1,0:T(8,128)(2,1)} %refs_7_.1), custom_call_target="tpu_custom_call" | custom-call | tf_op jit(solution)/shard_map/hop/pallas_call | solution.py:354
  17.3 1.9 %collective-permute-done.1.refs_2_ = bf16[64,1152]{1,0:T(8,128)(2,1)S(1)} collective-permute-done((bf16[64,1152]{1,0:T(8,128)(2,1)}, bf16[64,1152]{1,0:T(8,128)(2,1)S(1)}, u32[]{:S(2)}, u32[]{:S(2)}) %collective-permute-start.1) | collective-permute-done | bytes 147488 | tf_op jit(solution)/shard_map/ppermute | solution.py:545
  19.2 2.4 %collective-permute-done.2.refs_3_ = bf16[64,1152]{1,0:T(8,128)(2,1)S(1)} collective-permute-done((bf16[64,1152]{1,0:T(8,128)(2,1)}, bf16[64,1152]{1,0:T(8,128)(2,1)S(1)}, u32[]{:S(2)}, u32[]{:S(2)}) %collective-permute-start.2) | collective-permute-done | bytes 147488 | tf_op jit(solution)/shard_map/ppermute | solution.py:545
  21.6 0.6 down.1
  22.3 1.9 %collective-permute-start.3 = (bf16[256,768]{1,0:T(8,128)(2,1)S(1)}, bf16[256,768]{1,0:T(8,128)(2,1)S(1)}, u32[]{:S(2)}, u32[]{:S(2)}) collective-permute-start(bf16[256,768]{1,0:T(8,128)(2,1)S(1)} %hold.1.refs_4_), channel_id=1, source_target_pairs={{0,2},{2,3},{3,1},{1,0},{4,6},{6,7},{7,5},{5,4},{8,10},{10,11},{11... | collective-permute-start | bytes 1179656 | tf_op jit(solution)/shard_map/ppermute | solution.py:551
  24.2 4.2 %collective-permute-done.5 = bf16[128,128]{1,0:T(8,128)(2,1)S(1)} collective-permute-done((bf16[128,128]{1,0:T(8,128)(2,1)S(1)}, bf16[128,128]{1,0:T(8,128)(2,1)S(1)}, u32[]{:S(2)}, u32[]{:S(2)}) %collective-permute-start.5) | collective-permute-done | bytes 32800 | tf_op jit(solution)/shard_map/ppermute | solution.py:584
  28.4 2.6 %hop.6.refs_3_ = bf16[256,1280]{1,0:T(8,128)(2,1)S(1)} custom-call(bf16[256,1280]{1,0:T(8,128)(2,1)S(1)} %collective-permute-done.4.refs_0_, bf16[256,1024]{1,0:T(8,128)(2,1)S(1)} %copy-done.1, bf16[1024,8192]{1,0:T(8,128)(2,1)} %refs_7_.1, bf16[128,128]{1,0:T(8,128)(2,1)S(1)} %add_convert_fusion.refs_3_.refs_0_, bf16[256,768]{1,0:T(8,128)(2,1)S(1)} %hold.1.refs_4_), custom_call_target="tpu_custom_call" | custom-call | flops 20000000000 | bytes 40000000 | tf_op jit(solution)/shard_map/hop/pallas_call | solution.py:354
  31.0 2.7 %collective-permute-start.9 = (bf16[256,1280]{1,0:T(8,128)(2,1)S(1)}, bf16[256,1280]{1,0:T(8,128)(2,1)S(1)}, u32[]{:S(2)}, u32[]{:S(2)}) collective-permute-start(bf16[256,1280]{1,0:T(8,128)(2,1)S(1)} %hop.6.refs_3_), channel_id=1, source_target_pairs={{0,2},{2,3},{3,1},{1,0},{4,6},{6,7},{7,5},{5,4},{8,10},{10,11},{11... | collective-permute-start | bytes 1966088 | tf_op jit(solution)/shard_map/ppermute | solution.py:551
  33.7 4.1 %collective-permute-start.8 = (bf16[128,128]{1,0:T(8,128)(2,1)S(1)}, bf16[128,128]{1,0:T(8,128)(2,1)S(1)}, u32[]{:S(2)}, u32[]{:S(2)}) collective-permute-start(bf16[128,128]{1,0:T(8,128)(2,1)S(1)} %add_convert_fusion.refs_3_.refs_0_), channel_id=1, source_target_pairs={{0,3},{3,0},{4,7},{7,4},{8,11},{11,8},{12,15},{15,12},{16,19},{19,... | collective-permute-start | bytes 98312 | tf_op jit(solution)/shard_map/ppermute | solution.py:564
  37.8 1.3 %collective-permute-start.7 = (bf16[128,128]{1,0:T(8,128)(2,1)S(1)}, bf16[128,128]{1,0:T(8,128)(2,1)S(1)}, u32[]{:S(2)}, u32[]{:S(2)}) collective-permute-start(bf16[128,128]{1,0:T(8,128)(2,1)S(1)} %add_convert_fusion.refs_3_.refs_0_), channel_id=1, source_target_pairs={{0,2},{3,1},{4,6},{7,5},{8,10},{11,9},{12,14},{15,13},{16,18},{19,... | collective-permute-start | bytes 98312 | tf_op jit(solution)/shard_map/ppermute | solution.py:563
  39.1 2.0 %hop.7 = bf16[256,768]{1,0:T(8,128)(2,1)S(1)} custom-call(bf16[256,768]{1,0:T(8,128)(2,1)S(1)} %collective-permute-done.3.refs_0_, bf16[256,1024]{1,0:T(8,128)(2,1)S(1)} %copy-done.1, bf16[1024,8192]{1,0:T(8,128)(2,1)} %refs_7_.1, bf16[256,1280]{1,0:T(8,128)(2,1)S(1)} %hop.6.refs_3_), custom_call_target="tpu_custom_call" | custom-call | flops 3000000000 | bytes 6000000 | tf_op jit(solution)/shard_map/hop/pallas_call | solution.py:354
  41.1 1.1 %collective-permute-start.6 = (bf16[256,768]{1,0:T(8,128)(2,1)S(1)}, bf16[256,768]{1,0:T(8,128)(2,1)S(1)}, u32[]{:S(2)}, u32[]{:S(2)}) collective-permute-start(bf16[256,768]{1,0:T(8,128)(2,1)S(1)} %hop.7), channel_id=1, source_target_pairs={{0,2},{2,3},{3,1},{1,0},{4,6},{6,7},{7,5},{5,4},{8,10},{10,11},{11... | collective-permute-start | bytes 1179656 | tf_op jit(solution)/shard_map/ppermute | solution.py:551
  42.2 11.1 %collective-permute-done.8.refs_4_.refs_2_ = bf16[128,128]{1,0:T(8,128)(2,1)S(1)} collective-permute-done((bf16[128,128]{1,0:T(8,128)(2,1)S(1)}, bf16[128,128]{1,0:T(8,128)(2,1)S(1)}, u32[]{:S(2)}, u32[]{:S(2)}) %collective-permute-start.8) | collective-permute-done | bytes 32800 | tf_op jit(solution)/shard_map/ppermute | solution.py:564
  53.4 2.6 %hop.8.refs_5_ = bf16[256,1280]{1,0:T(8,128)(2,1)S(1)} custom-call(bf16[256,1280]{1,0:T(8,128)(2,1)S(1)} %collective-permute-done.9.refs_0_, bf16[256,1024]{1,0:T(8,128)(2,1)S(1)} %copy-done.1, bf16[1024,8192]{1,0:T(8,128)(2,1)} %refs_7_.1, bf16[128,128]{1,0:T(8,128)(2,1)S(1)} %collective-permute-done.7.refs_3_.refs_1_, ...), custom_call_target="tpu_custom_call" | custom-call | flops 20000000000 | bytes 40000000 | tf_op jit(solution)/shard_map/hop/pallas_call | solution.py:354
  56.0 0.8 up.1
  56.9 1.6 %collective-permute-start.12 = (bf16[64,2048]{1,0:T(8,128)(2,1)S(1)}, bf16[64,2048]{1,0:T(8,128)(2,1)S(1)}, u32[]{:S(2)}, u32[]{:S(2)}) collective-permute-start(bf16[64,2048]{1,0:T(8,128)(2,1)S(1)} %get-tuple-element.30), channel_id=1, source_target_pairs={{0,8},{4,12},{8,0},{12,4},{1,9},{5,13},{9,1},{13,5},{2,10},{6,14},... | collective-permute-start | bytes 786440 | tf_op jit(solution)/shard_map/ppermute | solution.py:545
  58.7 2.3 %collective-permute-start.14 = (bf16[256,1280]{1,0:T(8,128)(2,1)S(1)}, bf16[256,1280]{1,0:T(8,128)(2,1)S(1)}, u32[]{:S(2)}, u32[]{:S(2)}) collective-permute-start(bf16[256,1280]{1,0:T(8,128)(2,1)S(1)} %hop.8.refs_5_), channel_id=1, source_target_pairs={{0,2},{2,3},{3,1},{1,0},{4,6},{6,7},{7,5},{5,4},{8,10},{10,11},{11... | collective-permute-start | bytes 1966088 | tf_op jit(solution)/shard_map/ppermute | solution.py:551
  61.0 2.1 %hop.9.refs_8_ = bf16[256,768]{1,0:T(8,128)(2,1)S(1)} custom-call(bf16[256,768]{1,0:T(8,128)(2,1)S(1)} %collective-permute-done.6.refs_0_, bf16[256,1024]{1,0:T(8,128)(2,1)S(1)} %copy-done.1, bf16[1024,8192]{1,0:T(8,128)(2,1)} %refs_7_.1, bf16[64,2048]{1,0:T(8,128)(2,1)S(1)} %get-tuple-element.28.refs_3_.refs_0_), custom_call_target="tpu_custom_call" | custom-call | tf_op jit(solution)/shard_map/hop/pallas_call | solution.py:354
  63.1 2.0 %collective-permute-start.10 = (bf16[256,768]{1,0:T(8,128)(2,1)S(1)}, bf16[256,768]{1,0:T(8,128)(2,1)S(1)}, u32[]{:S(2)}, u32[]{:S(2)}) collective-permute-start(bf16[256,768]{1,0:T(8,128)(2,1)S(1)} %hop.9.refs_8_), channel_id=1, source_target_pairs={{0,2},{2,3},{3,1},{1,0},{4,6},{6,7},{7,5},{5,4},{8,10},{10,11},{11... | collective-permute-start | bytes 1179656 | tf_op jit(solution)/shard_map/ppermute | solution.py:551
  65.0 1.0 %collective-permute-done.12.refs_2_ = bf16[64,2048]{1,0:T(8,128)(2,1)S(1)} collective-permute-done((bf16[64,2048]{1,0:T(8,128)(2,1)S(1)}, bf16[64,2048]{1,0:T(8,128)(2,1)S(1)}, u32[]{:S(2)}, u32[]{:S(2)}) %collective-permute-start.12) | collective-permute-done | bytes 262176 | tf_op jit(solution)/shard_map/ppermute | solution.py:545
  66.0 4.7 %collective-permute-done.13.refs_3_ = bf16[64,2048]{1,0:T(8,128)(2,1)S(1)} collective-permute-done((bf16[64,2048]{1,0:T(8,128)(2,1)S(1)}, bf16[64,2048]{1,0:T(8,128)(2,1)S(1)}, u32[]{:S(2)}, u32[]{:S(2)}) %collective-permute-start.13) | collective-permute-done | bytes 262176 | tf_op jit(solution)/shard_map/ppermute | solution.py:545
  70.8 4.5 %settle.1 = (f32[256,1280]{1,0:T(8,128)}, f32[256,768]{1,0:T(8,128)S(1)}) custom-call(bf16[64,2048]{1,0:T(8,128)(2,1)S(1)} %get-tuple-element.28.refs_3_.refs_0_, bf16[64,2048]{1,0:T(8,128)(2,1)S(1)} %collective-permute-done.11.refs_1_, bf16[64,2048]{1,0:T(8,128)(2,1)S(1)} %collective-permute-done.12.refs_2_, ...), custom_call_target="tpu_custom_call" | custom-call | flops 20000000000 | bytes 40000000 | tf_op jit(solution)/shard_map/settle/pallas_call | solution.py:460
  75.3 1.0 %collective-permute-done.14.arrived_ref = bf16[256,1280]{1,0:T(8,128)(2,1)S(1)} collective-permute-done((bf16[256,1280]{1,0:T(8,128)(2,1)S(1)}, bf16[256,1280]{1,0:T(8,128)(2,1)S(1)}, u32[]{:S(2)}, u32[]{:S(2)}) %collective-permute-start.14) | collective-permute-done | bytes 655392 | tf_op jit(solution)/shard_map/ppermute | solution.py:551
  76.3 1.3 %copy-done.3 = f32[256,1280]{1,0:T(8,128)S(1)} copy-done((f32[256,1280]{1,0:T(8,128)S(1)}, f32[256,1280]{1,0:T(8,128)}, u32[]{:S(2)}) %copy-start.3) | copy-done | bytes 1310744
  77.6 0.9 %finish.2.refs_0_ = bf16[256,2048]{1,0:T(8,128)(2,1)} custom-call(bf16[256,1280]{1,0:T(8,128)(2,1)S(1)} %collective-permute-done.14.arrived_ref, f32[256,1280]{1,0:T(8,128)S(1)} %copy-done.3), custom_call_target="tpu_custom_call" | custom-call | tf_op jit(solution)/shard_map/finish/pallas_call | solution.py:492
  78.5 5.6 %collective-permute-done.10.arrived_ref = bf16[256,768]{1,0:T(8,128)(2,1)S(1)} collective-permute-done((bf16[256,768]{1,0:T(8,128)(2,1)S(1)}, bf16[256,768]{1,0:T(8,128)(2,1)S(1)}, u32[]{:S(2)}, u32[]{:S(2)}) %collective-permute-start.10) | collective-permute-done | bytes 393248 | tf_op jit(solution)/shard_map/ppermute | solution.py:551
  84.1 0.8 finish.3
  (27 shorter events, 0.5 us)
Async XLA Ops:
  8.2 20.2 %collective-permute-start.4 = (bf16[256,1280]{1,0:T(8,128)(2,1)}, bf16[256,1280]{1,0:T(8,128)(2,1)S(1)}, u32[]{:S(2)}, u32[]{:S(2)}) collective-permute-start(bf16[256,1280]{1,0:T(8,128)(2,1)} %get-tuple-element.26), channel_id=1, source_target_pairs={{0,2},{2,3},{3,1},{1,0},{4,6},{6,7},{7,5},{5,4},{8,10},{10,11},{11... | collective-permute-start | bytes 1966088 | tf_op jit(solution)/shard_map/ppermute | solution.py:551
  12.3 5.0 %collective-permute-start = (bf16[64,1152]{1,0:T(8,128)(2,1)}, bf16[64,1152]{1,0:T(8,128)(2,1)S(1)}, u32[]{:S(2)}, u32[]{:S(2)}) collective-permute-start(bf16[64,1152]{1,0:T(8,128)(2,1)} %get-tuple-element.22), channel_id=1, source_target_pairs={{0,4},{4,0},{8,12},{12,8},{1,5},{5,1},{9,13},{13,9},{2,6},{6,2},{1... | collective-permute-start | bytes 442376 | tf_op jit(solution)/shard_map/ppermute | solution.py:545
  12.3 6.9 %collective-permute-start.1 = (bf16[64,1152]{1,0:T(8,128)(2,1)}, bf16[64,1152]{1,0:T(8,128)(2,1)S(1)}, u32[]{:S(2)}, u32[]{:S(2)}) collective-permute-start(bf16[64,1152]{1,0:T(8,128)(2,1)} %get-tuple-element.23), channel_id=1, source_target_pairs={{0,8},{4,12},{8,0},{12,4},{1,9},{5,13},{9,1},{13,5},{2,10},{6,14},... | collective-permute-start | bytes 442376 | tf_op jit(solution)/shard_map/ppermute | solution.py:545
  13.8 7.7 %collective-permute-start.2 = (bf16[64,1152]{1,0:T(8,128)(2,1)}, bf16[64,1152]{1,0:T(8,128)(2,1)S(1)}, u32[]{:S(2)}, u32[]{:S(2)}) collective-permute-start(bf16[64,1152]{1,0:T(8,128)(2,1)} %get-tuple-element.24), channel_id=1, source_target_pairs={{0,12},{4,8},{8,4},{12,0},{1,13},{5,9},{9,5},{13,1},{2,14},{6,10},... | collective-permute-start | bytes 442376 | tf_op jit(solution)/shard_map/ppermute | solution.py:545
  14.2 1.0 %copy-start = (bf16[256,1024]{1,0:T(8,128)(2,1)S(1)}, bf16[256,1024]{1,0:T(8,128)(2,1)}, u32[]{:S(2)}) copy-start(bf16[256,1024]{1,0:T(8,128)(2,1)} %get-tuple-element.20.refs_0_.refs_1_.refs_5_) | copy-start | bytes 1572868
  15.2 6.3 %copy-start.4 = (bf16[8,64,1024]{2,1,0:T(8,128)(2,1)S(1)}, bf16[8,64,1024]{2,1,0:T(8,128)(2,1)}, u32[]{:S(2)}) copy-start(bf16[8,64,1024]{2,1,0:T(8,128)(2,1)} %refs_4_.2) | copy-start | bytes 3145732
  15.2 6.3 %copy-start.5 = (bf16[64,1152]{1,0:T(8,128)(2,1)S(1)}, bf16[64,1152]{1,0:T(8,128)(2,1)}, u32[]{:S(2)}) copy-start(bf16[64,1152]{1,0:T(8,128)(2,1)} %get-tuple-element.21.refs_0_) | copy-start | bytes 442372
  17.3 11.1 %copy-start.1 = (bf16[256,1024]{1,0:T(8,128)(2,1)S(1)}, bf16[256,1024]{1,0:T(8,128)(2,1)}, u32[]{:S(2)}) copy-start(bf16[256,1024]{1,0:T(8,128)(2,1)} %get-tuple-element.20.refs_0_.refs_1_.refs_5_) | copy-start | bytes 1572868
  22.2 6.2 %collective-permute-start.5 = (bf16[128,128]{1,0:T(8,128)(2,1)S(1)}, bf16[128,128]{1,0:T(8,128)(2,1)S(1)}, u32[]{:S(2)}, u32[]{:S(2)}) collective-permute-start(bf16[128,128]{1,0:T(8,128)(2,1)S(1)} %get-tuple-element.25.refs_1_), channel_id=1, source_target_pairs={{0,1},{1,0},{2,3},{3,2},{4,5},{5,4},{6,7},{7,6},{8,9},{9,8},{10,11... | collective-permute-start | bytes 98312 | tf_op jit(solution)/shard_map/ppermute | solution.py:584
  22.3 16.8 %collective-permute-start.3 = (bf16[256,768]{1,0:T(8,128)(2,1)S(1)}, bf16[256,768]{1,0:T(8,128)(2,1)S(1)}, u32[]{:S(2)}, u32[]{:S(2)}) collective-permute-start(bf16[256,768]{1,0:T(8,128)(2,1)S(1)} %hold.1.refs_4_), channel_id=1, source_target_pairs={{0,2},{2,3},{3,1},{1,0},{4,6},{6,7},{7,5},{5,4},{8,10},{10,11},{11... | collective-permute-start | bytes 1179656 | tf_op jit(solution)/shard_map/ppermute | solution.py:551
  31.0 22.4 %collective-permute-start.9 = (bf16[256,1280]{1,0:T(8,128)(2,1)S(1)}, bf16[256,1280]{1,0:T(8,128)(2,1)S(1)}, u32[]{:S(2)}, u32[]{:S(2)}) collective-permute-start(bf16[256,1280]{1,0:T(8,128)(2,1)S(1)} %hop.6.refs_3_), channel_id=1, source_target_pairs={{0,2},{2,3},{3,1},{1,0},{4,6},{6,7},{7,5},{5,4},{8,10},{10,11},{11... | collective-permute-start | bytes 1966088 | tf_op jit(solution)/shard_map/ppermute | solution.py:551
  33.7 19.7 %collective-permute-start.8 = (bf16[128,128]{1,0:T(8,128)(2,1)S(1)}, bf16[128,128]{1,0:T(8,128)(2,1)S(1)}, u32[]{:S(2)}, u32[]{:S(2)}) collective-permute-start(bf16[128,128]{1,0:T(8,128)(2,1)S(1)} %add_convert_fusion.refs_3_.refs_0_), channel_id=1, source_target_pairs={{0,3},{3,0},{4,7},{7,4},{8,11},{11,8},{12,15},{15,12},{16,19},{19,... | collective-permute-start | bytes 98312 | tf_op jit(solution)/shard_map/ppermute | solution.py:564
  37.8 15.5 %collective-permute-start.7 = (bf16[128,128]{1,0:T(8,128)(2,1)S(1)}, bf16[128,128]{1,0:T(8,128)(2,1)S(1)}, u32[]{:S(2)}, u32[]{:S(2)}) collective-permute-start(bf16[128,128]{1,0:T(8,128)(2,1)S(1)} %add_convert_fusion.refs_3_.refs_0_), channel_id=1, source_target_pairs={{0,2},{3,1},{4,6},{7,5},{8,10},{11,9},{12,14},{15,13},{16,18},{19,... | collective-permute-start | bytes 98312 | tf_op jit(solution)/shard_map/ppermute | solution.py:563
  41.1 14.8 %copy-start.2 = (bf16[8,64,2048]{2,1,0:T(8,128)(2,1)S(1)}, bf16[8,64,2048]{2,1,0:T(8,128)(2,1)}, u32[]{:S(2)}) copy-start(bf16[8,64,2048]{2,1,0:T(8,128)(2,1)} %refs_4_.3) | copy-start | bytes 6291460
  41.1 19.9 %collective-permute-start.6 = (bf16[256,768]{1,0:T(8,128)(2,1)S(1)}, bf16[256,768]{1,0:T(8,128)(2,1)S(1)}, u32[]{:S(2)}, u32[]{:S(2)}) collective-permute-start(bf16[256,768]{1,0:T(8,128)(2,1)S(1)} %hop.7), channel_id=1, source_target_pairs={{0,2},{2,3},{3,1},{1,0},{4,6},{6,7},{7,5},{5,4},{8,10},{10,11},{11... | collective-permute-start | bytes 1179656 | tf_op jit(solution)/shard_map/ppermute | solution.py:551
  56.8 8.3 %collective-permute-start.11 = (bf16[64,2048]{1,0:T(8,128)(2,1)S(1)}, bf16[64,2048]{1,0:T(8,128)(2,1)S(1)}, u32[]{:S(2)}, u32[]{:S(2)}) collective-permute-start(bf16[64,2048]{1,0:T(8,128)(2,1)S(1)} %get-tuple-element.29), channel_id=1, source_target_pairs={{0,4},{4,0},{8,12},{12,8},{1,5},{5,1},{9,13},{13,9},{2,6},{6,2},{1... | collective-permute-start | bytes 786440 | tf_op jit(solution)/shard_map/ppermute | solution.py:545
  56.9 9.2 %collective-permute-start.12 = (bf16[64,2048]{1,0:T(8,128)(2,1)S(1)}, bf16[64,2048]{1,0:T(8,128)(2,1)S(1)}, u32[]{:S(2)}, u32[]{:S(2)}) collective-permute-start(bf16[64,2048]{1,0:T(8,128)(2,1)S(1)} %get-tuple-element.30), channel_id=1, source_target_pairs={{0,8},{4,12},{8,0},{12,4},{1,9},{5,13},{9,1},{13,5},{2,10},{6,14},... | collective-permute-start | bytes 786440 | tf_op jit(solution)/shard_map/ppermute | solution.py:545
  58.4 12.3 %collective-permute-start.13 = (bf16[64,2048]{1,0:T(8,128)(2,1)S(1)}, bf16[64,2048]{1,0:T(8,128)(2,1)S(1)}, u32[]{:S(2)}, u32[]{:S(2)}) collective-permute-start(bf16[64,2048]{1,0:T(8,128)(2,1)S(1)} %get-tuple-element.31), channel_id=1, source_target_pairs={{0,12},{4,8},{8,4},{12,0},{1,13},{5,9},{9,5},{13,1},{2,14},{6,10},... | collective-permute-start | bytes 786440 | tf_op jit(solution)/shard_map/ppermute | solution.py:545
  58.7 17.5 %collective-permute-start.14 = (bf16[256,1280]{1,0:T(8,128)(2,1)S(1)}, bf16[256,1280]{1,0:T(8,128)(2,1)S(1)}, u32[]{:S(2)}, u32[]{:S(2)}) collective-permute-start(bf16[256,1280]{1,0:T(8,128)(2,1)S(1)} %hop.8.refs_5_), channel_id=1, source_target_pairs={{0,2},{2,3},{3,1},{1,0},{4,6},{6,7},{7,5},{5,4},{8,10},{10,11},{11... | collective-permute-start | bytes 1966088 | tf_op jit(solution)/shard_map/ppermute | solution.py:551
  61.0 9.7 %copy-start.6 = (bf16[256,2048]{1,0:T(8,128)(2,1)S(1)}, bf16[256,2048]{1,0:T(8,128)(2,1)}, u32[]{:S(2)}) copy-start(bf16[256,2048]{1,0:T(8,128)(2,1)} %refs_6_.1) | copy-start | bytes 3145732
  61.0 9.7 %copy-start.7 = (bf16[256,256]{1,0:T(8,128)(2,1)S(1)}, bf16[256,256]{1,0:T(8,128)(2,1)}, u32[]{:S(2)}) copy-start(bf16[256,256]{1,0:T(8,128)(2,1)} %get-tuple-element.32.refs_4_) | copy-start | bytes 393220
  63.1 21.1 %collective-permute-start.10 = (bf16[256,768]{1,0:T(8,128)(2,1)S(1)}, bf16[256,768]{1,0:T(8,128)(2,1)S(1)}, u32[]{:S(2)}, u32[]{:S(2)}) collective-permute-start(bf16[256,768]{1,0:T(8,128)(2,1)S(1)} %hop.9.refs_8_), channel_id=1, source_target_pairs={{0,2},{2,3},{3,1},{1,0},{4,6},{6,7},{7,5},{5,4},{8,10},{10,11},{11... | collective-permute-start | bytes 1179656 | tf_op jit(solution)/shard_map/ppermute | solution.py:551
  76.3 1.3 %copy-start.3 = (f32[256,1280]{1,0:T(8,128)S(1)}, f32[256,1280]{1,0:T(8,128)}, u32[]{:S(2)}) copy-start(f32[256,1280]{1,0:T(8,128)} %get-tuple-element.34.settled_ref) | copy-start | bytes 3932164

commit v14 on v13

--- a/solution.py
+++ b/solution.py
@@ -21,7 +21,7 @@
 VMEM = pl.BlockSpec(memory_space=pltpu.VMEM)
 ANY = pl.BlockSpec(memory_space=pl.ANY)
 LONG = pl.CostEstimate(flops=20 * 10**9, transcendentals=0, bytes_accessed=40 * 10**6)
-MEDIUM = pl.CostEstimate(flops=3 * 10**9, transcendentals=0, bytes_accessed=6 * 10**6)
+MEDIUM = pl.CostEstimate(flops=4 * 10**9, transcendentals=0, bytes_accessed=8 * 10**6)
 PARAMS = pltpu.CompilerParams(vmem_limit_bytes=VMEM_LIMIT)
 
 
@@ -464,7 +464,7 @@
         out_shape=[jax.ShapeDtypeStruct((rows, chunk), jnp.float32) for _, chunk in chains],
         scratch_shapes=Weights.scratch(weight.shape[0], width),
         compiler_params=PARAMS,
-        cost_estimate=LONG,
+        cost_estimate=MEDIUM,
         name="settle",
     )(*returned, chosen, attended, residual, weight, *after)
 
@@ -588,7 +588,7 @@
     for step in range(2, count - 1):
         for chain in range(2):
             if (step, chain) == (2, 0):
-                next_hop(step, chain, after=rank_sums[1:], cost=LONG)
+                next_hop(step, chain, after=(), cost=LONG)
                 deltas = up(rank_sums, inside, slot_up_weight, after=[travelling[0]])
                 returned = exchange(deltas)
             else:

time: 85.3 us -> 83.2 us (0.975)
  waiting for transfers between devices: 31.9 us -> 27.1 us
  starting transfers between devices: 23.3 us -> 25.9 us
    ppermute x1, waiting for transfers between devices: 11.1 us -> 0.01 us  [pair_sums(): other = lax.ppermute(x, 'tensor', far)]
    ppermute x6, waiting for transfers between devices: 6.64 us -> 13.2 us  [forward(): return lax.ppermute(x, 'tensor', ring)]
    ppermute x6, starting transfers between devices: 14 us -> 16.6 us  [forward(): return lax.ppermute(x, 'tensor', ring)]
  transfers between devices with their start and end apart: 15 -> 15, of which waited for: 8 -> 8; matrix products, arithmetic and copies ran while one was open for 0% -> 0% of each run, Pallas kernels for 21% -> 22%
where the time goes in v14:
time: 83.2 us; the launch traced here: 82.8 us
  Pallas kernels  27.2 us (33%)
  waiting for transfers between devices  27.1 us (33%)
  starting transfers between devices  25.9 us (31%)
  local copies, waits for them, and re-layouts  2.38 us (3%)
    ppermute x6, starting transfers between devices, forward(): return lax.ppermute(x, 'tensor', ring)  16.6 us
    ppermute x6, waiting for transfers between devices, forward(): return lax.ppermute(x, 'tensor', ring)  13.2 us
    pallas_call x5, Pallas kernels, hop(): pl.pallas_call(functools.partial(hop_kernel, step, block, start, arriving...  11.3 us
    ppermute x6, waiting for transfers between devices, exchange(): lax.ppermute(blocks[r], 'dp', [(i, i ^ r) for i in range(replicas)])  9.72 us
    pallas_call x1, Pallas kernels, attend(): pl.pallas_call(functools.partial(attend_kernel, heads, kv, cache, steps,...  8.24 us
    pallas_call x1, Pallas kernels, settle(): pl.pallas_call(functools.partial(settle_kernel, step, replicas, len(after...  4.52 us
    ppermute x1, waiting for transfers between devices, per_device(): lax.ppermute(mid, 'tensor', [(i, i ^ 1) for i in range(count)])  4.18 us
    ppermute x1, starting transfers between devices, pair_sums(): other = lax.ppermute(x, 'tensor', far)  4.12 us
  transfers between devices with their start and end apart: 15, of which 8 were waited for; matrix products, arithmetic and copies ran while one was open for 0% of the time, Pallas kernels for 22%

profile of v14, /device:TPU:0, one launch (start us, length us, event | category | flops | bytes accessed | tf_op | source)
XLA Modules:
  0.0 82.8 jit_solution(806012326604070425)
XLA Ops:
  0.0 8.2 %attend.1 = (bf16[256,1024]{1,0:T(8,128)(2,1)}, bf16[256,1280]{1,0:T(8,128)(2,1)}, bf16[256,256]{1,0:T(8,128)(2,1)}, bf16[64,1152]{1,0:T(8,128)(2,1)}, bf16[64,1...) custom-call(s32[1,256]{1,0:T(1,128)} %bitcast.13, s32[1,256]{1,0:T(1,128)} %bitcast.14, ...), custom_call_target="tpu_custom_call" | custom-call | tf_op jit(solution)/shard_map/attend/pallas_call | solution.py:304
  8.2 4.1 %collective-permute-start.4 = (bf16[256,1280]{1,0:T(8,128)(2,1)}, bf16[256,1280]{1,0:T(8,128)(2,1)S(1)}, u32[]{:S(2)}, u32[]{:S(2)}) collective-permute-start(bf16[256,1280]{1,0:T(8,128)(2,1)} %get-tuple-element.26), channel_id=1, source_target_pairs={{0,2},{2,3},{3,1},{1,0},{4,6},{6,7},{7,5},{5,4},{8,10},{10,11},{11... | collective-permute-start | bytes 1966088 | tf_op jit(solution)/shard_map/ppermute | solution.py:551
  12.3 1.5 %collective-permute-start.1 = (bf16[64,1152]{1,0:T(8,128)(2,1)}, bf16[64,1152]{1,0:T(8,128)(2,1)S(1)}, u32[]{:S(2)}, u32[]{:S(2)}) collective-permute-start(bf16[64,1152]{1,0:T(8,128)(2,1)} %get-tuple-element.23), channel_id=1, source_target_pairs={{0,8},{4,12},{8,0},{12,4},{1,9},{5,13},{9,1},{13,5},{2,10},{6,14},... | collective-permute-start | bytes 442376 | tf_op jit(solution)/shard_map/ppermute | solution.py:545
  13.8 0.4 collective-permute-start.2
  14.2 1.0 %copy-done = bf16[256,1024]{1,0:T(8,128)(2,1)S(1)} copy-done((bf16[256,1024]{1,0:T(8,128)(2,1)S(1)}, bf16[256,1024]{1,0:T(8,128)(2,1)}, u32[]{:S(2)}) %copy-start) | copy-done | bytes 524312
  15.2 2.1 %hop.5.refs_5_.refs_0_ = bf16[256,768]{1,0:T(8,128)(2,1)S(1)} custom-call(bf16[256,1024]{1,0:T(8,128)(2,1)S(1)} %copy-done, bf16[1024,8192]{1,0:T(8,128)(2,1)} %refs_7_.1), custom_call_target="tpu_custom_call" | custom-call | tf_op jit(solution)/shard_map/hop/pallas_call | solution.py:354
  17.3 1.9 %collective-permute-done.1.refs_2_ = bf16[64,1152]{1,0:T(8,128)(2,1)S(1)} collective-permute-done((bf16[64,1152]{1,0:T(8,128)(2,1)}, bf16[64,1152]{1,0:T(8,128)(2,1)S(1)}, u32[]{:S(2)}, u32[]{:S(2)}) %collective-permute-start.1) | collective-permute-done | bytes 147488 | tf_op jit(solution)/shard_map/ppermute | solution.py:545
  19.2 2.4 %collective-permute-done.2.refs_3_ = bf16[64,1152]{1,0:T(8,128)(2,1)S(1)} collective-permute-done((bf16[64,1152]{1,0:T(8,128)(2,1)}, bf16[64,1152]{1,0:T(8,128)(2,1)S(1)}, u32[]{:S(2)}, u32[]{:S(2)}) %collective-permute-start.2) | collective-permute-done | bytes 147488 | tf_op jit(solution)/shard_map/ppermute | solution.py:545
  21.6 0.6 down.1
  22.3 1.9 %collective-permute-start.3 = (bf16[256,768]{1,0:T(8,128)(2,1)S(1)}, bf16[256,768]{1,0:T(8,128)(2,1)S(1)}, u32[]{:S(2)}, u32[]{:S(2)}) collective-permute-start(bf16[256,768]{1,0:T(8,128)(2,1)S(1)} %hold.1.refs_4_), channel_id=1, source_target_pairs={{0,2},{2,3},{3,1},{1,0},{4,6},{6,7},{7,5},{5,4},{8,10},{10,11},{11... | collective-permute-start | bytes 1179656 | tf_op jit(solution)/shard_map/ppermute | solution.py:551
  24.2 4.2 %collective-permute-done.5 = bf16[128,128]{1,0:T(8,128)(2,1)S(1)} collective-permute-done((bf16[128,128]{1,0:T(8,128)(2,1)S(1)}, bf16[128,128]{1,0:T(8,128)(2,1)S(1)}, u32[]{:S(2)}, u32[]{:S(2)}) %collective-permute-start.5) | collective-permute-done | bytes 32800 | tf_op jit(solution)/shard_map/ppermute | solution.py:584
  28.4 2.6 %hop.6.refs_3_ = bf16[256,1280]{1,0:T(8,128)(2,1)S(1)} custom-call(bf16[256,1280]{1,0:T(8,128)(2,1)S(1)} %collective-permute-done.4.refs_0_, bf16[256,1024]{1,0:T(8,128)(2,1)S(1)} %copy-done.1, bf16[1024,8192]{1,0:T(8,128)(2,1)} %refs_7_.1, bf16[128,128]{1,0:T(8,128)(2,1)S(1)} %add_convert_fusion.refs_3_.refs_0_, bf16[256,768]{1,0:T(8,128)(2,1)S(1)} %hold.1.refs_4_), custom_call_target="tpu_custom_call" | custom-call | flops 20000000000 | bytes 40000000 | tf_op jit(solution)/shard_map/hop/pallas_call | solution.py:354
  31.0 2.7 %collective-permute-start.9 = (bf16[256,1280]{1,0:T(8,128)(2,1)S(1)}, bf16[256,1280]{1,0:T(8,128)(2,1)S(1)}, u32[]{:S(2)}, u32[]{:S(2)}) collective-permute-start(bf16[256,1280]{1,0:T(8,128)(2,1)S(1)} %hop.6.refs_3_), channel_id=1, source_target_pairs={{0,2},{2,3},{3,1},{1,0},{4,6},{6,7},{7,5},{5,4},{8,10},{10,11},{11... | collective-permute-start | bytes 1966088 | tf_op jit(solution)/shard_map/ppermute | solution.py:551
  33.7 4.1 %collective-permute-start.8 = (bf16[128,128]{1,0:T(8,128)(2,1)S(1)}, bf16[128,128]{1,0:T(8,128)(2,1)S(1)}, u32[]{:S(2)}, u32[]{:S(2)}) collective-permute-start(bf16[128,128]{1,0:T(8,128)(2,1)S(1)} %add_convert_fusion.refs_3_.refs_0_), channel_id=1, source_target_pairs={{0,3},{3,0},{4,7},{7,4},{8,11},{11,8},{12,15},{15,12},{16,19},{19,... | collective-permute-start | bytes 98312 | tf_op jit(solution)/shard_map/ppermute | solution.py:564
  37.8 1.3 %collective-permute-start.7 = (bf16[128,128]{1,0:T(8,128)(2,1)S(1)}, bf16[128,128]{1,0:T(8,128)(2,1)S(1)}, u32[]{:S(2)}, u32[]{:S(2)}) collective-permute-start(bf16[128,128]{1,0:T(8,128)(2,1)S(1)} %add_convert_fusion.refs_3_.refs_0_), channel_id=1, source_target_pairs={{0,2},{3,1},{4,6},{7,5},{8,10},{11,9},{12,14},{15,13},{16,18},{19,... | collective-permute-start | bytes 98312 | tf_op jit(solution)/shard_map/ppermute | solution.py:563
  39.1 2.0 %hop.7 = bf16[256,768]{1,0:T(8,128)(2,1)S(1)} custom-call(bf16[256,768]{1,0:T(8,128)(2,1)S(1)} %collective-permute-done.3.refs_0_, bf16[256,1024]{1,0:T(8,128)(2,1)S(1)} %copy-done.1, bf16[1024,8192]{1,0:T(8,128)(2,1)} %refs_7_.1, bf16[256,1280]{1,0:T(8,128)(2,1)S(1)} %hop.6.refs_3_), custom_call_target="tpu_custom_call" | custom-call | flops 4000000000 | bytes 8000000 | tf_op jit(solution)/shard_map/hop/pallas_call | solution.py:354
  41.1 1.1 %collective-permute-start.6 = (bf16[256,768]{1,0:T(8,128)(2,1)S(1)}, bf16[256,768]{1,0:T(8,128)(2,1)S(1)}, u32[]{:S(2)}, u32[]{:S(2)}) collective-permute-start(bf16[256,768]{1,0:T(8,128)(2,1)S(1)} %hop.7), channel_id=1, source_target_pairs={{0,2},{2,3},{3,1},{1,0},{4,6},{6,7},{7,5},{5,4},{8,10},{10,11},{11... | collective-permute-start | bytes 1179656 | tf_op jit(solution)/shard_map/ppermute | solution.py:551
  42.2 8.6 %collective-permute-done.9.refs_0_ = bf16[256,1280]{1,0:T(8,128)(2,1)S(1)} collective-permute-done((bf16[256,1280]{1,0:T(8,128)(2,1)S(1)}, bf16[256,1280]{1,0:T(8,128)(2,1)S(1)}, u32[]{:S(2)}, u32[]{:S(2)}) %collective-permute-start.9) | collective-permute-done | bytes 655392 | tf_op jit(solution)/shard_map/ppermute | solution.py:551
  50.9 2.6 %hop.8.refs_5_ = bf16[256,1280]{1,0:T(8,128)(2,1)S(1)} custom-call(bf16[256,1280]{1,0:T(8,128)(2,1)S(1)} %collective-permute-done.9.refs_0_, bf16[256,1024]{1,0:T(8,128)(2,1)S(1)} %copy-done.1, bf16[1024,8192]{1,0:T(8,128)(2,1)} %refs_7_.1), custom_call_target="tpu_custom_call" | custom-call | flops 20000000000 | bytes 40000000 | tf_op jit(solution)/shard_map/hop/pallas_call | solution.py:354
  53.4 3.4 %collective-permute-start.14 = (bf16[256,1280]{1,0:T(8,128)(2,1)S(1)}, bf16[256,1280]{1,0:T(8,128)(2,1)S(1)}, u32[]{:S(2)}, u32[]{:S(2)}) collective-permute-start(bf16[256,1280]{1,0:T(8,128)(2,1)S(1)} %hop.8.refs_5_), channel_id=1, source_target_pairs={{0,2},{2,3},{3,1},{1,0},{4,6},{6,7},{7,5},{5,4},{8,10},{10,11},{11... | collective-permute-start | bytes 1966088 | tf_op jit(solution)/shard_map/ppermute | solution.py:551
  56.9 0.8 up.1
  57.8 1.6 %collective-permute-start.12 = (bf16[64,2048]{1,0:T(8,128)(2,1)S(1)}, bf16[64,2048]{1,0:T(8,128)(2,1)S(1)}, u32[]{:S(2)}, u32[]{:S(2)}) collective-permute-start(bf16[64,2048]{1,0:T(8,128)(2,1)S(1)} %get-tuple-element.30), channel_id=1, source_target_pairs={{0,8},{4,12},{8,0},{12,4},{1,9},{5,13},{9,1},{13,5},{2,10},{6,14},... | collective-permute-start | bytes 786440 | tf_op jit(solution)/shard_map/ppermute | solution.py:545
  59.7 1.0 %collective-permute-done.6.refs_0_ = bf16[256,768]{1,0:T(8,128)(2,1)S(1)} collective-permute-done((bf16[256,768]{1,0:T(8,128)(2,1)S(1)}, bf16[256,768]{1,0:T(8,128)(2,1)S(1)}, u32[]{:S(2)}, u32[]{:S(2)}) %collective-permute-start.6) | collective-permute-done | bytes 393248 | tf_op jit(solution)/shard_map/ppermute | solution.py:551
  60.7 2.1 %hop.9.refs_8_ = bf16[256,768]{1,0:T(8,128)(2,1)S(1)} custom-call(bf16[256,768]{1,0:T(8,128)(2,1)S(1)} %collective-permute-done.6.refs_0_, bf16[256,1024]{1,0:T(8,128)(2,1)S(1)} %copy-done.1, bf16[1024,8192]{1,0:T(8,128)(2,1)} %refs_7_.1, bf16[64,2048]{1,0:T(8,128)(2,1)S(1)} %get-tuple-element.28.refs_3_.refs_0_), custom_call_target="tpu_custom_call" | custom-call | tf_op jit(solution)/shard_map/hop/pallas_call | solution.py:354
  62.8 3.4 %collective-permute-start.10 = (bf16[256,768]{1,0:T(8,128)(2,1)S(1)}, bf16[256,768]{1,0:T(8,128)(2,1)S(1)}, u32[]{:S(2)}, u32[]{:S(2)}) collective-permute-start(bf16[256,768]{1,0:T(8,128)(2,1)S(1)} %hop.9.refs_8_), channel_id=1, source_target_pairs={{0,2},{2,3},{3,1},{1,0},{4,6},{6,7},{7,5},{5,4},{8,10},{10,11},{11... | collective-permute-start | bytes 1179656 | tf_op jit(solution)/shard_map/ppermute | solution.py:551
  66.2 0.8 collective-permute-done.12.refs_2_
  67.0 4.7 %collective-permute-done.13.refs_3_ = bf16[64,2048]{1,0:T(8,128)(2,1)S(1)} collective-permute-done((bf16[64,2048]{1,0:T(8,128)(2,1)S(1)}, bf16[64,2048]{1,0:T(8,128)(2,1)S(1)}, u32[]{:S(2)}, u32[]{:S(2)}) %collective-permute-start.13) | collective-permute-done | bytes 262176 | tf_op jit(solution)/shard_map/ppermute | solution.py:545
  71.7 4.5 %settle.1 = (f32[256,1280]{1,0:T(8,128)}, f32[256,768]{1,0:T(8,128)S(1)}) custom-call(bf16[64,2048]{1,0:T(8,128)(2,1)S(1)} %get-tuple-element.28.refs_3_.refs_0_, bf16[64,2048]{1,0:T(8,128)(2,1)S(1)} %collective-permute-done.11.refs_1_, bf16[64,2048]{1,0:T(8,128)(2,1)S(1)} %collective-permute-done.12.refs_2_, ...), custom_call_target="tpu_custom_call" | custom-call | flops 4000000000 | bytes 8000000 | tf_op jit(solution)/shard_map/settle/pallas_call | solution.py:460
  76.2 1.3 %copy-done.3 = f32[256,1280]{1,0:T(8,128)S(1)} copy-done((f32[256,1280]{1,0:T(8,128)S(1)}, f32[256,1280]{1,0:T(8,128)}, u32[]{:S(2)}) %copy-start.3) | copy-done | bytes 1310744
  77.5 0.9 %finish.2.refs_0_ = bf16[256,2048]{1,0:T(8,128)(2,1)} custom-call(bf16[256,1280]{1,0:T(8,128)(2,1)S(1)} %collective-permute-done.14.arrived_ref, f32[256,1280]{1,0:T(8,128)S(1)} %copy-done.3), custom_call_target="tpu_custom_call" | custom-call | tf_op jit(solution)/shard_map/finish/pallas_call | solution.py:492
  78.4 3.6 %collective-permute-done.10.arrived_ref = bf16[256,768]{1,0:T(8,128)(2,1)S(1)} collective-permute-done((bf16[256,768]{1,0:T(8,128)(2,1)S(1)}, bf16[256,768]{1,0:T(8,128)(2,1)S(1)}, u32[]{:S(2)}, u32[]{:S(2)}) %collective-permute-start.10) | collective-permute-done | bytes 393248 | tf_op jit(solution)/shard_map/ppermute | solution.py:551
  82.0 0.8 finish.3
  (27 shorter events, 0.5 us)
Async XLA Ops:
  8.2 20.2 %collective-permute-start.4 = (bf16[256,1280]{1,0:T(8,128)(2,1)}, bf16[256,1280]{1,0:T(8,128)(2,1)S(1)}, u32[]{:S(2)}, u32[]{:S(2)}) collective-permute-start(bf16[256,1280]{1,0:T(8,128)(2,1)} %get-tuple-element.26), channel_id=1, source_target_pairs={{0,2},{2,3},{3,1},{1,0},{4,6},{6,7},{7,5},{5,4},{8,10},{10,11},{11... | collective-permute-start | bytes 1966088 | tf_op jit(solution)/shard_map/ppermute | solution.py:551
  12.3 5.0 %collective-permute-start = (bf16[64,1152]{1,0:T(8,128)(2,1)}, bf16[64,1152]{1,0:T(8,128)(2,1)S(1)}, u32[]{:S(2)}, u32[]{:S(2)}) collective-permute-start(bf16[64,1152]{1,0:T(8,128)(2,1)} %get-tuple-element.22), channel_id=1, source_target_pairs={{0,4},{4,0},{8,12},{12,8},{1,5},{5,1},{9,13},{13,9},{2,6},{6,2},{1... | collective-permute-start | bytes 442376 | tf_op jit(solution)/shard_map/ppermute | solution.py:545
  12.3 6.9 %collective-permute-start.1 = (bf16[64,1152]{1,0:T(8,128)(2,1)}, bf16[64,1152]{1,0:T(8,128)(2,1)S(1)}, u32[]{:S(2)}, u32[]{:S(2)}) collective-permute-start(bf16[64,1152]{1,0:T(8,128)(2,1)} %get-tuple-element.23), channel_id=1, source_target_pairs={{0,8},{4,12},{8,0},{12,4},{1,9},{5,13},{9,1},{13,5},{2,10},{6,14},... | collective-permute-start | bytes 442376 | tf_op jit(solution)/shard_map/ppermute | solution.py:545
  13.8 7.7 %collective-permute-start.2 = (bf16[64,1152]{1,0:T(8,128)(2,1)}, bf16[64,1152]{1,0:T(8,128)(2,1)S(1)}, u32[]{:S(2)}, u32[]{:S(2)}) collective-permute-start(bf16[64,1152]{1,0:T(8,128)(2,1)} %get-tuple-element.24), channel_id=1, source_target_pairs={{0,12},{4,8},{8,4},{12,0},{1,13},{5,9},{9,5},{13,1},{2,14},{6,10},... | collective-permute-start | bytes 442376 | tf_op jit(solution)/shard_map/ppermute | solution.py:545
  14.2 1.0 %copy-start = (bf16[256,1024]{1,0:T(8,128)(2,1)S(1)}, bf16[256,1024]{1,0:T(8,128)(2,1)}, u32[]{:S(2)}) copy-start(bf16[256,1024]{1,0:T(8,128)(2,1)} %get-tuple-element.20.refs_0_.refs_1_.refs_5_) | copy-start | bytes 1572868
  15.2 6.3 %copy-start.5 = (bf16[8,64,1024]{2,1,0:T(8,128)(2,1)S(1)}, bf16[8,64,1024]{2,1,0:T(8,128)(2,1)}, u32[]{:S(2)}) copy-start(bf16[8,64,1024]{2,1,0:T(8,128)(2,1)} %refs_4_.2) | copy-start | bytes 3145732
  15.2 6.3 %copy-start.6 = (bf16[64,1152]{1,0:T(8,128)(2,1)S(1)}, bf16[64,1152]{1,0:T(8,128)(2,1)}, u32[]{:S(2)}) copy-start(bf16[64,1152]{1,0:T(8,128)(2,1)} %get-tuple-element.21.refs_0_) | copy-start | bytes 442372
  17.3 11.1 %copy-start.1 = (bf16[256,1024]{1,0:T(8,128)(2,1)S(1)}, bf16[256,1024]{1,0:T(8,128)(2,1)}, u32[]{:S(2)}) copy-start(bf16[256,1024]{1,0:T(8,128)(2,1)} %get-tuple-element.20.refs_0_.refs_1_.refs_5_) | copy-start | bytes 1572868
  22.2 6.2 %collective-permute-start.5 = (bf16[128,128]{1,0:T(8,128)(2,1)S(1)}, bf16[128,128]{1,0:T(8,128)(2,1)S(1)}, u32[]{:S(2)}, u32[]{:S(2)}) collective-permute-start(bf16[128,128]{1,0:T(8,128)(2,1)S(1)} %get-tuple-element.25.refs_1_), channel_id=1, source_target_pairs={{0,1},{1,0},{2,3},{3,2},{4,5},{5,4},{6,7},{7,6},{8,9},{9,8},{10,11... | collective-permute-start | bytes 98312 | tf_op jit(solution)/shard_map/ppermute | solution.py:584
  22.3 16.8 %collective-permute-start.3 = (bf16[256,768]{1,0:T(8,128)(2,1)S(1)}, bf16[256,768]{1,0:T(8,128)(2,1)S(1)}, u32[]{:S(2)}, u32[]{:S(2)}) collective-permute-start(bf16[256,768]{1,0:T(8,128)(2,1)S(1)} %hold.1.refs_4_), channel_id=1, source_target_pairs={{0,2},{2,3},{3,1},{1,0},{4,6},{6,7},{7,5},{5,4},{8,10},{10,11},{11... | collective-permute-start | bytes 1179656 | tf_op jit(solution)/shard_map/ppermute | solution.py:551
  31.0 19.8 %collective-permute-start.9 = (bf16[256,1280]{1,0:T(8,128)(2,1)S(1)}, bf16[256,1280]{1,0:T(8,128)(2,1)S(1)}, u32[]{:S(2)}, u32[]{:S(2)}) collective-permute-start(bf16[256,1280]{1,0:T(8,128)(2,1)S(1)} %hop.6.refs_3_), channel_id=1, source_target_pairs={{0,2},{2,3},{3,1},{1,0},{4,6},{6,7},{7,5},{5,4},{8,10},{10,11},{11... | collective-permute-start | bytes 1966088 | tf_op jit(solution)/shard_map/ppermute | solution.py:551
  33.7 23.2 %collective-permute-start.8 = (bf16[128,128]{1,0:T(8,128)(2,1)S(1)}, bf16[128,128]{1,0:T(8,128)(2,1)S(1)}, u32[]{:S(2)}, u32[]{:S(2)}) collective-permute-start(bf16[128,128]{1,0:T(8,128)(2,1)S(1)} %add_convert_fusion.refs_3_.refs_0_), channel_id=1, source_target_pairs={{0,3},{3,0},{4,7},{7,4},{8,11},{11,8},{12,15},{15,12},{16,19},{19,... | collective-permute-start | bytes 98312 | tf_op jit(solution)/shard_map/ppermute | solution.py:564
  37.8 19.1 %collective-permute-start.7 = (bf16[128,128]{1,0:T(8,128)(2,1)S(1)}, bf16[128,128]{1,0:T(8,128)(2,1)S(1)}, u32[]{:S(2)}, u32[]{:S(2)}) collective-permute-start(bf16[128,128]{1,0:T(8,128)(2,1)S(1)} %add_convert_fusion.refs_3_.refs_0_), channel_id=1, source_target_pairs={{0,2},{3,1},{4,6},{7,5},{8,10},{11,9},{12,14},{15,13},{16,18},{19,... | collective-permute-start | bytes 98312 | tf_op jit(solution)/shard_map/ppermute | solution.py:563
  41.1 15.7 %copy-start.2 = (bf16[8,64,2048]{2,1,0:T(8,128)(2,1)S(1)}, bf16[8,64,2048]{2,1,0:T(8,128)(2,1)}, u32[]{:S(2)}) copy-start(bf16[8,64,2048]{2,1,0:T(8,128)(2,1)} %refs_4_.3) | copy-start | bytes 6291460
  41.1 19.5 %collective-permute-start.6 = (bf16[256,768]{1,0:T(8,128)(2,1)S(1)}, bf16[256,768]{1,0:T(8,128)(2,1)S(1)}, u32[]{:S(2)}, u32[]{:S(2)}) collective-permute-start(bf16[256,768]{1,0:T(8,128)(2,1)S(1)} %hop.7), channel_id=1, source_target_pairs={{0,2},{2,3},{3,1},{1,0},{4,6},{6,7},{7,5},{5,4},{8,10},{10,11},{11... | collective-permute-start | bytes 1179656 | tf_op jit(solution)/shard_map/ppermute | solution.py:551
  53.4 22.8 %collective-permute-start.14 = (bf16[256,1280]{1,0:T(8,128)(2,1)S(1)}, bf16[256,1280]{1,0:T(8,128)(2,1)S(1)}, u32[]{:S(2)}, u32[]{:S(2)}) collective-permute-start(bf16[256,1280]{1,0:T(8,128)(2,1)S(1)} %hop.8.refs_5_), channel_id=1, source_target_pairs={{0,2},{2,3},{3,1},{1,0},{4,6},{6,7},{7,5},{5,4},{8,10},{10,11},{11... | collective-permute-start | bytes 1966088 | tf_op jit(solution)/shard_map/ppermute | solution.py:551
  57.7 8.5 %collective-permute-start.11 = (bf16[64,2048]{1,0:T(8,128)(2,1)S(1)}, bf16[64,2048]{1,0:T(8,128)(2,1)S(1)}, u32[]{:S(2)}, u32[]{:S(2)}) collective-permute-start(bf16[64,2048]{1,0:T(8,128)(2,1)S(1)} %get-tuple-element.29), channel_id=1, source_target_pairs={{0,4},{4,0},{8,12},{12,8},{1,5},{5,1},{9,13},{13,9},{2,6},{6,2},{1... | collective-permute-start | bytes 786440 | tf_op jit(solution)/shard_map/ppermute | solution.py:545
  57.8 9.2 %collective-permute-start.12 = (bf16[64,2048]{1,0:T(8,128)(2,1)S(1)}, bf16[64,2048]{1,0:T(8,128)(2,1)S(1)}, u32[]{:S(2)}, u32[]{:S(2)}) collective-permute-start(bf16[64,2048]{1,0:T(8,128)(2,1)S(1)} %get-tuple-element.30), channel_id=1, source_target_pairs={{0,8},{4,12},{8,0},{12,4},{1,9},{5,13},{9,1},{13,5},{2,10},{6,14},... | collective-permute-start | bytes 786440 | tf_op jit(solution)/shard_map/ppermute | solution.py:545
  59.3 12.3 %collective-permute-start.13 = (bf16[64,2048]{1,0:T(8,128)(2,1)S(1)}, bf16[64,2048]{1,0:T(8,128)(2,1)S(1)}, u32[]{:S(2)}, u32[]{:S(2)}) collective-permute-start(bf16[64,2048]{1,0:T(8,128)(2,1)S(1)} %get-tuple-element.31), channel_id=1, source_target_pairs={{0,12},{4,8},{8,4},{12,0},{1,13},{5,9},{9,5},{13,1},{2,14},{6,10},... | collective-permute-start | bytes 786440 | tf_op jit(solution)/shard_map/ppermute | solution.py:545
  60.7 11.0 %copy-start.4 = (bf16[256,2048]{1,0:T(8,128)(2,1)S(1)}, bf16[256,2048]{1,0:T(8,128)(2,1)}, u32[]{:S(2)}) copy-start(bf16[256,2048]{1,0:T(8,128)(2,1)} %refs_6_.1) | copy-start | bytes 3145732
  60.7 11.0 %copy-start.7 = (bf16[256,256]{1,0:T(8,128)(2,1)S(1)}, bf16[256,256]{1,0:T(8,128)(2,1)}, u32[]{:S(2)}) copy-start(bf16[256,256]{1,0:T(8,128)(2,1)} %get-tuple-element.32.refs_4_) | copy-start | bytes 393220
  62.8 19.2 %collective-permute-start.10 = (bf16[256,768]{1,0:T(8,128)(2,1)S(1)}, bf16[256,768]{1,0:T(8,128)(2,1)S(1)}, u32[]{:S(2)}, u32[]{:S(2)}) collective-permute-start(bf16[256,768]{1,0:T(8,128)(2,1)S(1)} %hop.9.refs_8_), channel_id=1, source_target_pairs={{0,2},{2,3},{3,1},{1,0},{4,6},{6,7},{7,5},{5,4},{8,10},{10,11},{11... | collective-permute-start | bytes 1179656 | tf_op jit(solution)/shard_map/ppermute | solution.py:551
  76.2 1.3 %copy-start.3 = (f32[256,1280]{1,0:T(8,128)S(1)}, f32[256,1280]{1,0:T(8,128)}, u32[]{:S(2)}) copy-start(f32[256,1280]{1,0:T(8,128)} %get-tuple-element.34.settled_ref) | copy-start | bytes 3932164

commit v15 on v14

--- a/solution.py
+++ b/solution.py
@@ -11,6 +11,7 @@
 GROUP = 4
 CAP = 64
 LANES = 128
+SPAN = 64
 MASKED = -1e30
 VMEM_LIMIT = 50 * 1024 * 1024
 FULL_VMEM = 61 * 1024 * 1024
@@ -115,7 +116,7 @@
     (
         a_ref, out_ref, chosen_ref, sent_ref, out_sems,
         len_ref, adapter_ref, placement_ref, q_ref, k_ref, v_ref, nk_ref, nv_ref,
-        scores_ref, mixed_ref, sems, small_sems, w_held, w_sems,
+        scores_ref, mixed_ref, fresh_bias_ref, sems, small_sems, w_held, w_sems,
     ) = refs[3 + replicas :]
     requests = len_ref.shape[1]
     width = q_hbm.shape[1]
@@ -153,6 +154,12 @@
         copy = pltpu.make_async_copy(source, target, out_sems.at[len(leaving)])
         copy.start()
         leaving.append(copy)
+
+    def multiply(first, count):
+        rows = pl.ds(first, count)
+        for columns, product in weights.products(a_ref[rows, :]):
+            out_ref[rows, columns] = product.astype(jnp.bfloat16)
+        leave(out_ref.at[rows, :], out_hbm.at[rows, :])
 
     chunk = out_ref.shape[1]
     weights = Weights(w_hbm, w_held, w_sems, column_owner(0) * block, chunk)
@@ -175,11 +182,14 @@
     col = _iota((group_rows, group_cols), 1)
     same = (row // heads == col // (cache * kv)) & ((row % heads) // per_kv == col % kv)
     own_bias = jnp.where(same, 0.0, MASKED)
-    row = _iota((group_rows, per * kv), 0)
-    col = _iota((group_rows, per * kv), 1)
-    fresh_kv = (row % heads) // per_kv == col % kv
-    fresh_distance = col // kv - row // heads
-    ones = jnp.ones((max(group_cols, per * kv), LANES), jnp.bfloat16)
+    row = _iota(fresh_bias_ref.shape, 0)
+    col = _iota(fresh_bias_ref.shape, 1)
+    same = (row // heads == col // kv) & ((row % heads) // per_kv == col % kv)
+    fresh_bias_ref[...] = jnp.where(same, 0.0, MASKED)
+    fresh_cols = SPAN * kv
+    span_rows = SPAN * heads
+    span_groups = SPAN // GROUP
+    ones = jnp.ones((max(group_cols, fresh_cols), LANES), jnp.bfloat16)
 
     def arrive(step):
         part(0, step).wait()
@@ -196,9 +206,14 @@
                 1,
                 1,
             )
-        scores_ref[side, :, pl.ds(group_cols, per * kv)] = _dot(
-            q_ref[pl.ds(q_at, per * heads), :], nk_ref[pl.ds(step * per * kv, per * kv), :], 1, 1
-        )
+        for span in range(per // SPAN):
+            rows = pl.ds(span * span_rows, span_rows)
+            scores_ref[side, rows, pl.ds(group_cols, fresh_cols)] = _dot(
+                q_ref[pl.ds(q_at + span * span_rows, span_rows), :],
+                nk_ref[pl.ds(step * per * kv + span * fresh_cols, fresh_cols), :],
+                1,
+                1,
+            )
 
     for copy in small:
         copy.wait()
@@ -223,25 +238,32 @@
         if step + 1 < steps:
             arrive(step + 1)
             scores(step + 1)
-        held = []
-        fresh = []
-        for g in range(groups):
-            rows = pl.ds(g * group_rows, group_rows)
-            bias = own_bias + length_bias[step * groups + g : step * groups + g + 1, :]
-            cached = scores_ref[side, rows, pl.ds(0, group_cols)] + bias
-            new = scores_ref[side, rows, pl.ds(group_cols, per * kv)]
-            new = jnp.where(fresh_kv & (fresh_distance == g * GROUP), new, MASKED)
-            top = row_max([cached, new])
-            cached = jnp.exp2((cached - top) * scale).astype(jnp.bfloat16)
-            fresh.append(jnp.exp2((new - top) * scale).astype(jnp.bfloat16))
-            values = v_ref[pl.ds(k_at + g * group_cols, group_cols), :]
-            held.append(_dot(cached, jnp.concatenate([values, ones[:group_cols]], axis=1)))
-        values = jnp.concatenate([nv_ref[pl.ds(f_at, per * kv), :], ones[: per * kv]], axis=1)
-        fresh = _dot(jnp.concatenate(fresh, axis=0), values)
-        for g in range(groups):
-            rows = slice(g * group_rows, (g + 1) * group_rows)
-            mixed = fresh[rows, :] + held[g]
-            mixed_ref[side, rows, :] = mixed[:, :width] / mixed[:, width:]
+        if step == steps - 1:
+            weights.wait()
+            multiply(0, requests - per)
+        for span in range(per // SPAN):
+            cached_weights = []
+            fresh_weights = []
+            mixed = []
+            for g in range(span * span_groups, (span + 1) * span_groups):
+                rows = pl.ds(g * group_rows, group_rows)
+                bias = own_bias + length_bias[step * groups + g : step * groups + g + 1, :]
+                cached = scores_ref[side, rows, pl.ds(0, group_cols)] + bias
+                inner = pl.ds((g % span_groups) * group_rows, group_rows)
+                new = scores_ref[side, rows, pl.ds(group_cols, fresh_cols)]
+                new = new + fresh_bias_ref[inner, :]
+                top = row_max([cached, new])
+                cached = jnp.exp2((cached - top) * scale).astype(jnp.bfloat16)
+                cached_weights.append(cached)
+                fresh_weights.append(jnp.exp2((new - top) * scale).astype(jnp.bfloat16))
+                mixed.append(_dot(cached, v_ref[pl.ds(k_at + g * group_cols, group_cols), :]))
+            fresh = jnp.concatenate(fresh_weights, axis=0)
+            values = nv_ref[pl.ds(f_at + span * fresh_cols, fresh_cols), :]
+            mixed = jnp.concatenate(mixed, axis=0) + _dot(fresh, values)
+            total = _dot(jnp.concatenate(cached_weights, axis=0), ones[:group_cols])
+            total = total + _dot(fresh, ones[:fresh_cols])
+            rows = pl.ds(span * span_rows, span_rows)
+            mixed_ref[side, rows, :] = mixed / total
         for h in range(heads):
             a_ref[pl.ds(step * per, per), pl.ds(h * width, width)] = mixed_ref[
                 side, pl.ds(h, per, stride=heads), :
@@ -249,10 +271,7 @@
         rows = pl.ds(step * per, per)
         leave(a_ref.at[rows, :], a_hbm.at[rows, :])
 
-    weights.wait()
-    for columns, product in weights.products(a_ref[...]):
-        out_ref[:, columns] = product.astype(jnp.bfloat16)
-        leave(out_ref.at[:, columns], out_hbm.at[:, columns])
+    multiply(requests - per, per)
     sent_ref[:, pl.ds(0, heads * width)] = _dot(chosen_ref[...], a_ref[...]).astype(jnp.bfloat16)
     for r in range(replicas):
         leave(sent_ref.at[pl.ds(r * CAP, CAP), :], sent_hbm[r])
@@ -288,9 +307,9 @@
 ):
     requests, heads, width = query.shape
     cache, kv = keys.shape[1], keys.shape[2]
-    steps = 4
+    steps = 2
     per = requests // steps
-    columns = GROUP * cache * kv + per * kv
+    columns = GROUP * cache * kv + SPAN * kv
     features = heads * width
     chunk = chain_columns(block)[0][1]
     small = [lengths.reshape(1, -1), request_adapter.reshape(1, -1), placement.reshape(1, -1)]
@@ -316,12 +335,13 @@
             pltpu.VMEM((requests, chunk), jnp.bfloat16),
             pltpu.VMEM((replicas * CAP, requests), jnp.bfloat16),
             pltpu.VMEM((replicas * CAP, features + LANES), jnp.bfloat16),
-            pltpu.SemaphoreType.DMA((1 + steps + pl.cdiv(chunk, PIECE) + replicas,)),
+            pltpu.SemaphoreType.DMA((1 + steps + 2 + replicas,)),
         ]
         + [pltpu.VMEM(x.shape, x.dtype) for x in small + operands]
         + [
             pltpu.VMEM((2, per * heads, columns), jnp.float32),
             pltpu.VMEM((2, per * heads, width), jnp.float32),
+            pltpu.VMEM((SPAN * heads, SPAN * kv), jnp.float32),
             pltpu.SemaphoreType.DMA((3, steps)),
             pltpu.SemaphoreType.DMA((5,)),
         ]

time: 83.2 us -> 82.6 us (level)
  no operation moved by 1% of the time
where the time goes in v15:
time: 82.6 us; the launch traced here: 82.2 us
  waiting for transfers between devices  27.1 us (33%)
  Pallas kernels  26.6 us (32%)
  starting transfers between devices  25.9 us (31%)
  local copies, waits for them, and re-layouts  2.38 us (3%)
    ppermute x6, starting transfers between devices, forward(): return lax.ppermute(x, 'tensor', ring)  16.6 us
    ppermute x6, waiting for transfers between devices, forward(): return lax.ppermute(x, 'tensor', ring)  13.2 us
    pallas_call x5, Pallas kernels, hop(): pl.pallas_call(functools.partial(hop_kernel, step, block, start, arriving...  11.3 us
    ppermute x6, waiting for transfers between devices, exchange(): lax.ppermute(blocks[r], 'dp', [(i, i ^ r) for i in range(replicas)])  9.72 us
    pallas_call x1, Pallas kernels, attend(): pl.pallas_call(functools.partial(attend_kernel, heads, kv, cache, steps,...  7.67 us
    pallas_call x1, Pallas kernels, settle(): pl.pallas_call(functools.partial(settle_kernel, step, replicas, len(after...  4.52 us
    ppermute x1, waiting for transfers between devices, per_device(): lax.ppermute(mid, 'tensor', [(i, i ^ 1) for i in range(count)])  4.17 us
    ppermute x1, starting transfers between devices, pair_sums(): other = lax.ppermute(x, 'tensor', far)  4.12 us
  transfers between devices with their start and end apart: 15, of which 8 were waited for; matrix products, arithmetic and copies ran while one was open for 0% of the time, Pallas kernels for 22%

profile of v15, /device:TPU:0, one launch (start us, length us, event | category | flops | bytes accessed | tf_op | source)
XLA Modules:
  0.0 82.2 jit_solution(1707065389721775555)
XLA Ops:
  0.0 7.7 %attend.1 = (bf16[256,1024]{1,0:T(8,128)(2,1)}, bf16[256,1280]{1,0:T(8,128)(2,1)}, bf16[256,256]{1,0:T(8,128)(2,1)}, bf16[64,1152]{1,0:T(8,128)(2,1)}, bf16[64,1...) custom-call(s32[1,256]{1,0:T(1,128)} %bitcast.13, s32[1,256]{1,0:T(1,128)} %bitcast.14, ...), custom_call_target="tpu_custom_call" | custom-call | tf_op jit(solution)/shard_map/attend/pallas_call | solution.py:323
  7.7 4.1 %collective-permute-start.4 = (bf16[256,1280]{1,0:T(8,128)(2,1)}, bf16[256,1280]{1,0:T(8,128)(2,1)S(1)}, u32[]{:S(2)}, u32[]{:S(2)}) collective-permute-start(bf16[256,1280]{1,0:T(8,128)(2,1)} %get-tuple-element.26), channel_id=1, source_target_pairs={{0,2},{2,3},{3,1},{1,0},{4,6},{6,7},{7,5},{5,4},{8,10},{10,11},{11... | collective-permute-start | bytes 1966088 | tf_op jit(solution)/shard_map/ppermute | solution.py:571
  11.8 1.5 %collective-permute-start.1 = (bf16[64,1152]{1,0:T(8,128)(2,1)}, bf16[64,1152]{1,0:T(8,128)(2,1)S(1)}, u32[]{:S(2)}, u32[]{:S(2)}) collective-permute-start(bf16[64,1152]{1,0:T(8,128)(2,1)} %get-tuple-element.23), channel_id=1, source_target_pairs={{0,8},{4,12},{8,0},{12,4},{1,9},{5,13},{9,1},{13,5},{2,10},{6,14},... | collective-permute-start | bytes 442376 | tf_op jit(solution)/shard_map/ppermute | solution.py:565
  13.3 0.4 collective-permute-start.2
  13.6 1.0 %copy-done = bf16[256,1024]{1,0:T(8,128)(2,1)S(1)} copy-done((bf16[256,1024]{1,0:T(8,128)(2,1)S(1)}, bf16[256,1024]{1,0:T(8,128)(2,1)}, u32[]{:S(2)}) %copy-start) | copy-done | bytes 524312
  14.7 2.1 %hop.5.refs_5_.refs_0_ = bf16[256,768]{1,0:T(8,128)(2,1)S(1)} custom-call(bf16[256,1024]{1,0:T(8,128)(2,1)S(1)} %copy-done, bf16[1024,8192]{1,0:T(8,128)(2,1)} %refs_7_.1), custom_call_target="tpu_custom_call" | custom-call | tf_op jit(solution)/shard_map/hop/pallas_call | solution.py:374
  16.8 1.9 %collective-permute-done.1.refs_2_ = bf16[64,1152]{1,0:T(8,128)(2,1)S(1)} collective-permute-done((bf16[64,1152]{1,0:T(8,128)(2,1)}, bf16[64,1152]{1,0:T(8,128)(2,1)S(1)}, u32[]{:S(2)}, u32[]{:S(2)}) %collective-permute-start.1) | collective-permute-done | bytes 147488 | tf_op jit(solution)/shard_map/ppermute | solution.py:565
  18.6 2.4 %collective-permute-done.2.refs_3_ = bf16[64,1152]{1,0:T(8,128)(2,1)S(1)} collective-permute-done((bf16[64,1152]{1,0:T(8,128)(2,1)}, bf16[64,1152]{1,0:T(8,128)(2,1)S(1)}, u32[]{:S(2)}, u32[]{:S(2)}) %collective-permute-start.2) | collective-permute-done | bytes 147488 | tf_op jit(solution)/shard_map/ppermute | solution.py:565
  21.0 0.6 down.1
  21.8 1.9 %collective-permute-start.3 = (bf16[256,768]{1,0:T(8,128)(2,1)S(1)}, bf16[256,768]{1,0:T(8,128)(2,1)S(1)}, u32[]{:S(2)}, u32[]{:S(2)}) collective-permute-start(bf16[256,768]{1,0:T(8,128)(2,1)S(1)} %hold.1.refs_4_), channel_id=1, source_target_pairs={{0,2},{2,3},{3,1},{1,0},{4,6},{6,7},{7,5},{5,4},{8,10},{10,11},{11... | collective-permute-start | bytes 1179656 | tf_op jit(solution)/shard_map/ppermute | solution.py:571
  23.7 4.2 %collective-permute-done.5 = bf16[128,128]{1,0:T(8,128)(2,1)S(1)} collective-permute-done((bf16[128,128]{1,0:T(8,128)(2,1)S(1)}, bf16[128,128]{1,0:T(8,128)(2,1)S(1)}, u32[]{:S(2)}, u32[]{:S(2)}) %collective-permute-start.5) | collective-permute-done | bytes 32800 | tf_op jit(solution)/shard_map/ppermute | solution.py:604
  27.9 2.6 %hop.6.refs_3_ = bf16[256,1280]{1,0:T(8,128)(2,1)S(1)} custom-call(bf16[256,1280]{1,0:T(8,128)(2,1)S(1)} %collective-permute-done.4.refs_0_, bf16[256,1024]{1,0:T(8,128)(2,1)S(1)} %copy-done.1, bf16[1024,8192]{1,0:T(8,128)(2,1)} %refs_7_.1, bf16[128,128]{1,0:T(8,128)(2,1)S(1)} %add_convert_fusion.refs_3_.refs_0_, bf16[256,768]{1,0:T(8,128)(2,1)S(1)} %hold.1.refs_4_), custom_call_target="tpu_custom_call" | custom-call | flops 20000000000 | bytes 40000000 | tf_op jit(solution)/shard_map/hop/pallas_call | solution.py:374
  30.5 2.7 %collective-permute-start.9 = (bf16[256,1280]{1,0:T(8,128)(2,1)S(1)}, bf16[256,1280]{1,0:T(8,128)(2,1)S(1)}, u32[]{:S(2)}, u32[]{:S(2)}) collective-permute-start(bf16[256,1280]{1,0:T(8,128)(2,1)S(1)} %hop.6.refs_3_), channel_id=1, source_target_pairs={{0,2},{2,3},{3,1},{1,0},{4,6},{6,7},{7,5},{5,4},{8,10},{10,11},{11... | collective-permute-start | bytes 1966088 | tf_op jit(solution)/shard_map/ppermute | solution.py:571
  33.1 4.1 %collective-permute-start.8 = (bf16[128,128]{1,0:T(8,128)(2,1)S(1)}, bf16[128,128]{1,0:T(8,128)(2,1)S(1)}, u32[]{:S(2)}, u32[]{:S(2)}) collective-permute-start(bf16[128,128]{1,0:T(8,128)(2,1)S(1)} %add_convert_fusion.refs_3_.refs_0_), channel_id=1, source_target_pairs={{0,3},{3,0},{4,7},{7,4},{8,11},{11,8},{12,15},{15,12},{16,19},{19,... | collective-permute-start | bytes 98312 | tf_op jit(solution)/shard_map/ppermute | solution.py:584
  37.3 1.3 %collective-permute-start.7 = (bf16[128,128]{1,0:T(8,128)(2,1)S(1)}, bf16[128,128]{1,0:T(8,128)(2,1)S(1)}, u32[]{:S(2)}, u32[]{:S(2)}) collective-permute-start(bf16[128,128]{1,0:T(8,128)(2,1)S(1)} %add_convert_fusion.refs_3_.refs_0_), channel_id=1, source_target_pairs={{0,2},{3,1},{4,6},{7,5},{8,10},{11,9},{12,14},{15,13},{16,18},{19,... | collective-permute-start | bytes 98312 | tf_op jit(solution)/shard_map/ppermute | solution.py:583
  38.6 2.0 %hop.7 = bf16[256,768]{1,0:T(8,128)(2,1)S(1)} custom-call(bf16[256,768]{1,0:T(8,128)(2,1)S(1)} %collective-permute-done.3.refs_0_, bf16[256,1024]{1,0:T(8,128)(2,1)S(1)} %copy-done.1, bf16[1024,8192]{1,0:T(8,128)(2,1)} %refs_7_.1, bf16[256,1280]{1,0:T(8,128)(2,1)S(1)} %hop.6.refs_3_), custom_call_target="tpu_custom_call" | custom-call | flops 4000000000 | bytes 8000000 | tf_op jit(solution)/shard_map/hop/pallas_call | solution.py:374
  40.6 1.1 %collective-permute-start.6 = (bf16[256,768]{1,0:T(8,128)(2,1)S(1)}, bf16[256,768]{1,0:T(8,128)(2,1)S(1)}, u32[]{:S(2)}, u32[]{:S(2)}) collective-permute-start(bf16[256,768]{1,0:T(8,128)(2,1)S(1)} %hop.7), channel_id=1, source_target_pairs={{0,2},{2,3},{3,1},{1,0},{4,6},{6,7},{7,5},{5,4},{8,10},{10,11},{11... | collective-permute-start | bytes 1179656 | tf_op jit(solution)/shard_map/ppermute | solution.py:571
  41.7 8.6 %collective-permute-done.9.refs_0_ = bf16[256,1280]{1,0:T(8,128)(2,1)S(1)} collective-permute-done((bf16[256,1280]{1,0:T(8,128)(2,1)S(1)}, bf16[256,1280]{1,0:T(8,128)(2,1)S(1)}, u32[]{:S(2)}, u32[]{:S(2)}) %collective-permute-start.9) | collective-permute-done | bytes 655392 | tf_op jit(solution)/shard_map/ppermute | solution.py:571
  50.3 2.6 %hop.8.refs_5_ = bf16[256,1280]{1,0:T(8,128)(2,1)S(1)} custom-call(bf16[256,1280]{1,0:T(8,128)(2,1)S(1)} %collective-permute-done.9.refs_0_, bf16[256,1024]{1,0:T(8,128)(2,1)S(1)} %copy-done.1, bf16[1024,8192]{1,0:T(8,128)(2,1)} %refs_7_.1), custom_call_target="tpu_custom_call" | custom-call | flops 20000000000 | bytes 40000000 | tf_op jit(solution)/shard_map/hop/pallas_call | solution.py:374
  52.9 3.4 %collective-permute-start.14 = (bf16[256,1280]{1,0:T(8,128)(2,1)S(1)}, bf16[256,1280]{1,0:T(8,128)(2,1)S(1)}, u32[]{:S(2)}, u32[]{:S(2)}) collective-permute-start(bf16[256,1280]{1,0:T(8,128)(2,1)S(1)} %hop.8.refs_5_), channel_id=1, source_target_pairs={{0,2},{2,3},{3,1},{1,0},{4,6},{6,7},{7,5},{5,4},{8,10},{10,11},{11... | collective-permute-start | bytes 1966088 | tf_op jit(solution)/shard_map/ppermute | solution.py:571
  56.3 0.8 up.1
  57.2 1.6 %collective-permute-start.12 = (bf16[64,2048]{1,0:T(8,128)(2,1)S(1)}, bf16[64,2048]{1,0:T(8,128)(2,1)S(1)}, u32[]{:S(2)}, u32[]{:S(2)}) collective-permute-start(bf16[64,2048]{1,0:T(8,128)(2,1)S(1)} %get-tuple-element.30), channel_id=1, source_target_pairs={{0,8},{4,12},{8,0},{12,4},{1,9},{5,13},{9,1},{13,5},{2,10},{6,14},... | collective-permute-start | bytes 786440 | tf_op jit(solution)/shard_map/ppermute | solution.py:565
  59.1 1.0 %collective-permute-done.6.refs_0_ = bf16[256,768]{1,0:T(8,128)(2,1)S(1)} collective-permute-done((bf16[256,768]{1,0:T(8,128)(2,1)S(1)}, bf16[256,768]{1,0:T(8,128)(2,1)S(1)}, u32[]{:S(2)}, u32[]{:S(2)}) %collective-permute-start.6) | collective-permute-done | bytes 393248 | tf_op jit(solution)/shard_map/ppermute | solution.py:571
  60.1 2.1 %hop.9.refs_8_ = bf16[256,768]{1,0:T(8,128)(2,1)S(1)} custom-call(bf16[256,768]{1,0:T(8,128)(2,1)S(1)} %collective-permute-done.6.refs_0_, bf16[256,1024]{1,0:T(8,128)(2,1)S(1)} %copy-done.1, bf16[1024,8192]{1,0:T(8,128)(2,1)} %refs_7_.1, bf16[64,2048]{1,0:T(8,128)(2,1)S(1)} %get-tuple-element.28.refs_3_.refs_0_), custom_call_target="tpu_custom_call" | custom-call | tf_op jit(solution)/shard_map/hop/pallas_call | solution.py:374
  62.2 3.4 %collective-permute-start.10 = (bf16[256,768]{1,0:T(8,128)(2,1)S(1)}, bf16[256,768]{1,0:T(8,128)(2,1)S(1)}, u32[]{:S(2)}, u32[]{:S(2)}) collective-permute-start(bf16[256,768]{1,0:T(8,128)(2,1)S(1)} %hop.9.refs_8_), channel_id=1, source_target_pairs={{0,2},{2,3},{3,1},{1,0},{4,6},{6,7},{7,5},{5,4},{8,10},{10,11},{11... | collective-permute-start | bytes 1179656 | tf_op jit(solution)/shard_map/ppermute | solution.py:571
  65.6 0.8 collective-permute-done.12.refs_2_
  66.4 4.7 %collective-permute-done.13.refs_3_ = bf16[64,2048]{1,0:T(8,128)(2,1)S(1)} collective-permute-done((bf16[64,2048]{1,0:T(8,128)(2,1)S(1)}, bf16[64,2048]{1,0:T(8,128)(2,1)S(1)}, u32[]{:S(2)}, u32[]{:S(2)}) %collective-permute-start.13) | collective-permute-done | bytes 262176 | tf_op jit(solution)/shard_map/ppermute | solution.py:565
  71.1 4.5 %settle.1 = (f32[256,1280]{1,0:T(8,128)}, f32[256,768]{1,0:T(8,128)S(1)}) custom-call(bf16[64,2048]{1,0:T(8,128)(2,1)S(1)} %get-tuple-element.28.refs_3_.refs_0_, bf16[64,2048]{1,0:T(8,128)(2,1)S(1)} %collective-permute-done.11.refs_1_, bf16[64,2048]{1,0:T(8,128)(2,1)S(1)} %collective-permute-done.12.refs_2_, ...), custom_call_target="tpu_custom_call" | custom-call | flops 4000000000 | bytes 8000000 | tf_op jit(solution)/shard_map/settle/pallas_call | solution.py:480
  75.7 1.3 %copy-done.3 = f32[256,1280]{1,0:T(8,128)S(1)} copy-done((f32[256,1280]{1,0:T(8,128)S(1)}, f32[256,1280]{1,0:T(8,128)}, u32[]{:S(2)}) %copy-start.3) | copy-done | bytes 1310744
  77.0 0.9 %finish.2.refs_0_ = bf16[256,2048]{1,0:T(8,128)(2,1)} custom-call(bf16[256,1280]{1,0:T(8,128)(2,1)S(1)} %collective-permute-done.14.arrived_ref, f32[256,1280]{1,0:T(8,128)S(1)} %copy-done.3), custom_call_target="tpu_custom_call" | custom-call | tf_op jit(solution)/shard_map/finish/pallas_call | solution.py:512
  77.9 3.6 %collective-permute-done.10.arrived_ref = bf16[256,768]{1,0:T(8,128)(2,1)S(1)} collective-permute-done((bf16[256,768]{1,0:T(8,128)(2,1)S(1)}, bf16[256,768]{1,0:T(8,128)(2,1)S(1)}, u32[]{:S(2)}, u32[]{:S(2)}) %collective-permute-start.10) | collective-permute-done | bytes 393248 | tf_op jit(solution)/shard_map/ppermute | solution.py:571
  81.5 0.8 finish.3
  (27 shorter events, 0.5 us)
Async XLA Ops:
  7.7 20.2 %collective-permute-start.4 = (bf16[256,1280]{1,0:T(8,128)(2,1)}, bf16[256,1280]{1,0:T(8,128)(2,1)S(1)}, u32[]{:S(2)}, u32[]{:S(2)}) collective-permute-start(bf16[256,1280]{1,0:T(8,128)(2,1)} %get-tuple-element.26), channel_id=1, source_target_pairs={{0,2},{2,3},{3,1},{1,0},{4,6},{6,7},{7,5},{5,4},{8,10},{10,11},{11... | collective-permute-start | bytes 1966088 | tf_op jit(solution)/shard_map/ppermute | solution.py:571
  11.8 5.0 %collective-permute-start = (bf16[64,1152]{1,0:T(8,128)(2,1)}, bf16[64,1152]{1,0:T(8,128)(2,1)S(1)}, u32[]{:S(2)}, u32[]{:S(2)}) collective-permute-start(bf16[64,1152]{1,0:T(8,128)(2,1)} %get-tuple-element.22), channel_id=1, source_target_pairs={{0,4},{4,0},{8,12},{12,8},{1,5},{5,1},{9,13},{13,9},{2,6},{6,2},{1... | collective-permute-start | bytes 442376 | tf_op jit(solution)/shard_map/ppermute | solution.py:565
  11.8 6.9 %collective-permute-start.1 = (bf16[64,1152]{1,0:T(8,128)(2,1)}, bf16[64,1152]{1,0:T(8,128)(2,1)S(1)}, u32[]{:S(2)}, u32[]{:S(2)}) collective-permute-start(bf16[64,1152]{1,0:T(8,128)(2,1)} %get-tuple-element.23), channel_id=1, source_target_pairs={{0,8},{4,12},{8,0},{12,4},{1,9},{5,13},{9,1},{13,5},{2,10},{6,14},... | collective-permute-start | bytes 442376 | tf_op jit(solution)/shard_map/ppermute | solution.py:565
  13.3 7.8 %collective-permute-start.2 = (bf16[64,1152]{1,0:T(8,128)(2,1)}, bf16[64,1152]{1,0:T(8,128)(2,1)S(1)}, u32[]{:S(2)}, u32[]{:S(2)}) collective-permute-start(bf16[64,1152]{1,0:T(8,128)(2,1)} %get-tuple-element.24), channel_id=1, source_target_pairs={{0,12},{4,8},{8,4},{12,0},{1,13},{5,9},{9,5},{13,1},{2,14},{6,10},... | collective-permute-start | bytes 442376 | tf_op jit(solution)/shard_map/ppermute | solution.py:565
  13.6 1.0 %copy-start = (bf16[256,1024]{1,0:T(8,128)(2,1)S(1)}, bf16[256,1024]{1,0:T(8,128)(2,1)}, u32[]{:S(2)}) copy-start(bf16[256,1024]{1,0:T(8,128)(2,1)} %get-tuple-element.20.refs_0_.refs_1_.refs_5_) | copy-start | bytes 1572868
  14.7 6.3 %copy-start.5 = (bf16[8,64,1024]{2,1,0:T(8,128)(2,1)S(1)}, bf16[8,64,1024]{2,1,0:T(8,128)(2,1)}, u32[]{:S(2)}) copy-start(bf16[8,64,1024]{2,1,0:T(8,128)(2,1)} %refs_4_.2) | copy-start | bytes 3145732
  14.7 6.3 %copy-start.6 = (bf16[64,1152]{1,0:T(8,128)(2,1)S(1)}, bf16[64,1152]{1,0:T(8,128)(2,1)}, u32[]{:S(2)}) copy-start(bf16[64,1152]{1,0:T(8,128)(2,1)} %get-tuple-element.21.refs_0_) | copy-start | bytes 442372
  16.8 11.1 %copy-start.1 = (bf16[256,1024]{1,0:T(8,128)(2,1)S(1)}, bf16[256,1024]{1,0:T(8,128)(2,1)}, u32[]{:S(2)}) copy-start(bf16[256,1024]{1,0:T(8,128)(2,1)} %get-tuple-element.20.refs_0_.refs_1_.refs_5_) | copy-start | bytes 1572868
  21.7 6.2 %collective-permute-start.5 = (bf16[128,128]{1,0:T(8,128)(2,1)S(1)}, bf16[128,128]{1,0:T(8,128)(2,1)S(1)}, u32[]{:S(2)}, u32[]{:S(2)}) collective-permute-start(bf16[128,128]{1,0:T(8,128)(2,1)S(1)} %get-tuple-element.25.refs_1_), channel_id=1, source_target_pairs={{0,1},{1,0},{2,3},{3,2},{4,5},{5,4},{6,7},{7,6},{8,9},{9,8},{10,11... | collective-permute-start | bytes 98312 | tf_op jit(solution)/shard_map/ppermute | solution.py:604
  21.8 16.8 %collective-permute-start.3 = (bf16[256,768]{1,0:T(8,128)(2,1)S(1)}, bf16[256,768]{1,0:T(8,128)(2,1)S(1)}, u32[]{:S(2)}, u32[]{:S(2)}) collective-permute-start(bf16[256,768]{1,0:T(8,128)(2,1)S(1)} %hold.1.refs_4_), channel_id=1, source_target_pairs={{0,2},{2,3},{3,1},{1,0},{4,6},{6,7},{7,5},{5,4},{8,10},{10,11},{11... | collective-permute-start | bytes 1179656 | tf_op jit(solution)/shard_map/ppermute | solution.py:571
  30.5 19.8 %collective-permute-start.9 = (bf16[256,1280]{1,0:T(8,128)(2,1)S(1)}, bf16[256,1280]{1,0:T(8,128)(2,1)S(1)}, u32[]{:S(2)}, u32[]{:S(2)}) collective-permute-start(bf16[256,1280]{1,0:T(8,128)(2,1)S(1)} %hop.6.refs_3_), channel_id=1, source_target_pairs={{0,2},{2,3},{3,1},{1,0},{4,6},{6,7},{7,5},{5,4},{8,10},{10,11},{11... | collective-permute-start | bytes 1966088 | tf_op jit(solution)/shard_map/ppermute | solution.py:571
  33.1 23.2 %collective-permute-start.8 = (bf16[128,128]{1,0:T(8,128)(2,1)S(1)}, bf16[128,128]{1,0:T(8,128)(2,1)S(1)}, u32[]{:S(2)}, u32[]{:S(2)}) collective-permute-start(bf16[128,128]{1,0:T(8,128)(2,1)S(1)} %add_convert_fusion.refs_3_.refs_0_), channel_id=1, source_target_pairs={{0,3},{3,0},{4,7},{7,4},{8,11},{11,8},{12,15},{15,12},{16,19},{19,... | collective-permute-start | bytes 98312 | tf_op jit(solution)/shard_map/ppermute | solution.py:584
  37.3 19.1 %collective-permute-start.7 = (bf16[128,128]{1,0:T(8,128)(2,1)S(1)}, bf16[128,128]{1,0:T(8,128)(2,1)S(1)}, u32[]{:S(2)}, u32[]{:S(2)}) collective-permute-start(bf16[128,128]{1,0:T(8,128)(2,1)S(1)} %add_convert_fusion.refs_3_.refs_0_), channel_id=1, source_target_pairs={{0,2},{3,1},{4,6},{7,5},{8,10},{11,9},{12,14},{15,13},{16,18},{19,... | collective-permute-start | bytes 98312 | tf_op jit(solution)/shard_map/ppermute | solution.py:583
  40.6 15.7 %copy-start.2 = (bf16[8,64,2048]{2,1,0:T(8,128)(2,1)S(1)}, bf16[8,64,2048]{2,1,0:T(8,128)(2,1)}, u32[]{:S(2)}) copy-start(bf16[8,64,2048]{2,1,0:T(8,128)(2,1)} %refs_4_.3) | copy-start | bytes 6291460
  40.6 19.5 %collective-permute-start.6 = (bf16[256,768]{1,0:T(8,128)(2,1)S(1)}, bf16[256,768]{1,0:T(8,128)(2,1)S(1)}, u32[]{:S(2)}, u32[]{:S(2)}) collective-permute-start(bf16[256,768]{1,0:T(8,128)(2,1)S(1)} %hop.7), channel_id=1, source_target_pairs={{0,2},{2,3},{3,1},{1,0},{4,6},{6,7},{7,5},{5,4},{8,10},{10,11},{11... | collective-permute-start | bytes 1179656 | tf_op jit(solution)/shard_map/ppermute | solution.py:571
  52.9 22.8 %collective-permute-start.14 = (bf16[256,1280]{1,0:T(8,128)(2,1)S(1)}, bf16[256,1280]{1,0:T(8,128)(2,1)S(1)}, u32[]{:S(2)}, u32[]{:S(2)}) collective-permute-start(bf16[256,1280]{1,0:T(8,128)(2,1)S(1)} %hop.8.refs_5_), channel_id=1, source_target_pairs={{0,2},{2,3},{3,1},{1,0},{4,6},{6,7},{7,5},{5,4},{8,10},{10,11},{11... | collective-permute-start | bytes 1966088 | tf_op jit(solution)/shard_map/ppermute | solution.py:571
  57.1 8.5 %collective-permute-start.11 = (bf16[64,2048]{1,0:T(8,128)(2,1)S(1)}, bf16[64,2048]{1,0:T(8,128)(2,1)S(1)}, u32[]{:S(2)}, u32[]{:S(2)}) collective-permute-start(bf16[64,2048]{1,0:T(8,128)(2,1)S(1)} %get-tuple-element.29), channel_id=1, source_target_pairs={{0,4},{4,0},{8,12},{12,8},{1,5},{5,1},{9,13},{13,9},{2,6},{6,2},{1... | collective-permute-start | bytes 786440 | tf_op jit(solution)/shard_map/ppermute | solution.py:565
  57.2 9.2 %collective-permute-start.12 = (bf16[64,2048]{1,0:T(8,128)(2,1)S(1)}, bf16[64,2048]{1,0:T(8,128)(2,1)S(1)}, u32[]{:S(2)}, u32[]{:S(2)}) collective-permute-start(bf16[64,2048]{1,0:T(8,128)(2,1)S(1)} %get-tuple-element.30), channel_id=1, source_target_pairs={{0,8},{4,12},{8,0},{12,4},{1,9},{5,13},{9,1},{13,5},{2,10},{6,14},... | collective-permute-start | bytes 786440 | tf_op jit(solution)/shard_map/ppermute | solution.py:565
  58.8 12.3 %collective-permute-start.13 = (bf16[64,2048]{1,0:T(8,128)(2,1)S(1)}, bf16[64,2048]{1,0:T(8,128)(2,1)S(1)}, u32[]{:S(2)}, u32[]{:S(2)}) collective-permute-start(bf16[64,2048]{1,0:T(8,128)(2,1)S(1)} %get-tuple-element.31), channel_id=1, source_target_pairs={{0,12},{4,8},{8,4},{12,0},{1,13},{5,9},{9,5},{13,1},{2,14},{6,10},... | collective-permute-start | bytes 786440 | tf_op jit(solution)/shard_map/ppermute | solution.py:565
  60.1 11.0 %copy-start.4 = (bf16[256,2048]{1,0:T(8,128)(2,1)S(1)}, bf16[256,2048]{1,0:T(8,128)(2,1)}, u32[]{:S(2)}) copy-start(bf16[256,2048]{1,0:T(8,128)(2,1)} %refs_6_.1) | copy-start | bytes 3145732
  60.1 11.0 %copy-start.7 = (bf16[256,256]{1,0:T(8,128)(2,1)S(1)}, bf16[256,256]{1,0:T(8,128)(2,1)}, u32[]{:S(2)}) copy-start(bf16[256,256]{1,0:T(8,128)(2,1)} %get-tuple-element.32.refs_4_) | copy-start | bytes 393220
  62.2 19.2 %collective-permute-start.10 = (bf16[256,768]{1,0:T(8,128)(2,1)S(1)}, bf16[256,768]{1,0:T(8,128)(2,1)S(1)}, u32[]{:S(2)}, u32[]{:S(2)}) collective-permute-start(bf16[256,768]{1,0:T(8,128)(2,1)S(1)} %hop.9.refs_8_), channel_id=1, source_target_pairs={{0,2},{2,3},{3,1},{1,0},{4,6},{6,7},{7,5},{5,4},{8,10},{10,11},{11... | collective-permute-start | bytes 1179656 | tf_op jit(solution)/shard_map/ppermute | solution.py:571
  75.6 1.3 %copy-start.3 = (f32[256,1280]{1,0:T(8,128)S(1)}, f32[256,1280]{1,0:T(8,128)}, u32[]{:S(2)}) copy-start(f32[256,1280]{1,0:T(8,128)} %get-tuple-element.34.settled_ref) | copy-start | bytes 3932164

commit v16 on v15

--- a/solution.py
+++ b/solution.py
@@ -217,8 +217,6 @@
 
     for copy in small:
         copy.wait()
-    plan_routes(slots, adapter_ref, placement_ref, chosen_ref, sent_ref)
-    leave(chosen_ref, chosen_hbm)
     counts = len_ref[...].astype(jnp.float32)
     all_groups = requests // GROUP
     of_group = _iota((all_groups, requests), 1) // GROUP == _iota((all_groups, requests), 0)
@@ -238,6 +236,9 @@
         if step + 1 < steps:
             arrive(step + 1)
             scores(step + 1)
+        if step == 0:
+            plan_routes(slots, adapter_ref, placement_ref, chosen_ref, sent_ref)
+            leave(chosen_ref, chosen_hbm)
         if step == steps - 1:
             weights.wait()
             multiply(0, requests - per)
@@ -263,7 +264,8 @@
             total = _dot(jnp.concatenate(cached_weights, axis=0), ones[:group_cols])
             total = total + _dot(fresh, ones[:fresh_cols])
             rows = pl.ds(span * span_rows, span_rows)
-            mixed_ref[side, rows, :] = mixed / total
+            inverse = pl.reciprocal(total, approx=True)
+            mixed_ref[side, rows, :] = mixed * (inverse * (2.0 - total * inverse))
         for h in range(heads):
             a_ref[pl.ds(step * per, per), pl.ds(h * width, width)] = mixed_ref[
                 side, pl.ds(h, per, stride=heads), :
@@ -271,10 +273,10 @@
         rows = pl.ds(step * per, per)
         leave(a_ref.at[rows, :], a_hbm.at[rows, :])
 
-    multiply(requests - per, per)
     sent_ref[:, pl.ds(0, heads * width)] = _dot(chosen_ref[...], a_ref[...]).astype(jnp.bfloat16)
     for r in range(replicas):
         leave(sent_ref.at[pl.ds(r * CAP, CAP), :], sent_hbm[r])
+    multiply(requests - per, per)
     for copy in leaving:
         copy.wait()
 

time: 82.6 us -> 82.4 us (level)
  no operation moved by 1% of the time
where the time goes in v16:
time: 82.4 us; the launch traced here: 82.1 us
  waiting for transfers between devices  27.1 us (33%)
  Pallas kernels  26.4 us (32%)
  starting transfers between devices  25.9 us (31%)
  local copies, waits for them, and re-layouts  2.38 us (3%)
    ppermute x6, starting transfers between devices, forward(): return lax.ppermute(x, 'tensor', ring)  16.6 us
    ppermute x6, waiting for transfers between devices, forward(): return lax.ppermute(x, 'tensor', ring)  13.3 us
    pallas_call x5, Pallas kernels, hop(): pl.pallas_call(functools.partial(hop_kernel, step, block, start, arriving...  11.3 us
    ppermute x6, waiting for transfers between devices, exchange(): lax.ppermute(blocks[r], 'dp', [(i, i ^ r) for i in range(replicas)])  9.71 us
    pallas_call x1, Pallas kernels, attend(): pl.pallas_call(functools.partial(attend_kernel, heads, kv, cache, steps,...  7.49 us
    pallas_call x1, Pallas kernels, settle(): pl.pallas_call(functools.partial(settle_kernel, step, replicas, len(after...  4.51 us
    ppermute x1, waiting for transfers between devices, per_device(): lax.ppermute(mid, 'tensor', [(i, i ^ 1) for i in range(count)])  4.17 us
    ppermute x1, starting transfers between devices, pair_sums(): other = lax.ppermute(x, 'tensor', far)  4.12 us
  transfers between devices with their start and end apart: 15, of which 8 were waited for; matrix products, arithmetic and copies ran while one was open for 0% of the time, Pallas kernels for 22%

profile of v16, /device:TPU:0, one launch (start us, length us, event | category | flops | bytes accessed | tf_op | source)
XLA Modules:
  0.0 82.1 jit_solution(925388253164255082)
XLA Ops:
  0.0 7.5 %attend.1 = (bf16[256,1024]{1,0:T(8,128)(2,1)}, bf16[256,1280]{1,0:T(8,128)(2,1)}, bf16[256,256]{1,0:T(8,128)(2,1)}, bf16[64,1152]{1,0:T(8,128)(2,1)}, bf16[64,1...) custom-call(s32[1,256]{1,0:T(1,128)} %bitcast.13, s32[1,256]{1,0:T(1,128)} %bitcast.14, ...), custom_call_target="tpu_custom_call" | custom-call | tf_op jit(solution)/shard_map/attend/pallas_call | solution.py:325
  7.5 4.1 %collective-permute-start.4 = (bf16[256,1280]{1,0:T(8,128)(2,1)}, bf16[256,1280]{1,0:T(8,128)(2,1)S(1)}, u32[]{:S(2)}, u32[]{:S(2)}) collective-permute-start(bf16[256,1280]{1,0:T(8,128)(2,1)} %get-tuple-element.26), channel_id=1, source_target_pairs={{0,2},{2,3},{3,1},{1,0},{4,6},{6,7},{7,5},{5,4},{8,10},{10,11},{11... | collective-permute-start | bytes 1966088 | tf_op jit(solution)/shard_map/ppermute | solution.py:573
  11.6 1.5 %collective-permute-start.1 = (bf16[64,1152]{1,0:T(8,128)(2,1)}, bf16[64,1152]{1,0:T(8,128)(2,1)S(1)}, u32[]{:S(2)}, u32[]{:S(2)}) collective-permute-start(bf16[64,1152]{1,0:T(8,128)(2,1)} %get-tuple-element.23), channel_id=1, source_target_pairs={{0,8},{4,12},{8,0},{12,4},{1,9},{5,13},{9,1},{13,5},{2,10},{6,14},... | collective-permute-start | bytes 442376 | tf_op jit(solution)/shard_map/ppermute | solution.py:567
  13.1 0.4 collective-permute-start.2
  13.4 1.0 %copy-done = bf16[256,1024]{1,0:T(8,128)(2,1)S(1)} copy-done((bf16[256,1024]{1,0:T(8,128)(2,1)S(1)}, bf16[256,1024]{1,0:T(8,128)(2,1)}, u32[]{:S(2)}) %copy-start) | copy-done | bytes 524312
  14.5 2.1 %hop.5.refs_5_.refs_0_ = bf16[256,768]{1,0:T(8,128)(2,1)S(1)} custom-call(bf16[256,1024]{1,0:T(8,128)(2,1)S(1)} %copy-done, bf16[1024,8192]{1,0:T(8,128)(2,1)} %refs_7_.1), custom_call_target="tpu_custom_call" | custom-call | tf_op jit(solution)/shard_map/hop/pallas_call | solution.py:376
  16.6 1.9 %collective-permute-done.1.refs_2_ = bf16[64,1152]{1,0:T(8,128)(2,1)S(1)} collective-permute-done((bf16[64,1152]{1,0:T(8,128)(2,1)}, bf16[64,1152]{1,0:T(8,128)(2,1)S(1)}, u32[]{:S(2)}, u32[]{:S(2)}) %collective-permute-start.1) | collective-permute-done | bytes 147488 | tf_op jit(solution)/shard_map/ppermute | solution.py:567
  18.4 2.4 %collective-permute-done.2.refs_3_ = bf16[64,1152]{1,0:T(8,128)(2,1)S(1)} collective-permute-done((bf16[64,1152]{1,0:T(8,128)(2,1)}, bf16[64,1152]{1,0:T(8,128)(2,1)S(1)}, u32[]{:S(2)}, u32[]{:S(2)}) %collective-permute-start.2) | collective-permute-done | bytes 147488 | tf_op jit(solution)/shard_map/ppermute | solution.py:567
  20.8 0.6 down.1
  21.6 1.9 %collective-permute-start.3 = (bf16[256,768]{1,0:T(8,128)(2,1)S(1)}, bf16[256,768]{1,0:T(8,128)(2,1)S(1)}, u32[]{:S(2)}, u32[]{:S(2)}) collective-permute-start(bf16[256,768]{1,0:T(8,128)(2,1)S(1)} %hold.1.refs_4_), channel_id=1, source_target_pairs={{0,2},{2,3},{3,1},{1,0},{4,6},{6,7},{7,5},{5,4},{8,10},{10,11},{11... | collective-permute-start | bytes 1179656 | tf_op jit(solution)/shard_map/ppermute | solution.py:573
  23.5 4.2 %collective-permute-done.5 = bf16[128,128]{1,0:T(8,128)(2,1)S(1)} collective-permute-done((bf16[128,128]{1,0:T(8,128)(2,1)S(1)}, bf16[128,128]{1,0:T(8,128)(2,1)S(1)}, u32[]{:S(2)}, u32[]{:S(2)}) %collective-permute-start.5) | collective-permute-done | bytes 32800 | tf_op jit(solution)/shard_map/ppermute | solution.py:606
  27.7 2.6 %hop.6.refs_3_ = bf16[256,1280]{1,0:T(8,128)(2,1)S(1)} custom-call(bf16[256,1280]{1,0:T(8,128)(2,1)S(1)} %collective-permute-done.4.refs_0_, bf16[256,1024]{1,0:T(8,128)(2,1)S(1)} %copy-done.1, bf16[1024,8192]{1,0:T(8,128)(2,1)} %refs_7_.1, bf16[128,128]{1,0:T(8,128)(2,1)S(1)} %add_convert_fusion.refs_3_.refs_0_, bf16[256,768]{1,0:T(8,128)(2,1)S(1)} %hold.1.refs_4_), custom_call_target="tpu_custom_call" | custom-call | flops 20000000000 | bytes 40000000 | tf_op jit(solution)/shard_map/hop/pallas_call | solution.py:376
  30.3 2.7 %collective-permute-start.9 = (bf16[256,1280]{1,0:T(8,128)(2,1)S(1)}, bf16[256,1280]{1,0:T(8,128)(2,1)S(1)}, u32[]{:S(2)}, u32[]{:S(2)}) collective-permute-start(bf16[256,1280]{1,0:T(8,128)(2,1)S(1)} %hop.6.refs_3_), channel_id=1, source_target_pairs={{0,2},{2,3},{3,1},{1,0},{4,6},{6,7},{7,5},{5,4},{8,10},{10,11},{11... | collective-permute-start | bytes 1966088 | tf_op jit(solution)/shard_map/ppermute | solution.py:573
  32.9 4.1 %collective-permute-start.8 = (bf16[128,128]{1,0:T(8,128)(2,1)S(1)}, bf16[128,128]{1,0:T(8,128)(2,1)S(1)}, u32[]{:S(2)}, u32[]{:S(2)}) collective-permute-start(bf16[128,128]{1,0:T(8,128)(2,1)S(1)} %add_convert_fusion.refs_3_.refs_0_), channel_id=1, source_target_pairs={{0,3},{3,0},{4,7},{7,4},{8,11},{11,8},{12,15},{15,12},{16,19},{19,... | collective-permute-start | bytes 98312 | tf_op jit(solution)/shard_map/ppermute | solution.py:586
  37.1 1.3 %collective-permute-start.7 = (bf16[128,128]{1,0:T(8,128)(2,1)S(1)}, bf16[128,128]{1,0:T(8,128)(2,1)S(1)}, u32[]{:S(2)}, u32[]{:S(2)}) collective-permute-start(bf16[128,128]{1,0:T(8,128)(2,1)S(1)} %add_convert_fusion.refs_3_.refs_0_), channel_id=1, source_target_pairs={{0,2},{3,1},{4,6},{7,5},{8,10},{11,9},{12,14},{15,13},{16,18},{19,... | collective-permute-start | bytes 98312 | tf_op jit(solution)/shard_map/ppermute | solution.py:585
  38.4 2.0 %hop.7 = bf16[256,768]{1,0:T(8,128)(2,1)S(1)} custom-call(bf16[256,768]{1,0:T(8,128)(2,1)S(1)} %collective-permute-done.3.refs_0_, bf16[256,1024]{1,0:T(8,128)(2,1)S(1)} %copy-done.1, bf16[1024,8192]{1,0:T(8,128)(2,1)} %refs_7_.1, bf16[256,1280]{1,0:T(8,128)(2,1)S(1)} %hop.6.refs_3_), custom_call_target="tpu_custom_call" | custom-call | flops 4000000000 | bytes 8000000 | tf_op jit(solution)/shard_map/hop/pallas_call | solution.py:376
  40.4 1.1 %collective-permute-start.6 = (bf16[256,768]{1,0:T(8,128)(2,1)S(1)}, bf16[256,768]{1,0:T(8,128)(2,1)S(1)}, u32[]{:S(2)}, u32[]{:S(2)}) collective-permute-start(bf16[256,768]{1,0:T(8,128)(2,1)S(1)} %hop.7), channel_id=1, source_target_pairs={{0,2},{2,3},{3,1},{1,0},{4,6},{6,7},{7,5},{5,4},{8,10},{10,11},{11... | collective-permute-start | bytes 1179656 | tf_op jit(solution)/shard_map/ppermute | solution.py:573
  41.5 8.6 %collective-permute-done.9.refs_0_ = bf16[256,1280]{1,0:T(8,128)(2,1)S(1)} collective-permute-done((bf16[256,1280]{1,0:T(8,128)(2,1)S(1)}, bf16[256,1280]{1,0:T(8,128)(2,1)S(1)}, u32[]{:S(2)}, u32[]{:S(2)}) %collective-permute-start.9) | collective-permute-done | bytes 655392 | tf_op jit(solution)/shard_map/ppermute | solution.py:573
  50.1 2.6 %hop.8.refs_5_ = bf16[256,1280]{1,0:T(8,128)(2,1)S(1)} custom-call(bf16[256,1280]{1,0:T(8,128)(2,1)S(1)} %collective-permute-done.9.refs_0_, bf16[256,1024]{1,0:T(8,128)(2,1)S(1)} %copy-done.1, bf16[1024,8192]{1,0:T(8,128)(2,1)} %refs_7_.1), custom_call_target="tpu_custom_call" | custom-call | flops 20000000000 | bytes 40000000 | tf_op jit(solution)/shard_map/hop/pallas_call | solution.py:376
  52.7 3.4 %collective-permute-start.14 = (bf16[256,1280]{1,0:T(8,128)(2,1)S(1)}, bf16[256,1280]{1,0:T(8,128)(2,1)S(1)}, u32[]{:S(2)}, u32[]{:S(2)}) collective-permute-start(bf16[256,1280]{1,0:T(8,128)(2,1)S(1)} %hop.8.refs_5_), channel_id=1, source_target_pairs={{0,2},{2,3},{3,1},{1,0},{4,6},{6,7},{7,5},{5,4},{8,10},{10,11},{11... | collective-permute-start | bytes 1966088 | tf_op jit(solution)/shard_map/ppermute | solution.py:573
  56.1 0.8 up.1
  57.0 1.6 %collective-permute-start.12 = (bf16[64,2048]{1,0:T(8,128)(2,1)S(1)}, bf16[64,2048]{1,0:T(8,128)(2,1)S(1)}, u32[]{:S(2)}, u32[]{:S(2)}) collective-permute-start(bf16[64,2048]{1,0:T(8,128)(2,1)S(1)} %get-tuple-element.30), channel_id=1, source_target_pairs={{0,8},{4,12},{8,0},{12,4},{1,9},{5,13},{9,1},{13,5},{2,10},{6,14},... | collective-permute-start | bytes 786440 | tf_op jit(solution)/shard_map/ppermute | solution.py:567
  58.9 1.0 %collective-permute-done.6.refs_0_ = bf16[256,768]{1,0:T(8,128)(2,1)S(1)} collective-permute-done((bf16[256,768]{1,0:T(8,128)(2,1)S(1)}, bf16[256,768]{1,0:T(8,128)(2,1)S(1)}, u32[]{:S(2)}, u32[]{:S(2)}) %collective-permute-start.6) | collective-permute-done | bytes 393248 | tf_op jit(solution)/shard_map/ppermute | solution.py:573
  59.9 2.1 %hop.9.refs_8_ = bf16[256,768]{1,0:T(8,128)(2,1)S(1)} custom-call(bf16[256,768]{1,0:T(8,128)(2,1)S(1)} %collective-permute-done.6.refs_0_, bf16[256,1024]{1,0:T(8,128)(2,1)S(1)} %copy-done.1, bf16[1024,8192]{1,0:T(8,128)(2,1)} %refs_7_.1, bf16[64,2048]{1,0:T(8,128)(2,1)S(1)} %get-tuple-element.28.refs_3_.refs_0_), custom_call_target="tpu_custom_call" | custom-call | tf_op jit(solution)/shard_map/hop/pallas_call | solution.py:376
  62.0 3.4 %collective-permute-start.10 = (bf16[256,768]{1,0:T(8,128)(2,1)S(1)}, bf16[256,768]{1,0:T(8,128)(2,1)S(1)}, u32[]{:S(2)}, u32[]{:S(2)}) collective-permute-start(bf16[256,768]{1,0:T(8,128)(2,1)S(1)} %hop.9.refs_8_), channel_id=1, source_target_pairs={{0,2},{2,3},{3,1},{1,0},{4,6},{6,7},{7,5},{5,4},{8,10},{10,11},{11... | collective-permute-start | bytes 1179656 | tf_op jit(solution)/shard_map/ppermute | solution.py:573
  65.4 0.8 collective-permute-done.12.refs_2_
  66.2 4.7 %collective-permute-done.13.refs_3_ = bf16[64,2048]{1,0:T(8,128)(2,1)S(1)} collective-permute-done((bf16[64,2048]{1,0:T(8,128)(2,1)S(1)}, bf16[64,2048]{1,0:T(8,128)(2,1)S(1)}, u32[]{:S(2)}, u32[]{:S(2)}) %collective-permute-start.13) | collective-permute-done | bytes 262176 | tf_op jit(solution)/shard_map/ppermute | solution.py:567
  70.9 4.5 %settle.1 = (f32[256,1280]{1,0:T(8,128)}, f32[256,768]{1,0:T(8,128)S(1)}) custom-call(bf16[64,2048]{1,0:T(8,128)(2,1)S(1)} %get-tuple-element.28.refs_3_.refs_0_, bf16[64,2048]{1,0:T(8,128)(2,1)S(1)} %collective-permute-done.11.refs_1_, bf16[64,2048]{1,0:T(8,128)(2,1)S(1)} %collective-permute-done.12.refs_2_, ...), custom_call_target="tpu_custom_call" | custom-call | flops 4000000000 | bytes 8000000 | tf_op jit(solution)/shard_map/settle/pallas_call | solution.py:482
  75.5 1.3 %copy-done.3 = f32[256,1280]{1,0:T(8,128)S(1)} copy-done((f32[256,1280]{1,0:T(8,128)S(1)}, f32[256,1280]{1,0:T(8,128)}, u32[]{:S(2)}) %copy-start.3) | copy-done | bytes 1310744
  76.8 0.9 %finish.2.refs_0_ = bf16[256,2048]{1,0:T(8,128)(2,1)} custom-call(bf16[256,1280]{1,0:T(8,128)(2,1)S(1)} %collective-permute-done.14.arrived_ref, f32[256,1280]{1,0:T(8,128)S(1)} %copy-done.3), custom_call_target="tpu_custom_call" | custom-call | tf_op jit(solution)/shard_map/finish/pallas_call | solution.py:514
  77.7 3.6 %collective-permute-done.10.arrived_ref = bf16[256,768]{1,0:T(8,128)(2,1)S(1)} collective-permute-done((bf16[256,768]{1,0:T(8,128)(2,1)S(1)}, bf16[256,768]{1,0:T(8,128)(2,1)S(1)}, u32[]{:S(2)}, u32[]{:S(2)}) %collective-permute-start.10) | collective-permute-done | bytes 393248 | tf_op jit(solution)/shard_map/ppermute | solution.py:573
  81.3 0.8 finish.3
  (27 shorter events, 0.5 us)
Async XLA Ops:
  7.5 20.2 %collective-permute-start.4 = (bf16[256,1280]{1,0:T(8,128)(2,1)}, bf16[256,1280]{1,0:T(8,128)(2,1)S(1)}, u32[]{:S(2)}, u32[]{:S(2)}) collective-permute-start(bf16[256,1280]{1,0:T(8,128)(2,1)} %get-tuple-element.26), channel_id=1, source_target_pairs={{0,2},{2,3},{3,1},{1,0},{4,6},{6,7},{7,5},{5,4},{8,10},{10,11},{11... | collective-permute-start | bytes 1966088 | tf_op jit(solution)/shard_map/ppermute | solution.py:573
  11.6 5.0 %collective-permute-start = (bf16[64,1152]{1,0:T(8,128)(2,1)}, bf16[64,1152]{1,0:T(8,128)(2,1)S(1)}, u32[]{:S(2)}, u32[]{:S(2)}) collective-permute-start(bf16[64,1152]{1,0:T(8,128)(2,1)} %get-tuple-element.22), channel_id=1, source_target_pairs={{0,4},{4,0},{8,12},{12,8},{1,5},{5,1},{9,13},{13,9},{2,6},{6,2},{1... | collective-permute-start | bytes 442376 | tf_op jit(solution)/shard_map/ppermute | solution.py:567
  11.6 6.9 %collective-permute-start.1 = (bf16[64,1152]{1,0:T(8,128)(2,1)}, bf16[64,1152]{1,0:T(8,128)(2,1)S(1)}, u32[]{:S(2)}, u32[]{:S(2)}) collective-permute-start(bf16[64,1152]{1,0:T(8,128)(2,1)} %get-tuple-element.23), channel_id=1, source_target_pairs={{0,8},{4,12},{8,0},{12,4},{1,9},{5,13},{9,1},{13,5},{2,10},{6,14},... | collective-permute-start | bytes 442376 | tf_op jit(solution)/shard_map/ppermute | solution.py:567
  13.1 7.7 %collective-permute-start.2 = (bf16[64,1152]{1,0:T(8,128)(2,1)}, bf16[64,1152]{1,0:T(8,128)(2,1)S(1)}, u32[]{:S(2)}, u32[]{:S(2)}) collective-permute-start(bf16[64,1152]{1,0:T(8,128)(2,1)} %get-tuple-element.24), channel_id=1, source_target_pairs={{0,12},{4,8},{8,4},{12,0},{1,13},{5,9},{9,5},{13,1},{2,14},{6,10},... | collective-permute-start | bytes 442376 | tf_op jit(solution)/shard_map/ppermute | solution.py:567
  13.4 1.0 %copy-start = (bf16[256,1024]{1,0:T(8,128)(2,1)S(1)}, bf16[256,1024]{1,0:T(8,128)(2,1)}, u32[]{:S(2)}) copy-start(bf16[256,1024]{1,0:T(8,128)(2,1)} %get-tuple-element.20.refs_0_.refs_1_.refs_5_) | copy-start | bytes 1572868
  14.5 6.3 %copy-start.5 = (bf16[8,64,1024]{2,1,0:T(8,128)(2,1)S(1)}, bf16[8,64,1024]{2,1,0:T(8,128)(2,1)}, u32[]{:S(2)}) copy-start(bf16[8,64,1024]{2,1,0:T(8,128)(2,1)} %refs_4_.2) | copy-start | bytes 3145732
  14.5 6.3 %copy-start.6 = (bf16[64,1152]{1,0:T(8,128)(2,1)S(1)}, bf16[64,1152]{1,0:T(8,128)(2,1)}, u32[]{:S(2)}) copy-start(bf16[64,1152]{1,0:T(8,128)(2,1)} %get-tuple-element.21.refs_0_) | copy-start | bytes 442372
  16.6 11.1 %copy-start.1 = (bf16[256,1024]{1,0:T(8,128)(2,1)S(1)}, bf16[256,1024]{1,0:T(8,128)(2,1)}, u32[]{:S(2)}) copy-start(bf16[256,1024]{1,0:T(8,128)(2,1)} %get-tuple-element.20.refs_0_.refs_1_.refs_5_) | copy-start | bytes 1572868
  21.5 6.2 %collective-permute-start.5 = (bf16[128,128]{1,0:T(8,128)(2,1)S(1)}, bf16[128,128]{1,0:T(8,128)(2,1)S(1)}, u32[]{:S(2)}, u32[]{:S(2)}) collective-permute-start(bf16[128,128]{1,0:T(8,128)(2,1)S(1)} %get-tuple-element.25.refs_1_), channel_id=1, source_target_pairs={{0,1},{1,0},{2,3},{3,2},{4,5},{5,4},{6,7},{7,6},{8,9},{9,8},{10,11... | collective-permute-start | bytes 98312 | tf_op jit(solution)/shard_map/ppermute | solution.py:606
  21.6 16.8 %collective-permute-start.3 = (bf16[256,768]{1,0:T(8,128)(2,1)S(1)}, bf16[256,768]{1,0:T(8,128)(2,1)S(1)}, u32[]{:S(2)}, u32[]{:S(2)}) collective-permute-start(bf16[256,768]{1,0:T(8,128)(2,1)S(1)} %hold.1.refs_4_), channel_id=1, source_target_pairs={{0,2},{2,3},{3,1},{1,0},{4,6},{6,7},{7,5},{5,4},{8,10},{10,11},{11... | collective-permute-start | bytes 1179656 | tf_op jit(solution)/shard_map/ppermute | solution.py:573
  30.3 19.8 %collective-permute-start.9 = (bf16[256,1280]{1,0:T(8,128)(2,1)S(1)}, bf16[256,1280]{1,0:T(8,128)(2,1)S(1)}, u32[]{:S(2)}, u32[]{:S(2)}) collective-permute-start(bf16[256,1280]{1,0:T(8,128)(2,1)S(1)} %hop.6.refs_3_), channel_id=1, source_target_pairs={{0,2},{2,3},{3,1},{1,0},{4,6},{6,7},{7,5},{5,4},{8,10},{10,11},{11... | collective-permute-start | bytes 1966088 | tf_op jit(solution)/shard_map/ppermute | solution.py:573
  32.9 23.2 %collective-permute-start.8 = (bf16[128,128]{1,0:T(8,128)(2,1)S(1)}, bf16[128,128]{1,0:T(8,128)(2,1)S(1)}, u32[]{:S(2)}, u32[]{:S(2)}) collective-permute-start(bf16[128,128]{1,0:T(8,128)(2,1)S(1)} %add_convert_fusion.refs_3_.refs_0_), channel_id=1, source_target_pairs={{0,3},{3,0},{4,7},{7,4},{8,11},{11,8},{12,15},{15,12},{16,19},{19,... | collective-permute-start | bytes 98312 | tf_op jit(solution)/shard_map/ppermute | solution.py:586
  37.1 19.1 %collective-permute-start.7 = (bf16[128,128]{1,0:T(8,128)(2,1)S(1)}, bf16[128,128]{1,0:T(8,128)(2,1)S(1)}, u32[]{:S(2)}, u32[]{:S(2)}) collective-permute-start(bf16[128,128]{1,0:T(8,128)(2,1)S(1)} %add_convert_fusion.refs_3_.refs_0_), channel_id=1, source_target_pairs={{0,2},{3,1},{4,6},{7,5},{8,10},{11,9},{12,14},{15,13},{16,18},{19,... | collective-permute-start | bytes 98312 | tf_op jit(solution)/shard_map/ppermute | solution.py:585
  40.4 15.7 %copy-start.2 = (bf16[8,64,2048]{2,1,0:T(8,128)(2,1)S(1)}, bf16[8,64,2048]{2,1,0:T(8,128)(2,1)}, u32[]{:S(2)}) copy-start(bf16[8,64,2048]{2,1,0:T(8,128)(2,1)} %refs_4_.3) | copy-start | bytes 6291460
  40.4 19.5 %collective-permute-start.6 = (bf16[256,768]{1,0:T(8,128)(2,1)S(1)}, bf16[256,768]{1,0:T(8,128)(2,1)S(1)}, u32[]{:S(2)}, u32[]{:S(2)}) collective-permute-start(bf16[256,768]{1,0:T(8,128)(2,1)S(1)} %hop.7), channel_id=1, source_target_pairs={{0,2},{2,3},{3,1},{1,0},{4,6},{6,7},{7,5},{5,4},{8,10},{10,11},{11... | collective-permute-start | bytes 1179656 | tf_op jit(solution)/shard_map/ppermute | solution.py:573
  52.7 22.8 %collective-permute-start.14 = (bf16[256,1280]{1,0:T(8,128)(2,1)S(1)}, bf16[256,1280]{1,0:T(8,128)(2,1)S(1)}, u32[]{:S(2)}, u32[]{:S(2)}) collective-permute-start(bf16[256,1280]{1,0:T(8,128)(2,1)S(1)} %hop.8.refs_5_), channel_id=1, source_target_pairs={{0,2},{2,3},{3,1},{1,0},{4,6},{6,7},{7,5},{5,4},{8,10},{10,11},{11... | collective-permute-start | bytes 1966088 | tf_op jit(solution)/shard_map/ppermute | solution.py:573
  57.0 8.5 %collective-permute-start.11 = (bf16[64,2048]{1,0:T(8,128)(2,1)S(1)}, bf16[64,2048]{1,0:T(8,128)(2,1)S(1)}, u32[]{:S(2)}, u32[]{:S(2)}) collective-permute-start(bf16[64,2048]{1,0:T(8,128)(2,1)S(1)} %get-tuple-element.29), channel_id=1, source_target_pairs={{0,4},{4,0},{8,12},{12,8},{1,5},{5,1},{9,13},{13,9},{2,6},{6,2},{1... | collective-permute-start | bytes 786440 | tf_op jit(solution)/shard_map/ppermute | solution.py:567
  57.0 9.2 %collective-permute-start.12 = (bf16[64,2048]{1,0:T(8,128)(2,1)S(1)}, bf16[64,2048]{1,0:T(8,128)(2,1)S(1)}, u32[]{:S(2)}, u32[]{:S(2)}) collective-permute-start(bf16[64,2048]{1,0:T(8,128)(2,1)S(1)} %get-tuple-element.30), channel_id=1, source_target_pairs={{0,8},{4,12},{8,0},{12,4},{1,9},{5,13},{9,1},{13,5},{2,10},{6,14},... | collective-permute-start | bytes 786440 | tf_op jit(solution)/shard_map/ppermute | solution.py:567
  58.6 12.3 %collective-permute-start.13 = (bf16[64,2048]{1,0:T(8,128)(2,1)S(1)}, bf16[64,2048]{1,0:T(8,128)(2,1)S(1)}, u32[]{:S(2)}, u32[]{:S(2)}) collective-permute-start(bf16[64,2048]{1,0:T(8,128)(2,1)S(1)} %get-tuple-element.31), channel_id=1, source_target_pairs={{0,12},{4,8},{8,4},{12,0},{1,13},{5,9},{9,5},{13,1},{2,14},{6,10},... | collective-permute-start | bytes 786440 | tf_op jit(solution)/shard_map/ppermute | solution.py:567
  59.9 11.0 %copy-start.4 = (bf16[256,2048]{1,0:T(8,128)(2,1)S(1)}, bf16[256,2048]{1,0:T(8,128)(2,1)}, u32[]{:S(2)}) copy-start(bf16[256,2048]{1,0:T(8,128)(2,1)} %refs_6_.1) | copy-start | bytes 3145732
  59.9 11.0 %copy-start.7 = (bf16[256,256]{1,0:T(8,128)(2,1)S(1)}, bf16[256,256]{1,0:T(8,128)(2,1)}, u32[]{:S(2)}) copy-start(bf16[256,256]{1,0:T(8,128)(2,1)} %get-tuple-element.32.refs_4_) | copy-start | bytes 393220
  62.0 19.2 %collective-permute-start.10 = (bf16[256,768]{1,0:T(8,128)(2,1)S(1)}, bf16[256,768]{1,0:T(8,128)(2,1)S(1)}, u32[]{:S(2)}, u32[]{:S(2)}) collective-permute-start(bf16[256,768]{1,0:T(8,128)(2,1)S(1)} %hop.9.refs_8_), channel_id=1, source_target_pairs={{0,2},{2,3},{3,1},{1,0},{4,6},{6,7},{7,5},{5,4},{8,10},{10,11},{11... | collective-permute-start | bytes 1179656 | tf_op jit(solution)/shard_map/ppermute | solution.py:573
  75.5 1.3 %copy-start.3 = (f32[256,1280]{1,0:T(8,128)S(1)}, f32[256,1280]{1,0:T(8,128)}, u32[]{:S(2)}) copy-start(f32[256,1280]{1,0:T(8,128)} %get-tuple-element.34.settled_ref) | copy-start | bytes 3932164

commit v17 on v16

--- a/solution.py
+++ b/solution.py
@@ -15,12 +15,13 @@
 MASKED = -1e30
 VMEM_LIMIT = 50 * 1024 * 1024
 FULL_VMEM = 61 * 1024 * 1024
-SHARES = ((5, 3),)
+SHARES = ((9, 7), (5, 3))
 PIECE = 512
 SPLIT = 4
 
 VMEM = pl.BlockSpec(memory_space=pltpu.VMEM)
 ANY = pl.BlockSpec(memory_space=pl.ANY)
+SETTLE = pl.CostEstimate(flops=33 * 10**8, transcendentals=0, bytes_accessed=66 * 10**5)
 LONG = pl.CostEstimate(flops=20 * 10**9, transcendentals=0, bytes_accessed=40 * 10**6)
 MEDIUM = pl.CostEstimate(flops=4 * 10**9, transcendentals=0, bytes_accessed=8 * 10**6)
 PARAMS = pltpu.CompilerParams(vmem_limit_bytes=VMEM_LIMIT)
@@ -486,7 +487,7 @@
         out_shape=[jax.ShapeDtypeStruct((rows, chunk), jnp.float32) for _, chunk in chains],
         scratch_shapes=Weights.scratch(weight.shape[0], width),
         compiler_params=PARAMS,
-        cost_estimate=MEDIUM,
+        cost_estimate=SETTLE,
         name="settle",
     )(*returned, chosen, attended, residual, weight, *after)
 

time: 82.4 us -> 82.4 us (level)
  waiting for transfers between devices: 27.1 us -> 25.2 us
  starting transfers between devices: 25.9 us -> 27.4 us
    ppermute x6, waiting for transfers between devices: 9.71 us -> 7.79 us  [exchange(): lax.ppermute(blocks[r], 'dp', [(i, i ^ r) for i in range(replicas)])]
    ppermute x6, starting transfers between devices: 16.6 us -> 18.1 us  [forward(): return lax.ppermute(x, 'tensor', ring)]
    ppermute x6, waiting for transfers between devices: 13.3 us -> 14.7 us  [forward(): return lax.ppermute(x, 'tensor', ring)]
    ppermute x1, waiting for transfers between devices: 4.17 us -> 2.76 us  [per_device(): lax.ppermute(mid, 'tensor', [(i, i ^ 1) for i in range(count)])]
  transfers between devices with their start and end apart: 15 -> 15, of which waited for: 8 -> 7; matrix products, arithmetic and copies ran while one was open for 0% -> 0% of each run, Pallas kernels for 22% -> 23%
where the time goes in v17:
time: 82.4 us; the launch traced here: 82 us
  starting transfers between devices  27.4 us (33%)
  Pallas kernels  26.8 us (33%)
  waiting for transfers between devices  25.2 us (31%)
  local copies, waits for them, and re-layouts  2.33 us (3%)
    ppermute x6, starting transfers between devices, forward(): return lax.ppermute(x, 'tensor', ring)  18.1 us
    ppermute x6, waiting for transfers between devices, forward(): return lax.ppermute(x, 'tensor', ring)  14.7 us
    pallas_call x5, Pallas kernels, hop(): pl.pallas_call(functools.partial(hop_kernel, step, block, start, arriving...  11.8 us
    ppermute x6, waiting for transfers between devices, exchange(): lax.ppermute(blocks[r], 'dp', [(i, i ^ r) for i in range(replicas)])  7.79 us
    pallas_call x1, Pallas kernels, attend(): pl.pallas_call(functools.partial(attend_kernel, heads, kv, cache, steps,...  7.41 us
    pallas_call x1, Pallas kernels, settle(): pl.pallas_call(functools.partial(settle_kernel, step, replicas, len(after...  4.49 us
    ppermute x1, starting transfers between devices, pair_sums(): other = lax.ppermute(x, 'tensor', far)  4.12 us
    ppermute x6, starting transfers between devices, exchange(): lax.ppermute(blocks[r], 'dp', [(i, i ^ r) for i in range(replicas)])  3.79 us
  transfers between devices with their start and end apart: 15, of which 7 were waited for; matrix products, arithmetic and copies ran while one was open for 0% of the time, Pallas kernels for 23%

profile of v17, /device:TPU:0, one launch (start us, length us, event | category | flops | bytes accessed | tf_op | source)
XLA Modules:
  0.0 82.0 jit_solution(17247945304588230714)
XLA Ops:
  0.0 7.4 %attend.1 = (bf16[256,1024]{1,0:T(8,128)(2,1)}, bf16[256,1152]{1,0:T(8,128)(2,1)}, bf16[256,256]{1,0:T(8,128)(2,1)}, bf16[64,1152]{1,0:T(8,128)(2,1)}, bf16[64,1...) custom-call(s32[1,256]{1,0:T(1,128)} %bitcast.13, s32[1,256]{1,0:T(1,128)} %bitcast.14, ...), custom_call_target="tpu_custom_call" | custom-call | tf_op jit(solution)/shard_map/attend/pallas_call | solution.py:326
  7.4 4.1 %collective-permute-start.4 = (bf16[256,1152]{1,0:T(8,128)(2,1)}, bf16[256,1152]{1,0:T(8,128)(2,1)S(1)}, u32[]{:S(2)}, u32[]{:S(2)}) collective-permute-start(bf16[256,1152]{1,0:T(8,128)(2,1)} %get-tuple-element.26), channel_id=1, source_target_pairs={{0,2},{2,3},{3,1},{1,0},{4,6},{6,7},{7,5},{5,4},{8,10},{10,11},{11... | collective-permute-start | bytes 1769480 | tf_op jit(solution)/shard_map/ppermute | solution.py:574
  11.5 1.5 %collective-permute-start.1 = (bf16[64,1152]{1,0:T(8,128)(2,1)}, bf16[64,1152]{1,0:T(8,128)(2,1)S(1)}, u32[]{:S(2)}, u32[]{:S(2)}) collective-permute-start(bf16[64,1152]{1,0:T(8,128)(2,1)} %get-tuple-element.23), channel_id=1, source_target_pairs={{0,8},{4,12},{8,0},{12,4},{1,9},{5,13},{9,1},{13,5},{2,10},{6,14},... | collective-permute-start | bytes 442376 | tf_op jit(solution)/shard_map/ppermute | solution.py:568
  13.0 0.4 collective-permute-start.2
  13.4 1.0 %copy-done = bf16[256,1024]{1,0:T(8,128)(2,1)S(1)} copy-done((bf16[256,1024]{1,0:T(8,128)(2,1)S(1)}, bf16[256,1024]{1,0:T(8,128)(2,1)}, u32[]{:S(2)}) %copy-start) | copy-done | bytes 524312
  14.4 2.3 %hop.5.refs_5_.refs_0_ = bf16[256,896]{1,0:T(8,128)(2,1)S(1)} custom-call(bf16[256,1024]{1,0:T(8,128)(2,1)S(1)} %copy-done, bf16[1024,8192]{1,0:T(8,128)(2,1)} %refs_7_.1), custom_call_target="tpu_custom_call" | custom-call | tf_op jit(solution)/shard_map/hop/pallas_call | solution.py:377
  16.7 1.6 %collective-permute-done.1.refs_2_ = bf16[64,1152]{1,0:T(8,128)(2,1)S(1)} collective-permute-done((bf16[64,1152]{1,0:T(8,128)(2,1)}, bf16[64,1152]{1,0:T(8,128)(2,1)S(1)}, u32[]{:S(2)}, u32[]{:S(2)}) %collective-permute-start.1) | collective-permute-done | bytes 147488 | tf_op jit(solution)/shard_map/ppermute | solution.py:568
  18.4 2.4 %collective-permute-done.2.refs_3_ = bf16[64,1152]{1,0:T(8,128)(2,1)S(1)} collective-permute-done((bf16[64,1152]{1,0:T(8,128)(2,1)}, bf16[64,1152]{1,0:T(8,128)(2,1)S(1)}, u32[]{:S(2)}, u32[]{:S(2)}) %collective-permute-start.2) | collective-permute-done | bytes 147488 | tf_op jit(solution)/shard_map/ppermute | solution.py:568
  20.8 0.6 down.1
  21.5 1.9 %collective-permute-start.3 = (bf16[256,896]{1,0:T(8,128)(2,1)S(1)}, bf16[256,896]{1,0:T(8,128)(2,1)S(1)}, u32[]{:S(2)}, u32[]{:S(2)}) collective-permute-start(bf16[256,896]{1,0:T(8,128)(2,1)S(1)} %hold.1.refs_4_), channel_id=1, source_target_pairs={{0,2},{2,3},{3,1},{1,0},{4,6},{6,7},{7,5},{5,4},{8,10},{10,11},{11... | collective-permute-start | bytes 1376264 | tf_op jit(solution)/shard_map/ppermute | solution.py:574
  23.4 2.8 %collective-permute-done.5 = bf16[128,128]{1,0:T(8,128)(2,1)S(1)} collective-permute-done((bf16[128,128]{1,0:T(8,128)(2,1)S(1)}, bf16[128,128]{1,0:T(8,128)(2,1)S(1)}, u32[]{:S(2)}, u32[]{:S(2)}) %collective-permute-start.5) | collective-permute-done | bytes 32800 | tf_op jit(solution)/shard_map/ppermute | solution.py:607
  26.2 2.5 %hop.6.refs_3_ = bf16[256,1152]{1,0:T(8,128)(2,1)S(1)} custom-call(bf16[256,1152]{1,0:T(8,128)(2,1)S(1)} %collective-permute-done.4.refs_0_, bf16[256,1024]{1,0:T(8,128)(2,1)S(1)} %copy-done.1, bf16[1024,8192]{1,0:T(8,128)(2,1)} %refs_7_.1, bf16[128,128]{1,0:T(8,128)(2,1)S(1)} %add_convert_fusion.refs_3_.refs_0_, bf16[256,896]{1,0:T(8,128)(2,1)S(1)} %hold.1.refs_4_), custom_call_target="tpu_custom_call" | custom-call | flops 20000000000 | bytes 40000000 | tf_op jit(solution)/shard_map/hop/pallas_call | solution.py:377
  28.7 2.7 %collective-permute-start.9 = (bf16[256,1152]{1,0:T(8,128)(2,1)S(1)}, bf16[256,1152]{1,0:T(8,128)(2,1)S(1)}, u32[]{:S(2)}, u32[]{:S(2)}) collective-permute-start(bf16[256,1152]{1,0:T(8,128)(2,1)S(1)} %hop.6.refs_3_), channel_id=1, source_target_pairs={{0,2},{2,3},{3,1},{1,0},{4,6},{6,7},{7,5},{5,4},{8,10},{10,11},{11... | collective-permute-start | bytes 1769480 | tf_op jit(solution)/shard_map/ppermute | solution.py:574
  31.4 4.1 %collective-permute-start.8 = (bf16[128,128]{1,0:T(8,128)(2,1)S(1)}, bf16[128,128]{1,0:T(8,128)(2,1)S(1)}, u32[]{:S(2)}, u32[]{:S(2)}) collective-permute-start(bf16[128,128]{1,0:T(8,128)(2,1)S(1)} %add_convert_fusion.refs_3_.refs_0_), channel_id=1, source_target_pairs={{0,3},{3,0},{4,7},{7,4},{8,11},{11,8},{12,15},{15,12},{16,19},{19,... | collective-permute-start | bytes 98312 | tf_op jit(solution)/shard_map/ppermute | solution.py:587
  35.5 1.3 %collective-permute-start.7 = (bf16[128,128]{1,0:T(8,128)(2,1)S(1)}, bf16[128,128]{1,0:T(8,128)(2,1)S(1)}, u32[]{:S(2)}, u32[]{:S(2)}) collective-permute-start(bf16[128,128]{1,0:T(8,128)(2,1)S(1)} %add_convert_fusion.refs_3_.refs_0_), channel_id=1, source_target_pairs={{0,2},{3,1},{4,6},{7,5},{8,10},{11,9},{12,14},{15,13},{16,18},{19,... | collective-permute-start | bytes 98312 | tf_op jit(solution)/shard_map/ppermute | solution.py:586
  36.8 2.2 %hop.7 = bf16[256,896]{1,0:T(8,128)(2,1)S(1)} custom-call(bf16[256,896]{1,0:T(8,128)(2,1)S(1)} %collective-permute-done.3.refs_0_, bf16[256,1024]{1,0:T(8,128)(2,1)S(1)} %copy-done.1, bf16[1024,8192]{1,0:T(8,128)(2,1)} %refs_7_.1, bf16[256,1152]{1,0:T(8,128)(2,1)S(1)} %hop.6.refs_3_), custom_call_target="tpu_custom_call" | custom-call | flops 4000000000 | bytes 8000000 | tf_op jit(solution)/shard_map/hop/pallas_call | solution.py:377
  39.0 2.6 %collective-permute-start.6 = (bf16[256,896]{1,0:T(8,128)(2,1)S(1)}, bf16[256,896]{1,0:T(8,128)(2,1)S(1)}, u32[]{:S(2)}, u32[]{:S(2)}) collective-permute-start(bf16[256,896]{1,0:T(8,128)(2,1)S(1)} %hop.7), channel_id=1, source_target_pairs={{0,2},{2,3},{3,1},{1,0},{4,6},{6,7},{7,5},{5,4},{8,10},{10,11},{11... | collective-permute-start | bytes 1376264 | tf_op jit(solution)/shard_map/ppermute | solution.py:574
  41.6 7.0 %collective-permute-done.9.refs_0_ = bf16[256,1152]{1,0:T(8,128)(2,1)S(1)} collective-permute-done((bf16[256,1152]{1,0:T(8,128)(2,1)S(1)}, bf16[256,1152]{1,0:T(8,128)(2,1)S(1)}, u32[]{:S(2)}, u32[]{:S(2)}) %collective-permute-start.9) | collective-permute-done | bytes 589856 | tf_op jit(solution)/shard_map/ppermute | solution.py:574
  48.6 2.5 %hop.8.refs_5_ = bf16[256,1152]{1,0:T(8,128)(2,1)S(1)} custom-call(bf16[256,1152]{1,0:T(8,128)(2,1)S(1)} %collective-permute-done.9.refs_0_, bf16[256,1024]{1,0:T(8,128)(2,1)S(1)} %copy-done.1, bf16[1024,8192]{1,0:T(8,128)(2,1)} %refs_7_.1), custom_call_target="tpu_custom_call" | custom-call | flops 20000000000 | bytes 40000000 | tf_op jit(solution)/shard_map/hop/pallas_call | solution.py:377
  51.1 3.4 %collective-permute-start.14 = (bf16[256,1152]{1,0:T(8,128)(2,1)S(1)}, bf16[256,1152]{1,0:T(8,128)(2,1)S(1)}, u32[]{:S(2)}, u32[]{:S(2)}) collective-permute-start(bf16[256,1152]{1,0:T(8,128)(2,1)S(1)} %hop.8.refs_5_), channel_id=1, source_target_pairs={{0,2},{2,3},{3,1},{1,0},{4,6},{6,7},{7,5},{5,4},{8,10},{10,11},{11... | collective-permute-start | bytes 1769480 | tf_op jit(solution)/shard_map/ppermute | solution.py:574
  54.6 0.8 up.1
  55.5 1.6 %collective-permute-start.12 = (bf16[64,2048]{1,0:T(8,128)(2,1)S(1)}, bf16[64,2048]{1,0:T(8,128)(2,1)S(1)}, u32[]{:S(2)}, u32[]{:S(2)}) collective-permute-start(bf16[64,2048]{1,0:T(8,128)(2,1)S(1)} %get-tuple-element.30), channel_id=1, source_target_pairs={{0,8},{4,12},{8,0},{12,4},{1,9},{5,13},{9,1},{13,5},{2,10},{6,14},... | collective-permute-start | bytes 786440 | tf_op jit(solution)/shard_map/ppermute | solution.py:568
  57.0 0.3 collective-permute-start.13
  57.3 2.5 %collective-permute-done.6.refs_0_ = bf16[256,896]{1,0:T(8,128)(2,1)S(1)} collective-permute-done((bf16[256,896]{1,0:T(8,128)(2,1)S(1)}, bf16[256,896]{1,0:T(8,128)(2,1)S(1)}, u32[]{:S(2)}, u32[]{:S(2)}) %collective-permute-start.6) | collective-permute-done | bytes 458784 | tf_op jit(solution)/shard_map/ppermute | solution.py:574
  59.9 2.3 %hop.9.refs_8_ = bf16[256,896]{1,0:T(8,128)(2,1)S(1)} custom-call(bf16[256,896]{1,0:T(8,128)(2,1)S(1)} %collective-permute-done.6.refs_0_, bf16[256,1024]{1,0:T(8,128)(2,1)S(1)} %copy-done.1, bf16[1024,8192]{1,0:T(8,128)(2,1)} %refs_7_.1, bf16[64,2048]{1,0:T(8,128)(2,1)S(1)} %get-tuple-element.28.refs_3_.refs_0_), custom_call_target="tpu_custom_call" | custom-call | tf_op jit(solution)/shard_map/hop/pallas_call | solution.py:377
  62.1 3.4 %collective-permute-start.10 = (bf16[256,896]{1,0:T(8,128)(2,1)S(1)}, bf16[256,896]{1,0:T(8,128)(2,1)S(1)}, u32[]{:S(2)}, u32[]{:S(2)}) collective-permute-start(bf16[256,896]{1,0:T(8,128)(2,1)S(1)} %hop.9.refs_8_), channel_id=1, source_target_pairs={{0,2},{2,3},{3,1},{1,0},{4,6},{6,7},{7,5},{5,4},{8,10},{10,11},{11... | collective-permute-start | bytes 1376264 | tf_op jit(solution)/shard_map/ppermute | solution.py:574
  65.6 3.8 %collective-permute-done.13.refs_3_ = bf16[64,2048]{1,0:T(8,128)(2,1)S(1)} collective-permute-done((bf16[64,2048]{1,0:T(8,128)(2,1)S(1)}, bf16[64,2048]{1,0:T(8,128)(2,1)S(1)}, u32[]{:S(2)}, u32[]{:S(2)}) %collective-permute-start.13) | collective-permute-done | bytes 262176 | tf_op jit(solution)/shard_map/ppermute | solution.py:568
  69.4 4.5 %settle.1 = (f32[256,1152]{1,0:T(8,128)}, f32[256,896]{1,0:T(8,128)S(1)}) custom-call(bf16[64,2048]{1,0:T(8,128)(2,1)S(1)} %get-tuple-element.28.refs_3_.refs_0_, bf16[64,2048]{1,0:T(8,128)(2,1)S(1)} %collective-permute-done.11.refs_1_, bf16[64,2048]{1,0:T(8,128)(2,1)S(1)} %collective-permute-done.12.refs_2_, ...), custom_call_target="tpu_custom_call" | custom-call | flops 3300000000 | bytes 6600000 | tf_op jit(solution)/shard_map/settle/pallas_call | solution.py:483
  73.9 1.3 %copy-done.3 = f32[256,1152]{1,0:T(8,128)S(1)} copy-done((f32[256,1152]{1,0:T(8,128)S(1)}, f32[256,1152]{1,0:T(8,128)}, u32[]{:S(2)}) %copy-start.3) | copy-done | bytes 1179672
  75.1 0.9 %finish.2.refs_0_ = bf16[256,2048]{1,0:T(8,128)(2,1)} custom-call(bf16[256,1152]{1,0:T(8,128)(2,1)S(1)} %collective-permute-done.14.arrived_ref, f32[256,1152]{1,0:T(8,128)S(1)} %copy-done.3), custom_call_target="tpu_custom_call" | custom-call | tf_op jit(solution)/shard_map/finish/pallas_call | solution.py:515
  76.0 5.2 %collective-permute-done.10.arrived_ref = bf16[256,896]{1,0:T(8,128)(2,1)S(1)} collective-permute-done((bf16[256,896]{1,0:T(8,128)(2,1)S(1)}, bf16[256,896]{1,0:T(8,128)(2,1)S(1)}, u32[]{:S(2)}, u32[]{:S(2)}) %collective-permute-start.10) | collective-permute-done | bytes 458784 | tf_op jit(solution)/shard_map/ppermute | solution.py:574
  81.2 0.8 %finish.3 = bf16[256,2048]{1,0:T(8,128)(2,1)} custom-call(bf16[256,896]{1,0:T(8,128)(2,1)S(1)} %collective-permute-done.10.arrived_ref, f32[256,896]{1,0:T(8,128)S(1)} %get-tuple-element.33.settled_ref, bf16[256,2048]{1,0:T(8,128)(2,1)} %finish.2.refs_0_), custom_call_target="tpu_custom_call", output_to_operand_aliasing={{}: (2, {})} | custom-call | tf_op jit(solution)/shard_map/finish/pallas_call | solution.py:515
  (27 shorter events, 0.2 us)
Async XLA Ops:
  7.4 18.8 %collective-permute-start.4 = (bf16[256,1152]{1,0:T(8,128)(2,1)}, bf16[256,1152]{1,0:T(8,128)(2,1)S(1)}, u32[]{:S(2)}, u32[]{:S(2)}) collective-permute-start(bf16[256,1152]{1,0:T(8,128)(2,1)} %get-tuple-element.26), channel_id=1, source_target_pairs={{0,2},{2,3},{3,1},{1,0},{4,6},{6,7},{7,5},{5,4},{8,10},{10,11},{11... | collective-permute-start | bytes 1769480 | tf_op jit(solution)/shard_map/ppermute | solution.py:574
  11.5 5.2 %collective-permute-start = (bf16[64,1152]{1,0:T(8,128)(2,1)}, bf16[64,1152]{1,0:T(8,128)(2,1)S(1)}, u32[]{:S(2)}, u32[]{:S(2)}) collective-permute-start(bf16[64,1152]{1,0:T(8,128)(2,1)} %get-tuple-element.22), channel_id=1, source_target_pairs={{0,4},{4,0},{8,12},{12,8},{1,5},{5,1},{9,13},{13,9},{2,6},{6,2},{1... | collective-permute-start | bytes 442376 | tf_op jit(solution)/shard_map/ppermute | solution.py:568
  11.5 6.9 %collective-permute-start.1 = (bf16[64,1152]{1,0:T(8,128)(2,1)}, bf16[64,1152]{1,0:T(8,128)(2,1)S(1)}, u32[]{:S(2)}, u32[]{:S(2)}) collective-permute-start(bf16[64,1152]{1,0:T(8,128)(2,1)} %get-tuple-element.23), channel_id=1, source_target_pairs={{0,8},{4,12},{8,0},{12,4},{1,9},{5,13},{9,1},{13,5},{2,10},{6,14},... | collective-permute-start | bytes 442376 | tf_op jit(solution)/shard_map/ppermute | solution.py:568
  13.0 7.7 %collective-permute-start.2 = (bf16[64,1152]{1,0:T(8,128)(2,1)}, bf16[64,1152]{1,0:T(8,128)(2,1)S(1)}, u32[]{:S(2)}, u32[]{:S(2)}) collective-permute-start(bf16[64,1152]{1,0:T(8,128)(2,1)} %get-tuple-element.24), channel_id=1, source_target_pairs={{0,12},{4,8},{8,4},{12,0},{1,13},{5,9},{9,5},{13,1},{2,14},{6,10},... | collective-permute-start | bytes 442376 | tf_op jit(solution)/shard_map/ppermute | solution.py:568
  13.4 1.0 %copy-start = (bf16[256,1024]{1,0:T(8,128)(2,1)S(1)}, bf16[256,1024]{1,0:T(8,128)(2,1)}, u32[]{:S(2)}) copy-start(bf16[256,1024]{1,0:T(8,128)(2,1)} %get-tuple-element.20.refs_0_.refs_1_.refs_5_) | copy-start | bytes 1572868
  14.4 6.3 %copy-start.5 = (bf16[8,64,1024]{2,1,0:T(8,128)(2,1)S(1)}, bf16[8,64,1024]{2,1,0:T(8,128)(2,1)}, u32[]{:S(2)}) copy-start(bf16[8,64,1024]{2,1,0:T(8,128)(2,1)} %refs_4_.2) | copy-start | bytes 3145732
  14.4 6.3 %copy-start.6 = (bf16[64,1152]{1,0:T(8,128)(2,1)S(1)}, bf16[64,1152]{1,0:T(8,128)(2,1)}, u32[]{:S(2)}) copy-start(bf16[64,1152]{1,0:T(8,128)(2,1)} %get-tuple-element.21.refs_0_) | copy-start | bytes 442372
  16.7 9.5 %copy-start.1 = (bf16[256,1024]{1,0:T(8,128)(2,1)S(1)}, bf16[256,1024]{1,0:T(8,128)(2,1)}, u32[]{:S(2)}) copy-start(bf16[256,1024]{1,0:T(8,128)(2,1)} %get-tuple-element.20.refs_0_.refs_1_.refs_5_) | copy-start | bytes 1572868
  21.4 4.7 %collective-permute-start.5 = (bf16[128,128]{1,0:T(8,128)(2,1)S(1)}, bf16[128,128]{1,0:T(8,128)(2,1)S(1)}, u32[]{:S(2)}, u32[]{:S(2)}) collective-permute-start(bf16[128,128]{1,0:T(8,128)(2,1)S(1)} %get-tuple-element.25.refs_1_), channel_id=1, source_target_pairs={{0,1},{1,0},{2,3},{3,2},{4,5},{5,4},{6,7},{7,6},{8,9},{9,8},{10,11... | collective-permute-start | bytes 98312 | tf_op jit(solution)/shard_map/ppermute | solution.py:607
  21.5 15.3 %collective-permute-start.3 = (bf16[256,896]{1,0:T(8,128)(2,1)S(1)}, bf16[256,896]{1,0:T(8,128)(2,1)S(1)}, u32[]{:S(2)}, u32[]{:S(2)}) collective-permute-start(bf16[256,896]{1,0:T(8,128)(2,1)S(1)} %hold.1.refs_4_), channel_id=1, source_target_pairs={{0,2},{2,3},{3,1},{1,0},{4,6},{6,7},{7,5},{5,4},{8,10},{10,11},{11... | collective-permute-start | bytes 1376264 | tf_op jit(solution)/shard_map/ppermute | solution.py:574
  28.7 19.9 %collective-permute-start.9 = (bf16[256,1152]{1,0:T(8,128)(2,1)S(1)}, bf16[256,1152]{1,0:T(8,128)(2,1)S(1)}, u32[]{:S(2)}, u32[]{:S(2)}) collective-permute-start(bf16[256,1152]{1,0:T(8,128)(2,1)S(1)} %hop.6.refs_3_), channel_id=1, source_target_pairs={{0,2},{2,3},{3,1},{1,0},{4,6},{6,7},{7,5},{5,4},{8,10},{10,11},{11... | collective-permute-start | bytes 1769480 | tf_op jit(solution)/shard_map/ppermute | solution.py:574
  31.4 23.2 %collective-permute-start.8 = (bf16[128,128]{1,0:T(8,128)(2,1)S(1)}, bf16[128,128]{1,0:T(8,128)(2,1)S(1)}, u32[]{:S(2)}, u32[]{:S(2)}) collective-permute-start(bf16[128,128]{1,0:T(8,128)(2,1)S(1)} %add_convert_fusion.refs_3_.refs_0_), channel_id=1, source_target_pairs={{0,3},{3,0},{4,7},{7,4},{8,11},{11,8},{12,15},{15,12},{16,19},{19,... | collective-permute-start | bytes 98312 | tf_op jit(solution)/shard_map/ppermute | solution.py:587
  35.5 19.1 %collective-permute-start.7 = (bf16[128,128]{1,0:T(8,128)(2,1)S(1)}, bf16[128,128]{1,0:T(8,128)(2,1)S(1)}, u32[]{:S(2)}, u32[]{:S(2)}) collective-permute-start(bf16[128,128]{1,0:T(8,128)(2,1)S(1)} %add_convert_fusion.refs_3_.refs_0_), channel_id=1, source_target_pairs={{0,2},{3,1},{4,6},{7,5},{8,10},{11,9},{12,14},{15,13},{16,18},{19,... | collective-permute-start | bytes 98312 | tf_op jit(solution)/shard_map/ppermute | solution.py:586
  39.0 15.5 %copy-start.2 = (bf16[8,64,2048]{2,1,0:T(8,128)(2,1)S(1)}, bf16[8,64,2048]{2,1,0:T(8,128)(2,1)}, u32[]{:S(2)}) copy-start(bf16[8,64,2048]{2,1,0:T(8,128)(2,1)} %refs_4_.3) | copy-start | bytes 6291460
  39.0 20.8 %collective-permute-start.6 = (bf16[256,896]{1,0:T(8,128)(2,1)S(1)}, bf16[256,896]{1,0:T(8,128)(2,1)S(1)}, u32[]{:S(2)}, u32[]{:S(2)}) collective-permute-start(bf16[256,896]{1,0:T(8,128)(2,1)S(1)} %hop.7), channel_id=1, source_target_pairs={{0,2},{2,3},{3,1},{1,0},{4,6},{6,7},{7,5},{5,4},{8,10},{10,11},{11... | collective-permute-start | bytes 1376264 | tf_op jit(solution)/shard_map/ppermute | solution.py:574
  51.1 22.7 %collective-permute-start.14 = (bf16[256,1152]{1,0:T(8,128)(2,1)S(1)}, bf16[256,1152]{1,0:T(8,128)(2,1)S(1)}, u32[]{:S(2)}, u32[]{:S(2)}) collective-permute-start(bf16[256,1152]{1,0:T(8,128)(2,1)S(1)} %hop.8.refs_5_), channel_id=1, source_target_pairs={{0,2},{2,3},{3,1},{1,0},{4,6},{6,7},{7,5},{5,4},{8,10},{10,11},{11... | collective-permute-start | bytes 1769480 | tf_op jit(solution)/shard_map/ppermute | solution.py:574
  55.4 10.2 %collective-permute-start.11 = (bf16[64,2048]{1,0:T(8,128)(2,1)S(1)}, bf16[64,2048]{1,0:T(8,128)(2,1)S(1)}, u32[]{:S(2)}, u32[]{:S(2)}) collective-permute-start(bf16[64,2048]{1,0:T(8,128)(2,1)S(1)} %get-tuple-element.29), channel_id=1, source_target_pairs={{0,4},{4,0},{8,12},{12,8},{1,5},{5,1},{9,13},{13,9},{2,6},{6,2},{1... | collective-permute-start | bytes 786440 | tf_op jit(solution)/shard_map/ppermute | solution.py:568
  55.5 10.1 %collective-permute-start.12 = (bf16[64,2048]{1,0:T(8,128)(2,1)S(1)}, bf16[64,2048]{1,0:T(8,128)(2,1)S(1)}, u32[]{:S(2)}, u32[]{:S(2)}) collective-permute-start(bf16[64,2048]{1,0:T(8,128)(2,1)S(1)} %get-tuple-element.30), channel_id=1, source_target_pairs={{0,8},{4,12},{8,0},{12,4},{1,9},{5,13},{9,1},{13,5},{2,10},{6,14},... | collective-permute-start | bytes 786440 | tf_op jit(solution)/shard_map/ppermute | solution.py:568
  57.0 12.3 %collective-permute-start.13 = (bf16[64,2048]{1,0:T(8,128)(2,1)S(1)}, bf16[64,2048]{1,0:T(8,128)(2,1)S(1)}, u32[]{:S(2)}, u32[]{:S(2)}) collective-permute-start(bf16[64,2048]{1,0:T(8,128)(2,1)S(1)} %get-tuple-element.31), channel_id=1, source_target_pairs={{0,12},{4,8},{8,4},{12,0},{1,13},{5,9},{9,5},{13,1},{2,14},{6,10},... | collective-permute-start | bytes 786440 | tf_op jit(solution)/shard_map/ppermute | solution.py:568
  59.9 9.5 %copy-start.4 = (bf16[256,2048]{1,0:T(8,128)(2,1)S(1)}, bf16[256,2048]{1,0:T(8,128)(2,1)}, u32[]{:S(2)}) copy-start(bf16[256,2048]{1,0:T(8,128)(2,1)} %refs_6_.1) | copy-start | bytes 3145732
  59.9 9.5 %copy-start.7 = (bf16[256,256]{1,0:T(8,128)(2,1)S(1)}, bf16[256,256]{1,0:T(8,128)(2,1)}, u32[]{:S(2)}) copy-start(bf16[256,256]{1,0:T(8,128)(2,1)} %get-tuple-element.32.refs_4_) | copy-start | bytes 393220
  62.1 19.0 %collective-permute-start.10 = (bf16[256,896]{1,0:T(8,128)(2,1)S(1)}, bf16[256,896]{1,0:T(8,128)(2,1)S(1)}, u32[]{:S(2)}, u32[]{:S(2)}) collective-permute-start(bf16[256,896]{1,0:T(8,128)(2,1)S(1)} %hop.9.refs_8_), channel_id=1, source_target_pairs={{0,2},{2,3},{3,1},{1,0},{4,6},{6,7},{7,5},{5,4},{8,10},{10,11},{11... | collective-permute-start | bytes 1376264 | tf_op jit(solution)/shard_map/ppermute | solution.py:574
  73.9 1.3 %copy-start.3 = (f32[256,1152]{1,0:T(8,128)S(1)}, f32[256,1152]{1,0:T(8,128)}, u32[]{:S(2)}) copy-start(f32[256,1152]{1,0:T(8,128)} %get-tuple-element.34.settled_ref) | copy-start | bytes 3538948

commit v18 on v16

--- a/solution.py
+++ b/solution.py
@@ -239,10 +239,10 @@
         if step == 0:
             plan_routes(slots, adapter_ref, placement_ref, chosen_ref, sent_ref)
             leave(chosen_ref, chosen_hbm)
-        if step == steps - 1:
-            weights.wait()
-            multiply(0, requests - per)
         for span in range(per // SPAN):
+            if step == steps - 1 and span == per // SPAN - 1:
+                weights.wait()
+                multiply(0, requests - per)
             cached_weights = []
             fresh_weights = []
             mixed = []

time: 82.4 us -> 82.6 us (level)
  no operation moved by 1% of the time
where the time goes in v18:
time: 82.6 us; the launch traced here: 82.3 us
  waiting for transfers between devices  27.1 us (33%)
  Pallas kernels  26.6 us (32%)
  starting transfers between devices  25.9 us (31%)
  local copies, waits for them, and re-layouts  2.38 us (3%)
    ppermute x6, starting transfers between devices, forward(): return lax.ppermute(x, 'tensor', ring)  16.6 us
    ppermute x6, waiting for transfers between devices, forward(): return lax.ppermute(x, 'tensor', ring)  13.2 us
    pallas_call x5, Pallas kernels, hop(): pl.pallas_call(functools.partial(hop_kernel, step, block, start, arriving...  11.3 us
    ppermute x6, waiting for transfers between devices, exchange(): lax.ppermute(blocks[r], 'dp', [(i, i ^ r) for i in range(replicas)])  9.72 us
    pallas_call x1, Pallas kernels, attend(): pl.pallas_call(functools.partial(attend_kernel, heads, kv, cache, steps,...  7.68 us
    pallas_call x1, Pallas kernels, settle(): pl.pallas_call(functools.partial(settle_kernel, step, replicas, len(after...  4.51 us
    ppermute x1, waiting for transfers between devices, per_device(): lax.ppermute(mid, 'tensor', [(i, i ^ 1) for i in range(count)])  4.17 us
    ppermute x1, starting transfers between devices, pair_sums(): other = lax.ppermute(x, 'tensor', far)  4.12 us
  transfers between devices with their start and end apart: 15, of which 8 were waited for; matrix products, arithmetic and copies ran while one was open for 0% of the time, Pallas kernels for 22%

profile of v18, /device:TPU:0, one launch (start us, length us, event | category | flops | bytes accessed | tf_op | source)
XLA Modules:
  0.0 82.3 jit_solution(428507282317118644)
XLA Ops:
  0.0 7.7 %attend.1 = (bf16[256,1024]{1,0:T(8,128)(2,1)}, bf16[256,1280]{1,0:T(8,128)(2,1)}, bf16[256,256]{1,0:T(8,128)(2,1)}, bf16[64,1152]{1,0:T(8,128)(2,1)}, bf16[64,1...) custom-call(s32[1,256]{1,0:T(1,128)} %bitcast.13, s32[1,256]{1,0:T(1,128)} %bitcast.14, ...), custom_call_target="tpu_custom_call" | custom-call | tf_op jit(solution)/shard_map/attend/pallas_call | solution.py:325
  7.7 4.1 %collective-permute-start.4 = (bf16[256,1280]{1,0:T(8,128)(2,1)}, bf16[256,1280]{1,0:T(8,128)(2,1)S(1)}, u32[]{:S(2)}, u32[]{:S(2)}) collective-permute-start(bf16[256,1280]{1,0:T(8,128)(2,1)} %get-tuple-element.26), channel_id=1, source_target_pairs={{0,2},{2,3},{3,1},{1,0},{4,6},{6,7},{7,5},{5,4},{8,10},{10,11},{11... | collective-permute-start | bytes 1966088 | tf_op jit(solution)/shard_map/ppermute | solution.py:573
  11.8 1.5 %collective-permute-start.1 = (bf16[64,1152]{1,0:T(8,128)(2,1)}, bf16[64,1152]{1,0:T(8,128)(2,1)S(1)}, u32[]{:S(2)}, u32[]{:S(2)}) collective-permute-start(bf16[64,1152]{1,0:T(8,128)(2,1)} %get-tuple-element.23), channel_id=1, source_target_pairs={{0,8},{4,12},{8,0},{12,4},{1,9},{5,13},{9,1},{13,5},{2,10},{6,14},... | collective-permute-start | bytes 442376 | tf_op jit(solution)/shard_map/ppermute | solution.py:567
  13.3 0.4 collective-permute-start.2
  13.6 1.0 %copy-done = bf16[256,1024]{1,0:T(8,128)(2,1)S(1)} copy-done((bf16[256,1024]{1,0:T(8,128)(2,1)S(1)}, bf16[256,1024]{1,0:T(8,128)(2,1)}, u32[]{:S(2)}) %copy-start) | copy-done | bytes 524312
  14.7 2.1 %hop.5.refs_5_.refs_0_ = bf16[256,768]{1,0:T(8,128)(2,1)S(1)} custom-call(bf16[256,1024]{1,0:T(8,128)(2,1)S(1)} %copy-done, bf16[1024,8192]{1,0:T(8,128)(2,1)} %refs_7_.1), custom_call_target="tpu_custom_call" | custom-call | tf_op jit(solution)/shard_map/hop/pallas_call | solution.py:376
  16.8 1.9 %collective-permute-done.1.refs_2_ = bf16[64,1152]{1,0:T(8,128)(2,1)S(1)} collective-permute-done((bf16[64,1152]{1,0:T(8,128)(2,1)}, bf16[64,1152]{1,0:T(8,128)(2,1)S(1)}, u32[]{:S(2)}, u32[]{:S(2)}) %collective-permute-start.1) | collective-permute-done | bytes 147488 | tf_op jit(solution)/shard_map/ppermute | solution.py:567
  18.6 2.4 %collective-permute-done.2.refs_3_ = bf16[64,1152]{1,0:T(8,128)(2,1)S(1)} collective-permute-done((bf16[64,1152]{1,0:T(8,128)(2,1)}, bf16[64,1152]{1,0:T(8,128)(2,1)S(1)}, u32[]{:S(2)}, u32[]{:S(2)}) %collective-permute-start.2) | collective-permute-done | bytes 147488 | tf_op jit(solution)/shard_map/ppermute | solution.py:567
  21.0 0.6 down.1
  21.8 1.9 %collective-permute-start.3 = (bf16[256,768]{1,0:T(8,128)(2,1)S(1)}, bf16[256,768]{1,0:T(8,128)(2,1)S(1)}, u32[]{:S(2)}, u32[]{:S(2)}) collective-permute-start(bf16[256,768]{1,0:T(8,128)(2,1)S(1)} %hold.1.refs_4_), channel_id=1, source_target_pairs={{0,2},{2,3},{3,1},{1,0},{4,6},{6,7},{7,5},{5,4},{8,10},{10,11},{11... | collective-permute-start | bytes 1179656 | tf_op jit(solution)/shard_map/ppermute | solution.py:573
  23.7 4.2 %collective-permute-done.5 = bf16[128,128]{1,0:T(8,128)(2,1)S(1)} collective-permute-done((bf16[128,128]{1,0:T(8,128)(2,1)S(1)}, bf16[128,128]{1,0:T(8,128)(2,1)S(1)}, u32[]{:S(2)}, u32[]{:S(2)}) %collective-permute-start.5) | collective-permute-done | bytes 32800 | tf_op jit(solution)/shard_map/ppermute | solution.py:606
  27.9 2.6 %hop.6.refs_3_ = bf16[256,1280]{1,0:T(8,128)(2,1)S(1)} custom-call(bf16[256,1280]{1,0:T(8,128)(2,1)S(1)} %collective-permute-done.4.refs_0_, bf16[256,1024]{1,0:T(8,128)(2,1)S(1)} %copy-done.1, bf16[1024,8192]{1,0:T(8,128)(2,1)} %refs_7_.1, bf16[128,128]{1,0:T(8,128)(2,1)S(1)} %add_convert_fusion.refs_3_.refs_0_, bf16[256,768]{1,0:T(8,128)(2,1)S(1)} %hold.1.refs_4_), custom_call_target="tpu_custom_call" | custom-call | flops 20000000000 | bytes 40000000 | tf_op jit(solution)/shard_map/hop/pallas_call | solution.py:376
  30.5 2.7 %collective-permute-start.9 = (bf16[256,1280]{1,0:T(8,128)(2,1)S(1)}, bf16[256,1280]{1,0:T(8,128)(2,1)S(1)}, u32[]{:S(2)}, u32[]{:S(2)}) collective-permute-start(bf16[256,1280]{1,0:T(8,128)(2,1)S(1)} %hop.6.refs_3_), channel_id=1, source_target_pairs={{0,2},{2,3},{3,1},{1,0},{4,6},{6,7},{7,5},{5,4},{8,10},{10,11},{11... | collective-permute-start | bytes 1966088 | tf_op jit(solution)/shard_map/ppermute | solution.py:573
  33.1 4.1 %collective-permute-start.8 = (bf16[128,128]{1,0:T(8,128)(2,1)S(1)}, bf16[128,128]{1,0:T(8,128)(2,1)S(1)}, u32[]{:S(2)}, u32[]{:S(2)}) collective-permute-start(bf16[128,128]{1,0:T(8,128)(2,1)S(1)} %add_convert_fusion.refs_3_.refs_0_), channel_id=1, source_target_pairs={{0,3},{3,0},{4,7},{7,4},{8,11},{11,8},{12,15},{15,12},{16,19},{19,... | collective-permute-start | bytes 98312 | tf_op jit(solution)/shard_map/ppermute | solution.py:586
  37.3 1.3 %collective-permute-start.7 = (bf16[128,128]{1,0:T(8,128)(2,1)S(1)}, bf16[128,128]{1,0:T(8,128)(2,1)S(1)}, u32[]{:S(2)}, u32[]{:S(2)}) collective-permute-start(bf16[128,128]{1,0:T(8,128)(2,1)S(1)} %add_convert_fusion.refs_3_.refs_0_), channel_id=1, source_target_pairs={{0,2},{3,1},{4,6},{7,5},{8,10},{11,9},{12,14},{15,13},{16,18},{19,... | collective-permute-start | bytes 98312 | tf_op jit(solution)/shard_map/ppermute | solution.py:585
  38.6 2.0 %hop.7 = bf16[256,768]{1,0:T(8,128)(2,1)S(1)} custom-call(bf16[256,768]{1,0:T(8,128)(2,1)S(1)} %collective-permute-done.3.refs_0_, bf16[256,1024]{1,0:T(8,128)(2,1)S(1)} %copy-done.1, bf16[1024,8192]{1,0:T(8,128)(2,1)} %refs_7_.1, bf16[256,1280]{1,0:T(8,128)(2,1)S(1)} %hop.6.refs_3_), custom_call_target="tpu_custom_call" | custom-call | flops 4000000000 | bytes 8000000 | tf_op jit(solution)/shard_map/hop/pallas_call | solution.py:376
  40.6 1.1 %collective-permute-start.6 = (bf16[256,768]{1,0:T(8,128)(2,1)S(1)}, bf16[256,768]{1,0:T(8,128)(2,1)S(1)}, u32[]{:S(2)}, u32[]{:S(2)}) collective-permute-start(bf16[256,768]{1,0:T(8,128)(2,1)S(1)} %hop.7), channel_id=1, source_target_pairs={{0,2},{2,3},{3,1},{1,0},{4,6},{6,7},{7,5},{5,4},{8,10},{10,11},{11... | collective-permute-start | bytes 1179656 | tf_op jit(solution)/shard_map/ppermute | solution.py:573
  41.7 8.6 %collective-permute-done.9.refs_0_ = bf16[256,1280]{1,0:T(8,128)(2,1)S(1)} collective-permute-done((bf16[256,1280]{1,0:T(8,128)(2,1)S(1)}, bf16[256,1280]{1,0:T(8,128)(2,1)S(1)}, u32[]{:S(2)}, u32[]{:S(2)}) %collective-permute-start.9) | collective-permute-done | bytes 655392 | tf_op jit(solution)/shard_map/ppermute | solution.py:573
  50.3 2.6 %hop.8.refs_5_ = bf16[256,1280]{1,0:T(8,128)(2,1)S(1)} custom-call(bf16[256,1280]{1,0:T(8,128)(2,1)S(1)} %collective-permute-done.9.refs_0_, bf16[256,1024]{1,0:T(8,128)(2,1)S(1)} %copy-done.1, bf16[1024,8192]{1,0:T(8,128)(2,1)} %refs_7_.1), custom_call_target="tpu_custom_call" | custom-call | flops 20000000000 | bytes 40000000 | tf_op jit(solution)/shard_map/hop/pallas_call | solution.py:376
  52.9 3.4 %collective-permute-start.14 = (bf16[256,1280]{1,0:T(8,128)(2,1)S(1)}, bf16[256,1280]{1,0:T(8,128)(2,1)S(1)}, u32[]{:S(2)}, u32[]{:S(2)}) collective-permute-start(bf16[256,1280]{1,0:T(8,128)(2,1)S(1)} %hop.8.refs_5_), channel_id=1, source_target_pairs={{0,2},{2,3},{3,1},{1,0},{4,6},{6,7},{7,5},{5,4},{8,10},{10,11},{11... | collective-permute-start | bytes 1966088 | tf_op jit(solution)/shard_map/ppermute | solution.py:573
  56.3 0.8 %up.1 = (bf16[64,2048]{1,0:T(8,128)(2,1)S(1)}, bf16[64,2048]{1,0:T(8,128)(2,1)S(1)}, bf16[64,2048]{1,0:T(8,128)(2,1)S(1)}, bf16[64,2048]{1,0:T(8,128)(2,1)S(1)}) custom-call(bf16[128,128]{1,0:T(8,128)(2,1)S(1)} %add_convert_fusion.refs_3_.refs_0_, bf16[128,128]{1,0:T(8,128)(2,1)S(1)} %collective-permute-done.7.refs_1_, ...), custom_call_target="tpu_custom_call" | custom-call | tf_op jit(solution)/shard_map/up/pallas_call | solution.py:452
  57.2 1.6 %collective-permute-start.12 = (bf16[64,2048]{1,0:T(8,128)(2,1)S(1)}, bf16[64,2048]{1,0:T(8,128)(2,1)S(1)}, u32[]{:S(2)}, u32[]{:S(2)}) collective-permute-start(bf16[64,2048]{1,0:T(8,128)(2,1)S(1)} %get-tuple-element.30), channel_id=1, source_target_pairs={{0,8},{4,12},{8,0},{12,4},{1,9},{5,13},{9,1},{13,5},{2,10},{6,14},... | collective-permute-start | bytes 786440 | tf_op jit(solution)/shard_map/ppermute | solution.py:567
  59.1 1.0 %collective-permute-done.6.refs_0_ = bf16[256,768]{1,0:T(8,128)(2,1)S(1)} collective-permute-done((bf16[256,768]{1,0:T(8,128)(2,1)S(1)}, bf16[256,768]{1,0:T(8,128)(2,1)S(1)}, u32[]{:S(2)}, u32[]{:S(2)}) %collective-permute-start.6) | collective-permute-done | bytes 393248 | tf_op jit(solution)/shard_map/ppermute | solution.py:573
  60.1 2.1 %hop.9.refs_8_ = bf16[256,768]{1,0:T(8,128)(2,1)S(1)} custom-call(bf16[256,768]{1,0:T(8,128)(2,1)S(1)} %collective-permute-done.6.refs_0_, bf16[256,1024]{1,0:T(8,128)(2,1)S(1)} %copy-done.1, bf16[1024,8192]{1,0:T(8,128)(2,1)} %refs_7_.1, bf16[64,2048]{1,0:T(8,128)(2,1)S(1)} %get-tuple-element.28.refs_3_.refs_0_), custom_call_target="tpu_custom_call" | custom-call | tf_op jit(solution)/shard_map/hop/pallas_call | solution.py:376
  62.2 3.4 %collective-permute-start.10 = (bf16[256,768]{1,0:T(8,128)(2,1)S(1)}, bf16[256,768]{1,0:T(8,128)(2,1)S(1)}, u32[]{:S(2)}, u32[]{:S(2)}) collective-permute-start(bf16[256,768]{1,0:T(8,128)(2,1)S(1)} %hop.9.refs_8_), channel_id=1, source_target_pairs={{0,2},{2,3},{3,1},{1,0},{4,6},{6,7},{7,5},{5,4},{8,10},{10,11},{11... | collective-permute-start | bytes 1179656 | tf_op jit(solution)/shard_map/ppermute | solution.py:573
  65.6 0.8 collective-permute-done.12.refs_2_
  66.4 4.7 %collective-permute-done.13.refs_3_ = bf16[64,2048]{1,0:T(8,128)(2,1)S(1)} collective-permute-done((bf16[64,2048]{1,0:T(8,128)(2,1)S(1)}, bf16[64,2048]{1,0:T(8,128)(2,1)S(1)}, u32[]{:S(2)}, u32[]{:S(2)}) %collective-permute-start.13) | collective-permute-done | bytes 262176 | tf_op jit(solution)/shard_map/ppermute | solution.py:567
  71.1 4.5 %settle.1 = (f32[256,1280]{1,0:T(8,128)}, f32[256,768]{1,0:T(8,128)S(1)}) custom-call(bf16[64,2048]{1,0:T(8,128)(2,1)S(1)} %get-tuple-element.28.refs_3_.refs_0_, bf16[64,2048]{1,0:T(8,128)(2,1)S(1)} %collective-permute-done.11.refs_1_, bf16[64,2048]{1,0:T(8,128)(2,1)S(1)} %collective-permute-done.12.refs_2_, ...), custom_call_target="tpu_custom_call" | custom-call | flops 4000000000 | bytes 8000000 | tf_op jit(solution)/shard_map/settle/pallas_call | solution.py:482
  75.7 1.3 %copy-done.3 = f32[256,1280]{1,0:T(8,128)S(1)} copy-done((f32[256,1280]{1,0:T(8,128)S(1)}, f32[256,1280]{1,0:T(8,128)}, u32[]{:S(2)}) %copy-start.3) | copy-done | bytes 1310744
  77.0 0.9 %finish.2.refs_0_ = bf16[256,2048]{1,0:T(8,128)(2,1)} custom-call(bf16[256,1280]{1,0:T(8,128)(2,1)S(1)} %collective-permute-done.14.arrived_ref, f32[256,1280]{1,0:T(8,128)S(1)} %copy-done.3), custom_call_target="tpu_custom_call" | custom-call | tf_op jit(solution)/shard_map/finish/pallas_call | solution.py:514
  77.9 3.6 %collective-permute-done.10.arrived_ref = bf16[256,768]{1,0:T(8,128)(2,1)S(1)} collective-permute-done((bf16[256,768]{1,0:T(8,128)(2,1)S(1)}, bf16[256,768]{1,0:T(8,128)(2,1)S(1)}, u32[]{:S(2)}, u32[]{:S(2)}) %collective-permute-start.10) | collective-permute-done | bytes 393248 | tf_op jit(solution)/shard_map/ppermute | solution.py:573
  81.5 0.8 finish.3
  (27 shorter events, 0.5 us)
Async XLA Ops:
  7.7 20.2 %collective-permute-start.4 = (bf16[256,1280]{1,0:T(8,128)(2,1)}, bf16[256,1280]{1,0:T(8,128)(2,1)S(1)}, u32[]{:S(2)}, u32[]{:S(2)}) collective-permute-start(bf16[256,1280]{1,0:T(8,128)(2,1)} %get-tuple-element.26), channel_id=1, source_target_pairs={{0,2},{2,3},{3,1},{1,0},{4,6},{6,7},{7,5},{5,4},{8,10},{10,11},{11... | collective-permute-start | bytes 1966088 | tf_op jit(solution)/shard_map/ppermute | solution.py:573
  11.8 5.0 %collective-permute-start = (bf16[64,1152]{1,0:T(8,128)(2,1)}, bf16[64,1152]{1,0:T(8,128)(2,1)S(1)}, u32[]{:S(2)}, u32[]{:S(2)}) collective-permute-start(bf16[64,1152]{1,0:T(8,128)(2,1)} %get-tuple-element.22), channel_id=1, source_target_pairs={{0,4},{4,0},{8,12},{12,8},{1,5},{5,1},{9,13},{13,9},{2,6},{6,2},{1... | collective-permute-start | bytes 442376 | tf_op jit(solution)/shard_map/ppermute | solution.py:567
  11.8 6.9 %collective-permute-start.1 = (bf16[64,1152]{1,0:T(8,128)(2,1)}, bf16[64,1152]{1,0:T(8,128)(2,1)S(1)}, u32[]{:S(2)}, u32[]{:S(2)}) collective-permute-start(bf16[64,1152]{1,0:T(8,128)(2,1)} %get-tuple-element.23), channel_id=1, source_target_pairs={{0,8},{4,12},{8,0},{12,4},{1,9},{5,13},{9,1},{13,5},{2,10},{6,14},... | collective-permute-start | bytes 442376 | tf_op jit(solution)/shard_map/ppermute | solution.py:567
  13.3 7.8 %collective-permute-start.2 = (bf16[64,1152]{1,0:T(8,128)(2,1)}, bf16[64,1152]{1,0:T(8,128)(2,1)S(1)}, u32[]{:S(2)}, u32[]{:S(2)}) collective-permute-start(bf16[64,1152]{1,0:T(8,128)(2,1)} %get-tuple-element.24), channel_id=1, source_target_pairs={{0,12},{4,8},{8,4},{12,0},{1,13},{5,9},{9,5},{13,1},{2,14},{6,10},... | collective-permute-start | bytes 442376 | tf_op jit(solution)/shard_map/ppermute | solution.py:567
  13.6 1.0 %copy-start = (bf16[256,1024]{1,0:T(8,128)(2,1)S(1)}, bf16[256,1024]{1,0:T(8,128)(2,1)}, u32[]{:S(2)}) copy-start(bf16[256,1024]{1,0:T(8,128)(2,1)} %get-tuple-element.20.refs_0_.refs_1_.refs_5_) | copy-start | bytes 1572868
  14.7 6.3 %copy-start.5 = (bf16[8,64,1024]{2,1,0:T(8,128)(2,1)S(1)}, bf16[8,64,1024]{2,1,0:T(8,128)(2,1)}, u32[]{:S(2)}) copy-start(bf16[8,64,1024]{2,1,0:T(8,128)(2,1)} %refs_4_.2) | copy-start | bytes 3145732
  14.7 6.3 %copy-start.6 = (bf16[64,1152]{1,0:T(8,128)(2,1)S(1)}, bf16[64,1152]{1,0:T(8,128)(2,1)}, u32[]{:S(2)}) copy-start(bf16[64,1152]{1,0:T(8,128)(2,1)} %get-tuple-element.21.refs_0_) | copy-start | bytes 442372
  16.8 11.1 %copy-start.1 = (bf16[256,1024]{1,0:T(8,128)(2,1)S(1)}, bf16[256,1024]{1,0:T(8,128)(2,1)}, u32[]{:S(2)}) copy-start(bf16[256,1024]{1,0:T(8,128)(2,1)} %get-tuple-element.20.refs_0_.refs_1_.refs_5_) | copy-start | bytes 1572868
  21.7 6.1 %collective-permute-start.5 = (bf16[128,128]{1,0:T(8,128)(2,1)S(1)}, bf16[128,128]{1,0:T(8,128)(2,1)S(1)}, u32[]{:S(2)}, u32[]{:S(2)}) collective-permute-start(bf16[128,128]{1,0:T(8,128)(2,1)S(1)} %get-tuple-element.25.refs_1_), channel_id=1, source_target_pairs={{0,1},{1,0},{2,3},{3,2},{4,5},{5,4},{6,7},{7,6},{8,9},{9,8},{10,11... | collective-permute-start | bytes 98312 | tf_op jit(solution)/shard_map/ppermute | solution.py:606
  21.8 16.8 %collective-permute-start.3 = (bf16[256,768]{1,0:T(8,128)(2,1)S(1)}, bf16[256,768]{1,0:T(8,128)(2,1)S(1)}, u32[]{:S(2)}, u32[]{:S(2)}) collective-permute-start(bf16[256,768]{1,0:T(8,128)(2,1)S(1)} %hold.1.refs_4_), channel_id=1, source_target_pairs={{0,2},{2,3},{3,1},{1,0},{4,6},{6,7},{7,5},{5,4},{8,10},{10,11},{11... | collective-permute-start | bytes 1179656 | tf_op jit(solution)/shard_map/ppermute | solution.py:573
  30.5 19.8 %collective-permute-start.9 = (bf16[256,1280]{1,0:T(8,128)(2,1)S(1)}, bf16[256,1280]{1,0:T(8,128)(2,1)S(1)}, u32[]{:S(2)}, u32[]{:S(2)}) collective-permute-start(bf16[256,1280]{1,0:T(8,128)(2,1)S(1)} %hop.6.refs_3_), channel_id=1, source_target_pairs={{0,2},{2,3},{3,1},{1,0},{4,6},{6,7},{7,5},{5,4},{8,10},{10,11},{11... | collective-permute-start | bytes 1966088 | tf_op jit(solution)/shard_map/ppermute | solution.py:573
  33.1 23.2 %collective-permute-start.8 = (bf16[128,128]{1,0:T(8,128)(2,1)S(1)}, bf16[128,128]{1,0:T(8,128)(2,1)S(1)}, u32[]{:S(2)}, u32[]{:S(2)}) collective-permute-start(bf16[128,128]{1,0:T(8,128)(2,1)S(1)} %add_convert_fusion.refs_3_.refs_0_), channel_id=1, source_target_pairs={{0,3},{3,0},{4,7},{7,4},{8,11},{11,8},{12,15},{15,12},{16,19},{19,... | collective-permute-start | bytes 98312 | tf_op jit(solution)/shard_map/ppermute | solution.py:586
  37.3 19.1 %collective-permute-start.7 = (bf16[128,128]{1,0:T(8,128)(2,1)S(1)}, bf16[128,128]{1,0:T(8,128)(2,1)S(1)}, u32[]{:S(2)}, u32[]{:S(2)}) collective-permute-start(bf16[128,128]{1,0:T(8,128)(2,1)S(1)} %add_convert_fusion.refs_3_.refs_0_), channel_id=1, source_target_pairs={{0,2},{3,1},{4,6},{7,5},{8,10},{11,9},{12,14},{15,13},{16,18},{19,... | collective-permute-start | bytes 98312 | tf_op jit(solution)/shard_map/ppermute | solution.py:585
  40.6 15.7 %copy-start.2 = (bf16[8,64,2048]{2,1,0:T(8,128)(2,1)S(1)}, bf16[8,64,2048]{2,1,0:T(8,128)(2,1)}, u32[]{:S(2)}) copy-start(bf16[8,64,2048]{2,1,0:T(8,128)(2,1)} %refs_4_.3) | copy-start | bytes 6291460
  40.6 19.5 %collective-permute-start.6 = (bf16[256,768]{1,0:T(8,128)(2,1)S(1)}, bf16[256,768]{1,0:T(8,128)(2,1)S(1)}, u32[]{:S(2)}, u32[]{:S(2)}) collective-permute-start(bf16[256,768]{1,0:T(8,128)(2,1)S(1)} %hop.7), channel_id=1, source_target_pairs={{0,2},{2,3},{3,1},{1,0},{4,6},{6,7},{7,5},{5,4},{8,10},{10,11},{11... | collective-permute-start | bytes 1179656 | tf_op jit(solution)/shard_map/ppermute | solution.py:573
  52.9 22.8 %collective-permute-start.14 = (bf16[256,1280]{1,0:T(8,128)(2,1)S(1)}, bf16[256,1280]{1,0:T(8,128)(2,1)S(1)}, u32[]{:S(2)}, u32[]{:S(2)}) collective-permute-start(bf16[256,1280]{1,0:T(8,128)(2,1)S(1)} %hop.8.refs_5_), channel_id=1, source_target_pairs={{0,2},{2,3},{3,1},{1,0},{4,6},{6,7},{7,5},{5,4},{8,10},{10,11},{11... | collective-permute-start | bytes 1966088 | tf_op jit(solution)/shard_map/ppermute | solution.py:573
  57.2 8.5 %collective-permute-start.11 = (bf16[64,2048]{1,0:T(8,128)(2,1)S(1)}, bf16[64,2048]{1,0:T(8,128)(2,1)S(1)}, u32[]{:S(2)}, u32[]{:S(2)}) collective-permute-start(bf16[64,2048]{1,0:T(8,128)(2,1)S(1)} %get-tuple-element.29), channel_id=1, source_target_pairs={{0,4},{4,0},{8,12},{12,8},{1,5},{5,1},{9,13},{13,9},{2,6},{6,2},{1... | collective-permute-start | bytes 786440 | tf_op jit(solution)/shard_map/ppermute | solution.py:567
  57.2 9.2 %collective-permute-start.12 = (bf16[64,2048]{1,0:T(8,128)(2,1)S(1)}, bf16[64,2048]{1,0:T(8,128)(2,1)S(1)}, u32[]{:S(2)}, u32[]{:S(2)}) collective-permute-start(bf16[64,2048]{1,0:T(8,128)(2,1)S(1)} %get-tuple-element.30), channel_id=1, source_target_pairs={{0,8},{4,12},{8,0},{12,4},{1,9},{5,13},{9,1},{13,5},{2,10},{6,14},... | collective-permute-start | bytes 786440 | tf_op jit(solution)/shard_map/ppermute | solution.py:567
  58.8 12.3 %collective-permute-start.13 = (bf16[64,2048]{1,0:T(8,128)(2,1)S(1)}, bf16[64,2048]{1,0:T(8,128)(2,1)S(1)}, u32[]{:S(2)}, u32[]{:S(2)}) collective-permute-start(bf16[64,2048]{1,0:T(8,128)(2,1)S(1)} %get-tuple-element.31), channel_id=1, source_target_pairs={{0,12},{4,8},{8,4},{12,0},{1,13},{5,9},{9,5},{13,1},{2,14},{6,10},... | collective-permute-start | bytes 786440 | tf_op jit(solution)/shard_map/ppermute | solution.py:567
  60.1 11.0 %copy-start.4 = (bf16[256,2048]{1,0:T(8,128)(2,1)S(1)}, bf16[256,2048]{1,0:T(8,128)(2,1)}, u32[]{:S(2)}) copy-start(bf16[256,2048]{1,0:T(8,128)(2,1)} %refs_6_.1) | copy-start | bytes 3145732
  60.1 11.0 %copy-start.7 = (bf16[256,256]{1,0:T(8,128)(2,1)S(1)}, bf16[256,256]{1,0:T(8,128)(2,1)}, u32[]{:S(2)}) copy-start(bf16[256,256]{1,0:T(8,128)(2,1)} %get-tuple-element.32.refs_4_) | copy-start | bytes 393220
  62.2 19.2 %collective-permute-start.10 = (bf16[256,768]{1,0:T(8,128)(2,1)S(1)}, bf16[256,768]{1,0:T(8,128)(2,1)S(1)}, u32[]{:S(2)}, u32[]{:S(2)}) collective-permute-start(bf16[256,768]{1,0:T(8,128)(2,1)S(1)} %hop.9.refs_8_), channel_id=1, source_target_pairs={{0,2},{2,3},{3,1},{1,0},{4,6},{6,7},{7,5},{5,4},{8,10},{10,11},{11... | collective-permute-start | bytes 1179656 | tf_op jit(solution)/shard_map/ppermute | solution.py:573
  75.7 1.3 %copy-start.3 = (f32[256,1280]{1,0:T(8,128)S(1)}, f32[256,1280]{1,0:T(8,128)}, u32[]{:S(2)}) copy-start(f32[256,1280]{1,0:T(8,128)} %get-tuple-element.34.settled_ref) | copy-start | bytes 3932164

commit v19 on v16

--- a/solution.py
+++ b/solution.py
@@ -215,7 +215,7 @@
                 1,
             )
 
-    for copy in small:
+    for copy in small[:2]:
         copy.wait()
     counts = len_ref[...].astype(jnp.float32)
     all_groups = requests // GROUP
@@ -233,12 +233,14 @@
         k_at = step * per * cache * kv
         f_at = step * per * kv
         part(2, step).wait()
+        if step == 0:
+            for copy in small[2:]:
+                copy.wait()
         if step + 1 < steps:
             arrive(step + 1)
             scores(step + 1)
         if step == 0:
             plan_routes(slots, adapter_ref, placement_ref, chosen_ref, sent_ref)
-            leave(chosen_ref, chosen_hbm)
         if step == steps - 1:
             weights.wait()
             multiply(0, requests - per)
@@ -274,6 +276,7 @@
         leave(a_ref.at[rows, :], a_hbm.at[rows, :])
 
     sent_ref[:, pl.ds(0, heads * width)] = _dot(chosen_ref[...], a_ref[...]).astype(jnp.bfloat16)
+    leave(chosen_ref, chosen_hbm)
     for r in range(replicas):
         leave(sent_ref.at[pl.ds(r * CAP, CAP), :], sent_hbm[r])
     multiply(requests - per, per)

time: 82.4 us -> 81.5 us (0.989)
  Pallas kernels: 26.4 us -> 25.5 us
    pallas_call x1, Pallas kernels: 7.49 us -> 6.56 us  [attend(): pl.pallas_call(functools.partial(attend_kernel, heads, kv, cache, steps,...]
where the time goes in v19:
time: 81.5 us; the launch traced here: 81.1 us
  waiting for transfers between devices  27.1 us (33%)
  starting transfers between devices  25.9 us (32%)
  Pallas kernels  25.5 us (31%)
  local copies, waits for them, and re-layouts  2.38 us (3%)
    ppermute x6, starting transfers between devices, forward(): return lax.ppermute(x, 'tensor', ring)  16.6 us
    ppermute x6, waiting for transfers between devices, forward(): return lax.ppermute(x, 'tensor', ring)  13.2 us
    pallas_call x5, Pallas kernels, hop(): pl.pallas_call(functools.partial(hop_kernel, step, block, start, arriving...  11.3 us
    ppermute x6, waiting for transfers between devices, exchange(): lax.ppermute(blocks[r], 'dp', [(i, i ^ r) for i in range(replicas)])  9.72 us
    pallas_call x1, Pallas kernels, attend(): pl.pallas_call(functools.partial(attend_kernel, heads, kv, cache, steps,...  6.56 us
    pallas_call x1, Pallas kernels, settle(): pl.pallas_call(functools.partial(settle_kernel, step, replicas, len(after...  4.52 us
    ppermute x1, waiting for transfers between devices, per_device(): lax.ppermute(mid, 'tensor', [(i, i ^ 1) for i in range(count)])  4.17 us
    ppermute x1, starting transfers between devices, pair_sums(): other = lax.ppermute(x, 'tensor', far)  4.12 us
  transfers between devices with their start and end apart: 15, of which 8 were waited for; matrix products, arithmetic and copies ran while one was open for 0% of the time, Pallas kernels for 22%

profile of v19, /device:TPU:0, one launch (start us, length us, event | category | flops | bytes accessed | tf_op | source)
XLA Modules:
  0.0 81.1 jit_solution(13406411872576204826)
XLA Ops:
  0.0 6.6 %attend.1 = (bf16[256,1024]{1,0:T(8,128)(2,1)}, bf16[256,1280]{1,0:T(8,128)(2,1)}, bf16[256,256]{1,0:T(8,128)(2,1)}, bf16[64,1152]{1,0:T(8,128)(2,1)}, bf16[64,1...) custom-call(s32[1,256]{1,0:T(1,128)} %bitcast.13, s32[1,256]{1,0:T(1,128)} %bitcast.14, ...), custom_call_target="tpu_custom_call" | custom-call | tf_op jit(solution)/shard_map/attend/pallas_call | solution.py:328
  6.6 4.1 %collective-permute-start.4 = (bf16[256,1280]{1,0:T(8,128)(2,1)}, bf16[256,1280]{1,0:T(8,128)(2,1)S(1)}, u32[]{:S(2)}, u32[]{:S(2)}) collective-permute-start(bf16[256,1280]{1,0:T(8,128)(2,1)} %get-tuple-element.26), channel_id=1, source_target_pairs={{0,2},{2,3},{3,1},{1,0},{4,6},{6,7},{7,5},{5,4},{8,10},{10,11},{11... | collective-permute-start | bytes 1966088 | tf_op jit(solution)/shard_map/ppermute | solution.py:576
  10.7 1.5 %collective-permute-start.1 = (bf16[64,1152]{1,0:T(8,128)(2,1)}, bf16[64,1152]{1,0:T(8,128)(2,1)S(1)}, u32[]{:S(2)}, u32[]{:S(2)}) collective-permute-start(bf16[64,1152]{1,0:T(8,128)(2,1)} %get-tuple-element.23), channel_id=1, source_target_pairs={{0,8},{4,12},{8,0},{12,4},{1,9},{5,13},{9,1},{13,5},{2,10},{6,14},... | collective-permute-start | bytes 442376 | tf_op jit(solution)/shard_map/ppermute | solution.py:570
  12.1 0.4 collective-permute-start.2
  12.5 1.0 %copy-done = bf16[256,1024]{1,0:T(8,128)(2,1)S(1)} copy-done((bf16[256,1024]{1,0:T(8,128)(2,1)S(1)}, bf16[256,1024]{1,0:T(8,128)(2,1)}, u32[]{:S(2)}) %copy-start) | copy-done | bytes 524312
  13.6 2.1 %hop.5.refs_5_.refs_0_ = bf16[256,768]{1,0:T(8,128)(2,1)S(1)} custom-call(bf16[256,1024]{1,0:T(8,128)(2,1)S(1)} %copy-done, bf16[1024,8192]{1,0:T(8,128)(2,1)} %refs_7_.1), custom_call_target="tpu_custom_call" | custom-call | tf_op jit(solution)/shard_map/hop/pallas_call | solution.py:379
  15.7 1.9 %collective-permute-done.1.refs_2_ = bf16[64,1152]{1,0:T(8,128)(2,1)S(1)} collective-permute-done((bf16[64,1152]{1,0:T(8,128)(2,1)}, bf16[64,1152]{1,0:T(8,128)(2,1)S(1)}, u32[]{:S(2)}, u32[]{:S(2)}) %collective-permute-start.1) | collective-permute-done | bytes 147488 | tf_op jit(solution)/shard_map/ppermute | solution.py:570
  17.5 2.4 %collective-permute-done.2.refs_3_ = bf16[64,1152]{1,0:T(8,128)(2,1)S(1)} collective-permute-done((bf16[64,1152]{1,0:T(8,128)(2,1)}, bf16[64,1152]{1,0:T(8,128)(2,1)S(1)}, u32[]{:S(2)}, u32[]{:S(2)}) %collective-permute-start.2) | collective-permute-done | bytes 147488 | tf_op jit(solution)/shard_map/ppermute | solution.py:570
  19.9 0.6 down.1
  20.6 1.9 %collective-permute-start.3 = (bf16[256,768]{1,0:T(8,128)(2,1)S(1)}, bf16[256,768]{1,0:T(8,128)(2,1)S(1)}, u32[]{:S(2)}, u32[]{:S(2)}) collective-permute-start(bf16[256,768]{1,0:T(8,128)(2,1)S(1)} %hold.1.refs_4_), channel_id=1, source_target_pairs={{0,2},{2,3},{3,1},{1,0},{4,6},{6,7},{7,5},{5,4},{8,10},{10,11},{11... | collective-permute-start | bytes 1179656 | tf_op jit(solution)/shard_map/ppermute | solution.py:576
  22.5 4.2 %collective-permute-done.5 = bf16[128,128]{1,0:T(8,128)(2,1)S(1)} collective-permute-done((bf16[128,128]{1,0:T(8,128)(2,1)S(1)}, bf16[128,128]{1,0:T(8,128)(2,1)S(1)}, u32[]{:S(2)}, u32[]{:S(2)}) %collective-permute-start.5) | collective-permute-done | bytes 32800 | tf_op jit(solution)/shard_map/ppermute | solution.py:609
  26.7 2.6 %hop.6.refs_3_ = bf16[256,1280]{1,0:T(8,128)(2,1)S(1)} custom-call(bf16[256,1280]{1,0:T(8,128)(2,1)S(1)} %collective-permute-done.4.refs_0_, bf16[256,1024]{1,0:T(8,128)(2,1)S(1)} %copy-done.1, bf16[1024,8192]{1,0:T(8,128)(2,1)} %refs_7_.1, bf16[128,128]{1,0:T(8,128)(2,1)S(1)} %add_convert_fusion.refs_3_.refs_0_, bf16[256,768]{1,0:T(8,128)(2,1)S(1)} %hold.1.refs_4_), custom_call_target="tpu_custom_call" | custom-call | flops 20000000000 | bytes 40000000 | tf_op jit(solution)/shard_map/hop/pallas_call | solution.py:379
  29.3 2.7 %collective-permute-start.9 = (bf16[256,1280]{1,0:T(8,128)(2,1)S(1)}, bf16[256,1280]{1,0:T(8,128)(2,1)S(1)}, u32[]{:S(2)}, u32[]{:S(2)}) collective-permute-start(bf16[256,1280]{1,0:T(8,128)(2,1)S(1)} %hop.6.refs_3_), channel_id=1, source_target_pairs={{0,2},{2,3},{3,1},{1,0},{4,6},{6,7},{7,5},{5,4},{8,10},{10,11},{11... | collective-permute-start | bytes 1966088 | tf_op jit(solution)/shard_map/ppermute | solution.py:576
  32.0 4.1 %collective-permute-start.8 = (bf16[128,128]{1,0:T(8,128)(2,1)S(1)}, bf16[128,128]{1,0:T(8,128)(2,1)S(1)}, u32[]{:S(2)}, u32[]{:S(2)}) collective-permute-start(bf16[128,128]{1,0:T(8,128)(2,1)S(1)} %add_convert_fusion.refs_3_.refs_0_), channel_id=1, source_target_pairs={{0,3},{3,0},{4,7},{7,4},{8,11},{11,8},{12,15},{15,12},{16,19},{19,... | collective-permute-start | bytes 98312 | tf_op jit(solution)/shard_map/ppermute | solution.py:589
  36.1 1.3 %collective-permute-start.7 = (bf16[128,128]{1,0:T(8,128)(2,1)S(1)}, bf16[128,128]{1,0:T(8,128)(2,1)S(1)}, u32[]{:S(2)}, u32[]{:S(2)}) collective-permute-start(bf16[128,128]{1,0:T(8,128)(2,1)S(1)} %add_convert_fusion.refs_3_.refs_0_), channel_id=1, source_target_pairs={{0,2},{3,1},{4,6},{7,5},{8,10},{11,9},{12,14},{15,13},{16,18},{19,... | collective-permute-start | bytes 98312 | tf_op jit(solution)/shard_map/ppermute | solution.py:588
  37.4 2.0 %hop.7 = bf16[256,768]{1,0:T(8,128)(2,1)S(1)} custom-call(bf16[256,768]{1,0:T(8,128)(2,1)S(1)} %collective-permute-done.3.refs_0_, bf16[256,1024]{1,0:T(8,128)(2,1)S(1)} %copy-done.1, bf16[1024,8192]{1,0:T(8,128)(2,1)} %refs_7_.1, bf16[256,1280]{1,0:T(8,128)(2,1)S(1)} %hop.6.refs_3_), custom_call_target="tpu_custom_call" | custom-call | flops 4000000000 | bytes 8000000 | tf_op jit(solution)/shard_map/hop/pallas_call | solution.py:379
  39.5 1.1 %collective-permute-start.6 = (bf16[256,768]{1,0:T(8,128)(2,1)S(1)}, bf16[256,768]{1,0:T(8,128)(2,1)S(1)}, u32[]{:S(2)}, u32[]{:S(2)}) collective-permute-start(bf16[256,768]{1,0:T(8,128)(2,1)S(1)} %hop.7), channel_id=1, source_target_pairs={{0,2},{2,3},{3,1},{1,0},{4,6},{6,7},{7,5},{5,4},{8,10},{10,11},{11... | collective-permute-start | bytes 1179656 | tf_op jit(solution)/shard_map/ppermute | solution.py:576
  40.6 8.6 %collective-permute-done.9.refs_0_ = bf16[256,1280]{1,0:T(8,128)(2,1)S(1)} collective-permute-done((bf16[256,1280]{1,0:T(8,128)(2,1)S(1)}, bf16[256,1280]{1,0:T(8,128)(2,1)S(1)}, u32[]{:S(2)}, u32[]{:S(2)}) %collective-permute-start.9) | collective-permute-done | bytes 655392 | tf_op jit(solution)/shard_map/ppermute | solution.py:576
  49.2 2.6 %hop.8.refs_5_ = bf16[256,1280]{1,0:T(8,128)(2,1)S(1)} custom-call(bf16[256,1280]{1,0:T(8,128)(2,1)S(1)} %collective-permute-done.9.refs_0_, bf16[256,1024]{1,0:T(8,128)(2,1)S(1)} %copy-done.1, bf16[1024,8192]{1,0:T(8,128)(2,1)} %refs_7_.1), custom_call_target="tpu_custom_call" | custom-call | flops 20000000000 | bytes 40000000 | tf_op jit(solution)/shard_map/hop/pallas_call | solution.py:379
  51.8 3.4 %collective-permute-start.14 = (bf16[256,1280]{1,0:T(8,128)(2,1)S(1)}, bf16[256,1280]{1,0:T(8,128)(2,1)S(1)}, u32[]{:S(2)}, u32[]{:S(2)}) collective-permute-start(bf16[256,1280]{1,0:T(8,128)(2,1)S(1)} %hop.8.refs_5_), channel_id=1, source_target_pairs={{0,2},{2,3},{3,1},{1,0},{4,6},{6,7},{7,5},{5,4},{8,10},{10,11},{11... | collective-permute-start | bytes 1966088 | tf_op jit(solution)/shard_map/ppermute | solution.py:576
  55.2 0.8 %up.1 = (bf16[64,2048]{1,0:T(8,128)(2,1)S(1)}, bf16[64,2048]{1,0:T(8,128)(2,1)S(1)}, bf16[64,2048]{1,0:T(8,128)(2,1)S(1)}, bf16[64,2048]{1,0:T(8,128)(2,1)S(1)}) custom-call(bf16[128,128]{1,0:T(8,128)(2,1)S(1)} %add_convert_fusion.refs_3_.refs_0_, bf16[128,128]{1,0:T(8,128)(2,1)S(1)} %collective-permute-done.7.refs_1_, ...), custom_call_target="tpu_custom_call" | custom-call | tf_op jit(solution)/shard_map/up/pallas_call | solution.py:455
  56.1 1.6 %collective-permute-start.12 = (bf16[64,2048]{1,0:T(8,128)(2,1)S(1)}, bf16[64,2048]{1,0:T(8,128)(2,1)S(1)}, u32[]{:S(2)}, u32[]{:S(2)}) collective-permute-start(bf16[64,2048]{1,0:T(8,128)(2,1)S(1)} %get-tuple-element.30), channel_id=1, source_target_pairs={{0,8},{4,12},{8,0},{12,4},{1,9},{5,13},{9,1},{13,5},{2,10},{6,14},... | collective-permute-start | bytes 786440 | tf_op jit(solution)/shard_map/ppermute | solution.py:570
  58.0 1.0 %collective-permute-done.6.refs_0_ = bf16[256,768]{1,0:T(8,128)(2,1)S(1)} collective-permute-done((bf16[256,768]{1,0:T(8,128)(2,1)S(1)}, bf16[256,768]{1,0:T(8,128)(2,1)S(1)}, u32[]{:S(2)}, u32[]{:S(2)}) %collective-permute-start.6) | collective-permute-done | bytes 393248 | tf_op jit(solution)/shard_map/ppermute | solution.py:576
  59.0 2.1 %hop.9.refs_8_ = bf16[256,768]{1,0:T(8,128)(2,1)S(1)} custom-call(bf16[256,768]{1,0:T(8,128)(2,1)S(1)} %collective-permute-done.6.refs_0_, bf16[256,1024]{1,0:T(8,128)(2,1)S(1)} %copy-done.1, bf16[1024,8192]{1,0:T(8,128)(2,1)} %refs_7_.1, bf16[64,2048]{1,0:T(8,128)(2,1)S(1)} %get-tuple-element.28.refs_3_.refs_0_), custom_call_target="tpu_custom_call" | custom-call | tf_op jit(solution)/shard_map/hop/pallas_call | solution.py:379
  61.1 3.4 %collective-permute-start.10 = (bf16[256,768]{1,0:T(8,128)(2,1)S(1)}, bf16[256,768]{1,0:T(8,128)(2,1)S(1)}, u32[]{:S(2)}, u32[]{:S(2)}) collective-permute-start(bf16[256,768]{1,0:T(8,128)(2,1)S(1)} %hop.9.refs_8_), channel_id=1, source_target_pairs={{0,2},{2,3},{3,1},{1,0},{4,6},{6,7},{7,5},{5,4},{8,10},{10,11},{11... | collective-permute-start | bytes 1179656 | tf_op jit(solution)/shard_map/ppermute | solution.py:576
  64.5 0.8 collective-permute-done.12.refs_2_
  65.3 4.7 %collective-permute-done.13.refs_3_ = bf16[64,2048]{1,0:T(8,128)(2,1)S(1)} collective-permute-done((bf16[64,2048]{1,0:T(8,128)(2,1)S(1)}, bf16[64,2048]{1,0:T(8,128)(2,1)S(1)}, u32[]{:S(2)}, u32[]{:S(2)}) %collective-permute-start.13) | collective-permute-done | bytes 262176 | tf_op jit(solution)/shard_map/ppermute | solution.py:570
  70.0 4.5 %settle.1 = (f32[256,1280]{1,0:T(8,128)}, f32[256,768]{1,0:T(8,128)S(1)}) custom-call(bf16[64,2048]{1,0:T(8,128)(2,1)S(1)} %get-tuple-element.28.refs_3_.refs_0_, bf16[64,2048]{1,0:T(8,128)(2,1)S(1)} %collective-permute-done.11.refs_1_, bf16[64,2048]{1,0:T(8,128)(2,1)S(1)} %collective-permute-done.12.refs_2_, ...), custom_call_target="tpu_custom_call" | custom-call | flops 4000000000 | bytes 8000000 | tf_op jit(solution)/shard_map/settle/pallas_call | solution.py:485
  74.5 1.3 %copy-done.3 = f32[256,1280]{1,0:T(8,128)S(1)} copy-done((f32[256,1280]{1,0:T(8,128)S(1)}, f32[256,1280]{1,0:T(8,128)}, u32[]{:S(2)}) %copy-start.3) | copy-done | bytes 1310744
  75.8 0.9 %finish.2.refs_0_ = bf16[256,2048]{1,0:T(8,128)(2,1)} custom-call(bf16[256,1280]{1,0:T(8,128)(2,1)S(1)} %collective-permute-done.14.arrived_ref, f32[256,1280]{1,0:T(8,128)S(1)} %copy-done.3), custom_call_target="tpu_custom_call" | custom-call | tf_op jit(solution)/shard_map/finish/pallas_call | solution.py:517
  76.8 3.6 %collective-permute-done.10.arrived_ref = bf16[256,768]{1,0:T(8,128)(2,1)S(1)} collective-permute-done((bf16[256,768]{1,0:T(8,128)(2,1)S(1)}, bf16[256,768]{1,0:T(8,128)(2,1)S(1)}, u32[]{:S(2)}, u32[]{:S(2)}) %collective-permute-start.10) | collective-permute-done | bytes 393248 | tf_op jit(solution)/shard_map/ppermute | solution.py:576
  80.3 0.8 finish.3
  (27 shorter events, 0.5 us)
Async XLA Ops:
  6.6 20.2 %collective-permute-start.4 = (bf16[256,1280]{1,0:T(8,128)(2,1)}, bf16[256,1280]{1,0:T(8,128)(2,1)S(1)}, u32[]{:S(2)}, u32[]{:S(2)}) collective-permute-start(bf16[256,1280]{1,0:T(8,128)(2,1)} %get-tuple-element.26), channel_id=1, source_target_pairs={{0,2},{2,3},{3,1},{1,0},{4,6},{6,7},{7,5},{5,4},{8,10},{10,11},{11... | collective-permute-start | bytes 1966088 | tf_op jit(solution)/shard_map/ppermute | solution.py:576
  10.7 5.0 %collective-permute-start = (bf16[64,1152]{1,0:T(8,128)(2,1)}, bf16[64,1152]{1,0:T(8,128)(2,1)S(1)}, u32[]{:S(2)}, u32[]{:S(2)}) collective-permute-start(bf16[64,1152]{1,0:T(8,128)(2,1)} %get-tuple-element.22), channel_id=1, source_target_pairs={{0,4},{4,0},{8,12},{12,8},{1,5},{5,1},{9,13},{13,9},{2,6},{6,2},{1... | collective-permute-start | bytes 442376 | tf_op jit(solution)/shard_map/ppermute | solution.py:570
  10.7 6.9 %collective-permute-start.1 = (bf16[64,1152]{1,0:T(8,128)(2,1)}, bf16[64,1152]{1,0:T(8,128)(2,1)S(1)}, u32[]{:S(2)}, u32[]{:S(2)}) collective-permute-start(bf16[64,1152]{1,0:T(8,128)(2,1)} %get-tuple-element.23), channel_id=1, source_target_pairs={{0,8},{4,12},{8,0},{12,4},{1,9},{5,13},{9,1},{13,5},{2,10},{6,14},... | collective-permute-start | bytes 442376 | tf_op jit(solution)/shard_map/ppermute | solution.py:570
  12.1 7.7 %collective-permute-start.2 = (bf16[64,1152]{1,0:T(8,128)(2,1)}, bf16[64,1152]{1,0:T(8,128)(2,1)S(1)}, u32[]{:S(2)}, u32[]{:S(2)}) collective-permute-start(bf16[64,1152]{1,0:T(8,128)(2,1)} %get-tuple-element.24), channel_id=1, source_target_pairs={{0,12},{4,8},{8,4},{12,0},{1,13},{5,9},{9,5},{13,1},{2,14},{6,10},... | collective-permute-start | bytes 442376 | tf_op jit(solution)/shard_map/ppermute | solution.py:570
  12.5 1.0 %copy-start = (bf16[256,1024]{1,0:T(8,128)(2,1)S(1)}, bf16[256,1024]{1,0:T(8,128)(2,1)}, u32[]{:S(2)}) copy-start(bf16[256,1024]{1,0:T(8,128)(2,1)} %get-tuple-element.20.refs_0_.refs_1_.refs_5_) | copy-start | bytes 1572868
  13.6 6.3 %copy-start.5 = (bf16[8,64,1024]{2,1,0:T(8,128)(2,1)S(1)}, bf16[8,64,1024]{2,1,0:T(8,128)(2,1)}, u32[]{:S(2)}) copy-start(bf16[8,64,1024]{2,1,0:T(8,128)(2,1)} %refs_4_.2) | copy-start | bytes 3145732
  13.6 6.3 %copy-start.6 = (bf16[64,1152]{1,0:T(8,128)(2,1)S(1)}, bf16[64,1152]{1,0:T(8,128)(2,1)}, u32[]{:S(2)}) copy-start(bf16[64,1152]{1,0:T(8,128)(2,1)} %get-tuple-element.21.refs_0_) | copy-start | bytes 442372
  15.6 11.1 %copy-start.1 = (bf16[256,1024]{1,0:T(8,128)(2,1)S(1)}, bf16[256,1024]{1,0:T(8,128)(2,1)}, u32[]{:S(2)}) copy-start(bf16[256,1024]{1,0:T(8,128)(2,1)} %get-tuple-element.20.refs_0_.refs_1_.refs_5_) | copy-start | bytes 1572868
  20.6 6.1 %collective-permute-start.5 = (bf16[128,128]{1,0:T(8,128)(2,1)S(1)}, bf16[128,128]{1,0:T(8,128)(2,1)S(1)}, u32[]{:S(2)}, u32[]{:S(2)}) collective-permute-start(bf16[128,128]{1,0:T(8,128)(2,1)S(1)} %get-tuple-element.25.refs_1_), channel_id=1, source_target_pairs={{0,1},{1,0},{2,3},{3,2},{4,5},{5,4},{6,7},{7,6},{8,9},{9,8},{10,11... | collective-permute-start | bytes 98312 | tf_op jit(solution)/shard_map/ppermute | solution.py:609
  20.6 16.8 %collective-permute-start.3 = (bf16[256,768]{1,0:T(8,128)(2,1)S(1)}, bf16[256,768]{1,0:T(8,128)(2,1)S(1)}, u32[]{:S(2)}, u32[]{:S(2)}) collective-permute-start(bf16[256,768]{1,0:T(8,128)(2,1)S(1)} %hold.1.refs_4_), channel_id=1, source_target_pairs={{0,2},{2,3},{3,1},{1,0},{4,6},{6,7},{7,5},{5,4},{8,10},{10,11},{11... | collective-permute-start | bytes 1179656 | tf_op jit(solution)/shard_map/ppermute | solution.py:576
  29.3 19.8 %collective-permute-start.9 = (bf16[256,1280]{1,0:T(8,128)(2,1)S(1)}, bf16[256,1280]{1,0:T(8,128)(2,1)S(1)}, u32[]{:S(2)}, u32[]{:S(2)}) collective-permute-start(bf16[256,1280]{1,0:T(8,128)(2,1)S(1)} %hop.6.refs_3_), channel_id=1, source_target_pairs={{0,2},{2,3},{3,1},{1,0},{4,6},{6,7},{7,5},{5,4},{8,10},{10,11},{11... | collective-permute-start | bytes 1966088 | tf_op jit(solution)/shard_map/ppermute | solution.py:576
  32.0 23.2 %collective-permute-start.8 = (bf16[128,128]{1,0:T(8,128)(2,1)S(1)}, bf16[128,128]{1,0:T(8,128)(2,1)S(1)}, u32[]{:S(2)}, u32[]{:S(2)}) collective-permute-start(bf16[128,128]{1,0:T(8,128)(2,1)S(1)} %add_convert_fusion.refs_3_.refs_0_), channel_id=1, source_target_pairs={{0,3},{3,0},{4,7},{7,4},{8,11},{11,8},{12,15},{15,12},{16,19},{19,... | collective-permute-start | bytes 98312 | tf_op jit(solution)/shard_map/ppermute | solution.py:589
  36.1 19.1 %collective-permute-start.7 = (bf16[128,128]{1,0:T(8,128)(2,1)S(1)}, bf16[128,128]{1,0:T(8,128)(2,1)S(1)}, u32[]{:S(2)}, u32[]{:S(2)}) collective-permute-start(bf16[128,128]{1,0:T(8,128)(2,1)S(1)} %add_convert_fusion.refs_3_.refs_0_), channel_id=1, source_target_pairs={{0,2},{3,1},{4,6},{7,5},{8,10},{11,9},{12,14},{15,13},{16,18},{19,... | collective-permute-start | bytes 98312 | tf_op jit(solution)/shard_map/ppermute | solution.py:588
  39.4 15.7 %copy-start.2 = (bf16[8,64,2048]{2,1,0:T(8,128)(2,1)S(1)}, bf16[8,64,2048]{2,1,0:T(8,128)(2,1)}, u32[]{:S(2)}) copy-start(bf16[8,64,2048]{2,1,0:T(8,128)(2,1)} %refs_4_.3) | copy-start | bytes 6291460
  39.5 19.5 %collective-permute-start.6 = (bf16[256,768]{1,0:T(8,128)(2,1)S(1)}, bf16[256,768]{1,0:T(8,128)(2,1)S(1)}, u32[]{:S(2)}, u32[]{:S(2)}) collective-permute-start(bf16[256,768]{1,0:T(8,128)(2,1)S(1)} %hop.7), channel_id=1, source_target_pairs={{0,2},{2,3},{3,1},{1,0},{4,6},{6,7},{7,5},{5,4},{8,10},{10,11},{11... | collective-permute-start | bytes 1179656 | tf_op jit(solution)/shard_map/ppermute | solution.py:576
  51.8 22.8 %collective-permute-start.14 = (bf16[256,1280]{1,0:T(8,128)(2,1)S(1)}, bf16[256,1280]{1,0:T(8,128)(2,1)S(1)}, u32[]{:S(2)}, u32[]{:S(2)}) collective-permute-start(bf16[256,1280]{1,0:T(8,128)(2,1)S(1)} %hop.8.refs_5_), channel_id=1, source_target_pairs={{0,2},{2,3},{3,1},{1,0},{4,6},{6,7},{7,5},{5,4},{8,10},{10,11},{11... | collective-permute-start | bytes 1966088 | tf_op jit(solution)/shard_map/ppermute | solution.py:576
  56.0 8.5 %collective-permute-start.11 = (bf16[64,2048]{1,0:T(8,128)(2,1)S(1)}, bf16[64,2048]{1,0:T(8,128)(2,1)S(1)}, u32[]{:S(2)}, u32[]{:S(2)}) collective-permute-start(bf16[64,2048]{1,0:T(8,128)(2,1)S(1)} %get-tuple-element.29), channel_id=1, source_target_pairs={{0,4},{4,0},{8,12},{12,8},{1,5},{5,1},{9,13},{13,9},{2,6},{6,2},{1... | collective-permute-start | bytes 786440 | tf_op jit(solution)/shard_map/ppermute | solution.py:570
  56.1 9.2 %collective-permute-start.12 = (bf16[64,2048]{1,0:T(8,128)(2,1)S(1)}, bf16[64,2048]{1,0:T(8,128)(2,1)S(1)}, u32[]{:S(2)}, u32[]{:S(2)}) collective-permute-start(bf16[64,2048]{1,0:T(8,128)(2,1)S(1)} %get-tuple-element.30), channel_id=1, source_target_pairs={{0,8},{4,12},{8,0},{12,4},{1,9},{5,13},{9,1},{13,5},{2,10},{6,14},... | collective-permute-start | bytes 786440 | tf_op jit(solution)/shard_map/ppermute | solution.py:570
  57.7 12.3 %collective-permute-start.13 = (bf16[64,2048]{1,0:T(8,128)(2,1)S(1)}, bf16[64,2048]{1,0:T(8,128)(2,1)S(1)}, u32[]{:S(2)}, u32[]{:S(2)}) collective-permute-start(bf16[64,2048]{1,0:T(8,128)(2,1)S(1)} %get-tuple-element.31), channel_id=1, source_target_pairs={{0,12},{4,8},{8,4},{12,0},{1,13},{5,9},{9,5},{13,1},{2,14},{6,10},... | collective-permute-start | bytes 786440 | tf_op jit(solution)/shard_map/ppermute | solution.py:570
  59.0 11.0 %copy-start.4 = (bf16[256,2048]{1,0:T(8,128)(2,1)S(1)}, bf16[256,2048]{1,0:T(8,128)(2,1)}, u32[]{:S(2)}) copy-start(bf16[256,2048]{1,0:T(8,128)(2,1)} %refs_6_.1) | copy-start | bytes 3145732
  59.0 11.0 %copy-start.7 = (bf16[256,256]{1,0:T(8,128)(2,1)S(1)}, bf16[256,256]{1,0:T(8,128)(2,1)}, u32[]{:S(2)}) copy-start(bf16[256,256]{1,0:T(8,128)(2,1)} %get-tuple-element.32.refs_4_) | copy-start | bytes 393220
  61.1 19.2 %collective-permute-start.10 = (bf16[256,768]{1,0:T(8,128)(2,1)S(1)}, bf16[256,768]{1,0:T(8,128)(2,1)S(1)}, u32[]{:S(2)}, u32[]{:S(2)}) collective-permute-start(bf16[256,768]{1,0:T(8,128)(2,1)S(1)} %hop.9.refs_8_), channel_id=1, source_target_pairs={{0,2},{2,3},{3,1},{1,0},{4,6},{6,7},{7,5},{5,4},{8,10},{10,11},{11... | collective-permute-start | bytes 1179656 | tf_op jit(solution)/shard_map/ppermute | solution.py:576
  74.5 1.3 %copy-start.3 = (f32[256,1280]{1,0:T(8,128)S(1)}, f32[256,1280]{1,0:T(8,128)}, u32[]{:S(2)}) copy-start(f32[256,1280]{1,0:T(8,128)} %get-tuple-element.34.settled_ref) | copy-start | bytes 3932164

commit v20 on v19

--- a/solution.py
+++ b/solution.py
@@ -226,12 +226,49 @@
     position = (_iota((all_groups, group_cols), 1) // kv) % cache
     length_bias = jnp.where(position.astype(jnp.float32) < counts, 0.0, MASKED)
 
-    arrive(0)
-    scores(0)
-    for step in range(steps):
+    def soften(step):
+        side = step % 2
+        cached_weights = []
+        fresh_weights = []
+        for g in range(groups):
+            rows = pl.ds(g * group_rows, group_rows)
+            bias = own_bias + length_bias[step * groups + g : step * groups + g + 1, :]
+            cached = scores_ref[side, rows, pl.ds(0, group_cols)] + bias
+            inner = pl.ds((g % span_groups) * group_rows, group_rows)
+            new = scores_ref[side, rows, pl.ds(group_cols, fresh_cols)]
+            new = new + fresh_bias_ref[inner, :]
+            top = row_max([cached, new])
+            cached_weights.append(jnp.exp2((cached - top) * scale).astype(jnp.bfloat16))
+            fresh_weights.append(jnp.exp2((new - top) * scale).astype(jnp.bfloat16))
+        return cached_weights, fresh_weights
+
+    def mix(step, cached_weights, fresh_weights):
         side = step % 2
         k_at = step * per * cache * kv
         f_at = step * per * kv
+        for span in range(per // SPAN):
+            inside = range(span * span_groups, (span + 1) * span_groups)
+            mixed = [
+                _dot(cached_weights[g], v_ref[pl.ds(k_at + g * group_cols, group_cols), :])
+                for g in inside
+            ]
+            fresh = jnp.concatenate([fresh_weights[g] for g in inside], axis=0)
+            values = nv_ref[pl.ds(f_at + span * fresh_cols, fresh_cols), :]
+            mixed = jnp.concatenate(mixed, axis=0) + _dot(fresh, values)
+            cached = jnp.concatenate([cached_weights[g] for g in inside], axis=0)
+            total = _dot(cached, ones[:group_cols]) + _dot(fresh, ones[:fresh_cols])
+            rows = pl.ds(span * span_rows, span_rows)
+            inverse = pl.reciprocal(total, approx=True)
+            mixed_ref[side, rows, :] = mixed * (inverse * (2.0 - total * inverse))
+        for h in range(heads):
+            a_ref[pl.ds(step * per, per), pl.ds(h * width, width)] = mixed_ref[
+                side, pl.ds(h, per, stride=heads), :
+            ].astype(jnp.bfloat16)
+
+    arrive(0)
+    scores(0)
+    softened = soften(0)
+    for step in range(steps):
         part(2, step).wait()
         if step == 0:
             for copy in small[2:]:
@@ -244,34 +281,9 @@
         if step == steps - 1:
             weights.wait()
             multiply(0, requests - per)
-        for span in range(per // SPAN):
-            cached_weights = []
-            fresh_weights = []
-            mixed = []
-            for g in range(span * span_groups, (span + 1) * span_groups):
-                rows = pl.ds(g * group_rows, group_rows)
-                bias = own_bias + length_bias[step * groups + g : step * groups + g + 1, :]
-                cached = scores_ref[side, rows, pl.ds(0, group_cols)] + bias
-                inner = pl.ds((g % span_groups) * group_rows, group_rows)
-                new = scores_ref[side, rows, pl.ds(group_cols, fresh_cols)]
-                new = new + fresh_bias_ref[inner, :]
-                top = row_max([cached, new])
-                cached = jnp.exp2((cached - top) * scale).astype(jnp.bfloat16)
-                cached_weights.append(cached)
-                fresh_weights.append(jnp.exp2((new - top) * scale).astype(jnp.bfloat16))
-                mixed.append(_dot(cached, v_ref[pl.ds(k_at + g * group_cols, group_cols), :]))
-            fresh = jnp.concatenate(fresh_weights, axis=0)
-            values = nv_ref[pl.ds(f_at + span * fresh_cols, fresh_cols), :]
-            mixed = jnp.concatenate(mixed, axis=0) + _dot(fresh, values)
-            total = _dot(jnp.concatenate(cached_weights, axis=0), ones[:group_cols])
-            total = total + _dot(fresh, ones[:fresh_cols])
-            rows = pl.ds(span * span_rows, span_rows)
-            inverse = pl.reciprocal(total, approx=True)
-            mixed_ref[side, rows, :] = mixed * (inverse * (2.0 - total * inverse))
-        for h in range(heads):
-            a_ref[pl.ds(step * per, per), pl.ds(h * width, width)] = mixed_ref[
-                side, pl.ds(h, per, stride=heads), :
-            ].astype(jnp.bfloat16)
+        mix(step, *softened)
+        if step + 1 < steps:
+            softened = soften(step + 1)
         rows = pl.ds(step * per, per)
         leave(a_ref.at[rows, :], a_hbm.at[rows, :])
 

time: 81.5 us -> 81.5 us (level)
  no operation moved by 1% of the time
where the time goes in v20:
time: 81.5 us; the launch traced here: 81.1 us
  waiting for transfers between devices  27.1 us (33%)
  starting transfers between devices  25.9 us (32%)
  Pallas kernels  25.5 us (31%)
  local copies, waits for them, and re-layouts  2.38 us (3%)
    ppermute x6, starting transfers between devices, forward(): return lax.ppermute(x, 'tensor', ring)  16.6 us
    ppermute x6, waiting for transfers between devices, forward(): return lax.ppermute(x, 'tensor', ring)  13.2 us
    pallas_call x5, Pallas kernels, hop(): pl.pallas_call(functools.partial(hop_kernel, step, block, start, arriving...  11.3 us
    ppermute x6, waiting for transfers between devices, exchange(): lax.ppermute(blocks[r], 'dp', [(i, i ^ r) for i in range(replicas)])  9.72 us
    pallas_call x1, Pallas kernels, attend(): pl.pallas_call(functools.partial(attend_kernel, heads, kv, cache, steps,...  6.58 us
    pallas_call x1, Pallas kernels, settle(): pl.pallas_call(functools.partial(settle_kernel, step, replicas, len(after...  4.51 us
    ppermute x1, waiting for transfers between devices, per_device(): lax.ppermute(mid, 'tensor', [(i, i ^ 1) for i in range(count)])  4.17 us
    ppermute x1, starting transfers between devices, pair_sums(): other = lax.ppermute(x, 'tensor', far)  4.12 us
  transfers between devices with their start and end apart: 15, of which 8 were waited for; matrix products, arithmetic and copies ran while one was open for 0% of the time, Pallas kernels for 22%

profile of v20, /device:TPU:0, one launch (start us, length us, event | category | flops | bytes accessed | tf_op | source)
XLA Modules:
  0.0 81.1 jit_solution(9741321046776821476)
XLA Ops:
  0.0 6.6 %attend.1 = (bf16[256,1024]{1,0:T(8,128)(2,1)}, bf16[256,1280]{1,0:T(8,128)(2,1)}, bf16[256,256]{1,0:T(8,128)(2,1)}, bf16[64,1152]{1,0:T(8,128)(2,1)}, bf16[64,1...) custom-call(s32[1,256]{1,0:T(1,128)} %bitcast.13, s32[1,256]{1,0:T(1,128)} %bitcast.14, ...), custom_call_target="tpu_custom_call" | custom-call | tf_op jit(solution)/shard_map/attend/pallas_call | solution.py:340
  6.6 4.1 %collective-permute-start.4 = (bf16[256,1280]{1,0:T(8,128)(2,1)}, bf16[256,1280]{1,0:T(8,128)(2,1)S(1)}, u32[]{:S(2)}, u32[]{:S(2)}) collective-permute-start(bf16[256,1280]{1,0:T(8,128)(2,1)} %get-tuple-element.26), channel_id=1, source_target_pairs={{0,2},{2,3},{3,1},{1,0},{4,6},{6,7},{7,5},{5,4},{8,10},{10,11},{11... | collective-permute-start | bytes 1966088 | tf_op jit(solution)/shard_map/ppermute | solution.py:588
  10.7 1.5 %collective-permute-start.1 = (bf16[64,1152]{1,0:T(8,128)(2,1)}, bf16[64,1152]{1,0:T(8,128)(2,1)S(1)}, u32[]{:S(2)}, u32[]{:S(2)}) collective-permute-start(bf16[64,1152]{1,0:T(8,128)(2,1)} %get-tuple-element.23), channel_id=1, source_target_pairs={{0,8},{4,12},{8,0},{12,4},{1,9},{5,13},{9,1},{13,5},{2,10},{6,14},... | collective-permute-start | bytes 442376 | tf_op jit(solution)/shard_map/ppermute | solution.py:582
  12.2 0.4 collective-permute-start.2
  12.5 1.0 %copy-done = bf16[256,1024]{1,0:T(8,128)(2,1)S(1)} copy-done((bf16[256,1024]{1,0:T(8,128)(2,1)S(1)}, bf16[256,1024]{1,0:T(8,128)(2,1)}, u32[]{:S(2)}) %copy-start) | copy-done | bytes 524312
  13.6 2.1 %hop.5.refs_5_.refs_0_ = bf16[256,768]{1,0:T(8,128)(2,1)S(1)} custom-call(bf16[256,1024]{1,0:T(8,128)(2,1)S(1)} %copy-done, bf16[1024,8192]{1,0:T(8,128)(2,1)} %refs_7_.1), custom_call_target="tpu_custom_call" | custom-call | tf_op jit(solution)/shard_map/hop/pallas_call | solution.py:391
  15.7 1.9 %collective-permute-done.1.refs_2_ = bf16[64,1152]{1,0:T(8,128)(2,1)S(1)} collective-permute-done((bf16[64,1152]{1,0:T(8,128)(2,1)}, bf16[64,1152]{1,0:T(8,128)(2,1)S(1)}, u32[]{:S(2)}, u32[]{:S(2)}) %collective-permute-start.1) | collective-permute-done | bytes 147488 | tf_op jit(solution)/shard_map/ppermute | solution.py:582
  17.5 2.4 %collective-permute-done.2.refs_3_ = bf16[64,1152]{1,0:T(8,128)(2,1)S(1)} collective-permute-done((bf16[64,1152]{1,0:T(8,128)(2,1)}, bf16[64,1152]{1,0:T(8,128)(2,1)S(1)}, u32[]{:S(2)}, u32[]{:S(2)}) %collective-permute-start.2) | collective-permute-done | bytes 147488 | tf_op jit(solution)/shard_map/ppermute | solution.py:582
  19.9 0.6 down.1
  20.7 1.9 %collective-permute-start.3 = (bf16[256,768]{1,0:T(8,128)(2,1)S(1)}, bf16[256,768]{1,0:T(8,128)(2,1)S(1)}, u32[]{:S(2)}, u32[]{:S(2)}) collective-permute-start(bf16[256,768]{1,0:T(8,128)(2,1)S(1)} %hold.1.refs_4_), channel_id=1, source_target_pairs={{0,2},{2,3},{3,1},{1,0},{4,6},{6,7},{7,5},{5,4},{8,10},{10,11},{11... | collective-permute-start | bytes 1179656 | tf_op jit(solution)/shard_map/ppermute | solution.py:588
  22.6 4.2 %collective-permute-done.5 = bf16[128,128]{1,0:T(8,128)(2,1)S(1)} collective-permute-done((bf16[128,128]{1,0:T(8,128)(2,1)S(1)}, bf16[128,128]{1,0:T(8,128)(2,1)S(1)}, u32[]{:S(2)}, u32[]{:S(2)}) %collective-permute-start.5) | collective-permute-done | bytes 32800 | tf_op jit(solution)/shard_map/ppermute | solution.py:621
  26.8 2.6 %hop.6.refs_3_ = bf16[256,1280]{1,0:T(8,128)(2,1)S(1)} custom-call(bf16[256,1280]{1,0:T(8,128)(2,1)S(1)} %collective-permute-done.4.refs_0_, bf16[256,1024]{1,0:T(8,128)(2,1)S(1)} %copy-done.1, bf16[1024,8192]{1,0:T(8,128)(2,1)} %refs_7_.1, bf16[128,128]{1,0:T(8,128)(2,1)S(1)} %add_convert_fusion.refs_3_.refs_0_, bf16[256,768]{1,0:T(8,128)(2,1)S(1)} %hold.1.refs_4_), custom_call_target="tpu_custom_call" | custom-call | flops 20000000000 | bytes 40000000 | tf_op jit(solution)/shard_map/hop/pallas_call | solution.py:391
  29.4 2.7 %collective-permute-start.9 = (bf16[256,1280]{1,0:T(8,128)(2,1)S(1)}, bf16[256,1280]{1,0:T(8,128)(2,1)S(1)}, u32[]{:S(2)}, u32[]{:S(2)}) collective-permute-start(bf16[256,1280]{1,0:T(8,128)(2,1)S(1)} %hop.6.refs_3_), channel_id=1, source_target_pairs={{0,2},{2,3},{3,1},{1,0},{4,6},{6,7},{7,5},{5,4},{8,10},{10,11},{11... | collective-permute-start | bytes 1966088 | tf_op jit(solution)/shard_map/ppermute | solution.py:588
  32.0 4.1 %collective-permute-start.8 = (bf16[128,128]{1,0:T(8,128)(2,1)S(1)}, bf16[128,128]{1,0:T(8,128)(2,1)S(1)}, u32[]{:S(2)}, u32[]{:S(2)}) collective-permute-start(bf16[128,128]{1,0:T(8,128)(2,1)S(1)} %add_convert_fusion.refs_3_.refs_0_), channel_id=1, source_target_pairs={{0,3},{3,0},{4,7},{7,4},{8,11},{11,8},{12,15},{15,12},{16,19},{19,... | collective-permute-start | bytes 98312 | tf_op jit(solution)/shard_map/ppermute | solution.py:601
  36.2 1.3 %collective-permute-start.7 = (bf16[128,128]{1,0:T(8,128)(2,1)S(1)}, bf16[128,128]{1,0:T(8,128)(2,1)S(1)}, u32[]{:S(2)}, u32[]{:S(2)}) collective-permute-start(bf16[128,128]{1,0:T(8,128)(2,1)S(1)} %add_convert_fusion.refs_3_.refs_0_), channel_id=1, source_target_pairs={{0,2},{3,1},{4,6},{7,5},{8,10},{11,9},{12,14},{15,13},{16,18},{19,... | collective-permute-start | bytes 98312 | tf_op jit(solution)/shard_map/ppermute | solution.py:600
  37.5 2.0 %hop.7 = bf16[256,768]{1,0:T(8,128)(2,1)S(1)} custom-call(bf16[256,768]{1,0:T(8,128)(2,1)S(1)} %collective-permute-done.3.refs_0_, bf16[256,1024]{1,0:T(8,128)(2,1)S(1)} %copy-done.1, bf16[1024,8192]{1,0:T(8,128)(2,1)} %refs_7_.1, bf16[256,1280]{1,0:T(8,128)(2,1)S(1)} %hop.6.refs_3_), custom_call_target="tpu_custom_call" | custom-call | flops 4000000000 | bytes 8000000 | tf_op jit(solution)/shard_map/hop/pallas_call | solution.py:391
  39.5 1.1 %collective-permute-start.6 = (bf16[256,768]{1,0:T(8,128)(2,1)S(1)}, bf16[256,768]{1,0:T(8,128)(2,1)S(1)}, u32[]{:S(2)}, u32[]{:S(2)}) collective-permute-start(bf16[256,768]{1,0:T(8,128)(2,1)S(1)} %hop.7), channel_id=1, source_target_pairs={{0,2},{2,3},{3,1},{1,0},{4,6},{6,7},{7,5},{5,4},{8,10},{10,11},{11... | collective-permute-start | bytes 1179656 | tf_op jit(solution)/shard_map/ppermute | solution.py:588
  40.6 8.6 %collective-permute-done.9.refs_0_ = bf16[256,1280]{1,0:T(8,128)(2,1)S(1)} collective-permute-done((bf16[256,1280]{1,0:T(8,128)(2,1)S(1)}, bf16[256,1280]{1,0:T(8,128)(2,1)S(1)}, u32[]{:S(2)}, u32[]{:S(2)}) %collective-permute-start.9) | collective-permute-done | bytes 655392 | tf_op jit(solution)/shard_map/ppermute | solution.py:588
  49.2 2.6 %hop.8.refs_5_ = bf16[256,1280]{1,0:T(8,128)(2,1)S(1)} custom-call(bf16[256,1280]{1,0:T(8,128)(2,1)S(1)} %collective-permute-done.9.refs_0_, bf16[256,1024]{1,0:T(8,128)(2,1)S(1)} %copy-done.1, bf16[1024,8192]{1,0:T(8,128)(2,1)} %refs_7_.1), custom_call_target="tpu_custom_call" | custom-call | flops 20000000000 | bytes 40000000 | tf_op jit(solution)/shard_map/hop/pallas_call | solution.py:391
  51.8 3.4 %collective-permute-start.14 = (bf16[256,1280]{1,0:T(8,128)(2,1)S(1)}, bf16[256,1280]{1,0:T(8,128)(2,1)S(1)}, u32[]{:S(2)}, u32[]{:S(2)}) collective-permute-start(bf16[256,1280]{1,0:T(8,128)(2,1)S(1)} %hop.8.refs_5_), channel_id=1, source_target_pairs={{0,2},{2,3},{3,1},{1,0},{4,6},{6,7},{7,5},{5,4},{8,10},{10,11},{11... | collective-permute-start | bytes 1966088 | tf_op jit(solution)/shard_map/ppermute | solution.py:588
  55.2 0.8 %up.1 = (bf16[64,2048]{1,0:T(8,128)(2,1)S(1)}, bf16[64,2048]{1,0:T(8,128)(2,1)S(1)}, bf16[64,2048]{1,0:T(8,128)(2,1)S(1)}, bf16[64,2048]{1,0:T(8,128)(2,1)S(1)}) custom-call(bf16[128,128]{1,0:T(8,128)(2,1)S(1)} %add_convert_fusion.refs_3_.refs_0_, bf16[128,128]{1,0:T(8,128)(2,1)S(1)} %collective-permute-done.7.refs_1_, ...), custom_call_target="tpu_custom_call" | custom-call | tf_op jit(solution)/shard_map/up/pallas_call | solution.py:467
  56.1 1.6 %collective-permute-start.12 = (bf16[64,2048]{1,0:T(8,128)(2,1)S(1)}, bf16[64,2048]{1,0:T(8,128)(2,1)S(1)}, u32[]{:S(2)}, u32[]{:S(2)}) collective-permute-start(bf16[64,2048]{1,0:T(8,128)(2,1)S(1)} %get-tuple-element.30), channel_id=1, source_target_pairs={{0,8},{4,12},{8,0},{12,4},{1,9},{5,13},{9,1},{13,5},{2,10},{6,14},... | collective-permute-start | bytes 786440 | tf_op jit(solution)/shard_map/ppermute | solution.py:582
  58.0 1.0 %collective-permute-done.6.refs_0_ = bf16[256,768]{1,0:T(8,128)(2,1)S(1)} collective-permute-done((bf16[256,768]{1,0:T(8,128)(2,1)S(1)}, bf16[256,768]{1,0:T(8,128)(2,1)S(1)}, u32[]{:S(2)}, u32[]{:S(2)}) %collective-permute-start.6) | collective-permute-done | bytes 393248 | tf_op jit(solution)/shard_map/ppermute | solution.py:588
  59.0 2.1 %hop.9.refs_8_ = bf16[256,768]{1,0:T(8,128)(2,1)S(1)} custom-call(bf16[256,768]{1,0:T(8,128)(2,1)S(1)} %collective-permute-done.6.refs_0_, bf16[256,1024]{1,0:T(8,128)(2,1)S(1)} %copy-done.1, bf16[1024,8192]{1,0:T(8,128)(2,1)} %refs_7_.1, bf16[64,2048]{1,0:T(8,128)(2,1)S(1)} %get-tuple-element.28.refs_3_.refs_0_), custom_call_target="tpu_custom_call" | custom-call | tf_op jit(solution)/shard_map/hop/pallas_call | solution.py:391
  61.1 3.4 %collective-permute-start.10 = (bf16[256,768]{1,0:T(8,128)(2,1)S(1)}, bf16[256,768]{1,0:T(8,128)(2,1)S(1)}, u32[]{:S(2)}, u32[]{:S(2)}) collective-permute-start(bf16[256,768]{1,0:T(8,128)(2,1)S(1)} %hop.9.refs_8_), channel_id=1, source_target_pairs={{0,2},{2,3},{3,1},{1,0},{4,6},{6,7},{7,5},{5,4},{8,10},{10,11},{11... | collective-permute-start | bytes 1179656 | tf_op jit(solution)/shard_map/ppermute | solution.py:588
  64.5 0.8 collective-permute-done.12.refs_2_
  65.3 4.7 %collective-permute-done.13.refs_3_ = bf16[64,2048]{1,0:T(8,128)(2,1)S(1)} collective-permute-done((bf16[64,2048]{1,0:T(8,128)(2,1)S(1)}, bf16[64,2048]{1,0:T(8,128)(2,1)S(1)}, u32[]{:S(2)}, u32[]{:S(2)}) %collective-permute-start.13) | collective-permute-done | bytes 262176 | tf_op jit(solution)/shard_map/ppermute | solution.py:582
  70.0 4.5 %settle.1 = (f32[256,1280]{1,0:T(8,128)}, f32[256,768]{1,0:T(8,128)S(1)}) custom-call(bf16[64,2048]{1,0:T(8,128)(2,1)S(1)} %get-tuple-element.28.refs_3_.refs_0_, bf16[64,2048]{1,0:T(8,128)(2,1)S(1)} %collective-permute-done.11.refs_1_, bf16[64,2048]{1,0:T(8,128)(2,1)S(1)} %collective-permute-done.12.refs_2_, ...), custom_call_target="tpu_custom_call" | custom-call | flops 4000000000 | bytes 8000000 | tf_op jit(solution)/shard_map/settle/pallas_call | solution.py:497
  74.6 1.3 %copy-done.3 = f32[256,1280]{1,0:T(8,128)S(1)} copy-done((f32[256,1280]{1,0:T(8,128)S(1)}, f32[256,1280]{1,0:T(8,128)}, u32[]{:S(2)}) %copy-start.3) | copy-done | bytes 1310744
  75.9 0.9 %finish.2.refs_0_ = bf16[256,2048]{1,0:T(8,128)(2,1)} custom-call(bf16[256,1280]{1,0:T(8,128)(2,1)S(1)} %collective-permute-done.14.arrived_ref, f32[256,1280]{1,0:T(8,128)S(1)} %copy-done.3), custom_call_target="tpu_custom_call" | custom-call | tf_op jit(solution)/shard_map/finish/pallas_call | solution.py:529
  76.8 3.6 %collective-permute-done.10.arrived_ref = bf16[256,768]{1,0:T(8,128)(2,1)S(1)} collective-permute-done((bf16[256,768]{1,0:T(8,128)(2,1)S(1)}, bf16[256,768]{1,0:T(8,128)(2,1)S(1)}, u32[]{:S(2)}, u32[]{:S(2)}) %collective-permute-start.10) | collective-permute-done | bytes 393248 | tf_op jit(solution)/shard_map/ppermute | solution.py:588
  80.4 0.8 finish.3
  (27 shorter events, 0.5 us)
Async XLA Ops:
  6.6 20.2 %collective-permute-start.4 = (bf16[256,1280]{1,0:T(8,128)(2,1)}, bf16[256,1280]{1,0:T(8,128)(2,1)S(1)}, u32[]{:S(2)}, u32[]{:S(2)}) collective-permute-start(bf16[256,1280]{1,0:T(8,128)(2,1)} %get-tuple-element.26), channel_id=1, source_target_pairs={{0,2},{2,3},{3,1},{1,0},{4,6},{6,7},{7,5},{5,4},{8,10},{10,11},{11... | collective-permute-start | bytes 1966088 | tf_op jit(solution)/shard_map/ppermute | solution.py:588
  10.7 5.0 %collective-permute-start = (bf16[64,1152]{1,0:T(8,128)(2,1)}, bf16[64,1152]{1,0:T(8,128)(2,1)S(1)}, u32[]{:S(2)}, u32[]{:S(2)}) collective-permute-start(bf16[64,1152]{1,0:T(8,128)(2,1)} %get-tuple-element.22), channel_id=1, source_target_pairs={{0,4},{4,0},{8,12},{12,8},{1,5},{5,1},{9,13},{13,9},{2,6},{6,2},{1... | collective-permute-start | bytes 442376 | tf_op jit(solution)/shard_map/ppermute | solution.py:582
  10.7 6.9 %collective-permute-start.1 = (bf16[64,1152]{1,0:T(8,128)(2,1)}, bf16[64,1152]{1,0:T(8,128)(2,1)S(1)}, u32[]{:S(2)}, u32[]{:S(2)}) collective-permute-start(bf16[64,1152]{1,0:T(8,128)(2,1)} %get-tuple-element.23), channel_id=1, source_target_pairs={{0,8},{4,12},{8,0},{12,4},{1,9},{5,13},{9,1},{13,5},{2,10},{6,14},... | collective-permute-start | bytes 442376 | tf_op jit(solution)/shard_map/ppermute | solution.py:582
  12.2 7.7 %collective-permute-start.2 = (bf16[64,1152]{1,0:T(8,128)(2,1)}, bf16[64,1152]{1,0:T(8,128)(2,1)S(1)}, u32[]{:S(2)}, u32[]{:S(2)}) collective-permute-start(bf16[64,1152]{1,0:T(8,128)(2,1)} %get-tuple-element.24), channel_id=1, source_target_pairs={{0,12},{4,8},{8,4},{12,0},{1,13},{5,9},{9,5},{13,1},{2,14},{6,10},... | collective-permute-start | bytes 442376 | tf_op jit(solution)/shard_map/ppermute | solution.py:582
  12.5 1.0 %copy-start = (bf16[256,1024]{1,0:T(8,128)(2,1)S(1)}, bf16[256,1024]{1,0:T(8,128)(2,1)}, u32[]{:S(2)}) copy-start(bf16[256,1024]{1,0:T(8,128)(2,1)} %get-tuple-element.20.refs_0_.refs_1_.refs_5_) | copy-start | bytes 1572868
  13.6 6.3 %copy-start.5 = (bf16[8,64,1024]{2,1,0:T(8,128)(2,1)S(1)}, bf16[8,64,1024]{2,1,0:T(8,128)(2,1)}, u32[]{:S(2)}) copy-start(bf16[8,64,1024]{2,1,0:T(8,128)(2,1)} %refs_4_.2) | copy-start | bytes 3145732
  13.6 6.3 %copy-start.6 = (bf16[64,1152]{1,0:T(8,128)(2,1)S(1)}, bf16[64,1152]{1,0:T(8,128)(2,1)}, u32[]{:S(2)}) copy-start(bf16[64,1152]{1,0:T(8,128)(2,1)} %get-tuple-element.21.refs_0_) | copy-start | bytes 442372
  15.7 11.1 %copy-start.1 = (bf16[256,1024]{1,0:T(8,128)(2,1)S(1)}, bf16[256,1024]{1,0:T(8,128)(2,1)}, u32[]{:S(2)}) copy-start(bf16[256,1024]{1,0:T(8,128)(2,1)} %get-tuple-element.20.refs_0_.refs_1_.refs_5_) | copy-start | bytes 1572868
  20.6 6.1 %collective-permute-start.5 = (bf16[128,128]{1,0:T(8,128)(2,1)S(1)}, bf16[128,128]{1,0:T(8,128)(2,1)S(1)}, u32[]{:S(2)}, u32[]{:S(2)}) collective-permute-start(bf16[128,128]{1,0:T(8,128)(2,1)S(1)} %get-tuple-element.25.refs_1_), channel_id=1, source_target_pairs={{0,1},{1,0},{2,3},{3,2},{4,5},{5,4},{6,7},{7,6},{8,9},{9,8},{10,11... | collective-permute-start | bytes 98312 | tf_op jit(solution)/shard_map/ppermute | solution.py:621
  20.7 16.8 %collective-permute-start.3 = (bf16[256,768]{1,0:T(8,128)(2,1)S(1)}, bf16[256,768]{1,0:T(8,128)(2,1)S(1)}, u32[]{:S(2)}, u32[]{:S(2)}) collective-permute-start(bf16[256,768]{1,0:T(8,128)(2,1)S(1)} %hold.1.refs_4_), channel_id=1, source_target_pairs={{0,2},{2,3},{3,1},{1,0},{4,6},{6,7},{7,5},{5,4},{8,10},{10,11},{11... | collective-permute-start | bytes 1179656 | tf_op jit(solution)/shard_map/ppermute | solution.py:588
  29.4 19.8 %collective-permute-start.9 = (bf16[256,1280]{1,0:T(8,128)(2,1)S(1)}, bf16[256,1280]{1,0:T(8,128)(2,1)S(1)}, u32[]{:S(2)}, u32[]{:S(2)}) collective-permute-start(bf16[256,1280]{1,0:T(8,128)(2,1)S(1)} %hop.6.refs_3_), channel_id=1, source_target_pairs={{0,2},{2,3},{3,1},{1,0},{4,6},{6,7},{7,5},{5,4},{8,10},{10,11},{11... | collective-permute-start | bytes 1966088 | tf_op jit(solution)/shard_map/ppermute | solution.py:588
  32.0 23.2 %collective-permute-start.8 = (bf16[128,128]{1,0:T(8,128)(2,1)S(1)}, bf16[128,128]{1,0:T(8,128)(2,1)S(1)}, u32[]{:S(2)}, u32[]{:S(2)}) collective-permute-start(bf16[128,128]{1,0:T(8,128)(2,1)S(1)} %add_convert_fusion.refs_3_.refs_0_), channel_id=1, source_target_pairs={{0,3},{3,0},{4,7},{7,4},{8,11},{11,8},{12,15},{15,12},{16,19},{19,... | collective-permute-start | bytes 98312 | tf_op jit(solution)/shard_map/ppermute | solution.py:601
  36.2 19.1 %collective-permute-start.7 = (bf16[128,128]{1,0:T(8,128)(2,1)S(1)}, bf16[128,128]{1,0:T(8,128)(2,1)S(1)}, u32[]{:S(2)}, u32[]{:S(2)}) collective-permute-start(bf16[128,128]{1,0:T(8,128)(2,1)S(1)} %add_convert_fusion.refs_3_.refs_0_), channel_id=1, source_target_pairs={{0,2},{3,1},{4,6},{7,5},{8,10},{11,9},{12,14},{15,13},{16,18},{19,... | collective-permute-start | bytes 98312 | tf_op jit(solution)/shard_map/ppermute | solution.py:600
  39.5 15.7 %copy-start.2 = (bf16[8,64,2048]{2,1,0:T(8,128)(2,1)S(1)}, bf16[8,64,2048]{2,1,0:T(8,128)(2,1)}, u32[]{:S(2)}) copy-start(bf16[8,64,2048]{2,1,0:T(8,128)(2,1)} %refs_4_.3) | copy-start | bytes 6291460
  39.5 19.5 %collective-permute-start.6 = (bf16[256,768]{1,0:T(8,128)(2,1)S(1)}, bf16[256,768]{1,0:T(8,128)(2,1)S(1)}, u32[]{:S(2)}, u32[]{:S(2)}) collective-permute-start(bf16[256,768]{1,0:T(8,128)(2,1)S(1)} %hop.7), channel_id=1, source_target_pairs={{0,2},{2,3},{3,1},{1,0},{4,6},{6,7},{7,5},{5,4},{8,10},{10,11},{11... | collective-permute-start | bytes 1179656 | tf_op jit(solution)/shard_map/ppermute | solution.py:588
  51.8 22.8 %collective-permute-start.14 = (bf16[256,1280]{1,0:T(8,128)(2,1)S(1)}, bf16[256,1280]{1,0:T(8,128)(2,1)S(1)}, u32[]{:S(2)}, u32[]{:S(2)}) collective-permute-start(bf16[256,1280]{1,0:T(8,128)(2,1)S(1)} %hop.8.refs_5_), channel_id=1, source_target_pairs={{0,2},{2,3},{3,1},{1,0},{4,6},{6,7},{7,5},{5,4},{8,10},{10,11},{11... | collective-permute-start | bytes 1966088 | tf_op jit(solution)/shard_map/ppermute | solution.py:588
  56.1 8.5 %collective-permute-start.11 = (bf16[64,2048]{1,0:T(8,128)(2,1)S(1)}, bf16[64,2048]{1,0:T(8,128)(2,1)S(1)}, u32[]{:S(2)}, u32[]{:S(2)}) collective-permute-start(bf16[64,2048]{1,0:T(8,128)(2,1)S(1)} %get-tuple-element.29), channel_id=1, source_target_pairs={{0,4},{4,0},{8,12},{12,8},{1,5},{5,1},{9,13},{13,9},{2,6},{6,2},{1... | collective-permute-start | bytes 786440 | tf_op jit(solution)/shard_map/ppermute | solution.py:582
  56.1 9.2 %collective-permute-start.12 = (bf16[64,2048]{1,0:T(8,128)(2,1)S(1)}, bf16[64,2048]{1,0:T(8,128)(2,1)S(1)}, u32[]{:S(2)}, u32[]{:S(2)}) collective-permute-start(bf16[64,2048]{1,0:T(8,128)(2,1)S(1)} %get-tuple-element.30), channel_id=1, source_target_pairs={{0,8},{4,12},{8,0},{12,4},{1,9},{5,13},{9,1},{13,5},{2,10},{6,14},... | collective-permute-start | bytes 786440 | tf_op jit(solution)/shard_map/ppermute | solution.py:582
  57.7 12.3 %collective-permute-start.13 = (bf16[64,2048]{1,0:T(8,128)(2,1)S(1)}, bf16[64,2048]{1,0:T(8,128)(2,1)S(1)}, u32[]{:S(2)}, u32[]{:S(2)}) collective-permute-start(bf16[64,2048]{1,0:T(8,128)(2,1)S(1)} %get-tuple-element.31), channel_id=1, source_target_pairs={{0,12},{4,8},{8,4},{12,0},{1,13},{5,9},{9,5},{13,1},{2,14},{6,10},... | collective-permute-start | bytes 786440 | tf_op jit(solution)/shard_map/ppermute | solution.py:582
  59.0 11.0 %copy-start.4 = (bf16[256,2048]{1,0:T(8,128)(2,1)S(1)}, bf16[256,2048]{1,0:T(8,128)(2,1)}, u32[]{:S(2)}) copy-start(bf16[256,2048]{1,0:T(8,128)(2,1)} %refs_6_.1) | copy-start | bytes 3145732
  59.0 11.0 %copy-start.7 = (bf16[256,256]{1,0:T(8,128)(2,1)S(1)}, bf16[256,256]{1,0:T(8,128)(2,1)}, u32[]{:S(2)}) copy-start(bf16[256,256]{1,0:T(8,128)(2,1)} %get-tuple-element.32.refs_4_) | copy-start | bytes 393220
  61.1 19.2 %collective-permute-start.10 = (bf16[256,768]{1,0:T(8,128)(2,1)S(1)}, bf16[256,768]{1,0:T(8,128)(2,1)S(1)}, u32[]{:S(2)}, u32[]{:S(2)}) collective-permute-start(bf16[256,768]{1,0:T(8,128)(2,1)S(1)} %hop.9.refs_8_), channel_id=1, source_target_pairs={{0,2},{2,3},{3,1},{1,0},{4,6},{6,7},{7,5},{5,4},{8,10},{10,11},{11... | collective-permute-start | bytes 1179656 | tf_op jit(solution)/shard_map/ppermute | solution.py:588
  74.6 1.3 %copy-start.3 = (f32[256,1280]{1,0:T(8,128)S(1)}, f32[256,1280]{1,0:T(8,128)}, u32[]{:S(2)}) copy-start(f32[256,1280]{1,0:T(8,128)} %get-tuple-element.34.settled_ref) | copy-start | bytes 3932164

commit v21 on v20

--- a/solution.py
+++ b/solution.py
@@ -133,8 +133,24 @@
             (k_hbm, k_ref, cache * kv),
             (v_hbm, v_ref, cache * kv),
         )[kind]
-        rows = pl.ds(step * per * count, per * count)
-        return pltpu.make_async_copy(source.at[rows, :], target.at[rows, :], sems.at[kind, step])
+        half = per * count // 2
+        halves = []
+        for i in range(2):
+            rows = pl.ds(step * per * count + i * half, half)
+            halves.append(
+                pltpu.make_async_copy(
+                    source.at[rows, :], target.at[rows, :], sems.at[kind, step, i]
+                )
+            )
+        return halves
+
+    def start(kind, step):
+        for copy in part(kind, step):
+            copy.start()
+
+    def finished(kind, step):
+        for copy in part(kind, step):
+            copy.wait()
 
     small = [
         pltpu.make_async_copy(source, target, small_sems.at[i])
@@ -163,19 +179,19 @@
 
     chunk = out_ref.shape[1]
     weights = Weights(w_hbm, w_held, w_sems, column_owner(0) * block, chunk)
-    part(0, 0).start()
-    part(1, 0).start()
+    start(0, 0)
+    start(1, 0)
     for copy in small[:2]:
         copy.start()
-    part(0, 1).start()
-    part(1, 1).start()
-    part(2, 0).start()
+    start(0, 1)
+    start(1, 1)
+    start(2, 0)
     for copy in small[2:]:
         copy.start()
-    part(2, 1).start()
+    start(2, 1)
     for step in range(2, steps):
         for kind in range(3):
-            part(kind, step).start()
+            start(kind, step)
     weights.start()
 
     row = _iota((group_rows, group_cols), 0)
@@ -192,8 +208,8 @@
     ones = jnp.ones((max(group_cols, fresh_cols), LANES), jnp.bfloat16)
 
     def arrive(step):
-        part(0, step).wait()
-        part(1, step).wait()
+        finished(0, step)
+        finished(1, step)
 
     def scores(step):
         side = step % 2
@@ -269,7 +285,7 @@
     scores(0)
     softened = soften(0)
     for step in range(steps):
-        part(2, step).wait()
+        finished(2, step)
         if step == 0:
             for copy in small[2:]:
                 copy.wait()
@@ -359,7 +375,7 @@
             pltpu.VMEM((2, per * heads, columns), jnp.float32),
             pltpu.VMEM((2, per * heads, width), jnp.float32),
             pltpu.VMEM((SPAN * heads, SPAN * kv), jnp.float32),
-            pltpu.SemaphoreType.DMA((3, steps)),
+            pltpu.SemaphoreType.DMA((3, steps, 2)),
             pltpu.SemaphoreType.DMA((5,)),
         ]
         + Weights.scratch(weight.shape[0], chunk),

time: 81.5 us -> 81.9 us (level)
  no operation moved by 1% of the time
where the time goes in v21:
time: 81.9 us; the launch traced here: 81.5 us
  waiting for transfers between devices  27.1 us (33%)
  Pallas kernels  25.9 us (32%)
  starting transfers between devices  25.9 us (32%)
  local copies, waits for them, and re-layouts  2.38 us (3%)
    ppermute x6, starting transfers between devices, forward(): return lax.ppermute(x, 'tensor', ring)  16.6 us
    ppermute x6, waiting for transfers between devices, forward(): return lax.ppermute(x, 'tensor', ring)  13.2 us
    pallas_call x5, Pallas kernels, hop(): pl.pallas_call(functools.partial(hop_kernel, step, block, start, arriving...  11.3 us
    ppermute x6, waiting for transfers between devices, exchange(): lax.ppermute(blocks[r], 'dp', [(i, i ^ r) for i in range(replicas)])  9.72 us
    pallas_call x1, Pallas kernels, attend(): pl.pallas_call(functools.partial(attend_kernel, heads, kv, cache, steps,...  6.9 us
    pallas_call x1, Pallas kernels, settle(): pl.pallas_call(functools.partial(settle_kernel, step, replicas, len(after...  4.52 us
    ppermute x1, waiting for transfers between devices, per_device(): lax.ppermute(mid, 'tensor', [(i, i ^ 1) for i in range(count)])  4.17 us
    ppermute x1, starting transfers between devices, pair_sums(): other = lax.ppermute(x, 'tensor', far)  4.12 us
  transfers between devices with their start and end apart: 15, of which 8 were waited for; matrix products, arithmetic and copies ran while one was open for 0% of the time, Pallas kernels for 22%

profile of v21, /device:TPU:0, one launch (start us, length us, event | category | flops | bytes accessed | tf_op | source)
XLA Modules:
  0.0 81.5 jit_solution(16655428458215647160)
XLA Ops:
  0.0 6.9 %attend.1 = (bf16[256,1024]{1,0:T(8,128)(2,1)}, bf16[256,1280]{1,0:T(8,128)(2,1)}, bf16[256,256]{1,0:T(8,128)(2,1)}, bf16[64,1152]{1,0:T(8,128)(2,1)}, bf16[64,1...) custom-call(s32[1,256]{1,0:T(1,128)} %bitcast.13, s32[1,256]{1,0:T(1,128)} %bitcast.14, ...), custom_call_target="tpu_custom_call" | custom-call | tf_op jit(solution)/shard_map/attend/pallas_call | solution.py:356
  6.9 4.1 %collective-permute-start.4 = (bf16[256,1280]{1,0:T(8,128)(2,1)}, bf16[256,1280]{1,0:T(8,128)(2,1)S(1)}, u32[]{:S(2)}, u32[]{:S(2)}) collective-permute-start(bf16[256,1280]{1,0:T(8,128)(2,1)} %get-tuple-element.26), channel_id=1, source_target_pairs={{0,2},{2,3},{3,1},{1,0},{4,6},{6,7},{7,5},{5,4},{8,10},{10,11},{11... | collective-permute-start | bytes 1966088 | tf_op jit(solution)/shard_map/ppermute | solution.py:604
  11.0 1.5 %collective-permute-start.1 = (bf16[64,1152]{1,0:T(8,128)(2,1)}, bf16[64,1152]{1,0:T(8,128)(2,1)S(1)}, u32[]{:S(2)}, u32[]{:S(2)}) collective-permute-start(bf16[64,1152]{1,0:T(8,128)(2,1)} %get-tuple-element.23), channel_id=1, source_target_pairs={{0,8},{4,12},{8,0},{12,4},{1,9},{5,13},{9,1},{13,5},{2,10},{6,14},... | collective-permute-start | bytes 442376 | tf_op jit(solution)/shard_map/ppermute | solution.py:598
  12.5 0.4 collective-permute-start.2
  12.9 1.0 %copy-done = bf16[256,1024]{1,0:T(8,128)(2,1)S(1)} copy-done((bf16[256,1024]{1,0:T(8,128)(2,1)S(1)}, bf16[256,1024]{1,0:T(8,128)(2,1)}, u32[]{:S(2)}) %copy-start) | copy-done | bytes 524312
  13.9 2.1 %hop.5.refs_5_.refs_0_ = bf16[256,768]{1,0:T(8,128)(2,1)S(1)} custom-call(bf16[256,1024]{1,0:T(8,128)(2,1)S(1)} %copy-done, bf16[1024,8192]{1,0:T(8,128)(2,1)} %refs_7_.1), custom_call_target="tpu_custom_call" | custom-call | tf_op jit(solution)/shard_map/hop/pallas_call | solution.py:407
  16.0 1.9 %collective-permute-done.1.refs_2_ = bf16[64,1152]{1,0:T(8,128)(2,1)S(1)} collective-permute-done((bf16[64,1152]{1,0:T(8,128)(2,1)}, bf16[64,1152]{1,0:T(8,128)(2,1)S(1)}, u32[]{:S(2)}, u32[]{:S(2)}) %collective-permute-start.1) | collective-permute-done | bytes 147488 | tf_op jit(solution)/shard_map/ppermute | solution.py:598
  17.9 2.4 %collective-permute-done.2.refs_3_ = bf16[64,1152]{1,0:T(8,128)(2,1)S(1)} collective-permute-done((bf16[64,1152]{1,0:T(8,128)(2,1)}, bf16[64,1152]{1,0:T(8,128)(2,1)S(1)}, u32[]{:S(2)}, u32[]{:S(2)}) %collective-permute-start.2) | collective-permute-done | bytes 147488 | tf_op jit(solution)/shard_map/ppermute | solution.py:598
  20.2 0.6 down.1
  21.0 1.9 %collective-permute-start.3 = (bf16[256,768]{1,0:T(8,128)(2,1)S(1)}, bf16[256,768]{1,0:T(8,128)(2,1)S(1)}, u32[]{:S(2)}, u32[]{:S(2)}) collective-permute-start(bf16[256,768]{1,0:T(8,128)(2,1)S(1)} %hold.1.refs_4_), channel_id=1, source_target_pairs={{0,2},{2,3},{3,1},{1,0},{4,6},{6,7},{7,5},{5,4},{8,10},{10,11},{11... | collective-permute-start | bytes 1179656 | tf_op jit(solution)/shard_map/ppermute | solution.py:604
  22.9 4.2 %collective-permute-done.5 = bf16[128,128]{1,0:T(8,128)(2,1)S(1)} collective-permute-done((bf16[128,128]{1,0:T(8,128)(2,1)S(1)}, bf16[128,128]{1,0:T(8,128)(2,1)S(1)}, u32[]{:S(2)}, u32[]{:S(2)}) %collective-permute-start.5) | collective-permute-done | bytes 32800 | tf_op jit(solution)/shard_map/ppermute | solution.py:637
  27.1 2.6 %hop.6.refs_3_ = bf16[256,1280]{1,0:T(8,128)(2,1)S(1)} custom-call(bf16[256,1280]{1,0:T(8,128)(2,1)S(1)} %collective-permute-done.4.refs_0_, bf16[256,1024]{1,0:T(8,128)(2,1)S(1)} %copy-done.1, bf16[1024,8192]{1,0:T(8,128)(2,1)} %refs_7_.1, bf16[128,128]{1,0:T(8,128)(2,1)S(1)} %add_convert_fusion.refs_3_.refs_0_, bf16[256,768]{1,0:T(8,128)(2,1)S(1)} %hold.1.refs_4_), custom_call_target="tpu_custom_call" | custom-call | flops 20000000000 | bytes 40000000 | tf_op jit(solution)/shard_map/hop/pallas_call | solution.py:407
  29.7 2.7 %collective-permute-start.9 = (bf16[256,1280]{1,0:T(8,128)(2,1)S(1)}, bf16[256,1280]{1,0:T(8,128)(2,1)S(1)}, u32[]{:S(2)}, u32[]{:S(2)}) collective-permute-start(bf16[256,1280]{1,0:T(8,128)(2,1)S(1)} %hop.6.refs_3_), channel_id=1, source_target_pairs={{0,2},{2,3},{3,1},{1,0},{4,6},{6,7},{7,5},{5,4},{8,10},{10,11},{11... | collective-permute-start | bytes 1966088 | tf_op jit(solution)/shard_map/ppermute | solution.py:604
  32.4 4.1 %collective-permute-start.8 = (bf16[128,128]{1,0:T(8,128)(2,1)S(1)}, bf16[128,128]{1,0:T(8,128)(2,1)S(1)}, u32[]{:S(2)}, u32[]{:S(2)}) collective-permute-start(bf16[128,128]{1,0:T(8,128)(2,1)S(1)} %add_convert_fusion.refs_3_.refs_0_), channel_id=1, source_target_pairs={{0,3},{3,0},{4,7},{7,4},{8,11},{11,8},{12,15},{15,12},{16,19},{19,... | collective-permute-start | bytes 98312 | tf_op jit(solution)/shard_map/ppermute | solution.py:617
  36.5 1.3 %collective-permute-start.7 = (bf16[128,128]{1,0:T(8,128)(2,1)S(1)}, bf16[128,128]{1,0:T(8,128)(2,1)S(1)}, u32[]{:S(2)}, u32[]{:S(2)}) collective-permute-start(bf16[128,128]{1,0:T(8,128)(2,1)S(1)} %add_convert_fusion.refs_3_.refs_0_), channel_id=1, source_target_pairs={{0,2},{3,1},{4,6},{7,5},{8,10},{11,9},{12,14},{15,13},{16,18},{19,... | collective-permute-start | bytes 98312 | tf_op jit(solution)/shard_map/ppermute | solution.py:616
  37.8 2.0 %hop.7 = bf16[256,768]{1,0:T(8,128)(2,1)S(1)} custom-call(bf16[256,768]{1,0:T(8,128)(2,1)S(1)} %collective-permute-done.3.refs_0_, bf16[256,1024]{1,0:T(8,128)(2,1)S(1)} %copy-done.1, bf16[1024,8192]{1,0:T(8,128)(2,1)} %refs_7_.1, bf16[256,1280]{1,0:T(8,128)(2,1)S(1)} %hop.6.refs_3_), custom_call_target="tpu_custom_call" | custom-call | flops 4000000000 | bytes 8000000 | tf_op jit(solution)/shard_map/hop/pallas_call | solution.py:407
  39.8 1.1 %collective-permute-start.6 = (bf16[256,768]{1,0:T(8,128)(2,1)S(1)}, bf16[256,768]{1,0:T(8,128)(2,1)S(1)}, u32[]{:S(2)}, u32[]{:S(2)}) collective-permute-start(bf16[256,768]{1,0:T(8,128)(2,1)S(1)} %hop.7), channel_id=1, source_target_pairs={{0,2},{2,3},{3,1},{1,0},{4,6},{6,7},{7,5},{5,4},{8,10},{10,11},{11... | collective-permute-start | bytes 1179656 | tf_op jit(solution)/shard_map/ppermute | solution.py:604
  40.9 8.6 %collective-permute-done.9.refs_0_ = bf16[256,1280]{1,0:T(8,128)(2,1)S(1)} collective-permute-done((bf16[256,1280]{1,0:T(8,128)(2,1)S(1)}, bf16[256,1280]{1,0:T(8,128)(2,1)S(1)}, u32[]{:S(2)}, u32[]{:S(2)}) %collective-permute-start.9) | collective-permute-done | bytes 655392 | tf_op jit(solution)/shard_map/ppermute | solution.py:604
  49.5 2.6 %hop.8.refs_5_ = bf16[256,1280]{1,0:T(8,128)(2,1)S(1)} custom-call(bf16[256,1280]{1,0:T(8,128)(2,1)S(1)} %collective-permute-done.9.refs_0_, bf16[256,1024]{1,0:T(8,128)(2,1)S(1)} %copy-done.1, bf16[1024,8192]{1,0:T(8,128)(2,1)} %refs_7_.1), custom_call_target="tpu_custom_call" | custom-call | flops 20000000000 | bytes 40000000 | tf_op jit(solution)/shard_map/hop/pallas_call | solution.py:407
  52.1 3.4 %collective-permute-start.14 = (bf16[256,1280]{1,0:T(8,128)(2,1)S(1)}, bf16[256,1280]{1,0:T(8,128)(2,1)S(1)}, u32[]{:S(2)}, u32[]{:S(2)}) collective-permute-start(bf16[256,1280]{1,0:T(8,128)(2,1)S(1)} %hop.8.refs_5_), channel_id=1, source_target_pairs={{0,2},{2,3},{3,1},{1,0},{4,6},{6,7},{7,5},{5,4},{8,10},{10,11},{11... | collective-permute-start | bytes 1966088 | tf_op jit(solution)/shard_map/ppermute | solution.py:604
  55.5 0.8 %up.1 = (bf16[64,2048]{1,0:T(8,128)(2,1)S(1)}, bf16[64,2048]{1,0:T(8,128)(2,1)S(1)}, bf16[64,2048]{1,0:T(8,128)(2,1)S(1)}, bf16[64,2048]{1,0:T(8,128)(2,1)S(1)}) custom-call(bf16[128,128]{1,0:T(8,128)(2,1)S(1)} %add_convert_fusion.refs_3_.refs_0_, bf16[128,128]{1,0:T(8,128)(2,1)S(1)} %collective-permute-done.7.refs_1_, ...), custom_call_target="tpu_custom_call" | custom-call | tf_op jit(solution)/shard_map/up/pallas_call | solution.py:483
  56.5 1.6 %collective-permute-start.12 = (bf16[64,2048]{1,0:T(8,128)(2,1)S(1)}, bf16[64,2048]{1,0:T(8,128)(2,1)S(1)}, u32[]{:S(2)}, u32[]{:S(2)}) collective-permute-start(bf16[64,2048]{1,0:T(8,128)(2,1)S(1)} %get-tuple-element.30), channel_id=1, source_target_pairs={{0,8},{4,12},{8,0},{12,4},{1,9},{5,13},{9,1},{13,5},{2,10},{6,14},... | collective-permute-start | bytes 786440 | tf_op jit(solution)/shard_map/ppermute | solution.py:598
  58.3 1.0 %collective-permute-done.6.refs_0_ = bf16[256,768]{1,0:T(8,128)(2,1)S(1)} collective-permute-done((bf16[256,768]{1,0:T(8,128)(2,1)S(1)}, bf16[256,768]{1,0:T(8,128)(2,1)S(1)}, u32[]{:S(2)}, u32[]{:S(2)}) %collective-permute-start.6) | collective-permute-done | bytes 393248 | tf_op jit(solution)/shard_map/ppermute | solution.py:604
  59.4 2.1 %hop.9.refs_8_ = bf16[256,768]{1,0:T(8,128)(2,1)S(1)} custom-call(bf16[256,768]{1,0:T(8,128)(2,1)S(1)} %collective-permute-done.6.refs_0_, bf16[256,1024]{1,0:T(8,128)(2,1)S(1)} %copy-done.1, bf16[1024,8192]{1,0:T(8,128)(2,1)} %refs_7_.1, bf16[64,2048]{1,0:T(8,128)(2,1)S(1)} %get-tuple-element.28.refs_3_.refs_0_), custom_call_target="tpu_custom_call" | custom-call | tf_op jit(solution)/shard_map/hop/pallas_call | solution.py:407
  61.4 3.4 %collective-permute-start.10 = (bf16[256,768]{1,0:T(8,128)(2,1)S(1)}, bf16[256,768]{1,0:T(8,128)(2,1)S(1)}, u32[]{:S(2)}, u32[]{:S(2)}) collective-permute-start(bf16[256,768]{1,0:T(8,128)(2,1)S(1)} %hop.9.refs_8_), channel_id=1, source_target_pairs={{0,2},{2,3},{3,1},{1,0},{4,6},{6,7},{7,5},{5,4},{8,10},{10,11},{11... | collective-permute-start | bytes 1179656 | tf_op jit(solution)/shard_map/ppermute | solution.py:604
  64.9 0.8 collective-permute-done.12.refs_2_
  65.6 4.7 %collective-permute-done.13.refs_3_ = bf16[64,2048]{1,0:T(8,128)(2,1)S(1)} collective-permute-done((bf16[64,2048]{1,0:T(8,128)(2,1)S(1)}, bf16[64,2048]{1,0:T(8,128)(2,1)S(1)}, u32[]{:S(2)}, u32[]{:S(2)}) %collective-permute-start.13) | collective-permute-done | bytes 262176 | tf_op jit(solution)/shard_map/ppermute | solution.py:598
  70.3 4.5 %settle.1 = (f32[256,1280]{1,0:T(8,128)}, f32[256,768]{1,0:T(8,128)S(1)}) custom-call(bf16[64,2048]{1,0:T(8,128)(2,1)S(1)} %get-tuple-element.28.refs_3_.refs_0_, bf16[64,2048]{1,0:T(8,128)(2,1)S(1)} %collective-permute-done.11.refs_1_, bf16[64,2048]{1,0:T(8,128)(2,1)S(1)} %collective-permute-done.12.refs_2_, ...), custom_call_target="tpu_custom_call" | custom-call | flops 4000000000 | bytes 8000000 | tf_op jit(solution)/shard_map/settle/pallas_call | solution.py:513
  74.9 1.3 %copy-done.3 = f32[256,1280]{1,0:T(8,128)S(1)} copy-done((f32[256,1280]{1,0:T(8,128)S(1)}, f32[256,1280]{1,0:T(8,128)}, u32[]{:S(2)}) %copy-start.3) | copy-done | bytes 1310744
  76.2 0.9 %finish.2.refs_0_ = bf16[256,2048]{1,0:T(8,128)(2,1)} custom-call(bf16[256,1280]{1,0:T(8,128)(2,1)S(1)} %collective-permute-done.14.arrived_ref, f32[256,1280]{1,0:T(8,128)S(1)} %copy-done.3), custom_call_target="tpu_custom_call" | custom-call | tf_op jit(solution)/shard_map/finish/pallas_call | solution.py:545
  77.1 3.6 %collective-permute-done.10.arrived_ref = bf16[256,768]{1,0:T(8,128)(2,1)S(1)} collective-permute-done((bf16[256,768]{1,0:T(8,128)(2,1)S(1)}, bf16[256,768]{1,0:T(8,128)(2,1)S(1)}, u32[]{:S(2)}, u32[]{:S(2)}) %collective-permute-start.10) | collective-permute-done | bytes 393248 | tf_op jit(solution)/shard_map/ppermute | solution.py:604
  80.7 0.8 finish.3
  (27 shorter events, 0.5 us)
Async XLA Ops:
  6.9 20.2 %collective-permute-start.4 = (bf16[256,1280]{1,0:T(8,128)(2,1)}, bf16[256,1280]{1,0:T(8,128)(2,1)S(1)}, u32[]{:S(2)}, u32[]{:S(2)}) collective-permute-start(bf16[256,1280]{1,0:T(8,128)(2,1)} %get-tuple-element.26), channel_id=1, source_target_pairs={{0,2},{2,3},{3,1},{1,0},{4,6},{6,7},{7,5},{5,4},{8,10},{10,11},{11... | collective-permute-start | bytes 1966088 | tf_op jit(solution)/shard_map/ppermute | solution.py:604
  11.0 5.0 %collective-permute-start = (bf16[64,1152]{1,0:T(8,128)(2,1)}, bf16[64,1152]{1,0:T(8,128)(2,1)S(1)}, u32[]{:S(2)}, u32[]{:S(2)}) collective-permute-start(bf16[64,1152]{1,0:T(8,128)(2,1)} %get-tuple-element.22), channel_id=1, source_target_pairs={{0,4},{4,0},{8,12},{12,8},{1,5},{5,1},{9,13},{13,9},{2,6},{6,2},{1... | collective-permute-start | bytes 442376 | tf_op jit(solution)/shard_map/ppermute | solution.py:598
  11.0 6.9 %collective-permute-start.1 = (bf16[64,1152]{1,0:T(8,128)(2,1)}, bf16[64,1152]{1,0:T(8,128)(2,1)S(1)}, u32[]{:S(2)}, u32[]{:S(2)}) collective-permute-start(bf16[64,1152]{1,0:T(8,128)(2,1)} %get-tuple-element.23), channel_id=1, source_target_pairs={{0,8},{4,12},{8,0},{12,4},{1,9},{5,13},{9,1},{13,5},{2,10},{6,14},... | collective-permute-start | bytes 442376 | tf_op jit(solution)/shard_map/ppermute | solution.py:598
  12.5 7.8 %collective-permute-start.2 = (bf16[64,1152]{1,0:T(8,128)(2,1)}, bf16[64,1152]{1,0:T(8,128)(2,1)S(1)}, u32[]{:S(2)}, u32[]{:S(2)}) collective-permute-start(bf16[64,1152]{1,0:T(8,128)(2,1)} %get-tuple-element.24), channel_id=1, source_target_pairs={{0,12},{4,8},{8,4},{12,0},{1,13},{5,9},{9,5},{13,1},{2,14},{6,10},... | collective-permute-start | bytes 442376 | tf_op jit(solution)/shard_map/ppermute | solution.py:598
  12.9 1.0 %copy-start = (bf16[256,1024]{1,0:T(8,128)(2,1)S(1)}, bf16[256,1024]{1,0:T(8,128)(2,1)}, u32[]{:S(2)}) copy-start(bf16[256,1024]{1,0:T(8,128)(2,1)} %get-tuple-element.20.refs_0_.refs_1_.refs_5_) | copy-start | bytes 1572868
  13.9 6.3 %copy-start.5 = (bf16[8,64,1024]{2,1,0:T(8,128)(2,1)S(1)}, bf16[8,64,1024]{2,1,0:T(8,128)(2,1)}, u32[]{:S(2)}) copy-start(bf16[8,64,1024]{2,1,0:T(8,128)(2,1)} %refs_4_.2) | copy-start | bytes 3145732
  13.9 6.3 %copy-start.6 = (bf16[64,1152]{1,0:T(8,128)(2,1)S(1)}, bf16[64,1152]{1,0:T(8,128)(2,1)}, u32[]{:S(2)}) copy-start(bf16[64,1152]{1,0:T(8,128)(2,1)} %get-tuple-element.21.refs_0_) | copy-start | bytes 442372
  16.0 11.1 %copy-start.1 = (bf16[256,1024]{1,0:T(8,128)(2,1)S(1)}, bf16[256,1024]{1,0:T(8,128)(2,1)}, u32[]{:S(2)}) copy-start(bf16[256,1024]{1,0:T(8,128)(2,1)} %get-tuple-element.20.refs_0_.refs_1_.refs_5_) | copy-start | bytes 1572868
  20.9 6.2 %collective-permute-start.5 = (bf16[128,128]{1,0:T(8,128)(2,1)S(1)}, bf16[128,128]{1,0:T(8,128)(2,1)S(1)}, u32[]{:S(2)}, u32[]{:S(2)}) collective-permute-start(bf16[128,128]{1,0:T(8,128)(2,1)S(1)} %get-tuple-element.25.refs_1_), channel_id=1, source_target_pairs={{0,1},{1,0},{2,3},{3,2},{4,5},{5,4},{6,7},{7,6},{8,9},{9,8},{10,11... | collective-permute-start | bytes 98312 | tf_op jit(solution)/shard_map/ppermute | solution.py:637
  21.0 16.8 %collective-permute-start.3 = (bf16[256,768]{1,0:T(8,128)(2,1)S(1)}, bf16[256,768]{1,0:T(8,128)(2,1)S(1)}, u32[]{:S(2)}, u32[]{:S(2)}) collective-permute-start(bf16[256,768]{1,0:T(8,128)(2,1)S(1)} %hold.1.refs_4_), channel_id=1, source_target_pairs={{0,2},{2,3},{3,1},{1,0},{4,6},{6,7},{7,5},{5,4},{8,10},{10,11},{11... | collective-permute-start | bytes 1179656 | tf_op jit(solution)/shard_map/ppermute | solution.py:604
  29.7 19.8 %collective-permute-start.9 = (bf16[256,1280]{1,0:T(8,128)(2,1)S(1)}, bf16[256,1280]{1,0:T(8,128)(2,1)S(1)}, u32[]{:S(2)}, u32[]{:S(2)}) collective-permute-start(bf16[256,1280]{1,0:T(8,128)(2,1)S(1)} %hop.6.refs_3_), channel_id=1, source_target_pairs={{0,2},{2,3},{3,1},{1,0},{4,6},{6,7},{7,5},{5,4},{8,10},{10,11},{11... | collective-permute-start | bytes 1966088 | tf_op jit(solution)/shard_map/ppermute | solution.py:604
  32.4 23.2 %collective-permute-start.8 = (bf16[128,128]{1,0:T(8,128)(2,1)S(1)}, bf16[128,128]{1,0:T(8,128)(2,1)S(1)}, u32[]{:S(2)}, u32[]{:S(2)}) collective-permute-start(bf16[128,128]{1,0:T(8,128)(2,1)S(1)} %add_convert_fusion.refs_3_.refs_0_), channel_id=1, source_target_pairs={{0,3},{3,0},{4,7},{7,4},{8,11},{11,8},{12,15},{15,12},{16,19},{19,... | collective-permute-start | bytes 98312 | tf_op jit(solution)/shard_map/ppermute | solution.py:617
  36.5 19.1 %collective-permute-start.7 = (bf16[128,128]{1,0:T(8,128)(2,1)S(1)}, bf16[128,128]{1,0:T(8,128)(2,1)S(1)}, u32[]{:S(2)}, u32[]{:S(2)}) collective-permute-start(bf16[128,128]{1,0:T(8,128)(2,1)S(1)} %add_convert_fusion.refs_3_.refs_0_), channel_id=1, source_target_pairs={{0,2},{3,1},{4,6},{7,5},{8,10},{11,9},{12,14},{15,13},{16,18},{19,... | collective-permute-start | bytes 98312 | tf_op jit(solution)/shard_map/ppermute | solution.py:616
  39.8 15.7 %copy-start.2 = (bf16[8,64,2048]{2,1,0:T(8,128)(2,1)S(1)}, bf16[8,64,2048]{2,1,0:T(8,128)(2,1)}, u32[]{:S(2)}) copy-start(bf16[8,64,2048]{2,1,0:T(8,128)(2,1)} %refs_4_.3) | copy-start | bytes 6291460
  39.8 19.5 %collective-permute-start.6 = (bf16[256,768]{1,0:T(8,128)(2,1)S(1)}, bf16[256,768]{1,0:T(8,128)(2,1)S(1)}, u32[]{:S(2)}, u32[]{:S(2)}) collective-permute-start(bf16[256,768]{1,0:T(8,128)(2,1)S(1)} %hop.7), channel_id=1, source_target_pairs={{0,2},{2,3},{3,1},{1,0},{4,6},{6,7},{7,5},{5,4},{8,10},{10,11},{11... | collective-permute-start | bytes 1179656 | tf_op jit(solution)/shard_map/ppermute | solution.py:604
  52.1 22.8 %collective-permute-start.14 = (bf16[256,1280]{1,0:T(8,128)(2,1)S(1)}, bf16[256,1280]{1,0:T(8,128)(2,1)S(1)}, u32[]{:S(2)}, u32[]{:S(2)}) collective-permute-start(bf16[256,1280]{1,0:T(8,128)(2,1)S(1)} %hop.8.refs_5_), channel_id=1, source_target_pairs={{0,2},{2,3},{3,1},{1,0},{4,6},{6,7},{7,5},{5,4},{8,10},{10,11},{11... | collective-permute-start | bytes 1966088 | tf_op jit(solution)/shard_map/ppermute | solution.py:604
  56.4 8.5 %collective-permute-start.11 = (bf16[64,2048]{1,0:T(8,128)(2,1)S(1)}, bf16[64,2048]{1,0:T(8,128)(2,1)S(1)}, u32[]{:S(2)}, u32[]{:S(2)}) collective-permute-start(bf16[64,2048]{1,0:T(8,128)(2,1)S(1)} %get-tuple-element.29), channel_id=1, source_target_pairs={{0,4},{4,0},{8,12},{12,8},{1,5},{5,1},{9,13},{13,9},{2,6},{6,2},{1... | collective-permute-start | bytes 786440 | tf_op jit(solution)/shard_map/ppermute | solution.py:598
  56.5 9.2 %collective-permute-start.12 = (bf16[64,2048]{1,0:T(8,128)(2,1)S(1)}, bf16[64,2048]{1,0:T(8,128)(2,1)S(1)}, u32[]{:S(2)}, u32[]{:S(2)}) collective-permute-start(bf16[64,2048]{1,0:T(8,128)(2,1)S(1)} %get-tuple-element.30), channel_id=1, source_target_pairs={{0,8},{4,12},{8,0},{12,4},{1,9},{5,13},{9,1},{13,5},{2,10},{6,14},... | collective-permute-start | bytes 786440 | tf_op jit(solution)/shard_map/ppermute | solution.py:598
  58.0 12.3 %collective-permute-start.13 = (bf16[64,2048]{1,0:T(8,128)(2,1)S(1)}, bf16[64,2048]{1,0:T(8,128)(2,1)S(1)}, u32[]{:S(2)}, u32[]{:S(2)}) collective-permute-start(bf16[64,2048]{1,0:T(8,128)(2,1)S(1)} %get-tuple-element.31), channel_id=1, source_target_pairs={{0,12},{4,8},{8,4},{12,0},{1,13},{5,9},{9,5},{13,1},{2,14},{6,10},... | collective-permute-start | bytes 786440 | tf_op jit(solution)/shard_map/ppermute | solution.py:598
  59.4 11.0 %copy-start.4 = (bf16[256,2048]{1,0:T(8,128)(2,1)S(1)}, bf16[256,2048]{1,0:T(8,128)(2,1)}, u32[]{:S(2)}) copy-start(bf16[256,2048]{1,0:T(8,128)(2,1)} %refs_6_.1) | copy-start | bytes 3145732
  59.4 11.0 %copy-start.7 = (bf16[256,256]{1,0:T(8,128)(2,1)S(1)}, bf16[256,256]{1,0:T(8,128)(2,1)}, u32[]{:S(2)}) copy-start(bf16[256,256]{1,0:T(8,128)(2,1)} %get-tuple-element.32.refs_4_) | copy-start | bytes 393220
  61.4 19.2 %collective-permute-start.10 = (bf16[256,768]{1,0:T(8,128)(2,1)S(1)}, bf16[256,768]{1,0:T(8,128)(2,1)S(1)}, u32[]{:S(2)}, u32[]{:S(2)}) collective-permute-start(bf16[256,768]{1,0:T(8,128)(2,1)S(1)} %hop.9.refs_8_), channel_id=1, source_target_pairs={{0,2},{2,3},{3,1},{1,0},{4,6},{6,7},{7,5},{5,4},{8,10},{10,11},{11... | collective-permute-start | bytes 1179656 | tf_op jit(solution)/shard_map/ppermute | solution.py:604
  74.9 1.3 %copy-start.3 = (f32[256,1280]{1,0:T(8,128)S(1)}, f32[256,1280]{1,0:T(8,128)}, u32[]{:S(2)}) copy-start(f32[256,1280]{1,0:T(8,128)} %get-tuple-element.34.settled_ref) | copy-start | bytes 3932164

commit v22 on v19

--- a/solution.py
+++ b/solution.py
@@ -272,14 +272,17 @@
             a_ref[pl.ds(step * per, per), pl.ds(h * width, width)] = mixed_ref[
                 side, pl.ds(h, per, stride=heads), :
             ].astype(jnp.bfloat16)
-        rows = pl.ds(step * per, per)
-        leave(a_ref.at[rows, :], a_hbm.at[rows, :])
+        if step + 1 < steps:
+            rows = pl.ds(step * per, per)
+            leave(a_ref.at[rows, :], a_hbm.at[rows, :])
 
     sent_ref[:, pl.ds(0, heads * width)] = _dot(chosen_ref[...], a_ref[...]).astype(jnp.bfloat16)
-    leave(chosen_ref, chosen_hbm)
+    multiply(requests - per, per)
     for r in range(replicas):
         leave(sent_ref.at[pl.ds(r * CAP, CAP), :], sent_hbm[r])
-    multiply(requests - per, per)
+    rows = pl.ds(requests - per, per)
+    leave(a_ref.at[rows, :], a_hbm.at[rows, :])
+    leave(chosen_ref, chosen_hbm)
     for copy in leaving:
         copy.wait()
 

time: 81.5 us -> 81.8 us (level)
  no operation moved by 1% of the time
where the time goes in v22:
time: 81.8 us; the launch traced here: 81.4 us
  waiting for transfers between devices  27.1 us (33%)
  starting transfers between devices  25.9 us (32%)
  Pallas kernels  25.8 us (32%)
  local copies, waits for them, and re-layouts  2.38 us (3%)
    ppermute x6, starting transfers between devices, forward(): return lax.ppermute(x, 'tensor', ring)  16.6 us
    ppermute x6, waiting for transfers between devices, forward(): return lax.ppermute(x, 'tensor', ring)  13.2 us
    pallas_call x5, Pallas kernels, hop(): pl.pallas_call(functools.partial(hop_kernel, step, block, start, arriving...  11.3 us
    ppermute x6, waiting for transfers between devices, exchange(): lax.ppermute(blocks[r], 'dp', [(i, i ^ r) for i in range(replicas)])  9.72 us
    pallas_call x1, Pallas kernels, attend(): pl.pallas_call(functools.partial(attend_kernel, heads, kv, cache, steps,...  6.87 us
    pallas_call x1, Pallas kernels, settle(): pl.pallas_call(functools.partial(settle_kernel, step, replicas, len(after...  4.52 us
    ppermute x1, waiting for transfers between devices, per_device(): lax.ppermute(mid, 'tensor', [(i, i ^ 1) for i in range(count)])  4.17 us
    ppermute x1, starting transfers between devices, pair_sums(): other = lax.ppermute(x, 'tensor', far)  4.12 us
  transfers between devices with their start and end apart: 15, of which 8 were waited for; matrix products, arithmetic and copies ran while one was open for 0% of the time, Pallas kernels for 22%

profile of v22, /device:TPU:0, one launch (start us, length us, event | category | flops | bytes accessed | tf_op | source)
XLA Modules:
  0.0 81.4 jit_solution(1956885621554967012)
XLA Ops:
  0.0 6.9 %attend.1 = (bf16[256,1024]{1,0:T(8,128)(2,1)}, bf16[256,1280]{1,0:T(8,128)(2,1)}, bf16[256,256]{1,0:T(8,128)(2,1)}, bf16[64,1152]{1,0:T(8,128)(2,1)}, bf16[64,1...) custom-call(s32[1,256]{1,0:T(1,128)} %bitcast.13, s32[1,256]{1,0:T(1,128)} %bitcast.14, ...), custom_call_target="tpu_custom_call" | custom-call | tf_op jit(solution)/shard_map/attend/pallas_call | solution.py:331
  6.9 4.1 %collective-permute-start.4 = (bf16[256,1280]{1,0:T(8,128)(2,1)}, bf16[256,1280]{1,0:T(8,128)(2,1)S(1)}, u32[]{:S(2)}, u32[]{:S(2)}) collective-permute-start(bf16[256,1280]{1,0:T(8,128)(2,1)} %get-tuple-element.26), channel_id=1, source_target_pairs={{0,2},{2,3},{3,1},{1,0},{4,6},{6,7},{7,5},{5,4},{8,10},{10,11},{11... | collective-permute-start | bytes 1966088 | tf_op jit(solution)/shard_map/ppermute | solution.py:579
  11.0 1.5 %collective-permute-start.1 = (bf16[64,1152]{1,0:T(8,128)(2,1)}, bf16[64,1152]{1,0:T(8,128)(2,1)S(1)}, u32[]{:S(2)}, u32[]{:S(2)}) collective-permute-start(bf16[64,1152]{1,0:T(8,128)(2,1)} %get-tuple-element.23), channel_id=1, source_target_pairs={{0,8},{4,12},{8,0},{12,4},{1,9},{5,13},{9,1},{13,5},{2,10},{6,14},... | collective-permute-start | bytes 442376 | tf_op jit(solution)/shard_map/ppermute | solution.py:573
  12.5 0.4 collective-permute-start.2
  12.8 1.0 %copy-done = bf16[256,1024]{1,0:T(8,128)(2,1)S(1)} copy-done((bf16[256,1024]{1,0:T(8,128)(2,1)S(1)}, bf16[256,1024]{1,0:T(8,128)(2,1)}, u32[]{:S(2)}) %copy-start) | copy-done | bytes 524312
  13.9 2.1 %hop.5.refs_5_.refs_0_ = bf16[256,768]{1,0:T(8,128)(2,1)S(1)} custom-call(bf16[256,1024]{1,0:T(8,128)(2,1)S(1)} %copy-done, bf16[1024,8192]{1,0:T(8,128)(2,1)} %refs_7_.1), custom_call_target="tpu_custom_call" | custom-call | tf_op jit(solution)/shard_map/hop/pallas_call | solution.py:382
  16.0 1.9 %collective-permute-done.1.refs_2_ = bf16[64,1152]{1,0:T(8,128)(2,1)S(1)} collective-permute-done((bf16[64,1152]{1,0:T(8,128)(2,1)}, bf16[64,1152]{1,0:T(8,128)(2,1)S(1)}, u32[]{:S(2)}, u32[]{:S(2)}) %collective-permute-start.1) | collective-permute-done | bytes 147488 | tf_op jit(solution)/shard_map/ppermute | solution.py:573
  17.8 2.4 %collective-permute-done.2.refs_3_ = bf16[64,1152]{1,0:T(8,128)(2,1)S(1)} collective-permute-done((bf16[64,1152]{1,0:T(8,128)(2,1)}, bf16[64,1152]{1,0:T(8,128)(2,1)S(1)}, u32[]{:S(2)}, u32[]{:S(2)}) %collective-permute-start.2) | collective-permute-done | bytes 147488 | tf_op jit(solution)/shard_map/ppermute | solution.py:573
  20.2 0.6 down.1
  21.0 1.9 %collective-permute-start.3 = (bf16[256,768]{1,0:T(8,128)(2,1)S(1)}, bf16[256,768]{1,0:T(8,128)(2,1)S(1)}, u32[]{:S(2)}, u32[]{:S(2)}) collective-permute-start(bf16[256,768]{1,0:T(8,128)(2,1)S(1)} %hold.1.refs_4_), channel_id=1, source_target_pairs={{0,2},{2,3},{3,1},{1,0},{4,6},{6,7},{7,5},{5,4},{8,10},{10,11},{11... | collective-permute-start | bytes 1179656 | tf_op jit(solution)/shard_map/ppermute | solution.py:579
  22.8 4.2 %collective-permute-done.5 = bf16[128,128]{1,0:T(8,128)(2,1)S(1)} collective-permute-done((bf16[128,128]{1,0:T(8,128)(2,1)S(1)}, bf16[128,128]{1,0:T(8,128)(2,1)S(1)}, u32[]{:S(2)}, u32[]{:S(2)}) %collective-permute-start.5) | collective-permute-done | bytes 32800 | tf_op jit(solution)/shard_map/ppermute | solution.py:612
  27.1 2.6 %hop.6.refs_3_ = bf16[256,1280]{1,0:T(8,128)(2,1)S(1)} custom-call(bf16[256,1280]{1,0:T(8,128)(2,1)S(1)} %collective-permute-done.4.refs_0_, bf16[256,1024]{1,0:T(8,128)(2,1)S(1)} %copy-done.1, bf16[1024,8192]{1,0:T(8,128)(2,1)} %refs_7_.1, bf16[128,128]{1,0:T(8,128)(2,1)S(1)} %add_convert_fusion.refs_3_.refs_0_, bf16[256,768]{1,0:T(8,128)(2,1)S(1)} %hold.1.refs_4_), custom_call_target="tpu_custom_call" | custom-call | flops 20000000000 | bytes 40000000 | tf_op jit(solution)/shard_map/hop/pallas_call | solution.py:382
  29.7 2.7 %collective-permute-start.9 = (bf16[256,1280]{1,0:T(8,128)(2,1)S(1)}, bf16[256,1280]{1,0:T(8,128)(2,1)S(1)}, u32[]{:S(2)}, u32[]{:S(2)}) collective-permute-start(bf16[256,1280]{1,0:T(8,128)(2,1)S(1)} %hop.6.refs_3_), channel_id=1, source_target_pairs={{0,2},{2,3},{3,1},{1,0},{4,6},{6,7},{7,5},{5,4},{8,10},{10,11},{11... | collective-permute-start | bytes 1966088 | tf_op jit(solution)/shard_map/ppermute | solution.py:579
  32.3 4.1 %collective-permute-start.8 = (bf16[128,128]{1,0:T(8,128)(2,1)S(1)}, bf16[128,128]{1,0:T(8,128)(2,1)S(1)}, u32[]{:S(2)}, u32[]{:S(2)}) collective-permute-start(bf16[128,128]{1,0:T(8,128)(2,1)S(1)} %add_convert_fusion.refs_3_.refs_0_), channel_id=1, source_target_pairs={{0,3},{3,0},{4,7},{7,4},{8,11},{11,8},{12,15},{15,12},{16,19},{19,... | collective-permute-start | bytes 98312 | tf_op jit(solution)/shard_map/ppermute | solution.py:592
  36.5 1.3 %collective-permute-start.7 = (bf16[128,128]{1,0:T(8,128)(2,1)S(1)}, bf16[128,128]{1,0:T(8,128)(2,1)S(1)}, u32[]{:S(2)}, u32[]{:S(2)}) collective-permute-start(bf16[128,128]{1,0:T(8,128)(2,1)S(1)} %add_convert_fusion.refs_3_.refs_0_), channel_id=1, source_target_pairs={{0,2},{3,1},{4,6},{7,5},{8,10},{11,9},{12,14},{15,13},{16,18},{19,... | collective-permute-start | bytes 98312 | tf_op jit(solution)/shard_map/ppermute | solution.py:591
  37.8 2.0 %hop.7 = bf16[256,768]{1,0:T(8,128)(2,1)S(1)} custom-call(bf16[256,768]{1,0:T(8,128)(2,1)S(1)} %collective-permute-done.3.refs_0_, bf16[256,1024]{1,0:T(8,128)(2,1)S(1)} %copy-done.1, bf16[1024,8192]{1,0:T(8,128)(2,1)} %refs_7_.1, bf16[256,1280]{1,0:T(8,128)(2,1)S(1)} %hop.6.refs_3_), custom_call_target="tpu_custom_call" | custom-call | flops 4000000000 | bytes 8000000 | tf_op jit(solution)/shard_map/hop/pallas_call | solution.py:382
  39.8 1.1 %collective-permute-start.6 = (bf16[256,768]{1,0:T(8,128)(2,1)S(1)}, bf16[256,768]{1,0:T(8,128)(2,1)S(1)}, u32[]{:S(2)}, u32[]{:S(2)}) collective-permute-start(bf16[256,768]{1,0:T(8,128)(2,1)S(1)} %hop.7), channel_id=1, source_target_pairs={{0,2},{2,3},{3,1},{1,0},{4,6},{6,7},{7,5},{5,4},{8,10},{10,11},{11... | collective-permute-start | bytes 1179656 | tf_op jit(solution)/shard_map/ppermute | solution.py:579
  40.9 8.6 %collective-permute-done.9.refs_0_ = bf16[256,1280]{1,0:T(8,128)(2,1)S(1)} collective-permute-done((bf16[256,1280]{1,0:T(8,128)(2,1)S(1)}, bf16[256,1280]{1,0:T(8,128)(2,1)S(1)}, u32[]{:S(2)}, u32[]{:S(2)}) %collective-permute-start.9) | collective-permute-done | bytes 655392 | tf_op jit(solution)/shard_map/ppermute | solution.py:579
  49.5 2.6 %hop.8.refs_5_ = bf16[256,1280]{1,0:T(8,128)(2,1)S(1)} custom-call(bf16[256,1280]{1,0:T(8,128)(2,1)S(1)} %collective-permute-done.9.refs_0_, bf16[256,1024]{1,0:T(8,128)(2,1)S(1)} %copy-done.1, bf16[1024,8192]{1,0:T(8,128)(2,1)} %refs_7_.1), custom_call_target="tpu_custom_call" | custom-call | flops 20000000000 | bytes 40000000 | tf_op jit(solution)/shard_map/hop/pallas_call | solution.py:382
  52.1 3.4 %collective-permute-start.14 = (bf16[256,1280]{1,0:T(8,128)(2,1)S(1)}, bf16[256,1280]{1,0:T(8,128)(2,1)S(1)}, u32[]{:S(2)}, u32[]{:S(2)}) collective-permute-start(bf16[256,1280]{1,0:T(8,128)(2,1)S(1)} %hop.8.refs_5_), channel_id=1, source_target_pairs={{0,2},{2,3},{3,1},{1,0},{4,6},{6,7},{7,5},{5,4},{8,10},{10,11},{11... | collective-permute-start | bytes 1966088 | tf_op jit(solution)/shard_map/ppermute | solution.py:579
  55.5 0.8 %up.1 = (bf16[64,2048]{1,0:T(8,128)(2,1)S(1)}, bf16[64,2048]{1,0:T(8,128)(2,1)S(1)}, bf16[64,2048]{1,0:T(8,128)(2,1)S(1)}, bf16[64,2048]{1,0:T(8,128)(2,1)S(1)}) custom-call(bf16[128,128]{1,0:T(8,128)(2,1)S(1)} %add_convert_fusion.refs_3_.refs_0_, bf16[128,128]{1,0:T(8,128)(2,1)S(1)} %collective-permute-done.7.refs_1_, ...), custom_call_target="tpu_custom_call" | custom-call | tf_op jit(solution)/shard_map/up/pallas_call | solution.py:458
  56.4 1.6 %collective-permute-start.12 = (bf16[64,2048]{1,0:T(8,128)(2,1)S(1)}, bf16[64,2048]{1,0:T(8,128)(2,1)S(1)}, u32[]{:S(2)}, u32[]{:S(2)}) collective-permute-start(bf16[64,2048]{1,0:T(8,128)(2,1)S(1)} %get-tuple-element.30), channel_id=1, source_target_pairs={{0,8},{4,12},{8,0},{12,4},{1,9},{5,13},{9,1},{13,5},{2,10},{6,14},... | collective-permute-start | bytes 786440 | tf_op jit(solution)/shard_map/ppermute | solution.py:573
  58.3 1.0 %collective-permute-done.6.refs_0_ = bf16[256,768]{1,0:T(8,128)(2,1)S(1)} collective-permute-done((bf16[256,768]{1,0:T(8,128)(2,1)S(1)}, bf16[256,768]{1,0:T(8,128)(2,1)S(1)}, u32[]{:S(2)}, u32[]{:S(2)}) %collective-permute-start.6) | collective-permute-done | bytes 393248 | tf_op jit(solution)/shard_map/ppermute | solution.py:579
  59.3 2.1 %hop.9.refs_8_ = bf16[256,768]{1,0:T(8,128)(2,1)S(1)} custom-call(bf16[256,768]{1,0:T(8,128)(2,1)S(1)} %collective-permute-done.6.refs_0_, bf16[256,1024]{1,0:T(8,128)(2,1)S(1)} %copy-done.1, bf16[1024,8192]{1,0:T(8,128)(2,1)} %refs_7_.1, bf16[64,2048]{1,0:T(8,128)(2,1)S(1)} %get-tuple-element.28.refs_3_.refs_0_), custom_call_target="tpu_custom_call" | custom-call | tf_op jit(solution)/shard_map/hop/pallas_call | solution.py:382
  61.4 3.4 %collective-permute-start.10 = (bf16[256,768]{1,0:T(8,128)(2,1)S(1)}, bf16[256,768]{1,0:T(8,128)(2,1)S(1)}, u32[]{:S(2)}, u32[]{:S(2)}) collective-permute-start(bf16[256,768]{1,0:T(8,128)(2,1)S(1)} %hop.9.refs_8_), channel_id=1, source_target_pairs={{0,2},{2,3},{3,1},{1,0},{4,6},{6,7},{7,5},{5,4},{8,10},{10,11},{11... | collective-permute-start | bytes 1179656 | tf_op jit(solution)/shard_map/ppermute | solution.py:579
  64.8 0.8 collective-permute-done.12.refs_2_
  65.6 4.7 %collective-permute-done.13.refs_3_ = bf16[64,2048]{1,0:T(8,128)(2,1)S(1)} collective-permute-done((bf16[64,2048]{1,0:T(8,128)(2,1)S(1)}, bf16[64,2048]{1,0:T(8,128)(2,1)S(1)}, u32[]{:S(2)}, u32[]{:S(2)}) %collective-permute-start.13) | collective-permute-done | bytes 262176 | tf_op jit(solution)/shard_map/ppermute | solution.py:573
  70.3 4.5 %settle.1 = (f32[256,1280]{1,0:T(8,128)}, f32[256,768]{1,0:T(8,128)S(1)}) custom-call(bf16[64,2048]{1,0:T(8,128)(2,1)S(1)} %get-tuple-element.28.refs_3_.refs_0_, bf16[64,2048]{1,0:T(8,128)(2,1)S(1)} %collective-permute-done.11.refs_1_, bf16[64,2048]{1,0:T(8,128)(2,1)S(1)} %collective-permute-done.12.refs_2_, ...), custom_call_target="tpu_custom_call" | custom-call | flops 4000000000 | bytes 8000000 | tf_op jit(solution)/shard_map/settle/pallas_call | solution.py:488
  74.9 1.3 %copy-done.3 = f32[256,1280]{1,0:T(8,128)S(1)} copy-done((f32[256,1280]{1,0:T(8,128)S(1)}, f32[256,1280]{1,0:T(8,128)}, u32[]{:S(2)}) %copy-start.3) | copy-done | bytes 1310744
  76.2 0.9 %finish.2.refs_0_ = bf16[256,2048]{1,0:T(8,128)(2,1)} custom-call(bf16[256,1280]{1,0:T(8,128)(2,1)S(1)} %collective-permute-done.14.arrived_ref, f32[256,1280]{1,0:T(8,128)S(1)} %copy-done.3), custom_call_target="tpu_custom_call" | custom-call | tf_op jit(solution)/shard_map/finish/pallas_call | solution.py:520
  77.1 3.6 %collective-permute-done.10.arrived_ref = bf16[256,768]{1,0:T(8,128)(2,1)S(1)} collective-permute-done((bf16[256,768]{1,0:T(8,128)(2,1)S(1)}, bf16[256,768]{1,0:T(8,128)(2,1)S(1)}, u32[]{:S(2)}, u32[]{:S(2)}) %collective-permute-start.10) | collective-permute-done | bytes 393248 | tf_op jit(solution)/shard_map/ppermute | solution.py:579
  80.6 0.8 finish.3
  (27 shorter events, 0.5 us)
Async XLA Ops:
  6.9 20.2 %collective-permute-start.4 = (bf16[256,1280]{1,0:T(8,128)(2,1)}, bf16[256,1280]{1,0:T(8,128)(2,1)S(1)}, u32[]{:S(2)}, u32[]{:S(2)}) collective-permute-start(bf16[256,1280]{1,0:T(8,128)(2,1)} %get-tuple-element.26), channel_id=1, source_target_pairs={{0,2},{2,3},{3,1},{1,0},{4,6},{6,7},{7,5},{5,4},{8,10},{10,11},{11... | collective-permute-start | bytes 1966088 | tf_op jit(solution)/shard_map/ppermute | solution.py:579
  11.0 5.0 %collective-permute-start = (bf16[64,1152]{1,0:T(8,128)(2,1)}, bf16[64,1152]{1,0:T(8,128)(2,1)S(1)}, u32[]{:S(2)}, u32[]{:S(2)}) collective-permute-start(bf16[64,1152]{1,0:T(8,128)(2,1)} %get-tuple-element.22), channel_id=1, source_target_pairs={{0,4},{4,0},{8,12},{12,8},{1,5},{5,1},{9,13},{13,9},{2,6},{6,2},{1... | collective-permute-start | bytes 442376 | tf_op jit(solution)/shard_map/ppermute | solution.py:573
  11.0 6.9 %collective-permute-start.1 = (bf16[64,1152]{1,0:T(8,128)(2,1)}, bf16[64,1152]{1,0:T(8,128)(2,1)S(1)}, u32[]{:S(2)}, u32[]{:S(2)}) collective-permute-start(bf16[64,1152]{1,0:T(8,128)(2,1)} %get-tuple-element.23), channel_id=1, source_target_pairs={{0,8},{4,12},{8,0},{12,4},{1,9},{5,13},{9,1},{13,5},{2,10},{6,14},... | collective-permute-start | bytes 442376 | tf_op jit(solution)/shard_map/ppermute | solution.py:573
  12.5 7.7 %collective-permute-start.2 = (bf16[64,1152]{1,0:T(8,128)(2,1)}, bf16[64,1152]{1,0:T(8,128)(2,1)S(1)}, u32[]{:S(2)}, u32[]{:S(2)}) collective-permute-start(bf16[64,1152]{1,0:T(8,128)(2,1)} %get-tuple-element.24), channel_id=1, source_target_pairs={{0,12},{4,8},{8,4},{12,0},{1,13},{5,9},{9,5},{13,1},{2,14},{6,10},... | collective-permute-start | bytes 442376 | tf_op jit(solution)/shard_map/ppermute | solution.py:573
  12.8 1.0 %copy-start = (bf16[256,1024]{1,0:T(8,128)(2,1)S(1)}, bf16[256,1024]{1,0:T(8,128)(2,1)}, u32[]{:S(2)}) copy-start(bf16[256,1024]{1,0:T(8,128)(2,1)} %get-tuple-element.20.refs_0_.refs_1_.refs_5_) | copy-start | bytes 1572868
  13.9 6.3 %copy-start.5 = (bf16[8,64,1024]{2,1,0:T(8,128)(2,1)S(1)}, bf16[8,64,1024]{2,1,0:T(8,128)(2,1)}, u32[]{:S(2)}) copy-start(bf16[8,64,1024]{2,1,0:T(8,128)(2,1)} %refs_4_.2) | copy-start | bytes 3145732
  13.9 6.3 %copy-start.6 = (bf16[64,1152]{1,0:T(8,128)(2,1)S(1)}, bf16[64,1152]{1,0:T(8,128)(2,1)}, u32[]{:S(2)}) copy-start(bf16[64,1152]{1,0:T(8,128)(2,1)} %get-tuple-element.21.refs_0_) | copy-start | bytes 442372
  15.9 11.1 %copy-start.1 = (bf16[256,1024]{1,0:T(8,128)(2,1)S(1)}, bf16[256,1024]{1,0:T(8,128)(2,1)}, u32[]{:S(2)}) copy-start(bf16[256,1024]{1,0:T(8,128)(2,1)} %get-tuple-element.20.refs_0_.refs_1_.refs_5_) | copy-start | bytes 1572868
  20.9 6.1 %collective-permute-start.5 = (bf16[128,128]{1,0:T(8,128)(2,1)S(1)}, bf16[128,128]{1,0:T(8,128)(2,1)S(1)}, u32[]{:S(2)}, u32[]{:S(2)}) collective-permute-start(bf16[128,128]{1,0:T(8,128)(2,1)S(1)} %get-tuple-element.25.refs_1_), channel_id=1, source_target_pairs={{0,1},{1,0},{2,3},{3,2},{4,5},{5,4},{6,7},{7,6},{8,9},{9,8},{10,11... | collective-permute-start | bytes 98312 | tf_op jit(solution)/shard_map/ppermute | solution.py:612
  21.0 16.8 %collective-permute-start.3 = (bf16[256,768]{1,0:T(8,128)(2,1)S(1)}, bf16[256,768]{1,0:T(8,128)(2,1)S(1)}, u32[]{:S(2)}, u32[]{:S(2)}) collective-permute-start(bf16[256,768]{1,0:T(8,128)(2,1)S(1)} %hold.1.refs_4_), channel_id=1, source_target_pairs={{0,2},{2,3},{3,1},{1,0},{4,6},{6,7},{7,5},{5,4},{8,10},{10,11},{11... | collective-permute-start | bytes 1179656 | tf_op jit(solution)/shard_map/ppermute | solution.py:579
  29.7 19.8 %collective-permute-start.9 = (bf16[256,1280]{1,0:T(8,128)(2,1)S(1)}, bf16[256,1280]{1,0:T(8,128)(2,1)S(1)}, u32[]{:S(2)}, u32[]{:S(2)}) collective-permute-start(bf16[256,1280]{1,0:T(8,128)(2,1)S(1)} %hop.6.refs_3_), channel_id=1, source_target_pairs={{0,2},{2,3},{3,1},{1,0},{4,6},{6,7},{7,5},{5,4},{8,10},{10,11},{11... | collective-permute-start | bytes 1966088 | tf_op jit(solution)/shard_map/ppermute | solution.py:579
  32.3 23.2 %collective-permute-start.8 = (bf16[128,128]{1,0:T(8,128)(2,1)S(1)}, bf16[128,128]{1,0:T(8,128)(2,1)S(1)}, u32[]{:S(2)}, u32[]{:S(2)}) collective-permute-start(bf16[128,128]{1,0:T(8,128)(2,1)S(1)} %add_convert_fusion.refs_3_.refs_0_), channel_id=1, source_target_pairs={{0,3},{3,0},{4,7},{7,4},{8,11},{11,8},{12,15},{15,12},{16,19},{19,... | collective-permute-start | bytes 98312 | tf_op jit(solution)/shard_map/ppermute | solution.py:592
  36.5 19.1 %collective-permute-start.7 = (bf16[128,128]{1,0:T(8,128)(2,1)S(1)}, bf16[128,128]{1,0:T(8,128)(2,1)S(1)}, u32[]{:S(2)}, u32[]{:S(2)}) collective-permute-start(bf16[128,128]{1,0:T(8,128)(2,1)S(1)} %add_convert_fusion.refs_3_.refs_0_), channel_id=1, source_target_pairs={{0,2},{3,1},{4,6},{7,5},{8,10},{11,9},{12,14},{15,13},{16,18},{19,... | collective-permute-start | bytes 98312 | tf_op jit(solution)/shard_map/ppermute | solution.py:591
  39.8 15.7 %copy-start.2 = (bf16[8,64,2048]{2,1,0:T(8,128)(2,1)S(1)}, bf16[8,64,2048]{2,1,0:T(8,128)(2,1)}, u32[]{:S(2)}) copy-start(bf16[8,64,2048]{2,1,0:T(8,128)(2,1)} %refs_4_.3) | copy-start | bytes 6291460
  39.8 19.5 %collective-permute-start.6 = (bf16[256,768]{1,0:T(8,128)(2,1)S(1)}, bf16[256,768]{1,0:T(8,128)(2,1)S(1)}, u32[]{:S(2)}, u32[]{:S(2)}) collective-permute-start(bf16[256,768]{1,0:T(8,128)(2,1)S(1)} %hop.7), channel_id=1, source_target_pairs={{0,2},{2,3},{3,1},{1,0},{4,6},{6,7},{7,5},{5,4},{8,10},{10,11},{11... | collective-permute-start | bytes 1179656 | tf_op jit(solution)/shard_map/ppermute | solution.py:579
  52.1 22.8 %collective-permute-start.14 = (bf16[256,1280]{1,0:T(8,128)(2,1)S(1)}, bf16[256,1280]{1,0:T(8,128)(2,1)S(1)}, u32[]{:S(2)}, u32[]{:S(2)}) collective-permute-start(bf16[256,1280]{1,0:T(8,128)(2,1)S(1)} %hop.8.refs_5_), channel_id=1, source_target_pairs={{0,2},{2,3},{3,1},{1,0},{4,6},{6,7},{7,5},{5,4},{8,10},{10,11},{11... | collective-permute-start | bytes 1966088 | tf_op jit(solution)/shard_map/ppermute | solution.py:579
  56.3 8.5 %collective-permute-start.11 = (bf16[64,2048]{1,0:T(8,128)(2,1)S(1)}, bf16[64,2048]{1,0:T(8,128)(2,1)S(1)}, u32[]{:S(2)}, u32[]{:S(2)}) collective-permute-start(bf16[64,2048]{1,0:T(8,128)(2,1)S(1)} %get-tuple-element.29), channel_id=1, source_target_pairs={{0,4},{4,0},{8,12},{12,8},{1,5},{5,1},{9,13},{13,9},{2,6},{6,2},{1... | collective-permute-start | bytes 786440 | tf_op jit(solution)/shard_map/ppermute | solution.py:573
  56.4 9.2 %collective-permute-start.12 = (bf16[64,2048]{1,0:T(8,128)(2,1)S(1)}, bf16[64,2048]{1,0:T(8,128)(2,1)S(1)}, u32[]{:S(2)}, u32[]{:S(2)}) collective-permute-start(bf16[64,2048]{1,0:T(8,128)(2,1)S(1)} %get-tuple-element.30), channel_id=1, source_target_pairs={{0,8},{4,12},{8,0},{12,4},{1,9},{5,13},{9,1},{13,5},{2,10},{6,14},... | collective-permute-start | bytes 786440 | tf_op jit(solution)/shard_map/ppermute | solution.py:573
  58.0 12.3 %collective-permute-start.13 = (bf16[64,2048]{1,0:T(8,128)(2,1)S(1)}, bf16[64,2048]{1,0:T(8,128)(2,1)S(1)}, u32[]{:S(2)}, u32[]{:S(2)}) collective-permute-start(bf16[64,2048]{1,0:T(8,128)(2,1)S(1)} %get-tuple-element.31), channel_id=1, source_target_pairs={{0,12},{4,8},{8,4},{12,0},{1,13},{5,9},{9,5},{13,1},{2,14},{6,10},... | collective-permute-start | bytes 786440 | tf_op jit(solution)/shard_map/ppermute | solution.py:573
  59.3 11.0 %copy-start.4 = (bf16[256,2048]{1,0:T(8,128)(2,1)S(1)}, bf16[256,2048]{1,0:T(8,128)(2,1)}, u32[]{:S(2)}) copy-start(bf16[256,2048]{1,0:T(8,128)(2,1)} %refs_6_.1) | copy-start | bytes 3145732
  59.3 11.0 %copy-start.7 = (bf16[256,256]{1,0:T(8,128)(2,1)S(1)}, bf16[256,256]{1,0:T(8,128)(2,1)}, u32[]{:S(2)}) copy-start(bf16[256,256]{1,0:T(8,128)(2,1)} %get-tuple-element.32.refs_4_) | copy-start | bytes 393220
  61.4 19.2 %collective-permute-start.10 = (bf16[256,768]{1,0:T(8,128)(2,1)S(1)}, bf16[256,768]{1,0:T(8,128)(2,1)S(1)}, u32[]{:S(2)}, u32[]{:S(2)}) collective-permute-start(bf16[256,768]{1,0:T(8,128)(2,1)S(1)} %hop.9.refs_8_), channel_id=1, source_target_pairs={{0,2},{2,3},{3,1},{1,0},{4,6},{6,7},{7,5},{5,4},{8,10},{10,11},{11... | collective-permute-start | bytes 1179656 | tf_op jit(solution)/shard_map/ppermute | solution.py:579
  74.8 1.3 %copy-start.3 = (f32[256,1280]{1,0:T(8,128)S(1)}, f32[256,1280]{1,0:T(8,128)}, u32[]{:S(2)}) copy-start(f32[256,1280]{1,0:T(8,128)} %get-tuple-element.34.settled_ref) | copy-start | bytes 3932164

commit v23 on v19

--- a/solution.py
+++ b/solution.py
@@ -159,7 +159,7 @@
         rows = pl.ds(first, count)
         for columns, product in weights.products(a_ref[rows, :]):
             out_ref[rows, columns] = product.astype(jnp.bfloat16)
-        leave(out_ref.at[rows, :], out_hbm.at[rows, :])
+            leave(out_ref.at[rows, columns], out_hbm.at[rows, columns])
 
     chunk = out_ref.shape[1]
     weights = Weights(w_hbm, w_held, w_sems, column_owner(0) * block, chunk)
@@ -340,7 +340,7 @@
             pltpu.VMEM((requests, chunk), jnp.bfloat16),
             pltpu.VMEM((replicas * CAP, requests), jnp.bfloat16),
             pltpu.VMEM((replicas * CAP, features + LANES), jnp.bfloat16),
-            pltpu.SemaphoreType.DMA((1 + steps + 2 + replicas,)),
+            pltpu.SemaphoreType.DMA((1 + steps + 2 * pl.cdiv(chunk, PIECE) + replicas,)),
         ]
         + [pltpu.VMEM(x.shape, x.dtype) for x in small + operands]
         + [

time: 81.5 us -> 81.5 us (level)
  no operation moved by 1% of the time
where the time goes in v23:
time: 81.5 us; the launch traced here: 81.1 us
  waiting for transfers between devices  27.1 us (33%)
  starting transfers between devices  25.9 us (32%)
  Pallas kernels  25.5 us (31%)
  local copies, waits for them, and re-layouts  2.38 us (3%)
    ppermute x6, starting transfers between devices, forward(): return lax.ppermute(x, 'tensor', ring)  16.6 us
    ppermute x6, waiting for transfers between devices, forward(): return lax.ppermute(x, 'tensor', ring)  13.2 us
    pallas_call x5, Pallas kernels, hop(): pl.pallas_call(functools.partial(hop_kernel, step, block, start, arriving...  11.3 us
    ppermute x6, waiting for transfers between devices, exchange(): lax.ppermute(blocks[r], 'dp', [(i, i ^ r) for i in range(replicas)])  9.72 us
    pallas_call x1, Pallas kernels, attend(): pl.pallas_call(functools.partial(attend_kernel, heads, kv, cache, steps,...  6.5 us
    pallas_call x1, Pallas kernels, settle(): pl.pallas_call(functools.partial(settle_kernel, step, replicas, len(after...  4.52 us
    ppermute x1, waiting for transfers between devices, per_device(): lax.ppermute(mid, 'tensor', [(i, i ^ 1) for i in range(count)])  4.17 us
    ppermute x1, starting transfers between devices, pair_sums(): other = lax.ppermute(x, 'tensor', far)  4.12 us
  transfers between devices with their start and end apart: 15, of which 8 were waited for; matrix products, arithmetic and copies ran while one was open for 0% of the time, Pallas kernels for 22%

profile of v23, /device:TPU:0, one launch (start us, length us, event | category | flops | bytes accessed | tf_op | source)
XLA Modules:
  0.0 81.1 jit_solution(5941463354466171788)
XLA Ops:
  0.0 6.5 %attend.1 = (bf16[256,1024]{1,0:T(8,128)(2,1)}, bf16[256,1280]{1,0:T(8,128)(2,1)}, bf16[256,256]{1,0:T(8,128)(2,1)}, bf16[64,1152]{1,0:T(8,128)(2,1)}, bf16[64,1...) custom-call(s32[1,256]{1,0:T(1,128)} %bitcast.13, s32[1,256]{1,0:T(1,128)} %bitcast.14, ...), custom_call_target="tpu_custom_call" | custom-call | tf_op jit(solution)/shard_map/attend/pallas_call | solution.py:328
  6.5 4.1 %collective-permute-start.4 = (bf16[256,1280]{1,0:T(8,128)(2,1)}, bf16[256,1280]{1,0:T(8,128)(2,1)S(1)}, u32[]{:S(2)}, u32[]{:S(2)}) collective-permute-start(bf16[256,1280]{1,0:T(8,128)(2,1)} %get-tuple-element.26), channel_id=1, source_target_pairs={{0,2},{2,3},{3,1},{1,0},{4,6},{6,7},{7,5},{5,4},{8,10},{10,11},{11... | collective-permute-start | bytes 1966088 | tf_op jit(solution)/shard_map/ppermute | solution.py:576
  10.6 1.5 %collective-permute-start.1 = (bf16[64,1152]{1,0:T(8,128)(2,1)}, bf16[64,1152]{1,0:T(8,128)(2,1)S(1)}, u32[]{:S(2)}, u32[]{:S(2)}) collective-permute-start(bf16[64,1152]{1,0:T(8,128)(2,1)} %get-tuple-element.23), channel_id=1, source_target_pairs={{0,8},{4,12},{8,0},{12,4},{1,9},{5,13},{9,1},{13,5},{2,10},{6,14},... | collective-permute-start | bytes 442376 | tf_op jit(solution)/shard_map/ppermute | solution.py:570
  12.1 0.4 collective-permute-start.2
  12.5 1.0 %copy-done = bf16[256,1024]{1,0:T(8,128)(2,1)S(1)} copy-done((bf16[256,1024]{1,0:T(8,128)(2,1)S(1)}, bf16[256,1024]{1,0:T(8,128)(2,1)}, u32[]{:S(2)}) %copy-start) | copy-done | bytes 524312
  13.5 2.1 %hop.5.refs_5_.refs_0_ = bf16[256,768]{1,0:T(8,128)(2,1)S(1)} custom-call(bf16[256,1024]{1,0:T(8,128)(2,1)S(1)} %copy-done, bf16[1024,8192]{1,0:T(8,128)(2,1)} %refs_7_.1), custom_call_target="tpu_custom_call" | custom-call | tf_op jit(solution)/shard_map/hop/pallas_call | solution.py:379
  15.6 1.9 %collective-permute-done.1.refs_2_ = bf16[64,1152]{1,0:T(8,128)(2,1)S(1)} collective-permute-done((bf16[64,1152]{1,0:T(8,128)(2,1)}, bf16[64,1152]{1,0:T(8,128)(2,1)S(1)}, u32[]{:S(2)}, u32[]{:S(2)}) %collective-permute-start.1) | collective-permute-done | bytes 147488 | tf_op jit(solution)/shard_map/ppermute | solution.py:570
  17.5 2.4 %collective-permute-done.2.refs_3_ = bf16[64,1152]{1,0:T(8,128)(2,1)S(1)} collective-permute-done((bf16[64,1152]{1,0:T(8,128)(2,1)}, bf16[64,1152]{1,0:T(8,128)(2,1)S(1)}, u32[]{:S(2)}, u32[]{:S(2)}) %collective-permute-start.2) | collective-permute-done | bytes 147488 | tf_op jit(solution)/shard_map/ppermute | solution.py:570
  19.8 0.6 down.1
  20.6 1.9 %collective-permute-start.3 = (bf16[256,768]{1,0:T(8,128)(2,1)S(1)}, bf16[256,768]{1,0:T(8,128)(2,1)S(1)}, u32[]{:S(2)}, u32[]{:S(2)}) collective-permute-start(bf16[256,768]{1,0:T(8,128)(2,1)S(1)} %hold.1.refs_4_), channel_id=1, source_target_pairs={{0,2},{2,3},{3,1},{1,0},{4,6},{6,7},{7,5},{5,4},{8,10},{10,11},{11... | collective-permute-start | bytes 1179656 | tf_op jit(solution)/shard_map/ppermute | solution.py:576
  22.5 4.2 %collective-permute-done.5 = bf16[128,128]{1,0:T(8,128)(2,1)S(1)} collective-permute-done((bf16[128,128]{1,0:T(8,128)(2,1)S(1)}, bf16[128,128]{1,0:T(8,128)(2,1)S(1)}, u32[]{:S(2)}, u32[]{:S(2)}) %collective-permute-start.5) | collective-permute-done | bytes 32800 | tf_op jit(solution)/shard_map/ppermute | solution.py:609
  26.7 2.6 %hop.6.refs_3_ = bf16[256,1280]{1,0:T(8,128)(2,1)S(1)} custom-call(bf16[256,1280]{1,0:T(8,128)(2,1)S(1)} %collective-permute-done.4.refs_0_, bf16[256,1024]{1,0:T(8,128)(2,1)S(1)} %copy-done.1, bf16[1024,8192]{1,0:T(8,128)(2,1)} %refs_7_.1, bf16[128,128]{1,0:T(8,128)(2,1)S(1)} %add_convert_fusion.refs_3_.refs_0_, bf16[256,768]{1,0:T(8,128)(2,1)S(1)} %hold.1.refs_4_), custom_call_target="tpu_custom_call" | custom-call | flops 20000000000 | bytes 40000000 | tf_op jit(solution)/shard_map/hop/pallas_call | solution.py:379
  29.3 2.7 %collective-permute-start.9 = (bf16[256,1280]{1,0:T(8,128)(2,1)S(1)}, bf16[256,1280]{1,0:T(8,128)(2,1)S(1)}, u32[]{:S(2)}, u32[]{:S(2)}) collective-permute-start(bf16[256,1280]{1,0:T(8,128)(2,1)S(1)} %hop.6.refs_3_), channel_id=1, source_target_pairs={{0,2},{2,3},{3,1},{1,0},{4,6},{6,7},{7,5},{5,4},{8,10},{10,11},{11... | collective-permute-start | bytes 1966088 | tf_op jit(solution)/shard_map/ppermute | solution.py:576
  32.0 4.1 %collective-permute-start.8 = (bf16[128,128]{1,0:T(8,128)(2,1)S(1)}, bf16[128,128]{1,0:T(8,128)(2,1)S(1)}, u32[]{:S(2)}, u32[]{:S(2)}) collective-permute-start(bf16[128,128]{1,0:T(8,128)(2,1)S(1)} %add_convert_fusion.refs_3_.refs_0_), channel_id=1, source_target_pairs={{0,3},{3,0},{4,7},{7,4},{8,11},{11,8},{12,15},{15,12},{16,19},{19,... | collective-permute-start | bytes 98312 | tf_op jit(solution)/shard_map/ppermute | solution.py:589
  36.1 1.3 %collective-permute-start.7 = (bf16[128,128]{1,0:T(8,128)(2,1)S(1)}, bf16[128,128]{1,0:T(8,128)(2,1)S(1)}, u32[]{:S(2)}, u32[]{:S(2)}) collective-permute-start(bf16[128,128]{1,0:T(8,128)(2,1)S(1)} %add_convert_fusion.refs_3_.refs_0_), channel_id=1, source_target_pairs={{0,2},{3,1},{4,6},{7,5},{8,10},{11,9},{12,14},{15,13},{16,18},{19,... | collective-permute-start | bytes 98312 | tf_op jit(solution)/shard_map/ppermute | solution.py:588
  37.4 2.0 %hop.7 = bf16[256,768]{1,0:T(8,128)(2,1)S(1)} custom-call(bf16[256,768]{1,0:T(8,128)(2,1)S(1)} %collective-permute-done.3.refs_0_, bf16[256,1024]{1,0:T(8,128)(2,1)S(1)} %copy-done.1, bf16[1024,8192]{1,0:T(8,128)(2,1)} %refs_7_.1, bf16[256,1280]{1,0:T(8,128)(2,1)S(1)} %hop.6.refs_3_), custom_call_target="tpu_custom_call" | custom-call | flops 4000000000 | bytes 8000000 | tf_op jit(solution)/shard_map/hop/pallas_call | solution.py:379
  39.4 1.1 %collective-permute-start.6 = (bf16[256,768]{1,0:T(8,128)(2,1)S(1)}, bf16[256,768]{1,0:T(8,128)(2,1)S(1)}, u32[]{:S(2)}, u32[]{:S(2)}) collective-permute-start(bf16[256,768]{1,0:T(8,128)(2,1)S(1)} %hop.7), channel_id=1, source_target_pairs={{0,2},{2,3},{3,1},{1,0},{4,6},{6,7},{7,5},{5,4},{8,10},{10,11},{11... | collective-permute-start | bytes 1179656 | tf_op jit(solution)/shard_map/ppermute | solution.py:576
  40.5 8.6 %collective-permute-done.9.refs_0_ = bf16[256,1280]{1,0:T(8,128)(2,1)S(1)} collective-permute-done((bf16[256,1280]{1,0:T(8,128)(2,1)S(1)}, bf16[256,1280]{1,0:T(8,128)(2,1)S(1)}, u32[]{:S(2)}, u32[]{:S(2)}) %collective-permute-start.9) | collective-permute-done | bytes 655392 | tf_op jit(solution)/shard_map/ppermute | solution.py:576
  49.1 2.6 %hop.8.refs_5_ = bf16[256,1280]{1,0:T(8,128)(2,1)S(1)} custom-call(bf16[256,1280]{1,0:T(8,128)(2,1)S(1)} %collective-permute-done.9.refs_0_, bf16[256,1024]{1,0:T(8,128)(2,1)S(1)} %copy-done.1, bf16[1024,8192]{1,0:T(8,128)(2,1)} %refs_7_.1), custom_call_target="tpu_custom_call" | custom-call | flops 20000000000 | bytes 40000000 | tf_op jit(solution)/shard_map/hop/pallas_call | solution.py:379
  51.7 3.4 %collective-permute-start.14 = (bf16[256,1280]{1,0:T(8,128)(2,1)S(1)}, bf16[256,1280]{1,0:T(8,128)(2,1)S(1)}, u32[]{:S(2)}, u32[]{:S(2)}) collective-permute-start(bf16[256,1280]{1,0:T(8,128)(2,1)S(1)} %hop.8.refs_5_), channel_id=1, source_target_pairs={{0,2},{2,3},{3,1},{1,0},{4,6},{6,7},{7,5},{5,4},{8,10},{10,11},{11... | collective-permute-start | bytes 1966088 | tf_op jit(solution)/shard_map/ppermute | solution.py:576
  55.1 0.8 %up.1 = (bf16[64,2048]{1,0:T(8,128)(2,1)S(1)}, bf16[64,2048]{1,0:T(8,128)(2,1)S(1)}, bf16[64,2048]{1,0:T(8,128)(2,1)S(1)}, bf16[64,2048]{1,0:T(8,128)(2,1)S(1)}) custom-call(bf16[128,128]{1,0:T(8,128)(2,1)S(1)} %add_convert_fusion.refs_3_.refs_0_, bf16[128,128]{1,0:T(8,128)(2,1)S(1)} %collective-permute-done.7.refs_1_, ...), custom_call_target="tpu_custom_call" | custom-call | tf_op jit(solution)/shard_map/up/pallas_call | solution.py:455
  56.0 1.6 %collective-permute-start.12 = (bf16[64,2048]{1,0:T(8,128)(2,1)S(1)}, bf16[64,2048]{1,0:T(8,128)(2,1)S(1)}, u32[]{:S(2)}, u32[]{:S(2)}) collective-permute-start(bf16[64,2048]{1,0:T(8,128)(2,1)S(1)} %get-tuple-element.30), channel_id=1, source_target_pairs={{0,8},{4,12},{8,0},{12,4},{1,9},{5,13},{9,1},{13,5},{2,10},{6,14},... | collective-permute-start | bytes 786440 | tf_op jit(solution)/shard_map/ppermute | solution.py:570
  57.9 1.0 %collective-permute-done.6.refs_0_ = bf16[256,768]{1,0:T(8,128)(2,1)S(1)} collective-permute-done((bf16[256,768]{1,0:T(8,128)(2,1)S(1)}, bf16[256,768]{1,0:T(8,128)(2,1)S(1)}, u32[]{:S(2)}, u32[]{:S(2)}) %collective-permute-start.6) | collective-permute-done | bytes 393248 | tf_op jit(solution)/shard_map/ppermute | solution.py:576
  59.0 2.1 %hop.9.refs_8_ = bf16[256,768]{1,0:T(8,128)(2,1)S(1)} custom-call(bf16[256,768]{1,0:T(8,128)(2,1)S(1)} %collective-permute-done.6.refs_0_, bf16[256,1024]{1,0:T(8,128)(2,1)S(1)} %copy-done.1, bf16[1024,8192]{1,0:T(8,128)(2,1)} %refs_7_.1, bf16[64,2048]{1,0:T(8,128)(2,1)S(1)} %get-tuple-element.28.refs_3_.refs_0_), custom_call_target="tpu_custom_call" | custom-call | tf_op jit(solution)/shard_map/hop/pallas_call | solution.py:379
  61.0 3.4 %collective-permute-start.10 = (bf16[256,768]{1,0:T(8,128)(2,1)S(1)}, bf16[256,768]{1,0:T(8,128)(2,1)S(1)}, u32[]{:S(2)}, u32[]{:S(2)}) collective-permute-start(bf16[256,768]{1,0:T(8,128)(2,1)S(1)} %hop.9.refs_8_), channel_id=1, source_target_pairs={{0,2},{2,3},{3,1},{1,0},{4,6},{6,7},{7,5},{5,4},{8,10},{10,11},{11... | collective-permute-start | bytes 1179656 | tf_op jit(solution)/shard_map/ppermute | solution.py:576
  64.5 0.8 collective-permute-done.12.refs_2_
  65.2 4.7 %collective-permute-done.13.refs_3_ = bf16[64,2048]{1,0:T(8,128)(2,1)S(1)} collective-permute-done((bf16[64,2048]{1,0:T(8,128)(2,1)S(1)}, bf16[64,2048]{1,0:T(8,128)(2,1)S(1)}, u32[]{:S(2)}, u32[]{:S(2)}) %collective-permute-start.13) | collective-permute-done | bytes 262176 | tf_op jit(solution)/shard_map/ppermute | solution.py:570
  69.9 4.5 %settle.1 = (f32[256,1280]{1,0:T(8,128)}, f32[256,768]{1,0:T(8,128)S(1)}) custom-call(bf16[64,2048]{1,0:T(8,128)(2,1)S(1)} %get-tuple-element.28.refs_3_.refs_0_, bf16[64,2048]{1,0:T(8,128)(2,1)S(1)} %collective-permute-done.11.refs_1_, bf16[64,2048]{1,0:T(8,128)(2,1)S(1)} %collective-permute-done.12.refs_2_, ...), custom_call_target="tpu_custom_call" | custom-call | flops 4000000000 | bytes 8000000 | tf_op jit(solution)/shard_map/settle/pallas_call | solution.py:485
  74.5 1.3 %copy-done.3 = f32[256,1280]{1,0:T(8,128)S(1)} copy-done((f32[256,1280]{1,0:T(8,128)S(1)}, f32[256,1280]{1,0:T(8,128)}, u32[]{:S(2)}) %copy-start.3) | copy-done | bytes 1310744
  75.8 0.9 %finish.2.refs_0_ = bf16[256,2048]{1,0:T(8,128)(2,1)} custom-call(bf16[256,1280]{1,0:T(8,128)(2,1)S(1)} %collective-permute-done.14.arrived_ref, f32[256,1280]{1,0:T(8,128)S(1)} %copy-done.3), custom_call_target="tpu_custom_call" | custom-call | tf_op jit(solution)/shard_map/finish/pallas_call | solution.py:517
  76.7 3.6 %collective-permute-done.10.arrived_ref = bf16[256,768]{1,0:T(8,128)(2,1)S(1)} collective-permute-done((bf16[256,768]{1,0:T(8,128)(2,1)S(1)}, bf16[256,768]{1,0:T(8,128)(2,1)S(1)}, u32[]{:S(2)}, u32[]{:S(2)}) %collective-permute-start.10) | collective-permute-done | bytes 393248 | tf_op jit(solution)/shard_map/ppermute | solution.py:576
  80.3 0.8 finish.3
  (27 shorter events, 0.5 us)
Async XLA Ops:
  6.5 20.2 %collective-permute-start.4 = (bf16[256,1280]{1,0:T(8,128)(2,1)}, bf16[256,1280]{1,0:T(8,128)(2,1)S(1)}, u32[]{:S(2)}, u32[]{:S(2)}) collective-permute-start(bf16[256,1280]{1,0:T(8,128)(2,1)} %get-tuple-element.26), channel_id=1, source_target_pairs={{0,2},{2,3},{3,1},{1,0},{4,6},{6,7},{7,5},{5,4},{8,10},{10,11},{11... | collective-permute-start | bytes 1966088 | tf_op jit(solution)/shard_map/ppermute | solution.py:576
  10.6 5.0 %collective-permute-start = (bf16[64,1152]{1,0:T(8,128)(2,1)}, bf16[64,1152]{1,0:T(8,128)(2,1)S(1)}, u32[]{:S(2)}, u32[]{:S(2)}) collective-permute-start(bf16[64,1152]{1,0:T(8,128)(2,1)} %get-tuple-element.22), channel_id=1, source_target_pairs={{0,4},{4,0},{8,12},{12,8},{1,5},{5,1},{9,13},{13,9},{2,6},{6,2},{1... | collective-permute-start | bytes 442376 | tf_op jit(solution)/shard_map/ppermute | solution.py:570
  10.6 6.9 %collective-permute-start.1 = (bf16[64,1152]{1,0:T(8,128)(2,1)}, bf16[64,1152]{1,0:T(8,128)(2,1)S(1)}, u32[]{:S(2)}, u32[]{:S(2)}) collective-permute-start(bf16[64,1152]{1,0:T(8,128)(2,1)} %get-tuple-element.23), channel_id=1, source_target_pairs={{0,8},{4,12},{8,0},{12,4},{1,9},{5,13},{9,1},{13,5},{2,10},{6,14},... | collective-permute-start | bytes 442376 | tf_op jit(solution)/shard_map/ppermute | solution.py:570
  12.1 7.7 %collective-permute-start.2 = (bf16[64,1152]{1,0:T(8,128)(2,1)}, bf16[64,1152]{1,0:T(8,128)(2,1)S(1)}, u32[]{:S(2)}, u32[]{:S(2)}) collective-permute-start(bf16[64,1152]{1,0:T(8,128)(2,1)} %get-tuple-element.24), channel_id=1, source_target_pairs={{0,12},{4,8},{8,4},{12,0},{1,13},{5,9},{9,5},{13,1},{2,14},{6,10},... | collective-permute-start | bytes 442376 | tf_op jit(solution)/shard_map/ppermute | solution.py:570
  12.5 1.0 %copy-start = (bf16[256,1024]{1,0:T(8,128)(2,1)S(1)}, bf16[256,1024]{1,0:T(8,128)(2,1)}, u32[]{:S(2)}) copy-start(bf16[256,1024]{1,0:T(8,128)(2,1)} %get-tuple-element.20.refs_0_.refs_1_.refs_5_) | copy-start | bytes 1572868
  13.5 6.3 %copy-start.5 = (bf16[8,64,1024]{2,1,0:T(8,128)(2,1)S(1)}, bf16[8,64,1024]{2,1,0:T(8,128)(2,1)}, u32[]{:S(2)}) copy-start(bf16[8,64,1024]{2,1,0:T(8,128)(2,1)} %refs_4_.2) | copy-start | bytes 3145732
  13.5 6.3 %copy-start.6 = (bf16[64,1152]{1,0:T(8,128)(2,1)S(1)}, bf16[64,1152]{1,0:T(8,128)(2,1)}, u32[]{:S(2)}) copy-start(bf16[64,1152]{1,0:T(8,128)(2,1)} %get-tuple-element.21.refs_0_) | copy-start | bytes 442372
  15.6 11.1 %copy-start.1 = (bf16[256,1024]{1,0:T(8,128)(2,1)S(1)}, bf16[256,1024]{1,0:T(8,128)(2,1)}, u32[]{:S(2)}) copy-start(bf16[256,1024]{1,0:T(8,128)(2,1)} %get-tuple-element.20.refs_0_.refs_1_.refs_5_) | copy-start | bytes 1572868
  20.5 6.1 %collective-permute-start.5 = (bf16[128,128]{1,0:T(8,128)(2,1)S(1)}, bf16[128,128]{1,0:T(8,128)(2,1)S(1)}, u32[]{:S(2)}, u32[]{:S(2)}) collective-permute-start(bf16[128,128]{1,0:T(8,128)(2,1)S(1)} %get-tuple-element.25.refs_1_), channel_id=1, source_target_pairs={{0,1},{1,0},{2,3},{3,2},{4,5},{5,4},{6,7},{7,6},{8,9},{9,8},{10,11... | collective-permute-start | bytes 98312 | tf_op jit(solution)/shard_map/ppermute | solution.py:609
  20.6 16.8 %collective-permute-start.3 = (bf16[256,768]{1,0:T(8,128)(2,1)S(1)}, bf16[256,768]{1,0:T(8,128)(2,1)S(1)}, u32[]{:S(2)}, u32[]{:S(2)}) collective-permute-start(bf16[256,768]{1,0:T(8,128)(2,1)S(1)} %hold.1.refs_4_), channel_id=1, source_target_pairs={{0,2},{2,3},{3,1},{1,0},{4,6},{6,7},{7,5},{5,4},{8,10},{10,11},{11... | collective-permute-start | bytes 1179656 | tf_op jit(solution)/shard_map/ppermute | solution.py:576
  29.3 19.8 %collective-permute-start.9 = (bf16[256,1280]{1,0:T(8,128)(2,1)S(1)}, bf16[256,1280]{1,0:T(8,128)(2,1)S(1)}, u32[]{:S(2)}, u32[]{:S(2)}) collective-permute-start(bf16[256,1280]{1,0:T(8,128)(2,1)S(1)} %hop.6.refs_3_), channel_id=1, source_target_pairs={{0,2},{2,3},{3,1},{1,0},{4,6},{6,7},{7,5},{5,4},{8,10},{10,11},{11... | collective-permute-start | bytes 1966088 | tf_op jit(solution)/shard_map/ppermute | solution.py:576
  32.0 23.2 %collective-permute-start.8 = (bf16[128,128]{1,0:T(8,128)(2,1)S(1)}, bf16[128,128]{1,0:T(8,128)(2,1)S(1)}, u32[]{:S(2)}, u32[]{:S(2)}) collective-permute-start(bf16[128,128]{1,0:T(8,128)(2,1)S(1)} %add_convert_fusion.refs_3_.refs_0_), channel_id=1, source_target_pairs={{0,3},{3,0},{4,7},{7,4},{8,11},{11,8},{12,15},{15,12},{16,19},{19,... | collective-permute-start | bytes 98312 | tf_op jit(solution)/shard_map/ppermute | solution.py:589
  36.1 19.1 %collective-permute-start.7 = (bf16[128,128]{1,0:T(8,128)(2,1)S(1)}, bf16[128,128]{1,0:T(8,128)(2,1)S(1)}, u32[]{:S(2)}, u32[]{:S(2)}) collective-permute-start(bf16[128,128]{1,0:T(8,128)(2,1)S(1)} %add_convert_fusion.refs_3_.refs_0_), channel_id=1, source_target_pairs={{0,2},{3,1},{4,6},{7,5},{8,10},{11,9},{12,14},{15,13},{16,18},{19,... | collective-permute-start | bytes 98312 | tf_op jit(solution)/shard_map/ppermute | solution.py:588
  39.4 15.7 %copy-start.2 = (bf16[8,64,2048]{2,1,0:T(8,128)(2,1)S(1)}, bf16[8,64,2048]{2,1,0:T(8,128)(2,1)}, u32[]{:S(2)}) copy-start(bf16[8,64,2048]{2,1,0:T(8,128)(2,1)} %refs_4_.3) | copy-start | bytes 6291460
  39.4 19.5 %collective-permute-start.6 = (bf16[256,768]{1,0:T(8,128)(2,1)S(1)}, bf16[256,768]{1,0:T(8,128)(2,1)S(1)}, u32[]{:S(2)}, u32[]{:S(2)}) collective-permute-start(bf16[256,768]{1,0:T(8,128)(2,1)S(1)} %hop.7), channel_id=1, source_target_pairs={{0,2},{2,3},{3,1},{1,0},{4,6},{6,7},{7,5},{5,4},{8,10},{10,11},{11... | collective-permute-start | bytes 1179656 | tf_op jit(solution)/shard_map/ppermute | solution.py:576
  51.7 22.8 %collective-permute-start.14 = (bf16[256,1280]{1,0:T(8,128)(2,1)S(1)}, bf16[256,1280]{1,0:T(8,128)(2,1)S(1)}, u32[]{:S(2)}, u32[]{:S(2)}) collective-permute-start(bf16[256,1280]{1,0:T(8,128)(2,1)S(1)} %hop.8.refs_5_), channel_id=1, source_target_pairs={{0,2},{2,3},{3,1},{1,0},{4,6},{6,7},{7,5},{5,4},{8,10},{10,11},{11... | collective-permute-start | bytes 1966088 | tf_op jit(solution)/shard_map/ppermute | solution.py:576
  56.0 8.5 %collective-permute-start.11 = (bf16[64,2048]{1,0:T(8,128)(2,1)S(1)}, bf16[64,2048]{1,0:T(8,128)(2,1)S(1)}, u32[]{:S(2)}, u32[]{:S(2)}) collective-permute-start(bf16[64,2048]{1,0:T(8,128)(2,1)S(1)} %get-tuple-element.29), channel_id=1, source_target_pairs={{0,4},{4,0},{8,12},{12,8},{1,5},{5,1},{9,13},{13,9},{2,6},{6,2},{1... | collective-permute-start | bytes 786440 | tf_op jit(solution)/shard_map/ppermute | solution.py:570
  56.0 9.2 %collective-permute-start.12 = (bf16[64,2048]{1,0:T(8,128)(2,1)S(1)}, bf16[64,2048]{1,0:T(8,128)(2,1)S(1)}, u32[]{:S(2)}, u32[]{:S(2)}) collective-permute-start(bf16[64,2048]{1,0:T(8,128)(2,1)S(1)} %get-tuple-element.30), channel_id=1, source_target_pairs={{0,8},{4,12},{8,0},{12,4},{1,9},{5,13},{9,1},{13,5},{2,10},{6,14},... | collective-permute-start | bytes 786440 | tf_op jit(solution)/shard_map/ppermute | solution.py:570
  57.6 12.3 %collective-permute-start.13 = (bf16[64,2048]{1,0:T(8,128)(2,1)S(1)}, bf16[64,2048]{1,0:T(8,128)(2,1)S(1)}, u32[]{:S(2)}, u32[]{:S(2)}) collective-permute-start(bf16[64,2048]{1,0:T(8,128)(2,1)S(1)} %get-tuple-element.31), channel_id=1, source_target_pairs={{0,12},{4,8},{8,4},{12,0},{1,13},{5,9},{9,5},{13,1},{2,14},{6,10},... | collective-permute-start | bytes 786440 | tf_op jit(solution)/shard_map/ppermute | solution.py:570
  58.9 11.0 %copy-start.4 = (bf16[256,2048]{1,0:T(8,128)(2,1)S(1)}, bf16[256,2048]{1,0:T(8,128)(2,1)}, u32[]{:S(2)}) copy-start(bf16[256,2048]{1,0:T(8,128)(2,1)} %refs_6_.1) | copy-start | bytes 3145732
  59.0 11.0 %copy-start.7 = (bf16[256,256]{1,0:T(8,128)(2,1)S(1)}, bf16[256,256]{1,0:T(8,128)(2,1)}, u32[]{:S(2)}) copy-start(bf16[256,256]{1,0:T(8,128)(2,1)} %get-tuple-element.32.refs_4_) | copy-start | bytes 393220
  61.0 19.2 %collective-permute-start.10 = (bf16[256,768]{1,0:T(8,128)(2,1)S(1)}, bf16[256,768]{1,0:T(8,128)(2,1)S(1)}, u32[]{:S(2)}, u32[]{:S(2)}) collective-permute-start(bf16[256,768]{1,0:T(8,128)(2,1)S(1)} %hop.9.refs_8_), channel_id=1, source_target_pairs={{0,2},{2,3},{3,1},{1,0},{4,6},{6,7},{7,5},{5,4},{8,10},{10,11},{11... | collective-permute-start | bytes 1179656 | tf_op jit(solution)/shard_map/ppermute | solution.py:576
  74.5 1.3 %copy-start.3 = (f32[256,1280]{1,0:T(8,128)S(1)}, f32[256,1280]{1,0:T(8,128)}, u32[]{:S(2)}) copy-start(f32[256,1280]{1,0:T(8,128)} %get-tuple-element.34.settled_ref) | copy-start | bytes 3932164
